TPU v7x, 32 devices: a whole 2x2x4 slice. The times are simulated.
32 devices in a mesh: grp: 2 (over y), seq: 4 (over z), dp: 2 (over x), head: 2 (over core).
Axes of the slice: x: 2, y: 2, z: 4, core: 2. Of those that a mesh axis runs over, the one named last changes fastest.
Arguments:
- tokens: bfloat16 [4, 512, 4096], P(('grp', 'dp'), 'seq', 'head'), parts along dimension 0, may hold values from -6 to 6
- ssd_input: bfloat16 [4, 512, 4096], P(('grp', 'dp'), 'seq', 'head'), parts along dimension 0, may hold values from -6 to 6
- grad_out: bfloat16 [4, 512, 4096], P(('grp', 'dp'), 'seq', 'head'), parts along dimension 0, may hold values from -6 to 6
- w_bc: bfloat16 [4096, 256], P(('head', 'dp')), may hold values from -0.0029296875 to 0.0029296875
- w_dt: bfloat16 [4096, 64], P(('head', 'dp')), may hold values from -0.09375 to 0.09375
- decay_rate: float32 [64], P('head'), may hold values from 0 to 1, as said below
- dt_bias: float32 [64], P('head'), may hold values from -2 to 0.5
Outputs:
- grad_input: bfloat16 [4, 512, 4096], P(('grp', 'dp'), 'seq', 'head'), parts along dimension 0
- grad_tokens: bfloat16 [4, 512, 4096], P(('grp', 'dp'), 'seq', 'head'), parts along dimension 0
- grad_w_bc: float32 [8192, 256], P(('grp', 'head', 'dp')), parts along dimension 0
- grad_w_dt: float32 [8192, 64], P(('grp', 'head', 'dp')), parts along dimension 0
There are 2 independent parts, one for each index of `grp`. A program takes and returns all parts, laid end to end along the dimension named above; an argument that names none is the same for every part. Nothing has to cross between parts.
Inputs may be any that keep to these rules, and one draw needn't show every extreme that they name: `decay_rate`: each head's decay rate is positive.
All inputs are finite; a program needn't handle non-finite values.
Results may differ from a plain program's by a relative error of at most 0.0049.
Values may be sent and summed in bfloat16 or wider, within the bound.
No kernel may reach another device: no remote copies, remote signals or barrier semaphores. Data moves between devices by JAX's collectives and lax.ppermute only.
A program may use at most 64 MiB of HBM per device.

v0:
```python
import jax
import jax.numpy as jnp
from jax import lax
from jax.sharding import PartitionSpec as P


def carried_in(part, axis, combine, identity, reverse):
    count = lax.axis_size(axis)
    place = lax.axis_index(axis)
    ahead = count - 1 - place if reverse else place
    gathered = jax.tree.map(lambda a: lax.all_gather(a, axis), part)
    state = jax.tree.map(lambda a, e: jnp.zeros_like(a) + jnp.asarray(e, a.dtype), part, identity)

    def one(step, state):
        source = count - 1 - step if reverse else step
        return combine(
            state, jax.tree.map(lambda a: lax.dynamic_index_in_dim(a, source, 0, False), gathered)
        )

    return lax.fori_loop(0, ahead, one, state)


def unpack_block(values, bc_block, raw_block, decay_rate, dt_bias):
    row_count = values.shape[0]
    head_count = decay_rate.shape[0]
    state_size = bc_block.shape[1] // 2
    step_size = jax.nn.softplus(raw_block + dt_bias[None, :])
    cumulative = jnp.cumsum(-step_size * decay_rate[None, :], axis=0)
    per_head = values.reshape(row_count, head_count, -1)
    return (per_head, bc_block[:, :state_size], bc_block[:, state_size:], step_size, cumulative)


def block_state(values, bc_block, raw_block, decay_rate, dt_bias):
    per_head, input_vec, readout, step_size, cumulative = unpack_block(
        values, bc_block, raw_block, decay_rate, dt_bias
    )
    weights = jnp.exp(cumulative[-1][None, :] - cumulative) * step_size
    state = jnp.einsum(
        "sh,shp,sn->hpn", weights, per_head, input_vec, precision=lax.Precision.HIGHEST
    )
    return (state, jnp.exp(cumulative[-1]))


def block_output(values, bc_block, raw_block, decay_rate, dt_bias, incoming):
    per_head, input_vec, readout, step_size, cumulative = unpack_block(
        values, bc_block, raw_block, decay_rate, dt_bias
    )
    row_count = values.shape[0]
    scores = jnp.dot(readout, input_vec.T, precision=lax.Precision.HIGHEST)
    position = jnp.arange(row_count)
    causal = position[:, None] >= position[None, :]
    leading = cumulative.T
    gap_matrix = leading[:, :, None] - leading[:, None, :]
    kernel = (
        jnp.exp(jnp.where(causal[None], gap_matrix, -jnp.inf))
        * scores[None]
        * step_size.T[:, None, :]
    )
    within = jnp.einsum("hts,shp->thp", kernel, per_head, precision=lax.Precision.HIGHEST)
    carried = jnp.einsum("tn,hpn->thp", readout, incoming, precision=lax.Precision.HIGHEST)
    carried = carried * jnp.exp(cumulative)[:, :, None]
    return (within + carried).reshape(row_count, -1)


def combine_states(earlier, later):
    return (earlier[0] * later[0], later[0][:, None, None] * earlier[1] + later[1])


def body(tokens, ssd_input, grad_out, w_bc, w_dt, decay_rate, dt_bias):
    features = tokens[0]
    values = ssd_input[0].astype(jnp.float32)
    cotangent = grad_out[0].astype(jnp.float32)
    row_count = features.shape[0]
    head_local = decay_rate.shape[0]
    state_cols = w_bc.shape[1]
    first_head = lax.axis_index("head") * head_local
    panel = jnp.concatenate([w_bc, w_dt], axis=1)
    half_panel = lax.all_gather(panel, "dp", axis=0, tiled=True)
    partial_proj = jnp.dot(features, half_panel, preferred_element_type=jnp.float32)
    projected = lax.psum(partial_proj, "head")
    bc_cols = projected[:, :state_cols]
    raw_cols = projected[:, state_cols:]

    def state_part(value_arg, bc_arg, raw_arg):
        local_raw = lax.dynamic_slice_in_dim(raw_arg, first_head, head_local, 1)
        return block_state(value_arg, bc_arg, local_raw, decay_rate, dt_bias)

    def output_part(value_arg, bc_arg, raw_arg, carried_arg):
        local_raw = lax.dynamic_slice_in_dim(raw_arg, first_head, head_local, 1)
        return block_output(value_arg, bc_arg, local_raw, decay_rate, dt_bias, carried_arg)

    (state, decay), state_pull = jax.vjp(state_part, values, bc_cols, raw_cols)
    identity = (jnp.ones_like(decay), jnp.zeros_like(state))
    _, incoming = carried_in((decay, state), "seq", combine_states, identity, False)
    _, output_pull = jax.vjp(output_part, values, bc_cols, raw_cols, incoming)
    values_out, bc_out, raw_out, local_back = output_pull(cotangent)
    _, outgoing_back = carried_in((decay, local_back), "seq", combine_states, identity, True)
    decay_back = jnp.sum(outgoing_back * incoming, axis=(1, 2))
    values_state, bc_state, raw_state = state_pull((outgoing_back, decay_back))
    grad_values = (values_out + values_state).astype(jnp.bfloat16)
    local_proj = jnp.concatenate([bc_out + bc_state, raw_out + raw_state], axis=1)
    proj_back = lax.psum(local_proj, "head")
    proj_low = proj_back.astype(jnp.bfloat16)
    grad_features = lax.dot_general(
        proj_low, half_panel, (((1,), (1,)), ((), ())), preferred_element_type=jnp.float32
    )
    grad_features = grad_features.astype(jnp.bfloat16)
    panel_term = lax.dot_general(
        features, proj_low, (((0,), (0,)), ((), ())), preferred_element_type=jnp.float32
    )
    summed = lax.psum(panel_term, "seq")
    reduced = lax.psum_scatter(summed, "dp", scatter_dimension=0, tiled=True)
    reduced = reduced * (1.0 / (row_count * lax.axis_size("seq") * lax.axis_size("dp")))
    return (
        grad_values[None],
        grad_features[None],
        reduced[:, :state_cols],
        reduced[:, state_cols:],
    )


def solution(mesh):
    in_specs = (
        P(("grp", "dp"), "seq", "head"),
        P(("grp", "dp"), "seq", "head"),
        P(("grp", "dp"), "seq", "head"),
        P(("head", "dp"), None),
        P(("head", "dp"), None),
        P("head"),
        P("head"),
    )
    out_specs = (
        P(("grp", "dp"), "seq", "head"),
        P(("grp", "dp"), "seq", "head"),
        P(("grp", "head", "dp"), None),
        P(("grp", "head", "dp"), None),
    )
    return jax.shard_map(body, mesh=mesh, in_specs=in_specs, out_specs=out_specs, check_vma=False)
```

profile of v0, /device:TPU:0, one launch (start us, length us, event | category | flops | bytes accessed | tf_op | source)
XLA Modules:
  0.0 365.6 jit_solution(2430438048992957858)
XLA Ops:
  8.4 2.0 pad_maximum_fusion
  10.5 30.0 %all-gather.7.cloned.1.call-done = bf16[2048,320]{1,0:T(8,128)(2,1)} async-done(((bf16[1024,320]{1,0:T(8,128)(2,1)}), bf16[2048,320]{1,0:T(8,128)(2,1)}) %all-gather.7.cloned.1.call-update) | async-done | bytes 1310736 | tf_op jit(solution)/shard_map/all_gather | solution.py:78
  40.4 2.7 convolution_bitcast_fusion.1
  43.5 17.9 %all-reduce.9.cloned.1.call-done = f32[128,320]{0,1:T(8,128)} async-done(((f32[128,320]{0,1:T(8,128)}), f32[128,320]{0,1:T(8,128)}) %all-reduce.9.cloned.1.call-update) | async-done | bytes 163856 | tf_op jit(solution)/shard_map/psum | solution.py:80
  62.6 2.8 fusion.15
  66.0 11.1 %all-gather.2 = f32[4,1,32]{2,1,0:T(1,128)S(1)} all-gather(f32[1,1,32]{2,1,0:T(1,128)S(1)} %bitcast.101), channel_id=1, replica_groups=mesh['grp'=2,'seq'=4,'dp'=2,'head'=2] {'seq'}, dimensions={0}, use_global_device_ids=true | all-gather | bytes 640 | tf_op jit(solution)/shard_map/all_gather | solution.py:11
  77.1 70.5 %all-gather.9.cloned.1.call-done = f32[128,64,128]{2,1,0:T(8,128)} async-done(((f32[32,64,128]{2,1,0:T(8,128)}), f32[128,64,128]{2,1,0:T(8,128)}) %all-gather.9.cloned.1.call-update) | async-done | bytes 4194320 | tf_op jit(solution)/shard_map/all_gather | solution.py:11
  147.7 4.5 %while.26 = (s32[]{:T(128)}, f32[32,64,128]{2,1,0:T(8,128)S(1)}, s32[]{:T(128)}, f32[4,32]{1,0:T(4,128)S(1)}, f32[4,32,64,128]{3,2,1,0:T(8,128)}, /*index=5*/s32[]{:T(128)}, s32[]{:T(128)}, s32[]{:T(128)}, s32[]{:T(128)}) while((s32[]{:T(128)}, f32[32,64,128]{2,1,0:T(8,128)S(1)}, s32[]{:T(128)}, f32[4,32]{1,0:T(4,128)S(1)}, ...), condition=%wide.region_3.5_spmd, body=%wide.region_2.4_spmd.sunk | while | flops 524294 | bytes 3146267 | solution.py:20
  147.7 1.5 bitcast_add_fusion.6
  149.2 1.4 bitcast_add_fusion.6
  150.7 1.4 bitcast_add_fusion.6
  152.2 2.0 fusion.23
  155.0 2.0 fusion.17
  158.1 1.8 fusion.21
  160.0 2.6 fusion.20
  162.8 73.3 %all-gather.11.cloned.1.call-done = f32[128,64,128]{2,1,0:T(8,128)} async-done(((f32[32,64,128]{2,1,0:T(8,128)}), f32[128,64,128]{2,1,0:T(8,128)}) %all-gather.11.cloned.1.call-update) | async-done | bytes 4194320 | tf_op jit(solution)/shard_map/all_gather | solution.py:11
  237.4 1.8 fusion.22
  244.3 3.8 %all-reduce.12 = bf16[128,320]{0,1:T(8,128)(2,1)S(1)} all-reduce(f32[128,320]{0,1:T(8,128)S(1)} %pad_maximum_fusion.1), channel_id=1, replica_groups=mesh['grp'=2,'seq'=4,'dp'=2,'head'=2] {'head'}, use_global_device_ids=true, to_apply=%region_15.17 | all-reduce | flops 40960 | bytes 245760 | tf_op jit(solution)/shard_map/psum | solution.py:102
  248.2 2.0 convolution_bitcast_fusion
  250.2 42.6 %reduce-scatter.2.cloned.1.call-done = f32[1024,320]{0,1:T(8,128)} async-done(((f32[2048,320]{0,1:T(8,128)}), f32[1024,320]{0,1:T(8,128)}) %reduce-scatter.2.cloned.1.call-update) | async-done | bytes 1310736 | tf_op jit(solution)/shard_map/reduce_scatter | solution.py:112
  292.9 3.0 fusion.11
  296.9 1.4 fusion
  298.3 56.9 %all-reduce.11.cloned.1.call-done = f32[1024,320]{0,1:T(8,128)} async-done(((f32[1024,320]{0,1:T(8,128)}), f32[1024,320]{0,1:T(8,128)}) %all-reduce.11.cloned.1.call-update) | async-done | bytes 1310736 | tf_op jit(solution)/shard_map/psum | solution.py:111
  355.2 1.4 broadcast_multiply_fusion
  (118 shorter events, 15.0 us)
Async XLA Ops:
  7.2 33.3 %copy-start = (bf16[1,128,2048]{2,1,0:T(8,128)(2,1)S(1)}, bf16[1,128,2048]{2,1,0:T(8,128)(2,1)}, u32[]{:S(2)}) copy-start(bf16[1,128,2048]{2,1,0:T(8,128)(2,1)} %param.12) | copy-start | bytes 1572868
  7.2 33.3 %all-gather.7.cloned.1.call-start = ((), (), s32[]{:S(2)}) async-start(), calls=%async_computation.1 | async-start | bytes 2359296 | tf_op jit(solution)/shard_map/all_gather | solution.py:78
  10.4 32.8 %copy-start.3 = (bf16[1,128,2048]{2,1,0:T(8,128)(2,1)S(1)}, bf16[1,128,2048]{2,1,0:T(8,128)(2,1)}, u32[]{:S(2)}) copy-start(bf16[1,128,2048]{2,1,0:T(8,128)(2,1)} %param.14) | copy-start | bytes 1572868
  10.4 51.8 %copy-start.24 = (f32[32]{0:T(128)S(1)}, f32[32]{0:T(128)}, u32[]{:S(2)}) copy-start(f32[32]{0:T(128)} %param.18) | copy-start | bytes 388
  10.4 51.8 %copy-start.26 = (f32[32]{0:T(128)S(1)}, f32[32]{0:T(128)}, u32[]{:S(2)}) copy-start(f32[32]{0:T(128)} %param.17) | copy-start | bytes 388
  10.4 51.0 %all-reduce.9.cloned.1.call-start = ((), (), s32[]{:S(2)}) async-start(), calls=%async_computation.2 | async-start | bytes 327680 | tf_op jit(solution)/shard_map/psum | solution.py:80
  43.1 104.4 %all-gather.9.cloned.1.call-start = ((), (), s32[]{:S(2)}) async-start(), calls=%async_computation.3 | async-start | bytes 5242880 | tf_op jit(solution)/shard_map/all_gather | solution.py:11
  43.2 22.3 %copy-start.4 = (bf16[1,128,2048]{2,1,0:T(8,128)(2,1)S(1)}, bf16[1,128,2048]{2,1,0:T(8,128)(2,1)}, u32[]{:S(2)}) copy-start(bf16[1,128,2048]{2,1,0:T(8,128)(2,1)} %param.13) | copy-start | bytes 1572868
  62.6 84.9 %copy-start.7 = (f32[128,32]{0,1:T(8,128)}, f32[128,32]{0,1:T(8,128)S(1)}, u32[]{:S(2)}) copy-start(f32[128,32]{0,1:T(8,128)S(1)} %exp.26) | copy-start | bytes 49156
  65.4 170.7 %all-gather.11.cloned.1.call-start = ((), (), s32[]{:S(2)}) async-start(), calls=%async_computation.4 | async-start | bytes 5242880 | tf_op jit(solution)/shard_map/all_gather | solution.py:11
  66.0 88.2 %copy-start.28 = (f32[32]{0:T(128)}, f32[32]{0:T(128)S(1)}, u32[]{:S(2)}) copy-start(f32[32]{0:T(128)S(1)} %get-tuple-element.158) | copy-start | bytes 388
  154.1 5.8 %copy-start.9 = (f32[128,32]{0,1:T(8,128)}, f32[128,32]{0,1:T(8,128)S(1)}, u32[]{:S(2)}) copy-start(f32[128,32]{0,1:T(8,128)S(1)} %get-tuple-element.184) | copy-start | bytes 49156
  157.0 135.8 %reduce-scatter.2.cloned.1.call-start = ((), (), s32[]{:S(2)}) async-start(), calls=%async_computation.5 | async-start | bytes 3932160 | tf_op jit(solution)/shard_map/reduce_scatter | solution.py:112
  237.3 6.4 %copy-start.23 = (f32[32,128]{1,0:T(8,128)S(1)}, f32[32,128]{1,0:T(8,128)}, u32[]{:S(2)}) copy-start(f32[32,128]{1,0:T(8,128)} %get-tuple-element.156) | copy-start | bytes 49156
  237.3 6.4 %copy-start.25 = (f32[32]{0:T(128)S(1)}, f32[32]{0:T(128)}, u32[]{:S(2)}) copy-start(f32[32]{0:T(128)} %param.18) | copy-start | bytes 388
  237.4 6.4 %copy-start.27 = (f32[32]{0:T(128)S(1)}, f32[32]{0:T(128)}, u32[]{:S(2)}) copy-start(f32[32]{0:T(128)} %param.17) | copy-start | bytes 388
  237.4 6.5 %copy-start.10 = (f32[128,32]{0,1:T(8,128)S(1)}, f32[128,32]{0,1:T(8,128)}, u32[]{:S(2)}) copy-start(f32[128,32]{0,1:T(8,128)} %copy-done.9) | copy-start | bytes 49156
  237.4 6.5 %copy-start.29 = (f32[32]{0:T(128)S(1)}, f32[32]{0:T(128)}, u32[]{:S(2)}) copy-start(f32[32]{0:T(128)} %copy-done.28) | copy-start | bytes 388
  250.2 42.7 %copy-start.6 = (f32[128,32]{0,1:T(8,128)S(1)}, f32[128,32]{0,1:T(8,128)}, u32[]{:S(2)}) copy-start(f32[128,32]{0,1:T(8,128)} %copy-done.5) | copy-start | bytes 49156
  250.2 42.7 %copy-start.12 = (f32[128,128]{1,0:T(8,128)S(1)}, f32[128,128]{1,0:T(8,128)}, u32[]{:S(2)}) copy-start(f32[128,128]{1,0:T(8,128)} %copy-done.11) | copy-start | bytes 196612
  250.2 42.7 %copy-start.16 = (f32[32,128]{1,0:T(8,128)S(1)}, f32[32,128]{1,0:T(8,128)}, u32[]{:S(2)}) copy-start(f32[32,128]{1,0:T(8,128)} %copy-done.15) | copy-start | bytes 49156
  250.2 42.7 %copy-start.18 = (f32[32,128]{1,0:T(8,128)S(1)}, f32[32,128]{1,0:T(8,128)}, u32[]{:S(2)}) copy-start(f32[32,128]{1,0:T(8,128)} %copy-done.17) | copy-start | bytes 49156
  250.2 42.7 %copy-start.22 = (pred[128,128]{1,0:T(8,128)(4,1)S(1)}, pred[128,128]{1,0:T(8,128)(4,1)}, u32[]{:S(2)}) copy-start(pred[128,128]{1,0:T(8,128)(4,1)} %copy-done.21) | copy-start | bytes 49156
  250.2 105.0 %all-reduce.11.cloned.1.call-start = ((), (), s32[]{:S(2)}) async-start(), calls=%async_computation.6 | async-start | bytes 2621440 | tf_op jit(solution)/shard_map/psum | solution.py:111
  (13 other events, 55.1 us)
Sparse Core Ops, SparseCore 0:
  10.5 29.8 all-gather.6
  43.3 18.0 all-reduce.8
  65.6 81.9 all-gather.8
  157.1 78.9 all-gather.10
  250.3 42.4 reduce-scatter.1
  295.2 60.0 all-reduce.10
where the time goes:
time: 366 us
  waiting for transfers between devices  291 us (80%)
  matrix products  23.8 us (7%)
  blocking collectives  14.9 us (4%)
  between operations  14.6 us (4%)
  other arithmetic  12.4 us (3%)
  local copies, waits for them, and re-layouts  8.12 us (2%)
    all_gather x2, waiting for transfers between devices, carried_in(): gathered = jax.tree.map(lambda a: lax.all_gather(a, axis), part)  144 us
    psum x1, waiting for transfers between devices, body(): summed = lax.psum(panel_term, 'seq')  56.9 us
    reduce_scatter x1, waiting for transfers between devices, body(): reduced = lax.psum_scatter(summed, 'dp', scatter_dimension=0, tiled=True)  42.6 us
    all_gather x1, waiting for transfers between devices, body(): half_panel = lax.all_gather(panel, 'dp', axis=0, tiled=True)  30 us
    psum x1, waiting for transfers between devices, body(): projected = lax.psum(partial_proj, 'head')  17.9 us
    all_gather x1, blocking collectives, carried_in(): gathered = jax.tree.map(lambda a: lax.all_gather(a, axis), part)  11.1 us
  transfers between devices with their start and end apart: 6, of which 6 were waited for; matrix products, arithmetic and copies ran while one was open for 3% of the time, Pallas kernels for 0%

commit v1 on v0

v1 whole, which is shorter than its diff:
```python
import jax
import jax.numpy as jnp
from jax import lax
from jax.sharding import PartitionSpec as P

CHUNKS = 4
BF = jnp.bfloat16
F32 = jnp.float32


def cyclic(a, axis, by):
    count = lax.axis_size(axis)
    return lax.ppermute(a, axis, [(i, (i + by) % count) for i in range(count)])


def along(a, axis, by):
    count = lax.axis_size(axis)
    return lax.ppermute(a, axis, [(i, i + by) for i in range(count) if 0 <= i + by < count])


def mm(a, b, ca, cb):
    return lax.dot_general(a, b, (((ca,), (cb,)), ((), ())), preferred_element_type=F32)


def relay(block, axis):
    count = lax.axis_size(axis)
    slots = []
    for way in (1, -1):
        held = block
        for _ in range(count - 1):
            held = along(held, axis, way)
            slots.append(held)
    return slots


def chain(own, decay, axis, way):
    count = lax.axis_size(axis)
    sent, total = own.astype(BF), None
    for hop in range(1, count):
        source = hop - 1 if way > 0 else count - hop
        got = lax.ppermute(sent, axis, [(source, source + way)])
        total = got if total is None else total + got
        if hop < count - 1:
            sent = (decay * got.astype(F32) + own).astype(BF)
    return total


def body(tokens, ssd_input, grad_out, w_bc, w_dt, decay_rate, dt_bias):
    feats, xb, gb = tokens[0], ssd_input[0], grad_out[0]
    rows, width = feats.shape
    heads = decay_rate.shape[0]
    size = width // heads
    n_dp, n_seq, n_head = (lax.axis_size(a) for a in ("dp", "seq", "head"))
    d, c = lax.axis_index("dp"), lax.axis_index("head")
    part = width // n_dp
    state_n = w_bc.shape[1] // 2

    def piece(r):
        return lax.dynamic_slice_in_dim(feats, ((d + r) % n_dp) * part, part, 1)

    items = [piece(0)] + [cyclic(piece(r), "dp", r) for r in range(1, n_dp)]
    block = jnp.concatenate(items, axis=0)

    def project(a):
        return jnp.concatenate([mm(a, w_bc, 1, 0), mm(a, w_dt, 1, 0)], axis=1)

    total = project(items[0])
    for r in range(1, n_dp):
        total = total + cyclic(project(items[r]), "dp", -r)
    proj = total
    for r in range(1, n_head):
        proj = proj + cyclic(total, "head", r)
    b = proj[:, :state_n].astype(BF)
    cc = proj[:, state_n : 2 * state_n].astype(BF)
    raw = lax.dynamic_slice_in_dim(proj[:, 2 * state_n :], c * heads, heads, 1)
    pre = raw + dt_bias[None]
    dt = jax.nn.softplus(pre)
    cum = jnp.cumsum(-dt * decay_rate[None], axis=0)
    last = cum[-1]
    grow = jnp.exp(cum)
    tail = jnp.exp(last[None] - cum)
    w = tail * dt
    decay = jnp.exp(last)

    def spread(a):
        return jnp.repeat(a, size, axis=1)

    wx = (spread(w) * xb.astype(F32)).astype(BF)
    eg = (spread(grow) * gb.astype(F32)).astype(BF)
    state = mm(wx, b, 0, 0)
    back = mm(eg, cc, 0, 0)
    step = width // CHUNKS
    dec = jnp.repeat(decay, size)[:, None]
    ins, outs = [], []
    for k in range(CHUNKS):
        s = slice(k * step, (k + 1) * step)
        ins.append(chain(state[s], dec[s], "seq", 1))
        outs.append(chain(back[s], dec[s], "seq", -1))
    incoming = jnp.concatenate(ins, axis=0)
    outgoing = jnp.concatenate(outs, axis=0)

    pos = jnp.arange(rows)
    causal = pos[:, None] >= pos[None, :]
    scores = mm(cc, b, 1, 1)
    lead = cum.T
    decays = jnp.exp(jnp.where(causal[None], lead[:, :, None] - lead[:, None, :], -jnp.inf)) * dt.T[:, None, :]
    kern = (decays * scores[None]).astype(BF)
    xh = xb.reshape(rows, heads, size)
    gh = gb.reshape(rows, heads, size)
    y = jnp.einsum("hts,shp->thp", kern, xh, preferred_element_type=F32)
    gx = jnp.einsum("hts,thp->shp", kern, gh, preferred_element_type=F32)
    m = jnp.einsum("thp,shp->hts", gh, xh, preferred_element_type=F32)
    ds = jnp.sum(decays * m, axis=0).astype(BF)
    xf, gf = xh.astype(F32), gh.astype(F32)
    rowsum = jnp.sum(y * gf, axis=2)
    colsum = jnp.sum(gx * xf, axis=2)

    u = mm(cc, incoming, 1, 1).reshape(rows, heads, size)
    v = mm(b, outgoing, 1, 1).reshape(rows, heads, size)
    dgrow = jnp.sum(u * gf, axis=2)
    dw = jnp.sum(v * xf, axis=2)
    gx = gx + w[:, :, None] * v
    db = mm(ds, cc, 0, 0) + mm(wx, outgoing, 1, 0)
    dc = mm(ds, b, 1, 0) + mm(eg, incoming, 1, 0)
    ddecay = jnp.sum((incoming.astype(F32) * outgoing.astype(F32)).reshape(heads, -1), axis=1)
    wdw = w * dw
    dcum = rowsum - colsum + grow * dgrow - wdw
    dlast = jnp.sum(wdw, axis=0) + decay * ddecay
    rev = jnp.cumsum(dcum[::-1], axis=0)[::-1] + dlast[None]
    ddt = colsum / dt + tail * dw - decay_rate[None] * rev
    graw = ddt * jax.nn.sigmoid(pre)

    local = jnp.concatenate([db, dc], axis=1)
    bc_back = local
    for r in range(1, n_head):
        bc_back = bc_back + cyclic(local, "head", r)
    raws = lax.all_gather(graw.astype(BF), "head", axis=1, tiled=True)
    low = jnp.concatenate([bc_back.astype(BF), raws], axis=1)

    panel = jnp.concatenate([w_bc, w_dt], axis=1)
    grads = jnp.zeros((rows, width), BF)
    for r in range(n_dp):
        other = panel if r == 0 else cyclic(panel, "dp", r)
        term = mm(low, other, 1, 1).astype(BF)
        grads = lax.dynamic_update_slice_in_dim(grads, term, ((d - r) % n_dp) * part, 1)

    lows = jnp.concatenate([low] + [cyclic(low, "dp", r) for r in range(1, n_dp)], axis=0)
    half = lows.shape[0] // n_head
    mine = lax.dynamic_slice_in_dim(lows, c * half, half, 0)
    toks = [block] + relay(block, "seq")
    got = relay(mine, "seq")
    total = mm(block, lows, 0, 0)
    for t, q in zip(toks[1:], got):
        q = lax.all_gather(q, "head", axis=0, tiled=True)
        total = total + mm(t, q, 0, 0)
    total = total * (1.0 / (rows * n_seq * n_dp))
    return (
        gx.reshape(rows, width).astype(BF)[None],
        grads[None],
        total[:, : 2 * state_n],
        total[:, 2 * state_n :],
    )


def solution(mesh):
    in_specs = (
        P(("grp", "dp"), "seq", "head"),
        P(("grp", "dp"), "seq", "head"),
        P(("grp", "dp"), "seq", "head"),
        P(("head", "dp"), None),
        P(("head", "dp"), None),
        P("head"),
        P("head"),
    )
    out_specs = (
        P(("grp", "dp"), "seq", "head"),
        P(("grp", "dp"), "seq", "head"),
        P(("grp", "head", "dp"), None),
        P(("grp", "head", "dp"), None),
    )
    return jax.shard_map(body, mesh=mesh, in_specs=in_specs, out_specs=out_specs, check_vma=False)
```

time: 366 us -> 192 us (0.52)
  waiting for transfers between devices: 291 us -> 29.1 us
  starting transfers between devices: 0.25 us -> 92.5 us
  between operations: 14.6 us -> 2.19 us
  local copies, waits for them, and re-layouts: 8.12 us -> 13.5 us
  other arithmetic: 12.4 us -> 17.2 us
    all_gather x3 -> x0, waiting for transfers between devices: 174 us -> none  [the longest x2 144 us: carried_in(): gathered = jax.tree.map(lambda a: lax.all_gather(a, axis), part)]
    ppermute x0 -> x42, starting transfers between devices: none -> 92.5 us  [the longest x12 57.1 us: along(): lax.ppermute(a, axis, [(i, i + by) for i in range(count) if 0 <= i + by <...]
    psum x2 -> x0, waiting for transfers between devices: 74.8 us -> none  [the longest x1 56.9 us: body(): summed = lax.psum(panel_term, 'seq')]
    reduce_scatter x1 -> x0, waiting for transfers between devices: 42.6 us -> none  [body(): reduced = lax.psum_scatter(summed, 'dp', scatter_dimension=0, tiled=True)]
    ppermute x0 -> x42, waiting for transfers between devices: none -> 29.1 us  [the longest x24 17 us: chain(): got = lax.ppermute(sent, axis, [(source, source + way)])]
    convert_element_type x0 -> x10, other arithmetic: none -> 6.44 us  [the longest x6 5.12 us: chain(): sent = (decay * got.astype(F32) + own).astype(BF)]
    psum x1 -> x0, blocking collectives: 3.83 us -> none  [body(): proj_back = lax.psum(local_proj, 'head')]
    all_gather x1 -> x7, blocking collectives: 11.1 us -> 13.5 us  [the longest x6 11.5 us: body(): q = lax.all_gather(q, 'head', axis=0, tiled=True)]
  transfers between devices with their start and end apart: 6 -> 42, of which waited for: 6 -> 8; matrix products, arithmetic and copies ran while one was open for 3% -> 24% of each run, Pallas kernels for 0% -> 0%
where the time goes in v1:
time: 192 us; the launch traced here: 190 us
  starting transfers between devices  92.5 us (48%)
  waiting for transfers between devices  29.1 us (15%)
  matrix products  21.7 us (11%)
  other arithmetic  17.2 us (9%)
  local copies, waits for them, and re-layouts  13.5 us (7%)
  blocking collectives  13.5 us (7%)
  between operations  2.19 us (1%)
    ppermute x12, starting transfers between devices, along(): lax.ppermute(a, axis, [(i, i + by) for i in range(count) if 0 <= i + by <...  57.1 us
    ppermute x24, starting transfers between devices, chain(): got = lax.ppermute(sent, axis, [(source, source + way)])  28.3 us
    ppermute x24, waiting for transfers between devices, chain(): got = lax.ppermute(sent, axis, [(source, source + way)])  17 us
    dot_general x22, matrix products, mm(): lax.dot_general(a, b, (((ca,), (cb,)), ((), ())), preferred_element_type=...  16.5 us
    ppermute x6, waiting for transfers between devices, cyclic(): return lax.ppermute(a, axis, [(i, (i + by) % count) for i in range(count)])  11.7 us
    all_gather x6, blocking collectives, body(): q = lax.all_gather(q, 'head', axis=0, tiled=True)  11.5 us
    ppermute x6, starting transfers between devices, cyclic(): return lax.ppermute(a, axis, [(i, (i + by) % count) for i in range(count)])  7.11 us
    convert_element_type x6, other arithmetic, chain(): sent = (decay * got.astype(F32) + own).astype(BF)  5.12 us
  transfers between devices with their start and end apart: 42, of which 8 were waited for; matrix products, arithmetic and copies ran while one was open for 24% of the time, Pallas kernels for 0%

profile of v1, /device:TPU:0, one launch (start us, length us, event | category | flops | bytes accessed | tf_op | source)
XLA Modules:
  0.0 189.7 jit_solution(13776179397160238335)
XLA Ops:
  1.8 3.0 %collective-permute-start = (bf16[128,1024]{1,0:T(8,128)(2,1)S(1)}, bf16[128,1024]{1,0:T(8,128)(2,1)S(1)}, u32[]{:S(2)}, u32[]{:S(2)}) collective-permute-start(bf16[128,1024]{1,0:T(8,128)(2,1)S(1)} %get-tuple-element.49), channel_id=1, source_target_pairs={{0,2},{2,0},{1,3},{3,1},{4,6},{6,4},{5,7},{7,5},{8,10},{10,8},{9,1... | collective-permute-start | bytes 786440 | tf_op jit(solution)/shard_map/ppermute | solution.py:13
  6.1 5.0 %collective-permute-done = bf16[128,1024]{1,0:T(8,128)(2,1)S(1)} collective-permute-done((bf16[128,1024]{1,0:T(8,128)(2,1)S(1)}, bf16[128,1024]{1,0:T(8,128)(2,1)S(1)}, u32[]{:S(2)}, u32[]{:S(2)}) %collective-permute-start) | collective-permute-done | bytes 262176 | tf_op jit(solution)/shard_map/ppermute | solution.py:13
  11.6 1.8 collective-permute-start.1
  14.8 3.0 %collective-permute-done.1 = f32[128,320]{1,0:T(8,128)S(1)} collective-permute-done((f32[128,320]{1,0:T(8,128)S(1)}, f32[128,320]{1,0:T(8,128)S(1)}, u32[]{:S(2)}, u32[]{:S(2)}) %collective-permute-start.1) | collective-permute-done | bytes 163872 | tf_op jit(solution)/shard_map/ppermute | solution.py:13
  20.0 4.2 %collective-permute-start.30 = (bf16[256,1024]{1,0:T(8,128)(2,1)}, bf16[256,1024]{1,0:T(8,128)(2,1)}, u32[]{:S(2)}, u32[]{:S(2)}) collective-permute-start(bf16[256,1024]{1,0:T(8,128)(2,1)} %pad_maximum_fusion.3), channel_id=1, source_target_pairs={{0,4},{4,8},{8,12},{1,5},{5,9},{9,13},{2,6},{6,10},{10,14},{3,7},{... | collective-permute-start | bytes 1572872 | tf_op jit(solution)/shard_map/ppermute | solution.py:18
  48.8 13.9 %collective-permute-start.32 = (bf16[256,1024]{1,0:T(8,128)(2,1)}, bf16[256,1024]{1,0:T(8,128)(2,1)}, u32[]{:S(2)}, u32[]{:S(2)}) collective-permute-start(bf16[256,1024]{1,0:T(8,128)(2,1)} %collective-permute-done.30), channel_id=1, source_target_pairs={{0,4},{4,8},{8,12},{1,5},{5,9},{9,13},{2,6},{6,10},{10,14},{3,7},{... | collective-permute-start | bytes 1572872 | tf_op jit(solution)/shard_map/ppermute | solution.py:18
  68.3 14.1 %collective-permute-done.5 = bf16[512,128]{1,0:T(8,128)(2,1)S(1)} collective-permute-done((bf16[512,128]{1,0:T(8,128)(2,1)S(1)}, bf16[512,128]{1,0:T(8,128)(2,1)S(1)}, u32[]{:S(2)}, u32[]{:S(2)}) %collective-permute-start.5) | collective-permute-done | bytes 131104 | tf_op jit(solution)/shard_map/ppermute | solution.py:41
  86.9 2.4 %collective-permute-done.14 = bf16[512,128]{1,0:T(8,128)(2,1)S(1)} collective-permute-done((bf16[512,128]{1,0:T(8,128)(2,1)S(1)}, bf16[512,128]{1,0:T(8,128)(2,1)S(1)}, u32[]{:S(2)}, u32[]{:S(2)}) %collective-permute-start.14) | collective-permute-done | bytes 131104 | tf_op jit(solution)/shard_map/ppermute | solution.py:41
  90.2 1.8 fusion.9
  98.2 2.0 %collective-permute-start.15 = (bf16[512,128]{1,0:T(8,128)(2,1)S(1)}, bf16[512,128]{1,0:T(8,128)(2,1)S(1)}, u32[]{:S(2)}, u32[]{:S(2)}) collective-permute-start(bf16[512,128]{1,0:T(8,128)(2,1)S(1)} %get-tuple-element.30), channel_id=1, source_target_pairs={{0,4},{1,5},{2,6},{3,7},{16,20},{17,21},{18,22},{19,23}} | collective-permute-start | bytes 393224 | tf_op jit(solution)/shard_map/ppermute | solution.py:41
  101.6 1.9 %collective-permute-start.21 = (bf16[512,128]{1,0:T(8,128)(2,1)}, bf16[512,128]{1,0:T(8,128)(2,1)}, u32[]{:S(2)}, u32[]{:S(2)}) collective-permute-start(bf16[512,128]{1,0:T(8,128)(2,1)} %get-tuple-element.32), channel_id=1, source_target_pairs={{0,4},{1,5},{2,6},{3,7},{16,20},{17,21},{18,22},{19,23}} | collective-permute-start | bytes 393224 | tf_op jit(solution)/shard_map/ppermute | solution.py:41
  104.6 3.1 %collective-permute-start.24 = (bf16[512,128]{1,0:T(8,128)(2,1)}, bf16[512,128]{1,0:T(8,128)(2,1)S(1)}, u32[]{:S(2)}, u32[]{:S(2)}) collective-permute-start(bf16[512,128]{1,0:T(8,128)(2,1)} %get-tuple-element.31), channel_id=1, source_target_pairs={{0,4},{1,5},{2,6},{3,7},{16,20},{17,21},{18,22},{19,23}} | collective-permute-start | bytes 393224 | tf_op jit(solution)/shard_map/ppermute | solution.py:41
  115.8 9.8 %collective-permute-start.34 = (bf16[256,1024]{1,0:T(8,128)(2,1)}, bf16[256,1024]{1,0:T(8,128)(2,1)}, u32[]{:S(2)}, u32[]{:S(2)}) collective-permute-start(bf16[256,1024]{1,0:T(8,128)(2,1)} %collective-permute-done.32), channel_id=1, source_target_pairs={{0,4},{4,8},{8,12},{1,5},{5,9},{9,13},{2,6},{6,10},{10,14},{3,7},{... | collective-permute-start | bytes 1572872 | tf_op jit(solution)/shard_map/ppermute | solution.py:18
  134.4 2.0 %all_gather.21 = bf16[128,64]{0,1:T(8,128)(2,1)S(1)} all-gather(bf16[128,32]{0,1:T(8,128)(2,1)S(1)} %copy.85), channel_id=1, replica_groups=mesh['grp'=2,'seq'=4,'dp'=2,'head'=2] {'head'}, dimensions={1}, use_global_device_ids=true | all-gather | bytes 24576 | tf_op jit(solution)/shard_map/all_gather | solution.py:137
  137.4 3.7 %collective-permute-done.29 = bf16[128,320]{0,1:T(8,128)(2,1)S(1)} collective-permute-done((bf16[128,320]{0,1:T(8,128)(2,1)S(1)}, bf16[128,320]{0,1:T(8,128)(2,1)S(1)}, u32[]{:S(2)}, u32[]{:S(2)}) %collective-permute-start.29) | collective-permute-done | bytes 81952 | tf_op jit(solution)/shard_map/ppermute | solution.py:13
  141.2 4.5 %collective-permute-start.31 = (bf16[128,320]{0,1:T(8,128)(2,1)S(1)}, bf16[128,320]{0,1:T(8,128)(2,1)S(1)}, u32[]{:S(2)}, u32[]{:S(2)}) collective-permute-start(bf16[128,320]{0,1:T(8,128)(2,1)S(1)} %constant_dynamic-slice_fusion), channel_id=1, source_target_pairs={{0,4},{4,8},{8,12},{1,5},{5,9},{9,13},{2,6},{6,10},{10,14},{3,7},{... | collective-permute-start | bytes 245768 | tf_op jit(solution)/shard_map/ppermute | solution.py:18
  147.8 11.9 %collective-permute-start.33 = (bf16[128,320]{0,1:T(8,128)(2,1)S(1)}, bf16[128,320]{0,1:T(8,128)(2,1)S(1)}, u32[]{:S(2)}, u32[]{:S(2)}) collective-permute-start(bf16[128,320]{0,1:T(8,128)(2,1)S(1)} %collective-permute-done.31), channel_id=1, source_target_pairs={{0,4},{4,8},{8,12},{1,5},{5,9},{9,13},{2,6},{6,10},{10,14},{3,7},{... | collective-permute-start | bytes 245768 | tf_op jit(solution)/shard_map/ppermute | solution.py:18
  159.8 1.9 %all_gather.22 = bf16[256,320]{0,1:T(8,128)(2,1)S(1)} all-gather(bf16[128,320]{0,1:T(8,128)(2,1)S(1)} %collective-permute-done.31), channel_id=1, replica_groups=mesh['grp'=2,'seq'=4,'dp'=2,'head'=2] {'head'}, dimensions={0}, use_global_device_ids=true | all-gather | bytes 245760 | tf_op jit(solution)/shard_map/all_gather | solution.py:154
  161.7 1.9 %all_gather.25 = bf16[256,320]{0,1:T(8,128)(2,1)S(1)} all-gather(bf16[128,320]{0,1:T(8,128)(2,1)S(1)} %collective-permute-done.37), channel_id=1, replica_groups=mesh['grp'=2,'seq'=4,'dp'=2,'head'=2] {'head'}, dimensions={0}, use_global_device_ids=true | all-gather | bytes 245760 | tf_op jit(solution)/shard_map/all_gather | solution.py:154
  168.0 5.0 %collective-permute-start.35 = (bf16[128,320]{0,1:T(8,128)(2,1)S(1)}, bf16[128,320]{0,1:T(8,128)(2,1)S(1)}, u32[]{:S(2)}, u32[]{:S(2)}) collective-permute-start(bf16[128,320]{0,1:T(8,128)(2,1)S(1)} %collective-permute-done.33), channel_id=1, source_target_pairs={{0,4},{4,8},{8,12},{1,5},{5,9},{9,13},{2,6},{6,10},{10,14},{3,7},{... | collective-permute-start | bytes 245768 | tf_op jit(solution)/shard_map/ppermute | solution.py:18
  174.3 1.9 %all_gather.23 = bf16[256,320]{0,1:T(8,128)(2,1)S(1)} all-gather(bf16[128,320]{0,1:T(8,128)(2,1)S(1)} %collective-permute-done.33), channel_id=1, replica_groups=mesh['grp'=2,'seq'=4,'dp'=2,'head'=2] {'head'}, dimensions={0}, use_global_device_ids=true | all-gather | bytes 245760 | tf_op jit(solution)/shard_map/all_gather | solution.py:154
  177.6 1.9 %all_gather.26 = bf16[256,320]{0,1:T(8,128)(2,1)S(1)} all-gather(bf16[128,320]{0,1:T(8,128)(2,1)S(1)} %collective-permute-done.39), channel_id=1, replica_groups=mesh['grp'=2,'seq'=4,'dp'=2,'head'=2] {'head'}, dimensions={0}, use_global_device_ids=true | all-gather | bytes 245760 | tf_op jit(solution)/shard_map/all_gather | solution.py:154
  179.6 1.9 %all_gather.24 = bf16[256,320]{0,1:T(8,128)(2,1)S(1)} all-gather(bf16[128,320]{0,1:T(8,128)(2,1)S(1)} %collective-permute-done.35), channel_id=1, replica_groups=mesh['grp'=2,'seq'=4,'dp'=2,'head'=2] {'head'}, dimensions={0}, use_global_device_ids=true | all-gather | bytes 245760 | tf_op jit(solution)/shard_map/all_gather | solution.py:154
  181.5 1.9 %all_gather.27 = bf16[256,320]{0,1:T(8,128)(2,1)S(1)} all-gather(bf16[128,320]{0,1:T(8,128)(2,1)S(1)} %collective-permute-done.41), channel_id=1, replica_groups=mesh['grp'=2,'seq'=4,'dp'=2,'head'=2] {'head'}, dimensions={0}, use_global_device_ids=true | all-gather | bytes 245760 | tf_op jit(solution)/shard_map/all_gather | solution.py:154
  (292 shorter events, 82.7 us)
Async XLA Ops:
  1.8 9.3 %collective-permute-start = (bf16[128,1024]{1,0:T(8,128)(2,1)S(1)}, bf16[128,1024]{1,0:T(8,128)(2,1)S(1)}, u32[]{:S(2)}, u32[]{:S(2)}) collective-permute-start(bf16[128,1024]{1,0:T(8,128)(2,1)S(1)} %get-tuple-element.49), channel_id=1, source_target_pairs={{0,2},{2,0},{1,3},{3,1},{4,6},{6,4},{5,7},{7,5},{8,10},{10,8},{9,1... | collective-permute-start | bytes 786440 | tf_op jit(solution)/shard_map/ppermute | solution.py:13
  20.0 28.7 %collective-permute-start.30 = (bf16[256,1024]{1,0:T(8,128)(2,1)}, bf16[256,1024]{1,0:T(8,128)(2,1)}, u32[]{:S(2)}, u32[]{:S(2)}) collective-permute-start(bf16[256,1024]{1,0:T(8,128)(2,1)} %pad_maximum_fusion.3), channel_id=1, source_target_pairs={{0,4},{4,8},{8,12},{1,5},{5,9},{9,13},{2,6},{6,10},{10,14},{3,7},{... | collective-permute-start | bytes 1572872 | tf_op jit(solution)/shard_map/ppermute | solution.py:18
  24.2 38.4 %collective-permute-start.36 = (bf16[256,1024]{1,0:T(8,128)(2,1)}, bf16[256,1024]{1,0:T(8,128)(2,1)}, u32[]{:S(2)}, u32[]{:S(2)}) collective-permute-start(bf16[256,1024]{1,0:T(8,128)(2,1)} %pad_maximum_fusion.3), channel_id=1, source_target_pairs={{4,0},{8,4},{12,8},{5,1},{9,5},{13,9},{6,2},{10,6},{14,10},{7,3},{... | collective-permute-start | bytes 1572872 | tf_op jit(solution)/shard_map/ppermute | solution.py:18
  28.4 9.0 %collective-permute-start.3 = (bf16[512,128]{1,0:T(8,128)(2,1)}, bf16[512,128]{1,0:T(8,128)(2,1)}, u32[]{:S(2)}, u32[]{:S(2)}) collective-permute-start(bf16[512,128]{1,0:T(8,128)(2,1)} %get-tuple-element.41), channel_id=1, source_target_pairs={{12,8},{13,9},{14,10},{15,11},{28,24},{29,25},{30,26},{31,27}} | collective-permute-start | bytes 393224 | tf_op jit(solution)/shard_map/ppermute | solution.py:41
  29.9 10.5 %collective-permute-start.12 = (bf16[512,128]{1,0:T(8,128)(2,1)}, bf16[512,128]{1,0:T(8,128)(2,1)}, u32[]{:S(2)}, u32[]{:S(2)}) collective-permute-start(bf16[512,128]{1,0:T(8,128)(2,1)} %get-tuple-element.42), channel_id=1, source_target_pairs={{12,8},{13,9},{14,10},{15,11},{28,24},{29,25},{30,26},{31,27}} | collective-permute-start | bytes 393224 | tf_op jit(solution)/shard_map/ppermute | solution.py:41
  31.2 13.5 %collective-permute-start.6 = (bf16[512,128]{1,0:T(8,128)(2,1)}, bf16[512,128]{1,0:T(8,128)(2,1)}, u32[]{:S(2)}, u32[]{:S(2)}) collective-permute-start(bf16[512,128]{1,0:T(8,128)(2,1)} %get-tuple-element.44), channel_id=1, source_target_pairs={{12,8},{13,9},{14,10},{15,11},{28,24},{29,25},{30,26},{31,27}} | collective-permute-start | bytes 393224 | tf_op jit(solution)/shard_map/ppermute | solution.py:41
  46.1 17.8 %collective-permute-start.10 = (bf16[512,128]{1,0:T(8,128)(2,1)S(1)}, bf16[512,128]{1,0:T(8,128)(2,1)S(1)}, u32[]{:S(2)}, u32[]{:S(2)}) collective-permute-start(bf16[512,128]{1,0:T(8,128)(2,1)S(1)} %get-tuple-element.39), channel_id=1, source_target_pairs={{8,4},{9,5},{10,6},{11,7},{24,20},{25,21},{26,22},{27,23}} | collective-permute-start | bytes 393224 | tf_op jit(solution)/shard_map/ppermute | solution.py:41
  46.8 18.5 %collective-permute-start.13 = (bf16[512,128]{1,0:T(8,128)(2,1)S(1)}, bf16[512,128]{1,0:T(8,128)(2,1)S(1)}, u32[]{:S(2)}, u32[]{:S(2)}) collective-permute-start(bf16[512,128]{1,0:T(8,128)(2,1)S(1)} %get-tuple-element.40), channel_id=1, source_target_pairs={{8,4},{9,5},{10,6},{11,7},{24,20},{25,21},{26,22},{27,23}} | collective-permute-start | bytes 393224 | tf_op jit(solution)/shard_map/ppermute | solution.py:41
  47.5 17.8 %collective-permute-start.7 = (bf16[512,128]{1,0:T(8,128)(2,1)S(1)}, bf16[512,128]{1,0:T(8,128)(2,1)S(1)}, u32[]{:S(2)}, u32[]{:S(2)}) collective-permute-start(bf16[512,128]{1,0:T(8,128)(2,1)S(1)} %get-tuple-element.38), channel_id=1, source_target_pairs={{8,4},{9,5},{10,6},{11,7},{24,20},{25,21},{26,22},{27,23}} | collective-permute-start | bytes 393224 | tf_op jit(solution)/shard_map/ppermute | solution.py:41
  48.8 65.5 %collective-permute-start.32 = (bf16[256,1024]{1,0:T(8,128)(2,1)}, bf16[256,1024]{1,0:T(8,128)(2,1)}, u32[]{:S(2)}, u32[]{:S(2)}) collective-permute-start(bf16[256,1024]{1,0:T(8,128)(2,1)} %collective-permute-done.30), channel_id=1, source_target_pairs={{0,4},{4,8},{8,12},{1,5},{5,9},{9,13},{2,6},{6,10},{10,14},{3,7},{... | collective-permute-start | bytes 1572872 | tf_op jit(solution)/shard_map/ppermute | solution.py:18
  62.7 53.2 %collective-permute-start.38 = (bf16[256,1024]{1,0:T(8,128)(2,1)}, bf16[256,1024]{1,0:T(8,128)(2,1)}, u32[]{:S(2)}, u32[]{:S(2)}) collective-permute-start(bf16[256,1024]{1,0:T(8,128)(2,1)} %collective-permute-done.36), channel_id=1, source_target_pairs={{4,0},{8,4},{12,8},{5,1},{9,5},{13,9},{6,2},{10,6},{14,10},{7,3},{... | collective-permute-start | bytes 1572872 | tf_op jit(solution)/shard_map/ppermute | solution.py:18
  64.0 18.5 %collective-permute-start.5 = (bf16[512,128]{1,0:T(8,128)(2,1)S(1)}, bf16[512,128]{1,0:T(8,128)(2,1)S(1)}, u32[]{:S(2)}, u32[]{:S(2)}) collective-permute-start(bf16[512,128]{1,0:T(8,128)(2,1)S(1)} %get-tuple-element.37), channel_id=1, source_target_pairs={{4,0},{5,1},{6,2},{7,3},{20,16},{21,17},{22,18},{23,19}} | collective-permute-start | bytes 393224 | tf_op jit(solution)/shard_map/ppermute | solution.py:41
  65.6 19.1 %collective-permute-start.8 = (bf16[512,128]{1,0:T(8,128)(2,1)S(1)}, bf16[512,128]{1,0:T(8,128)(2,1)S(1)}, u32[]{:S(2)}, u32[]{:S(2)}) collective-permute-start(bf16[512,128]{1,0:T(8,128)(2,1)S(1)} %get-tuple-element.45), channel_id=1, source_target_pairs={{4,0},{5,1},{6,2},{7,3},{20,16},{21,17},{22,18},{23,19}} | collective-permute-start | bytes 393224 | tf_op jit(solution)/shard_map/ppermute | solution.py:41
  67.0 18.9 %collective-permute-start.11 = (bf16[512,128]{1,0:T(8,128)(2,1)S(1)}, bf16[512,128]{1,0:T(8,128)(2,1)S(1)}, u32[]{:S(2)}, u32[]{:S(2)}) collective-permute-start(bf16[512,128]{1,0:T(8,128)(2,1)S(1)} %get-tuple-element.46), channel_id=1, source_target_pairs={{4,0},{5,1},{6,2},{7,3},{20,16},{21,17},{22,18},{23,19}} | collective-permute-start | bytes 393224 | tf_op jit(solution)/shard_map/ppermute | solution.py:41
  111.9 13.8 %collective-permute-start.19 = (bf16[512,128]{1,0:T(8,128)(2,1)S(1)}, bf16[512,128]{1,0:T(8,128)(2,1)S(1)}, u32[]{:S(2)}, u32[]{:S(2)}) collective-permute-start(bf16[512,128]{1,0:T(8,128)(2,1)S(1)} %get-tuple-element.27), channel_id=1, source_target_pairs={{4,8},{5,9},{6,10},{7,11},{20,24},{21,25},{22,26},{23,27}} | collective-permute-start | bytes 393224 | tf_op jit(solution)/shard_map/ppermute | solution.py:41
  112.7 14.2 %collective-permute-start.22 = (bf16[512,128]{1,0:T(8,128)(2,1)S(1)}, bf16[512,128]{1,0:T(8,128)(2,1)S(1)}, u32[]{:S(2)}, u32[]{:S(2)}) collective-permute-start(bf16[512,128]{1,0:T(8,128)(2,1)S(1)} %get-tuple-element.28), channel_id=1, source_target_pairs={{4,8},{5,9},{6,10},{7,11},{20,24},{21,25},{22,26},{23,27}} | collective-permute-start | bytes 393224 | tf_op jit(solution)/shard_map/ppermute | solution.py:41
  113.4 14.2 %collective-permute-start.25 = (bf16[512,128]{1,0:T(8,128)(2,1)S(1)}, bf16[512,128]{1,0:T(8,128)(2,1)S(1)}, u32[]{:S(2)}, u32[]{:S(2)}) collective-permute-start(bf16[512,128]{1,0:T(8,128)(2,1)S(1)} %get-tuple-element.29), channel_id=1, source_target_pairs={{4,8},{5,9},{6,10},{7,11},{20,24},{21,25},{22,26},{23,27}} | collective-permute-start | bytes 393224 | tf_op jit(solution)/shard_map/ppermute | solution.py:41
  114.3 32.8 %collective-permute-start.28 = (bf16[1024,320]{0,1:T(8,128)(2,1)}, bf16[1024,320]{0,1:T(8,128)(2,1)S(1)}, u32[]{:S(2)}, u32[]{:S(2)}) collective-permute-start(bf16[1024,320]{0,1:T(8,128)(2,1)} %pad_maximum_fusion), channel_id=1, source_target_pairs={{0,2},{2,0},{1,3},{3,1},{4,6},{6,4},{5,7},{7,5},{8,10},{10,8},{9,1... | collective-permute-start | bytes 1966088 | tf_op jit(solution)/shard_map/ppermute | solution.py:13
  115.8 67.6 %collective-permute-start.34 = (bf16[256,1024]{1,0:T(8,128)(2,1)}, bf16[256,1024]{1,0:T(8,128)(2,1)}, u32[]{:S(2)}, u32[]{:S(2)}) collective-permute-start(bf16[256,1024]{1,0:T(8,128)(2,1)} %collective-permute-done.32), channel_id=1, source_target_pairs={{0,4},{4,8},{8,12},{1,5},{5,9},{9,13},{2,6},{6,10},{10,14},{3,7},{... | collective-permute-start | bytes 1572872 | tf_op jit(solution)/shard_map/ppermute | solution.py:18
  125.6 60.6 %collective-permute-start.40 = (bf16[256,1024]{1,0:T(8,128)(2,1)}, bf16[256,1024]{1,0:T(8,128)(2,1)}, u32[]{:S(2)}, u32[]{:S(2)}) collective-permute-start(bf16[256,1024]{1,0:T(8,128)(2,1)} %collective-permute-done.38), channel_id=1, source_target_pairs={{4,0},{8,4},{12,8},{5,1},{9,5},{13,9},{6,2},{10,6},{14,10},{7,3},{... | collective-permute-start | bytes 1572872 | tf_op jit(solution)/shard_map/ppermute | solution.py:18
  145.8 15.9 %collective-permute-start.37 = (bf16[128,320]{0,1:T(8,128)(2,1)S(1)}, bf16[128,320]{0,1:T(8,128)(2,1)S(1)}, u32[]{:S(2)}, u32[]{:S(2)}) collective-permute-start(bf16[128,320]{0,1:T(8,128)(2,1)S(1)} %constant_dynamic-slice_fusion), channel_id=1, source_target_pairs={{4,0},{8,4},{12,8},{5,1},{9,5},{13,9},{6,2},{10,6},{14,10},{7,3},{... | collective-permute-start | bytes 245768 | tf_op jit(solution)/shard_map/ppermute | solution.py:18
  147.8 20.2 %collective-permute-start.33 = (bf16[128,320]{0,1:T(8,128)(2,1)S(1)}, bf16[128,320]{0,1:T(8,128)(2,1)S(1)}, u32[]{:S(2)}, u32[]{:S(2)}) collective-permute-start(bf16[128,320]{0,1:T(8,128)(2,1)S(1)} %collective-permute-done.31), channel_id=1, source_target_pairs={{0,4},{4,8},{8,12},{1,5},{5,9},{9,13},{2,6},{6,10},{10,14},{3,7},{... | collective-permute-start | bytes 245768 | tf_op jit(solution)/shard_map/ppermute | solution.py:18
  163.6 9.4 %collective-permute-start.39 = (bf16[128,320]{0,1:T(8,128)(2,1)S(1)}, bf16[128,320]{0,1:T(8,128)(2,1)S(1)}, u32[]{:S(2)}, u32[]{:S(2)}) collective-permute-start(bf16[128,320]{0,1:T(8,128)(2,1)S(1)} %collective-permute-done.37), channel_id=1, source_target_pairs={{4,0},{8,4},{12,8},{5,1},{9,5},{13,9},{6,2},{10,6},{14,10},{7,3},{... | collective-permute-start | bytes 245768 | tf_op jit(solution)/shard_map/ppermute | solution.py:18
  168.0 11.5 %collective-permute-start.35 = (bf16[128,320]{0,1:T(8,128)(2,1)S(1)}, bf16[128,320]{0,1:T(8,128)(2,1)S(1)}, u32[]{:S(2)}, u32[]{:S(2)}) collective-permute-start(bf16[128,320]{0,1:T(8,128)(2,1)S(1)} %collective-permute-done.33), channel_id=1, source_target_pairs={{0,4},{4,8},{8,12},{1,5},{5,9},{9,13},{2,6},{6,10},{10,14},{3,7},{... | collective-permute-start | bytes 245768 | tf_op jit(solution)/shard_map/ppermute | solution.py:18
  (81 other events, 495.0 us)

commit v2 on v0

v2 whole, which is shorter than its diff:
```python
import functools

import jax
import jax.numpy as jnp
from jax import lax
from jax.experimental import pallas as pl
from jax.experimental.pallas import tpu as pltpu
from jax.sharding import PartitionSpec as P

CHUNKS = 4
PARTS = 4
BF = jnp.bfloat16
F32 = jnp.float32
TOP = lax.Precision.HIGHEST
LIMIT = 56 * 1024 * 1024


def cyclic(a, axis, by):
    count = lax.axis_size(axis)
    return lax.ppermute(a, axis, [(i, (i + by) % count) for i in range(count)])


def mm(a, b, ca, cb, precision=None):
    return lax.dot_general(
        a, b, (((ca,), (cb,)), ((), ())), preferred_element_type=F32, precision=precision
    )


def halves(a):
    high = a.astype(BF)
    return high, (a - high.astype(F32)).astype(BF)


def head_lanes(heads, width, size, first=0):
    row = lax.broadcasted_iota(jnp.int32, (heads, width), 0)
    col = lax.broadcasted_iota(jnp.int32, (heads, width), 1) + first
    low = row * size
    return jnp.where((col >= low) & (col < low + size), 1.0, 0.0).astype(F32)


def spread(a, pick):
    high, low = halves(a)
    both = jnp.concatenate([pick, pick], axis=0)
    return mm(jnp.concatenate([high, low], axis=0), both, 0, 0)


def call(kernel, out_shape, flops, *args, scratch=()):
    size = sum(a.size * a.dtype.itemsize for a in args)
    return pl.pallas_call(
        kernel,
        out_shape=out_shape,
        in_specs=[pl.BlockSpec(memory_space=pltpu.VMEM)] * len(args),
        out_specs=jax.tree.map(lambda _: pl.BlockSpec(memory_space=pltpu.VMEM), out_shape),
        scratch_shapes=list(scratch),
        compiler_params=pltpu.CompilerParams(vmem_limit_bytes=LIMIT),
        cost_estimate=pl.CostEstimate(flops=flops, bytes_accessed=size, transcendentals=0),
    )(*args)


def struct(shape, dtype):
    return jax.ShapeDtypeStruct(shape, dtype)


def project_kernel(a_ref, bc_ref, dt_ref, out_ref):
    a = a_ref[...]
    state_n = bc_ref.shape[1] // 2
    rows = a.shape[0]
    bc = mm(a, bc_ref[...], 1, 0)
    out_ref[0:rows, :] = bc[:, :state_n]
    out_ref[rows : 2 * rows, :] = bc[:, state_n:]
    out_ref[2 * rows :, :] = mm(a, dt_ref[...], 1, 0).T


def project(a, w_bc, w_dt):
    rows = a.shape[0]
    total = 2 * rows + w_dt.shape[1]
    return call(
        project_kernel,
        struct((total, w_bc.shape[1] // 2), F32),
        2 * a.size * (w_bc.shape[1] + w_dt.shape[1]),
        a,
        w_bc,
        w_dt,
    )


def state_kernel(count, size, *refs):
    proj = refs[:count]
    x_ref, g_ref, rate_ref, bias_ref, own_ref, decay_ref, bc_ref, hp_ref = refs[count:]
    heads = rate_ref.shape[0]
    rows = x_ref.shape[0]
    chunks, step = own_ref.shape[1], own_ref.shape[3]
    first = pl.multiple_of(2 * rows + lax.axis_index("head") * heads, 8)
    bc = proj[0][0 : 2 * rows, :]
    pre = proj[0][pl.ds(first, heads), :] + bias_ref[...]
    for ref in proj[1:]:
        bc = bc + ref[0 : 2 * rows, :]
        pre = pre + ref[pl.ds(first, heads), :]
    bc_ref[...] = bc
    dt = jnp.maximum(pre, 0.0) + jnp.log1p(jnp.exp(-jnp.abs(pre)))
    row = lax.broadcasted_iota(jnp.int32, (rows, rows), 0)
    col = lax.broadcasted_iota(jnp.int32, (rows, rows), 1)
    cum = mm(-dt * rate_ref[...], jnp.where(row <= col, 1.0, 0.0), 1, 0, TOP)
    last = cum[:, rows - 1 : rows]
    grow = jnp.exp(cum)
    w = jnp.exp(last - cum) * dt
    decay = jnp.exp(last)
    for k, part in enumerate((pre, dt, cum, grow, w)):
        hp_ref[k * heads : (k + 1) * heads, :] = part
    way = lax.rem(lax.axis_index("seq"), 2)
    kinds = ((w, x_ref, bc[:rows], way), (grow, g_ref, bc[rows:], 1 - way))
    for scale, ref, vec, place in kinds:
        high, low = halves(vec.T)
        wide = jnp.concatenate([high, low], axis=1)
        for k in range(chunks):
            pick = head_lanes(heads, step, size, k * step)
            if place is way:
                decay_ref[k] = jnp.sum(pick * decay, axis=0, keepdims=True)
            value = spread(scale, pick.astype(BF)) * ref[:, k * step : (k + 1) * step].astype(F32)
            top, rest = halves(value)
            own_ref[place, k] = mm(wide, jnp.concatenate([top, top], axis=0), 1, 0) + mm(
                high, rest, 1, 0
            )


def inner_kernel(first, pairs, size, bc_ref, hp_ref, x_ref, g_ref, gx_ref, ds_ref, sums_ref, gy_ref, xg_ref):
    rows = x_ref.shape[0]
    heads = hp_ref.shape[0] // 5
    lanes = 2 * size
    width = pairs * lanes
    b, c = bc_ref[0:rows, :], bc_ref[rows : 2 * rows, :]
    scores = mm(c, b, 1, 1, TOP)
    row = lax.broadcasted_iota(jnp.int32, (rows, rows), 0)
    col = lax.broadcasted_iota(jnp.int32, (rows, rows), 1)
    causal = row >= col
    dt = hp_ref[heads : 2 * heads, :]
    cum = hp_ref[2 * heads : 3 * heads, :]
    cum_t = cum.T
    lane = lax.broadcasted_iota(jnp.int32, (rows, lanes), 1)
    sides = [jnp.where(lane < size, 1.0, 0.0).astype(BF), jnp.where(lane < size, 0.0, 1.0).astype(BF)]
    ds = jnp.zeros((rows, rows), F32)
    for j in range(pairs):
        place = slice(j * lanes, (j + 1) * lanes)
        here = slice((first + j) * lanes, (first + j + 1) * lanes)
        x, g = x_ref[:, here], g_ref[:, here]
        xs = jnp.concatenate([x * s for s in sides], axis=0)
        gs = jnp.concatenate([g * s for s in sides], axis=0)
        m = mm(gs, x, 1, 1)
        kern = []
        for i in range(2):
            h = 2 * (first + j) + i
            gap = cum_t[:, h : h + 1] - cum[h : h + 1, :]
            fall = jnp.exp(jnp.where(causal, gap, -jnp.inf)) * dt[h : h + 1, :]
            kern.append((fall * scores).astype(BF))
            ds = ds + fall * m[i * rows : (i + 1) * rows]
        y = mm(jnp.concatenate(kern, axis=1), xs, 1, 0)
        gx = mm(jnp.concatenate(kern, axis=0), gs, 0, 0)
        gx_ref[:, place] = gx
        after = slice(width + j * lanes, width + (j + 1) * lanes)
        gy_ref[:, place], gy_ref[:, after] = halves(g.astype(F32) * y)
        xg_ref[:, place], xg_ref[:, after] = halves(x.astype(F32) * gx)
    ds_ref[...] = ds
    pick = head_lanes(2 * pairs, width, size).astype(BF)
    pick = jnp.concatenate([pick, pick], axis=1)
    sums_ref[0] = mm(pick, gy_ref[...], 1, 1)
    sums_ref[1] = mm(pick, xg_ref[...], 1, 1)


def outer_kernel(size, parts, *refs):
    in_ref, out_ref, x_ref, g_ref, bc_ref, hp_ref, decay_ref, rate_ref = refs[:8]
    gxs, dss, sums = (refs[8 + k * parts : 8 + (k + 1) * parts] for k in range(3))
    grad_ref, back_ref, wv_ref, eu_ref, io_ref = refs[8 + 3 * parts :]
    rows, width = x_ref.shape
    heads = rate_ref.shape[0]
    chunks, step = decay_ref.shape[0], decay_ref.shape[2]
    piece = width // parts
    b, c = bc_ref[0:rows, :], bc_ref[rows : 2 * rows, :]
    pre, dt, cum, grow, w = (hp_ref[k * heads : (k + 1) * heads, :] for k in range(5))
    ds = dss[0][...]
    for ref in dss[1:]:
        ds = ds + ref[...]
    db = mm(c, ds, 0, 0, TOP)
    dc = mm(b, ds, 0, 1, TOP)
    b_wide = jnp.concatenate(halves(b), axis=1)
    c_wide = jnp.concatenate(halves(c), axis=1)
    for k in range(chunks):
        place = slice(k * step, (k + 1) * step)
        after = slice(width + k * step, width + (k + 1) * step)
        pick = head_lanes(heads, step, size, k * step).astype(BF)
        incoming, outgoing = in_ref[k], out_ref[k]
        u = mm(c_wide, jnp.concatenate([incoming, incoming], axis=0), 1, 0)
        v = mm(b_wide, jnp.concatenate([outgoing, outgoing], axis=0), 1, 0)
        scale = spread(w, pick)
        wx = scale * x_ref[:, place].astype(F32)
        eg = spread(grow, pick) * g_ref[:, place].astype(F32)
        for q in range(step // piece) if step >= piece else (0,):
            if step >= piece:
                at = k * step + q * piece
                inner = slice(q * piece, (q + 1) * piece)
                term = gxs[at // piece][...]
            else:
                at, inner = k * step, slice(0, step)
                term = gxs[at // piece][:, at % piece : at % piece + step]
            total = term + scale[:, inner] * v[:, inner]
            grad_ref[:, at : at + total.shape[1]] = total.astype(BF)
        wv_ref[:, place], wv_ref[:, after] = halves(wx * v)
        eu_ref[:, place], eu_ref[:, after] = halves(eg * u)
        db = db + mm(
            jnp.concatenate([outgoing, outgoing], axis=1), jnp.concatenate(halves(wx), axis=1), 1, 1
        )
        dc = dc + mm(
            jnp.concatenate([incoming, incoming], axis=1), jnp.concatenate(halves(eg), axis=1), 1, 1
        )
        io_ref[:, place] = jnp.sum(incoming.astype(F32) * outgoing.astype(F32), axis=0, keepdims=True)
    pick = head_lanes(heads, width, size)
    ddecay = jnp.sum(pick * io_ref[...], axis=1, keepdims=True)
    pick = pick.astype(BF)
    pick = jnp.concatenate([pick, pick], axis=1)
    wdw = mm(pick, wv_ref[...], 1, 1)
    egu = mm(pick, eu_ref[...], 1, 1)
    rowsum = jnp.concatenate([s[0] for s in sums], axis=0)
    colsum = jnp.concatenate([s[1] for s in sums], axis=0)
    dcum = rowsum - colsum + egu - wdw
    row = lax.broadcasted_iota(jnp.int32, (rows, rows), 0)
    col = lax.broadcasted_iota(jnp.int32, (rows, rows), 1)
    rev = mm(dcum, jnp.where(row >= col, 1.0, 0.0), 1, 0, TOP)
    decay = grow[:, rows - 1 : rows]
    rev = rev + jnp.sum(wdw, axis=1, keepdims=True) + decay * ddecay
    gate = 1.0 / (1.0 + jnp.exp(-pre))
    small = 1e-30
    ratio = jnp.where(dt > small, gate / jnp.maximum(dt, small), 1.0)
    back_ref[0:rows, :] = db
    back_ref[rows : 2 * rows, :] = dc
    back_ref[2 * rows :, :] = (colsum + wdw) * ratio - rate_ref[...] * rev * gate


def low_kernel(count, heads, *refs):
    out_ref = refs[count]
    top = refs[0].shape[0] - heads
    me = lax.axis_index("head")
    total = refs[0][0:top, :]
    for ref in refs[1:count]:
        total = total + ref[0:top, :]
    out_ref[0:top, :] = total.astype(BF)
    for r in range(count):
        at = pl.multiple_of(top + lax.rem(me - r + count, count) * heads, 16)
        out_ref[pl.ds(at, heads), :] = refs[r][top:, :].astype(BF)


def token_kernel(count, low_ref, *refs):
    out_ref = refs[2 * count]
    me = lax.axis_index("dp")
    low = low_ref[...]
    cols = refs[0].shape[1]
    part = refs[0].shape[0]
    for r in range(count):
        at = pl.multiple_of(lax.rem(me - r + count, count) * part, 128)
        term = mm(low[:cols], refs[2 * r][...], 0, 1) + mm(low[cols:], refs[2 * r + 1][...], 0, 1)
        out_ref[:, pl.ds(at, part)] = term.astype(BF)


def weight_kernel(scale, count, low_ref, *refs):
    toks, bc_ref, dt_ref = refs[:count], refs[count], refs[count + 1]
    seqs, rows, part = toks[0].shape
    cols = bc_ref.shape[1]
    total = jnp.zeros((low_ref.shape[2], part), F32)
    me = lax.axis_index("seq")
    for r in range(count):
        for s in range(seqs):
            at = lax.rem(me - s + seqs, seqs)
            total = total + mm(low_ref[r, s], toks[r][at], 1, 0)
    total = total * scale
    bc_ref[...] = total[:cols].T
    dt_ref[...] = total[cols:].T


def chains(own, decay):
    count = lax.axis_size("seq")
    place = lax.axis_index("seq")
    chunks = own.shape[1]
    even = lax.rem(place, 2) == 0
    links = [
        [(i, i + 1) for i in range(0, count - 1, 2)],
        [(i, i + 1) for i in range(1, count - 1, 2)],
    ]
    pairs = []
    for group in links:
        to = {i: i for i in range(count)}
        for i, j in group:
            to[i], to[j] = j, i
        pairs.append(sorted(to.items()))
    shape = (chunks + 1,) + own.shape[2:]
    stores = [jnp.zeros(shape, BF), jnp.zeros(shape, BF)]
    got = [None, None]
    ends = (place == 0) | (place == count - 1)
    for slot in range(1, count + chunks - 1):
        fresh = [None, None]
        for kind in (0, 1):
            used = any(
                0 <= slot - hop < chunks
                for i, j in links[kind]
                for hop in (j, count - j)
            )
            if not used:
                continue
            goes_up = even if kind == 0 else ~even
            chunk = jnp.clip(jnp.where(goes_up, slot - place - 1, slot - count + place), 0, chunks - 1)
            value = lax.dynamic_index_in_dim(own[kind], chunk, 0, False)
            before = got[1 - kind]
            if before is not None:
                kept = before.astype(F32) * lax.dynamic_index_in_dim(decay, chunk, 0, False)
                value = value + (jnp.where(ends, 0.0, kept) if kind == 0 else kept)
            fresh[kind] = lax.ppermute(value.astype(BF), "seq", pairs[kind])
        got = fresh
        for kind in (0, 1):
            if got[kind] is None:
                continue
            below = ~even if kind == 0 else even
            chunk = jnp.where(below, slot - place, slot - count + place + 1)
            chunk = jnp.where((chunk >= 0) & (chunk < chunks), chunk, chunks)
            stores[kind] = lax.dynamic_update_index_in_dim(stores[kind], got[kind], chunk, 0)
    first, second = stores
    incoming = jnp.where(even, second, first)
    outgoing = jnp.where(even, first, second)
    incoming = jnp.where(place == 0, jnp.zeros_like(incoming), incoming)
    outgoing = jnp.where(place == count - 1, jnp.zeros_like(outgoing), outgoing)
    return incoming, outgoing


def body(tokens, ssd_input, grad_out, w_bc, w_dt, decay_rate, dt_bias):
    feats, x, g = tokens[0], ssd_input[0], grad_out[0]
    rows, width = feats.shape
    heads = decay_rate.shape[0]
    size = width // heads
    n_dp, n_seq, n_head = (lax.axis_size(a) for a in ("dp", "seq", "head"))
    d = lax.axis_index("dp")
    part = width // n_dp
    state_n = w_bc.shape[1] // 2
    rate, bias = decay_rate[:, None], dt_bias[:, None]

    def piece(r):
        return lax.dynamic_slice_in_dim(feats, ((d + r) % n_dp) * part, part, 1)

    items = [piece(0)] + [cyclic(piece(r), "dp", r) for r in range(1, n_dp)]
    toks = [lax.all_gather(a, "seq") for a in items]

    total = project(items[0], w_bc, w_dt)
    for r in range(1, n_dp):
        total = total + cyclic(project(items[r], w_bc, w_dt), "dp", -r)
    proj = [total] + [cyclic(total, "head", r) for r in range(1, n_head)]
    step = width // CHUNKS
    own, decay, bc, hp = call(
        functools.partial(state_kernel, n_head, size),
        (
            struct((2, CHUNKS, state_n, step), F32),
            struct((CHUNKS, 1, step), F32),
            struct((2 * rows, state_n), F32),
            struct((5 * heads, rows), F32),
        ),
        12 * rows * width * state_n,
        *proj,
        x,
        g,
        rate,
        bias,
    )
    incoming, outgoing = chains(own, decay)
    pairs = width // (2 * size) // PARTS
    span = width // PARTS
    inner = [
        call(
            functools.partial(inner_kernel, q * pairs, pairs, size),
            (
                struct((rows, span), F32),
                struct((rows, rows), F32),
                struct((2, 2 * pairs, rows), F32),
            ),
            8 * rows * rows * span,
            bc,
            hp,
            x,
            g,
            scratch=(pltpu.VMEM((rows, 2 * span), BF), pltpu.VMEM((rows, 2 * span), BF)),
        )
        for q in range(PARTS)
    ]
    grad_x, back = call(
        functools.partial(outer_kernel, size, PARTS),
        (struct((rows, width), BF), struct((2 * rows + heads, rows), F32)),
        16 * rows * width * state_n,
        incoming,
        outgoing,
        x,
        g,
        bc,
        hp,
        decay,
        rate,
        *[a[0] for a in inner],
        *[a[1] for a in inner],
        *[a[2] for a in inner],
        scratch=(
            pltpu.VMEM((rows, 2 * width), BF),
            pltpu.VMEM((rows, 2 * width), BF),
            pltpu.VMEM((1, width), F32),
        ),
    )
    backs = [back] + [cyclic(back, "head", r) for r in range(1, n_head)]
    low = call(
        functools.partial(low_kernel, n_head, heads),
        struct((2 * rows + n_head * heads, rows), BF),
        0,
        *backs,
    )
    weights = [(w_bc, w_dt)] + [
        (cyclic(w_bc, "dp", r), cyclic(w_dt, "dp", r)) for r in range(1, n_dp)
    ]
    grads = call(
        functools.partial(token_kernel, n_dp),
        struct((rows, width), BF),
        2 * rows * width * low.shape[0],
        low,
        *[a for pair in weights for a in pair],
    )
    share = low.shape[0] // n_head
    c = lax.axis_index("head")
    mine = lax.dynamic_slice_in_dim(low, c * share, share, 0)
    rest = []
    for r in range(n_dp):
        for s in range(n_seq):
            if r == 0 and s == 0:
                rest.append(mine)
                continue
            pairs_to = [
                (j * n_dp + i, (j + s) % n_seq * n_dp + (i + r) % n_dp)
                for i in range(n_dp)
                for j in range(n_seq)
            ]
            rest.append(lax.ppermute(mine, ("seq", "dp"), pairs_to))
    lows = jnp.stack(rest).reshape(n_dp, n_seq, share, rows)
    lows = lax.all_gather(lows, "head", axis=2, tiled=True)
    grad_bc, grad_dt = call(
        functools.partial(weight_kernel, 1.0 / (rows * n_seq * n_dp), n_dp),
        (struct((part, 2 * state_n), F32), struct((part, n_head * heads), F32)),
        2 * n_dp * n_seq * rows * part * low.shape[0],
        lows,
        *toks,
    )
    return grad_x[None], grads[None], grad_bc, grad_dt


def solution(mesh):
    in_specs = (
        P(("grp", "dp"), "seq", "head"),
        P(("grp", "dp"), "seq", "head"),
        P(("grp", "dp"), "seq", "head"),
        P(("head", "dp"), None),
        P(("head", "dp"), None),
        P("head"),
        P("head"),
    )
    out_specs = (
        P(("grp", "dp"), "seq", "head"),
        P(("grp", "dp"), "seq", "head"),
        P(("grp", "head", "dp"), None),
        P(("grp", "head", "dp"), None),
    )
    return jax.shard_map(body, mesh=mesh, in_specs=in_specs, out_specs=out_specs, check_vma=False)
```

time: 366 us -> 150 us (0.41)
  waiting for transfers between devices: 291 us -> 39.1 us
  starting transfers between devices: 0.25 us -> 42.9 us
  Pallas kernels: 0 us -> 36 us
  matrix products: 23.8 us -> 0 us
  blocking collectives: 14.9 us -> 2.4 us
  other arithmetic: 12.4 us -> 2.47 us
  local copies, waits for them, and re-layouts: 8.12 us -> 11.9 us
    all_gather x3 -> x2, waiting for transfers between devices: 174 us -> 12.1 us  [body(): toks = [lax.all_gather(a, 'seq') for a in items]]
    psum x2 -> x0, waiting for transfers between devices: 74.8 us -> none  [the longest x1 56.9 us: body(): summed = lax.psum(panel_term, 'seq')]
    ppermute x0 -> x23, starting transfers between devices: none -> 42.8 us  [the longest x10 23.7 us: chains(): fresh[kind] = lax.ppermute(value.astype(BF), 'seq', pairs[kind])]
    reduce_scatter x1 -> x0, waiting for transfers between devices: 42.6 us -> none  [body(): reduced = lax.psum_scatter(summed, 'dp', scatter_dimension=0, tiled=True)]
    pallas_call x0 -> x11, Pallas kernels: none -> 36 us  [call(): pl.pallas_call(kernel, out_shape=out_shape, in_specs=[pl.BlockSpec(memory...]
    ppermute x0 -> x23, waiting for transfers between devices: none -> 27.1 us  [the longest x10 16.7 us: chains(): fresh[kind] = lax.ppermute(value.astype(BF), 'seq', pairs[kind])]
    dot_general x14 -> x0, matrix products: 23.8 us -> none  [the longest x3 5.77 us: block_state(): jnp.einsum('sh,shp,sn->hpn', weights, per_head, input_vec, precision=lax....]
    all_gather x1, blocking collectives: 11.1 us -> 2.4 us  [body(): lows = lax.all_gather(lows, 'head', axis=2, tiled=True)]
  transfers between devices with their start and end apart: 6 -> 25, of which waited for: 6 -> 11; matrix products, arithmetic and copies ran while one was open for 3% -> 5% of each run, Pallas kernels for 0% -> 20%
where the time goes in v2:
time: 150 us; the launch traced here: 149 us
  starting transfers between devices  42.9 us (29%)
  waiting for transfers between devices  39.1 us (26%)
  Pallas kernels  36 us (24%)
  between operations  14.4 us (10%)
  local copies, waits for them, and re-layouts  11.9 us (8%)
  other arithmetic  2.47 us (2%)
  blocking collectives  2.4 us (2%)
    pallas_call x11, Pallas kernels, call(): pl.pallas_call(kernel, out_shape=out_shape, in_specs=[pl.BlockSpec(memory...  36 us
    ppermute x10, starting transfers between devices, chains(): fresh[kind] = lax.ppermute(value.astype(BF), 'seq', pairs[kind])  23.7 us
    ppermute x10, waiting for transfers between devices, chains(): fresh[kind] = lax.ppermute(value.astype(BF), 'seq', pairs[kind])  16.7 us
    all_gather x2, waiting for transfers between devices, body(): toks = [lax.all_gather(a, 'seq') for a in items]  12.1 us
    ppermute x7, starting transfers between devices, body(): rest.append(lax.ppermute(mine, ('seq', 'dp'), pairs_to))  11.3 us
    ppermute x6, starting transfers between devices, cyclic(): return lax.ppermute(a, axis, [(i, (i + by) % count) for i in range(count)])  7.92 us
    unnamed x31, local copies, waits for them, and re-layouts  6.57 us
    ppermute x6, waiting for transfers between devices, cyclic(): return lax.ppermute(a, axis, [(i, (i + by) % count) for i in range(count)])  6.38 us
  transfers between devices with their start and end apart: 25, of which 11 were waited for; matrix products, arithmetic and copies ran while one was open for 5% of the time, Pallas kernels for 20%

profile of v2, /device:TPU:0, one launch (start us, length us, event | category | flops | bytes accessed | tf_op | source)
XLA Modules:
  0.0 149.1 jit_solution(2651529568761788725)
XLA Ops:
  9.1 2.9 %collective-permute-start = (bf16[128,1024]{1,0:T(8,128)(2,1)S(1)}, bf16[128,1024]{1,0:T(8,128)(2,1)S(1)}, u32[]{:S(2)}, u32[]{:S(2)}) collective-permute-start(bf16[128,1024]{1,0:T(8,128)(2,1)S(1)} %get-tuple-element.68), channel_id=1, source_target_pairs={{0,2},{2,0},{1,3},{3,1},{4,6},{6,4},{5,7},{7,5},{8,10},{10,8},{9,1... | collective-permute-start | bytes 786440 | tf_op jit(solution)/shard_map/ppermute | solution.py:20
  13.8 4.6 %collective-permute-done.a_ref = bf16[128,1024]{1,0:T(8,128)(2,1)S(1)} collective-permute-done((bf16[128,1024]{1,0:T(8,128)(2,1)S(1)}, bf16[128,1024]{1,0:T(8,128)(2,1)S(1)}, u32[]{:S(2)}, u32[]{:S(2)}) %collective-permute-start) | collective-permute-done | bytes 262176 | tf_op jit(solution)/shard_map/ppermute | solution.py:20
  19.0 2.2 %shard_map.103 = f32[320,128]{1,0:T(8,128)} custom-call(bf16[128,1024]{1,0:T(8,128)(2,1)} %copy-done.2, bf16[1024,256]{1,0:T(8,128)(2,1)} %refs_0_.1, bf16[1024,64]{1,0:T(8,128)(2,1)} %copy.19.dt_ref.refs_1_), custom_call_target="tpu_custom_call" | custom-call | flops 83886080 | bytes 917504 | tf_op jit(solution)/shard_map/pallas_call | solution.py:49
  23.0 2.2 %shard_map.102 = f32[320,128]{1,0:T(8,128)} custom-call(bf16[128,1024]{1,0:T(8,128)(2,1)} %bitcast.103, bf16[1024,256]{1,0:T(8,128)(2,1)} %refs_0_.1, bf16[1024,64]{1,0:T(8,128)(2,1)} %copy.19.dt_ref.refs_1_), custom_call_target="tpu_custom_call" | custom-call | flops 83886080 | bytes 917504 | tf_op jit(solution)/shard_map/pallas_call | solution.py:49
  31.7 5.0 %shard_map.104 = (f32[2,4,128,512]{3,2,1,0:T(8,128)}, f32[4,1,512]{2,1,0:T(1,128)}, f32[256,128]{1,0:T(8,128)}, f32[160,128]{1,0:T(8,128)}) custom-call(f32[320,128]{1,0:T(8,128)} %copy-done.5, f32[320,128]{1,0:T(8,128)} %copy-done.10, bf16[128,2048]{1,0:T(8,128)(2,1)} %bitcast.91, bf16[128,2048]{1,0:T(8,128)(2,1)} %bitcast.97, ...), custom_call_target="tpu_custom_call" | custom-call | flops 402653184 | bytes 1376512 | tf_op jit(solution)/shard_map/pallas_call | solution.py:49
  40.7 3.0 %shard_map.105 = (f32[128,512]{1,0:T(8,128)}, f32[128,128]{1,0:T(8,128)}, f32[2,8,128]{2,1,0:T(8,128)}) custom-call(f32[256,128]{1,0:T(8,128)} %get-tuple-element.26.bc_ref.refs_4_, f32[160,128]{1,0:T(8,128)} %get-tuple-element.27.hp_ref.refs_5_, bf16[128,2048]{1,0:T(8,128)(2,1)} %bitcast.92, bf16[128,2048]{1,0:T(8,128)(2,1)} %bitcast.98), custom_call_target="tpu_custom_call" | custom-call | flops 67108864 | bytes 1261568 | tf_op jit(solution)/shard_map/pallas_call | solution.py:49
  43.6 3.0 %shard_map.106 = (f32[128,512]{1,0:T(8,128)}, f32[128,128]{1,0:T(8,128)}, f32[2,8,128]{2,1,0:T(8,128)}) custom-call(f32[256,128]{1,0:T(8,128)} %get-tuple-element.26.bc_ref.refs_4_, f32[160,128]{1,0:T(8,128)} %get-tuple-element.27.hp_ref.refs_5_, bf16[128,2048]{1,0:T(8,128)(2,1)} %bitcast.93, bf16[128,2048]{1,0:T(8,128)(2,1)} %bitcast.99), custom_call_target="tpu_custom_call" | custom-call | flops 67108864 | bytes 1261568 | tf_op jit(solution)/shard_map/pallas_call | solution.py:49
  46.6 3.0 %shard_map.107 = (f32[128,512]{1,0:T(8,128)}, f32[128,128]{1,0:T(8,128)}, f32[2,8,128]{2,1,0:T(8,128)}) custom-call(f32[256,128]{1,0:T(8,128)} %get-tuple-element.26.bc_ref.refs_4_, f32[160,128]{1,0:T(8,128)} %get-tuple-element.27.hp_ref.refs_5_, bf16[128,2048]{1,0:T(8,128)(2,1)} %bitcast.94, bf16[128,2048]{1,0:T(8,128)(2,1)} %bitcast.100), custom_call_target="tpu_custom_call" | custom-call | flops 67108864 | bytes 1261568 | tf_op jit(solution)/shard_map/pallas_call | solution.py:49
  49.6 3.0 %shard_map.108 = (f32[128,512]{1,0:T(8,128)}, f32[128,128]{1,0:T(8,128)}, f32[2,8,128]{2,1,0:T(8,128)}) custom-call(f32[256,128]{1,0:T(8,128)} %get-tuple-element.26.bc_ref.refs_4_, f32[160,128]{1,0:T(8,128)} %get-tuple-element.27.hp_ref.refs_5_, bf16[128,2048]{1,0:T(8,128)(2,1)} %bitcast.95, bf16[128,2048]{1,0:T(8,128)(2,1)} %bitcast.101), custom_call_target="tpu_custom_call" | custom-call | flops 67108864 | bytes 1261568 | tf_op jit(solution)/shard_map/pallas_call | solution.py:49
  52.6 7.1 %collective-permute-done.5 = bf16[128,512]{1,0:T(8,128)(2,1)S(1)} collective-permute-done((bf16[128,512]{1,0:T(8,128)(2,1)S(1)}, bf16[128,512]{1,0:T(8,128)(2,1)S(1)}, u32[]{:S(2)}, u32[]{:S(2)}) %collective-permute-start.5) | collective-permute-done | bytes 131104 | tf_op jit(solution)/shard_map/ppermute | solution.py:313
  61.3 8.7 %collective-permute-start.7 = (bf16[128,512]{1,0:T(8,128)(2,1)S(1)}, bf16[128,512]{1,0:T(8,128)(2,1)S(1)}, u32[]{:S(2)}, u32[]{:S(2)}) collective-permute-start(bf16[128,512]{1,0:T(8,128)(2,1)S(1)} %get-tuple-element.63), channel_id=1, source_target_pairs={{0,4},{4,0},{8,12},{12,8},{1,5},{5,1},{9,13},{13,9},{2,6},{6,2},{1... | collective-permute-start | bytes 393224 | tf_op jit(solution)/shard_map/ppermute | solution.py:313
  70.2 2.8 %collective-permute-done.7 = bf16[128,512]{1,0:T(8,128)(2,1)S(1)} collective-permute-done((bf16[128,512]{1,0:T(8,128)(2,1)S(1)}, bf16[128,512]{1,0:T(8,128)(2,1)S(1)}, u32[]{:S(2)}, u32[]{:S(2)}) %collective-permute-start.7) | collective-permute-done | bytes 131104 | tf_op jit(solution)/shard_map/ppermute | solution.py:313
  73.0 2.0 %collective-permute-done.9 = bf16[128,512]{1,0:T(8,128)(2,1)S(1)} collective-permute-done((bf16[128,512]{1,0:T(8,128)(2,1)S(1)}, bf16[128,512]{1,0:T(8,128)(2,1)S(1)}, u32[]{:S(2)}, u32[]{:S(2)}) %collective-permute-start.9) | collective-permute-done | bytes 131104 | tf_op jit(solution)/shard_map/ppermute | solution.py:313
  76.6 10.0 %collective-permute-start.11 = (bf16[128,512]{1,0:T(8,128)(2,1)S(1)}, bf16[128,512]{1,0:T(8,128)(2,1)S(1)}, u32[]{:S(2)}, u32[]{:S(2)}) collective-permute-start(bf16[128,512]{1,0:T(8,128)(2,1)S(1)} %get-tuple-element.59), channel_id=1, source_target_pairs={{0,4},{4,0},{8,12},{12,8},{1,5},{5,1},{9,13},{13,9},{2,6},{6,2},{1... | collective-permute-start | bytes 393224 | tf_op jit(solution)/shard_map/ppermute | solution.py:313
  86.8 2.8 %collective-permute-done.11 = bf16[128,512]{1,0:T(8,128)(2,1)S(1)} collective-permute-done((bf16[128,512]{1,0:T(8,128)(2,1)S(1)}, bf16[128,512]{1,0:T(8,128)(2,1)S(1)}, u32[]{:S(2)}, u32[]{:S(2)}) %collective-permute-start.11) | collective-permute-done | bytes 131104 | tf_op jit(solution)/shard_map/ppermute | solution.py:313
  89.6 2.0 %collective-permute-done.12 = bf16[128,512]{1,0:T(8,128)(2,1)S(1)} collective-permute-done((bf16[128,512]{1,0:T(8,128)(2,1)S(1)}, bf16[128,512]{1,0:T(8,128)(2,1)S(1)}, u32[]{:S(2)}, u32[]{:S(2)}) %collective-permute-start.12) | collective-permute-done | bytes 131104 | tf_op jit(solution)/shard_map/ppermute | solution.py:313
  92.8 5.6 %shard_map.109 = (bf16[128,2048]{1,0:T(8,128)(2,1)}, f32[288,128]{1,0:T(8,128)}) custom-call(bf16[5,128,512]{2,1,0:T(8,128)(2,1)} %get-tuple-element.57.refs_0_, bf16[5,128,512]{2,1,0:T(8,128)(2,1)} %get-tuple-element.56.refs_1_, bf16[128,2048]{1,0:T(8,128)(2,1)} %bitcast.96, bf16[128,2048]{1,0:T(8,128)(2,1)} %bitcast.102, ...), custom_call_target="tpu_custom_call" | custom-call | flops 536870912 | bytes 3924096 | tf_op jit(solution)/shard_map/pallas_call | solution.py:49
  105.5 2.3 %collective-permute-start.18 = (bf16[160,128]{1,0:T(8,128)(2,1)S(1)}, bf16[160,128]{1,0:T(8,128)(2,1)S(1)}, u32[]{:S(2)}, u32[]{:S(2)}) collective-permute-start(bf16[160,128]{1,0:T(8,128)(2,1)S(1)} %get-tuple-element.53), channel_id=1, source_target_pairs={{0,12},{4,0},{8,4},{12,8},{2,14},{6,2},{10,6},{14,10},{1,13},{5,1}... | collective-permute-start | bytes 122888 | tf_op jit(solution)/shard_map/ppermute | solution.py:439
  110.0 2.9 %shard_map.111 = bf16[128,2048]{1,0:T(8,128)(2,1)} custom-call(bf16[320,128]{1,0:T(8,128)(2,1)} %shard_map.110.low_ref, bf16[1024,256]{1,0:T(8,128)(2,1)} %refs_0_.1, bf16[1024,64]{1,0:T(8,128)(2,1)} %copy.19.dt_ref.refs_1_, bf16[1024,256]{1,0:T(8,128)(2,1)} %copy-done.3, bf16[1024,64]{1,0:T(8,128)(2,1)} %copy-done.4), custom_call_target="tpu_custom_call" | custom-call | flops 167772160 | bytes 1392640 | tf_op jit(solution)/shard_map/pallas_call | solution.py:49
  114.7 2.6 %collective-permute-start.22 = (bf16[160,128]{1,0:T(8,128)(2,1)S(1)}, bf16[160,128]{1,0:T(8,128)(2,1)S(1)}, u32[]{:S(2)}, u32[]{:S(2)}) collective-permute-start(bf16[160,128]{1,0:T(8,128)(2,1)S(1)} %get-tuple-element.53), channel_id=1, source_target_pairs={{0,14},{4,2},{8,6},{12,10},{2,12},{6,0},{10,4},{14,8},{1,15},{5,3}... | collective-permute-start | bytes 122888 | tf_op jit(solution)/shard_map/ppermute | solution.py:439
  117.3 3.6 %collective-permute-done.21 = bf16[160,128]{1,0:T(8,128)(2,1)S(1)} collective-permute-done((bf16[160,128]{1,0:T(8,128)(2,1)S(1)}, bf16[160,128]{1,0:T(8,128)(2,1)S(1)}, u32[]{:S(2)}, u32[]{:S(2)}) %collective-permute-start.21) | collective-permute-done | bytes 40992 | tf_op jit(solution)/shard_map/ppermute | solution.py:439
  121.3 2.4 %all_gather.13.low_ref = bf16[2,4,320,128]{3,2,1,0:T(8,128)(2,1)} all-gather(bf16[2,4,160,128]{3,2,1,0:T(8,128)(2,1)S(1)} %bitcast.106), channel_id=1, replica_groups=mesh['grp'=2,'seq'=4,'dp'=2,'head'=2] {'head'}, dimensions={2}, use_global_device_ids=true | all-gather | bytes 983040 | tf_op jit(solution)/shard_map/all_gather | solution.py:441
  123.7 12.1 %all-gather.6.cloned.1.call-done = bf16[512,1024]{1,0:T(8,128)(2,1)} async-done(((bf16[128,1024]{1,0:T(8,128)(2,1)}), bf16[512,1024]{1,0:T(8,128)(2,1)}) %all-gather.6.cloned.1.call-update) | async-done | bytes 1048592 | tf_op jit(solution)/shard_map/all_gather | solution.py:345
  135.8 4.6 %shard_map.112 = (f32[1024,256]{1,0:T(8,128)}, f32[1024,64]{1,0:T(8,128)}) custom-call(bf16[2,4,320,128]{3,2,1,0:T(8,128)(2,1)} %all_gather.13.low_ref, bf16[4,128,1024]{2,1,0:T(8,128)(2,1)} %all-gather.4.cloned.1.call-done.refs_0_, bf16[4,128,1024]{2,1,0:T(8,128)(2,1)} %bitcast.104), custom_call_target="tpu_custom_call" | custom-call | flops 671088640 | bytes 2752512 | tf_op jit(solution)/shard_map/pallas_call | solution.py:49
  (96 shorter events, 34.5 us)
Async XLA Ops:
  7.2 116.5 %all-gather.4.cloned.1.call-start = ((), (), s32[]{:S(2)}) async-start(), calls=%async_computation | async-start | bytes 1310720 | tf_op jit(solution)/shard_map/all_gather | solution.py:345
  9.1 9.2 %collective-permute-start = (bf16[128,1024]{1,0:T(8,128)(2,1)S(1)}, bf16[128,1024]{1,0:T(8,128)(2,1)S(1)}, u32[]{:S(2)}, u32[]{:S(2)}) collective-permute-start(bf16[128,1024]{1,0:T(8,128)(2,1)S(1)} %get-tuple-element.68), channel_id=1, source_target_pairs={{0,2},{2,0},{1,3},{3,1},{4,6},{6,4},{5,7},{7,5},{8,10},{10,8},{9,1... | collective-permute-start | bytes 786440 | tf_op jit(solution)/shard_map/ppermute | solution.py:20
  21.2 5.6 %collective-permute-start.1 = (f32[320,128]{1,0:T(8,128)}, f32[320,128]{1,0:T(8,128)S(1)}, u32[]{:S(2)}, u32[]{:S(2)}) collective-permute-start(f32[320,128]{1,0:T(8,128)} %shard_map.103), channel_id=1, source_target_pairs={{0,2},{2,0},{1,3},{3,1},{4,6},{6,4},{5,7},{7,5},{8,10},{10,8},{9,1... | collective-permute-start | bytes 491528 | tf_op jit(solution)/shard_map/ppermute | solution.py:20
  27.8 3.3 %collective-permute-start.2 = (f32[320,128]{1,0:T(8,128)S(1)}, f32[320,128]{1,0:T(8,128)S(1)}, u32[]{:S(2)}, u32[]{:S(2)}) collective-permute-start(f32[320,128]{1,0:T(8,128)S(1)} %add.162.refs_0_), channel_id=1, source_target_pairs={{0,1},{1,0},{2,3},{3,2},{4,5},{5,4},{6,7},{7,6},{8,9},{9,8},{10,11... | collective-permute-start | bytes 491528 | tf_op jit(solution)/shard_map/ppermute | solution.py:20
  27.9 107.9 %all-gather.6.cloned.1.call-start = ((), (), s32[]{:S(2)}) async-start(), calls=%async_computation.1 | async-start | bytes 1310720 | tf_op jit(solution)/shard_map/all_gather | solution.py:345
  27.9 81.1 %collective-permute-start.14 = (bf16[1024,256]{1,0:T(8,128)(2,1)S(1)}, bf16[1024,256]{1,0:T(8,128)(2,1)S(1)}, u32[]{:S(2)}, u32[]{:S(2)}) collective-permute-start(bf16[1024,256]{1,0:T(8,128)(2,1)S(1)} %copy-done), channel_id=1, source_target_pairs={{0,2},{2,0},{1,3},{3,1},{4,6},{6,4},{5,7},{7,5},{8,10},{10,8},{9,1... | collective-permute-start | bytes 1572872 | tf_op jit(solution)/shard_map/ppermute | solution.py:20
  38.6 14.0 %collective-permute-start.3 = (bf16[128,512]{1,0:T(8,128)(2,1)S(1)}, bf16[128,512]{1,0:T(8,128)(2,1)S(1)}, u32[]{:S(2)}, u32[]{:S(2)}) collective-permute-start(bf16[128,512]{1,0:T(8,128)(2,1)S(1)} %get-tuple-element.67), channel_id=1, source_target_pairs={{0,4},{4,0},{8,12},{12,8},{1,5},{5,1},{9,13},{13,9},{2,6},{6,2},{1... | collective-permute-start | bytes 393224 | tf_op jit(solution)/shard_map/ppermute | solution.py:313
  40.2 19.5 %collective-permute-start.5 = (bf16[128,512]{1,0:T(8,128)(2,1)S(1)}, bf16[128,512]{1,0:T(8,128)(2,1)S(1)}, u32[]{:S(2)}, u32[]{:S(2)}) collective-permute-start(bf16[128,512]{1,0:T(8,128)(2,1)S(1)} %get-tuple-element.66), channel_id=1, source_target_pairs={{0,4},{4,0},{8,12},{12,8},{1,5},{5,1},{9,13},{13,9},{2,6},{6,2},{1... | collective-permute-start | bytes 393224 | tf_op jit(solution)/shard_map/ppermute | solution.py:313
  59.7 1.5 collective-permute-start.4
  60.4 0.8 collective-permute-start.6
  61.3 11.7 %collective-permute-start.7 = (bf16[128,512]{1,0:T(8,128)(2,1)S(1)}, bf16[128,512]{1,0:T(8,128)(2,1)S(1)}, u32[]{:S(2)}, u32[]{:S(2)}) collective-permute-start(bf16[128,512]{1,0:T(8,128)(2,1)S(1)} %get-tuple-element.63), channel_id=1, source_target_pairs={{0,4},{4,0},{8,12},{12,8},{1,5},{5,1},{9,13},{13,9},{2,6},{6,2},{1... | collective-permute-start | bytes 393224 | tf_op jit(solution)/shard_map/ppermute | solution.py:313
  70.0 5.0 %collective-permute-start.9 = (bf16[128,512]{1,0:T(8,128)(2,1)S(1)}, bf16[128,512]{1,0:T(8,128)(2,1)S(1)}, u32[]{:S(2)}, u32[]{:S(2)}) collective-permute-start(bf16[128,512]{1,0:T(8,128)(2,1)S(1)} %get-tuple-element.62), channel_id=1, source_target_pairs={{0,4},{4,0},{8,12},{12,8},{1,5},{5,1},{9,13},{13,9},{2,6},{6,2},{1... | collective-permute-start | bytes 393224 | tf_op jit(solution)/shard_map/ppermute | solution.py:313
  75.1 1.4 collective-permute-start.8
  76.6 13.0 %collective-permute-start.11 = (bf16[128,512]{1,0:T(8,128)(2,1)S(1)}, bf16[128,512]{1,0:T(8,128)(2,1)S(1)}, u32[]{:S(2)}, u32[]{:S(2)}) collective-permute-start(bf16[128,512]{1,0:T(8,128)(2,1)S(1)} %get-tuple-element.59), channel_id=1, source_target_pairs={{0,4},{4,0},{8,12},{12,8},{1,5},{5,1},{9,13},{13,9},{2,6},{6,2},{1... | collective-permute-start | bytes 393224 | tf_op jit(solution)/shard_map/ppermute | solution.py:313
  86.6 5.0 %collective-permute-start.12 = (bf16[128,512]{1,0:T(8,128)(2,1)S(1)}, bf16[128,512]{1,0:T(8,128)(2,1)S(1)}, u32[]{:S(2)}, u32[]{:S(2)}) collective-permute-start(bf16[128,512]{1,0:T(8,128)(2,1)S(1)} %get-tuple-element.58), channel_id=1, source_target_pairs={{0,4},{4,0},{8,12},{12,8},{1,5},{5,1},{9,13},{13,9},{2,6},{6,2},{1... | collective-permute-start | bytes 393224 | tf_op jit(solution)/shard_map/ppermute | solution.py:313
  98.4 1.6 %collective-permute-start.13 = (f32[288,128]{1,0:T(8,128)}, f32[288,128]{1,0:T(8,128)S(1)}, u32[]{:S(2)}, u32[]{:S(2)}) collective-permute-start(f32[288,128]{1,0:T(8,128)} %get-tuple-element.41.refs_0_), channel_id=1, source_target_pairs={{0,1},{1,0},{2,3},{3,2},{4,5},{5,4},{6,7},{7,6},{8,9},{9,8},{10,11... | collective-permute-start | bytes 442376 | tf_op jit(solution)/shard_map/ppermute | solution.py:20
  98.4 9.4 %collective-permute-start.15 = (bf16[1024,64]{1,0:T(8,128)(2,1)S(1)}, bf16[1024,64]{1,0:T(8,128)(2,1)S(1)}, u32[]{:S(2)}, u32[]{:S(2)}) collective-permute-start(bf16[1024,64]{1,0:T(8,128)(2,1)S(1)} %copy-done.1), channel_id=1, source_target_pairs={{0,2},{2,0},{1,3},{3,1},{4,6},{6,4},{5,7},{7,5},{8,10},{10,8},{9,1... | collective-permute-start | bytes 393224 | tf_op jit(solution)/shard_map/ppermute | solution.py:20
  103.1 9.8 %collective-permute-start.16 = (bf16[160,128]{1,0:T(8,128)(2,1)S(1)}, bf16[160,128]{1,0:T(8,128)(2,1)S(1)}, u32[]{:S(2)}, u32[]{:S(2)}) collective-permute-start(bf16[160,128]{1,0:T(8,128)(2,1)S(1)} %get-tuple-element.53), channel_id=1, source_target_pairs={{0,4},{4,8},{8,12},{12,0},{2,6},{6,10},{10,14},{14,2},{1,5},{5,9},... | collective-permute-start | bytes 122888 | tf_op jit(solution)/shard_map/ppermute | solution.py:439
  104.5 10.1 %collective-permute-start.17 = (bf16[160,128]{1,0:T(8,128)(2,1)S(1)}, bf16[160,128]{1,0:T(8,128)(2,1)S(1)}, u32[]{:S(2)}, u32[]{:S(2)}) collective-permute-start(bf16[160,128]{1,0:T(8,128)(2,1)S(1)} %get-tuple-element.53), channel_id=1, source_target_pairs={{0,8},{4,12},{8,0},{12,4},{2,10},{6,14},{10,2},{14,6},{1,9},{5,13}... | collective-permute-start | bytes 122888 | tf_op jit(solution)/shard_map/ppermute | solution.py:439
  105.5 11.8 %collective-permute-start.18 = (bf16[160,128]{1,0:T(8,128)(2,1)S(1)}, bf16[160,128]{1,0:T(8,128)(2,1)S(1)}, u32[]{:S(2)}, u32[]{:S(2)}) collective-permute-start(bf16[160,128]{1,0:T(8,128)(2,1)S(1)} %get-tuple-element.53), channel_id=1, source_target_pairs={{0,12},{4,0},{8,4},{12,8},{2,14},{6,2},{10,6},{14,10},{1,13},{5,1}... | collective-permute-start | bytes 122888 | tf_op jit(solution)/shard_map/ppermute | solution.py:439
  107.8 9.5 %collective-permute-start.19 = (bf16[160,128]{1,0:T(8,128)(2,1)S(1)}, bf16[160,128]{1,0:T(8,128)(2,1)S(1)}, u32[]{:S(2)}, u32[]{:S(2)}) collective-permute-start(bf16[160,128]{1,0:T(8,128)(2,1)S(1)} %get-tuple-element.53), channel_id=1, source_target_pairs={{0,2},{4,6},{8,10},{12,14},{2,0},{6,4},{10,8},{14,12},{1,3},{5,7},... | collective-permute-start | bytes 122888 | tf_op jit(solution)/shard_map/ppermute | solution.py:439
  109.0 8.3 %collective-permute-start.20 = (bf16[160,128]{1,0:T(8,128)(2,1)S(1)}, bf16[160,128]{1,0:T(8,128)(2,1)S(1)}, u32[]{:S(2)}, u32[]{:S(2)}) collective-permute-start(bf16[160,128]{1,0:T(8,128)(2,1)S(1)} %get-tuple-element.53), channel_id=1, source_target_pairs={{0,6},{4,10},{8,14},{12,2},{2,4},{6,8},{10,12},{14,0},{1,7},{5,11}... | collective-permute-start | bytes 122888 | tf_op jit(solution)/shard_map/ppermute | solution.py:439
  112.9 8.1 %collective-permute-start.21 = (bf16[160,128]{1,0:T(8,128)(2,1)S(1)}, bf16[160,128]{1,0:T(8,128)(2,1)S(1)}, u32[]{:S(2)}, u32[]{:S(2)}) collective-permute-start(bf16[160,128]{1,0:T(8,128)(2,1)S(1)} %get-tuple-element.53), channel_id=1, source_target_pairs={{0,10},{4,14},{8,2},{12,6},{2,8},{6,12},{10,0},{14,4},{1,11},{5,15... | collective-permute-start | bytes 122888 | tf_op jit(solution)/shard_map/ppermute | solution.py:439
  114.7 6.6 %collective-permute-start.22 = (bf16[160,128]{1,0:T(8,128)(2,1)S(1)}, bf16[160,128]{1,0:T(8,128)(2,1)S(1)}, u32[]{:S(2)}, u32[]{:S(2)}) collective-permute-start(bf16[160,128]{1,0:T(8,128)(2,1)S(1)} %get-tuple-element.53), channel_id=1, source_target_pairs={{0,14},{4,2},{8,6},{12,10},{2,12},{6,0},{10,4},{14,8},{1,15},{5,3}... | collective-permute-start | bytes 122888 | tf_op jit(solution)/shard_map/ppermute | solution.py:439
  (12 other events, 86.3 us)
Sparse Core Ops, SparseCore 0:
  28.0 34.6 all-gather.3
  104.7 31.0 all-gather.5

commit v3 on v2

v3 whole, which is shorter than its diff:
```python
import functools

import jax
import jax.numpy as jnp
from jax import lax
from jax.experimental import pallas as pl
from jax.experimental.pallas import tpu as pltpu
from jax.sharding import PartitionSpec as P

CHUNKS = 4
PARTS = 4
EARLY = 2
GROUPS = 8
BF = jnp.bfloat16
F32 = jnp.float32
TOP = lax.Precision.HIGHEST
LIMIT = 56 * 1024 * 1024


def cyclic(a, axis, by):
    count = lax.axis_size(axis)
    return lax.ppermute(a, axis, [(i, (i + by) % count) for i in range(count)])


def mm(a, b, ca, cb, precision=None):
    return lax.dot_general(
        a, b, (((ca,), (cb,)), ((), ())), preferred_element_type=F32, precision=precision
    )


def halves(a):
    high = a.astype(BF)
    return high, (a - high.astype(F32)).astype(BF)


def head_lanes(heads, width, size, first=0):
    row = lax.broadcasted_iota(jnp.int32, (heads, width), 0)
    col = lax.broadcasted_iota(jnp.int32, (heads, width), 1) + first
    low = row * size
    return jnp.where((col >= low) & (col < low + size), 1.0, 0.0).astype(F32)


def spread(a, pick):
    high, low = halves(a)
    both = jnp.concatenate([pick, pick], axis=0)
    return mm(jnp.concatenate([high, low], axis=0), both, 0, 0)


VMEM = pl.BlockSpec(memory_space=pltpu.VMEM)
ANY = pl.BlockSpec(memory_space=pl.ANY)


def call(kernel, out_shape, flops, *args, scratch=(), specs=None, out_specs=None):
    size = sum(a.size * a.dtype.itemsize for a in args)
    return pl.pallas_call(
        kernel,
        out_shape=out_shape,
        grid=(1,),
        in_specs=specs or [VMEM] * len(args),
        out_specs=out_specs or jax.tree.map(lambda _: VMEM, out_shape),
        scratch_shapes=list(scratch),
        compiler_params=pltpu.CompilerParams(vmem_limit_bytes=LIMIT),
        cost_estimate=pl.CostEstimate(flops=flops, bytes_accessed=size, transcendentals=0),
    )(*args)


def struct(shape, dtype):
    return jax.ShapeDtypeStruct(shape, dtype)


def after(a, *others):
    return lax.optimization_barrier((a, others))[0]


def matchings(count):
    groups = [[(i, i + 1) for i in range(kind, count - 1, 2)] for kind in (0, 1)]
    pairs = []
    for group in groups:
        to = {i: i for i in range(count)}
        for i, j in group:
            to[i], to[j] = j, i
        pairs.append(sorted(to.items()))
    return groups, pairs


def split_kernel(count, a_ref, *refs):
    outs, sems = refs[:count], refs[count]
    me = lax.axis_index("dp")
    part = outs[0].shape[1]
    copies = []
    for r in range(count):
        at = pl.multiple_of(lax.rem(me + r, count) * part, 128)
        copies.append(pltpu.make_async_copy(a_ref.at[:, pl.ds(at, part)], outs[r], sems.at[r]))
    for copy in copies:
        copy.start()
    for copy in copies:
        copy.wait()


def project_kernel(a_ref, bc_ref, dt_ref, out_ref):
    a = a_ref[...]
    state_n = bc_ref.shape[1] // 2
    rows = a.shape[0]
    bc = mm(a, bc_ref[...], 1, 0)
    out_ref[0:rows, :] = bc[:, :state_n]
    out_ref[rows : 2 * rows, :] = bc[:, state_n:]
    out_ref[2 * rows :, :] = mm(dt_ref[...], a, 1, 1)


def project(a, w_bc, w_dt):
    rows = a.shape[0]
    total = 2 * rows + w_dt.shape[0]
    return call(
        project_kernel,
        struct((total, w_bc.shape[1] // 2), F32),
        2 * a.size * total,
        a,
        w_bc,
        w_dt,
    )


def state_kernel(count, size, *refs):
    proj = refs[:count]
    x_ref, g_ref, rate_ref, bias_ref, own_ref, decay_ref, bc_ref, hp_ref = refs[count:]
    heads = rate_ref.shape[1]
    rows = x_ref.shape[0]
    rate, bias = rate_ref[...].T, bias_ref[...].T
    chunks, step = own_ref.shape[1], own_ref.shape[3]
    first = pl.multiple_of(2 * rows + lax.axis_index("head") * heads, 8)
    bc = proj[0][0 : 2 * rows, :]
    pre = proj[0][pl.ds(first, heads), :] + bias
    for ref in proj[1:]:
        bc = bc + ref[0 : 2 * rows, :]
        pre = pre + ref[pl.ds(first, heads), :]
    bc_ref[...] = bc
    dt = jnp.maximum(pre, 0.0) + jnp.log1p(jnp.exp(-jnp.abs(pre)))
    row = lax.broadcasted_iota(jnp.int32, (rows, rows), 0)
    col = lax.broadcasted_iota(jnp.int32, (rows, rows), 1)
    cum = mm(-dt * rate, jnp.where(row <= col, 1.0, 0.0), 1, 0, TOP)
    last = cum[:, rows - 1 : rows]
    grow = jnp.exp(cum)
    w = jnp.exp(last - cum) * dt
    decay = jnp.exp(last)
    for k, part in enumerate((pre, dt, cum, grow, w)):
        hp_ref[k * heads : (k + 1) * heads, :] = part
    way = lax.rem(lax.axis_index("seq"), 2)
    kinds = ((w, x_ref, bc[:rows], way), (grow, g_ref, bc[rows:], 1 - way))
    for scale, ref, vec, place in kinds:
        high, low = halves(vec.T)
        wide = jnp.concatenate([high, low], axis=1)
        for k in range(chunks):
            pick = head_lanes(heads, step, size, k * step)
            if place is way:
                decay_ref[k] = jnp.sum(pick * decay, axis=0, keepdims=True)
            value = spread(scale, pick.astype(BF)) * ref[:, k * step : (k + 1) * step].astype(F32)
            top, rest = halves(value)
            own_ref[place, k] = mm(wide, jnp.concatenate([top, top], axis=0), 1, 0) + mm(
                high, rest, 1, 0
            )


def inner_kernel(first, pairs, size, bc_ref, hp_ref, x_ref, g_ref, *refs):
    gx_ref, ds_ref, sums_ref = refs[-5:-2]
    gy_ref, xg_ref = refs[-2:]
    rows = x_ref.shape[0]
    heads = hp_ref.shape[0] // 5
    lanes = 2 * size
    width = pairs * lanes
    if len(refs) == 6 and first > 0:
        scores = refs[0][...]
    else:
        scores = mm(bc_ref[rows : 2 * rows, :], bc_ref[0:rows, :], 1, 1, TOP)
        refs[0][...] = scores
    row = lax.broadcasted_iota(jnp.int32, (rows, rows), 0)
    col = lax.broadcasted_iota(jnp.int32, (rows, rows), 1)
    causal = row >= col
    dt = hp_ref[heads : 2 * heads, :]
    cum = hp_ref[2 * heads : 3 * heads, :]
    cum_t = cum.T
    lane = lax.broadcasted_iota(jnp.int32, (rows, lanes), 1)
    sides = [jnp.where(lane < size, 1.0, 0.0).astype(BF), jnp.where(lane < size, 0.0, 1.0).astype(BF)]
    ds = jnp.zeros((rows, rows), F32)
    for j in range(pairs):
        place = slice(j * lanes, (j + 1) * lanes)
        x, g = x_ref[:, place], g_ref[:, place]
        xs = jnp.concatenate([x * s for s in sides], axis=0)
        gs = jnp.concatenate([g * s for s in sides], axis=0)
        m = mm(gs, x, 1, 1)
        kern = []
        for i in range(2):
            h = 2 * (first + j) + i
            gap = cum_t[:, h : h + 1] - cum[h : h + 1, :]
            fall = jnp.exp(jnp.where(causal, gap, -jnp.inf)) * dt[h : h + 1, :]
            kern.append((fall * scores).astype(BF))
            ds = ds + fall * m[i * rows : (i + 1) * rows]
        y = mm(jnp.concatenate(kern, axis=1), xs, 1, 0)
        gx = mm(jnp.concatenate(kern, axis=0), gs, 0, 0)
        gx_ref[:, place] = gx
        late = slice(width + j * lanes, width + (j + 1) * lanes)
        gy_ref[:, place], gy_ref[:, late] = halves(g.astype(F32) * y)
        xg_ref[:, place], xg_ref[:, late] = halves(x.astype(F32) * gx)
    ds_ref[...] = ds
    pick = head_lanes(2 * pairs, width, size).astype(BF)
    pick = jnp.concatenate([pick, pick], axis=1)
    sums_ref[0] = mm(pick, gy_ref[...], 1, 1)
    sums_ref[1] = mm(pick, xg_ref[...], 1, 1)


def outer_kernel(size, parts, *refs):
    store_ref, x_ref, g_ref, bc_ref, hp_ref, decay_ref, rate_ref = refs[:7]
    gxs, dss, sums = (refs[7 + k * parts : 7 + (k + 1) * parts] for k in range(3))
    grad_ref, keep_ref, give_ref, wv_ref, eu_ref, io_ref = refs[7 + 3 * parts :]
    odd = lax.rem(lax.axis_index("seq"), 2)
    rate = rate_ref[...].T
    rows, width = x_ref.shape
    heads = rate_ref.shape[1]
    chunks, step = decay_ref.shape[0], decay_ref.shape[2]
    piece = width // parts
    b, c = bc_ref[0:rows, :], bc_ref[rows : 2 * rows, :]
    pre, dt, cum, grow, w = (hp_ref[k * heads : (k + 1) * heads, :] for k in range(5))
    ds = dss[0][...]
    for ref in dss[1:]:
        ds = ds + ref[...]
    db = mm(c, ds, 0, 0, TOP)
    dc = mm(b, ds, 0, 1, TOP)
    b_wide = jnp.concatenate(halves(b), axis=1)
    c_wide = jnp.concatenate(halves(c), axis=1)
    for k in range(chunks):
        place = slice(k * step, (k + 1) * step)
        late = slice(width + k * step, width + (k + 1) * step)
        pick = head_lanes(heads, step, size, k * step).astype(BF)
        incoming, outgoing = store_ref[1 - odd, k], store_ref[odd, k]
        u = mm(c_wide, jnp.concatenate([incoming, incoming], axis=0), 1, 0)
        v = mm(b_wide, jnp.concatenate([outgoing, outgoing], axis=0), 1, 0)
        scale = spread(w, pick)
        wx = scale * x_ref[:, place].astype(F32)
        eg = spread(grow, pick) * g_ref[:, place].astype(F32)
        for q in range(step // piece) if step >= piece else (0,):
            if step >= piece:
                at = k * step + q * piece
                inner = slice(q * piece, (q + 1) * piece)
                term = gxs[at // piece][...]
            else:
                at, inner = k * step, slice(0, step)
                term = gxs[at // piece][:, at % piece : at % piece + step]
            total = term + scale[:, inner] * v[:, inner]
            grad_ref[:, at : at + total.shape[1]] = total.astype(BF)
        wv_ref[:, place], wv_ref[:, late] = halves(wx * v)
        eu_ref[:, place], eu_ref[:, late] = halves(eg * u)
        db = db + mm(
            jnp.concatenate([outgoing, outgoing], axis=1), jnp.concatenate(halves(wx), axis=1), 1, 1
        )
        dc = dc + mm(
            jnp.concatenate([incoming, incoming], axis=1), jnp.concatenate(halves(eg), axis=1), 1, 1
        )
        io_ref[:, place] = jnp.sum(incoming.astype(F32) * outgoing.astype(F32), axis=0, keepdims=True)
    pick = head_lanes(heads, width, size)
    ddecay = jnp.sum(pick * io_ref[...], axis=1, keepdims=True)
    pick = pick.astype(BF)
    pick = jnp.concatenate([pick, pick], axis=1)
    wdw = mm(pick, wv_ref[...], 1, 1)
    egu = mm(pick, eu_ref[...], 1, 1)
    rowsum = jnp.concatenate([s[0] for s in sums], axis=0)
    colsum = jnp.concatenate([s[1] for s in sums], axis=0)
    dcum = rowsum - colsum + egu - wdw
    row = lax.broadcasted_iota(jnp.int32, (rows, rows), 0)
    col = lax.broadcasted_iota(jnp.int32, (rows, rows), 1)
    rev = mm(dcum, jnp.where(row >= col, 1.0, 0.0), 1, 0, TOP)
    decay = grow[:, rows - 1 : rows]
    rev = rev + jnp.sum(wdw, axis=1, keepdims=True) + decay * ddecay
    gate = 1.0 / (1.0 + jnp.exp(-pre))
    small = 1e-30
    ratio = jnp.where(dt > small, gate / jnp.maximum(dt, small), 1.0)
    core = lax.axis_index("head")
    keep_ref[0:rows, :] = jnp.where(core == 0, db, dc)
    keep_ref[rows:, :] = (colsum + wdw) * ratio - rate * rev * gate
    give_ref[...] = jnp.where(core == 0, dc, db)


def token_kernel(count, mine_ref, other_ref, *refs):
    out_ref = refs[2 * count]
    me, core = lax.axis_index("dp"), lax.axis_index("head")
    part, cols = refs[0].shape
    half = cols // 2
    heads = refs[1].shape[0] // 2
    for r in range(count):
        at = pl.multiple_of(lax.rem(me - r + count, count) * part, 128)
        total = None
        for k, ref in enumerate((mine_ref, other_ref)):
            at_col = pl.multiple_of(lax.rem(core + k, 2) * half, 128)
            at_row = pl.multiple_of(lax.rem(core + k, 2) * heads, 16)
            term = mm(ref[0:half, :], refs[2 * r][:, pl.ds(at_col, half)], 0, 1)
            term = term + mm(ref[half : mine_ref.shape[0], :], refs[2 * r + 1][pl.ds(at_row, heads), :], 0, 0)
            total = term if total is None else total + term
        out_ref[:, pl.ds(at, part)] = total.astype(BF)


def weight_kernel(scale, n_dp, n_seq, slots, *refs):
    count = 2 * len(slots) if n_dp > 1 else len(slots)
    toks, lows = refs[:count], refs[count:-6]
    bc_ref, dt_ref, tok_ref, low_ref, tok_sem, low_sem = refs[-6:]
    rows = toks[0].shape[0]
    share = lows[0].shape[0]
    per = lows[n_dp * n_seq].shape[0] // share
    core, place = lax.axis_index("head"), lax.axis_index("seq")
    even = lax.rem(place, 2) == 0
    copies = []
    for r in range(n_dp):
        for k, (kind, hop) in enumerate(slots):
            above = even if kind == 0 else ~even
            block = jnp.where(above, place + hop, place - hop)
            fits = (block >= 0) & (block < n_seq)
            if hop > 0 and kind == 1:
                fits = fits & jnp.where(above, place < n_seq - 1, place > 0)
            at = pl.multiple_of(jnp.clip(block, 0, n_seq - 1) * rows, 128)
            source = toks[k] if r == 0 else toks[len(slots) + k].at[pl.ds((r - 1) * rows, rows)]
            copy = pltpu.make_async_copy(source, tok_ref.at[r, pl.ds(at, rows)], tok_sem.at[r, k])
            copies.append((fits, copy))
    for r in range(n_dp):
        for s in range(n_seq):
            block = lax.rem(place - s + n_seq, n_seq)
            at = pl.multiple_of(block * rows, 128)
            for k in range(2):
                index = r * n_seq + s
                row = pl.multiple_of(lax.rem(core + k, 2) * share, 16)
                source = lows[index]
                if k == 1:
                    source = lows[n_dp * n_seq + index // per].at[pl.ds(index % per * share, share)]
                copy = pltpu.make_async_copy(
                    source, low_ref.at[r, pl.ds(row, share), pl.ds(at, rows)], low_sem.at[index, k]
                )
                copies.append((None, copy))
    for fits, copy in copies:
        if fits is None:
            copy.start()
        else:
            pl.when(fits)(copy.start)
    for fits, copy in copies:
        if fits is None:
            copy.wait()
        else:
            pl.when(fits)(copy.wait)
    total = mm(low_ref[0], tok_ref[0], 1, 0)
    for r in range(1, n_dp):
        total = total + mm(low_ref[r], tok_ref[r], 1, 0)
    total = total * scale
    half = bc_ref.shape[1] // 2
    heads = dt_ref.shape[0] // 2
    for k in range(2):
        bc_ref[:, k * half : (k + 1) * half] = total[k * share : k * share + half].T
        dt_ref[k * heads : (k + 1) * heads, :] = total[k * share + half : (k + 1) * share]


def relay(block, hops, held=None):
    count = lax.axis_size("seq")
    groups, pairs = matchings(count)
    held = held or [block, block]
    found, slots = [], []
    for hop in hops:
        fresh = [None, None]
        for kind in (0, 1):
            if any(i - hop + 1 >= 0 or j + hop - 1 < count for i, j in groups[kind]):
                fresh[kind] = lax.ppermute(held[1 - kind], "seq", pairs[kind])
                found.append(fresh[kind])
                slots.append((kind, hop))
        held = [h if f is None else f for f, h in zip(fresh, held)]
    return found, slots, held


def chains(own, decay, inner):
    count = lax.axis_size("seq")
    place = lax.axis_index("seq")
    chunks = own.shape[1]
    even = lax.rem(place, 2) == 0
    groups, pairs = matchings(count)
    store = jnp.zeros((2, chunks + 1) + own.shape[2:], BF)
    got = [None, None]
    done, todo = [], list(inner)
    ends = (place == 0) | (place == count - 1)
    for slot in range(1, count + chunks - 1):
        fresh, sent = [None, None], []
        for kind in (0, 1):
            used = any(
                0 <= slot - hop < chunks for i, j in groups[kind] for hop in (j, count - j)
            )
            if not used:
                continue
            goes_up = even if kind == 0 else ~even
            chunk = jnp.where(goes_up, slot - place - 1, slot - count + place)
            chunk = jnp.clip(chunk, 0, chunks - 1)
            zero = jnp.zeros_like(chunk)
            value = lax.dynamic_slice(
                own, (zero + kind, chunk, zero, zero), (1, 1) + own.shape[2:]
            )[0, 0]
            before = got[1 - kind]
            if before is not None:
                kept = before.astype(F32) * lax.dynamic_index_in_dim(decay, chunk, 0, False)
                value = value + (jnp.where(ends, 0.0, kept) if kind == 0 else kept)
            sent.append(value.astype(BF))
            fresh[kind] = lax.ppermute(sent[-1], "seq", pairs[kind])
        if todo:
            done.append(todo.pop(0)(*sent))
        ready = [a for a in fresh if a is not None] + ([done[-1][0]] if done else [])
        got = list(fresh)
        if len(ready) > 1:
            kept = lax.optimization_barrier(tuple(ready))
            live = [k for k in (0, 1) if fresh[k] is not None]
            for k, a in zip(live, kept):
                got[k] = a
        for kind in (0, 1):
            if got[kind] is None:
                continue
            below = ~even if kind == 0 else even
            chunk = jnp.where(below, slot - place, slot - count + place + 1)
            fits = (chunk >= 0) & (chunk < chunks)
            if kind == 1:
                fits = fits & ~ends
            chunk = jnp.where(fits, chunk, chunks)
            zero = jnp.zeros_like(chunk)
            store = lax.dynamic_update_slice(
                store, got[kind][None, None], (zero + kind, chunk, zero, zero)
            )
    done += [make() for make in todo]
    return store, done


def body(tokens, ssd_input, grad_out, w_bc, w_dt, decay_rate, dt_bias):
    feats, x, g = tokens[0], ssd_input[0], grad_out[0]
    rows, width = feats.shape
    heads = decay_rate.shape[0]
    size = width // heads
    n_dp, n_seq = lax.axis_size("dp"), lax.axis_size("seq")
    part = width // n_dp
    state_n = w_bc.shape[1] // 2
    w_dt = w_dt.T
    rate, bias = decay_rate[None], dt_bias[None]

    pieces = call(
        functools.partial(split_kernel, n_dp),
        [struct((rows, part), BF)] * n_dp,
        0,
        feats,
        scratch=[pltpu.SemaphoreType.DMA((n_dp,))],
        specs=[ANY],
        out_specs=[ANY] * n_dp,
    )
    items = [pieces[0]] + [cyclic(pieces[r], "dp", r) for r in range(1, n_dp)]
    first = project(items[0], w_bc, w_dt)
    partials = [first] + [
        cyclic(project(items[r], w_bc, w_dt), "dp", -r) for r in range(1, n_dp)
    ]
    proj = partials + [cyclic(a, "head", 1) for a in partials]
    cut = min(1 + EARLY, n_seq)
    early, slots, held = relay(items[0], range(1, cut))
    x = after(x, *early)
    step = width // CHUNKS
    own, decay, bc, hp = call(
        functools.partial(state_kernel, 2 * n_dp, size),
        (
            struct((2, CHUNKS, state_n, step), F32),
            struct((CHUNKS, 1, step), F32),
            struct((2 * rows, state_n), F32),
            struct((5 * heads, rows), F32),
        ),
        12 * rows * width * state_n,
        *proj,
        x,
        g,
        rate,
        bias,
    )
    pairs = width // (2 * size) // PARTS
    span = width // PARTS
    shared = []

    def inner(q, *others):
        held = after(bc, *others) if others else bc
        square = struct((rows, rows), F32)
        block = pl.BlockSpec((rows, span), lambda _: (0, q))
        out = call(
            functools.partial(inner_kernel, q * pairs, pairs, size),
            ([square] if q == 0 else [])
            + [struct((rows, span), F32), square, struct((2, 2 * pairs, rows), F32)],
            8 * rows * rows * span,
            held,
            hp,
            x,
            g,
            *shared,
            scratch=(pltpu.VMEM((rows, 2 * span), BF), pltpu.VMEM((rows, 2 * span), BF)),
            specs=[VMEM, VMEM, block, block] + [VMEM] * len(shared),
        )
        if q == 0:
            shared.append(out[0])
            out = out[1:]
        return out

    store, inners = chains(own, decay, [functools.partial(inner, q) for q in range(PARTS)])
    grad_x, keep, give = call(
        functools.partial(outer_kernel, size, PARTS),
        (
            struct((rows, width), BF),
            struct((rows + heads, rows), F32),
            struct((rows, rows), F32),
        ),
        16 * rows * width * state_n,
        store,
        x,
        g,
        bc,
        hp,
        decay,
        rate,
        *[a[0] for a in inners],
        *[a[1] for a in inners],
        *[a[2] for a in inners],
        scratch=(
            pltpu.VMEM((rows, 2 * width), BF),
            pltpu.VMEM((rows, 2 * width), BF),
            pltpu.VMEM((1, width), F32),
        ),
    )
    taken = cyclic(give, "head", 1)
    mine = jnp.concatenate([keep[:rows] + taken, keep[rows:]], axis=0).astype(BF)
    w_bc_later, w_dt_later = after((w_bc, w_dt), hp)
    weights = [w_bc, w_dt]
    for r in range(1, n_dp):
        weights += [cyclic(w_bc_later, "dp", r), cyclic(w_dt_later, "dp", r)]
    lows = []
    for r in range(n_dp):
        for s in range(n_seq):
            pairs_to = [
                (j * n_dp + i, (j + s) % n_seq * n_dp + (i + r) % n_dp)
                for i in range(n_dp)
                for j in range(n_seq)
            ]
            got = mine if r == s == 0 else lax.ppermute(mine, ("seq", "dp"), pairs_to)
            lows.append(got)
    per = -(-len(lows) // GROUPS)
    groups = [lows[k : k + per] for k in range(0, len(lows), per)]
    swapped = [cyclic(a[0] if per == 1 else jnp.concatenate(a, axis=0), "head", 1) for a in groups]
    grads = call(
        functools.partial(token_kernel, n_dp),
        struct((rows, width), BF),
        2 * rows * width * (2 * state_n + 2 * heads),
        lows[0],
        swapped[0],
        *weights,
    )
    held = after(tuple(held), store)
    found, rest, _ = relay(items[0], range(cut, n_seq), list(held))
    slots = [(0, 0)] + slots + rest
    toks = [items[0]] + early + found
    if n_dp > 1:
        others = items[1] if n_dp == 2 else jnp.concatenate(items[1:], axis=0)
        found, _, _ = relay(after(others, store), range(1, n_seq))
        toks += [others] + found
    cols = 2 * (rows + heads)
    grad_bc, grad_dt = call(
        functools.partial(weight_kernel, 1.0 / (rows * n_seq * n_dp), n_dp, n_seq, slots),
        (struct((part, 2 * state_n), F32), struct((2 * heads, part), F32)),
        2 * n_dp * n_seq * rows * part * cols,
        *toks,
        *lows,
        *swapped,
        specs=[ANY] * (len(toks) + len(lows) + len(swapped)),
        scratch=(
            pltpu.VMEM((n_dp, n_seq * rows, part), BF),
            pltpu.VMEM((n_dp, cols, n_seq * rows), BF),
            pltpu.SemaphoreType.DMA((n_dp, len(slots))),
            pltpu.SemaphoreType.DMA((len(lows), 2)),
        ),
    )
    return grad_x[None], grads[None], grad_bc, grad_dt.T


def solution(mesh):
    in_specs = (
        P(("grp", "dp"), "seq", "head"),
        P(("grp", "dp"), "seq", "head"),
        P(("grp", "dp"), "seq", "head"),
        P(("head", "dp"), None),
        P(("head", "dp"), None),
        P("head"),
        P("head"),
    )
    out_specs = (
        P(("grp", "dp"), "seq", "head"),
        P(("grp", "dp"), "seq", "head"),
        P(("grp", "head", "dp"), None),
        P(("grp", "head", "dp"), None),
    )
    return jax.shard_map(body, mesh=mesh, in_specs=in_specs, out_specs=out_specs, check_vma=False)
```

time: 150 us -> 156 us (1.040)
  starting transfers between devices: 42.9 us -> 65.1 us
  Pallas kernels: 36 us -> 49.5 us
  between operations: 14.4 us -> 1.2 us
  local copies, waits for them, and re-layouts: 11.9 us -> 4.97 us
  waiting for transfers between devices: 39.1 us -> 32.5 us
  blocking collectives: 2.4 us -> 0 us
    ppermute x17 -> x27, starting transfers between devices: 34.9 us -> 56.1 us  [the longest x10 23.7 us: chains(): fresh[kind] = lax.ppermute(sent[-1], 'seq', pairs[kind])]
    pallas_call x11, Pallas kernels: 36 us -> 49.5 us  [call(): pl.pallas_call(kernel, out_shape=out_shape, grid=(1,), in_specs=specs or...]
    all_gather x2 -> x0, waiting for transfers between devices: 12.1 us -> none  [body(): toks = [lax.all_gather(a, 'seq') for a in items]]
    ppermute x17 -> x27, waiting for transfers between devices: 20.7 us -> 29 us  [the longest x7 18.8 us: body(): got = mine if r == s == 0 else lax.ppermute(mine, ('seq', 'dp'), pairs_to)]
    unnamed x31 -> x76, local copies, waits for them, and re-layouts: 6.57 us -> 2.9 us
    ppermute x6 -> x15, waiting for transfers between devices: 6.38 us -> 3.53 us  [cyclic(): return lax.ppermute(a, axis, [(i, (i + by) % count) for i in range(count)])]
    all_gather x1 -> x0, blocking collectives: 2.4 us -> none  [body(): lows = lax.all_gather(lows, 'head', axis=2, tiled=True)]
    dynamic_slice x1 -> x0, local copies, waits for them, and re-layouts: 1.83 us -> none  [piece(): return lax.dynamic_slice_in_dim(feats, (d + r) % n_dp * part, part, 1)]
  transfers between devices with their start and end apart: 25 -> 42, of which waited for: 11 -> 12; matrix products, arithmetic and copies ran while one was open for 5% -> 2% of each run, Pallas kernels for 20% -> 15%
where the time goes in v3:
time: 156 us; the launch traced here: 155 us
  starting transfers between devices  65.1 us (42%)
  Pallas kernels  49.5 us (32%)
  waiting for transfers between devices  32.5 us (21%)
  local copies, waits for them, and re-layouts  4.97 us (3%)
  other arithmetic  2.14 us (1%)
    pallas_call x11, Pallas kernels, call(): pl.pallas_call(kernel, out_shape=out_shape, grid=(1,), in_specs=specs or...  49.5 us
    ppermute x10, starting transfers between devices, chains(): fresh[kind] = lax.ppermute(sent[-1], 'seq', pairs[kind])  23.7 us
    ppermute x10, starting transfers between devices, relay(): fresh[kind] = lax.ppermute(held[1 - kind], 'seq', pairs[kind])  19.3 us
    ppermute x7, waiting for transfers between devices, body(): got = mine if r == s == 0 else lax.ppermute(mine, ('seq', 'dp'), pairs_to)  18.8 us
    ppermute x7, starting transfers between devices, body(): got = mine if r == s == 0 else lax.ppermute(mine, ('seq', 'dp'), pairs_to)  13.1 us
    ppermute x15, starting transfers between devices, cyclic(): return lax.ppermute(a, axis, [(i, (i + by) % count) for i in range(count)])  9.03 us
    ppermute x10, waiting for transfers between devices, chains(): fresh[kind] = lax.ppermute(sent[-1], 'seq', pairs[kind])  8.1 us
    ppermute x15, waiting for transfers between devices, cyclic(): return lax.ppermute(a, axis, [(i, (i + by) % count) for i in range(count)])  3.53 us
  transfers between devices with their start and end apart: 42, of which 12 were waited for; matrix products, arithmetic and copies ran while one was open for 2% of the time, Pallas kernels for 15%

profile of v3, /device:TPU:0, one launch (start us, length us, event | category | flops | bytes accessed | tf_op | source)
XLA Modules:
  0.0 155.5 jit_solution(6005744044426547614)
XLA Ops:
  0.6 17.0 %shard_map.102 = (bf16[128,1024]{1,0:T(8,128)(2,1)}, bf16[128,1024]{1,0:T(8,128)(2,1)}) custom-call(bf16[128,2048]{1,0:T(8,128)(2,1)} %bitcast.89), custom_call_target="tpu_custom_call" | custom-call | bytes 524288 | tf_op jit(solution)/shard_map/pallas_call | solution.py:55
  17.7 3.0 %collective-permute-start = (bf16[128,1024]{1,0:T(8,128)(2,1)}, bf16[128,1024]{1,0:T(8,128)(2,1)S(1)}, u32[]{:S(2)}, u32[]{:S(2)}) collective-permute-start(bf16[128,1024]{1,0:T(8,128)(2,1)} %get-tuple-element.48), channel_id=1, source_target_pairs={{0,2},{2,0},{1,3},{3,1},{4,6},{6,4},{5,7},{7,5},{8,10},{10,8},{9,1... | collective-permute-start | bytes 786440 | tf_op jit(solution)/shard_map/ppermute | solution.py:22
  22.3 3.5 %collective-permute-start.4 = (bf16[128,1024]{1,0:T(8,128)(2,1)}, bf16[128,1024]{1,0:T(8,128)(2,1)S(1)}, u32[]{:S(2)}, u32[]{:S(2)}) collective-permute-start(bf16[128,1024]{1,0:T(8,128)(2,1)} %get-tuple-element.47.a_ref.refs_0_), channel_id=1, source_target_pairs={{0,4},{4,0},{8,12},{12,8},{1,5},{5,1},{9,13},{13,9},{2,6},{6,2},{1... | collective-permute-start | bytes 786440 | tf_op jit(solution)/shard_map/ppermute | solution.py:364
  39.4 5.2 %shard_map.105 = (f32[2,4,128,512]{3,2,1,0:T(8,128)}, f32[4,1,512]{2,1,0:T(1,128)}, f32[256,128]{1,0:T(8,128)}, f32[160,128]{1,0:T(8,128)}) custom-call(f32[320,128]{1,0:T(8,128)} %shard_map.103.refs_0_, f32[320,128]{1,0:T(8,128)} %copy-done.18, f32[320,128]{1,0:T(8,128)} %copy-done.19, f32[320,128]{1,0:T(8,128)} %copy-done.20, bf16[128,2048]{1,0:T(8,128)(2,1)} %bitcast.73, ...), custom_call_target="tpu_custom_call" | custom-call | flops 402653184 | bytes 1704192 | tf_op jit(solution)/shard_map/pallas_call | solution.py:55
  45.8 4.7 %collective-permute-start.8 = (bf16[128,512]{1,0:T(8,128)(2,1)S(1)}, bf16[128,512]{1,0:T(8,128)(2,1)S(1)}, u32[]{:S(2)}, u32[]{:S(2)}) collective-permute-start(bf16[128,512]{1,0:T(8,128)(2,1)S(1)} %get-tuple-element.97), channel_id=1, source_target_pairs={{0,4},{4,0},{8,12},{12,8},{1,5},{5,1},{9,13},{13,9},{2,6},{6,2},{1... | collective-permute-start | bytes 393224 | tf_op jit(solution)/shard_map/ppermute | solution.py:401
  50.6 2.7 %shard_map.106 = (f32[128,128]{1,0:T(8,128)}, f32[128,512]{1,0:T(8,128)}, f32[128,128]{1,0:T(8,128)}, f32[2,8,128]{2,1,0:T(8,128)}) custom-call(f32[256,128]{1,0:T(8,128)} %get-tuple-element.66.bc_ref.refs_3_, f32[160,128]{1,0:T(8,128)} %get-tuple-element.53.hp_ref.refs_4_, bf16[128,2048]{1,0:T(8,128)(2,1)} %bitcast.74, bf16[128,2048]{1,0:T(8,128)(2,1)} %bitcast.80), custom_call_target="tpu_custom_call" | custom-call | flops 67108864 | bytes 1261568 | tf_op jit(solution)/shard_map/pallas_call | solution.py:55
  56.3 2.7 %shard_map.107 = (f32[128,512]{1,0:T(8,128)}, f32[128,128]{1,0:T(8,128)}, f32[2,8,128]{2,1,0:T(8,128)}) custom-call(f32[256,128]{1,0:T(8,128)} %get-tuple-element.66.bc_ref.refs_3_, f32[160,128]{1,0:T(8,128)} %get-tuple-element.53.hp_ref.refs_4_, bf16[128,2048]{1,0:T(8,128)(2,1)} %bitcast.75, bf16[128,2048]{1,0:T(8,128)(2,1)} %bitcast.81, ...), custom_call_target="tpu_custom_call" | custom-call | flops 67108864 | bytes 1327104 | tf_op jit(solution)/shard_map/pallas_call | solution.py:55
  59.3 5.0 %collective-permute-start.11 = (bf16[128,512]{1,0:T(8,128)(2,1)S(1)}, bf16[128,512]{1,0:T(8,128)(2,1)S(1)}, u32[]{:S(2)}, u32[]{:S(2)}) collective-permute-start(bf16[128,512]{1,0:T(8,128)(2,1)S(1)} %get-tuple-element.95), channel_id=1, source_target_pairs={{0,4},{4,0},{8,12},{12,8},{1,5},{5,1},{9,13},{13,9},{2,6},{6,2},{1... | collective-permute-start | bytes 393224 | tf_op jit(solution)/shard_map/ppermute | solution.py:401
  65.0 2.6 %shard_map.108 = (f32[128,512]{1,0:T(8,128)}, f32[128,128]{1,0:T(8,128)}, f32[2,8,128]{2,1,0:T(8,128)}) custom-call(f32[256,128]{1,0:T(8,128)} %get-tuple-element.66.bc_ref.refs_3_, f32[160,128]{1,0:T(8,128)} %get-tuple-element.53.hp_ref.refs_4_, bf16[128,2048]{1,0:T(8,128)(2,1)} %bitcast.76, bf16[128,2048]{1,0:T(8,128)(2,1)} %bitcast.82, ...), custom_call_target="tpu_custom_call" | custom-call | flops 67108864 | bytes 1327104 | tf_op jit(solution)/shard_map/pallas_call | solution.py:55
  67.7 3.8 %collective-permute-start.13 = (bf16[128,512]{1,0:T(8,128)(2,1)S(1)}, bf16[128,512]{1,0:T(8,128)(2,1)S(1)}, u32[]{:S(2)}, u32[]{:S(2)}) collective-permute-start(bf16[128,512]{1,0:T(8,128)(2,1)S(1)} %get-tuple-element.93), channel_id=1, source_target_pairs={{0,4},{4,0},{8,12},{12,8},{1,5},{5,1},{9,13},{13,9},{2,6},{6,2},{1... | collective-permute-start | bytes 393224 | tf_op jit(solution)/shard_map/ppermute | solution.py:401
  72.2 2.6 %shard_map.109 = (f32[128,512]{1,0:T(8,128)}, f32[128,128]{1,0:T(8,128)}, f32[2,8,128]{2,1,0:T(8,128)}) custom-call(f32[256,128]{1,0:T(8,128)} %get-tuple-element.66.bc_ref.refs_3_, f32[160,128]{1,0:T(8,128)} %get-tuple-element.53.hp_ref.refs_4_, bf16[128,2048]{1,0:T(8,128)(2,1)} %bitcast.77, bf16[128,2048]{1,0:T(8,128)(2,1)} %bitcast.83, ...), custom_call_target="tpu_custom_call" | custom-call | flops 67108864 | bytes 1327104 | tf_op jit(solution)/shard_map/pallas_call | solution.py:55
  75.7 4.0 %collective-permute-start.15 = (bf16[128,512]{1,0:T(8,128)(2,1)S(1)}, bf16[128,512]{1,0:T(8,128)(2,1)S(1)}, u32[]{:S(2)}, u32[]{:S(2)}) collective-permute-start(bf16[128,512]{1,0:T(8,128)(2,1)S(1)} %get-tuple-element.91), channel_id=1, source_target_pairs={{0,4},{4,0},{8,12},{12,8},{1,5},{5,1},{9,13},{13,9},{2,6},{6,2},{1... | collective-permute-start | bytes 393224 | tf_op jit(solution)/shard_map/ppermute | solution.py:401
  80.5 3.0 %collective-permute-done.15 = bf16[128,512]{1,0:T(8,128)(2,1)S(1)} collective-permute-done((bf16[128,512]{1,0:T(8,128)(2,1)S(1)}, bf16[128,512]{1,0:T(8,128)(2,1)S(1)}, u32[]{:S(2)}, u32[]{:S(2)}) %collective-permute-start.15) | collective-permute-done | bytes 131104 | tf_op jit(solution)/shard_map/ppermute | solution.py:401
  83.5 3.3 %collective-permute-start.17 = (bf16[128,512]{1,0:T(8,128)(2,1)S(1)}, bf16[128,512]{1,0:T(8,128)(2,1)S(1)}, u32[]{:S(2)}, u32[]{:S(2)}) collective-permute-start(bf16[128,512]{1,0:T(8,128)(2,1)S(1)} %fusion), channel_id=1, source_target_pairs={{0,4},{4,0},{8,12},{12,8},{1,5},{5,1},{9,13},{13,9},{2,6},{6,2},{1... | collective-permute-start | bytes 393224 | tf_op jit(solution)/shard_map/ppermute | solution.py:401
  86.9 3.0 %collective-permute-done.17 = bf16[128,512]{1,0:T(8,128)(2,1)S(1)} collective-permute-done((bf16[128,512]{1,0:T(8,128)(2,1)S(1)}, bf16[128,512]{1,0:T(8,128)(2,1)S(1)}, u32[]{:S(2)}, u32[]{:S(2)}) %collective-permute-start.17) | collective-permute-done | bytes 131104 | tf_op jit(solution)/shard_map/ppermute | solution.py:401
  92.5 5.6 %shard_map.110 = (bf16[128,2048]{1,0:T(8,128)(2,1)}, f32[160,128]{1,0:T(8,128)}, f32[128,128]{1,0:T(8,128)}) custom-call(bf16[2,5,128,512]{3,2,1,0:T(8,128)(2,1)} %copy-done, bf16[128,2048]{1,0:T(8,128)(2,1)} %bitcast.78, bf16[128,2048]{1,0:T(8,128)(2,1)} %bitcast.84, f32[256,128]{1,0:T(8,128)} %get-tuple-element.66.bc_ref.refs_3_, ...), custom_call_target="tpu_custom_call" | custom-call | flops 536870912 | bytes 3924096 | tf_op jit(solution)/shard_map/pallas_call | solution.py:55
  102.6 4.7 %collective-permute-start.28 = (bf16[160,128]{1,0:T(8,128)(2,1)S(1)}, bf16[160,128]{1,0:T(8,128)(2,1)S(1)}, u32[]{:S(2)}, u32[]{:S(2)}) collective-permute-start(bf16[160,128]{1,0:T(8,128)(2,1)S(1)} %pad_maximum_fusion.mine_ref.refs_12_), channel_id=1, source_target_pairs={{0,4},{4,8},{8,12},{12,0},{2,6},{6,10},{10,14},{14,2},{1,5},{5,9},... | collective-permute-start | bytes 122888 | tf_op jit(solution)/shard_map/ppermute | solution.py:538
  107.6 2.8 %collective-permute-start.30 = (bf16[160,128]{1,0:T(8,128)(2,1)S(1)}, bf16[160,128]{1,0:T(8,128)(2,1)S(1)}, u32[]{:S(2)}, u32[]{:S(2)}) collective-permute-start(bf16[160,128]{1,0:T(8,128)(2,1)S(1)} %pad_maximum_fusion.mine_ref.refs_12_), channel_id=1, source_target_pairs={{0,12},{4,0},{8,4},{12,8},{2,14},{6,2},{10,6},{14,10},{1,13},{5,1}... | collective-permute-start | bytes 122888 | tf_op jit(solution)/shard_map/ppermute | solution.py:538
  110.5 6.6 %collective-permute-start.22 = (bf16[128,1024]{1,0:T(8,128)(2,1)S(1)}, bf16[128,1024]{1,0:T(8,128)(2,1)S(1)}, u32[]{:S(2)}, u32[]{:S(2)}) collective-permute-start(bf16[128,1024]{1,0:T(8,128)(2,1)S(1)} %collective-permute-done.7.refs_4_), channel_id=1, source_target_pairs={{0,4},{4,0},{8,12},{12,8},{1,5},{5,1},{9,13},{13,9},{2,6},{6,2},{1... | collective-permute-start | bytes 786440 | tf_op jit(solution)/shard_map/ppermute | solution.py:364
  120.7 2.4 %collective-permute-done.31.refs_16_ = bf16[160,128]{1,0:T(8,128)(2,1)S(1)} collective-permute-done((bf16[160,128]{1,0:T(8,128)(2,1)S(1)}, bf16[160,128]{1,0:T(8,128)(2,1)S(1)}, u32[]{:S(2)}, u32[]{:S(2)}) %collective-permute-start.31) | collective-permute-done | bytes 40992 | tf_op jit(solution)/shard_map/ppermute | solution.py:538
  125.4 12.9 %collective-permute-done.32.refs_17_ = bf16[160,128]{1,0:T(8,128)(2,1)S(1)} collective-permute-done((bf16[160,128]{1,0:T(8,128)(2,1)S(1)}, bf16[160,128]{1,0:T(8,128)(2,1)S(1)}, u32[]{:S(2)}, u32[]{:S(2)}) %collective-permute-start.32) | collective-permute-done | bytes 40992 | tf_op jit(solution)/shard_map/ppermute | solution.py:538
  139.8 3.4 %collective-permute-done.34.refs_19_ = bf16[160,128]{1,0:T(8,128)(2,1)S(1)} collective-permute-done((bf16[160,128]{1,0:T(8,128)(2,1)S(1)}, bf16[160,128]{1,0:T(8,128)(2,1)S(1)}, u32[]{:S(2)}, u32[]{:S(2)}) %collective-permute-start.34) | collective-permute-done | bytes 40992 | tf_op jit(solution)/shard_map/ppermute | solution.py:538
  147.1 2.9 %shard_map.111 = bf16[128,2048]{1,0:T(8,128)(2,1)} custom-call(bf16[160,128]{1,0:T(8,128)(2,1)} %copy-done.7, bf16[160,128]{1,0:T(8,128)(2,1)} %copy-done.21, bf16[1024,256]{1,0:T(8,128)(2,1)} %refs_0_.1, bf16[64,1024]{1,0:T(8,128)(2,1)} %bitcast.87, bf16[1024,256]{1,0:T(8,128)(2,1)} %copy-done.6, bf16[64,1024]{1,0:T(8,128)(2,1)} %copy-done.22), custom_call_target="tpu_custom_call" | custom-call | flops 167772160 | bytes 1392640 | tf_op jit(solution)/shard_map/pallas_call | solution.py:55
  151.5 4.0 %shard_map.112 = (f32[1024,256]{1,0:T(8,128)}, f32[64,1024]{1,0:T(8,128)}) custom-call(bf16[128,1024]{1,0:T(8,128)(2,1)} %get-tuple-element.47.a_ref.refs_0_, bf16[128,1024]{1,0:T(8,128)(2,1)} %copy-done.9, bf16[128,1024]{1,0:T(8,128)(2,1)} %copy-done.8, bf16[128,1024]{1,0:T(8,128)(2,1)} %copy-done.10, bf16[128,1024]{1,0:T(8,128)(2,1)} %copy-done.11, ...), custom_call_target="tpu_custom_call" | custom-call | flops 671088640 | bytes 3801088 | tf_op jit(solution)/shard_map/pallas_call | solution.py:55
  (168 shorter events, 42.6 us)
Async XLA Ops:
  17.7 9.5 %collective-permute-start = (bf16[128,1024]{1,0:T(8,128)(2,1)}, bf16[128,1024]{1,0:T(8,128)(2,1)S(1)}, u32[]{:S(2)}, u32[]{:S(2)}) collective-permute-start(bf16[128,1024]{1,0:T(8,128)(2,1)} %get-tuple-element.48), channel_id=1, source_target_pairs={{0,2},{2,0},{1,3},{3,1},{4,6},{6,4},{5,7},{7,5},{8,10},{10,8},{9,1... | collective-permute-start | bytes 786440 | tf_op jit(solution)/shard_map/ppermute | solution.py:22
  20.7 11.1 %collective-permute-start.5 = (bf16[128,1024]{1,0:T(8,128)(2,1)}, bf16[128,1024]{1,0:T(8,128)(2,1)S(1)}, u32[]{:S(2)}, u32[]{:S(2)}) collective-permute-start(bf16[128,1024]{1,0:T(8,128)(2,1)} %get-tuple-element.47.a_ref.refs_0_), channel_id=1, source_target_pairs={{0,0},{4,8},{8,4},{12,12},{1,1},{5,9},{9,5},{13,13},{2,2},{6,10},{... | collective-permute-start | bytes 786440 | tf_op jit(solution)/shard_map/ppermute | solution.py:364
  22.3 11.1 %collective-permute-start.4 = (bf16[128,1024]{1,0:T(8,128)(2,1)}, bf16[128,1024]{1,0:T(8,128)(2,1)S(1)}, u32[]{:S(2)}, u32[]{:S(2)}) collective-permute-start(bf16[128,1024]{1,0:T(8,128)(2,1)} %get-tuple-element.47.a_ref.refs_0_), channel_id=1, source_target_pairs={{0,4},{4,0},{8,12},{12,8},{1,5},{5,1},{9,13},{13,9},{2,6},{6,2},{1... | collective-permute-start | bytes 786440 | tf_op jit(solution)/shard_map/ppermute | solution.py:364
  30.0 6.1 %collective-permute-start.1 = (f32[320,128]{1,0:T(8,128)}, f32[320,128]{1,0:T(8,128)S(1)}, u32[]{:S(2)}, u32[]{:S(2)}) collective-permute-start(f32[320,128]{1,0:T(8,128)} %shard_map.104), channel_id=1, source_target_pairs={{0,2},{2,0},{1,3},{3,1},{4,6},{6,4},{5,7},{7,5},{8,10},{10,8},{9,1... | collective-permute-start | bytes 491528 | tf_op jit(solution)/shard_map/ppermute | solution.py:22
  31.8 6.9 %collective-permute-start.6 = (bf16[128,1024]{1,0:T(8,128)(2,1)S(1)}, bf16[128,1024]{1,0:T(8,128)(2,1)S(1)}, u32[]{:S(2)}, u32[]{:S(2)}) collective-permute-start(bf16[128,1024]{1,0:T(8,128)(2,1)S(1)} %collective-permute-done.5.refs_2_), channel_id=1, source_target_pairs={{0,4},{4,0},{8,12},{12,8},{1,5},{5,1},{9,13},{13,9},{2,6},{6,2},{1... | collective-permute-start | bytes 786440 | tf_op jit(solution)/shard_map/ppermute | solution.py:364
  45.8 8.8 %collective-permute-start.8 = (bf16[128,512]{1,0:T(8,128)(2,1)S(1)}, bf16[128,512]{1,0:T(8,128)(2,1)S(1)}, u32[]{:S(2)}, u32[]{:S(2)}) collective-permute-start(bf16[128,512]{1,0:T(8,128)(2,1)S(1)} %get-tuple-element.97), channel_id=1, source_target_pairs={{0,4},{4,0},{8,12},{12,8},{1,5},{5,1},{9,13},{13,9},{2,6},{6,2},{1... | collective-permute-start | bytes 393224 | tf_op jit(solution)/shard_map/ppermute | solution.py:401
  50.4 8.7 %collective-permute-start.9 = (bf16[128,512]{1,0:T(8,128)(2,1)S(1)}, bf16[128,512]{1,0:T(8,128)(2,1)S(1)}, u32[]{:S(2)}, u32[]{:S(2)}) collective-permute-start(bf16[128,512]{1,0:T(8,128)(2,1)S(1)} %get-tuple-element.96), channel_id=1, source_target_pairs={{0,4},{4,0},{8,12},{12,8},{1,5},{5,1},{9,13},{13,9},{2,6},{6,2},{1... | collective-permute-start | bytes 393224 | tf_op jit(solution)/shard_map/ppermute | solution.py:401
  59.3 8.3 %collective-permute-start.11 = (bf16[128,512]{1,0:T(8,128)(2,1)S(1)}, bf16[128,512]{1,0:T(8,128)(2,1)S(1)}, u32[]{:S(2)}, u32[]{:S(2)}) collective-permute-start(bf16[128,512]{1,0:T(8,128)(2,1)S(1)} %get-tuple-element.95), channel_id=1, source_target_pairs={{0,4},{4,0},{8,12},{12,8},{1,5},{5,1},{9,13},{13,9},{2,6},{6,2},{1... | collective-permute-start | bytes 393224 | tf_op jit(solution)/shard_map/ppermute | solution.py:401
  67.7 7.9 %collective-permute-start.13 = (bf16[128,512]{1,0:T(8,128)(2,1)S(1)}, bf16[128,512]{1,0:T(8,128)(2,1)S(1)}, u32[]{:S(2)}, u32[]{:S(2)}) collective-permute-start(bf16[128,512]{1,0:T(8,128)(2,1)S(1)} %get-tuple-element.93), channel_id=1, source_target_pairs={{0,4},{4,0},{8,12},{12,8},{1,5},{5,1},{9,13},{13,9},{2,6},{6,2},{1... | collective-permute-start | bytes 393224 | tf_op jit(solution)/shard_map/ppermute | solution.py:401
  75.7 7.8 %collective-permute-start.15 = (bf16[128,512]{1,0:T(8,128)(2,1)S(1)}, bf16[128,512]{1,0:T(8,128)(2,1)S(1)}, u32[]{:S(2)}, u32[]{:S(2)}) collective-permute-start(bf16[128,512]{1,0:T(8,128)(2,1)S(1)} %get-tuple-element.91), channel_id=1, source_target_pairs={{0,4},{4,0},{8,12},{12,8},{1,5},{5,1},{9,13},{13,9},{2,6},{6,2},{1... | collective-permute-start | bytes 393224 | tf_op jit(solution)/shard_map/ppermute | solution.py:401
  83.5 6.4 %collective-permute-start.17 = (bf16[128,512]{1,0:T(8,128)(2,1)S(1)}, bf16[128,512]{1,0:T(8,128)(2,1)S(1)}, u32[]{:S(2)}, u32[]{:S(2)}) collective-permute-start(bf16[128,512]{1,0:T(8,128)(2,1)S(1)} %fusion), channel_id=1, source_target_pairs={{0,4},{4,0},{8,12},{12,8},{1,5},{5,1},{9,13},{13,9},{2,6},{6,2},{1... | collective-permute-start | bytes 393224 | tf_op jit(solution)/shard_map/ppermute | solution.py:401
  90.0 11.1 %collective-permute-start.23 = (bf16[128,1024]{1,0:T(8,128)(2,1)S(1)}, bf16[128,1024]{1,0:T(8,128)(2,1)S(1)}, u32[]{:S(2)}, u32[]{:S(2)}) collective-permute-start(bf16[128,1024]{1,0:T(8,128)(2,1)S(1)} %copy-done.5), channel_id=1, source_target_pairs={{0,4},{4,0},{8,12},{12,8},{1,5},{5,1},{9,13},{13,9},{2,6},{6,2},{1... | collective-permute-start | bytes 786440 | tf_op jit(solution)/shard_map/ppermute | solution.py:364
  91.9 15.7 %collective-permute-start.20 = (bf16[1024,256]{1,0:T(8,128)(2,1)S(1)}, bf16[1024,256]{1,0:T(8,128)(2,1)S(1)}, u32[]{:S(2)}, u32[]{:S(2)}) collective-permute-start(bf16[1024,256]{1,0:T(8,128)(2,1)S(1)} %copy-done.1), channel_id=1, source_target_pairs={{0,2},{2,0},{1,3},{3,1},{4,6},{6,4},{5,7},{7,5},{8,10},{10,8},{9,1... | collective-permute-start | bytes 1572872 | tf_op jit(solution)/shard_map/ppermute | solution.py:22
  98.1 9.2 %collective-permute-start.21 = (bf16[64,1024]{1,0:T(8,128)(2,1)S(1)}, bf16[64,1024]{1,0:T(8,128)(2,1)S(1)}, u32[]{:S(2)}, u32[]{:S(2)}) collective-permute-start(bf16[64,1024]{1,0:T(8,128)(2,1)S(1)} %bitcast.88), channel_id=1, source_target_pairs={{0,2},{2,0},{1,3},{3,1},{4,6},{6,4},{5,7},{7,5},{8,10},{10,8},{9,1... | collective-permute-start | bytes 393224 | tf_op jit(solution)/shard_map/ppermute | solution.py:22
  99.7 17.4 %collective-permute-start.24 = (bf16[128,1024]{1,0:T(8,128)(2,1)S(1)}, bf16[128,1024]{1,0:T(8,128)(2,1)S(1)}, u32[]{:S(2)}, u32[]{:S(2)}) collective-permute-start(bf16[128,1024]{1,0:T(8,128)(2,1)S(1)} %copy-done.5), channel_id=1, source_target_pairs={{0,0},{4,8},{8,4},{12,12},{1,1},{5,9},{9,5},{13,13},{2,2},{6,10},{... | collective-permute-start | bytes 786440 | tf_op jit(solution)/shard_map/ppermute | solution.py:364
  101.1 16.1 %collective-permute-start.26 = (bf16[128,1024]{1,0:T(8,128)(2,1)S(1)}, bf16[128,1024]{1,0:T(8,128)(2,1)S(1)}, u32[]{:S(2)}, u32[]{:S(2)}) collective-permute-start(bf16[128,1024]{1,0:T(8,128)(2,1)S(1)} %collective-permute-done.23.refs_7_), channel_id=1, source_target_pairs={{0,0},{4,8},{8,4},{12,12},{1,1},{5,9},{9,5},{13,13},{2,2},{6,10},{... | collective-permute-start | bytes 786440 | tf_op jit(solution)/shard_map/ppermute | solution.py:364
  102.6 7.8 %collective-permute-start.28 = (bf16[160,128]{1,0:T(8,128)(2,1)S(1)}, bf16[160,128]{1,0:T(8,128)(2,1)S(1)}, u32[]{:S(2)}, u32[]{:S(2)}) collective-permute-start(bf16[160,128]{1,0:T(8,128)(2,1)S(1)} %pad_maximum_fusion.mine_ref.refs_12_), channel_id=1, source_target_pairs={{0,4},{4,8},{8,12},{12,0},{2,6},{6,10},{10,14},{14,2},{1,5},{5,9},... | collective-permute-start | bytes 122888 | tf_op jit(solution)/shard_map/ppermute | solution.py:538
  107.3 11.8 %collective-permute-start.29 = (bf16[160,128]{1,0:T(8,128)(2,1)S(1)}, bf16[160,128]{1,0:T(8,128)(2,1)S(1)}, u32[]{:S(2)}, u32[]{:S(2)}) collective-permute-start(bf16[160,128]{1,0:T(8,128)(2,1)S(1)} %pad_maximum_fusion.mine_ref.refs_12_), channel_id=1, source_target_pairs={{0,8},{4,12},{8,0},{12,4},{2,10},{6,14},{10,2},{14,6},{1,9},{5,13}... | collective-permute-start | bytes 122888 | tf_op jit(solution)/shard_map/ppermute | solution.py:538
  107.6 12.3 %collective-permute-start.30 = (bf16[160,128]{1,0:T(8,128)(2,1)S(1)}, bf16[160,128]{1,0:T(8,128)(2,1)S(1)}, u32[]{:S(2)}, u32[]{:S(2)}) collective-permute-start(bf16[160,128]{1,0:T(8,128)(2,1)S(1)} %pad_maximum_fusion.mine_ref.refs_12_), channel_id=1, source_target_pairs={{0,12},{4,0},{8,4},{12,8},{2,14},{6,2},{10,6},{14,10},{1,13},{5,1}... | collective-permute-start | bytes 122888 | tf_op jit(solution)/shard_map/ppermute | solution.py:538
  110.5 39.5 %collective-permute-start.22 = (bf16[128,1024]{1,0:T(8,128)(2,1)S(1)}, bf16[128,1024]{1,0:T(8,128)(2,1)S(1)}, u32[]{:S(2)}, u32[]{:S(2)}) collective-permute-start(bf16[128,1024]{1,0:T(8,128)(2,1)S(1)} %collective-permute-done.7.refs_4_), channel_id=1, source_target_pairs={{0,4},{4,0},{8,12},{12,8},{1,5},{5,1},{9,13},{13,9},{2,6},{6,2},{1... | collective-permute-start | bytes 786440 | tf_op jit(solution)/shard_map/ppermute | solution.py:364
  117.1 32.9 %collective-permute-start.25 = (bf16[128,1024]{1,0:T(8,128)(2,1)S(1)}, bf16[128,1024]{1,0:T(8,128)(2,1)S(1)}, u32[]{:S(2)}, u32[]{:S(2)}) collective-permute-start(bf16[128,1024]{1,0:T(8,128)(2,1)S(1)} %collective-permute-done.24.refs_8_), channel_id=1, source_target_pairs={{0,4},{4,0},{8,12},{12,8},{1,5},{5,1},{9,13},{13,9},{2,6},{6,2},{1... | collective-permute-start | bytes 786440 | tf_op jit(solution)/shard_map/ppermute | solution.py:364
  117.1 32.9 %collective-permute-start.27 = (bf16[128,1024]{1,0:T(8,128)(2,1)S(1)}, bf16[128,1024]{1,0:T(8,128)(2,1)S(1)}, u32[]{:S(2)}, u32[]{:S(2)}) collective-permute-start(bf16[128,1024]{1,0:T(8,128)(2,1)S(1)} %collective-permute-done.26.refs_10_), channel_id=1, source_target_pairs={{0,4},{4,0},{8,12},{12,8},{1,5},{5,1},{9,13},{13,9},{2,6},{6,2},{1... | collective-permute-start | bytes 786440 | tf_op jit(solution)/shard_map/ppermute | solution.py:364
  120.0 18.4 %collective-permute-start.32 = (bf16[160,128]{1,0:T(8,128)(2,1)S(1)}, bf16[160,128]{1,0:T(8,128)(2,1)S(1)}, u32[]{:S(2)}, u32[]{:S(2)}) collective-permute-start(bf16[160,128]{1,0:T(8,128)(2,1)S(1)} %pad_maximum_fusion.mine_ref.refs_12_), channel_id=1, source_target_pairs={{0,6},{4,10},{8,14},{12,2},{2,4},{6,8},{10,12},{14,0},{1,7},{5,11}... | collective-permute-start | bytes 122888 | tf_op jit(solution)/shard_map/ppermute | solution.py:538
  123.1 16.7 %collective-permute-start.33 = (bf16[160,128]{1,0:T(8,128)(2,1)S(1)}, bf16[160,128]{1,0:T(8,128)(2,1)S(1)}, u32[]{:S(2)}, u32[]{:S(2)}) collective-permute-start(bf16[160,128]{1,0:T(8,128)(2,1)S(1)} %pad_maximum_fusion.mine_ref.refs_12_), channel_id=1, source_target_pairs={{0,10},{4,14},{8,2},{12,6},{2,8},{6,12},{10,0},{14,4},{1,11},{5,15... | collective-permute-start | bytes 122888 | tf_op jit(solution)/shard_map/ppermute | solution.py:538
  (56 other events, 646.0 us)

commit v4 on v3

--- a/solution.py
+++ b/solution.py
@@ -7,10 +7,10 @@
 from jax.experimental.pallas import tpu as pltpu
 from jax.sharding import PartitionSpec as P
 
-CHUNKS = 4
+CHUNKS = 2
 PARTS = 4
-EARLY = 2
-GROUPS = 8
+EARLY = (3, 0)
+EAGER = 2
 BF = jnp.bfloat16
 F32 = jnp.float32
 TOP = lax.Precision.HIGHEST
@@ -83,18 +83,13 @@
     return groups, pairs
 
 
-def split_kernel(count, a_ref, *refs):
-    outs, sems = refs[:count], refs[count]
+def split_kernel(a_ref, *outs):
+    count = len(outs)
     me = lax.axis_index("dp")
     part = outs[0].shape[1]
-    copies = []
     for r in range(count):
         at = pl.multiple_of(lax.rem(me + r, count) * part, 128)
-        copies.append(pltpu.make_async_copy(a_ref.at[:, pl.ds(at, part)], outs[r], sems.at[r]))
-    for copy in copies:
-        copy.start()
-    for copy in copies:
-        copy.wait()
+        outs[r][...] = a_ref[:, pl.ds(at, part)]
 
 
 def project_kernel(a_ref, bc_ref, dt_ref, out_ref):
@@ -122,7 +117,8 @@
 
 def state_kernel(count, size, *refs):
     proj = refs[:count]
-    x_ref, g_ref, rate_ref, bias_ref, own_ref, decay_ref, bc_ref, hp_ref = refs[count:]
+    x_ref, g_ref, rate_ref, bias_ref, own_ref, decay_ref, bc_ref, hp_ref = refs[count : count + 8]
+    firsts = refs[count + 8 :]
     heads = rate_ref.shape[1]
     rows = x_ref.shape[0]
     rate, bias = rate_ref[...].T, bias_ref[...].T
@@ -144,20 +140,24 @@
     decay = jnp.exp(last)
     for k, part in enumerate((pre, dt, cum, grow, w)):
         hp_ref[k * heads : (k + 1) * heads, :] = part
-    way = lax.rem(lax.axis_index("seq"), 2)
-    kinds = ((w, x_ref, bc[:rows], way), (grow, g_ref, bc[rows:], 1 - way))
-    for scale, ref, vec, place in kinds:
+    lowest = lax.axis_index("seq") == 0
+    sides = []
+    for vec in (bc[:rows], bc[rows:]):
         high, low = halves(vec.T)
-        wide = jnp.concatenate([high, low], axis=1)
-        for k in range(chunks):
-            pick = head_lanes(heads, step, size, k * step)
-            if place is way:
-                decay_ref[k] = jnp.sum(pick * decay, axis=0, keepdims=True)
-            value = spread(scale, pick.astype(BF)) * ref[:, k * step : (k + 1) * step].astype(F32)
+        sides.append((jnp.concatenate([high, low], axis=1), high))
+    for k in range(chunks):
+        pick = head_lanes(heads, step, size, k * step)
+        decay_ref[k] = jnp.sum(pick * decay, axis=0, keepdims=True)
+        pick = pick.astype(BF)
+        both = []
+        for kind, (scale, ref) in enumerate(((w, x_ref), (grow, g_ref))):
+            wide, high = sides[kind]
+            value = spread(scale, pick) * ref[:, k * step : (k + 1) * step].astype(F32)
             top, rest = halves(value)
-            own_ref[place, k] = mm(wide, jnp.concatenate([top, top], axis=0), 1, 0) + mm(
-                high, rest, 1, 0
-            )
+            value = mm(wide, jnp.concatenate([top, top], axis=0), 1, 0) + mm(high, rest, 1, 0)
+            own_ref[kind, k] = value
+            both.append(value)
+        firsts[k][...] = jnp.where(lowest, both[0], both[1]).astype(BF)
 
 
 def inner_kernel(first, pairs, size, bc_ref, hp_ref, x_ref, g_ref, *refs):
@@ -211,7 +211,6 @@
     store_ref, x_ref, g_ref, bc_ref, hp_ref, decay_ref, rate_ref = refs[:7]
     gxs, dss, sums = (refs[7 + k * parts : 7 + (k + 1) * parts] for k in range(3))
     grad_ref, keep_ref, give_ref, wv_ref, eu_ref, io_ref = refs[7 + 3 * parts :]
-    odd = lax.rem(lax.axis_index("seq"), 2)
     rate = rate_ref[...].T
     rows, width = x_ref.shape
     heads = rate_ref.shape[1]
@@ -230,7 +229,7 @@
         place = slice(k * step, (k + 1) * step)
         late = slice(width + k * step, width + (k + 1) * step)
         pick = head_lanes(heads, step, size, k * step).astype(BF)
-        incoming, outgoing = store_ref[1 - odd, k], store_ref[odd, k]
+        incoming, outgoing = store_ref[0, k], store_ref[1, k]
         u = mm(c_wide, jnp.concatenate([incoming, incoming], axis=0), 1, 0)
         v = mm(b_wide, jnp.concatenate([outgoing, outgoing], axis=0), 1, 0)
         scale = spread(w, pick)
@@ -291,7 +290,7 @@
             at_col = pl.multiple_of(lax.rem(core + k, 2) * half, 128)
             at_row = pl.multiple_of(lax.rem(core + k, 2) * heads, 16)
             term = mm(ref[0:half, :], refs[2 * r][:, pl.ds(at_col, half)], 0, 1)
-            term = term + mm(ref[half : mine_ref.shape[0], :], refs[2 * r + 1][pl.ds(at_row, heads), :], 0, 0)
+            term = term + mm(ref[half:, :], refs[2 * r + 1][pl.ds(at_row, heads), :], 0, 0)
             total = term if total is None else total + term
         out_ref[:, pl.ds(at, part)] = total.astype(BF)
 
@@ -301,9 +300,8 @@
     toks, lows = refs[:count], refs[count:-6]
     bc_ref, dt_ref, tok_ref, low_ref, tok_sem, low_sem = refs[-6:]
     rows = toks[0].shape[0]
-    share = lows[0].shape[0]
-    per = lows[n_dp * n_seq].shape[0] // share
-    core, place = lax.axis_index("head"), lax.axis_index("seq")
+    share = lows[0].shape[1]
+    core, place, me = lax.axis_index("head"), lax.axis_index("seq"), lax.axis_index("dp")
     even = lax.rem(place, 2) == 0
     copies = []
     for r in range(n_dp):
@@ -319,16 +317,13 @@
             copies.append((fits, copy))
     for r in range(n_dp):
         for s in range(n_seq):
-            block = lax.rem(place - s + n_seq, n_seq)
-            at = pl.multiple_of(block * rows, 128)
+            index = s * n_dp + lax.rem(me - r + n_dp, n_dp)
             for k in range(2):
-                index = r * n_seq + s
                 row = pl.multiple_of(lax.rem(core + k, 2) * share, 16)
-                source = lows[index]
-                if k == 1:
-                    source = lows[n_dp * n_seq + index // per].at[pl.ds(index % per * share, share)]
                 copy = pltpu.make_async_copy(
-                    source, low_ref.at[r, pl.ds(row, share), pl.ds(at, rows)], low_sem.at[index, k]
+                    lows[k].at[index],
+                    low_ref.at[r, pl.ds(row, share), pl.ds(s * rows, rows)],
+                    low_sem.at[r * n_seq + s, k],
                 )
                 copies.append((None, copy))
     for fits, copy in copies:
@@ -368,60 +363,31 @@
     return found, slots, held
 
 
-def chains(own, decay, inner):
+def chains(first, own, decay, inner, early):
     count = lax.axis_size("seq")
     place = lax.axis_index("seq")
-    chunks = own.shape[1]
-    even = lax.rem(place, 2) == 0
-    groups, pairs = matchings(count)
+    chunks = len(first)
     store = jnp.zeros((2, chunks + 1) + own.shape[2:], BF)
-    got = [None, None]
-    done, todo = [], list(inner)
-    ends = (place == 0) | (place == count - 1)
-    for slot in range(1, count + chunks - 1):
-        fresh, sent = [None, None], []
-        for kind in (0, 1):
-            used = any(
-                0 <= slot - hop < chunks for i, j in groups[kind] for hop in (j, count - j)
-            )
-            if not used:
-                continue
-            goes_up = even if kind == 0 else ~even
-            chunk = jnp.where(goes_up, slot - place - 1, slot - count + place)
-            chunk = jnp.clip(chunk, 0, chunks - 1)
-            zero = jnp.zeros_like(chunk)
-            value = lax.dynamic_slice(
-                own, (zero + kind, chunk, zero, zero), (1, 1) + own.shape[2:]
-            )[0, 0]
-            before = got[1 - kind]
-            if before is not None:
-                kept = before.astype(F32) * lax.dynamic_index_in_dim(decay, chunk, 0, False)
-                value = value + (jnp.where(ends, 0.0, kept) if kind == 0 else kept)
-            sent.append(value.astype(BF))
-            fresh[kind] = lax.ppermute(sent[-1], "seq", pairs[kind])
-        if todo:
-            done.append(todo.pop(0)(*sent))
-        ready = [a for a in fresh if a is not None] + ([done[-1][0]] if done else [])
-        got = list(fresh)
-        if len(ready) > 1:
-            kept = lax.optimization_barrier(tuple(ready))
-            live = [k for k in (0, 1) if fresh[k] is not None]
-            for k, a in zip(live, kept):
-                got[k] = a
-        for kind in (0, 1):
-            if got[kind] is None:
-                continue
-            below = ~even if kind == 0 else even
-            chunk = jnp.where(below, slot - place, slot - count + place + 1)
-            fits = (chunk >= 0) & (chunk < chunks)
-            if kind == 1:
-                fits = fits & ~ends
-            chunk = jnp.where(fits, chunk, chunks)
-            zero = jnp.zeros_like(chunk)
-            store = lax.dynamic_update_slice(
-                store, got[kind][None, None], (zero + kind, chunk, zero, zero)
-            )
-    done += [make() for make in todo]
+    got = list(first)
+    done = [make() for make in inner[:EAGER]]
+    for hop in range(1, count):
+        to = {i: i for i in range(count)}
+        for i in (hop - 1, count - hop - 1):
+            to[i], to[i + 1] = i + 1, i
+        for k in range(chunks):
+            sent = got[k]
+            if hop > 1:
+                value = jnp.where(place == hop - 1, own[0, k], own[1, k])
+                sent = (value + decay[k] * sent.astype(F32)).astype(BF)
+            if hop == 2 and k == 0:
+                sent = after(sent, *early)
+                done += [make(sent) for make in inner[EAGER:]]
+            got[k] = lax.ppermute(sent, "seq", sorted(to.items()))
+            kind = jnp.where(place == hop, 0, 1)
+            fits = (place == hop) | (place == count - hop - 1)
+            at = jnp.where(fits, k, chunks)
+            zero = jnp.zeros_like(at)
+            store = lax.dynamic_update_slice(store, got[k][None, None], (kind, at, zero, zero))
     return store, done
 
 
@@ -436,33 +402,31 @@
     w_dt = w_dt.T
     rate, bias = decay_rate[None], dt_bias[None]
 
-    pieces = call(
-        functools.partial(split_kernel, n_dp),
-        [struct((rows, part), BF)] * n_dp,
-        0,
-        feats,
-        scratch=[pltpu.SemaphoreType.DMA((n_dp,))],
-        specs=[ANY],
-        out_specs=[ANY] * n_dp,
-    )
+    pieces = call(split_kernel, [struct((rows, part), BF)] * n_dp, 0, feats)
     items = [pieces[0]] + [cyclic(pieces[r], "dp", r) for r in range(1, n_dp)]
-    first = project(items[0], w_bc, w_dt)
-    partials = [first] + [
+    groups = items[:1]
+    if n_dp > 1:
+        groups.append(items[1] if n_dp == 2 else jnp.concatenate(items[1:], axis=0))
+    cuts = [min(1 + hop, n_seq) for hop in EARLY[: len(groups)]]
+    moved = [relay(a, range(1, cut)) for a, cut in zip(groups, cuts)]
+    early = [a for m in moved[1:] for a in m[0]] + moved[0][0][4:]
+    near = moved[0][0]
+    partials = [project(items[0], w_bc, w_dt)] + [
         cyclic(project(items[r], w_bc, w_dt), "dp", -r) for r in range(1, n_dp)
     ]
+    partials[1:] = [after(a, *near[:2]) for a in partials[1:]]
     proj = partials + [cyclic(a, "head", 1) for a in partials]
-    cut = min(1 + EARLY, n_seq)
-    early, slots, held = relay(items[0], range(1, cut))
-    x = after(x, *early)
+    x = after(x, *near[2:4])
     step = width // CHUNKS
-    own, decay, bc, hp = call(
+    own, decay, bc, hp, *first = call(
         functools.partial(state_kernel, 2 * n_dp, size),
         (
             struct((2, CHUNKS, state_n, step), F32),
             struct((CHUNKS, 1, step), F32),
             struct((2 * rows, state_n), F32),
             struct((5 * heads, rows), F32),
-        ),
+        )
+        + (struct((state_n, step), BF),) * CHUNKS,
         12 * rows * width * state_n,
         *proj,
         x,
@@ -496,7 +460,7 @@
             out = out[1:]
         return out
 
-    store, inners = chains(own, decay, [functools.partial(inner, q) for q in range(PARTS)])
+    store, inners = chains(first, own, decay, [functools.partial(inner, q) for q in range(PARTS)], early)
     grad_x, keep, give = call(
         functools.partial(outer_kernel, size, PARTS),
         (
@@ -527,49 +491,39 @@
     weights = [w_bc, w_dt]
     for r in range(1, n_dp):
         weights += [cyclic(w_bc_later, "dp", r), cyclic(w_dt_later, "dp", r)]
-    lows = []
-    for r in range(n_dp):
-        for s in range(n_seq):
-            pairs_to = [
-                (j * n_dp + i, (j + s) % n_seq * n_dp + (i + r) % n_dp)
-                for i in range(n_dp)
-                for j in range(n_seq)
-            ]
-            got = mine if r == s == 0 else lax.ppermute(mine, ("seq", "dp"), pairs_to)
-            lows.append(got)
-    per = -(-len(lows) // GROUPS)
-    groups = [lows[k : k + per] for k in range(0, len(lows), per)]
-    swapped = [cyclic(a[0] if per == 1 else jnp.concatenate(a, axis=0), "head", 1) for a in groups]
+    count = n_dp * n_seq
+    lows = lax.all_to_all(
+        jnp.broadcast_to(mine[None], (count,) + mine.shape), ("seq", "dp"), 0, 0, tiled=True
+    )
+    swapped = cyclic(lows, "head", 1)
+    other = cyclic(mine, "head", 1)
     grads = call(
         functools.partial(token_kernel, n_dp),
         struct((rows, width), BF),
         2 * rows * width * (2 * state_n + 2 * heads),
-        lows[0],
-        swapped[0],
+        mine,
+        other,
         *weights,
     )
-    held = after(tuple(held), store)
-    found, rest, _ = relay(items[0], range(cut, n_seq), list(held))
-    slots = [(0, 0)] + slots + rest
-    toks = [items[0]] + early + found
-    if n_dp > 1:
-        others = items[1] if n_dp == 2 else jnp.concatenate(items[1:], axis=0)
-        found, _, _ = relay(after(others, store), range(1, n_seq))
-        toks += [others] + found
+    toks = []
+    for a, cut, (found, near, held) in zip(groups, cuts, moved):
+        rest, far, _ = relay(a, range(cut, n_seq), list(after(tuple(held), store)))
+        slots = [(0, 0)] + near + far
+        toks += [a] + found + rest
     cols = 2 * (rows + heads)
     grad_bc, grad_dt = call(
         functools.partial(weight_kernel, 1.0 / (rows * n_seq * n_dp), n_dp, n_seq, slots),
         (struct((part, 2 * state_n), F32), struct((2 * heads, part), F32)),
         2 * n_dp * n_seq * rows * part * cols,
         *toks,
-        *lows,
-        *swapped,
-        specs=[ANY] * (len(toks) + len(lows) + len(swapped)),
+        lows,
+        swapped,
+        specs=[ANY] * (len(toks) + 2),
         scratch=(
             pltpu.VMEM((n_dp, n_seq * rows, part), BF),
             pltpu.VMEM((n_dp, cols, n_seq * rows), BF),
             pltpu.SemaphoreType.DMA((n_dp, len(slots))),
-            pltpu.SemaphoreType.DMA((len(lows), 2)),
+            pltpu.SemaphoreType.DMA((count, 2)),
         ),
     )
     return grad_x[None], grads[None], grad_bc, grad_dt.T

time: 156 us -> 123 us (0.79)
  starting transfers between devices: 65.1 us -> 46 us
  Pallas kernels: 49.5 us -> 33.6 us
  local copies, waits for them, and re-layouts: 4.97 us -> 7.91 us
    ppermute x17 -> x6, starting transfers between devices: 36.8 us -> 9.61 us  [chains(): got[k] = lax.ppermute(sent, 'seq', sorted(to.items()))]
    pallas_call x11, Pallas kernels: 49.5 us -> 33.6 us  [call(): pl.pallas_call(kernel, out_shape=out_shape, grid=(1,), in_specs=specs or...]
    ppermute x17 -> x6, waiting for transfers between devices: 26.9 us -> 13 us  [chains(): got[k] = lax.ppermute(sent, 'seq', sorted(to.items()))]
    ppermute x10, waiting for transfers between devices: 2.03 us -> 11.7 us  [relay(): fresh[kind] = lax.ppermute(held[1 - kind], 'seq', pairs[kind])]
    ppermute x10, starting transfers between devices: 19.3 us -> 24.8 us  [relay(): fresh[kind] = lax.ppermute(held[1 - kind], 'seq', pairs[kind])]
    all_to_all x0 -> x1, starting transfers between devices: none -> 3.43 us  [body(): lax.all_to_all(jnp.broadcast_to(mine[None], (count,) + mine.shape), ('seq...]
    ppermute x15 -> x9, waiting for transfers between devices: 3.53 us -> 6.84 us  [cyclic(): return lax.ppermute(a, axis, [(i, (i + by) % count) for i in range(count)])]
    unnamed x76 -> x50, local copies, waits for them, and re-layouts: 2.9 us -> 5.4 us
  transfers between devices with their start and end apart: 42 -> 26, of which waited for: 12 -> 8; matrix products, arithmetic and copies ran while one was open for 2% -> 3% of each run, Pallas kernels for 15% -> 14%
where the time goes in v4:
time: 123 us
  starting transfers between devices  46 us (37%)
  Pallas kernels  33.6 us (27%)
  waiting for transfers between devices  31.5 us (26%)
  local copies, waits for them, and re-layouts  7.91 us (6%)
  other arithmetic  2.54 us (2%)
    pallas_call x11, Pallas kernels, call(): pl.pallas_call(kernel, out_shape=out_shape, grid=(1,), in_specs=specs or...  33.6 us
    ppermute x10, starting transfers between devices, relay(): fresh[kind] = lax.ppermute(held[1 - kind], 'seq', pairs[kind])  24.8 us
    ppermute x6, waiting for transfers between devices, chains(): got[k] = lax.ppermute(sent, 'seq', sorted(to.items()))  13 us
    ppermute x10, waiting for transfers between devices, relay(): fresh[kind] = lax.ppermute(held[1 - kind], 'seq', pairs[kind])  11.7 us
    ppermute x6, starting transfers between devices, chains(): got[k] = lax.ppermute(sent, 'seq', sorted(to.items()))  9.61 us
    ppermute x9, starting transfers between devices, cyclic(): return lax.ppermute(a, axis, [(i, (i + by) % count) for i in range(count)])  8.2 us
    ppermute x9, waiting for transfers between devices, cyclic(): return lax.ppermute(a, axis, [(i, (i + by) % count) for i in range(count)])  6.84 us
    unnamed x50, local copies, waits for them, and re-layouts  5.4 us
  transfers between devices with their start and end apart: 26, of which 8 were waited for; matrix products, arithmetic and copies ran while one was open for 3% of the time, Pallas kernels for 14%

profile of v4, /device:TPU:0, one launch (start us, length us, event | category | flops | bytes accessed | tf_op | source)
XLA Modules:
  0.0 122.6 jit_solution(14618022629701232522)
XLA Ops:
  2.5 2.9 %collective-permute-start = (bf16[128,1024]{1,0:T(8,128)(2,1)}, bf16[128,1024]{1,0:T(8,128)(2,1)S(1)}, u32[]{:S(2)}, u32[]{:S(2)}) collective-permute-start(bf16[128,1024]{1,0:T(8,128)(2,1)} %get-tuple-element.39), channel_id=1, source_target_pairs={{0,2},{2,0},{1,3},{3,1},{4,6},{6,4},{5,7},{7,5},{8,10},{10,8},{9,1... | collective-permute-start | bytes 786440 | tf_op jit(solution)/shard_map/ppermute | solution.py:22
  7.0 3.5 %collective-permute-start.2 = (bf16[128,1024]{1,0:T(8,128)(2,1)}, bf16[128,1024]{1,0:T(8,128)(2,1)S(1)}, u32[]{:S(2)}, u32[]{:S(2)}) collective-permute-start(bf16[128,1024]{1,0:T(8,128)(2,1)} %get-tuple-element.38.a_ref.refs_0_), channel_id=1, source_target_pairs={{0,4},{4,0},{8,12},{12,8},{1,5},{5,1},{9,13},{13,9},{2,6},{6,2},{1... | collective-permute-start | bytes 786440 | tf_op jit(solution)/shard_map/ppermute | solution.py:359
  12.7 2.1 %shard_map.104 = f32[320,128]{1,0:T(8,128)} custom-call(bf16[128,1024]{1,0:T(8,128)(2,1)} %copy-done.5, bf16[1024,256]{1,0:T(8,128)(2,1)} %refs_0_.1, bf16[64,1024]{1,0:T(8,128)(2,1)} %bitcast.51), custom_call_target="tpu_custom_call" | custom-call | flops 83886080 | bytes 917504 | tf_op jit(solution)/shard_map/pallas_call | solution.py:55
  18.8 2.1 %shard_map.103.refs_0_ = f32[320,128]{1,0:T(8,128)} custom-call(bf16[128,1024]{1,0:T(8,128)(2,1)} %get-tuple-element.38.a_ref.refs_0_, bf16[1024,256]{1,0:T(8,128)(2,1)} %refs_0_.1, bf16[64,1024]{1,0:T(8,128)(2,1)} %bitcast.52), custom_call_target="tpu_custom_call" | custom-call | flops 83886080 | bytes 917504 | tf_op jit(solution)/shard_map/pallas_call | solution.py:55
  21.4 2.0 %collective-permute-done.6.refs_3_ = bf16[128,1024]{1,0:T(8,128)(2,1)S(1)} collective-permute-done((bf16[128,1024]{1,0:T(8,128)(2,1)S(1)}, bf16[128,1024]{1,0:T(8,128)(2,1)S(1)}, u32[]{:S(2)}, u32[]{:S(2)}) %collective-permute-start.6) | collective-permute-done | bytes 262176 | tf_op jit(solution)/shard_map/ppermute | solution.py:359
  24.2 4.9 %shard_map.105 = (f32[2,2,128,1024]{3,2,1,0:T(8,128)}, f32[2,1,1024]{2,1,0:T(1,128)}, f32[256,128]{1,0:T(8,128)}, f32[160,128]{1,0:T(8,128)}, bf16[128,1024]{1,0:T(8,128)(2,1)}, /*index=5*/bf16[128,1024]{1,0:T(8,128)(2,1)}) custom-call(f32[320,128]{1,0:T(8,128)} %shard_map.103.refs_0_, f32[320,128]{1,0:T(8,128)} %copy-done.20, f32[320,128]{1,0:T(8,128)} %copy-done.21, ...), custom_call_target="tpu_custom_call" | custom-call | flops 402653184 | bytes 1704192 | tf_op jit(solution)/shard_map/pallas_call | solution.py:55
  29.1 4.7 %collective-permute-start.9 = (bf16[128,1024]{1,0:T(8,128)(2,1)}, bf16[128,1024]{1,0:T(8,128)(2,1)S(1)}, u32[]{:S(2)}, u32[]{:S(2)}) collective-permute-start(bf16[128,1024]{1,0:T(8,128)(2,1)} %get-tuple-element.43), channel_id=1, source_target_pairs={{0,4},{4,0},{8,12},{12,8},{1,5},{5,1},{9,13},{13,9},{2,6},{6,2},{1... | collective-permute-start | bytes 786440 | tf_op jit(solution)/shard_map/ppermute | solution.py:385
  34.5 6.7 %collective-permute-done.9 = bf16[128,1024]{1,0:T(8,128)(2,1)S(1)} collective-permute-done((bf16[128,1024]{1,0:T(8,128)(2,1)}, bf16[128,1024]{1,0:T(8,128)(2,1)S(1)}, u32[]{:S(2)}, u32[]{:S(2)}) %collective-permute-start.9) | collective-permute-done | bytes 262176 | tf_op jit(solution)/shard_map/ppermute | solution.py:385
  43.3 4.3 %collective-permute-start.10 = (bf16[128,1024]{1,0:T(8,128)(2,1)}, bf16[128,1024]{1,0:T(8,128)(2,1)S(1)}, u32[]{:S(2)}, u32[]{:S(2)}) collective-permute-start(bf16[128,1024]{1,0:T(8,128)(2,1)} %copy-done.13), channel_id=1, source_target_pairs={{0,4},{4,0},{8,12},{12,8},{1,5},{5,1},{9,13},{13,9},{2,6},{6,2},{1... | collective-permute-start | bytes 786440 | tf_op jit(solution)/shard_map/ppermute | solution.py:359
  47.7 2.7 %shard_map.106 = (f32[128,128]{1,0:T(8,128)}, f32[128,512]{1,0:T(8,128)}, f32[128,128]{1,0:T(8,128)}, f32[2,8,128]{2,1,0:T(8,128)}) custom-call(f32[256,128]{1,0:T(8,128)} %get-tuple-element.52.bc_ref.refs_3_, f32[160,128]{1,0:T(8,128)} %get-tuple-element.48.hp_ref.refs_4_, bf16[128,2048]{1,0:T(8,128)(2,1)} %bitcast.40, bf16[128,2048]{1,0:T(8,128)(2,1)} %bitcast.46), custom_call_target="tpu_custom_call" | custom-call | flops 67108864 | bytes 1261568 | tf_op jit(solution)/shard_map/pallas_call | solution.py:55
  50.4 2.6 %shard_map.107 = (f32[128,512]{1,0:T(8,128)}, f32[128,128]{1,0:T(8,128)}, f32[2,8,128]{2,1,0:T(8,128)}) custom-call(f32[256,128]{1,0:T(8,128)} %get-tuple-element.52.bc_ref.refs_3_, f32[160,128]{1,0:T(8,128)} %get-tuple-element.48.hp_ref.refs_4_, bf16[128,2048]{1,0:T(8,128)(2,1)} %bitcast.41, bf16[128,2048]{1,0:T(8,128)(2,1)} %bitcast.47, ...), custom_call_target="tpu_custom_call" | custom-call | flops 67108864 | bytes 1327104 | tf_op jit(solution)/shard_map/pallas_call | solution.py:55
  54.9 3.3 %collective-permute-start.14 = (bf16[128,1024]{1,0:T(8,128)(2,1)S(1)}, bf16[128,1024]{1,0:T(8,128)(2,1)S(1)}, u32[]{:S(2)}, u32[]{:S(2)}) collective-permute-start(bf16[128,1024]{1,0:T(8,128)(2,1)S(1)} %get-tuple-element.72), channel_id=1, source_target_pairs={{0,4},{4,0},{8,12},{12,8},{1,5},{5,1},{9,13},{13,9},{2,6},{6,2},{1... | collective-permute-start | bytes 786440 | tf_op jit(solution)/shard_map/ppermute | solution.py:385
  58.2 2.6 %shard_map.109 = (f32[128,512]{1,0:T(8,128)}, f32[128,128]{1,0:T(8,128)}, f32[2,8,128]{2,1,0:T(8,128)}) custom-call(f32[256,128]{1,0:T(8,128)} %get-tuple-element.52.bc_ref.refs_3_, f32[160,128]{1,0:T(8,128)} %get-tuple-element.48.hp_ref.refs_4_, bf16[128,2048]{1,0:T(8,128)(2,1)} %bitcast.42, bf16[128,2048]{1,0:T(8,128)(2,1)} %bitcast.48, ...), custom_call_target="tpu_custom_call" | custom-call | flops 67108864 | bytes 1327104 | tf_op jit(solution)/shard_map/pallas_call | solution.py:55
  60.8 2.6 %shard_map.108 = (f32[128,512]{1,0:T(8,128)}, f32[128,128]{1,0:T(8,128)}, f32[2,8,128]{2,1,0:T(8,128)}) custom-call(f32[256,128]{1,0:T(8,128)} %get-tuple-element.52.bc_ref.refs_3_, f32[160,128]{1,0:T(8,128)} %get-tuple-element.48.hp_ref.refs_4_, bf16[128,2048]{1,0:T(8,128)(2,1)} %bitcast.43, bf16[128,2048]{1,0:T(8,128)(2,1)} %bitcast.49, ...), custom_call_target="tpu_custom_call" | custom-call | flops 67108864 | bytes 1327104 | tf_op jit(solution)/shard_map/pallas_call | solution.py:55
  63.6 6.3 %collective-permute-done.13 = bf16[128,1024]{1,0:T(8,128)(2,1)S(1)} collective-permute-done((bf16[128,1024]{1,0:T(8,128)(2,1)S(1)}, bf16[128,1024]{1,0:T(8,128)(2,1)S(1)}, u32[]{:S(2)}, u32[]{:S(2)}) %collective-permute-start.13) | collective-permute-done | bytes 262176 | tf_op jit(solution)/shard_map/ppermute | solution.py:385
  71.1 5.3 %shard_map.110 = (bf16[128,2048]{1,0:T(8,128)(2,1)}, f32[160,128]{1,0:T(8,128)}, f32[128,128]{1,0:T(8,128)}) custom-call(bf16[2,3,128,1024]{3,2,1,0:T(8,128)(2,1)} %copy-done.1, bf16[128,2048]{1,0:T(8,128)(2,1)} %bitcast.44, bf16[128,2048]{1,0:T(8,128)(2,1)} %bitcast.50, f32[256,128]{1,0:T(8,128)} %get-tuple-element.52.bc_ref.refs_3_, ...), custom_call_target="tpu_custom_call" | custom-call | flops 536870912 | bytes 4186240 | tf_op jit(solution)/shard_map/pallas_call | solution.py:55
  79.6 3.4 %all-to-all-start = ((bf16[8,160,128]{2,1,0:T(8,128)(2,1)}), bf16[8,160,128]{2,1,0:T(8,128)(2,1)S(1)}, u32[]{:S(2)}, u32[]{:S(2)}) async-start(bf16[8,160,128]{2,1,0:T(8,128)(2,1)} %broadcast_in_dim.50), calls=%async_computation | async-start | bytes 655360 | tf_op jit(solution)/shard_map/all_to_all | solution.py:495
  83.0 1.9 %collective-permute-start.19 = (bf16[128,1024]{1,0:T(8,128)(2,1)S(1)}, bf16[128,1024]{1,0:T(8,128)(2,1)S(1)}, u32[]{:S(2)}, u32[]{:S(2)}) collective-permute-start(bf16[128,1024]{1,0:T(8,128)(2,1)S(1)} %copy-done.6), channel_id=1, source_target_pairs={{0,4},{4,0},{8,12},{12,8},{1,5},{5,1},{9,13},{13,9},{2,6},{6,2},{1... | collective-permute-start | bytes 786440 | tf_op jit(solution)/shard_map/ppermute | solution.py:359
  87.1 9.7 %collective-permute-done.19.refs_7_ = bf16[128,1024]{1,0:T(8,128)(2,1)S(1)} collective-permute-done((bf16[128,1024]{1,0:T(8,128)(2,1)S(1)}, bf16[128,1024]{1,0:T(8,128)(2,1)S(1)}, u32[]{:S(2)}, u32[]{:S(2)}) %collective-permute-start.19) | collective-permute-done | bytes 262176 | tf_op jit(solution)/shard_map/ppermute | solution.py:359
  97.6 4.2 %collective-permute-start.21 = (bf16[128,1024]{1,0:T(8,128)(2,1)S(1)}, bf16[128,1024]{1,0:T(8,128)(2,1)S(1)}, u32[]{:S(2)}, u32[]{:S(2)}) collective-permute-start(bf16[128,1024]{1,0:T(8,128)(2,1)S(1)} %collective-permute-done.20.refs_8_), channel_id=1, source_target_pairs={{0,4},{4,0},{8,12},{12,8},{1,5},{5,1},{9,13},{13,9},{2,6},{6,2},{1... | collective-permute-start | bytes 786440 | tf_op jit(solution)/shard_map/ppermute | solution.py:359
  101.8 5.6 %collective-permute-start.23 = (bf16[128,1024]{1,0:T(8,128)(2,1)S(1)}, bf16[128,1024]{1,0:T(8,128)(2,1)S(1)}, u32[]{:S(2)}, u32[]{:S(2)}) collective-permute-start(bf16[128,1024]{1,0:T(8,128)(2,1)S(1)} %collective-permute-done.22.refs_10_), channel_id=1, source_target_pairs={{0,4},{4,0},{8,12},{12,8},{1,5},{5,1},{9,13},{13,9},{2,6},{6,2},{1... | collective-permute-start | bytes 786440 | tf_op jit(solution)/shard_map/ppermute | solution.py:359
  108.9 3.5 %collective-permute-done.18.refs_3_ = bf16[64,1024]{1,0:T(8,128)(2,1)S(1)} collective-permute-done((bf16[64,1024]{1,0:T(8,128)(2,1)S(1)}, bf16[64,1024]{1,0:T(8,128)(2,1)S(1)}, u32[]{:S(2)}, u32[]{:S(2)}) %collective-permute-start.18) | collective-permute-done | bytes 131104 | tf_op jit(solution)/shard_map/ppermute | solution.py:22
  114.2 2.9 %shard_map.111 = bf16[128,2048]{1,0:T(8,128)(2,1)} custom-call(bf16[160,128]{1,0:T(8,128)(2,1)} %copy-done.8, bf16[160,128]{1,0:T(8,128)(2,1)} %copy-done.24, bf16[1024,256]{1,0:T(8,128)(2,1)} %refs_0_.1, bf16[64,1024]{1,0:T(8,128)(2,1)} %bitcast.53, bf16[1024,256]{1,0:T(8,128)(2,1)} %copy-done.7, bf16[64,1024]{1,0:T(8,128)(2,1)} %copy-done.23), custom_call_target="tpu_custom_call" | custom-call | flops 167772160 | bytes 1392640 | tf_op jit(solution)/shard_map/pallas_call | solution.py:55
  118.6 4.0 %shard_map.112 = (f32[1024,256]{1,0:T(8,128)}, f32[64,1024]{1,0:T(8,128)}) custom-call(bf16[128,1024]{1,0:T(8,128)(2,1)} %get-tuple-element.38.a_ref.refs_0_, bf16[128,1024]{1,0:T(8,128)(2,1)} %copy-done.11, bf16[128,1024]{1,0:T(8,128)(2,1)} %copy-done.10, bf16[128,1024]{1,0:T(8,128)(2,1)} %copy-done.12, bf16[128,1024]{1,0:T(8,128)(2,1)} %copy-done.13, ...), custom_call_target="tpu_custom_call" | custom-call | flops 671088640 | bytes 3801088 | tf_op jit(solution)/shard_map/pallas_call | solution.py:55
  (104 shorter events, 27.8 us)
Async XLA Ops:
  2.5 9.5 %collective-permute-start = (bf16[128,1024]{1,0:T(8,128)(2,1)}, bf16[128,1024]{1,0:T(8,128)(2,1)S(1)}, u32[]{:S(2)}, u32[]{:S(2)}) collective-permute-start(bf16[128,1024]{1,0:T(8,128)(2,1)} %get-tuple-element.39), channel_id=1, source_target_pairs={{0,2},{2,0},{1,3},{3,1},{4,6},{6,4},{5,7},{7,5},{8,10},{10,8},{9,1... | collective-permute-start | bytes 786440 | tf_op jit(solution)/shard_map/ppermute | solution.py:22
  5.4 11.1 %collective-permute-start.3 = (bf16[128,1024]{1,0:T(8,128)(2,1)}, bf16[128,1024]{1,0:T(8,128)(2,1)S(1)}, u32[]{:S(2)}, u32[]{:S(2)}) collective-permute-start(bf16[128,1024]{1,0:T(8,128)(2,1)} %get-tuple-element.38.a_ref.refs_0_), channel_id=1, source_target_pairs={{0,0},{4,8},{8,4},{12,12},{1,1},{5,9},{9,5},{13,13},{2,2},{6,10},{... | collective-permute-start | bytes 786440 | tf_op jit(solution)/shard_map/ppermute | solution.py:359
  7.0 11.1 %collective-permute-start.2 = (bf16[128,1024]{1,0:T(8,128)(2,1)}, bf16[128,1024]{1,0:T(8,128)(2,1)S(1)}, u32[]{:S(2)}, u32[]{:S(2)}) collective-permute-start(bf16[128,1024]{1,0:T(8,128)(2,1)} %get-tuple-element.38.a_ref.refs_0_), channel_id=1, source_target_pairs={{0,4},{4,0},{8,12},{12,8},{1,5},{5,1},{9,13},{13,9},{2,6},{6,2},{1... | collective-permute-start | bytes 786440 | tf_op jit(solution)/shard_map/ppermute | solution.py:359
  14.8 6.1 %collective-permute-start.1 = (f32[320,128]{1,0:T(8,128)}, f32[320,128]{1,0:T(8,128)S(1)}, u32[]{:S(2)}, u32[]{:S(2)}) collective-permute-start(f32[320,128]{1,0:T(8,128)} %shard_map.104), channel_id=1, source_target_pairs={{0,2},{2,0},{1,3},{3,1},{4,6},{6,4},{5,7},{7,5},{8,10},{10,8},{9,1... | collective-permute-start | bytes 491528 | tf_op jit(solution)/shard_map/ppermute | solution.py:22
  16.5 6.9 %collective-permute-start.6 = (bf16[128,1024]{1,0:T(8,128)(2,1)S(1)}, bf16[128,1024]{1,0:T(8,128)(2,1)S(1)}, u32[]{:S(2)}, u32[]{:S(2)}) collective-permute-start(bf16[128,1024]{1,0:T(8,128)(2,1)S(1)} %collective-permute-done.3.refs_2_), channel_id=1, source_target_pairs={{0,4},{4,0},{8,12},{12,8},{1,5},{5,1},{9,13},{13,9},{2,6},{6,2},{1... | collective-permute-start | bytes 786440 | tf_op jit(solution)/shard_map/ppermute | solution.py:359
  18.1 5.3 %collective-permute-start.7 = (bf16[128,1024]{1,0:T(8,128)(2,1)S(1)}, bf16[128,1024]{1,0:T(8,128)(2,1)S(1)}, u32[]{:S(2)}, u32[]{:S(2)}) collective-permute-start(bf16[128,1024]{1,0:T(8,128)(2,1)S(1)} %collective-permute-done.2.refs_1_), channel_id=1, source_target_pairs={{0,0},{4,8},{8,4},{12,12},{1,1},{5,9},{9,5},{13,13},{2,2},{6,10},{... | collective-permute-start | bytes 786440 | tf_op jit(solution)/shard_map/ppermute | solution.py:359
  20.9 2.5 %collective-permute-start.4 = (f32[320,128]{1,0:T(8,128)}, f32[320,128]{1,0:T(8,128)S(1)}, u32[]{:S(2)}, u32[]{:S(2)}) collective-permute-start(f32[320,128]{1,0:T(8,128)} %shard_map.103.refs_0_), channel_id=1, source_target_pairs={{0,1},{1,0},{2,3},{3,2},{4,5},{5,4},{6,7},{7,6},{8,9},{9,8},{10,11... | collective-permute-start | bytes 491528 | tf_op jit(solution)/shard_map/ppermute | solution.py:22
  20.9 2.5 %collective-permute-start.5 = (f32[320,128]{1,0:T(8,128)S(1)}, f32[320,128]{1,0:T(8,128)S(1)}, u32[]{:S(2)}, u32[]{:S(2)}) collective-permute-start(f32[320,128]{1,0:T(8,128)S(1)} %collective-permute-done.1.refs_1_), channel_id=1, source_target_pairs={{0,1},{1,0},{2,3},{3,2},{4,5},{5,4},{6,7},{7,6},{8,9},{9,8},{10,11... | collective-permute-start | bytes 491528 | tf_op jit(solution)/shard_map/ppermute | solution.py:22
  29.1 12.1 %collective-permute-start.9 = (bf16[128,1024]{1,0:T(8,128)(2,1)}, bf16[128,1024]{1,0:T(8,128)(2,1)S(1)}, u32[]{:S(2)}, u32[]{:S(2)}) collective-permute-start(bf16[128,1024]{1,0:T(8,128)(2,1)} %get-tuple-element.43), channel_id=1, source_target_pairs={{0,4},{4,0},{8,12},{12,8},{1,5},{5,1},{9,13},{13,9},{2,6},{6,2},{1... | collective-permute-start | bytes 786440 | tf_op jit(solution)/shard_map/ppermute | solution.py:385
  33.7 19.2 %collective-permute-start.8 = (bf16[128,1024]{1,0:T(8,128)(2,1)}, bf16[128,1024]{1,0:T(8,128)(2,1)S(1)}, u32[]{:S(2)}, u32[]{:S(2)}) collective-permute-start(bf16[128,1024]{1,0:T(8,128)(2,1)} %get-tuple-element.42), channel_id=1, source_target_pairs={{0,4},{4,0},{8,12},{12,8},{1,5},{5,1},{9,13},{13,9},{2,6},{6,2},{1... | collective-permute-start | bytes 786440 | tf_op jit(solution)/shard_map/ppermute | solution.py:385
  42.5 10.5 %collective-permute-start.12 = (bf16[128,1024]{1,0:T(8,128)(2,1)S(1)}, bf16[128,1024]{1,0:T(8,128)(2,1)S(1)}, u32[]{:S(2)}, u32[]{:S(2)}) collective-permute-start(bf16[128,1024]{1,0:T(8,128)(2,1)S(1)} %fusion.2), channel_id=1, source_target_pairs={{0,0},{4,8},{8,4},{12,12},{1,1},{5,9},{9,5},{13,13},{2,2},{6,10},{... | collective-permute-start | bytes 786440 | tf_op jit(solution)/shard_map/ppermute | solution.py:385
  43.3 9.9 %collective-permute-start.10 = (bf16[128,1024]{1,0:T(8,128)(2,1)}, bf16[128,1024]{1,0:T(8,128)(2,1)S(1)}, u32[]{:S(2)}, u32[]{:S(2)}) collective-permute-start(bf16[128,1024]{1,0:T(8,128)(2,1)} %copy-done.13), channel_id=1, source_target_pairs={{0,4},{4,0},{8,12},{12,8},{1,5},{5,1},{9,13},{13,9},{2,6},{6,2},{1... | collective-permute-start | bytes 786440 | tf_op jit(solution)/shard_map/ppermute | solution.py:359
  54.0 9.4 %collective-permute-start.11 = (bf16[128,1024]{1,0:T(8,128)(2,1)S(1)}, bf16[128,1024]{1,0:T(8,128)(2,1)S(1)}, u32[]{:S(2)}, u32[]{:S(2)}) collective-permute-start(bf16[128,1024]{1,0:T(8,128)(2,1)S(1)} %get-tuple-element.46), channel_id=1, source_target_pairs={{0,0},{4,8},{8,4},{12,12},{1,1},{5,9},{9,5},{13,13},{2,2},{6,10},{... | collective-permute-start | bytes 786440 | tf_op jit(solution)/shard_map/ppermute | solution.py:385
  54.9 15.0 %collective-permute-start.14 = (bf16[128,1024]{1,0:T(8,128)(2,1)S(1)}, bf16[128,1024]{1,0:T(8,128)(2,1)S(1)}, u32[]{:S(2)}, u32[]{:S(2)}) collective-permute-start(bf16[128,1024]{1,0:T(8,128)(2,1)S(1)} %get-tuple-element.72), channel_id=1, source_target_pairs={{0,4},{4,0},{8,12},{12,8},{1,5},{5,1},{9,13},{13,9},{2,6},{6,2},{1... | collective-permute-start | bytes 786440 | tf_op jit(solution)/shard_map/ppermute | solution.py:385
  63.4 6.4 %collective-permute-start.13 = (bf16[128,1024]{1,0:T(8,128)(2,1)S(1)}, bf16[128,1024]{1,0:T(8,128)(2,1)S(1)}, u32[]{:S(2)}, u32[]{:S(2)}) collective-permute-start(bf16[128,1024]{1,0:T(8,128)(2,1)S(1)} %fusion.1), channel_id=1, source_target_pairs={{0,4},{4,0},{8,12},{12,8},{1,5},{5,1},{9,13},{13,9},{2,6},{6,2},{1... | collective-permute-start | bytes 786440 | tf_op jit(solution)/shard_map/ppermute | solution.py:385
  79.6 17.9 %all-to-all-start = ((bf16[8,160,128]{2,1,0:T(8,128)(2,1)}), bf16[8,160,128]{2,1,0:T(8,128)(2,1)S(1)}, u32[]{:S(2)}, u32[]{:S(2)}) async-start(bf16[8,160,128]{2,1,0:T(8,128)(2,1)} %broadcast_in_dim.50), calls=%async_computation | async-start | bytes 655360 | tf_op jit(solution)/shard_map/all_to_all | solution.py:495
  83.0 13.7 %collective-permute-start.19 = (bf16[128,1024]{1,0:T(8,128)(2,1)S(1)}, bf16[128,1024]{1,0:T(8,128)(2,1)S(1)}, u32[]{:S(2)}, u32[]{:S(2)}) collective-permute-start(bf16[128,1024]{1,0:T(8,128)(2,1)S(1)} %copy-done.6), channel_id=1, source_target_pairs={{0,4},{4,0},{8,12},{12,8},{1,5},{5,1},{9,13},{13,9},{2,6},{6,2},{1... | collective-permute-start | bytes 786440 | tf_op jit(solution)/shard_map/ppermute | solution.py:359
  85.0 27.4 %collective-permute-start.17 = (bf16[1024,256]{1,0:T(8,128)(2,1)S(1)}, bf16[1024,256]{1,0:T(8,128)(2,1)S(1)}, u32[]{:S(2)}, u32[]{:S(2)}) collective-permute-start(bf16[1024,256]{1,0:T(8,128)(2,1)S(1)} %copy-done.2), channel_id=1, source_target_pairs={{0,2},{2,0},{1,3},{3,1},{4,6},{6,4},{5,7},{7,5},{8,10},{10,8},{9,1... | collective-permute-start | bytes 1572872 | tf_op jit(solution)/shard_map/ppermute | solution.py:22
  86.4 11.1 %collective-permute-start.20 = (bf16[128,1024]{1,0:T(8,128)(2,1)S(1)}, bf16[128,1024]{1,0:T(8,128)(2,1)S(1)}, u32[]{:S(2)}, u32[]{:S(2)}) collective-permute-start(bf16[128,1024]{1,0:T(8,128)(2,1)S(1)} %copy-done.6), channel_id=1, source_target_pairs={{0,0},{4,8},{8,4},{12,12},{1,1},{5,9},{9,5},{13,13},{2,2},{6,10},{... | collective-permute-start | bytes 786440 | tf_op jit(solution)/shard_map/ppermute | solution.py:359
  96.8 5.0 %collective-permute-start.22 = (bf16[128,1024]{1,0:T(8,128)(2,1)S(1)}, bf16[128,1024]{1,0:T(8,128)(2,1)S(1)}, u32[]{:S(2)}, u32[]{:S(2)}) collective-permute-start(bf16[128,1024]{1,0:T(8,128)(2,1)S(1)} %collective-permute-done.19.refs_7_), channel_id=1, source_target_pairs={{0,0},{4,8},{8,4},{12,12},{1,1},{5,9},{9,5},{13,13},{2,2},{6,10},{... | collective-permute-start | bytes 786440 | tf_op jit(solution)/shard_map/ppermute | solution.py:359
  97.5 19.6 %collective-permute-start.24 = (bf16[8,160,128]{2,1,0:T(8,128)(2,1)S(1)}, bf16[8,160,128]{2,1,0:T(8,128)(2,1)S(1)}, u32[]{:S(2)}, u32[]{:S(2)}) collective-permute-start(bf16[8,160,128]{2,1,0:T(8,128)(2,1)S(1)} %all-to-all-done.refs_12_), channel_id=1, source_target_pairs={{0,1},{1,0},{2,3},{3,2},{4,5},{5,4},{6,7},{7,6},{8,9},{9,8},{10,11... | collective-permute-start | bytes 983048 | tf_op jit(solution)/shard_map/ppermute | solution.py:22
  97.6 19.5 %collective-permute-start.21 = (bf16[128,1024]{1,0:T(8,128)(2,1)S(1)}, bf16[128,1024]{1,0:T(8,128)(2,1)S(1)}, u32[]{:S(2)}, u32[]{:S(2)}) collective-permute-start(bf16[128,1024]{1,0:T(8,128)(2,1)S(1)} %collective-permute-done.20.refs_8_), channel_id=1, source_target_pairs={{0,4},{4,0},{8,12},{12,8},{1,5},{5,1},{9,13},{13,9},{2,6},{6,2},{1... | collective-permute-start | bytes 786440 | tf_op jit(solution)/shard_map/ppermute | solution.py:359
  101.8 15.3 %collective-permute-start.23 = (bf16[128,1024]{1,0:T(8,128)(2,1)S(1)}, bf16[128,1024]{1,0:T(8,128)(2,1)S(1)}, u32[]{:S(2)}, u32[]{:S(2)}) collective-permute-start(bf16[128,1024]{1,0:T(8,128)(2,1)S(1)} %collective-permute-done.22.refs_10_), channel_id=1, source_target_pairs={{0,4},{4,0},{8,12},{12,8},{1,5},{5,1},{9,13},{13,9},{2,6},{6,2},{1... | collective-permute-start | bytes 786440 | tf_op jit(solution)/shard_map/ppermute | solution.py:359
  107.4 5.0 %collective-permute-start.18 = (bf16[64,1024]{1,0:T(8,128)(2,1)S(1)}, bf16[64,1024]{1,0:T(8,128)(2,1)S(1)}, u32[]{:S(2)}, u32[]{:S(2)}) collective-permute-start(bf16[64,1024]{1,0:T(8,128)(2,1)S(1)} %bitcast.54), channel_id=1, source_target_pairs={{0,2},{2,0},{1,3},{3,1},{4,6},{6,4},{5,7},{7,5},{8,10},{10,8},{9,1... | collective-permute-start | bytes 393224 | tf_op jit(solution)/shard_map/ppermute | solution.py:22
  (27 other events, 249.7 us)

commit v5 on v4

--- a/solution.py
+++ b/solution.py
@@ -9,11 +9,12 @@
 
 CHUNKS = 2
 PARTS = 4
-EARLY = (3, 0)
+EARLY = (3, 1)
 EAGER = 2
 BF = jnp.bfloat16
 F32 = jnp.float32
 TOP = lax.Precision.HIGHEST
+PER_US = 1.15e9
 LIMIT = 56 * 1024 * 1024
 
 
@@ -50,7 +51,7 @@
 ANY = pl.BlockSpec(memory_space=pl.ANY)
 
 
-def call(kernel, out_shape, flops, *args, scratch=(), specs=None, out_specs=None):
+def call(kernel, out_shape, span_us, *args, scratch=(), specs=None, out_specs=None):
     size = sum(a.size * a.dtype.itemsize for a in args)
     return pl.pallas_call(
         kernel,
@@ -60,7 +61,9 @@
         out_specs=out_specs or jax.tree.map(lambda _: VMEM, out_shape),
         scratch_shapes=list(scratch),
         compiler_params=pltpu.CompilerParams(vmem_limit_bytes=LIMIT),
-        cost_estimate=pl.CostEstimate(flops=flops, bytes_accessed=size, transcendentals=0),
+        cost_estimate=pl.CostEstimate(
+            flops=int(span_us * PER_US), bytes_accessed=size, transcendentals=0
+        ),
     )(*args)
 
 
@@ -108,7 +111,7 @@
     return call(
         project_kernel,
         struct((total, w_bc.shape[1] // 2), F32),
-        2 * a.size * total,
+        2.1,
         a,
         w_bc,
         w_dt,
@@ -277,6 +280,14 @@
     give_ref[...] = jnp.where(core == 0, dc, db)
 
 
+def low_kernel(keep_ref, taken_ref, out_ref):
+    rows = taken_ref.shape[0]
+    low = keep_ref[0:rows, :] + taken_ref[...]
+    low = jnp.concatenate([low, keep_ref[rows:, :]], axis=0).astype(BF)
+    for k in range(out_ref.shape[0]):
+        out_ref[k] = low
+
+
 def token_kernel(count, mine_ref, other_ref, *refs):
     out_ref = refs[2 * count]
     me, core = lax.axis_index("dp"), lax.axis_index("head")
@@ -363,31 +374,50 @@
     return found, slots, held
 
 
-def chains(first, own, decay, inner, early):
+def chains(first, own, decay, inner, weights):
     count = lax.axis_size("seq")
     place = lax.axis_index("seq")
     chunks = len(first)
     store = jnp.zeros((2, chunks + 1) + own.shape[2:], BF)
     got = list(first)
-    done = [make() for make in inner[:EAGER]]
-    for hop in range(1, count):
-        to = {i: i for i in range(count)}
-        for i in (hop - 1, count - hop - 1):
-            to[i], to[i + 1] = i + 1, i
-        for k in range(chunks):
-            sent = got[k]
+    done, todo, extra = [], list(inner), []
+    last = count + chunks - 2
+    for slot in range(1, last + 1):
+        steps = [(hop, slot - hop) for hop in range(1, count) if 0 <= slot - hop < chunks]
+        sent = []
+        for hop, k in steps:
+            value = got[k]
             if hop > 1:
                 value = jnp.where(place == hop - 1, own[0, k], own[1, k])
-                sent = (value + decay[k] * sent.astype(F32)).astype(BF)
-            if hop == 2 and k == 0:
-                sent = after(sent, *early)
-                done += [make(sent) for make in inner[EAGER:]]
-            got[k] = lax.ppermute(sent, "seq", sorted(to.items()))
+                value = (value + decay[k] * got[k].astype(F32)).astype(BF)
+            sent.append(value)
+        for (hop, k), value in zip(steps, sent):
+            to = {i: i for i in range(count)}
+            for i in (hop - 1, count - hop - 1):
+                to[i], to[i + 1] = i + 1, i
+            got[k] = lax.ppermute(value, "seq", sorted(to.items()))
+        for _ in range(-(-len(todo) // (last + 1 - slot))):
+            done.append(todo.pop(0)(*sent))
+        if slot == 1:
+            extra = weights(*sent)
+        if slot < last:
+            held = [got[k] for _, k in steps] + [d[0] for d in done[-1:]]
+            if slot == last - 1:
+                held += extra
+            if slot == 1 and chunks > 1:
+                held.append(got[1])
+            kept = lax.optimization_barrier(tuple(held))
+            for (_, k), a in zip(steps, kept):
+                got[k] = a
+            if slot == 1 and chunks > 1:
+                got[1] = kept[-1]
+        for hop, k in steps:
             kind = jnp.where(place == hop, 0, 1)
             fits = (place == hop) | (place == count - hop - 1)
             at = jnp.where(fits, k, chunks)
             zero = jnp.zeros_like(at)
             store = lax.dynamic_update_slice(store, got[k][None, None], (kind, at, zero, zero))
+    done += [make() for make in todo]
     return store, done
 
 
@@ -402,7 +432,7 @@
     w_dt = w_dt.T
     rate, bias = decay_rate[None], dt_bias[None]
 
-    pieces = call(split_kernel, [struct((rows, part), BF)] * n_dp, 0, feats)
+    pieces = call(split_kernel, [struct((rows, part), BF)] * n_dp, 1.9, feats)
     items = [pieces[0]] + [cyclic(pieces[r], "dp", r) for r in range(1, n_dp)]
     groups = items[:1]
     if n_dp > 1:
@@ -427,7 +457,7 @@
             struct((5 * heads, rows), F32),
         )
         + (struct((state_n, step), BF),) * CHUNKS,
-        12 * rows * width * state_n,
+        4.9,
         *proj,
         x,
         g,
@@ -446,7 +476,7 @@
             functools.partial(inner_kernel, q * pairs, pairs, size),
             ([square] if q == 0 else [])
             + [struct((rows, span), F32), square, struct((2, 2 * pairs, rows), F32)],
-            8 * rows * rows * span,
+                2.6,
             held,
             hp,
             x,
@@ -460,7 +490,15 @@
             out = out[1:]
         return out
 
-    store, inners = chains(first, own, decay, [functools.partial(inner, q) for q in range(PARTS)], early)
+    weights = [w_bc, w_dt]
+
+    def fetch(*others):
+        for r in range(1, n_dp):
+            weights.extend(cyclic(after(a, *others), "dp", r) for a in (w_bc, w_dt))
+        return weights[2:]
+
+    first[0] = after(first[0], *early)
+    store, inners = chains(first, own, decay, [functools.partial(inner, q) for q in range(PARTS)], fetch)
     grad_x, keep, give = call(
         functools.partial(outer_kernel, size, PARTS),
         (
@@ -468,7 +506,7 @@
             struct((rows + heads, rows), F32),
             struct((rows, rows), F32),
         ),
-        16 * rows * width * state_n,
+        5.4,
         store,
         x,
         g,
@@ -486,21 +524,16 @@
         ),
     )
     taken = cyclic(give, "head", 1)
-    mine = jnp.concatenate([keep[:rows] + taken, keep[rows:]], axis=0).astype(BF)
-    w_bc_later, w_dt_later = after((w_bc, w_dt), hp)
-    weights = [w_bc, w_dt]
-    for r in range(1, n_dp):
-        weights += [cyclic(w_bc_later, "dp", r), cyclic(w_dt_later, "dp", r)]
     count = n_dp * n_seq
-    lows = lax.all_to_all(
-        jnp.broadcast_to(mine[None], (count,) + mine.shape), ("seq", "dp"), 0, 0, tiled=True
-    )
+    copies = call(low_kernel, struct((count, rows + heads, rows), BF), 1.2, keep, taken)
+    mine = copies[0]
+    lows = lax.all_to_all(copies, ("seq", "dp"), 0, 0, tiled=True)
     swapped = cyclic(lows, "head", 1)
     other = cyclic(mine, "head", 1)
     grads = call(
         functools.partial(token_kernel, n_dp),
         struct((rows, width), BF),
-        2 * rows * width * (2 * state_n + 2 * heads),
+        2.9,
         mine,
         other,
         *weights,
@@ -514,7 +547,7 @@
     grad_bc, grad_dt = call(
         functools.partial(weight_kernel, 1.0 / (rows * n_seq * n_dp), n_dp, n_seq, slots),
         (struct((part, 2 * state_n), F32), struct((2 * heads, part), F32)),
-        2 * n_dp * n_seq * rows * part * cols,
+        4.0,
         *toks,
         lows,
         swapped,

time: 123 us -> 118 us (0.959)
  starting transfers between devices: 46 us -> 42.8 us
  other arithmetic: 2.54 us -> 0.51 us
  Pallas kernels: 33.6 us -> 35.3 us
    all_to_all x1, waiting for transfers between devices: 0.01 us -> 9.95 us  [body(): lows = lax.all_to_all(copies, ('seq', 'dp'), 0, 0, tiled=True)]
    ppermute x6, waiting for transfers between devices: 13 us -> 5.64 us  [chains(): got[k] = lax.ppermute(value, 'seq', sorted(to.items()))]
    ppermute x10, starting transfers between devices: 24.8 us -> 18.7 us  [relay(): fresh[kind] = lax.ppermute(held[1 - kind], 'seq', pairs[kind])]
    ppermute x9, waiting for transfers between devices: 6.84 us -> 2.87 us  [cyclic(): return lax.ppermute(a, axis, [(i, (i + by) % count) for i in range(count)])]
    ppermute x6, starting transfers between devices: 9.61 us -> 13.4 us  [chains(): got[k] = lax.ppermute(value, 'seq', sorted(to.items()))]
    pallas_call x11 -> x12, Pallas kernels: 33.6 us -> 35.3 us  [call(): pl.pallas_call(kernel, out_shape=out_shape, grid=(1,), in_specs=specs or...]
    unnamed x50 -> x54, local copies, waits for them, and re-layouts: 5.4 us -> 5.31 us
  transfers between devices with their start and end apart: 26 -> 26, of which waited for: 8 -> 12; matrix products, arithmetic and copies ran while one was open for 3% -> 2% of each run, Pallas kernels for 14% -> 19%
where the time goes in v5:
time: 118 us
  starting transfers between devices  42.8 us (36%)
  Pallas kernels  35.3 us (30%)
  waiting for transfers between devices  30.9 us (26%)
  local copies, waits for them, and re-layouts  7.11 us (6%)
    pallas_call x12, Pallas kernels, call(): pl.pallas_call(kernel, out_shape=out_shape, grid=(1,), in_specs=specs or...  35.3 us
    ppermute x10, starting transfers between devices, relay(): fresh[kind] = lax.ppermute(held[1 - kind], 'seq', pairs[kind])  18.7 us
    ppermute x6, starting transfers between devices, chains(): got[k] = lax.ppermute(value, 'seq', sorted(to.items()))  13.4 us
    ppermute x10, waiting for transfers between devices, relay(): fresh[kind] = lax.ppermute(held[1 - kind], 'seq', pairs[kind])  12.4 us
    all_to_all x1, waiting for transfers between devices, body(): lows = lax.all_to_all(copies, ('seq', 'dp'), 0, 0, tiled=True)  9.95 us
    ppermute x9, starting transfers between devices, cyclic(): return lax.ppermute(a, axis, [(i, (i + by) % count) for i in range(count)])  7.36 us
    ppermute x6, waiting for transfers between devices, chains(): got[k] = lax.ppermute(value, 'seq', sorted(to.items()))  5.64 us
    unnamed x54, local copies, waits for them, and re-layouts  5.31 us
  transfers between devices with their start and end apart: 26, of which 12 were waited for; matrix products, arithmetic and copies ran while one was open for 2% of the time, Pallas kernels for 19%

profile of v5, /device:TPU:0, one launch (start us, length us, event | category | flops | bytes accessed | tf_op | source)
XLA Modules:
  0.0 117.6 jit_solution(796683376805046829)
XLA Ops:
  0.6 1.9 %shard_map.102 = (bf16[128,1024]{1,0:T(8,128)(2,1)}, bf16[128,1024]{1,0:T(8,128)(2,1)}) custom-call(bf16[128,2048]{1,0:T(8,128)(2,1)} %bitcast.45), custom_call_target="tpu_custom_call" | custom-call | flops 2184999936 | bytes 524288 | tf_op jit(solution)/shard_map/pallas_call | solution.py:56
  2.5 2.9 %collective-permute-start = (bf16[128,1024]{1,0:T(8,128)(2,1)}, bf16[128,1024]{1,0:T(8,128)(2,1)S(1)}, u32[]{:S(2)}, u32[]{:S(2)}) collective-permute-start(bf16[128,1024]{1,0:T(8,128)(2,1)} %get-tuple-element.48), channel_id=1, source_target_pairs={{0,2},{2,0},{1,3},{3,1},{4,6},{6,4},{5,7},{7,5},{8,10},{10,8},{9,1... | collective-permute-start | bytes 786440 | tf_op jit(solution)/shard_map/ppermute | solution.py:23
  7.0 3.5 %collective-permute-start.2 = (bf16[128,1024]{1,0:T(8,128)(2,1)}, bf16[128,1024]{1,0:T(8,128)(2,1)S(1)}, u32[]{:S(2)}, u32[]{:S(2)}) collective-permute-start(bf16[128,1024]{1,0:T(8,128)(2,1)} %get-tuple-element.47.a_ref.refs_0_), channel_id=1, source_target_pairs={{0,4},{4,0},{8,12},{12,8},{1,5},{5,1},{9,13},{13,9},{2,6},{6,2},{1... | collective-permute-start | bytes 786440 | tf_op jit(solution)/shard_map/ppermute | solution.py:370
  12.7 2.1 %shard_map.104 = f32[320,128]{1,0:T(8,128)} custom-call(bf16[128,1024]{1,0:T(8,128)(2,1)} %copy-done.7, bf16[1024,256]{1,0:T(8,128)(2,1)} %refs_0_.1, bf16[64,1024]{1,0:T(8,128)(2,1)} %bitcast.58), custom_call_target="tpu_custom_call" | custom-call | flops 2415000064 | bytes 917504 | tf_op jit(solution)/shard_map/pallas_call | solution.py:56
  14.8 1.7 %collective-permute-start.1 = (f32[320,128]{1,0:T(8,128)}, f32[320,128]{1,0:T(8,128)S(1)}, u32[]{:S(2)}, u32[]{:S(2)}) collective-permute-start(f32[320,128]{1,0:T(8,128)} %shard_map.104), channel_id=1, source_target_pairs={{0,2},{2,0},{1,3},{3,1},{4,6},{6,4},{5,7},{7,5},{8,10},{10,8},{9,1... | collective-permute-start | bytes 491528 | tf_op jit(solution)/shard_map/ppermute | solution.py:23
  18.8 2.1 %shard_map.103.refs_0_ = f32[320,128]{1,0:T(8,128)} custom-call(bf16[128,1024]{1,0:T(8,128)(2,1)} %get-tuple-element.47.a_ref.refs_0_, bf16[1024,256]{1,0:T(8,128)(2,1)} %refs_0_.1, bf16[64,1024]{1,0:T(8,128)(2,1)} %bitcast.59), custom_call_target="tpu_custom_call" | custom-call | flops 2415000064 | bytes 917504 | tf_op jit(solution)/shard_map/pallas_call | solution.py:56
  23.4 4.4 %collective-permute-start.8 = (bf16[128,1024]{1,0:T(8,128)(2,1)S(1)}, bf16[128,1024]{1,0:T(8,128)(2,1)S(1)}, u32[]{:S(2)}, u32[]{:S(2)}) collective-permute-start(bf16[128,1024]{1,0:T(8,128)(2,1)S(1)} %copy-done.8), channel_id=1, source_target_pairs={{0,4},{4,0},{8,12},{12,8},{1,5},{5,1},{9,13},{13,9},{2,6},{6,2},{1... | collective-permute-start | bytes 786440 | tf_op jit(solution)/shard_map/ppermute | solution.py:370
  28.8 4.9 %shard_map.105 = (f32[2,2,128,1024]{3,2,1,0:T(8,128)}, f32[2,1,1024]{2,1,0:T(1,128)}, f32[256,128]{1,0:T(8,128)}, f32[160,128]{1,0:T(8,128)}, bf16[128,1024]{1,0:T(8,128)(2,1)}, /*index=5*/bf16[128,1024]{1,0:T(8,128)(2,1)}) custom-call(f32[320,128]{1,0:T(8,128)} %shard_map.103.refs_0_, f32[320,128]{1,0:T(8,128)} %copy-done.20, f32[320,128]{1,0:T(8,128)} %copy-done.21, ...), custom_call_target="tpu_custom_call" | custom-call | flops 5634999808 | bytes 1704192 | tf_op jit(solution)/shard_map/pallas_call | solution.py:56
  34.9 5.1 %collective-permute-done.10.refs_5_ = bf16[128,1024]{1,0:T(8,128)(2,1)S(1)} collective-permute-done((bf16[128,1024]{1,0:T(8,128)(2,1)S(1)}, bf16[128,1024]{1,0:T(8,128)(2,1)S(1)}, u32[]{:S(2)}, u32[]{:S(2)}) %collective-permute-start.10) | collective-permute-done | bytes 262176 | tf_op jit(solution)/shard_map/ppermute | solution.py:370
  40.0 1.7 %collective-permute-start.11 = (bf16[128,1024]{1,0:T(8,128)(2,1)}, bf16[128,1024]{1,0:T(8,128)(2,1)S(1)}, u32[]{:S(2)}, u32[]{:S(2)}) collective-permute-start(bf16[128,1024]{1,0:T(8,128)(2,1)} %get-tuple-element.52), channel_id=1, source_target_pairs={{0,4},{4,0},{8,12},{12,8},{1,5},{5,1},{9,13},{13,9},{2,6},{6,2},{1... | collective-permute-start | bytes 786440 | tf_op jit(solution)/shard_map/ppermute | solution.py:398
  43.8 2.9 %shard_map.106 = (f32[128,128]{1,0:T(8,128)}, f32[128,512]{1,0:T(8,128)}, f32[128,128]{1,0:T(8,128)}, f32[2,8,128]{2,1,0:T(8,128)}) custom-call(f32[256,128]{1,0:T(8,128)} %get-tuple-element.73.bc_ref.refs_3_, f32[160,128]{1,0:T(8,128)} %get-tuple-element.55.hp_ref.refs_4_, bf16[128,2048]{1,0:T(8,128)(2,1)} %bitcast.47, bf16[128,2048]{1,0:T(8,128)(2,1)} %bitcast.53), custom_call_target="tpu_custom_call" | custom-call | flops 2990000128 | bytes 1261568 | tf_op jit(solution)/shard_map/pallas_call | solution.py:56
  48.8 4.1 %collective-permute-start.12 = (bf16[128,1024]{1,0:T(8,128)(2,1)S(1)}, bf16[128,1024]{1,0:T(8,128)(2,1)S(1)}, u32[]{:S(2)}, u32[]{:S(2)}) collective-permute-start(bf16[128,1024]{1,0:T(8,128)(2,1)S(1)} %copy-done.16), channel_id=1, source_target_pairs={{0,4},{4,0},{8,12},{12,8},{1,5},{5,1},{9,13},{13,9},{2,6},{6,2},{1... | collective-permute-start | bytes 786440 | tf_op jit(solution)/shard_map/ppermute | solution.py:398
  53.1 2.6 %shard_map.107 = (f32[128,512]{1,0:T(8,128)}, f32[128,128]{1,0:T(8,128)}, f32[2,8,128]{2,1,0:T(8,128)}) custom-call(f32[256,128]{1,0:T(8,128)} %get-tuple-element.73.bc_ref.refs_3_, f32[160,128]{1,0:T(8,128)} %get-tuple-element.55.hp_ref.refs_4_, bf16[128,2048]{1,0:T(8,128)(2,1)} %bitcast.48, bf16[128,2048]{1,0:T(8,128)(2,1)} %bitcast.54, ...), custom_call_target="tpu_custom_call" | custom-call | flops 2990000128 | bytes 1327104 | tf_op jit(solution)/shard_map/pallas_call | solution.py:56
  57.6 2.2 %collective-permute-start.15 = (bf16[128,1024]{1,0:T(8,128)(2,1)S(1)}, bf16[128,1024]{1,0:T(8,128)(2,1)S(1)}, u32[]{:S(2)}, u32[]{:S(2)}) collective-permute-start(bf16[128,1024]{1,0:T(8,128)(2,1)S(1)} %get-tuple-element.90), channel_id=1, source_target_pairs={{0,4},{4,0},{8,12},{12,8},{1,5},{5,1},{9,13},{13,9},{2,6},{6,2},{1... | collective-permute-start | bytes 786440 | tf_op jit(solution)/shard_map/ppermute | solution.py:398
  60.4 2.6 %shard_map.108 = (f32[128,512]{1,0:T(8,128)}, f32[128,128]{1,0:T(8,128)}, f32[2,8,128]{2,1,0:T(8,128)}) custom-call(f32[256,128]{1,0:T(8,128)} %get-tuple-element.73.bc_ref.refs_3_, f32[160,128]{1,0:T(8,128)} %get-tuple-element.55.hp_ref.refs_4_, bf16[128,2048]{1,0:T(8,128)(2,1)} %bitcast.49, bf16[128,2048]{1,0:T(8,128)(2,1)} %bitcast.55, ...), custom_call_target="tpu_custom_call" | custom-call | flops 2990000128 | bytes 1327104 | tf_op jit(solution)/shard_map/pallas_call | solution.py:56
  64.2 4.0 %collective-permute-start.18 = (bf16[128,1024]{1,0:T(8,128)(2,1)S(1)}, bf16[128,1024]{1,0:T(8,128)(2,1)S(1)}, u32[]{:S(2)}, u32[]{:S(2)}) collective-permute-start(bf16[128,1024]{1,0:T(8,128)(2,1)S(1)} %fusion), channel_id=1, source_target_pairs={{0,4},{4,0},{8,12},{12,8},{1,5},{5,1},{9,13},{13,9},{2,6},{6,2},{1... | collective-permute-start | bytes 786440 | tf_op jit(solution)/shard_map/ppermute | solution.py:398
  68.3 2.6 %shard_map.109 = (f32[128,512]{1,0:T(8,128)}, f32[128,128]{1,0:T(8,128)}, f32[2,8,128]{2,1,0:T(8,128)}) custom-call(f32[256,128]{1,0:T(8,128)} %get-tuple-element.73.bc_ref.refs_3_, f32[160,128]{1,0:T(8,128)} %get-tuple-element.55.hp_ref.refs_4_, bf16[128,2048]{1,0:T(8,128)(2,1)} %bitcast.50, bf16[128,2048]{1,0:T(8,128)(2,1)} %bitcast.56, ...), custom_call_target="tpu_custom_call" | custom-call | flops 2990000128 | bytes 1327104 | tf_op jit(solution)/shard_map/pallas_call | solution.py:56
  73.8 5.3 %shard_map.110 = (bf16[128,2048]{1,0:T(8,128)(2,1)}, f32[160,128]{1,0:T(8,128)}, f32[128,128]{1,0:T(8,128)}) custom-call(bf16[2,3,128,1024]{3,2,1,0:T(8,128)(2,1)} %copy-done.1, bf16[128,2048]{1,0:T(8,128)(2,1)} %bitcast.51, bf16[128,2048]{1,0:T(8,128)(2,1)} %bitcast.57, f32[256,128]{1,0:T(8,128)} %get-tuple-element.73.bc_ref.refs_3_, ...), custom_call_target="tpu_custom_call" | custom-call | flops 6209999872 | bytes 4186240 | tf_op jit(solution)/shard_map/pallas_call | solution.py:56
  82.8 3.4 %all-to-all-start = ((bf16[8,160,128]{2,1,0:T(8,128)(2,1)}), bf16[8,160,128]{2,1,0:T(8,128)(2,1)S(1)}, u32[]{:S(2)}, u32[]{:S(2)}) async-start(bf16[8,160,128]{2,1,0:T(8,128)(2,1)} %shard_map.111), calls=%async_computation | async-start | bytes 655360 | tf_op jit(solution)/shard_map/all_to_all | solution.py:530
  87.9 10.0 %all-to-all-done.refs_12_ = bf16[8,160,128]{2,1,0:T(8,128)(2,1)S(1)} async-done(((bf16[8,160,128]{2,1,0:T(8,128)(2,1)}), bf16[8,160,128]{2,1,0:T(8,128)(2,1)S(1)}, u32[]{:S(2)}, u32[]{:S(2)}) %all-to-all-start) | async-done | bytes 327712 | tf_op jit(solution)/shard_map/all_to_all | solution.py:530
  98.5 4.7 %collective-permute-start.23 = (bf16[128,1024]{1,0:T(8,128)(2,1)S(1)}, bf16[128,1024]{1,0:T(8,128)(2,1)S(1)}, u32[]{:S(2)}, u32[]{:S(2)}) collective-permute-start(bf16[128,1024]{1,0:T(8,128)(2,1)S(1)} %collective-permute-done.22.refs_10_), channel_id=1, source_target_pairs={{0,4},{4,0},{8,12},{12,8},{1,5},{5,1},{9,13},{13,9},{2,6},{6,2},{1... | collective-permute-start | bytes 786440 | tf_op jit(solution)/shard_map/ppermute | solution.py:370
  103.8 2.9 %shard_map.112 = bf16[128,2048]{1,0:T(8,128)(2,1)} custom-call(bf16[160,128]{1,0:T(8,128)(2,1)} %copy-done.3, bf16[160,128]{1,0:T(8,128)(2,1)} %copy-done.26, bf16[1024,256]{1,0:T(8,128)(2,1)} %refs_0_.1, bf16[64,1024]{1,0:T(8,128)(2,1)} %bitcast.60, bf16[1024,256]{1,0:T(8,128)(2,1)} %copy-done.5, bf16[64,1024]{1,0:T(8,128)(2,1)} %copy-done.24), custom_call_target="tpu_custom_call" | custom-call | flops 3335000064 | bytes 1392640 | tf_op jit(solution)/shard_map/pallas_call | solution.py:56
  107.0 5.2 %collective-permute-done.23.refs_11_ = bf16[128,1024]{1,0:T(8,128)(2,1)S(1)} collective-permute-done((bf16[128,1024]{1,0:T(8,128)(2,1)S(1)}, bf16[128,1024]{1,0:T(8,128)(2,1)S(1)}, u32[]{:S(2)}, u32[]{:S(2)}) %collective-permute-start.23) | collective-permute-done | bytes 262176 | tf_op jit(solution)/shard_map/ppermute | solution.py:370
  113.6 4.0 %shard_map.113 = (f32[1024,256]{1,0:T(8,128)}, f32[64,1024]{1,0:T(8,128)}) custom-call(bf16[128,1024]{1,0:T(8,128)(2,1)} %get-tuple-element.47.a_ref.refs_0_, bf16[128,1024]{1,0:T(8,128)(2,1)} %copy-done.10, bf16[128,1024]{1,0:T(8,128)(2,1)} %copy-done.9, bf16[128,1024]{1,0:T(8,128)(2,1)} %copy-done.11, bf16[128,1024]{1,0:T(8,128)(2,1)} %copy-done.12, ...), custom_call_target="tpu_custom_call" | custom-call | flops 4600000000 | bytes 3801088 | tf_op jit(solution)/shard_map/pallas_call | solution.py:56
  (106 shorter events, 30.0 us)
Async XLA Ops:
  2.5 9.5 %collective-permute-start = (bf16[128,1024]{1,0:T(8,128)(2,1)}, bf16[128,1024]{1,0:T(8,128)(2,1)S(1)}, u32[]{:S(2)}, u32[]{:S(2)}) collective-permute-start(bf16[128,1024]{1,0:T(8,128)(2,1)} %get-tuple-element.48), channel_id=1, source_target_pairs={{0,2},{2,0},{1,3},{3,1},{4,6},{6,4},{5,7},{7,5},{8,10},{10,8},{9,1... | collective-permute-start | bytes 786440 | tf_op jit(solution)/shard_map/ppermute | solution.py:23
  5.4 11.1 %collective-permute-start.3 = (bf16[128,1024]{1,0:T(8,128)(2,1)}, bf16[128,1024]{1,0:T(8,128)(2,1)S(1)}, u32[]{:S(2)}, u32[]{:S(2)}) collective-permute-start(bf16[128,1024]{1,0:T(8,128)(2,1)} %get-tuple-element.47.a_ref.refs_0_), channel_id=1, source_target_pairs={{0,0},{4,8},{8,4},{12,12},{1,1},{5,9},{9,5},{13,13},{2,2},{6,10},{... | collective-permute-start | bytes 786440 | tf_op jit(solution)/shard_map/ppermute | solution.py:370
  7.0 11.1 %collective-permute-start.2 = (bf16[128,1024]{1,0:T(8,128)(2,1)}, bf16[128,1024]{1,0:T(8,128)(2,1)S(1)}, u32[]{:S(2)}, u32[]{:S(2)}) collective-permute-start(bf16[128,1024]{1,0:T(8,128)(2,1)} %get-tuple-element.47.a_ref.refs_0_), channel_id=1, source_target_pairs={{0,4},{4,0},{8,12},{12,8},{1,5},{5,1},{9,13},{13,9},{2,6},{6,2},{1... | collective-permute-start | bytes 786440 | tf_op jit(solution)/shard_map/ppermute | solution.py:370
  14.8 6.1 %collective-permute-start.1 = (f32[320,128]{1,0:T(8,128)}, f32[320,128]{1,0:T(8,128)S(1)}, u32[]{:S(2)}, u32[]{:S(2)}) collective-permute-start(f32[320,128]{1,0:T(8,128)} %shard_map.104), channel_id=1, source_target_pairs={{0,2},{2,0},{1,3},{3,1},{4,6},{6,4},{5,7},{7,5},{8,10},{10,8},{9,1... | collective-permute-start | bytes 491528 | tf_op jit(solution)/shard_map/ppermute | solution.py:23
  16.5 6.9 %collective-permute-start.6 = (bf16[128,1024]{1,0:T(8,128)(2,1)S(1)}, bf16[128,1024]{1,0:T(8,128)(2,1)S(1)}, u32[]{:S(2)}, u32[]{:S(2)}) collective-permute-start(bf16[128,1024]{1,0:T(8,128)(2,1)S(1)} %collective-permute-done.3.refs_2_), channel_id=1, source_target_pairs={{0,4},{4,0},{8,12},{12,8},{1,5},{5,1},{9,13},{13,9},{2,6},{6,2},{1... | collective-permute-start | bytes 786440 | tf_op jit(solution)/shard_map/ppermute | solution.py:370
  18.1 9.7 %collective-permute-start.7 = (bf16[128,1024]{1,0:T(8,128)(2,1)S(1)}, bf16[128,1024]{1,0:T(8,128)(2,1)S(1)}, u32[]{:S(2)}, u32[]{:S(2)}) collective-permute-start(bf16[128,1024]{1,0:T(8,128)(2,1)S(1)} %collective-permute-done.2.refs_1_), channel_id=1, source_target_pairs={{0,0},{4,8},{8,4},{12,12},{1,1},{5,9},{9,5},{13,13},{2,2},{6,10},{... | collective-permute-start | bytes 786440 | tf_op jit(solution)/shard_map/ppermute | solution.py:370
  20.9 7.1 %collective-permute-start.4 = (f32[320,128]{1,0:T(8,128)}, f32[320,128]{1,0:T(8,128)S(1)}, u32[]{:S(2)}, u32[]{:S(2)}) collective-permute-start(f32[320,128]{1,0:T(8,128)} %shard_map.103.refs_0_), channel_id=1, source_target_pairs={{0,1},{1,0},{2,3},{3,2},{4,5},{5,4},{6,7},{7,6},{8,9},{9,8},{10,11... | collective-permute-start | bytes 491528 | tf_op jit(solution)/shard_map/ppermute | solution.py:23
  20.9 7.1 %collective-permute-start.5 = (f32[320,128]{1,0:T(8,128)S(1)}, f32[320,128]{1,0:T(8,128)S(1)}, u32[]{:S(2)}, u32[]{:S(2)}) collective-permute-start(f32[320,128]{1,0:T(8,128)S(1)} %collective-permute-done.1.refs_1_), channel_id=1, source_target_pairs={{0,1},{1,0},{2,3},{3,2},{4,5},{5,4},{6,7},{7,6},{8,9},{9,8},{10,11... | collective-permute-start | bytes 491528 | tf_op jit(solution)/shard_map/ppermute | solution.py:23
  21.4 13.0 %collective-permute-start.9 = (bf16[128,1024]{1,0:T(8,128)(2,1)S(1)}, bf16[128,1024]{1,0:T(8,128)(2,1)S(1)}, u32[]{:S(2)}, u32[]{:S(2)}) collective-permute-start(bf16[128,1024]{1,0:T(8,128)(2,1)S(1)} %copy-done.8), channel_id=1, source_target_pairs={{0,0},{4,8},{8,4},{12,12},{1,1},{5,9},{9,5},{13,13},{2,2},{6,10},{... | collective-permute-start | bytes 786440 | tf_op jit(solution)/shard_map/ppermute | solution.py:370
  23.4 11.5 %collective-permute-start.8 = (bf16[128,1024]{1,0:T(8,128)(2,1)S(1)}, bf16[128,1024]{1,0:T(8,128)(2,1)S(1)}, u32[]{:S(2)}, u32[]{:S(2)}) collective-permute-start(bf16[128,1024]{1,0:T(8,128)(2,1)S(1)} %copy-done.8), channel_id=1, source_target_pairs={{0,4},{4,0},{8,12},{12,8},{1,5},{5,1},{9,13},{13,9},{2,6},{6,2},{1... | collective-permute-start | bytes 786440 | tf_op jit(solution)/shard_map/ppermute | solution.py:370
  27.8 12.2 %collective-permute-start.10 = (bf16[128,1024]{1,0:T(8,128)(2,1)S(1)}, bf16[128,1024]{1,0:T(8,128)(2,1)S(1)}, u32[]{:S(2)}, u32[]{:S(2)}) collective-permute-start(bf16[128,1024]{1,0:T(8,128)(2,1)S(1)} %collective-permute-done.7.refs_4_), channel_id=1, source_target_pairs={{0,4},{4,0},{8,12},{12,8},{1,5},{5,1},{9,13},{13,9},{2,6},{6,2},{1... | collective-permute-start | bytes 786440 | tf_op jit(solution)/shard_map/ppermute | solution.py:370
  40.0 8.0 %collective-permute-start.11 = (bf16[128,1024]{1,0:T(8,128)(2,1)}, bf16[128,1024]{1,0:T(8,128)(2,1)S(1)}, u32[]{:S(2)}, u32[]{:S(2)}) collective-permute-start(bf16[128,1024]{1,0:T(8,128)(2,1)} %get-tuple-element.52), channel_id=1, source_target_pairs={{0,4},{4,0},{8,12},{12,8},{1,5},{5,1},{9,13},{13,9},{2,6},{6,2},{1... | collective-permute-start | bytes 786440 | tf_op jit(solution)/shard_map/ppermute | solution.py:398
  41.7 21.3 %collective-permute-start.17 = (bf16[64,1024]{1,0:T(8,128)(2,1)S(1)}, bf16[64,1024]{1,0:T(8,128)(2,1)S(1)}, u32[]{:S(2)}, u32[]{:S(2)}) collective-permute-start(bf16[64,1024]{1,0:T(8,128)(2,1)S(1)} %bitcast.61), channel_id=1, source_target_pairs={{0,2},{2,0},{1,3},{3,1},{4,6},{6,4},{5,7},{7,5},{8,10},{10,8},{9,1... | collective-permute-start | bytes 393224 | tf_op jit(solution)/shard_map/ppermute | solution.py:23
  42.3 20.8 %collective-permute-start.16 = (bf16[1024,256]{1,0:T(8,128)(2,1)S(1)}, bf16[1024,256]{1,0:T(8,128)(2,1)S(1)}, u32[]{:S(2)}, u32[]{:S(2)}) collective-permute-start(bf16[1024,256]{1,0:T(8,128)(2,1)S(1)} %copy-done.4), channel_id=1, source_target_pairs={{0,2},{2,0},{1,3},{3,1},{4,6},{6,4},{5,7},{7,5},{8,10},{10,8},{9,1... | collective-permute-start | bytes 1572872 | tf_op jit(solution)/shard_map/ppermute | solution.py:23
  48.1 7.6 %collective-permute-start.13 = (bf16[128,1024]{1,0:T(8,128)(2,1)S(1)}, bf16[128,1024]{1,0:T(8,128)(2,1)S(1)}, u32[]{:S(2)}, u32[]{:S(2)}) collective-permute-start(bf16[128,1024]{1,0:T(8,128)(2,1)S(1)} %fusion.3), channel_id=1, source_target_pairs={{0,0},{4,8},{8,4},{12,12},{1,1},{5,9},{9,5},{13,13},{2,2},{6,10},{... | collective-permute-start | bytes 786440 | tf_op jit(solution)/shard_map/ppermute | solution.py:398
  48.8 8.5 %collective-permute-start.12 = (bf16[128,1024]{1,0:T(8,128)(2,1)S(1)}, bf16[128,1024]{1,0:T(8,128)(2,1)S(1)}, u32[]{:S(2)}, u32[]{:S(2)}) collective-permute-start(bf16[128,1024]{1,0:T(8,128)(2,1)S(1)} %copy-done.16), channel_id=1, source_target_pairs={{0,4},{4,0},{8,12},{12,8},{1,5},{5,1},{9,13},{13,9},{2,6},{6,2},{1... | collective-permute-start | bytes 786440 | tf_op jit(solution)/shard_map/ppermute | solution.py:398
  57.6 6.5 %collective-permute-start.15 = (bf16[128,1024]{1,0:T(8,128)(2,1)S(1)}, bf16[128,1024]{1,0:T(8,128)(2,1)S(1)}, u32[]{:S(2)}, u32[]{:S(2)}) collective-permute-start(bf16[128,1024]{1,0:T(8,128)(2,1)S(1)} %get-tuple-element.90), channel_id=1, source_target_pairs={{0,4},{4,0},{8,12},{12,8},{1,5},{5,1},{9,13},{13,9},{2,6},{6,2},{1... | collective-permute-start | bytes 786440 | tf_op jit(solution)/shard_map/ppermute | solution.py:398
  64.2 8.3 %collective-permute-start.18 = (bf16[128,1024]{1,0:T(8,128)(2,1)S(1)}, bf16[128,1024]{1,0:T(8,128)(2,1)S(1)}, u32[]{:S(2)}, u32[]{:S(2)}) collective-permute-start(bf16[128,1024]{1,0:T(8,128)(2,1)S(1)} %fusion), channel_id=1, source_target_pairs={{0,4},{4,0},{8,12},{12,8},{1,5},{5,1},{9,13},{13,9},{2,6},{6,2},{1... | collective-permute-start | bytes 786440 | tf_op jit(solution)/shard_map/ppermute | solution.py:398
  82.8 15.0 %all-to-all-start = ((bf16[8,160,128]{2,1,0:T(8,128)(2,1)}), bf16[8,160,128]{2,1,0:T(8,128)(2,1)S(1)}, u32[]{:S(2)}, u32[]{:S(2)}) async-start(bf16[8,160,128]{2,1,0:T(8,128)(2,1)} %shard_map.111), calls=%async_computation | async-start | bytes 655360 | tf_op jit(solution)/shard_map/all_to_all | solution.py:530
  86.2 12.3 %collective-permute-start.22 = (bf16[128,1024]{1,0:T(8,128)(2,1)S(1)}, bf16[128,1024]{1,0:T(8,128)(2,1)S(1)}, u32[]{:S(2)}, u32[]{:S(2)}) collective-permute-start(bf16[128,1024]{1,0:T(8,128)(2,1)S(1)} %collective-permute-done.8.refs_7_), channel_id=1, source_target_pairs={{0,0},{4,8},{8,4},{12,12},{1,1},{5,9},{9,5},{13,13},{2,2},{6,10},{... | collective-permute-start | bytes 786440 | tf_op jit(solution)/shard_map/ppermute | solution.py:370
  87.7 15.5 %collective-permute-start.20 = (bf16[160,128]{1,0:T(8,128)(2,1)S(1)}, bf16[160,128]{1,0:T(8,128)(2,1)S(1)}, u32[]{:S(2)}, u32[]{:S(2)}) collective-permute-start(bf16[160,128]{1,0:T(8,128)(2,1)S(1)} %slice_bitcast_fusion.mine_ref), channel_id=1, source_target_pairs={{0,1},{1,0},{2,3},{3,2},{4,5},{5,4},{6,7},{7,6},{8,9},{9,8},{10,11... | collective-permute-start | bytes 122888 | tf_op jit(solution)/shard_map/ppermute | solution.py:23
  97.8 14.3 %collective-permute-start.24 = (bf16[8,160,128]{2,1,0:T(8,128)(2,1)S(1)}, bf16[8,160,128]{2,1,0:T(8,128)(2,1)S(1)}, u32[]{:S(2)}, u32[]{:S(2)}) collective-permute-start(bf16[8,160,128]{2,1,0:T(8,128)(2,1)S(1)} %all-to-all-done.refs_12_), channel_id=1, source_target_pairs={{0,1},{1,0},{2,3},{3,2},{4,5},{5,4},{6,7},{7,6},{8,9},{9,8},{10,11... | collective-permute-start | bytes 983048 | tf_op jit(solution)/shard_map/ppermute | solution.py:23
  97.8 9.2 %collective-permute-start.21 = (bf16[128,1024]{1,0:T(8,128)(2,1)S(1)}, bf16[128,1024]{1,0:T(8,128)(2,1)S(1)}, u32[]{:S(2)}, u32[]{:S(2)}) collective-permute-start(bf16[128,1024]{1,0:T(8,128)(2,1)S(1)} %collective-permute-done.9.refs_8_), channel_id=1, source_target_pairs={{0,4},{4,0},{8,12},{12,8},{1,5},{5,1},{9,13},{13,9},{2,6},{6,2},{1... | collective-permute-start | bytes 786440 | tf_op jit(solution)/shard_map/ppermute | solution.py:370
  98.5 13.7 %collective-permute-start.23 = (bf16[128,1024]{1,0:T(8,128)(2,1)S(1)}, bf16[128,1024]{1,0:T(8,128)(2,1)S(1)}, u32[]{:S(2)}, u32[]{:S(2)}) collective-permute-start(bf16[128,1024]{1,0:T(8,128)(2,1)S(1)} %collective-permute-done.22.refs_10_), channel_id=1, source_target_pairs={{0,4},{4,0},{8,12},{12,8},{1,5},{5,1},{9,13},{13,9},{2,6},{6,2},{1... | collective-permute-start | bytes 786440 | tf_op jit(solution)/shard_map/ppermute | solution.py:370
  (29 other events, 256.4 us)

commit v6 on v5

--- a/solution.py
+++ b/solution.py
@@ -9,8 +9,6 @@
 
 CHUNKS = 2
 PARTS = 4
-EARLY = (3, 1)
-EAGER = 2
 BF = jnp.bfloat16
 F32 = jnp.float32
 TOP = lax.Precision.HIGHEST
@@ -358,23 +356,27 @@
         dt_ref[k * heads : (k + 1) * heads, :] = total[k * share + half : (k + 1) * share]
 
 
-def relay(block, hops, held=None):
+def relays(count):
+    groups, _ = matchings(count)
+    return [
+        (kind, hop)
+        for hop in range(1, count)
+        for kind in (0, 1)
+        if any(i - hop + 1 >= 0 or j + hop - 1 < count for i, j in groups[kind])
+    ]
+
+
+def relay(found, block, steps, *others):
     count = lax.axis_size("seq")
-    groups, pairs = matchings(count)
-    held = held or [block, block]
-    found, slots = [], []
-    for hop in hops:
-        fresh = [None, None]
-        for kind in (0, 1):
-            if any(i - hop + 1 >= 0 or j + hop - 1 < count for i, j in groups[kind]):
-                fresh[kind] = lax.ppermute(held[1 - kind], "seq", pairs[kind])
-                found.append(fresh[kind])
-                slots.append((kind, hop))
-        held = [h if f is None else f for f, h in zip(fresh, held)]
-    return found, slots, held
-
-
-def chains(first, own, decay, inner, weights):
+    _, pairs = matchings(count)
+    for kind, hop in steps:
+        source = block if hop == 1 else found[1 - kind, hop - 1]
+        source = after(source, *others) if others else source
+        found[kind, hop] = lax.ppermute(source, "seq", pairs[kind])
+    return [found[step] for step in steps]
+
+
+def chains(first, own, decay, inner, beside, riders):
     count = lax.axis_size("seq")
     place = lax.axis_index("seq")
     chunks = len(first)
@@ -387,6 +389,8 @@
         sent = []
         for hop, k in steps:
             value = got[k]
+            if hop == 1 and k < len(riders):
+                value = jnp.where((place == 0) | (place == count - 1), value, riders[k])
             if hop > 1:
                 value = jnp.where(place == hop - 1, own[0, k], own[1, k])
                 value = (value + decay[k] * got[k].astype(F32)).astype(BF)
@@ -396,14 +400,18 @@
             for i in (hop - 1, count - hop - 1):
                 to[i], to[i + 1] = i + 1, i
             got[k] = lax.ppermute(value, "seq", sorted(to.items()))
+            if hop == 1 and k < len(riders):
+                riders[k] = got[k]
         for _ in range(-(-len(todo) // (last + 1 - slot))):
             done.append(todo.pop(0)(*sent))
         if slot == 1:
-            extra = weights(*sent)
+            extra, soon = beside(*sent)
         if slot < last:
             held = [got[k] for _, k in steps] + [d[0] for d in done[-1:]]
             if slot == last - 1:
                 held += extra
+            if slot == 2:
+                held += soon
             if slot == 1 and chunks > 1:
                 held.append(got[1])
             kept = lax.optimization_barrier(tuple(held))
@@ -437,17 +445,21 @@
     groups = items[:1]
     if n_dp > 1:
         groups.append(items[1] if n_dp == 2 else jnp.concatenate(items[1:], axis=0))
-    cuts = [min(1 + hop, n_seq) for hop in EARLY[: len(groups)]]
-    moved = [relay(a, range(1, cut)) for a, cut in zip(groups, cuts)]
-    early = [a for m in moved[1:] for a in m[0]] + moved[0][0][4:]
-    near = moved[0][0]
+    found = [{} for _ in groups]
+    slots = relays(n_seq)
+    step = width // CHUNKS
+    ride = n_seq == 4 and all(a.shape == (state_n, step) for a in groups)
+    second = [(kind, hop) for kind, hop in slots if hop == 2 and not (ride and kind == 0)]
+    near = relay(found[0], groups[0], slots[:2])
     partials = [project(items[0], w_bc, w_dt)] + [
         cyclic(project(items[r], w_bc, w_dt), "dp", -r) for r in range(1, n_dp)
     ]
-    partials[1:] = [after(a, *near[:2]) for a in partials[1:]]
+    partials[1:] = [after(a, *near) for a in partials[1:]]
     proj = partials + [cyclic(a, "head", 1) for a in partials]
-    x = after(x, *near[2:4])
-    step = width // CHUNKS
+    x = after(x, *relay(found[0], groups[0], second))
+    early = []
+    if n_dp > 1:
+        early = relay(found[1], groups[1], slots[:2], *proj[n_dp - 1 : n_dp])
     own, decay, bc, hp, *first = call(
         functools.partial(state_kernel, 2 * n_dp, size),
         (
@@ -492,13 +504,18 @@
 
     weights = [w_bc, w_dt]
 
-    def fetch(*others):
+    def beside(*others):
         for r in range(1, n_dp):
             weights.extend(cyclic(after(a, *others), "dp", r) for a in (w_bc, w_dt))
-        return weights[2:]
+        return weights[2:], relay(found[1], groups[1], second, *others) if n_dp > 1 else []
 
     first[0] = after(first[0], *early)
-    store, inners = chains(first, own, decay, [functools.partial(inner, q) for q in range(PARTS)], fetch)
+    riders = [f[1, 1] for f in found] if ride else []
+    calls = [functools.partial(inner, q) for q in range(PARTS)]
+    store, inners = chains(first, own, decay, calls, beside, riders)
+    for f, a in zip(found, riders):
+        f[0, 2] = a
+    done = relay(found[0], groups[0], [step for step in slots if step not in found[0]], store)
     grad_x, keep, give = call(
         functools.partial(outer_kernel, size, PARTS),
         (
@@ -523,7 +540,7 @@
             pltpu.VMEM((1, width), F32),
         ),
     )
-    taken = cyclic(give, "head", 1)
+    taken = after(cyclic(give, "head", 1), *done)
     count = n_dp * n_seq
     copies = call(low_kernel, struct((count, rows + heads, rows), BF), 1.2, keep, taken)
     mine = copies[0]
@@ -539,10 +556,10 @@
         *weights,
     )
     toks = []
-    for a, cut, (found, near, held) in zip(groups, cuts, moved):
-        rest, far, _ = relay(a, range(cut, n_seq), list(after(tuple(held), store)))
-        slots = [(0, 0)] + near + far
-        toks += [a] + found + rest
+    for f, a in zip(found, groups):
+        relay(f, a, [step for step in slots if step not in f], store)
+        toks += [a] + [f[step] for step in slots]
+    slots = [(0, 0)] + slots
     cols = 2 * (rows + heads)
     grad_bc, grad_dt = call(
         functools.partial(weight_kernel, 1.0 / (rows * n_seq * n_dp), n_dp, n_seq, slots),

time: 118 us -> 111 us (0.941)
  starting transfers between devices: 42.8 us -> 36.8 us
  waiting for transfers between devices: 30.9 us -> 29.1 us
  other arithmetic: 0.51 us -> 1.74 us
    ppermute x10 -> x8, waiting for transfers between devices: 12.4 us -> 4.16 us  [relay(): found[kind, hop] = lax.ppermute(source, 'seq', pairs[kind])]
    ppermute x10 -> x8, starting transfers between devices: 18.7 us -> 12.5 us  [relay(): found[kind, hop] = lax.ppermute(source, 'seq', pairs[kind])]
    ppermute x6, waiting for transfers between devices: 5.64 us -> 9.19 us  [chains(): got[k] = lax.ppermute(value, 'seq', sorted(to.items()))]
    ppermute x9, waiting for transfers between devices: 2.87 us -> 5.85 us  [cyclic(): return lax.ppermute(a, axis, [(i, (i + by) % count) for i in range(count)])]
    select_n x0 -> x2, other arithmetic: none -> 1.19 us  [chains(): value = jnp.where((place == 0) | (place == count - 1), value, riders[k])]
  transfers between devices with their start and end apart: 26 -> 24, of which waited for: 12 -> 9; matrix products, arithmetic and copies ran while one was open for 2% -> 2% of each run, Pallas kernels for 19% -> 25%
where the time goes in v6:
time: 111 us; the launch traced here: 110 us
  starting transfers between devices  36.8 us (33%)
  Pallas kernels  35.3 us (32%)
  waiting for transfers between devices  29.1 us (26%)
  local copies, waits for them, and re-layouts  5.97 us (5%)
  other arithmetic  1.74 us (2%)
    pallas_call x12, Pallas kernels, call(): pl.pallas_call(kernel, out_shape=out_shape, grid=(1,), in_specs=specs or...  35.3 us
    ppermute x6, starting transfers between devices, chains(): got[k] = lax.ppermute(value, 'seq', sorted(to.items()))  14 us
    ppermute x8, starting transfers between devices, relay(): found[kind, hop] = lax.ppermute(source, 'seq', pairs[kind])  12.5 us
    all_to_all x1, waiting for transfers between devices, body(): lows = lax.all_to_all(copies, ('seq', 'dp'), 0, 0, tiled=True)  9.85 us
    ppermute x6, waiting for transfers between devices, chains(): got[k] = lax.ppermute(value, 'seq', sorted(to.items()))  9.19 us
    ppermute x9, starting transfers between devices, cyclic(): return lax.ppermute(a, axis, [(i, (i + by) % count) for i in range(count)])  6.93 us
    ppermute x9, waiting for transfers between devices, cyclic(): return lax.ppermute(a, axis, [(i, (i + by) % count) for i in range(count)])  5.85 us
    unnamed x54, local copies, waits for them, and re-layouts  4.17 us
  transfers between devices with their start and end apart: 24, of which 9 were waited for; matrix products, arithmetic and copies ran while one was open for 2% of the time, Pallas kernels for 25%

profile of v6, /device:TPU:0, one launch (start us, length us, event | category | flops | bytes accessed | tf_op | source)
XLA Modules:
  0.0 109.9 jit_solution(1308764426541833827)
XLA Ops:
  2.5 2.9 %collective-permute-start = (bf16[128,1024]{1,0:T(8,128)(2,1)}, bf16[128,1024]{1,0:T(8,128)(2,1)S(1)}, u32[]{:S(2)}, u32[]{:S(2)}) collective-permute-start(bf16[128,1024]{1,0:T(8,128)(2,1)} %get-tuple-element.51), channel_id=1, source_target_pairs={{0,2},{2,0},{1,3},{3,1},{4,6},{6,4},{5,7},{7,5},{8,10},{10,8},{9,1... | collective-permute-start | bytes 786440 | tf_op jit(solution)/shard_map/ppermute | solution.py:21
  8.6 3.3 %collective-permute-done.a_ref.refs_6_ = bf16[128,1024]{1,0:T(8,128)(2,1)S(1)} collective-permute-done((bf16[128,1024]{1,0:T(8,128)(2,1)}, bf16[128,1024]{1,0:T(8,128)(2,1)S(1)}, u32[]{:S(2)}, u32[]{:S(2)}) %collective-permute-start) | collective-permute-done | bytes 262176 | tf_op jit(solution)/shard_map/ppermute | solution.py:21
  12.7 2.1 %shard_map.104 = f32[320,128]{1,0:T(8,128)} custom-call(bf16[128,1024]{1,0:T(8,128)(2,1)} %copy-done.12, bf16[1024,256]{1,0:T(8,128)(2,1)} %refs_0_.1, bf16[64,1024]{1,0:T(8,128)(2,1)} %bitcast.58), custom_call_target="tpu_custom_call" | custom-call | flops 2415000064 | bytes 917504 | tf_op jit(solution)/shard_map/pallas_call | solution.py:54
  17.2 2.1 %shard_map.103.refs_0_ = f32[320,128]{1,0:T(8,128)} custom-call(bf16[128,1024]{1,0:T(8,128)(2,1)} %get-tuple-element.50.a_ref.refs_0_, bf16[1024,256]{1,0:T(8,128)(2,1)} %refs_0_.1, bf16[64,1024]{1,0:T(8,128)(2,1)} %bitcast.59), custom_call_target="tpu_custom_call" | custom-call | flops 2415000064 | bytes 917504 | tf_op jit(solution)/shard_map/pallas_call | solution.py:54
  20.4 3.9 %collective-permute-start.7 = (bf16[128,1024]{1,0:T(8,128)(2,1)S(1)}, bf16[128,1024]{1,0:T(8,128)(2,1)S(1)}, u32[]{:S(2)}, u32[]{:S(2)}) collective-permute-start(bf16[128,1024]{1,0:T(8,128)(2,1)S(1)} %copy-done.13), channel_id=1, source_target_pairs={{0,4},{4,0},{8,12},{12,8},{1,5},{5,1},{9,13},{13,9},{2,6},{6,2},{1... | collective-permute-start | bytes 786440 | tf_op jit(solution)/shard_map/ppermute | solution.py:375
  25.8 4.9 %shard_map.105 = (f32[2,2,128,1024]{3,2,1,0:T(8,128)}, f32[2,1,1024]{2,1,0:T(1,128)}, f32[256,128]{1,0:T(8,128)}, f32[160,128]{1,0:T(8,128)}, bf16[128,1024]{1,0:T(8,128)(2,1)}, /*index=5*/bf16[128,1024]{1,0:T(8,128)(2,1)}) custom-call(f32[320,128]{1,0:T(8,128)} %shard_map.103.refs_0_, f32[320,128]{1,0:T(8,128)} %copy-done.20, f32[320,128]{1,0:T(8,128)} %copy-done.21, ...), custom_call_target="tpu_custom_call" | custom-call | flops 5634999808 | bytes 1704192 | tf_op jit(solution)/shard_map/pallas_call | solution.py:54
  32.6 2.0 %collective-permute-start.9 = (bf16[128,1024]{1,0:T(8,128)(2,1)S(1)}, bf16[128,1024]{1,0:T(8,128)(2,1)S(1)}, u32[]{:S(2)}, u32[]{:S(2)}) collective-permute-start(bf16[128,1024]{1,0:T(8,128)(2,1)S(1)} %broadcast_select_fusion.1), channel_id=1, source_target_pairs={{0,4},{4,0},{8,12},{12,8},{1,5},{5,1},{9,13},{13,9},{2,6},{6,2},{1... | collective-permute-start | bytes 786440 | tf_op jit(solution)/shard_map/ppermute | solution.py:402
  37.4 2.9 %shard_map.106 = (f32[128,128]{1,0:T(8,128)}, f32[128,512]{1,0:T(8,128)}, f32[128,128]{1,0:T(8,128)}, f32[2,8,128]{2,1,0:T(8,128)}) custom-call(f32[256,128]{1,0:T(8,128)} %get-tuple-element.78.bc_ref.refs_3_, f32[160,128]{1,0:T(8,128)} %get-tuple-element.59.hp_ref.refs_4_, bf16[128,2048]{1,0:T(8,128)(2,1)} %bitcast.47, bf16[128,2048]{1,0:T(8,128)(2,1)} %bitcast.53), custom_call_target="tpu_custom_call" | custom-call | flops 2990000128 | bytes 1261568 | tf_op jit(solution)/shard_map/pallas_call | solution.py:54
  41.6 4.3 %collective-permute-start.10 = (bf16[128,1024]{1,0:T(8,128)(2,1)S(1)}, bf16[128,1024]{1,0:T(8,128)(2,1)S(1)}, u32[]{:S(2)}, u32[]{:S(2)}) collective-permute-start(bf16[128,1024]{1,0:T(8,128)(2,1)S(1)} %broadcast_select_fusion), channel_id=1, source_target_pairs={{0,4},{4,0},{8,12},{12,8},{1,5},{5,1},{9,13},{13,9},{2,6},{6,2},{1... | collective-permute-start | bytes 786440 | tf_op jit(solution)/shard_map/ppermute | solution.py:402
  46.2 2.6 %shard_map.107 = (f32[128,512]{1,0:T(8,128)}, f32[128,128]{1,0:T(8,128)}, f32[2,8,128]{2,1,0:T(8,128)}) custom-call(f32[256,128]{1,0:T(8,128)} %get-tuple-element.78.bc_ref.refs_3_, f32[160,128]{1,0:T(8,128)} %get-tuple-element.59.hp_ref.refs_4_, bf16[128,2048]{1,0:T(8,128)(2,1)} %bitcast.48, bf16[128,2048]{1,0:T(8,128)(2,1)} %bitcast.54, ...), custom_call_target="tpu_custom_call" | custom-call | flops 2990000128 | bytes 1327104 | tf_op jit(solution)/shard_map/pallas_call | solution.py:54
  48.7 2.1 %collective-permute-done.10.refs_9_ = bf16[128,1024]{1,0:T(8,128)(2,1)S(1)} collective-permute-done((bf16[128,1024]{1,0:T(8,128)(2,1)S(1)}, bf16[128,1024]{1,0:T(8,128)(2,1)S(1)}, u32[]{:S(2)}, u32[]{:S(2)}) %collective-permute-start.10) | collective-permute-done | bytes 262176 | tf_op jit(solution)/shard_map/ppermute | solution.py:402
  51.8 3.9 %collective-permute-start.14 = (bf16[128,1024]{1,0:T(8,128)(2,1)S(1)}, bf16[128,1024]{1,0:T(8,128)(2,1)S(1)}, u32[]{:S(2)}, u32[]{:S(2)}) collective-permute-start(bf16[128,1024]{1,0:T(8,128)(2,1)S(1)} %get-tuple-element.96), channel_id=1, source_target_pairs={{0,4},{4,0},{8,12},{12,8},{1,5},{5,1},{9,13},{13,9},{2,6},{6,2},{1... | collective-permute-start | bytes 786440 | tf_op jit(solution)/shard_map/ppermute | solution.py:402
  55.7 2.6 %shard_map.108 = (f32[128,512]{1,0:T(8,128)}, f32[128,128]{1,0:T(8,128)}, f32[2,8,128]{2,1,0:T(8,128)}) custom-call(f32[256,128]{1,0:T(8,128)} %get-tuple-element.78.bc_ref.refs_3_, f32[160,128]{1,0:T(8,128)} %get-tuple-element.59.hp_ref.refs_4_, bf16[128,2048]{1,0:T(8,128)(2,1)} %bitcast.49, bf16[128,2048]{1,0:T(8,128)(2,1)} %bitcast.55, ...), custom_call_target="tpu_custom_call" | custom-call | flops 2990000128 | bytes 1327104 | tf_op jit(solution)/shard_map/pallas_call | solution.py:54
  58.4 2.7 %collective-permute-done.14 = bf16[128,1024]{1,0:T(8,128)(2,1)S(1)} collective-permute-done((bf16[128,1024]{1,0:T(8,128)(2,1)S(1)}, bf16[128,1024]{1,0:T(8,128)(2,1)S(1)}, u32[]{:S(2)}, u32[]{:S(2)}) %collective-permute-start.14) | collective-permute-done | bytes 262176 | tf_op jit(solution)/shard_map/ppermute | solution.py:402
  61.2 2.4 %collective-permute-start.17 = (bf16[128,1024]{1,0:T(8,128)(2,1)S(1)}, bf16[128,1024]{1,0:T(8,128)(2,1)S(1)}, u32[]{:S(2)}, u32[]{:S(2)}) collective-permute-start(bf16[128,1024]{1,0:T(8,128)(2,1)S(1)} %fusion), channel_id=1, source_target_pairs={{0,4},{4,0},{8,12},{12,8},{1,5},{5,1},{9,13},{13,9},{2,6},{6,2},{1... | collective-permute-start | bytes 786440 | tf_op jit(solution)/shard_map/ppermute | solution.py:402
  63.6 2.6 %shard_map.109 = (f32[128,512]{1,0:T(8,128)}, f32[128,128]{1,0:T(8,128)}, f32[2,8,128]{2,1,0:T(8,128)}) custom-call(f32[256,128]{1,0:T(8,128)} %get-tuple-element.78.bc_ref.refs_3_, f32[160,128]{1,0:T(8,128)} %get-tuple-element.59.hp_ref.refs_4_, bf16[128,2048]{1,0:T(8,128)(2,1)} %bitcast.50, bf16[128,2048]{1,0:T(8,128)(2,1)} %bitcast.56, ...), custom_call_target="tpu_custom_call" | custom-call | flops 2990000128 | bytes 1327104 | tf_op jit(solution)/shard_map/pallas_call | solution.py:54
  66.2 4.0 %collective-permute-done.17 = bf16[128,1024]{1,0:T(8,128)(2,1)S(1)} collective-permute-done((bf16[128,1024]{1,0:T(8,128)(2,1)S(1)}, bf16[128,1024]{1,0:T(8,128)(2,1)S(1)}, u32[]{:S(2)}, u32[]{:S(2)}) %collective-permute-start.17) | collective-permute-done | bytes 262176 | tf_op jit(solution)/shard_map/ppermute | solution.py:402
  70.2 2.3 %collective-permute-start.19 = (bf16[128,1024]{1,0:T(8,128)(2,1)S(1)}, bf16[128,1024]{1,0:T(8,128)(2,1)S(1)}, u32[]{:S(2)}, u32[]{:S(2)}) collective-permute-start(bf16[128,1024]{1,0:T(8,128)(2,1)S(1)} %collective-permute-done.6.refs_4_), channel_id=1, source_target_pairs={{0,4},{4,0},{8,12},{12,8},{1,5},{5,1},{9,13},{13,9},{2,6},{6,2},{1... | collective-permute-start | bytes 786440 | tf_op jit(solution)/shard_map/ppermute | solution.py:375
  72.5 5.3 %shard_map.110 = (bf16[128,2048]{1,0:T(8,128)(2,1)}, f32[160,128]{1,0:T(8,128)}, f32[128,128]{1,0:T(8,128)}) custom-call(bf16[2,3,128,1024]{3,2,1,0:T(8,128)(2,1)} %copy-done.1, bf16[128,2048]{1,0:T(8,128)(2,1)} %bitcast.51, bf16[128,2048]{1,0:T(8,128)(2,1)} %bitcast.57, f32[256,128]{1,0:T(8,128)} %get-tuple-element.78.bc_ref.refs_3_, ...), custom_call_target="tpu_custom_call" | custom-call | flops 6209999872 | bytes 4186240 | tf_op jit(solution)/shard_map/pallas_call | solution.py:54
  81.5 3.4 %all-to-all-start = ((bf16[8,160,128]{2,1,0:T(8,128)(2,1)}), bf16[8,160,128]{2,1,0:T(8,128)(2,1)S(1)}, u32[]{:S(2)}, u32[]{:S(2)}) async-start(bf16[8,160,128]{2,1,0:T(8,128)(2,1)} %shard_map.111), calls=%async_computation | async-start | bytes 655360 | tf_op jit(solution)/shard_map/all_to_all | solution.py:547
  85.9 9.8 %all-to-all-done.refs_12_ = bf16[8,160,128]{2,1,0:T(8,128)(2,1)S(1)} async-done(((bf16[8,160,128]{2,1,0:T(8,128)(2,1)}), bf16[8,160,128]{2,1,0:T(8,128)(2,1)S(1)}, u32[]{:S(2)}, u32[]{:S(2)}) %all-to-all-start) | async-done | bytes 327712 | tf_op jit(solution)/shard_map/all_to_all | solution.py:547
  97.5 2.9 %shard_map.112 = bf16[128,2048]{1,0:T(8,128)(2,1)} custom-call(bf16[160,128]{1,0:T(8,128)(2,1)} %copy-done.8, bf16[160,128]{1,0:T(8,128)(2,1)} %copy-done.26, bf16[1024,256]{1,0:T(8,128)(2,1)} %refs_0_.1, bf16[64,1024]{1,0:T(8,128)(2,1)} %bitcast.60, bf16[1024,256]{1,0:T(8,128)(2,1)} %copy-done.10, bf16[64,1024]{1,0:T(8,128)(2,1)} %copy-done.24), custom_call_target="tpu_custom_call" | custom-call | flops 3335000064 | bytes 1392640 | tf_op jit(solution)/shard_map/pallas_call | solution.py:54
  100.4 4.1 %collective-permute-done.21.refs_11_ = bf16[128,1024]{1,0:T(8,128)(2,1)S(1)} collective-permute-done((bf16[128,1024]{1,0:T(8,128)(2,1)S(1)}, bf16[128,1024]{1,0:T(8,128)(2,1)S(1)}, u32[]{:S(2)}, u32[]{:S(2)}) %collective-permute-start.21) | collective-permute-done | bytes 262176 | tf_op jit(solution)/shard_map/ppermute | solution.py:375
  105.9 4.0 %shard_map.113 = (f32[1024,256]{1,0:T(8,128)}, f32[64,1024]{1,0:T(8,128)}) custom-call(bf16[128,1024]{1,0:T(8,128)(2,1)} %get-tuple-element.50.a_ref.refs_0_, bf16[128,1024]{1,0:T(8,128)(2,1)} %copy-done.14, bf16[128,1024]{1,0:T(8,128)(2,1)} %copy-done.5, bf16[128,1024]{1,0:T(8,128)(2,1)} %copy-done.3, bf16[128,1024]{1,0:T(8,128)(2,1)} %copy-done.15, ...), custom_call_target="tpu_custom_call" | custom-call | flops 4600000000 | bytes 3801088 | tf_op jit(solution)/shard_map/pallas_call | solution.py:54
  (104 shorter events, 25.8 us)
Async XLA Ops:
  2.5 9.5 %collective-permute-start = (bf16[128,1024]{1,0:T(8,128)(2,1)}, bf16[128,1024]{1,0:T(8,128)(2,1)S(1)}, u32[]{:S(2)}, u32[]{:S(2)}) collective-permute-start(bf16[128,1024]{1,0:T(8,128)(2,1)} %get-tuple-element.51), channel_id=1, source_target_pairs={{0,2},{2,0},{1,3},{3,1},{4,6},{6,4},{5,7},{7,5},{8,10},{10,8},{9,1... | collective-permute-start | bytes 786440 | tf_op jit(solution)/shard_map/ppermute | solution.py:21
  5.4 11.1 %collective-permute-start.2 = (bf16[128,1024]{1,0:T(8,128)(2,1)}, bf16[128,1024]{1,0:T(8,128)(2,1)S(1)}, u32[]{:S(2)}, u32[]{:S(2)}) collective-permute-start(bf16[128,1024]{1,0:T(8,128)(2,1)} %get-tuple-element.50.a_ref.refs_0_), channel_id=1, source_target_pairs={{0,4},{4,0},{8,12},{12,8},{1,5},{5,1},{9,13},{13,9},{2,6},{6,2},{1... | collective-permute-start | bytes 786440 | tf_op jit(solution)/shard_map/ppermute | solution.py:375
  7.0 12.3 %collective-permute-start.3 = (bf16[128,1024]{1,0:T(8,128)(2,1)}, bf16[128,1024]{1,0:T(8,128)(2,1)S(1)}, u32[]{:S(2)}, u32[]{:S(2)}) collective-permute-start(bf16[128,1024]{1,0:T(8,128)(2,1)} %get-tuple-element.50.a_ref.refs_0_), channel_id=1, source_target_pairs={{0,0},{4,8},{8,4},{12,12},{1,1},{5,9},{9,5},{13,13},{2,2},{6,10},{... | collective-permute-start | bytes 786440 | tf_op jit(solution)/shard_map/ppermute | solution.py:375
  14.8 5.6 %collective-permute-start.1 = (f32[320,128]{1,0:T(8,128)}, f32[320,128]{1,0:T(8,128)S(1)}, u32[]{:S(2)}, u32[]{:S(2)}) collective-permute-start(f32[320,128]{1,0:T(8,128)} %shard_map.104), channel_id=1, source_target_pairs={{0,2},{2,0},{1,3},{3,1},{4,6},{6,4},{5,7},{7,5},{8,10},{10,8},{9,1... | collective-permute-start | bytes 491528 | tf_op jit(solution)/shard_map/ppermute | solution.py:21
  16.5 8.5 %collective-permute-start.6 = (bf16[128,1024]{1,0:T(8,128)(2,1)S(1)}, bf16[128,1024]{1,0:T(8,128)(2,1)S(1)}, u32[]{:S(2)}, u32[]{:S(2)}) collective-permute-start(bf16[128,1024]{1,0:T(8,128)(2,1)S(1)} %collective-permute-done.2.refs_1_), channel_id=1, source_target_pairs={{0,0},{4,8},{8,4},{12,12},{1,1},{5,9},{9,5},{13,13},{2,2},{6,10},{... | collective-permute-start | bytes 786440 | tf_op jit(solution)/shard_map/ppermute | solution.py:375
  19.3 5.7 %collective-permute-start.4 = (f32[320,128]{1,0:T(8,128)}, f32[320,128]{1,0:T(8,128)S(1)}, u32[]{:S(2)}, u32[]{:S(2)}) collective-permute-start(f32[320,128]{1,0:T(8,128)} %shard_map.103.refs_0_), channel_id=1, source_target_pairs={{0,1},{1,0},{2,3},{3,2},{4,5},{5,4},{6,7},{7,6},{8,9},{9,8},{10,11... | collective-permute-start | bytes 491528 | tf_op jit(solution)/shard_map/ppermute | solution.py:21
  20.4 4.6 %collective-permute-start.5 = (f32[320,128]{1,0:T(8,128)S(1)}, f32[320,128]{1,0:T(8,128)S(1)}, u32[]{:S(2)}, u32[]{:S(2)}) collective-permute-start(f32[320,128]{1,0:T(8,128)S(1)} %collective-permute-done.1.refs_1_), channel_id=1, source_target_pairs={{0,1},{1,0},{2,3},{3,2},{4,5},{5,4},{6,7},{7,6},{8,9},{9,8},{10,11... | collective-permute-start | bytes 491528 | tf_op jit(solution)/shard_map/ppermute | solution.py:21
  20.4 11.0 %collective-permute-start.7 = (bf16[128,1024]{1,0:T(8,128)(2,1)S(1)}, bf16[128,1024]{1,0:T(8,128)(2,1)S(1)}, u32[]{:S(2)}, u32[]{:S(2)}) collective-permute-start(bf16[128,1024]{1,0:T(8,128)(2,1)S(1)} %copy-done.13), channel_id=1, source_target_pairs={{0,4},{4,0},{8,12},{12,8},{1,5},{5,1},{9,13},{13,9},{2,6},{6,2},{1... | collective-permute-start | bytes 786440 | tf_op jit(solution)/shard_map/ppermute | solution.py:375
  24.3 7.1 %collective-permute-start.8 = (bf16[128,1024]{1,0:T(8,128)(2,1)S(1)}, bf16[128,1024]{1,0:T(8,128)(2,1)S(1)}, u32[]{:S(2)}, u32[]{:S(2)}) collective-permute-start(bf16[128,1024]{1,0:T(8,128)(2,1)S(1)} %copy-done.13), channel_id=1, source_target_pairs={{0,0},{4,8},{8,4},{12,12},{1,1},{5,9},{9,5},{13,13},{2,2},{6,10},{... | collective-permute-start | bytes 786440 | tf_op jit(solution)/shard_map/ppermute | solution.py:375
  32.6 8.1 %collective-permute-start.9 = (bf16[128,1024]{1,0:T(8,128)(2,1)S(1)}, bf16[128,1024]{1,0:T(8,128)(2,1)S(1)}, u32[]{:S(2)}, u32[]{:S(2)}) collective-permute-start(bf16[128,1024]{1,0:T(8,128)(2,1)S(1)} %broadcast_select_fusion.1), channel_id=1, source_target_pairs={{0,4},{4,0},{8,12},{12,8},{1,5},{5,1},{9,13},{13,9},{2,6},{6,2},{1... | collective-permute-start | bytes 786440 | tf_op jit(solution)/shard_map/ppermute | solution.py:402
  34.6 14.1 %collective-permute-start.12 = (bf16[128,1024]{1,0:T(8,128)(2,1)S(1)}, bf16[128,1024]{1,0:T(8,128)(2,1)S(1)}, u32[]{:S(2)}, u32[]{:S(2)}) collective-permute-start(bf16[128,1024]{1,0:T(8,128)(2,1)S(1)} %collective-permute-done.7.refs_7_), channel_id=1, source_target_pairs={{0,0},{4,8},{8,4},{12,12},{1,1},{5,9},{9,5},{13,13},{2,2},{6,10},{... | collective-permute-start | bytes 786440 | tf_op jit(solution)/shard_map/ppermute | solution.py:375
  35.3 23.0 %collective-permute-start.16 = (bf16[64,1024]{1,0:T(8,128)(2,1)S(1)}, bf16[64,1024]{1,0:T(8,128)(2,1)S(1)}, u32[]{:S(2)}, u32[]{:S(2)}) collective-permute-start(bf16[64,1024]{1,0:T(8,128)(2,1)S(1)} %bitcast.61), channel_id=1, source_target_pairs={{0,2},{2,0},{1,3},{3,1},{4,6},{6,4},{5,7},{7,5},{8,10},{10,8},{9,1... | collective-permute-start | bytes 393224 | tf_op jit(solution)/shard_map/ppermute | solution.py:21
  36.2 22.1 %collective-permute-start.15 = (bf16[1024,256]{1,0:T(8,128)(2,1)S(1)}, bf16[1024,256]{1,0:T(8,128)(2,1)S(1)}, u32[]{:S(2)}, u32[]{:S(2)}) collective-permute-start(bf16[1024,256]{1,0:T(8,128)(2,1)S(1)} %copy-done.9), channel_id=1, source_target_pairs={{0,2},{2,0},{1,3},{3,1},{4,6},{6,4},{5,7},{7,5},{8,10},{10,8},{9,1... | collective-permute-start | bytes 1572872 | tf_op jit(solution)/shard_map/ppermute | solution.py:21
  40.8 7.9 %collective-permute-start.11 = (bf16[128,1024]{1,0:T(8,128)(2,1)S(1)}, bf16[128,1024]{1,0:T(8,128)(2,1)S(1)}, u32[]{:S(2)}, u32[]{:S(2)}) collective-permute-start(bf16[128,1024]{1,0:T(8,128)(2,1)S(1)} %fusion.3), channel_id=1, source_target_pairs={{0,0},{4,8},{8,4},{12,12},{1,1},{5,9},{9,5},{13,13},{2,2},{6,10},{... | collective-permute-start | bytes 786440 | tf_op jit(solution)/shard_map/ppermute | solution.py:402
  41.6 9.3 %collective-permute-start.10 = (bf16[128,1024]{1,0:T(8,128)(2,1)S(1)}, bf16[128,1024]{1,0:T(8,128)(2,1)S(1)}, u32[]{:S(2)}, u32[]{:S(2)}) collective-permute-start(bf16[128,1024]{1,0:T(8,128)(2,1)S(1)} %broadcast_select_fusion), channel_id=1, source_target_pairs={{0,4},{4,0},{8,12},{12,8},{1,5},{5,1},{9,13},{13,9},{2,6},{6,2},{1... | collective-permute-start | bytes 786440 | tf_op jit(solution)/shard_map/ppermute | solution.py:402
  51.2 7.2 %collective-permute-start.13 = (bf16[128,1024]{1,0:T(8,128)(2,1)S(1)}, bf16[128,1024]{1,0:T(8,128)(2,1)S(1)}, u32[]{:S(2)}, u32[]{:S(2)}) collective-permute-start(bf16[128,1024]{1,0:T(8,128)(2,1)S(1)} %get-tuple-element.97), channel_id=1, source_target_pairs={{0,0},{4,8},{8,4},{12,12},{1,1},{5,9},{9,5},{13,13},{2,2},{6,10},{... | collective-permute-start | bytes 786440 | tf_op jit(solution)/shard_map/ppermute | solution.py:402
  51.8 9.2 %collective-permute-start.14 = (bf16[128,1024]{1,0:T(8,128)(2,1)S(1)}, bf16[128,1024]{1,0:T(8,128)(2,1)S(1)}, u32[]{:S(2)}, u32[]{:S(2)}) collective-permute-start(bf16[128,1024]{1,0:T(8,128)(2,1)S(1)} %get-tuple-element.96), channel_id=1, source_target_pairs={{0,4},{4,0},{8,12},{12,8},{1,5},{5,1},{9,13},{13,9},{2,6},{6,2},{1... | collective-permute-start | bytes 786440 | tf_op jit(solution)/shard_map/ppermute | solution.py:402
  61.2 9.0 %collective-permute-start.17 = (bf16[128,1024]{1,0:T(8,128)(2,1)S(1)}, bf16[128,1024]{1,0:T(8,128)(2,1)S(1)}, u32[]{:S(2)}, u32[]{:S(2)}) collective-permute-start(bf16[128,1024]{1,0:T(8,128)(2,1)S(1)} %fusion), channel_id=1, source_target_pairs={{0,4},{4,0},{8,12},{12,8},{1,5},{5,1},{9,13},{13,9},{2,6},{6,2},{1... | collective-permute-start | bytes 786440 | tf_op jit(solution)/shard_map/ppermute | solution.py:402
  70.2 9.0 %collective-permute-start.19 = (bf16[128,1024]{1,0:T(8,128)(2,1)S(1)}, bf16[128,1024]{1,0:T(8,128)(2,1)S(1)}, u32[]{:S(2)}, u32[]{:S(2)}) collective-permute-start(bf16[128,1024]{1,0:T(8,128)(2,1)S(1)} %collective-permute-done.6.refs_4_), channel_id=1, source_target_pairs={{0,4},{4,0},{8,12},{12,8},{1,5},{5,1},{9,13},{13,9},{2,6},{6,2},{1... | collective-permute-start | bytes 786440 | tf_op jit(solution)/shard_map/ppermute | solution.py:375
  77.8 1.5 %collective-permute-start.18 = (f32[128,128]{1,0:T(8,128)}, f32[128,128]{1,0:T(8,128)S(1)}, u32[]{:S(2)}, u32[]{:S(2)}) collective-permute-start(f32[128,128]{1,0:T(8,128)} %get-tuple-element.90), channel_id=1, source_target_pairs={{0,1},{1,0},{2,3},{3,2},{4,5},{5,4},{6,7},{7,6},{8,9},{9,8},{10,11... | collective-permute-start | bytes 196616 | tf_op jit(solution)/shard_map/ppermute | solution.py:21
  81.5 14.2 %all-to-all-start = ((bf16[8,160,128]{2,1,0:T(8,128)(2,1)}), bf16[8,160,128]{2,1,0:T(8,128)(2,1)S(1)}, u32[]{:S(2)}, u32[]{:S(2)}) async-start(bf16[8,160,128]{2,1,0:T(8,128)(2,1)} %shard_map.111), calls=%async_computation | async-start | bytes 655360 | tf_op jit(solution)/shard_map/all_to_all | solution.py:547
  85.8 11.1 %collective-permute-start.20 = (bf16[160,128]{1,0:T(8,128)(2,1)S(1)}, bf16[160,128]{1,0:T(8,128)(2,1)S(1)}, u32[]{:S(2)}, u32[]{:S(2)}) collective-permute-start(bf16[160,128]{1,0:T(8,128)(2,1)S(1)} %slice_bitcast_fusion.mine_ref), channel_id=1, source_target_pairs={{0,1},{1,0},{2,3},{3,2},{4,5},{5,4},{6,7},{7,6},{8,9},{9,8},{10,11... | collective-permute-start | bytes 122888 | tf_op jit(solution)/shard_map/ppermute | solution.py:21
  95.8 8.7 %collective-permute-start.22 = (bf16[8,160,128]{2,1,0:T(8,128)(2,1)S(1)}, bf16[8,160,128]{2,1,0:T(8,128)(2,1)S(1)}, u32[]{:S(2)}, u32[]{:S(2)}) collective-permute-start(bf16[8,160,128]{2,1,0:T(8,128)(2,1)S(1)} %all-to-all-done.refs_12_), channel_id=1, source_target_pairs={{0,1},{1,0},{2,3},{3,2},{4,5},{5,4},{6,7},{7,6},{8,9},{9,8},{10,11... | collective-permute-start | bytes 983048 | tf_op jit(solution)/shard_map/ppermute | solution.py:21
  95.8 8.7 %collective-permute-start.21 = (bf16[128,1024]{1,0:T(8,128)(2,1)S(1)}, bf16[128,1024]{1,0:T(8,128)(2,1)S(1)}, u32[]{:S(2)}, u32[]{:S(2)}) collective-permute-start(bf16[128,1024]{1,0:T(8,128)(2,1)S(1)} %collective-permute-done.12.refs_10_), channel_id=1, source_target_pairs={{0,4},{4,0},{8,12},{12,8},{1,5},{5,1},{9,13},{13,9},{2,6},{6,2},{1... | collective-permute-start | bytes 786440 | tf_op jit(solution)/shard_map/ppermute | solution.py:375
  (27 other events, 214.6 us)

commit v7 on v6

--- a/solution.py
+++ b/solution.py
@@ -116,10 +116,13 @@
     )
 
 
-def state_kernel(count, size, *refs):
+def state_kernel(count, size, ride, *refs):
     proj = refs[:count]
-    x_ref, g_ref, rate_ref, bias_ref, own_ref, decay_ref, bc_ref, hp_ref = refs[count : count + 8]
-    firsts = refs[count + 8 :]
+    x_ref, g_ref, rate_ref, bias_ref = refs[count : count + 4]
+    riders = refs[count + 4 : count + 4 + ride]
+    own_ref, bc_ref, hp_ref = refs[count + 4 + ride : count + 7 + ride]
+    outs = refs[count + 7 + ride :]
+    firsts, decays = outs[: len(outs) // 2], outs[len(outs) // 2 :]
     heads = rate_ref.shape[1]
     rows = x_ref.shape[0]
     rate, bias = rate_ref[...].T, bias_ref[...].T
@@ -141,14 +144,15 @@
     decay = jnp.exp(last)
     for k, part in enumerate((pre, dt, cum, grow, w)):
         hp_ref[k * heads : (k + 1) * heads, :] = part
-    lowest = lax.axis_index("seq") == 0
+    place = lax.axis_index("seq")
+    lowest = place == 0
     sides = []
     for vec in (bc[:rows], bc[rows:]):
         high, low = halves(vec.T)
         sides.append((jnp.concatenate([high, low], axis=1), high))
     for k in range(chunks):
         pick = head_lanes(heads, step, size, k * step)
-        decay_ref[k] = jnp.sum(pick * decay, axis=0, keepdims=True)
+        decays[k][...] = jnp.sum(pick * decay, axis=0, keepdims=True)
         pick = pick.astype(BF)
         both = []
         for kind, (scale, ref) in enumerate(((w, x_ref), (grow, g_ref))):
@@ -159,6 +163,12 @@
             own_ref[kind, k] = value
             both.append(value)
         firsts[k][...] = jnp.where(lowest, both[0], both[1]).astype(BF)
+        if k < ride:
+            rider = riders[k]
+
+            @pl.when((place > 0) & (place < lax.axis_size("seq") - 1))
+            def _():
+                firsts[k][...] = rider[...]
 
 
 def inner_kernel(first, pairs, size, bc_ref, hp_ref, x_ref, g_ref, *refs):
@@ -209,13 +219,13 @@
 
 
 def outer_kernel(size, parts, *refs):
-    store_ref, x_ref, g_ref, bc_ref, hp_ref, decay_ref, rate_ref = refs[:7]
-    gxs, dss, sums = (refs[7 + k * parts : 7 + (k + 1) * parts] for k in range(3))
-    grad_ref, keep_ref, give_ref, wv_ref, eu_ref, io_ref = refs[7 + 3 * parts :]
+    store_ref, x_ref, g_ref, bc_ref, hp_ref, rate_ref = refs[:6]
+    gxs, dss, sums = (refs[6 + k * parts : 6 + (k + 1) * parts] for k in range(3))
+    grad_ref, keep_ref, give_ref, wv_ref, eu_ref, io_ref = refs[6 + 3 * parts :]
     rate = rate_ref[...].T
     rows, width = x_ref.shape
     heads = rate_ref.shape[1]
-    chunks, step = decay_ref.shape[0], decay_ref.shape[2]
+    chunks, step = store_ref.shape[1] - 1, store_ref.shape[3]
     piece = width // parts
     b, c = bc_ref[0:rows, :], bc_ref[rows : 2 * rows, :]
     pre, dt, cum, grow, w = (hp_ref[k * heads : (k + 1) * heads, :] for k in range(5))
@@ -376,7 +386,7 @@
     return [found[step] for step in steps]
 
 
-def chains(first, own, decay, inner, beside, riders):
+def chains(first, own, decay, inner, beside, riders, late):
     count = lax.axis_size("seq")
     place = lax.axis_index("seq")
     chunks = len(first)
@@ -389,7 +399,7 @@
         sent = []
         for hop, k in steps:
             value = got[k]
-            if hop == 1 and k < len(riders):
+            if hop == 1 and 0 < k < len(riders):
                 value = jnp.where((place == 0) | (place == count - 1), value, riders[k])
             if hop > 1:
                 value = jnp.where(place == hop - 1, own[0, k], own[1, k])
@@ -406,19 +416,22 @@
             done.append(todo.pop(0)(*sent))
         if slot == 1:
             extra, soon = beside(*sent)
+        if slot == last:
+            late(*sent)
         if slot < last:
             held = [got[k] for _, k in steps] + [d[0] for d in done[-1:]]
             if slot == last - 1:
                 held += extra
-            if slot == 2:
+            if slot == 1:
                 held += soon
-            if slot == 1 and chunks > 1:
-                held.append(got[1])
+            new = slot < chunks
+            if new:
+                held.append(got[slot])
             kept = lax.optimization_barrier(tuple(held))
             for (_, k), a in zip(steps, kept):
                 got[k] = a
-            if slot == 1 and chunks > 1:
-                got[1] = kept[-1]
+            if new:
+                got[slot] = kept[-1]
         for hop, k in steps:
             kind = jnp.where(place == hop, 0, 1)
             fits = (place == hop) | (place == count - hop - 1)
@@ -451,31 +464,35 @@
     ride = n_seq == 4 and all(a.shape == (state_n, step) for a in groups)
     second = [(kind, hop) for kind, hop in slots if hop == 2 and not (ride and kind == 0)]
     near = relay(found[0], groups[0], slots[:2])
-    partials = [project(items[0], w_bc, w_dt)] + [
-        cyclic(project(items[r], w_bc, w_dt), "dp", -r) for r in range(1, n_dp)
-    ]
+    partials = [project(items[0], w_bc, w_dt)]
+    for r in range(1, n_dp):
+        item = after(items[r], partials[0])
+        partials.append(cyclic(project(item, w_bc, w_dt), "dp", -r))
     partials[1:] = [after(a, *near) for a in partials[1:]]
     proj = partials + [cyclic(a, "head", 1) for a in partials]
     x = after(x, *relay(found[0], groups[0], second))
     early = []
     if n_dp > 1:
-        early = relay(found[1], groups[1], slots[:2], *proj[n_dp - 1 : n_dp])
-    own, decay, bc, hp, *first = call(
-        functools.partial(state_kernel, 2 * n_dp, size),
+        early = relay(found[1], groups[1], slots[: 1 if ride else 2])
+        x = after(x, *early)
+    own, bc, hp, *outs = call(
+        functools.partial(state_kernel, 2 * n_dp, size, int(ride)),
         (
             struct((2, CHUNKS, state_n, step), F32),
-            struct((CHUNKS, 1, step), F32),
             struct((2 * rows, state_n), F32),
             struct((5 * heads, rows), F32),
         )
-        + (struct((state_n, step), BF),) * CHUNKS,
-        4.9,
+        + (struct((state_n, step), BF),) * CHUNKS
+        + (struct((1, step), F32),) * CHUNKS,
+        1.0,
         *proj,
         x,
         g,
         rate,
         bias,
-    )
+        *([found[0][1, 1]] if ride else []),
+    )
+    first, decay = outs[:CHUNKS], outs[CHUNKS:]
     pairs = width // (2 * size) // PARTS
     span = width // PARTS
     shared = []
@@ -507,15 +524,23 @@
     def beside(*others):
         for r in range(1, n_dp):
             weights.extend(cyclic(after(a, *others), "dp", r) for a in (w_bc, w_dt))
-        return weights[2:], relay(found[1], groups[1], second, *others) if n_dp > 1 else []
-
-    first[0] = after(first[0], *early)
-    riders = [f[1, 1] for f in found] if ride else []
+        if not ride or n_dp == 1:
+            return weights[2:], []
+        riders.extend(relay(found[1], groups[1], [(1, 1)], *others))
+        return weights[2:], riders[1:]
+
+    def late(*others):
+        if n_dp > 1:
+            relay(found[1], groups[1], second, *others)
+
+    riders = [found[0][1, 1]] if ride else []
     calls = [functools.partial(inner, q) for q in range(PARTS)]
-    store, inners = chains(first, own, decay, calls, beside, riders)
+    store, inners = chains(first, own, decay, calls, beside, riders, late)
     for f, a in zip(found, riders):
         f[0, 2] = a
-    done = relay(found[0], groups[0], [step for step in slots if step not in found[0]], store)
+    done = []
+    for f, a in zip(found, groups):
+        done += relay(f, a, [step for step in slots if step not in f], store)
     grad_x, keep, give = call(
         functools.partial(outer_kernel, size, PARTS),
         (
@@ -529,7 +554,6 @@
         g,
         bc,
         hp,
-        decay,
         rate,
         *[a[0] for a in inners],
         *[a[1] for a in inners],
@@ -557,7 +581,6 @@
     )
     toks = []
     for f, a in zip(found, groups):
-        relay(f, a, [step for step in slots if step not in f], store)
         toks += [a] + [f[step] for step in slots]
     slots = [(0, 0)] + slots
     cols = 2 * (rows + heads)

time: 111 us -> 107 us (0.964)
  waiting for transfers between devices: 29.1 us -> 27.4 us
  local copies, waits for them, and re-layouts: 5.97 us -> 4.44 us
  other arithmetic: 1.74 us -> 0.51 us
    ppermute x9, waiting for transfers between devices: 5.85 us -> 2.69 us  [cyclic(): return lax.ppermute(a, axis, [(i, (i + by) % count) for i in range(count)])]
    select_n x2 -> x1, other arithmetic: 1.19 us -> 0.03 us  [chains(): value = jnp.where((place == 0) | (place == count - 1), value, riders[k])]
    unnamed x54 -> x60, local copies, waits for them, and re-layouts: 4.17 us -> 3.33 us
  transfers between devices with their start and end apart: 24 -> 24, of which waited for: 9 -> 8; matrix products, arithmetic and copies ran while one was open for 2% -> 1% of each run, Pallas kernels for 25% -> 22%
where the time goes in v7:
time: 107 us; the launch traced here: 106 us
  starting transfers between devices  37.1 us (35%)
  Pallas kernels  35.6 us (33%)
  waiting for transfers between devices  27.4 us (26%)
  local copies, waits for them, and re-layouts  4.44 us (4%)
    pallas_call x12, Pallas kernels, call(): pl.pallas_call(kernel, out_shape=out_shape, grid=(1,), in_specs=specs or...  35.6 us
    ppermute x6, starting transfers between devices, chains(): got[k] = lax.ppermute(value, 'seq', sorted(to.items()))  14.4 us
    ppermute x8, starting transfers between devices, relay(): found[kind, hop] = lax.ppermute(source, 'seq', pairs[kind])  11.7 us
    ppermute x6, waiting for transfers between devices, chains(): got[k] = lax.ppermute(value, 'seq', sorted(to.items()))  10.1 us
    all_to_all x1, waiting for transfers between devices, body(): lows = lax.all_to_all(copies, ('seq', 'dp'), 0, 0, tiled=True)  9.85 us
    ppermute x9, starting transfers between devices, cyclic(): return lax.ppermute(a, axis, [(i, (i + by) % count) for i in range(count)])  7.41 us
    ppermute x8, waiting for transfers between devices, relay(): found[kind, hop] = lax.ppermute(source, 'seq', pairs[kind])  4.81 us
    all_to_all x1, starting transfers between devices, body(): lows = lax.all_to_all(copies, ('seq', 'dp'), 0, 0, tiled=True)  3.6 us
  transfers between devices with their start and end apart: 24, of which 8 were waited for; matrix products, arithmetic and copies ran while one was open for 1% of the time, Pallas kernels for 22%

profile of v7, /device:TPU:0, one launch (start us, length us, event | category | flops | bytes accessed | tf_op | source)
XLA Modules:
  0.0 106.0 jit_solution(15083481516869434841)
XLA Ops:
  0.6 1.9 %shard_map.102 = (bf16[128,1024]{1,0:T(8,128)(2,1)}, bf16[128,1024]{1,0:T(8,128)(2,1)}) custom-call(bf16[128,2048]{1,0:T(8,128)(2,1)} %bitcast.45), custom_call_target="tpu_custom_call" | custom-call | flops 2184999936 | bytes 524288 | tf_op jit(solution)/shard_map/pallas_call | solution.py:54
  2.5 2.9 %collective-permute-start = (bf16[128,1024]{1,0:T(8,128)(2,1)}, bf16[128,1024]{1,0:T(8,128)(2,1)S(1)}, u32[]{:S(2)}, u32[]{:S(2)}) collective-permute-start(bf16[128,1024]{1,0:T(8,128)(2,1)} %get-tuple-element.53), channel_id=1, source_target_pairs={{0,2},{2,0},{1,3},{3,1},{4,6},{6,4},{5,7},{7,5},{8,10},{10,8},{9,1... | collective-permute-start | bytes 786440 | tf_op jit(solution)/shard_map/ppermute | solution.py:21
  8.6 2.1 %shard_map.103.refs_0_ = f32[320,128]{1,0:T(8,128)} custom-call(bf16[128,1024]{1,0:T(8,128)(2,1)} %get-tuple-element.52.a_ref.refs_0_, bf16[1024,256]{1,0:T(8,128)(2,1)} %refs_0_.1, bf16[64,1024]{1,0:T(8,128)(2,1)} %bitcast.58), custom_call_target="tpu_custom_call" | custom-call | flops 2415000064 | bytes 917504 | tf_op jit(solution)/shard_map/pallas_call | solution.py:54
  12.7 2.1 %shard_map.104 = f32[320,128]{1,0:T(8,128)} custom-call(bf16[128,1024]{1,0:T(8,128)(2,1)} %copy-done.13, bf16[1024,256]{1,0:T(8,128)(2,1)} %refs_0_.1, bf16[64,1024]{1,0:T(8,128)(2,1)} %bitcast.59), custom_call_target="tpu_custom_call" | custom-call | flops 2415000064 | bytes 917504 | tf_op jit(solution)/shard_map/pallas_call | solution.py:54
  14.8 1.7 %collective-permute-start.1 = (f32[320,128]{1,0:T(8,128)}, f32[320,128]{1,0:T(8,128)S(1)}, u32[]{:S(2)}, u32[]{:S(2)}) collective-permute-start(f32[320,128]{1,0:T(8,128)} %shard_map.104), channel_id=1, source_target_pairs={{0,2},{2,0},{1,3},{3,1},{4,6},{6,4},{5,7},{7,5},{8,10},{10,8},{9,1... | collective-permute-start | bytes 491528 | tf_op jit(solution)/shard_map/ppermute | solution.py:21
  17.2 4.5 %collective-permute-start.7 = (bf16[128,1024]{1,0:T(8,128)(2,1)}, bf16[128,1024]{1,0:T(8,128)(2,1)S(1)}, u32[]{:S(2)}, u32[]{:S(2)}) collective-permute-start(bf16[128,1024]{1,0:T(8,128)(2,1)} %copy-done.13), channel_id=1, source_target_pairs={{0,4},{4,0},{8,12},{12,8},{1,5},{5,1},{9,13},{13,9},{2,6},{6,2},{1... | collective-permute-start | bytes 786440 | tf_op jit(solution)/shard_map/ppermute | solution.py:385
  22.3 4.5 %collective-permute-done.7.refs_7_ = bf16[128,1024]{1,0:T(8,128)(2,1)S(1)} collective-permute-done((bf16[128,1024]{1,0:T(8,128)(2,1)}, bf16[128,1024]{1,0:T(8,128)(2,1)S(1)}, u32[]{:S(2)}, u32[]{:S(2)}) %collective-permute-start.7) | collective-permute-done | bytes 262176 | tf_op jit(solution)/shard_map/ppermute | solution.py:385
  27.5 5.2 %shard_map.105 = (f32[2,2,128,1024]{3,2,1,0:T(8,128)}, f32[256,128]{1,0:T(8,128)}, f32[160,128]{1,0:T(8,128)}, bf16[128,1024]{1,0:T(8,128)(2,1)}, bf16[128,1024]...) custom-call(f32[320,128]{1,0:T(8,128)} %shard_map.103.refs_0_, f32[320,128]{1,0:T(8,128)} %copy-done.23, ...), custom_call_target="tpu_custom_call" | custom-call | flops 1150000000 | bytes 1966336 | tf_op jit(solution)/shard_map/pallas_call | solution.py:54
  32.7 1.8 %collective-permute-start.8 = (bf16[128,1024]{1,0:T(8,128)(2,1)}, bf16[128,1024]{1,0:T(8,128)(2,1)S(1)}, u32[]{:S(2)}, u32[]{:S(2)}) collective-permute-start(bf16[128,1024]{1,0:T(8,128)(2,1)} %get-tuple-element.58), channel_id=1, source_target_pairs={{0,4},{4,0},{8,12},{12,8},{1,5},{5,1},{9,13},{13,9},{2,6},{6,2},{1... | collective-permute-start | bytes 786440 | tf_op jit(solution)/shard_map/ppermute | solution.py:412
  37.3 2.9 %shard_map.106 = (f32[128,128]{1,0:T(8,128)}, f32[128,512]{1,0:T(8,128)}, f32[128,128]{1,0:T(8,128)}, f32[2,8,128]{2,1,0:T(8,128)}) custom-call(f32[256,128]{1,0:T(8,128)} %get-tuple-element.81.bc_ref.refs_3_, f32[160,128]{1,0:T(8,128)} %get-tuple-element.61.hp_ref.refs_4_, bf16[128,2048]{1,0:T(8,128)(2,1)} %bitcast.47, bf16[128,2048]{1,0:T(8,128)(2,1)} %bitcast.53), custom_call_target="tpu_custom_call" | custom-call | flops 2990000128 | bytes 1261568 | tf_op jit(solution)/shard_map/pallas_call | solution.py:54
  41.3 4.7 %collective-permute-start.10 = (bf16[128,1024]{1,0:T(8,128)(2,1)S(1)}, bf16[128,1024]{1,0:T(8,128)(2,1)S(1)}, u32[]{:S(2)}, u32[]{:S(2)}) collective-permute-start(bf16[128,1024]{1,0:T(8,128)(2,1)S(1)} %broadcast_select_fusion), channel_id=1, source_target_pairs={{0,4},{4,0},{8,12},{12,8},{1,5},{5,1},{9,13},{13,9},{2,6},{6,2},{1... | collective-permute-start | bytes 786440 | tf_op jit(solution)/shard_map/ppermute | solution.py:412
  46.2 2.6 %shard_map.107 = (f32[128,512]{1,0:T(8,128)}, f32[128,128]{1,0:T(8,128)}, f32[2,8,128]{2,1,0:T(8,128)}) custom-call(f32[256,128]{1,0:T(8,128)} %get-tuple-element.81.bc_ref.refs_3_, f32[160,128]{1,0:T(8,128)} %get-tuple-element.61.hp_ref.refs_4_, bf16[128,2048]{1,0:T(8,128)(2,1)} %bitcast.48, bf16[128,2048]{1,0:T(8,128)(2,1)} %bitcast.54, ...), custom_call_target="tpu_custom_call" | custom-call | flops 2990000128 | bytes 1327104 | tf_op jit(solution)/shard_map/pallas_call | solution.py:54
  51.3 4.5 %collective-permute-start.13 = (bf16[128,1024]{1,0:T(8,128)(2,1)S(1)}, bf16[128,1024]{1,0:T(8,128)(2,1)S(1)}, u32[]{:S(2)}, u32[]{:S(2)}) collective-permute-start(bf16[128,1024]{1,0:T(8,128)(2,1)S(1)} %get-tuple-element.100), channel_id=1, source_target_pairs={{0,4},{4,0},{8,12},{12,8},{1,5},{5,1},{9,13},{13,9},{2,6},{6,2},{1... | collective-permute-start | bytes 786440 | tf_op jit(solution)/shard_map/ppermute | solution.py:412
  55.9 2.6 %shard_map.108 = (f32[128,512]{1,0:T(8,128)}, f32[128,128]{1,0:T(8,128)}, f32[2,8,128]{2,1,0:T(8,128)}) custom-call(f32[256,128]{1,0:T(8,128)} %get-tuple-element.81.bc_ref.refs_3_, f32[160,128]{1,0:T(8,128)} %get-tuple-element.61.hp_ref.refs_4_, bf16[128,2048]{1,0:T(8,128)(2,1)} %bitcast.49, bf16[128,2048]{1,0:T(8,128)(2,1)} %bitcast.55, ...), custom_call_target="tpu_custom_call" | custom-call | flops 2990000128 | bytes 1327104 | tf_op jit(solution)/shard_map/pallas_call | solution.py:54
  58.5 4.4 %collective-permute-done.13 = bf16[128,1024]{1,0:T(8,128)(2,1)S(1)} collective-permute-done((bf16[128,1024]{1,0:T(8,128)(2,1)S(1)}, bf16[128,1024]{1,0:T(8,128)(2,1)S(1)}, u32[]{:S(2)}, u32[]{:S(2)}) %collective-permute-start.13) | collective-permute-done | bytes 262176 | tf_op jit(solution)/shard_map/ppermute | solution.py:412
  63.0 1.8 %collective-permute-start.16 = (bf16[128,1024]{1,0:T(8,128)(2,1)S(1)}, bf16[128,1024]{1,0:T(8,128)(2,1)S(1)}, u32[]{:S(2)}, u32[]{:S(2)}) collective-permute-start(bf16[128,1024]{1,0:T(8,128)(2,1)S(1)} %fusion), channel_id=1, source_target_pairs={{0,4},{4,0},{8,12},{12,8},{1,5},{5,1},{9,13},{13,9},{2,6},{6,2},{1... | collective-permute-start | bytes 786440 | tf_op jit(solution)/shard_map/ppermute | solution.py:412
  65.5 2.6 %shard_map.109 = (f32[128,512]{1,0:T(8,128)}, f32[128,128]{1,0:T(8,128)}, f32[2,8,128]{2,1,0:T(8,128)}) custom-call(f32[256,128]{1,0:T(8,128)} %get-tuple-element.81.bc_ref.refs_3_, f32[160,128]{1,0:T(8,128)} %get-tuple-element.61.hp_ref.refs_4_, bf16[128,2048]{1,0:T(8,128)(2,1)} %bitcast.50, bf16[128,2048]{1,0:T(8,128)(2,1)} %bitcast.56, ...), custom_call_target="tpu_custom_call" | custom-call | flops 2990000128 | bytes 1327104 | tf_op jit(solution)/shard_map/pallas_call | solution.py:54
  68.2 4.1 %collective-permute-done.16 = bf16[128,1024]{1,0:T(8,128)(2,1)S(1)} collective-permute-done((bf16[128,1024]{1,0:T(8,128)(2,1)S(1)}, bf16[128,1024]{1,0:T(8,128)(2,1)S(1)}, u32[]{:S(2)}, u32[]{:S(2)}) %collective-permute-start.16) | collective-permute-done | bytes 262176 | tf_op jit(solution)/shard_map/ppermute | solution.py:412
  72.3 1.8 %collective-permute-start.20 = (bf16[128,1024]{1,0:T(8,128)(2,1)S(1)}, bf16[128,1024]{1,0:T(8,128)(2,1)S(1)}, u32[]{:S(2)}, u32[]{:S(2)}) collective-permute-start(bf16[128,1024]{1,0:T(8,128)(2,1)S(1)} %collective-permute-done.19.refs_10_), channel_id=1, source_target_pairs={{0,4},{4,0},{8,12},{12,8},{1,5},{5,1},{9,13},{13,9},{2,6},{6,2},{1... | collective-permute-start | bytes 786440 | tf_op jit(solution)/shard_map/ppermute | solution.py:385
  74.4 5.3 %shard_map.110 = (bf16[128,2048]{1,0:T(8,128)(2,1)}, f32[160,128]{1,0:T(8,128)}, f32[128,128]{1,0:T(8,128)}) custom-call(bf16[2,3,128,1024]{3,2,1,0:T(8,128)(2,1)} %copy-done.1, bf16[128,2048]{1,0:T(8,128)(2,1)} %bitcast.51, bf16[128,2048]{1,0:T(8,128)(2,1)} %bitcast.57, f32[256,128]{1,0:T(8,128)} %get-tuple-element.81.bc_ref.refs_3_, ...), custom_call_target="tpu_custom_call" | custom-call | flops 6209999872 | bytes 4178048 | tf_op jit(solution)/shard_map/pallas_call | solution.py:54
  83.5 3.6 %all-to-all-start = ((bf16[8,160,128]{2,1,0:T(8,128)(2,1)}), bf16[8,160,128]{2,1,0:T(8,128)(2,1)S(1)}, u32[]{:S(2)}, u32[]{:S(2)}) async-start(bf16[8,160,128]{2,1,0:T(8,128)(2,1)} %shard_map.111), calls=%async_computation | async-start | bytes 655360 | tf_op jit(solution)/shard_map/all_to_all | solution.py:571
  87.9 9.8 %all-to-all-done.refs_12_ = bf16[8,160,128]{2,1,0:T(8,128)(2,1)S(1)} async-done(((bf16[8,160,128]{2,1,0:T(8,128)(2,1)}), bf16[8,160,128]{2,1,0:T(8,128)(2,1)S(1)}, u32[]{:S(2)}, u32[]{:S(2)}) %all-to-all-start) | async-done | bytes 327712 | tf_op jit(solution)/shard_map/all_to_all | solution.py:571
  98.5 2.9 %shard_map.112 = bf16[128,2048]{1,0:T(8,128)(2,1)} custom-call(bf16[160,128]{1,0:T(8,128)(2,1)} %copy-done.7, bf16[160,128]{1,0:T(8,128)(2,1)} %copy-done.29, bf16[1024,256]{1,0:T(8,128)(2,1)} %refs_0_.1, bf16[64,1024]{1,0:T(8,128)(2,1)} %bitcast.60, bf16[1024,256]{1,0:T(8,128)(2,1)} %copy-done.11, bf16[64,1024]{1,0:T(8,128)(2,1)} %copy-done.27), custom_call_target="tpu_custom_call" | custom-call | flops 3335000064 | bytes 1392640 | tf_op jit(solution)/shard_map/pallas_call | solution.py:54
  102.0 4.0 %shard_map.113 = (f32[1024,256]{1,0:T(8,128)}, f32[64,1024]{1,0:T(8,128)}) custom-call(bf16[128,1024]{1,0:T(8,128)(2,1)} %get-tuple-element.52.a_ref.refs_0_, bf16[128,1024]{1,0:T(8,128)(2,1)} %copy-done.15, bf16[128,1024]{1,0:T(8,128)(2,1)} %copy-done.16, bf16[128,1024]{1,0:T(8,128)(2,1)} %copy-done.3, bf16[128,1024]{1,0:T(8,128)(2,1)} %copy-done.17, ...), custom_call_target="tpu_custom_call" | custom-call | flops 4600000000 | bytes 3801088 | tf_op jit(solution)/shard_map/pallas_call | solution.py:54
  (108 shorter events, 20.8 us)
Async XLA Ops:
  2.5 9.5 %collective-permute-start = (bf16[128,1024]{1,0:T(8,128)(2,1)}, bf16[128,1024]{1,0:T(8,128)(2,1)S(1)}, u32[]{:S(2)}, u32[]{:S(2)}) collective-permute-start(bf16[128,1024]{1,0:T(8,128)(2,1)} %get-tuple-element.53), channel_id=1, source_target_pairs={{0,2},{2,0},{1,3},{3,1},{4,6},{6,4},{5,7},{7,5},{8,10},{10,8},{9,1... | collective-permute-start | bytes 786440 | tf_op jit(solution)/shard_map/ppermute | solution.py:21
  5.4 11.1 %collective-permute-start.2 = (bf16[128,1024]{1,0:T(8,128)(2,1)}, bf16[128,1024]{1,0:T(8,128)(2,1)S(1)}, u32[]{:S(2)}, u32[]{:S(2)}) collective-permute-start(bf16[128,1024]{1,0:T(8,128)(2,1)} %get-tuple-element.52.a_ref.refs_0_), channel_id=1, source_target_pairs={{0,4},{4,0},{8,12},{12,8},{1,5},{5,1},{9,13},{13,9},{2,6},{6,2},{1... | collective-permute-start | bytes 786440 | tf_op jit(solution)/shard_map/ppermute | solution.py:385
  7.0 14.6 %collective-permute-start.3 = (bf16[128,1024]{1,0:T(8,128)(2,1)}, bf16[128,1024]{1,0:T(8,128)(2,1)S(1)}, u32[]{:S(2)}, u32[]{:S(2)}) collective-permute-start(bf16[128,1024]{1,0:T(8,128)(2,1)} %get-tuple-element.52.a_ref.refs_0_), channel_id=1, source_target_pairs={{0,0},{4,8},{8,4},{12,12},{1,1},{5,9},{9,5},{13,13},{2,2},{6,10},{... | collective-permute-start | bytes 786440 | tf_op jit(solution)/shard_map/ppermute | solution.py:385
  14.8 6.9 %collective-permute-start.1 = (f32[320,128]{1,0:T(8,128)}, f32[320,128]{1,0:T(8,128)S(1)}, u32[]{:S(2)}, u32[]{:S(2)}) collective-permute-start(f32[320,128]{1,0:T(8,128)} %shard_map.104), channel_id=1, source_target_pairs={{0,2},{2,0},{1,3},{3,1},{4,6},{6,4},{5,7},{7,5},{8,10},{10,8},{9,1... | collective-permute-start | bytes 491528 | tf_op jit(solution)/shard_map/ppermute | solution.py:21
  16.5 5.7 %collective-permute-start.6 = (bf16[128,1024]{1,0:T(8,128)(2,1)S(1)}, bf16[128,1024]{1,0:T(8,128)(2,1)S(1)}, u32[]{:S(2)}, u32[]{:S(2)}) collective-permute-start(bf16[128,1024]{1,0:T(8,128)(2,1)S(1)} %collective-permute-done.2.refs_1_), channel_id=1, source_target_pairs={{0,0},{4,8},{8,4},{12,12},{1,1},{5,9},{9,5},{13,13},{2,2},{6,10},{... | collective-permute-start | bytes 786440 | tf_op jit(solution)/shard_map/ppermute | solution.py:385
  17.2 9.5 %collective-permute-start.7 = (bf16[128,1024]{1,0:T(8,128)(2,1)}, bf16[128,1024]{1,0:T(8,128)(2,1)S(1)}, u32[]{:S(2)}, u32[]{:S(2)}) collective-permute-start(bf16[128,1024]{1,0:T(8,128)(2,1)} %copy-done.13), channel_id=1, source_target_pairs={{0,4},{4,0},{8,12},{12,8},{1,5},{5,1},{9,13},{13,9},{2,6},{6,2},{1... | collective-permute-start | bytes 786440 | tf_op jit(solution)/shard_map/ppermute | solution.py:385
  21.6 5.1 %collective-permute-start.4 = (f32[320,128]{1,0:T(8,128)S(1)}, f32[320,128]{1,0:T(8,128)S(1)}, u32[]{:S(2)}, u32[]{:S(2)}) collective-permute-start(f32[320,128]{1,0:T(8,128)S(1)} %copy-done.22), channel_id=1, source_target_pairs={{0,1},{1,0},{2,3},{3,2},{4,5},{5,4},{6,7},{7,6},{8,9},{9,8},{10,11... | collective-permute-start | bytes 491528 | tf_op jit(solution)/shard_map/ppermute | solution.py:21
  21.7 5.0 %collective-permute-start.5 = (f32[320,128]{1,0:T(8,128)S(1)}, f32[320,128]{1,0:T(8,128)S(1)}, u32[]{:S(2)}, u32[]{:S(2)}) collective-permute-start(f32[320,128]{1,0:T(8,128)S(1)} %collective-permute-done.1.refs_1_), channel_id=1, source_target_pairs={{0,1},{1,0},{2,3},{3,2},{4,5},{5,4},{6,7},{7,6},{8,9},{9,8},{10,11... | collective-permute-start | bytes 491528 | tf_op jit(solution)/shard_map/ppermute | solution.py:21
  32.7 7.5 %collective-permute-start.8 = (bf16[128,1024]{1,0:T(8,128)(2,1)}, bf16[128,1024]{1,0:T(8,128)(2,1)S(1)}, u32[]{:S(2)}, u32[]{:S(2)}) collective-permute-start(bf16[128,1024]{1,0:T(8,128)(2,1)} %get-tuple-element.58), channel_id=1, source_target_pairs={{0,4},{4,0},{8,12},{12,8},{1,5},{5,1},{9,13},{13,9},{2,6},{6,2},{1... | collective-permute-start | bytes 786440 | tf_op jit(solution)/shard_map/ppermute | solution.py:412
  34.5 5.7 %collective-permute-start.9 = (bf16[128,1024]{1,0:T(8,128)(2,1)S(1)}, bf16[128,1024]{1,0:T(8,128)(2,1)S(1)}, u32[]{:S(2)}, u32[]{:S(2)}) collective-permute-start(bf16[128,1024]{1,0:T(8,128)(2,1)S(1)} %copy-done.14), channel_id=1, source_target_pairs={{0,0},{4,8},{8,4},{12,12},{1,1},{5,9},{9,5},{13,13},{2,2},{6,10},{... | collective-permute-start | bytes 786440 | tf_op jit(solution)/shard_map/ppermute | solution.py:385
  35.2 23.3 %collective-permute-start.15 = (bf16[64,1024]{1,0:T(8,128)(2,1)S(1)}, bf16[64,1024]{1,0:T(8,128)(2,1)S(1)}, u32[]{:S(2)}, u32[]{:S(2)}) collective-permute-start(bf16[64,1024]{1,0:T(8,128)(2,1)S(1)} %bitcast.61), channel_id=1, source_target_pairs={{0,2},{2,0},{1,3},{3,1},{4,6},{6,4},{5,7},{7,5},{8,10},{10,8},{9,1... | collective-permute-start | bytes 393224 | tf_op jit(solution)/shard_map/ppermute | solution.py:21
  35.8 22.7 %collective-permute-start.14 = (bf16[1024,256]{1,0:T(8,128)(2,1)S(1)}, bf16[1024,256]{1,0:T(8,128)(2,1)S(1)}, u32[]{:S(2)}, u32[]{:S(2)}) collective-permute-start(bf16[1024,256]{1,0:T(8,128)(2,1)S(1)} %copy-done.10), channel_id=1, source_target_pairs={{0,2},{2,0},{1,3},{3,1},{4,6},{6,4},{5,7},{7,5},{8,10},{10,8},{9,1... | collective-permute-start | bytes 1572872 | tf_op jit(solution)/shard_map/ppermute | solution.py:21
  40.3 8.5 %collective-permute-start.11 = (bf16[128,1024]{1,0:T(8,128)(2,1)S(1)}, bf16[128,1024]{1,0:T(8,128)(2,1)S(1)}, u32[]{:S(2)}, u32[]{:S(2)}) collective-permute-start(bf16[128,1024]{1,0:T(8,128)(2,1)S(1)} %fusion.3), channel_id=1, source_target_pairs={{0,0},{4,8},{8,4},{12,12},{1,1},{5,9},{9,5},{13,13},{2,2},{6,10},{... | collective-permute-start | bytes 786440 | tf_op jit(solution)/shard_map/ppermute | solution.py:412
  41.3 9.1 %collective-permute-start.10 = (bf16[128,1024]{1,0:T(8,128)(2,1)S(1)}, bf16[128,1024]{1,0:T(8,128)(2,1)S(1)}, u32[]{:S(2)}, u32[]{:S(2)}) collective-permute-start(bf16[128,1024]{1,0:T(8,128)(2,1)S(1)} %broadcast_select_fusion), channel_id=1, source_target_pairs={{0,4},{4,0},{8,12},{12,8},{1,5},{5,1},{9,13},{13,9},{2,6},{6,2},{1... | collective-permute-start | bytes 786440 | tf_op jit(solution)/shard_map/ppermute | solution.py:412
  50.6 7.9 %collective-permute-start.12 = (bf16[128,1024]{1,0:T(8,128)(2,1)S(1)}, bf16[128,1024]{1,0:T(8,128)(2,1)S(1)}, u32[]{:S(2)}, u32[]{:S(2)}) collective-permute-start(bf16[128,1024]{1,0:T(8,128)(2,1)S(1)} %get-tuple-element.101), channel_id=1, source_target_pairs={{0,0},{4,8},{8,4},{12,12},{1,1},{5,9},{9,5},{13,13},{2,2},{6,10},{... | collective-permute-start | bytes 786440 | tf_op jit(solution)/shard_map/ppermute | solution.py:412
  51.3 11.6 %collective-permute-start.13 = (bf16[128,1024]{1,0:T(8,128)(2,1)S(1)}, bf16[128,1024]{1,0:T(8,128)(2,1)S(1)}, u32[]{:S(2)}, u32[]{:S(2)}) collective-permute-start(bf16[128,1024]{1,0:T(8,128)(2,1)S(1)} %get-tuple-element.100), channel_id=1, source_target_pairs={{0,4},{4,0},{8,12},{12,8},{1,5},{5,1},{9,13},{13,9},{2,6},{6,2},{1... | collective-permute-start | bytes 786440 | tf_op jit(solution)/shard_map/ppermute | solution.py:412
  63.0 9.2 %collective-permute-start.16 = (bf16[128,1024]{1,0:T(8,128)(2,1)S(1)}, bf16[128,1024]{1,0:T(8,128)(2,1)S(1)}, u32[]{:S(2)}, u32[]{:S(2)}) collective-permute-start(bf16[128,1024]{1,0:T(8,128)(2,1)S(1)} %fusion), channel_id=1, source_target_pairs={{0,4},{4,0},{8,12},{12,8},{1,5},{5,1},{9,13},{13,9},{2,6},{6,2},{1... | collective-permute-start | bytes 786440 | tf_op jit(solution)/shard_map/ppermute | solution.py:412
  64.8 7.5 %collective-permute-start.19 = (bf16[128,1024]{1,0:T(8,128)(2,1)S(1)}, bf16[128,1024]{1,0:T(8,128)(2,1)S(1)}, u32[]{:S(2)}, u32[]{:S(2)}) collective-permute-start(bf16[128,1024]{1,0:T(8,128)(2,1)S(1)} %collective-permute-done.7.refs_7_), channel_id=1, source_target_pairs={{0,0},{4,8},{8,4},{12,12},{1,1},{5,9},{9,5},{13,13},{2,2},{6,10},{... | collective-permute-start | bytes 786440 | tf_op jit(solution)/shard_map/ppermute | solution.py:385
  72.3 8.9 %collective-permute-start.20 = (bf16[128,1024]{1,0:T(8,128)(2,1)S(1)}, bf16[128,1024]{1,0:T(8,128)(2,1)S(1)}, u32[]{:S(2)}, u32[]{:S(2)}) collective-permute-start(bf16[128,1024]{1,0:T(8,128)(2,1)S(1)} %collective-permute-done.19.refs_10_), channel_id=1, source_target_pairs={{0,4},{4,0},{8,12},{12,8},{1,5},{5,1},{9,13},{13,9},{2,6},{6,2},{1... | collective-permute-start | bytes 786440 | tf_op jit(solution)/shard_map/ppermute | solution.py:385
  74.2 7.4 %collective-permute-start.18 = (bf16[128,1024]{1,0:T(8,128)(2,1)S(1)}, bf16[128,1024]{1,0:T(8,128)(2,1)S(1)}, u32[]{:S(2)}, u32[]{:S(2)}) collective-permute-start(bf16[128,1024]{1,0:T(8,128)(2,1)S(1)} %collective-permute-done.6.refs_4_), channel_id=1, source_target_pairs={{0,4},{4,0},{8,12},{12,8},{1,5},{5,1},{9,13},{13,9},{2,6},{6,2},{1... | collective-permute-start | bytes 786440 | tf_op jit(solution)/shard_map/ppermute | solution.py:385
  79.7 1.5 %collective-permute-start.17 = (f32[128,128]{1,0:T(8,128)}, f32[128,128]{1,0:T(8,128)S(1)}, u32[]{:S(2)}, u32[]{:S(2)}) collective-permute-start(f32[128,128]{1,0:T(8,128)} %get-tuple-element.93), channel_id=1, source_target_pairs={{0,1},{1,0},{2,3},{3,2},{4,5},{5,4},{6,7},{7,6},{8,9},{9,8},{10,11... | collective-permute-start | bytes 196616 | tf_op jit(solution)/shard_map/ppermute | solution.py:21
  83.5 14.2 %all-to-all-start = ((bf16[8,160,128]{2,1,0:T(8,128)(2,1)}), bf16[8,160,128]{2,1,0:T(8,128)(2,1)S(1)}, u32[]{:S(2)}, u32[]{:S(2)}) async-start(bf16[8,160,128]{2,1,0:T(8,128)(2,1)} %shard_map.111), calls=%async_computation | async-start | bytes 655360 | tf_op jit(solution)/shard_map/all_to_all | solution.py:571
  87.9 9.9 %collective-permute-start.21 = (bf16[160,128]{1,0:T(8,128)(2,1)S(1)}, bf16[160,128]{1,0:T(8,128)(2,1)S(1)}, u32[]{:S(2)}, u32[]{:S(2)}) collective-permute-start(bf16[160,128]{1,0:T(8,128)(2,1)S(1)} %slice_bitcast_fusion.mine_ref), channel_id=1, source_target_pairs={{0,1},{1,0},{2,3},{3,2},{4,5},{5,4},{6,7},{7,6},{8,9},{9,8},{10,11... | collective-permute-start | bytes 122888 | tf_op jit(solution)/shard_map/ppermute | solution.py:21
  97.8 3.5 %collective-permute-start.22 = (bf16[8,160,128]{2,1,0:T(8,128)(2,1)S(1)}, bf16[8,160,128]{2,1,0:T(8,128)(2,1)S(1)}, u32[]{:S(2)}, u32[]{:S(2)}) collective-permute-start(bf16[8,160,128]{2,1,0:T(8,128)(2,1)S(1)} %all-to-all-done.refs_12_), channel_id=1, source_target_pairs={{0,1},{1,0},{2,3},{3,2},{4,5},{5,4},{6,7},{7,6},{8,9},{9,8},{10,11... | collective-permute-start | bytes 983048 | tf_op jit(solution)/shard_map/ppermute | solution.py:21
  (30 other events, 231.9 us)

commit v8 on v7

--- a/solution.py
+++ b/solution.py
@@ -13,7 +13,7 @@
 F32 = jnp.float32
 TOP = lax.Precision.HIGHEST
 PER_US = 1.15e9
-LIMIT = 56 * 1024 * 1024
+LIMIT = 16 * 1024 * 1024
 
 
 def cyclic(a, axis, by):
@@ -49,16 +49,16 @@
 ANY = pl.BlockSpec(memory_space=pl.ANY)
 
 
-def call(kernel, out_shape, span_us, *args, scratch=(), specs=None, out_specs=None):
+def call(kernel, out_shape, span_us, *args, scratch=(), specs=None, limit=LIMIT):
     size = sum(a.size * a.dtype.itemsize for a in args)
     return pl.pallas_call(
         kernel,
         out_shape=out_shape,
         grid=(1,),
         in_specs=specs or [VMEM] * len(args),
-        out_specs=out_specs or jax.tree.map(lambda _: VMEM, out_shape),
+        out_specs=jax.tree.map(lambda _: VMEM, out_shape),
         scratch_shapes=list(scratch),
-        compiler_params=pltpu.CompilerParams(vmem_limit_bytes=LIMIT),
+        compiler_params=pltpu.CompilerParams(vmem_limit_bytes=limit),
         cost_estimate=pl.CostEstimate(
             flops=int(span_us * PER_US), bytes_accessed=size, transcendentals=0
         ),
@@ -468,13 +468,11 @@
     for r in range(1, n_dp):
         item = after(items[r], partials[0])
         partials.append(cyclic(project(item, w_bc, w_dt), "dp", -r))
+    if n_dp > 1:
+        near += relay(found[1], groups[1], slots[: 1 if ride else 2])
     partials[1:] = [after(a, *near) for a in partials[1:]]
     proj = partials + [cyclic(a, "head", 1) for a in partials]
-    x = after(x, *relay(found[0], groups[0], second))
-    early = []
-    if n_dp > 1:
-        early = relay(found[1], groups[1], slots[: 1 if ride else 2])
-        x = after(x, *early)
+    spare = relay(found[0], groups[0], second)
     own, bc, hp, *outs = call(
         functools.partial(state_kernel, 2 * n_dp, size, int(ride)),
         (
@@ -525,9 +523,9 @@
         for r in range(1, n_dp):
             weights.extend(cyclic(after(a, *others), "dp", r) for a in (w_bc, w_dt))
         if not ride or n_dp == 1:
-            return weights[2:], []
+            return weights[2:], spare
         riders.extend(relay(found[1], groups[1], [(1, 1)], *others))
-        return weights[2:], riders[1:]
+        return weights[2:], riders[1:] + spare
 
     def late(*others):
         if n_dp > 1:
@@ -569,7 +567,6 @@
     copies = call(low_kernel, struct((count, rows + heads, rows), BF), 1.2, keep, taken)
     mine = copies[0]
     lows = lax.all_to_all(copies, ("seq", "dp"), 0, 0, tiled=True)
-    swapped = cyclic(lows, "head", 1)
     other = cyclic(mine, "head", 1)
     grads = call(
         functools.partial(token_kernel, n_dp),
@@ -579,6 +576,8 @@
         other,
         *weights,
     )
+    lows = after(lows, grads)
+    swapped = cyclic(lows, "head", 1)
     toks = []
     for f, a in zip(found, groups):
         toks += [a] + [f[step] for step in slots]
@@ -592,6 +591,7 @@
         lows,
         swapped,
         specs=[ANY] * (len(toks) + 2),
+        limit=2 * LIMIT,
         scratch=(
             pltpu.VMEM((n_dp, n_seq * rows, part), BF),
             pltpu.VMEM((n_dp, cols, n_seq * rows), BF),

time: 107 us -> 98.6 us (0.921)
  Pallas kernels: 35.6 us -> 14.4 us
  waiting for transfers between devices: 27.4 us -> 33.6 us
  local copies, waits for them, and re-layouts: 4.44 us -> 9.99 us
  starting transfers between devices: 37.1 us -> 38.4 us
    pallas_call x12, Pallas kernels: 35.6 us -> 14.4 us  [call(): pl.pallas_call(kernel, out_shape=out_shape, grid=(1,), in_specs=specs or...]
    ppermute x9, waiting for transfers between devices: 2.69 us -> 12.3 us  [cyclic(): return lax.ppermute(a, axis, [(i, (i + by) % count) for i in range(count)])]
    all_to_all x1, waiting for transfers between devices: 9.85 us -> 3.25 us  [body(): lows = lax.all_to_all(copies, ('seq', 'dp'), 0, 0, tiled=True)]
    unnamed x60 -> x56, local copies, waits for them, and re-layouts: 3.33 us -> 8.83 us
    ppermute x6, waiting for transfers between devices: 10.1 us -> 14.5 us  [chains(): got[k] = lax.ppermute(value, 'seq', sorted(to.items()))]
    ppermute x6, starting transfers between devices: 14.4 us -> 16.9 us  [chains(): got[k] = lax.ppermute(value, 'seq', sorted(to.items()))]
    ppermute x8, starting transfers between devices: 11.7 us -> 10 us  [relay(): found[kind, hop] = lax.ppermute(source, 'seq', pairs[kind])]
    ppermute x8, waiting for transfers between devices: 4.81 us -> 3.63 us  [relay(): found[kind, hop] = lax.ppermute(source, 'seq', pairs[kind])]
  transfers between devices with their start and end apart: 24 -> 24, of which waited for: 8 -> 13; matrix products, arithmetic and copies ran while one was open for 1% -> 2% of each run, Pallas kernels for 22% -> 11%
where the time goes in v8:
time: 98.6 us; the launch traced here: 98 us
  starting transfers between devices  38.4 us (39%)
  waiting for transfers between devices  33.6 us (34%)
  Pallas kernels  14.4 us (15%)
  local copies, waits for them, and re-layouts  9.99 us (10%)
  between operations  1.03 us (1%)
    ppermute x6, starting transfers between devices, chains(): got[k] = lax.ppermute(value, 'seq', sorted(to.items()))  16.9 us
    ppermute x6, waiting for transfers between devices, chains(): got[k] = lax.ppermute(value, 'seq', sorted(to.items()))  14.5 us
    pallas_call x12, Pallas kernels, call(): pl.pallas_call(kernel, out_shape=out_shape, grid=(1,), in_specs=specs or...  14.4 us
    ppermute x9, waiting for transfers between devices, cyclic(): return lax.ppermute(a, axis, [(i, (i + by) % count) for i in range(count)])  12.3 us
    ppermute x8, starting transfers between devices, relay(): found[kind, hop] = lax.ppermute(source, 'seq', pairs[kind])  10 us
    unnamed x56, local copies, waits for them, and re-layouts  8.83 us
    ppermute x9, starting transfers between devices, cyclic(): return lax.ppermute(a, axis, [(i, (i + by) % count) for i in range(count)])  6.73 us
    all_to_all x1, starting transfers between devices, body(): lows = lax.all_to_all(copies, ('seq', 'dp'), 0, 0, tiled=True)  4.76 us
  transfers between devices with their start and end apart: 24, of which 13 were waited for; matrix products, arithmetic and copies ran while one was open for 2% of the time, Pallas kernels for 11%

profile of v8, /device:TPU:0, one launch (start us, length us, event | category | flops | bytes accessed | tf_op | source)
XLA Modules:
  0.0 98.0 jit_solution(10709486011955793684)
XLA Ops:
  1.7 3.0 %collective-permute-start = (bf16[128,1024]{1,0:T(8,128)(2,1)S(1)}, bf16[128,1024]{1,0:T(8,128)(2,1)S(1)}, u32[]{:S(2)}, u32[]{:S(2)}) collective-permute-start(bf16[128,1024]{1,0:T(8,128)(2,1)S(1)} %get-tuple-element.52), channel_id=1, source_target_pairs={{0,2},{2,0},{1,3},{3,1},{4,6},{6,4},{5,7},{7,5},{8,10},{10,8},{9,1... | collective-permute-start | bytes 786440 | tf_op jit(solution)/shard_map/ppermute | solution.py:21
  4.7 1.6 %collective-permute-start.2 = (bf16[128,1024]{1,0:T(8,128)(2,1)S(1)}, bf16[128,1024]{1,0:T(8,128)(2,1)S(1)}, u32[]{:S(2)}, u32[]{:S(2)}) collective-permute-start(bf16[128,1024]{1,0:T(8,128)(2,1)S(1)} %get-tuple-element.51.a_ref.refs_0_), channel_id=1, source_target_pairs={{0,4},{4,0},{8,12},{12,8},{1,5},{5,1},{9,13},{13,9},{2,6},{6,2},{1... | collective-permute-start | bytes 786440 | tf_op jit(solution)/shard_map/ppermute | solution.py:385
  7.3 3.7 %collective-permute-done.a_ref.refs_6_ = bf16[128,1024]{1,0:T(8,128)(2,1)S(1)} collective-permute-done((bf16[128,1024]{1,0:T(8,128)(2,1)S(1)}, bf16[128,1024]{1,0:T(8,128)(2,1)S(1)}, u32[]{:S(2)}, u32[]{:S(2)}) %collective-permute-start) | collective-permute-done | bytes 262176 | tf_op jit(solution)/shard_map/ppermute | solution.py:21
  11.0 1.8 %collective-permute-start.4 = (bf16[128,1024]{1,0:T(8,128)(2,1)S(1)}, bf16[128,1024]{1,0:T(8,128)(2,1)S(1)}, u32[]{:S(2)}, u32[]{:S(2)}) collective-permute-start(bf16[128,1024]{1,0:T(8,128)(2,1)S(1)} %collective-permute-done.a_ref.refs_6_), channel_id=1, source_target_pairs={{0,4},{4,0},{8,12},{12,8},{1,5},{5,1},{9,13},{13,9},{2,6},{6,2},{1... | collective-permute-start | bytes 786440 | tf_op jit(solution)/shard_map/ppermute | solution.py:385
  13.2 1.6 %collective-permute-start.1 = (f32[320,128]{1,0:T(8,128)S(1)}, f32[320,128]{1,0:T(8,128)S(1)}, u32[]{:S(2)}, u32[]{:S(2)}) collective-permute-start(f32[320,128]{1,0:T(8,128)S(1)} %shard_map.104), channel_id=1, source_target_pairs={{0,2},{2,0},{1,3},{3,1},{4,6},{6,4},{5,7},{7,5},{8,10},{10,8},{9,1... | collective-permute-start | bytes 491528 | tf_op jit(solution)/shard_map/ppermute | solution.py:21
  14.7 3.8 %collective-permute-done.1.refs_1_ = f32[320,128]{1,0:T(8,128)S(1)} collective-permute-done((f32[320,128]{1,0:T(8,128)S(1)}, f32[320,128]{1,0:T(8,128)S(1)}, u32[]{:S(2)}, u32[]{:S(2)}) %collective-permute-start.1) | collective-permute-done | bytes 163872 | tf_op jit(solution)/shard_map/ppermute | solution.py:21
  20.7 2.1 %shard_map.105 = (f32[2,2,128,1024]{3,2,1,0:T(8,128)S(1)}, f32[256,128]{1,0:T(8,128)S(1)}, f32[160,128]{1,0:T(8,128)S(1)}, bf16[128,1024]{1,0:T(8,128)(2,1)S(1)}...) custom-call(f32[320,128]{1,0:T(8,128)S(1)} %shard_map.103.refs_0_, ...), custom_call_target="tpu_custom_call" | custom-call | flops 1150000000 | bytes 1966336 | tf_op jit(solution)/shard_map/pallas_call | solution.py:54
  22.9 3.8 %collective-permute-start.7 = (bf16[128,1024]{1,0:T(8,128)(2,1)S(1)}, bf16[128,1024]{1,0:T(8,128)(2,1)S(1)}, u32[]{:S(2)}, u32[]{:S(2)}) collective-permute-start(bf16[128,1024]{1,0:T(8,128)(2,1)S(1)} %get-tuple-element.55), channel_id=1, source_target_pairs={{0,4},{4,0},{8,12},{12,8},{1,5},{5,1},{9,13},{13,9},{2,6},{6,2},{1... | collective-permute-start | bytes 786440 | tf_op jit(solution)/shard_map/ppermute | solution.py:412
  27.3 1.6 %collective-permute-start.15 = (bf16[64,1024]{1,0:T(8,128)(2,1)S(1)}, bf16[64,1024]{1,0:T(8,128)(2,1)S(1)}, u32[]{:S(2)}, u32[]{:S(2)}) collective-permute-start(bf16[64,1024]{1,0:T(8,128)(2,1)S(1)} %bitcast.60), channel_id=1, source_target_pairs={{0,2},{2,0},{1,3},{3,1},{4,6},{6,4},{5,7},{7,5},{8,10},{10,8},{9,1... | collective-permute-start | bytes 393224 | tf_op jit(solution)/shard_map/ppermute | solution.py:21
  30.5 2.8 %collective-permute-done.7.refs_3_ = bf16[128,1024]{1,0:T(8,128)(2,1)S(1)} collective-permute-done((bf16[128,1024]{1,0:T(8,128)(2,1)S(1)}, bf16[128,1024]{1,0:T(8,128)(2,1)S(1)}, u32[]{:S(2)}, u32[]{:S(2)}) %collective-permute-start.7) | collective-permute-done | bytes 262176 | tf_op jit(solution)/shard_map/ppermute | solution.py:412
  34.2 6.6 %collective-permute-start.10 = (bf16[128,1024]{1,0:T(8,128)(2,1)S(1)}, bf16[128,1024]{1,0:T(8,128)(2,1)S(1)}, u32[]{:S(2)}, u32[]{:S(2)}) collective-permute-start(bf16[128,1024]{1,0:T(8,128)(2,1)S(1)} %broadcast_select_fusion), channel_id=1, source_target_pairs={{0,4},{4,0},{8,12},{12,8},{1,5},{5,1},{9,13},{13,9},{2,6},{6,2},{1... | collective-permute-start | bytes 786440 | tf_op jit(solution)/shard_map/ppermute | solution.py:412
  41.9 4.8 %collective-permute-done.10.refs_9_ = bf16[128,1024]{1,0:T(8,128)(2,1)S(1)} collective-permute-done((bf16[128,1024]{1,0:T(8,128)(2,1)S(1)}, bf16[128,1024]{1,0:T(8,128)(2,1)S(1)}, u32[]{:S(2)}, u32[]{:S(2)}) %collective-permute-start.10) | collective-permute-done | bytes 262176 | tf_op jit(solution)/shard_map/ppermute | solution.py:412
  47.7 3.3 %collective-permute-start.13 = (bf16[128,1024]{1,0:T(8,128)(2,1)S(1)}, bf16[128,1024]{1,0:T(8,128)(2,1)S(1)}, u32[]{:S(2)}, u32[]{:S(2)}) collective-permute-start(bf16[128,1024]{1,0:T(8,128)(2,1)S(1)} %get-tuple-element.98), channel_id=1, source_target_pairs={{0,4},{4,0},{8,12},{12,8},{1,5},{5,1},{9,13},{13,9},{2,6},{6,2},{1... | collective-permute-start | bytes 786440 | tf_op jit(solution)/shard_map/ppermute | solution.py:412
  52.1 3.9 %collective-permute-done.13 = bf16[128,1024]{1,0:T(8,128)(2,1)S(1)} collective-permute-done((bf16[128,1024]{1,0:T(8,128)(2,1)S(1)}, bf16[128,1024]{1,0:T(8,128)(2,1)S(1)}, u32[]{:S(2)}, u32[]{:S(2)}) %collective-permute-start.13) | collective-permute-done | bytes 262176 | tf_op jit(solution)/shard_map/ppermute | solution.py:412
  56.0 1.8 %collective-permute-start.16 = (bf16[128,1024]{1,0:T(8,128)(2,1)S(1)}, bf16[128,1024]{1,0:T(8,128)(2,1)S(1)}, u32[]{:S(2)}, u32[]{:S(2)}) collective-permute-start(bf16[128,1024]{1,0:T(8,128)(2,1)S(1)} %fusion), channel_id=1, source_target_pairs={{0,4},{4,0},{8,12},{12,8},{1,5},{5,1},{9,13},{13,9},{2,6},{6,2},{1... | collective-permute-start | bytes 786440 | tf_op jit(solution)/shard_map/ppermute | solution.py:412
  59.5 3.0 %collective-permute-done.16 = bf16[128,1024]{1,0:T(8,128)(2,1)S(1)} collective-permute-done((bf16[128,1024]{1,0:T(8,128)(2,1)S(1)}, bf16[128,1024]{1,0:T(8,128)(2,1)S(1)}, u32[]{:S(2)}, u32[]{:S(2)}) %collective-permute-start.16) | collective-permute-done | bytes 262176 | tf_op jit(solution)/shard_map/ppermute | solution.py:412
  62.5 3.9 %collective-permute-start.20 = (bf16[128,1024]{1,0:T(8,128)(2,1)S(1)}, bf16[128,1024]{1,0:T(8,128)(2,1)S(1)}, u32[]{:S(2)}, u32[]{:S(2)}) collective-permute-start(bf16[128,1024]{1,0:T(8,128)(2,1)S(1)} %collective-permute-done.19.refs_10_), channel_id=1, source_target_pairs={{0,4},{4,0},{8,12},{12,8},{1,5},{5,1},{9,13},{13,9},{2,6},{6,2},{1... | collective-permute-start | bytes 786440 | tf_op jit(solution)/shard_map/ppermute | solution.py:385
  66.5 3.1 %shard_map.110 = (bf16[128,2048]{1,0:T(8,128)(2,1)}, f32[160,128]{1,0:T(8,128)S(1)}, f32[128,128]{1,0:T(8,128)S(1)}) custom-call(bf16[2,3,128,1024]{3,2,1,0:T(8,128)(2,1)S(1)} %bitcast_dynamic-update-slice_fusion.refs_0_, bf16[128,2048]{1,0:T(8,128)(2,1)S(1)} %bitcast.51, bf16[128,2048]{1,0:T(8,128)(2,1)S(1)} %bitcast.57, ...), custom_call_target="tpu_custom_call" | custom-call | flops 6209999872 | bytes 4178048 | tf_op jit(solution)/shard_map/pallas_call | solution.py:54
  73.0 2.1 %collective-permute-done.18.refs_5_ = bf16[128,1024]{1,0:T(8,128)(2,1)S(1)} collective-permute-done((bf16[128,1024]{1,0:T(8,128)(2,1)S(1)}, bf16[128,1024]{1,0:T(8,128)(2,1)S(1)}, u32[]{:S(2)}, u32[]{:S(2)}) %collective-permute-start.18) | collective-permute-done | bytes 262176 | tf_op jit(solution)/shard_map/ppermute | solution.py:385
  76.6 4.8 %all-to-all-start = ((bf16[8,160,128]{2,1,0:T(8,128)(2,1)}), bf16[8,160,128]{2,1,0:T(8,128)(2,1)S(1)}, u32[]{:S(2)}, u32[]{:S(2)}) async-start(bf16[8,160,128]{2,1,0:T(8,128)(2,1)} %shard_map.111), calls=%async_computation | async-start | bytes 655360 | tf_op jit(solution)/shard_map/all_to_all | solution.py:569
  85.2 1.5 %shard_map.112 = bf16[128,2048]{1,0:T(8,128)(2,1)} custom-call(bf16[160,128]{1,0:T(8,128)(2,1)S(1)} %slice_bitcast_fusion.mine_ref, bf16[160,128]{1,0:T(8,128)(2,1)S(1)} %collective-permute-done.21.other_ref, bf16[1024,256]{1,0:T(8,128)(2,1)S(1)} %copy-done.3, bf16[64,1024]{1,0:T(8,128)(2,1)S(1)} %bitcast.61, ...), custom_call_target="tpu_custom_call" | custom-call | flops 3335000064 | bytes 1392640 | tf_op jit(solution)/shard_map/pallas_call | solution.py:54
  86.8 3.2 %all-to-all-done.refs_12_ = bf16[8,160,128]{2,1,0:T(8,128)(2,1)S(1)} async-done(((bf16[8,160,128]{2,1,0:T(8,128)(2,1)}), bf16[8,160,128]{2,1,0:T(8,128)(2,1)S(1)}, u32[]{:S(2)}, u32[]{:S(2)}) %all-to-all-start) | async-done | bytes 327712 | tf_op jit(solution)/shard_map/all_to_all | solution.py:569
  90.0 1.6 %collective-permute-done.22.refs_13_ = bf16[8,160,128]{2,1,0:T(8,128)(2,1)S(1)} collective-permute-done((bf16[8,160,128]{2,1,0:T(8,128)(2,1)S(1)}, bf16[8,160,128]{2,1,0:T(8,128)(2,1)S(1)}, u32[]{:S(2)}, u32[]{:S(2)}) %collective-permute-start.22) | collective-permute-done | bytes 327712 | tf_op jit(solution)/shard_map/ppermute | solution.py:21
  95.5 2.5 %shard_map.113 = (f32[1024,256]{1,0:T(8,128)}, f32[64,1024]{1,0:T(8,128)}) custom-call(bf16[128,1024]{1,0:T(8,128)(2,1)S(1)} %get-tuple-element.51.a_ref.refs_0_, bf16[128,1024]{1,0:T(8,128)(2,1)S(1)} %copy-done.7, bf16[128,1024]{1,0:T(8,128)(2,1)S(1)} %copy-done.9, bf16[128,1024]{1,0:T(8,128)(2,1)S(1)} %collective-permute-done.7.refs_3_, ...), custom_call_target="tpu_custom_call" | custom-call | flops 4600000000 | bytes 3801088 | tf_op jit(solution)/shard_map/pallas_call | solution.py:54
  (104 shorter events, 25.1 us)
Async XLA Ops:
  1.7 9.3 %collective-permute-start = (bf16[128,1024]{1,0:T(8,128)(2,1)S(1)}, bf16[128,1024]{1,0:T(8,128)(2,1)S(1)}, u32[]{:S(2)}, u32[]{:S(2)}) collective-permute-start(bf16[128,1024]{1,0:T(8,128)(2,1)S(1)} %get-tuple-element.52), channel_id=1, source_target_pairs={{0,2},{2,0},{1,3},{3,1},{4,6},{6,4},{5,7},{7,5},{8,10},{10,8},{9,1... | collective-permute-start | bytes 786440 | tf_op jit(solution)/shard_map/ppermute | solution.py:21
  4.7 10.0 %collective-permute-start.2 = (bf16[128,1024]{1,0:T(8,128)(2,1)S(1)}, bf16[128,1024]{1,0:T(8,128)(2,1)S(1)}, u32[]{:S(2)}, u32[]{:S(2)}) collective-permute-start(bf16[128,1024]{1,0:T(8,128)(2,1)S(1)} %get-tuple-element.51.a_ref.refs_0_), channel_id=1, source_target_pairs={{0,4},{4,0},{8,12},{12,8},{1,5},{5,1},{9,13},{13,9},{2,6},{6,2},{1... | collective-permute-start | bytes 786440 | tf_op jit(solution)/shard_map/ppermute | solution.py:385
  6.3 8.4 %collective-permute-start.3 = (bf16[128,1024]{1,0:T(8,128)(2,1)S(1)}, bf16[128,1024]{1,0:T(8,128)(2,1)S(1)}, u32[]{:S(2)}, u32[]{:S(2)}) collective-permute-start(bf16[128,1024]{1,0:T(8,128)(2,1)S(1)} %get-tuple-element.51.a_ref.refs_0_), channel_id=1, source_target_pairs={{0,0},{4,8},{8,4},{12,12},{1,1},{5,9},{9,5},{13,13},{2,2},{6,10},{... | collective-permute-start | bytes 786440 | tf_op jit(solution)/shard_map/ppermute | solution.py:385
  11.0 7.5 %collective-permute-start.4 = (bf16[128,1024]{1,0:T(8,128)(2,1)S(1)}, bf16[128,1024]{1,0:T(8,128)(2,1)S(1)}, u32[]{:S(2)}, u32[]{:S(2)}) collective-permute-start(bf16[128,1024]{1,0:T(8,128)(2,1)S(1)} %collective-permute-done.a_ref.refs_6_), channel_id=1, source_target_pairs={{0,4},{4,0},{8,12},{12,8},{1,5},{5,1},{9,13},{13,9},{2,6},{6,2},{1... | collective-permute-start | bytes 786440 | tf_op jit(solution)/shard_map/ppermute | solution.py:385
  13.2 5.4 %collective-permute-start.1 = (f32[320,128]{1,0:T(8,128)S(1)}, f32[320,128]{1,0:T(8,128)S(1)}, u32[]{:S(2)}, u32[]{:S(2)}) collective-permute-start(f32[320,128]{1,0:T(8,128)S(1)} %shard_map.104), channel_id=1, source_target_pairs={{0,2},{2,0},{1,3},{3,1},{4,6},{6,4},{5,7},{7,5},{8,10},{10,8},{9,1... | collective-permute-start | bytes 491528 | tf_op jit(solution)/shard_map/ppermute | solution.py:21
  14.7 5.2 %collective-permute-start.5 = (f32[320,128]{1,0:T(8,128)S(1)}, f32[320,128]{1,0:T(8,128)S(1)}, u32[]{:S(2)}, u32[]{:S(2)}) collective-permute-start(f32[320,128]{1,0:T(8,128)S(1)} %shard_map.103.refs_0_), channel_id=1, source_target_pairs={{0,1},{1,0},{2,3},{3,2},{4,5},{5,4},{6,7},{7,6},{8,9},{9,8},{10,11... | collective-permute-start | bytes 491528 | tf_op jit(solution)/shard_map/ppermute | solution.py:21
  19.3 1.4 %collective-permute-start.6 = (f32[320,128]{1,0:T(8,128)S(1)}, f32[320,128]{1,0:T(8,128)S(1)}, u32[]{:S(2)}, u32[]{:S(2)}) collective-permute-start(f32[320,128]{1,0:T(8,128)S(1)} %collective-permute-done.1.refs_1_), channel_id=1, source_target_pairs={{0,1},{1,0},{2,3},{3,2},{4,5},{5,4},{6,7},{7,6},{8,9},{9,8},{10,11... | collective-permute-start | bytes 491528 | tf_op jit(solution)/shard_map/ppermute | solution.py:21
  19.3 11.2 %collective-permute-start.9 = (bf16[128,1024]{1,0:T(8,128)(2,1)S(1)}, bf16[128,1024]{1,0:T(8,128)(2,1)S(1)}, u32[]{:S(2)}, u32[]{:S(2)}) collective-permute-start(bf16[128,1024]{1,0:T(8,128)(2,1)S(1)} %collective-permute-done.2.refs_1_), channel_id=1, source_target_pairs={{0,0},{4,8},{8,4},{12,12},{1,1},{5,9},{9,5},{13,13},{2,2},{6,10},{... | collective-permute-start | bytes 786440 | tf_op jit(solution)/shard_map/ppermute | solution.py:385
  22.9 10.5 %collective-permute-start.7 = (bf16[128,1024]{1,0:T(8,128)(2,1)S(1)}, bf16[128,1024]{1,0:T(8,128)(2,1)S(1)}, u32[]{:S(2)}, u32[]{:S(2)}) collective-permute-start(bf16[128,1024]{1,0:T(8,128)(2,1)S(1)} %get-tuple-element.55), channel_id=1, source_target_pairs={{0,4},{4,0},{8,12},{12,8},{1,5},{5,1},{9,13},{13,9},{2,6},{6,2},{1... | collective-permute-start | bytes 786440 | tf_op jit(solution)/shard_map/ppermute | solution.py:412
  26.7 3.9 %collective-permute-start.8 = (bf16[128,1024]{1,0:T(8,128)(2,1)S(1)}, bf16[128,1024]{1,0:T(8,128)(2,1)S(1)}, u32[]{:S(2)}, u32[]{:S(2)}) collective-permute-start(bf16[128,1024]{1,0:T(8,128)(2,1)S(1)} %collective-permute-done.a_ref.refs_6_), channel_id=1, source_target_pairs={{0,0},{4,8},{8,4},{12,12},{1,1},{5,9},{9,5},{13,13},{2,2},{6,10},{... | collective-permute-start | bytes 786440 | tf_op jit(solution)/shard_map/ppermute | solution.py:385
  27.3 24.7 %collective-permute-start.15 = (bf16[64,1024]{1,0:T(8,128)(2,1)S(1)}, bf16[64,1024]{1,0:T(8,128)(2,1)S(1)}, u32[]{:S(2)}, u32[]{:S(2)}) collective-permute-start(bf16[64,1024]{1,0:T(8,128)(2,1)S(1)} %bitcast.60), channel_id=1, source_target_pairs={{0,2},{2,0},{1,3},{3,1},{4,6},{6,4},{5,7},{7,5},{8,10},{10,8},{9,1... | collective-permute-start | bytes 393224 | tf_op jit(solution)/shard_map/ppermute | solution.py:21
  28.9 23.1 %collective-permute-start.14 = (bf16[1024,256]{1,0:T(8,128)(2,1)S(1)}, bf16[1024,256]{1,0:T(8,128)(2,1)S(1)}, u32[]{:S(2)}, u32[]{:S(2)}) collective-permute-start(bf16[1024,256]{1,0:T(8,128)(2,1)S(1)} %copy-done.3), channel_id=1, source_target_pairs={{0,2},{2,0},{1,3},{3,1},{4,6},{6,4},{5,7},{7,5},{8,10},{10,8},{9,1... | collective-permute-start | bytes 1572872 | tf_op jit(solution)/shard_map/ppermute | solution.py:21
  33.5 8.4 %collective-permute-start.11 = (bf16[128,1024]{1,0:T(8,128)(2,1)S(1)}, bf16[128,1024]{1,0:T(8,128)(2,1)S(1)}, u32[]{:S(2)}, u32[]{:S(2)}) collective-permute-start(bf16[128,1024]{1,0:T(8,128)(2,1)S(1)} %fusion.3), channel_id=1, source_target_pairs={{0,0},{4,8},{8,4},{12,12},{1,1},{5,9},{9,5},{13,13},{2,2},{6,10},{... | collective-permute-start | bytes 786440 | tf_op jit(solution)/shard_map/ppermute | solution.py:412
  34.2 12.5 %collective-permute-start.10 = (bf16[128,1024]{1,0:T(8,128)(2,1)S(1)}, bf16[128,1024]{1,0:T(8,128)(2,1)S(1)}, u32[]{:S(2)}, u32[]{:S(2)}) collective-permute-start(bf16[128,1024]{1,0:T(8,128)(2,1)S(1)} %broadcast_select_fusion), channel_id=1, source_target_pairs={{0,4},{4,0},{8,12},{12,8},{1,5},{5,1},{9,13},{13,9},{2,6},{6,2},{1... | collective-permute-start | bytes 786440 | tf_op jit(solution)/shard_map/ppermute | solution.py:412
  47.0 5.0 %collective-permute-start.12 = (bf16[128,1024]{1,0:T(8,128)(2,1)S(1)}, bf16[128,1024]{1,0:T(8,128)(2,1)S(1)}, u32[]{:S(2)}, u32[]{:S(2)}) collective-permute-start(bf16[128,1024]{1,0:T(8,128)(2,1)S(1)} %get-tuple-element.99), channel_id=1, source_target_pairs={{0,0},{4,8},{8,4},{12,12},{1,1},{5,9},{9,5},{13,13},{2,2},{6,10},{... | collective-permute-start | bytes 786440 | tf_op jit(solution)/shard_map/ppermute | solution.py:412
  47.7 8.2 %collective-permute-start.13 = (bf16[128,1024]{1,0:T(8,128)(2,1)S(1)}, bf16[128,1024]{1,0:T(8,128)(2,1)S(1)}, u32[]{:S(2)}, u32[]{:S(2)}) collective-permute-start(bf16[128,1024]{1,0:T(8,128)(2,1)S(1)} %get-tuple-element.98), channel_id=1, source_target_pairs={{0,4},{4,0},{8,12},{12,8},{1,5},{5,1},{9,13},{13,9},{2,6},{6,2},{1... | collective-permute-start | bytes 786440 | tf_op jit(solution)/shard_map/ppermute | solution.py:412
  56.0 6.4 %collective-permute-start.16 = (bf16[128,1024]{1,0:T(8,128)(2,1)S(1)}, bf16[128,1024]{1,0:T(8,128)(2,1)S(1)}, u32[]{:S(2)}, u32[]{:S(2)}) collective-permute-start(bf16[128,1024]{1,0:T(8,128)(2,1)S(1)} %fusion), channel_id=1, source_target_pairs={{0,4},{4,0},{8,12},{12,8},{1,5},{5,1},{9,13},{13,9},{2,6},{6,2},{1... | collective-permute-start | bytes 786440 | tf_op jit(solution)/shard_map/ppermute | solution.py:412
  57.9 4.7 %collective-permute-start.19 = (bf16[128,1024]{1,0:T(8,128)(2,1)S(1)}, bf16[128,1024]{1,0:T(8,128)(2,1)S(1)}, u32[]{:S(2)}, u32[]{:S(2)}) collective-permute-start(bf16[128,1024]{1,0:T(8,128)(2,1)S(1)} %copy-done.11), channel_id=1, source_target_pairs={{0,0},{4,8},{8,4},{12,12},{1,1},{5,9},{9,5},{13,13},{2,2},{6,10},{... | collective-permute-start | bytes 786440 | tf_op jit(solution)/shard_map/ppermute | solution.py:385
  62.5 9.8 %collective-permute-start.20 = (bf16[128,1024]{1,0:T(8,128)(2,1)S(1)}, bf16[128,1024]{1,0:T(8,128)(2,1)S(1)}, u32[]{:S(2)}, u32[]{:S(2)}) collective-permute-start(bf16[128,1024]{1,0:T(8,128)(2,1)S(1)} %collective-permute-done.19.refs_10_), channel_id=1, source_target_pairs={{0,4},{4,0},{8,12},{12,8},{1,5},{5,1},{9,13},{13,9},{2,6},{6,2},{1... | collective-permute-start | bytes 786440 | tf_op jit(solution)/shard_map/ppermute | solution.py:385
  66.4 8.7 %collective-permute-start.18 = (bf16[128,1024]{1,0:T(8,128)(2,1)S(1)}, bf16[128,1024]{1,0:T(8,128)(2,1)S(1)}, u32[]{:S(2)}, u32[]{:S(2)}) collective-permute-start(bf16[128,1024]{1,0:T(8,128)(2,1)S(1)} %collective-permute-done.9.refs_4_), channel_id=1, source_target_pairs={{0,4},{4,0},{8,12},{12,8},{1,5},{5,1},{9,13},{13,9},{2,6},{6,2},{1... | collective-permute-start | bytes 786440 | tf_op jit(solution)/shard_map/ppermute | solution.py:385
  69.6 1.3 %collective-permute-start.17 = (f32[128,128]{1,0:T(8,128)S(1)}, f32[128,128]{1,0:T(8,128)S(1)}, u32[]{:S(2)}, u32[]{:S(2)}) collective-permute-start(f32[128,128]{1,0:T(8,128)S(1)} %get-tuple-element.90), channel_id=1, source_target_pairs={{0,1},{1,0},{2,3},{3,2},{4,5},{5,4},{6,7},{7,6},{8,9},{9,8},{10,11... | collective-permute-start | bytes 196616 | tf_op jit(solution)/shard_map/ppermute | solution.py:21
  76.6 13.4 %all-to-all-start = ((bf16[8,160,128]{2,1,0:T(8,128)(2,1)}), bf16[8,160,128]{2,1,0:T(8,128)(2,1)S(1)}, u32[]{:S(2)}, u32[]{:S(2)}) async-start(bf16[8,160,128]{2,1,0:T(8,128)(2,1)} %shard_map.111), calls=%async_computation | async-start | bytes 655360 | tf_op jit(solution)/shard_map/all_to_all | solution.py:569
  82.1 1.3 %collective-permute-start.21 = (bf16[160,128]{1,0:T(8,128)(2,1)S(1)}, bf16[160,128]{1,0:T(8,128)(2,1)S(1)}, u32[]{:S(2)}, u32[]{:S(2)}) collective-permute-start(bf16[160,128]{1,0:T(8,128)(2,1)S(1)} %slice_bitcast_fusion.mine_ref), channel_id=1, source_target_pairs={{0,1},{1,0},{2,3},{3,2},{4,5},{5,4},{6,7},{7,6},{8,9},{9,8},{10,11... | collective-permute-start | bytes 122888 | tf_op jit(solution)/shard_map/ppermute | solution.py:21
  90.0 1.6 %collective-permute-start.22 = (bf16[8,160,128]{2,1,0:T(8,128)(2,1)S(1)}, bf16[8,160,128]{2,1,0:T(8,128)(2,1)S(1)}, u32[]{:S(2)}, u32[]{:S(2)}) collective-permute-start(bf16[8,160,128]{2,1,0:T(8,128)(2,1)S(1)} %all-to-all-done.refs_12_), channel_id=1, source_target_pairs={{0,1},{1,0},{2,3},{3,2},{4,5},{5,4},{6,7},{7,6},{8,9},{9,8},{10,11... | collective-permute-start | bytes 983048 | tf_op jit(solution)/shard_map/ppermute | solution.py:21
  (28 other events, 205.7 us)

commit v9 on v8

--- a/solution.py
+++ b/solution.py
@@ -13,7 +13,7 @@
 F32 = jnp.float32
 TOP = lax.Precision.HIGHEST
 PER_US = 1.15e9
-LIMIT = 16 * 1024 * 1024
+LIMIT = 8 * 1024 * 1024
 
 
 def cyclic(a, axis, by):
@@ -109,7 +109,7 @@
     return call(
         project_kernel,
         struct((total, w_bc.shape[1] // 2), F32),
-        2.1,
+        0.3,
         a,
         w_bc,
         w_dt,
@@ -453,7 +453,7 @@
     w_dt = w_dt.T
     rate, bias = decay_rate[None], dt_bias[None]
 
-    pieces = call(split_kernel, [struct((rows, part), BF)] * n_dp, 1.9, feats)
+    pieces = call(split_kernel, [struct((rows, part), BF)] * n_dp, 0.7, feats)
     items = [pieces[0]] + [cyclic(pieces[r], "dp", r) for r in range(1, n_dp)]
     groups = items[:1]
     if n_dp > 1:
@@ -482,7 +482,7 @@
         )
         + (struct((state_n, step), BF),) * CHUNKS
         + (struct((1, step), F32),) * CHUNKS,
-        1.0,
+        0.1,
         *proj,
         x,
         g,
@@ -503,7 +503,7 @@
             functools.partial(inner_kernel, q * pairs, pairs, size),
             ([square] if q == 0 else [])
             + [struct((rows, span), F32), square, struct((2, 2 * pairs, rows), F32)],
-                2.6,
+                0.9,
             held,
             hp,
             x,
@@ -522,16 +522,16 @@
     def beside(*others):
         for r in range(1, n_dp):
             weights.extend(cyclic(after(a, *others), "dp", r) for a in (w_bc, w_dt))
-        if not ride or n_dp == 1:
-            return weights[2:], spare
-        riders.extend(relay(found[1], groups[1], [(1, 1)], *others))
-        return weights[2:], riders[1:] + spare
+        return weights[2:], []
 
     def late(*others):
         if n_dp > 1:
             relay(found[1], groups[1], second, *others)
 
-    riders = [found[0][1, 1]] if ride else []
+    if ride and n_dp > 1:
+        spare += relay(found[1], groups[1], [(1, 1)])
+    first[0] = after(first[0], *spare)
+    riders = [f[1, 1] for f in found] if ride else []
     calls = [functools.partial(inner, q) for q in range(PARTS)]
     store, inners = chains(first, own, decay, calls, beside, riders, late)
     for f, a in zip(found, riders):
@@ -546,7 +546,7 @@
             struct((rows + heads, rows), F32),
             struct((rows, rows), F32),
         ),
-        5.4,
+        3.1,
         store,
         x,
         g,
@@ -564,14 +564,14 @@
     )
     taken = after(cyclic(give, "head", 1), *done)
     count = n_dp * n_seq
-    copies = call(low_kernel, struct((count, rows + heads, rows), BF), 1.2, keep, taken)
+    copies = call(low_kernel, struct((count, rows + heads, rows), BF), 0.7, keep, taken)
     mine = copies[0]
     lows = lax.all_to_all(copies, ("seq", "dp"), 0, 0, tiled=True)
     other = cyclic(mine, "head", 1)
     grads = call(
         functools.partial(token_kernel, n_dp),
         struct((rows, width), BF),
-        2.9,
+        1.5,
         mine,
         other,
         *weights,
@@ -586,12 +586,12 @@
     grad_bc, grad_dt = call(
         functools.partial(weight_kernel, 1.0 / (rows * n_seq * n_dp), n_dp, n_seq, slots),
         (struct((part, 2 * state_n), F32), struct((2 * heads, part), F32)),
-        4.0,
+        2.5,
         *toks,
         lows,
         swapped,
         specs=[ANY] * (len(toks) + 2),
-        limit=2 * LIMIT,
+        limit=LIMIT + 2 * n_dp * n_seq * rows * (part + cols),
         scratch=(
             pltpu.VMEM((n_dp, n_seq * rows, part), BF),
             pltpu.VMEM((n_dp, cols, n_seq * rows), BF),

time: 98.6 us -> 100 us (1.014)
  local copies, waits for them, and re-layouts: 9.99 us -> 15 us
  starting transfers between devices: 38.4 us -> 36.3 us
  waiting for transfers between devices: 33.6 us -> 31.8 us
    unnamed x56 -> x86, local copies, waits for them, and re-layouts: 8.83 us -> 13.9 us
    ppermute x8, starting transfers between devices: 10 us -> 8.27 us  [relay(): found[kind, hop] = lax.ppermute(source, 'seq', pairs[kind])]
    ppermute x8, waiting for transfers between devices: 3.63 us -> 2.03 us  [relay(): found[kind, hop] = lax.ppermute(source, 'seq', pairs[kind])]
  transfers between devices with their start and end apart: 24 -> 24, of which waited for: 13 -> 11; matrix products, arithmetic and copies ran while one was open for 2% -> 2% of each run, Pallas kernels for 11% -> 12%
where the time goes in v9:
time: 100 us; the launch traced here: 99.5 us
  starting transfers between devices  36.3 us (36%)
  waiting for transfers between devices  31.8 us (32%)
  local copies, waits for them, and re-layouts  15 us (15%)
  Pallas kernels  14.8 us (15%)
  between operations  1.08 us (1%)
    ppermute x6, starting transfers between devices, chains(): got[k] = lax.ppermute(value, 'seq', sorted(to.items()))  16.6 us
    pallas_call x12, Pallas kernels, call(): pl.pallas_call(kernel, out_shape=out_shape, grid=(1,), in_specs=specs or...  14.8 us
    unnamed x86, local copies, waits for them, and re-layouts  13.9 us
    ppermute x6, waiting for transfers between devices, chains(): got[k] = lax.ppermute(value, 'seq', sorted(to.items()))  13.7 us
    ppermute x9, waiting for transfers between devices, cyclic(): return lax.ppermute(a, axis, [(i, (i + by) % count) for i in range(count)])  11.9 us
    ppermute x8, starting transfers between devices, relay(): found[kind, hop] = lax.ppermute(source, 'seq', pairs[kind])  8.27 us
    ppermute x9, starting transfers between devices, cyclic(): return lax.ppermute(a, axis, [(i, (i + by) % count) for i in range(count)])  6.74 us
    all_to_all x1, starting transfers between devices, body(): lows = lax.all_to_all(copies, ('seq', 'dp'), 0, 0, tiled=True)  4.64 us
  transfers between devices with their start and end apart: 24, of which 11 were waited for; matrix products, arithmetic and copies ran while one was open for 2% of the time, Pallas kernels for 12%

profile of v9, /device:TPU:0, one launch (start us, length us, event | category | flops | bytes accessed | tf_op | source)
XLA Modules:
  0.0 99.5 jit_solution(6212619585724795272)
XLA Ops:
  1.8 3.0 %collective-permute-start = (bf16[128,1024]{1,0:T(8,128)(2,1)S(1)}, bf16[128,1024]{1,0:T(8,128)(2,1)S(1)}, u32[]{:S(2)}, u32[]{:S(2)}) collective-permute-start(bf16[128,1024]{1,0:T(8,128)(2,1)S(1)} %get-tuple-element.52), channel_id=1, source_target_pairs={{0,2},{2,0},{1,3},{3,1},{4,6},{6,4},{5,7},{7,5},{8,10},{10,8},{9,1... | collective-permute-start | bytes 786440 | tf_op jit(solution)/shard_map/ppermute | solution.py:21
  4.8 1.6 %collective-permute-start.2 = (bf16[128,1024]{1,0:T(8,128)(2,1)S(1)}, bf16[128,1024]{1,0:T(8,128)(2,1)S(1)}, u32[]{:S(2)}, u32[]{:S(2)}) collective-permute-start(bf16[128,1024]{1,0:T(8,128)(2,1)S(1)} %get-tuple-element.51.a_ref.refs_0_), channel_id=1, source_target_pairs={{0,4},{4,0},{8,12},{12,8},{1,5},{5,1},{9,13},{13,9},{2,6},{6,2},{1... | collective-permute-start | bytes 786440 | tf_op jit(solution)/shard_map/ppermute | solution.py:385
  7.0 4.1 %collective-permute-done.a_ref.refs_6_ = bf16[128,1024]{1,0:T(8,128)(2,1)S(1)} collective-permute-done((bf16[128,1024]{1,0:T(8,128)(2,1)S(1)}, bf16[128,1024]{1,0:T(8,128)(2,1)S(1)}, u32[]{:S(2)}, u32[]{:S(2)}) %collective-permute-start) | collective-permute-done | bytes 262176 | tf_op jit(solution)/shard_map/ppermute | solution.py:21
  11.1 1.8 %collective-permute-start.4 = (bf16[128,1024]{1,0:T(8,128)(2,1)S(1)}, bf16[128,1024]{1,0:T(8,128)(2,1)S(1)}, u32[]{:S(2)}, u32[]{:S(2)}) collective-permute-start(bf16[128,1024]{1,0:T(8,128)(2,1)S(1)} %collective-permute-done.a_ref.refs_6_), channel_id=1, source_target_pairs={{0,4},{4,0},{8,12},{12,8},{1,5},{5,1},{9,13},{13,9},{2,6},{6,2},{1... | collective-permute-start | bytes 786440 | tf_op jit(solution)/shard_map/ppermute | solution.py:385
  13.5 1.6 %collective-permute-start.1 = (f32[320,128]{1,0:T(8,128)S(1)}, f32[320,128]{1,0:T(8,128)S(1)}, u32[]{:S(2)}, u32[]{:S(2)}) collective-permute-start(f32[320,128]{1,0:T(8,128)S(1)} %shard_map.104), channel_id=1, source_target_pairs={{0,2},{2,0},{1,3},{3,1},{4,6},{6,4},{5,7},{7,5},{8,10},{10,8},{9,1... | collective-permute-start | bytes 491528 | tf_op jit(solution)/shard_map/ppermute | solution.py:21
  16.5 2.4 %collective-permute-done.1.refs_1_ = f32[320,128]{1,0:T(8,128)S(1)} collective-permute-done((f32[320,128]{1,0:T(8,128)S(1)}, f32[320,128]{1,0:T(8,128)S(1)}, u32[]{:S(2)}, u32[]{:S(2)}) %collective-permute-start.1) | collective-permute-done | bytes 163872 | tf_op jit(solution)/shard_map/ppermute | solution.py:21
  18.9 1.4 %collective-permute-done.6.refs_3_ = f32[320,128]{1,0:T(8,128)S(1)} collective-permute-done((f32[320,128]{1,0:T(8,128)S(1)}, f32[320,128]{1,0:T(8,128)S(1)}, u32[]{:S(2)}, u32[]{:S(2)}) %collective-permute-start.6) | collective-permute-done | bytes 163872 | tf_op jit(solution)/shard_map/ppermute | solution.py:21
  20.3 2.6 %shard_map.105 = (f32[2,2,128,1024]{3,2,1,0:T(8,128)S(1)}, f32[256,128]{1,0:T(8,128)S(1)}, f32[160,128]{1,0:T(8,128)S(1)}, bf16[128,1024]{1,0:T(8,128)(2,1)}, bf...) custom-call(f32[320,128]{1,0:T(8,128)S(1)} %shard_map.103.refs_0_, ...), custom_call_target="tpu_custom_call" | custom-call | flops 115000000 | bytes 1966336 | tf_op jit(solution)/shard_map/pallas_call | solution.py:54
  25.7 5.7 %collective-permute-start.9 = (bf16[128,1024]{1,0:T(8,128)(2,1)}, bf16[128,1024]{1,0:T(8,128)(2,1)S(1)}, u32[]{:S(2)}, u32[]{:S(2)}) collective-permute-start(bf16[128,1024]{1,0:T(8,128)(2,1)} %get-tuple-element.56), channel_id=1, source_target_pairs={{0,4},{4,0},{8,12},{12,8},{1,5},{5,1},{9,13},{13,9},{2,6},{6,2},{1... | collective-permute-start | bytes 786440 | tf_op jit(solution)/shard_map/ppermute | solution.py:412
  31.9 1.5 %collective-permute-start.14 = (bf16[1024,256]{1,0:T(8,128)(2,1)}, bf16[1024,256]{1,0:T(8,128)(2,1)S(1)}, u32[]{:S(2)}, u32[]{:S(2)}) collective-permute-start(bf16[1024,256]{1,0:T(8,128)(2,1)} %refs_0_.1), channel_id=1, source_target_pairs={{0,2},{2,0},{1,3},{3,1},{4,6},{6,4},{5,7},{7,5},{8,10},{10,8},{9,1... | collective-permute-start | bytes 1572872 | tf_op jit(solution)/shard_map/ppermute | solution.py:21
  38.4 3.8 %collective-permute-start.10 = (bf16[128,1024]{1,0:T(8,128)(2,1)S(1)}, bf16[128,1024]{1,0:T(8,128)(2,1)S(1)}, u32[]{:S(2)}, u32[]{:S(2)}) collective-permute-start(bf16[128,1024]{1,0:T(8,128)(2,1)S(1)} %broadcast_select_fusion), channel_id=1, source_target_pairs={{0,4},{4,0},{8,12},{12,8},{1,5},{5,1},{9,13},{13,9},{2,6},{6,2},{1... | collective-permute-start | bytes 786440 | tf_op jit(solution)/shard_map/ppermute | solution.py:412
  43.3 3.2 %collective-permute-done.10.refs_9_ = bf16[128,1024]{1,0:T(8,128)(2,1)S(1)} collective-permute-done((bf16[128,1024]{1,0:T(8,128)(2,1)S(1)}, bf16[128,1024]{1,0:T(8,128)(2,1)S(1)}, u32[]{:S(2)}, u32[]{:S(2)}) %collective-permute-start.10) | collective-permute-done | bytes 262176 | tf_op jit(solution)/shard_map/ppermute | solution.py:412
  47.5 3.3 %collective-permute-start.13 = (bf16[128,1024]{1,0:T(8,128)(2,1)S(1)}, bf16[128,1024]{1,0:T(8,128)(2,1)S(1)}, u32[]{:S(2)}, u32[]{:S(2)}) collective-permute-start(bf16[128,1024]{1,0:T(8,128)(2,1)S(1)} %get-tuple-element.98), channel_id=1, source_target_pairs={{0,4},{4,0},{8,12},{12,8},{1,5},{5,1},{9,13},{13,9},{2,6},{6,2},{1... | collective-permute-start | bytes 786440 | tf_op jit(solution)/shard_map/ppermute | solution.py:412
  51.8 5.0 %collective-permute-done.13 = bf16[128,1024]{1,0:T(8,128)(2,1)S(1)} collective-permute-done((bf16[128,1024]{1,0:T(8,128)(2,1)S(1)}, bf16[128,1024]{1,0:T(8,128)(2,1)S(1)}, u32[]{:S(2)}, u32[]{:S(2)}) %collective-permute-start.13) | collective-permute-done | bytes 262176 | tf_op jit(solution)/shard_map/ppermute | solution.py:412
  56.9 2.4 %collective-permute-start.16 = (bf16[128,1024]{1,0:T(8,128)(2,1)S(1)}, bf16[128,1024]{1,0:T(8,128)(2,1)S(1)}, u32[]{:S(2)}, u32[]{:S(2)}) collective-permute-start(bf16[128,1024]{1,0:T(8,128)(2,1)S(1)} %fusion), channel_id=1, source_target_pairs={{0,4},{4,0},{8,12},{12,8},{1,5},{5,1},{9,13},{13,9},{2,6},{6,2},{1... | collective-permute-start | bytes 786440 | tf_op jit(solution)/shard_map/ppermute | solution.py:412
  61.0 5.5 %collective-permute-done.16 = bf16[128,1024]{1,0:T(8,128)(2,1)S(1)} collective-permute-done((bf16[128,1024]{1,0:T(8,128)(2,1)S(1)}, bf16[128,1024]{1,0:T(8,128)(2,1)S(1)}, u32[]{:S(2)}, u32[]{:S(2)}) %collective-permute-start.16) | collective-permute-done | bytes 262176 | tf_op jit(solution)/shard_map/ppermute | solution.py:412
  66.5 2.1 %collective-permute-start.20 = (bf16[128,1024]{1,0:T(8,128)(2,1)S(1)}, bf16[128,1024]{1,0:T(8,128)(2,1)S(1)}, u32[]{:S(2)}, u32[]{:S(2)}) collective-permute-start(bf16[128,1024]{1,0:T(8,128)(2,1)S(1)} %collective-permute-done.19.refs_10_), channel_id=1, source_target_pairs={{0,4},{4,0},{8,12},{12,8},{1,5},{5,1},{9,13},{13,9},{2,6},{6,2},{1... | collective-permute-start | bytes 786440 | tf_op jit(solution)/shard_map/ppermute | solution.py:385
  68.7 3.1 %shard_map.110 = (bf16[128,2048]{1,0:T(8,128)(2,1)}, f32[160,128]{1,0:T(8,128)S(1)}, f32[128,128]{1,0:T(8,128)S(1)}) custom-call(bf16[2,3,128,1024]{3,2,1,0:T(8,128)(2,1)S(1)} %bitcast_dynamic-update-slice_fusion.refs_0_, bf16[128,2048]{1,0:T(8,128)(2,1)S(1)} %bitcast.46, bf16[128,2048]{1,0:T(8,128)(2,1)S(1)} %bitcast.52, f32[256,128]{1,0:T(8,128)S(1)} %copy-done.37, ...), custom_call_target="tpu_custom_call" | custom-call | flops 3564999936 | bytes 4178048 | tf_op jit(solution)/shard_map/pallas_call | solution.py:54
  73.8 2.0 %collective-permute-done.18.refs_5_ = bf16[128,1024]{1,0:T(8,128)(2,1)S(1)} collective-permute-done((bf16[128,1024]{1,0:T(8,128)(2,1)S(1)}, bf16[128,1024]{1,0:T(8,128)(2,1)S(1)}, u32[]{:S(2)}, u32[]{:S(2)}) %collective-permute-start.18) | collective-permute-done | bytes 262176 | tf_op jit(solution)/shard_map/ppermute | solution.py:385
  77.3 4.6 %all-to-all-start = ((bf16[8,160,128]{2,1,0:T(8,128)(2,1)}), bf16[8,160,128]{2,1,0:T(8,128)(2,1)S(1)}, u32[]{:S(2)}, u32[]{:S(2)}) async-start(bf16[8,160,128]{2,1,0:T(8,128)(2,1)} %shard_map.111), calls=%async_computation | async-start | bytes 655360 | tf_op jit(solution)/shard_map/all_to_all | solution.py:569
  84.9 1.5 %shard_map.112 = bf16[128,2048]{1,0:T(8,128)(2,1)} custom-call(bf16[160,128]{1,0:T(8,128)(2,1)S(1)} %slice_bitcast_fusion.mine_ref, bf16[160,128]{1,0:T(8,128)(2,1)S(1)} %collective-permute-done.21.other_ref, bf16[1024,256]{1,0:T(8,128)(2,1)S(1)} %copy-done.13, bf16[64,1024]{1,0:T(8,128)(2,1)S(1)} %bitcast.64, bf16[1024,256]{1,0:T(8,128)(2,1)S(1)} %copy-done.15, ...), custom_call_target="tpu_custom_call" | custom-call | flops 1724999936 | bytes 1392640 | tf_op jit(solution)/shard_map/pallas_call | solution.py:54
  86.4 4.2 %all-to-all-done.refs_12_ = bf16[8,160,128]{2,1,0:T(8,128)(2,1)S(1)} async-done(((bf16[8,160,128]{2,1,0:T(8,128)(2,1)}), bf16[8,160,128]{2,1,0:T(8,128)(2,1)S(1)}, u32[]{:S(2)}, u32[]{:S(2)}) %all-to-all-start) | async-done | bytes 327712 | tf_op jit(solution)/shard_map/all_to_all | solution.py:569
  90.6 1.6 %collective-permute-done.22.refs_13_ = bf16[8,160,128]{2,1,0:T(8,128)(2,1)S(1)} collective-permute-done((bf16[8,160,128]{2,1,0:T(8,128)(2,1)S(1)}, bf16[8,160,128]{2,1,0:T(8,128)(2,1)S(1)}, u32[]{:S(2)}, u32[]{:S(2)}) %collective-permute-start.22) | collective-permute-done | bytes 327712 | tf_op jit(solution)/shard_map/ppermute | solution.py:21
  97.0 2.5 %shard_map.113 = (f32[1024,256]{1,0:T(8,128)}, f32[64,1024]{1,0:T(8,128)}) custom-call(bf16[128,1024]{1,0:T(8,128)(2,1)S(1)} %copy-done.17, bf16[128,1024]{1,0:T(8,128)(2,1)S(1)} %copy-done.21, bf16[128,1024]{1,0:T(8,128)(2,1)S(1)} %collective-permute-done.3.refs_8_.refs_2_, bf16[128,1024]{1,0:T(8,128)(2,1)S(1)} %collective-permute-done.9.refs_3_, ...), custom_call_target="tpu_custom_call" | custom-call | flops 2875000064 | bytes 3801088 | tf_op jit(solution)/shard_map/pallas_call | solution.py:54
  (134 shorter events, 28.0 us)
Async XLA Ops:
  1.8 9.3 %collective-permute-start = (bf16[128,1024]{1,0:T(8,128)(2,1)S(1)}, bf16[128,1024]{1,0:T(8,128)(2,1)S(1)}, u32[]{:S(2)}, u32[]{:S(2)}) collective-permute-start(bf16[128,1024]{1,0:T(8,128)(2,1)S(1)} %get-tuple-element.52), channel_id=1, source_target_pairs={{0,2},{2,0},{1,3},{3,1},{4,6},{6,4},{5,7},{7,5},{8,10},{10,8},{9,1... | collective-permute-start | bytes 786440 | tf_op jit(solution)/shard_map/ppermute | solution.py:21
  4.8 10.3 %collective-permute-start.2 = (bf16[128,1024]{1,0:T(8,128)(2,1)S(1)}, bf16[128,1024]{1,0:T(8,128)(2,1)S(1)}, u32[]{:S(2)}, u32[]{:S(2)}) collective-permute-start(bf16[128,1024]{1,0:T(8,128)(2,1)S(1)} %get-tuple-element.51.a_ref.refs_0_), channel_id=1, source_target_pairs={{0,4},{4,0},{8,12},{12,8},{1,5},{5,1},{9,13},{13,9},{2,6},{6,2},{1... | collective-permute-start | bytes 786440 | tf_op jit(solution)/shard_map/ppermute | solution.py:385
  6.4 10.1 %collective-permute-start.3 = (bf16[128,1024]{1,0:T(8,128)(2,1)S(1)}, bf16[128,1024]{1,0:T(8,128)(2,1)S(1)}, u32[]{:S(2)}, u32[]{:S(2)}) collective-permute-start(bf16[128,1024]{1,0:T(8,128)(2,1)S(1)} %get-tuple-element.51.a_ref.refs_0_), channel_id=1, source_target_pairs={{0,0},{4,8},{8,4},{12,12},{1,1},{5,9},{9,5},{13,13},{2,2},{6,10},{... | collective-permute-start | bytes 786440 | tf_op jit(solution)/shard_map/ppermute | solution.py:385
  11.1 7.8 %collective-permute-start.4 = (bf16[128,1024]{1,0:T(8,128)(2,1)S(1)}, bf16[128,1024]{1,0:T(8,128)(2,1)S(1)}, u32[]{:S(2)}, u32[]{:S(2)}) collective-permute-start(bf16[128,1024]{1,0:T(8,128)(2,1)S(1)} %collective-permute-done.a_ref.refs_6_), channel_id=1, source_target_pairs={{0,4},{4,0},{8,12},{12,8},{1,5},{5,1},{9,13},{13,9},{2,6},{6,2},{1... | collective-permute-start | bytes 786440 | tf_op jit(solution)/shard_map/ppermute | solution.py:385
  13.5 5.4 %collective-permute-start.1 = (f32[320,128]{1,0:T(8,128)S(1)}, f32[320,128]{1,0:T(8,128)S(1)}, u32[]{:S(2)}, u32[]{:S(2)}) collective-permute-start(f32[320,128]{1,0:T(8,128)S(1)} %shard_map.104), channel_id=1, source_target_pairs={{0,2},{2,0},{1,3},{3,1},{4,6},{6,4},{5,7},{7,5},{8,10},{10,8},{9,1... | collective-permute-start | bytes 491528 | tf_op jit(solution)/shard_map/ppermute | solution.py:21
  15.1 9.8 %collective-permute-start.7 = (bf16[128,1024]{1,0:T(8,128)(2,1)S(1)}, bf16[128,1024]{1,0:T(8,128)(2,1)S(1)}, u32[]{:S(2)}, u32[]{:S(2)}) collective-permute-start(bf16[128,1024]{1,0:T(8,128)(2,1)S(1)} %collective-permute-done.2.refs_1_), channel_id=1, source_target_pairs={{0,0},{4,8},{8,4},{12,12},{1,1},{5,9},{9,5},{13,13},{2,2},{6,10},{... | collective-permute-start | bytes 786440 | tf_op jit(solution)/shard_map/ppermute | solution.py:385
  15.8 9.2 %collective-permute-start.8 = (bf16[128,1024]{1,0:T(8,128)(2,1)S(1)}, bf16[128,1024]{1,0:T(8,128)(2,1)S(1)}, u32[]{:S(2)}, u32[]{:S(2)}) collective-permute-start(bf16[128,1024]{1,0:T(8,128)(2,1)S(1)} %collective-permute-done.a_ref.refs_6_), channel_id=1, source_target_pairs={{0,0},{4,8},{8,4},{12,12},{1,1},{5,9},{9,5},{13,13},{2,2},{6,10},{... | collective-permute-start | bytes 786440 | tf_op jit(solution)/shard_map/ppermute | solution.py:385
  16.5 2.5 %collective-permute-start.5 = (f32[320,128]{1,0:T(8,128)S(1)}, f32[320,128]{1,0:T(8,128)S(1)}, u32[]{:S(2)}, u32[]{:S(2)}) collective-permute-start(f32[320,128]{1,0:T(8,128)S(1)} %shard_map.103.refs_0_), channel_id=1, source_target_pairs={{0,1},{1,0},{2,3},{3,2},{4,5},{5,4},{6,7},{7,6},{8,9},{9,8},{10,11... | collective-permute-start | bytes 491528 | tf_op jit(solution)/shard_map/ppermute | solution.py:21
  18.9 1.4 %collective-permute-start.6 = (f32[320,128]{1,0:T(8,128)S(1)}, f32[320,128]{1,0:T(8,128)S(1)}, u32[]{:S(2)}, u32[]{:S(2)}) collective-permute-start(f32[320,128]{1,0:T(8,128)S(1)} %collective-permute-done.1.refs_1_), channel_id=1, source_target_pairs={{0,1},{1,0},{2,3},{3,2},{4,5},{5,4},{6,7},{7,6},{8,9},{9,8},{10,11... | collective-permute-start | bytes 491528 | tf_op jit(solution)/shard_map/ppermute | solution.py:21
  25.7 11.6 %collective-permute-start.9 = (bf16[128,1024]{1,0:T(8,128)(2,1)}, bf16[128,1024]{1,0:T(8,128)(2,1)S(1)}, u32[]{:S(2)}, u32[]{:S(2)}) collective-permute-start(bf16[128,1024]{1,0:T(8,128)(2,1)} %get-tuple-element.56), channel_id=1, source_target_pairs={{0,4},{4,0},{8,12},{12,8},{1,5},{5,1},{9,13},{13,9},{2,6},{6,2},{1... | collective-permute-start | bytes 786440 | tf_op jit(solution)/shard_map/ppermute | solution.py:412
  31.4 20.4 %collective-permute-start.15 = (bf16[64,1024]{1,0:T(8,128)(2,1)S(1)}, bf16[64,1024]{1,0:T(8,128)(2,1)S(1)}, u32[]{:S(2)}, u32[]{:S(2)}) collective-permute-start(bf16[64,1024]{1,0:T(8,128)(2,1)S(1)} %bitcast.63), channel_id=1, source_target_pairs={{0,2},{2,0},{1,3},{3,1},{4,6},{6,4},{5,7},{7,5},{8,10},{10,8},{9,1... | collective-permute-start | bytes 393224 | tf_op jit(solution)/shard_map/ppermute | solution.py:21
  31.9 19.9 %collective-permute-start.14 = (bf16[1024,256]{1,0:T(8,128)(2,1)}, bf16[1024,256]{1,0:T(8,128)(2,1)S(1)}, u32[]{:S(2)}, u32[]{:S(2)}) collective-permute-start(bf16[1024,256]{1,0:T(8,128)(2,1)} %refs_0_.1), channel_id=1, source_target_pairs={{0,2},{2,0},{1,3},{3,1},{4,6},{6,4},{5,7},{7,5},{8,10},{10,8},{9,1... | collective-permute-start | bytes 1572872 | tf_op jit(solution)/shard_map/ppermute | solution.py:21
  37.4 5.8 %collective-permute-start.11 = (bf16[128,1024]{1,0:T(8,128)(2,1)S(1)}, bf16[128,1024]{1,0:T(8,128)(2,1)S(1)}, u32[]{:S(2)}, u32[]{:S(2)}) collective-permute-start(bf16[128,1024]{1,0:T(8,128)(2,1)S(1)} %fusion.3), channel_id=1, source_target_pairs={{0,0},{4,8},{8,4},{12,12},{1,1},{5,9},{9,5},{13,13},{2,2},{6,10},{... | collective-permute-start | bytes 786440 | tf_op jit(solution)/shard_map/ppermute | solution.py:412
  38.4 8.1 %collective-permute-start.10 = (bf16[128,1024]{1,0:T(8,128)(2,1)S(1)}, bf16[128,1024]{1,0:T(8,128)(2,1)S(1)}, u32[]{:S(2)}, u32[]{:S(2)}) collective-permute-start(bf16[128,1024]{1,0:T(8,128)(2,1)S(1)} %broadcast_select_fusion), channel_id=1, source_target_pairs={{0,4},{4,0},{8,12},{12,8},{1,5},{5,1},{9,13},{13,9},{2,6},{6,2},{1... | collective-permute-start | bytes 786440 | tf_op jit(solution)/shard_map/ppermute | solution.py:412
  46.8 5.0 %collective-permute-start.12 = (bf16[128,1024]{1,0:T(8,128)(2,1)S(1)}, bf16[128,1024]{1,0:T(8,128)(2,1)S(1)}, u32[]{:S(2)}, u32[]{:S(2)}) collective-permute-start(bf16[128,1024]{1,0:T(8,128)(2,1)S(1)} %get-tuple-element.99), channel_id=1, source_target_pairs={{0,0},{4,8},{8,4},{12,12},{1,1},{5,9},{9,5},{13,13},{2,2},{6,10},{... | collective-permute-start | bytes 786440 | tf_op jit(solution)/shard_map/ppermute | solution.py:412
  47.5 9.4 %collective-permute-start.13 = (bf16[128,1024]{1,0:T(8,128)(2,1)S(1)}, bf16[128,1024]{1,0:T(8,128)(2,1)S(1)}, u32[]{:S(2)}, u32[]{:S(2)}) collective-permute-start(bf16[128,1024]{1,0:T(8,128)(2,1)S(1)} %get-tuple-element.98), channel_id=1, source_target_pairs={{0,4},{4,0},{8,12},{12,8},{1,5},{5,1},{9,13},{13,9},{2,6},{6,2},{1... | collective-permute-start | bytes 786440 | tf_op jit(solution)/shard_map/ppermute | solution.py:412
  56.9 9.5 %collective-permute-start.16 = (bf16[128,1024]{1,0:T(8,128)(2,1)S(1)}, bf16[128,1024]{1,0:T(8,128)(2,1)S(1)}, u32[]{:S(2)}, u32[]{:S(2)}) collective-permute-start(bf16[128,1024]{1,0:T(8,128)(2,1)S(1)} %fusion), channel_id=1, source_target_pairs={{0,4},{4,0},{8,12},{12,8},{1,5},{5,1},{9,13},{13,9},{2,6},{6,2},{1... | collective-permute-start | bytes 786440 | tf_op jit(solution)/shard_map/ppermute | solution.py:412
  59.4 7.1 %collective-permute-start.19 = (bf16[128,1024]{1,0:T(8,128)(2,1)S(1)}, bf16[128,1024]{1,0:T(8,128)(2,1)S(1)}, u32[]{:S(2)}, u32[]{:S(2)}) collective-permute-start(bf16[128,1024]{1,0:T(8,128)(2,1)S(1)} %copy-done.23), channel_id=1, source_target_pairs={{0,0},{4,8},{8,4},{12,12},{1,1},{5,9},{9,5},{13,13},{2,2},{6,10},{... | collective-permute-start | bytes 786440 | tf_op jit(solution)/shard_map/ppermute | solution.py:385
  66.5 6.5 %collective-permute-start.20 = (bf16[128,1024]{1,0:T(8,128)(2,1)S(1)}, bf16[128,1024]{1,0:T(8,128)(2,1)S(1)}, u32[]{:S(2)}, u32[]{:S(2)}) collective-permute-start(bf16[128,1024]{1,0:T(8,128)(2,1)S(1)} %collective-permute-done.19.refs_10_), channel_id=1, source_target_pairs={{0,4},{4,0},{8,12},{12,8},{1,5},{5,1},{9,13},{13,9},{2,6},{6,2},{1... | collective-permute-start | bytes 786440 | tf_op jit(solution)/shard_map/ppermute | solution.py:385
  68.6 7.2 %collective-permute-start.18 = (bf16[128,1024]{1,0:T(8,128)(2,1)S(1)}, bf16[128,1024]{1,0:T(8,128)(2,1)S(1)}, u32[]{:S(2)}, u32[]{:S(2)}) collective-permute-start(bf16[128,1024]{1,0:T(8,128)(2,1)S(1)} %copy-done.26), channel_id=1, source_target_pairs={{0,4},{4,0},{8,12},{12,8},{1,5},{5,1},{9,13},{13,9},{2,6},{6,2},{1... | collective-permute-start | bytes 786440 | tf_op jit(solution)/shard_map/ppermute | solution.py:385
  71.8 1.3 %collective-permute-start.17 = (f32[128,128]{1,0:T(8,128)S(1)}, f32[128,128]{1,0:T(8,128)S(1)}, u32[]{:S(2)}, u32[]{:S(2)}) collective-permute-start(f32[128,128]{1,0:T(8,128)S(1)} %get-tuple-element.90), channel_id=1, source_target_pairs={{0,1},{1,0},{2,3},{3,2},{4,5},{5,4},{6,7},{7,6},{8,9},{9,8},{10,11... | collective-permute-start | bytes 196616 | tf_op jit(solution)/shard_map/ppermute | solution.py:21
  77.3 13.3 %all-to-all-start = ((bf16[8,160,128]{2,1,0:T(8,128)(2,1)}), bf16[8,160,128]{2,1,0:T(8,128)(2,1)S(1)}, u32[]{:S(2)}, u32[]{:S(2)}) async-start(bf16[8,160,128]{2,1,0:T(8,128)(2,1)} %shard_map.111), calls=%async_computation | async-start | bytes 655360 | tf_op jit(solution)/shard_map/all_to_all | solution.py:569
  82.7 1.3 %collective-permute-start.21 = (bf16[160,128]{1,0:T(8,128)(2,1)S(1)}, bf16[160,128]{1,0:T(8,128)(2,1)S(1)}, u32[]{:S(2)}, u32[]{:S(2)}) collective-permute-start(bf16[160,128]{1,0:T(8,128)(2,1)S(1)} %slice_bitcast_fusion.mine_ref), channel_id=1, source_target_pairs={{0,1},{1,0},{2,3},{3,2},{4,5},{5,4},{6,7},{7,6},{8,9},{9,8},{10,11... | collective-permute-start | bytes 122888 | tf_op jit(solution)/shard_map/ppermute | solution.py:21
  90.6 1.6 %collective-permute-start.22 = (bf16[8,160,128]{2,1,0:T(8,128)(2,1)S(1)}, bf16[8,160,128]{2,1,0:T(8,128)(2,1)S(1)}, u32[]{:S(2)}, u32[]{:S(2)}) collective-permute-start(bf16[8,160,128]{2,1,0:T(8,128)(2,1)S(1)} %all-to-all-done.refs_12_), channel_id=1, source_target_pairs={{0,1},{1,0},{2,3},{3,2},{4,5},{5,4},{6,7},{7,6},{8,9},{9,8},{10,11... | collective-permute-start | bytes 983048 | tf_op jit(solution)/shard_map/ppermute | solution.py:21
  (43 other events, 282.5 us)

commit v10 on v9

--- a/solution.py
+++ b/solution.py
@@ -13,7 +13,7 @@
 F32 = jnp.float32
 TOP = lax.Precision.HIGHEST
 PER_US = 1.15e9
-LIMIT = 8 * 1024 * 1024
+LIMIT = 16 * 1024 * 1024
 
 
 def cyclic(a, axis, by):
@@ -46,7 +46,7 @@
 
 
 VMEM = pl.BlockSpec(memory_space=pltpu.VMEM)
-ANY = pl.BlockSpec(memory_space=pl.ANY)
+HBM = pl.BlockSpec(memory_space=pltpu.HBM)
 
 
 def call(kernel, out_shape, span_us, *args, scratch=(), specs=None, limit=LIMIT):
@@ -536,9 +536,7 @@
     store, inners = chains(first, own, decay, calls, beside, riders, late)
     for f, a in zip(found, riders):
         f[0, 2] = a
-    done = []
-    for f, a in zip(found, groups):
-        done += relay(f, a, [step for step in slots if step not in f], store)
+    done = [relay(f, a, [t for t in slots if t not in f], store) for f, a in zip(found, groups)]
     grad_x, keep, give = call(
         functools.partial(outer_kernel, size, PARTS),
         (
@@ -562,7 +560,7 @@
             pltpu.VMEM((1, width), F32),
         ),
     )
-    taken = after(cyclic(give, "head", 1), *done)
+    taken = after(cyclic(give, "head", 1), *done[0])
     count = n_dp * n_seq
     copies = call(low_kernel, struct((count, rows + heads, rows), BF), 0.7, keep, taken)
     mine = copies[0]
@@ -572,7 +570,7 @@
         functools.partial(token_kernel, n_dp),
         struct((rows, width), BF),
         1.5,
-        mine,
+        after(mine, *done[-1]),
         other,
         *weights,
     )
@@ -590,7 +588,7 @@
         *toks,
         lows,
         swapped,
-        specs=[ANY] * (len(toks) + 2),
+        specs=[HBM] * len(toks) + [VMEM] * 2,
         limit=LIMIT + 2 * n_dp * n_seq * rows * (part + cols),
         scratch=(
             pltpu.VMEM((n_dp, n_seq * rows, part), BF),

time: 100 us -> 103 us (1.030)
  starting transfers between devices: 36.3 us -> 41.1 us
  local copies, waits for them, and re-layouts: 15 us -> 13.1 us
    ppermute x8, waiting for transfers between devices: 2.03 us -> 8.36 us  [relay(): found[kind, hop] = lax.ppermute(source, 'seq', pairs[kind])]
    ppermute x8, starting transfers between devices: 8.27 us -> 13.3 us  [relay(): found[kind, hop] = lax.ppermute(source, 'seq', pairs[kind])]
    all_to_all x1, waiting for transfers between devices: 4.15 us -> 0.01 us  [body(): lows = lax.all_to_all(copies, ('seq', 'dp'), 0, 0, tiled=True)]
    ppermute x9, waiting for transfers between devices: 11.9 us -> 9.46 us  [cyclic(): return lax.ppermute(a, axis, [(i, (i + by) % count) for i in range(count)])]
    unnamed x86 -> x82, local copies, waits for them, and re-layouts: 13.9 us -> 12 us
  transfers between devices with their start and end apart: 24 -> 24, of which waited for: 11 -> 9; matrix products, arithmetic and copies ran while one was open for 2% -> 2% of each run, Pallas kernels for 12% -> 12%
where the time goes in v10:
time: 103 us
  starting transfers between devices  41.1 us (40%)
  waiting for transfers between devices  32 us (31%)
  Pallas kernels  14.9 us (14%)
  local copies, waits for them, and re-layouts  13.1 us (13%)
  between operations  1.06 us (1%)
    ppermute x6, starting transfers between devices, chains(): got[k] = lax.ppermute(value, 'seq', sorted(to.items()))  16.6 us
    pallas_call x12, Pallas kernels, call(): pl.pallas_call(kernel, out_shape=out_shape, grid=(1,), in_specs=specs or...  14.9 us
    ppermute x6, waiting for transfers between devices, chains(): got[k] = lax.ppermute(value, 'seq', sorted(to.items()))  14.2 us
    ppermute x8, starting transfers between devices, relay(): found[kind, hop] = lax.ppermute(source, 'seq', pairs[kind])  13.3 us
    unnamed x82, local copies, waits for them, and re-layouts  12 us
    ppermute x9, waiting for transfers between devices, cyclic(): return lax.ppermute(a, axis, [(i, (i + by) % count) for i in range(count)])  9.46 us
    ppermute x8, waiting for transfers between devices, relay(): found[kind, hop] = lax.ppermute(source, 'seq', pairs[kind])  8.36 us
    ppermute x9, starting transfers between devices, cyclic(): return lax.ppermute(a, axis, [(i, (i + by) % count) for i in range(count)])  6.73 us
  transfers between devices with their start and end apart: 24, of which 9 were waited for; matrix products, arithmetic and copies ran while one was open for 2% of the time, Pallas kernels for 12%

profile of v10, /device:TPU:0, one launch (start us, length us, event | category | flops | bytes accessed | tf_op | source)
XLA Modules:
  0.0 102.7 jit_solution(7034838448542338695)
XLA Ops:
  1.8 3.0 %collective-permute-start = (bf16[128,1024]{1,0:T(8,128)(2,1)S(1)}, bf16[128,1024]{1,0:T(8,128)(2,1)S(1)}, u32[]{:S(2)}, u32[]{:S(2)}) collective-permute-start(bf16[128,1024]{1,0:T(8,128)(2,1)S(1)} %get-tuple-element.53), channel_id=1, source_target_pairs={{0,2},{2,0},{1,3},{3,1},{4,6},{6,4},{5,7},{7,5},{8,10},{10,8},{9,1... | collective-permute-start | bytes 786440 | tf_op jit(solution)/shard_map/ppermute | solution.py:21
  4.8 1.6 %collective-permute-start.2 = (bf16[128,1024]{1,0:T(8,128)(2,1)S(1)}, bf16[128,1024]{1,0:T(8,128)(2,1)S(1)}, u32[]{:S(2)}, u32[]{:S(2)}) collective-permute-start(bf16[128,1024]{1,0:T(8,128)(2,1)S(1)} %get-tuple-element.52.a_ref.refs_0_), channel_id=1, source_target_pairs={{0,4},{4,0},{8,12},{12,8},{1,5},{5,1},{9,13},{13,9},{2,6},{6,2},{1... | collective-permute-start | bytes 786440 | tf_op jit(solution)/shard_map/ppermute | solution.py:385
  7.0 4.1 %collective-permute-done.a_ref.refs_6_ = bf16[128,1024]{1,0:T(8,128)(2,1)S(1)} collective-permute-done((bf16[128,1024]{1,0:T(8,128)(2,1)S(1)}, bf16[128,1024]{1,0:T(8,128)(2,1)S(1)}, u32[]{:S(2)}, u32[]{:S(2)}) %collective-permute-start) | collective-permute-done | bytes 262176 | tf_op jit(solution)/shard_map/ppermute | solution.py:21
  11.1 1.8 %collective-permute-start.4 = (bf16[128,1024]{1,0:T(8,128)(2,1)S(1)}, bf16[128,1024]{1,0:T(8,128)(2,1)S(1)}, u32[]{:S(2)}, u32[]{:S(2)}) collective-permute-start(bf16[128,1024]{1,0:T(8,128)(2,1)S(1)} %collective-permute-done.a_ref.refs_6_), channel_id=1, source_target_pairs={{0,4},{4,0},{8,12},{12,8},{1,5},{5,1},{9,13},{13,9},{2,6},{6,2},{1... | collective-permute-start | bytes 786440 | tf_op jit(solution)/shard_map/ppermute | solution.py:385
  13.5 1.6 %collective-permute-start.1 = (f32[320,128]{1,0:T(8,128)S(1)}, f32[320,128]{1,0:T(8,128)S(1)}, u32[]{:S(2)}, u32[]{:S(2)}) collective-permute-start(f32[320,128]{1,0:T(8,128)S(1)} %shard_map.104), channel_id=1, source_target_pairs={{0,2},{2,0},{1,3},{3,1},{4,6},{6,4},{5,7},{7,5},{8,10},{10,8},{9,1... | collective-permute-start | bytes 491528 | tf_op jit(solution)/shard_map/ppermute | solution.py:21
  16.5 2.4 %collective-permute-done.1.refs_1_ = f32[320,128]{1,0:T(8,128)S(1)} collective-permute-done((f32[320,128]{1,0:T(8,128)S(1)}, f32[320,128]{1,0:T(8,128)S(1)}, u32[]{:S(2)}, u32[]{:S(2)}) %collective-permute-start.1) | collective-permute-done | bytes 163872 | tf_op jit(solution)/shard_map/ppermute | solution.py:21
  18.9 1.4 %collective-permute-done.6.refs_3_ = f32[320,128]{1,0:T(8,128)S(1)} collective-permute-done((f32[320,128]{1,0:T(8,128)S(1)}, f32[320,128]{1,0:T(8,128)S(1)}, u32[]{:S(2)}, u32[]{:S(2)}) %collective-permute-start.6) | collective-permute-done | bytes 163872 | tf_op jit(solution)/shard_map/ppermute | solution.py:21
  20.3 2.6 %shard_map.105 = (f32[2,2,128,1024]{3,2,1,0:T(8,128)S(1)}, f32[256,128]{1,0:T(8,128)S(1)}, f32[160,128]{1,0:T(8,128)S(1)}, bf16[128,1024]{1,0:T(8,128)(2,1)}, bf...) custom-call(f32[320,128]{1,0:T(8,128)S(1)} %shard_map.103.refs_0_, ...), custom_call_target="tpu_custom_call" | custom-call | flops 115000000 | bytes 1966336 | tf_op jit(solution)/shard_map/pallas_call | solution.py:54
  25.7 5.7 %collective-permute-start.9 = (bf16[128,1024]{1,0:T(8,128)(2,1)}, bf16[128,1024]{1,0:T(8,128)(2,1)S(1)}, u32[]{:S(2)}, u32[]{:S(2)}) collective-permute-start(bf16[128,1024]{1,0:T(8,128)(2,1)} %get-tuple-element.57), channel_id=1, source_target_pairs={{0,4},{4,0},{8,12},{12,8},{1,5},{5,1},{9,13},{13,9},{2,6},{6,2},{1... | collective-permute-start | bytes 786440 | tf_op jit(solution)/shard_map/ppermute | solution.py:412
  31.9 1.5 %collective-permute-start.14 = (bf16[1024,256]{1,0:T(8,128)(2,1)}, bf16[1024,256]{1,0:T(8,128)(2,1)S(1)}, u32[]{:S(2)}, u32[]{:S(2)}) collective-permute-start(bf16[1024,256]{1,0:T(8,128)(2,1)} %refs_0_.1), channel_id=1, source_target_pairs={{0,2},{2,0},{1,3},{3,1},{4,6},{6,4},{5,7},{7,5},{8,10},{10,8},{9,1... | collective-permute-start | bytes 1572872 | tf_op jit(solution)/shard_map/ppermute | solution.py:21
  38.3 3.8 %collective-permute-start.10 = (bf16[128,1024]{1,0:T(8,128)(2,1)S(1)}, bf16[128,1024]{1,0:T(8,128)(2,1)S(1)}, u32[]{:S(2)}, u32[]{:S(2)}) collective-permute-start(bf16[128,1024]{1,0:T(8,128)(2,1)S(1)} %broadcast_select_fusion), channel_id=1, source_target_pairs={{0,4},{4,0},{8,12},{12,8},{1,5},{5,1},{9,13},{13,9},{2,6},{6,2},{1... | collective-permute-start | bytes 786440 | tf_op jit(solution)/shard_map/ppermute | solution.py:412
  43.3 3.2 %collective-permute-done.10.refs_9_ = bf16[128,1024]{1,0:T(8,128)(2,1)S(1)} collective-permute-done((bf16[128,1024]{1,0:T(8,128)(2,1)S(1)}, bf16[128,1024]{1,0:T(8,128)(2,1)S(1)}, u32[]{:S(2)}, u32[]{:S(2)}) %collective-permute-start.10) | collective-permute-done | bytes 262176 | tf_op jit(solution)/shard_map/ppermute | solution.py:412
  47.4 3.3 %collective-permute-start.13 = (bf16[128,1024]{1,0:T(8,128)(2,1)S(1)}, bf16[128,1024]{1,0:T(8,128)(2,1)S(1)}, u32[]{:S(2)}, u32[]{:S(2)}) collective-permute-start(bf16[128,1024]{1,0:T(8,128)(2,1)S(1)} %get-tuple-element.100), channel_id=1, source_target_pairs={{0,4},{4,0},{8,12},{12,8},{1,5},{5,1},{9,13},{13,9},{2,6},{6,2},{1... | collective-permute-start | bytes 786440 | tf_op jit(solution)/shard_map/ppermute | solution.py:412
  51.8 5.0 %collective-permute-done.13 = bf16[128,1024]{1,0:T(8,128)(2,1)S(1)} collective-permute-done((bf16[128,1024]{1,0:T(8,128)(2,1)S(1)}, bf16[128,1024]{1,0:T(8,128)(2,1)S(1)}, u32[]{:S(2)}, u32[]{:S(2)}) %collective-permute-start.13) | collective-permute-done | bytes 262176 | tf_op jit(solution)/shard_map/ppermute | solution.py:412
  56.9 2.4 %collective-permute-start.16 = (bf16[128,1024]{1,0:T(8,128)(2,1)S(1)}, bf16[128,1024]{1,0:T(8,128)(2,1)S(1)}, u32[]{:S(2)}, u32[]{:S(2)}) collective-permute-start(bf16[128,1024]{1,0:T(8,128)(2,1)S(1)} %fusion), channel_id=1, source_target_pairs={{0,4},{4,0},{8,12},{12,8},{1,5},{5,1},{9,13},{13,9},{2,6},{6,2},{1... | collective-permute-start | bytes 786440 | tf_op jit(solution)/shard_map/ppermute | solution.py:412
  60.3 6.0 %collective-permute-done.16 = bf16[128,1024]{1,0:T(8,128)(2,1)S(1)} collective-permute-done((bf16[128,1024]{1,0:T(8,128)(2,1)S(1)}, bf16[128,1024]{1,0:T(8,128)(2,1)S(1)}, u32[]{:S(2)}, u32[]{:S(2)}) %collective-permute-start.16) | collective-permute-done | bytes 262176 | tf_op jit(solution)/shard_map/ppermute | solution.py:412
  66.4 1.8 %collective-permute-start.18 = (bf16[128,1024]{1,0:T(8,128)(2,1)S(1)}, bf16[128,1024]{1,0:T(8,128)(2,1)S(1)}, u32[]{:S(2)}, u32[]{:S(2)}) collective-permute-start(bf16[128,1024]{1,0:T(8,128)(2,1)S(1)} %copy-done.26), channel_id=1, source_target_pairs={{0,4},{4,0},{8,12},{12,8},{1,5},{5,1},{9,13},{13,9},{2,6},{6,2},{1... | collective-permute-start | bytes 786440 | tf_op jit(solution)/shard_map/ppermute | solution.py:385
  68.2 3.1 %shard_map.110 = (bf16[128,2048]{1,0:T(8,128)(2,1)}, f32[160,128]{1,0:T(8,128)S(1)}, f32[128,128]{1,0:T(8,128)S(1)}) custom-call(bf16[2,3,128,1024]{3,2,1,0:T(8,128)(2,1)S(1)} %bitcast_dynamic-update-slice_fusion.refs_0_, bf16[128,2048]{1,0:T(8,128)(2,1)S(1)} %bitcast.46, bf16[128,2048]{1,0:T(8,128)(2,1)S(1)} %bitcast.52, f32[256,128]{1,0:T(8,128)S(1)} %copy-done.37, ...), custom_call_target="tpu_custom_call" | custom-call | flops 3564999936 | bytes 4178048 | tf_op jit(solution)/shard_map/pallas_call | solution.py:54
  74.3 4.5 %all-to-all-start = ((bf16[8,160,128]{2,1,0:T(8,128)(2,1)}), bf16[8,160,128]{2,1,0:T(8,128)(2,1)S(1)}, u32[]{:S(2)}, u32[]{:S(2)}) async-start(bf16[8,160,128]{2,1,0:T(8,128)(2,1)} %shard_map.111), calls=%async_computation | async-start | bytes 655360 | tf_op jit(solution)/shard_map/all_to_all | solution.py:567
  78.7 4.7 %collective-permute-start.20 = (bf16[128,1024]{1,0:T(8,128)(2,1)}, bf16[128,1024]{1,0:T(8,128)(2,1)S(1)}, u32[]{:S(2)}, u32[]{:S(2)}) collective-permute-start(bf16[128,1024]{1,0:T(8,128)(2,1)} %collective-permute-done.19.refs_10_), channel_id=1, source_target_pairs={{0,4},{4,0},{8,12},{12,8},{1,5},{5,1},{9,13},{13,9},{2,6},{6,2},{1... | collective-permute-start | bytes 786440 | tf_op jit(solution)/shard_map/ppermute | solution.py:385
  84.3 8.2 %collective-permute-done.20.refs_11_ = bf16[128,1024]{1,0:T(8,128)(2,1)S(1)} collective-permute-done((bf16[128,1024]{1,0:T(8,128)(2,1)}, bf16[128,1024]{1,0:T(8,128)(2,1)S(1)}, u32[]{:S(2)}, u32[]{:S(2)}) %collective-permute-start.20) | collective-permute-done | bytes 262176 | tf_op jit(solution)/shard_map/ppermute | solution.py:385
  93.2 1.5 %shard_map.112 = bf16[128,2048]{1,0:T(8,128)(2,1)} custom-call(bf16[160,128]{1,0:T(8,128)(2,1)S(1)} %slice_bitcast_fusion.mine_ref, bf16[160,128]{1,0:T(8,128)(2,1)S(1)} %collective-permute-done.21.other_ref, bf16[1024,256]{1,0:T(8,128)(2,1)S(1)} %copy-done.13, bf16[64,1024]{1,0:T(8,128)(2,1)S(1)} %bitcast.64, bf16[1024,256]{1,0:T(8,128)(2,1)S(1)} %copy-done.15, ...), custom_call_target="tpu_custom_call" | custom-call | flops 1724999936 | bytes 1392640 | tf_op jit(solution)/shard_map/pallas_call | solution.py:54
  94.8 1.6 %collective-permute-done.22.refs_13_ = bf16[8,160,128]{2,1,0:T(8,128)(2,1)S(1)} collective-permute-done((bf16[8,160,128]{2,1,0:T(8,128)(2,1)S(1)}, bf16[8,160,128]{2,1,0:T(8,128)(2,1)S(1)}, u32[]{:S(2)}, u32[]{:S(2)}) %collective-permute-start.22) | collective-permute-done | bytes 327712 | tf_op jit(solution)/shard_map/ppermute | solution.py:21
  100.2 2.5 %shard_map.113 = (f32[1024,256]{1,0:T(8,128)}, f32[64,1024]{1,0:T(8,128)}) custom-call(bf16[128,1024]{1,0:T(8,128)(2,1)S(1)} %copy-done.17, bf16[128,1024]{1,0:T(8,128)(2,1)S(1)} %copy-done.21, bf16[128,1024]{1,0:T(8,128)(2,1)S(1)} %collective-permute-done.3.refs_8_.refs_2_, bf16[128,1024]{1,0:T(8,128)(2,1)S(1)} %collective-permute-done.9.refs_3_, ...), custom_call_target="tpu_custom_call" | custom-call | flops 2875000064 | bytes 3801088 | tf_op jit(solution)/shard_map/pallas_call | solution.py:54
  (130 shorter events, 24.5 us)
Async XLA Ops:
  1.8 9.3 %collective-permute-start = (bf16[128,1024]{1,0:T(8,128)(2,1)S(1)}, bf16[128,1024]{1,0:T(8,128)(2,1)S(1)}, u32[]{:S(2)}, u32[]{:S(2)}) collective-permute-start(bf16[128,1024]{1,0:T(8,128)(2,1)S(1)} %get-tuple-element.53), channel_id=1, source_target_pairs={{0,2},{2,0},{1,3},{3,1},{4,6},{6,4},{5,7},{7,5},{8,10},{10,8},{9,1... | collective-permute-start | bytes 786440 | tf_op jit(solution)/shard_map/ppermute | solution.py:21
  4.8 10.3 %collective-permute-start.2 = (bf16[128,1024]{1,0:T(8,128)(2,1)S(1)}, bf16[128,1024]{1,0:T(8,128)(2,1)S(1)}, u32[]{:S(2)}, u32[]{:S(2)}) collective-permute-start(bf16[128,1024]{1,0:T(8,128)(2,1)S(1)} %get-tuple-element.52.a_ref.refs_0_), channel_id=1, source_target_pairs={{0,4},{4,0},{8,12},{12,8},{1,5},{5,1},{9,13},{13,9},{2,6},{6,2},{1... | collective-permute-start | bytes 786440 | tf_op jit(solution)/shard_map/ppermute | solution.py:385
  6.4 10.1 %collective-permute-start.3 = (bf16[128,1024]{1,0:T(8,128)(2,1)S(1)}, bf16[128,1024]{1,0:T(8,128)(2,1)S(1)}, u32[]{:S(2)}, u32[]{:S(2)}) collective-permute-start(bf16[128,1024]{1,0:T(8,128)(2,1)S(1)} %get-tuple-element.52.a_ref.refs_0_), channel_id=1, source_target_pairs={{0,0},{4,8},{8,4},{12,12},{1,1},{5,9},{9,5},{13,13},{2,2},{6,10},{... | collective-permute-start | bytes 786440 | tf_op jit(solution)/shard_map/ppermute | solution.py:385
  11.1 7.8 %collective-permute-start.4 = (bf16[128,1024]{1,0:T(8,128)(2,1)S(1)}, bf16[128,1024]{1,0:T(8,128)(2,1)S(1)}, u32[]{:S(2)}, u32[]{:S(2)}) collective-permute-start(bf16[128,1024]{1,0:T(8,128)(2,1)S(1)} %collective-permute-done.a_ref.refs_6_), channel_id=1, source_target_pairs={{0,4},{4,0},{8,12},{12,8},{1,5},{5,1},{9,13},{13,9},{2,6},{6,2},{1... | collective-permute-start | bytes 786440 | tf_op jit(solution)/shard_map/ppermute | solution.py:385
  13.5 5.4 %collective-permute-start.1 = (f32[320,128]{1,0:T(8,128)S(1)}, f32[320,128]{1,0:T(8,128)S(1)}, u32[]{:S(2)}, u32[]{:S(2)}) collective-permute-start(f32[320,128]{1,0:T(8,128)S(1)} %shard_map.104), channel_id=1, source_target_pairs={{0,2},{2,0},{1,3},{3,1},{4,6},{6,4},{5,7},{7,5},{8,10},{10,8},{9,1... | collective-permute-start | bytes 491528 | tf_op jit(solution)/shard_map/ppermute | solution.py:21
  15.1 9.8 %collective-permute-start.7 = (bf16[128,1024]{1,0:T(8,128)(2,1)S(1)}, bf16[128,1024]{1,0:T(8,128)(2,1)S(1)}, u32[]{:S(2)}, u32[]{:S(2)}) collective-permute-start(bf16[128,1024]{1,0:T(8,128)(2,1)S(1)} %collective-permute-done.2.refs_1_), channel_id=1, source_target_pairs={{0,0},{4,8},{8,4},{12,12},{1,1},{5,9},{9,5},{13,13},{2,2},{6,10},{... | collective-permute-start | bytes 786440 | tf_op jit(solution)/shard_map/ppermute | solution.py:385
  15.8 9.2 %collective-permute-start.8 = (bf16[128,1024]{1,0:T(8,128)(2,1)S(1)}, bf16[128,1024]{1,0:T(8,128)(2,1)S(1)}, u32[]{:S(2)}, u32[]{:S(2)}) collective-permute-start(bf16[128,1024]{1,0:T(8,128)(2,1)S(1)} %collective-permute-done.a_ref.refs_6_), channel_id=1, source_target_pairs={{0,0},{4,8},{8,4},{12,12},{1,1},{5,9},{9,5},{13,13},{2,2},{6,10},{... | collective-permute-start | bytes 786440 | tf_op jit(solution)/shard_map/ppermute | solution.py:385
  16.5 2.5 %collective-permute-start.5 = (f32[320,128]{1,0:T(8,128)S(1)}, f32[320,128]{1,0:T(8,128)S(1)}, u32[]{:S(2)}, u32[]{:S(2)}) collective-permute-start(f32[320,128]{1,0:T(8,128)S(1)} %shard_map.103.refs_0_), channel_id=1, source_target_pairs={{0,1},{1,0},{2,3},{3,2},{4,5},{5,4},{6,7},{7,6},{8,9},{9,8},{10,11... | collective-permute-start | bytes 491528 | tf_op jit(solution)/shard_map/ppermute | solution.py:21
  18.9 1.4 %collective-permute-start.6 = (f32[320,128]{1,0:T(8,128)S(1)}, f32[320,128]{1,0:T(8,128)S(1)}, u32[]{:S(2)}, u32[]{:S(2)}) collective-permute-start(f32[320,128]{1,0:T(8,128)S(1)} %collective-permute-done.1.refs_1_), channel_id=1, source_target_pairs={{0,1},{1,0},{2,3},{3,2},{4,5},{5,4},{6,7},{7,6},{8,9},{9,8},{10,11... | collective-permute-start | bytes 491528 | tf_op jit(solution)/shard_map/ppermute | solution.py:21
  25.7 11.6 %collective-permute-start.9 = (bf16[128,1024]{1,0:T(8,128)(2,1)}, bf16[128,1024]{1,0:T(8,128)(2,1)S(1)}, u32[]{:S(2)}, u32[]{:S(2)}) collective-permute-start(bf16[128,1024]{1,0:T(8,128)(2,1)} %get-tuple-element.57), channel_id=1, source_target_pairs={{0,4},{4,0},{8,12},{12,8},{1,5},{5,1},{9,13},{13,9},{2,6},{6,2},{1... | collective-permute-start | bytes 786440 | tf_op jit(solution)/shard_map/ppermute | solution.py:412
  31.3 20.4 %collective-permute-start.15 = (bf16[64,1024]{1,0:T(8,128)(2,1)S(1)}, bf16[64,1024]{1,0:T(8,128)(2,1)S(1)}, u32[]{:S(2)}, u32[]{:S(2)}) collective-permute-start(bf16[64,1024]{1,0:T(8,128)(2,1)S(1)} %bitcast.63), channel_id=1, source_target_pairs={{0,2},{2,0},{1,3},{3,1},{4,6},{6,4},{5,7},{7,5},{8,10},{10,8},{9,1... | collective-permute-start | bytes 393224 | tf_op jit(solution)/shard_map/ppermute | solution.py:21
  31.9 19.9 %collective-permute-start.14 = (bf16[1024,256]{1,0:T(8,128)(2,1)}, bf16[1024,256]{1,0:T(8,128)(2,1)S(1)}, u32[]{:S(2)}, u32[]{:S(2)}) collective-permute-start(bf16[1024,256]{1,0:T(8,128)(2,1)} %refs_0_.1), channel_id=1, source_target_pairs={{0,2},{2,0},{1,3},{3,1},{4,6},{6,4},{5,7},{7,5},{8,10},{10,8},{9,1... | collective-permute-start | bytes 1572872 | tf_op jit(solution)/shard_map/ppermute | solution.py:21
  37.4 5.9 %collective-permute-start.11 = (bf16[128,1024]{1,0:T(8,128)(2,1)S(1)}, bf16[128,1024]{1,0:T(8,128)(2,1)S(1)}, u32[]{:S(2)}, u32[]{:S(2)}) collective-permute-start(bf16[128,1024]{1,0:T(8,128)(2,1)S(1)} %fusion.3), channel_id=1, source_target_pairs={{0,0},{4,8},{8,4},{12,12},{1,1},{5,9},{9,5},{13,13},{2,2},{6,10},{... | collective-permute-start | bytes 786440 | tf_op jit(solution)/shard_map/ppermute | solution.py:412
  38.3 8.1 %collective-permute-start.10 = (bf16[128,1024]{1,0:T(8,128)(2,1)S(1)}, bf16[128,1024]{1,0:T(8,128)(2,1)S(1)}, u32[]{:S(2)}, u32[]{:S(2)}) collective-permute-start(bf16[128,1024]{1,0:T(8,128)(2,1)S(1)} %broadcast_select_fusion), channel_id=1, source_target_pairs={{0,4},{4,0},{8,12},{12,8},{1,5},{5,1},{9,13},{13,9},{2,6},{6,2},{1... | collective-permute-start | bytes 786440 | tf_op jit(solution)/shard_map/ppermute | solution.py:412
  46.7 5.0 %collective-permute-start.12 = (bf16[128,1024]{1,0:T(8,128)(2,1)S(1)}, bf16[128,1024]{1,0:T(8,128)(2,1)S(1)}, u32[]{:S(2)}, u32[]{:S(2)}) collective-permute-start(bf16[128,1024]{1,0:T(8,128)(2,1)S(1)} %get-tuple-element.101), channel_id=1, source_target_pairs={{0,0},{4,8},{8,4},{12,12},{1,1},{5,9},{9,5},{13,13},{2,2},{6,10},{... | collective-permute-start | bytes 786440 | tf_op jit(solution)/shard_map/ppermute | solution.py:412
  47.4 9.4 %collective-permute-start.13 = (bf16[128,1024]{1,0:T(8,128)(2,1)S(1)}, bf16[128,1024]{1,0:T(8,128)(2,1)S(1)}, u32[]{:S(2)}, u32[]{:S(2)}) collective-permute-start(bf16[128,1024]{1,0:T(8,128)(2,1)S(1)} %get-tuple-element.100), channel_id=1, source_target_pairs={{0,4},{4,0},{8,12},{12,8},{1,5},{5,1},{9,13},{13,9},{2,6},{6,2},{1... | collective-permute-start | bytes 786440 | tf_op jit(solution)/shard_map/ppermute | solution.py:412
  56.9 9.4 %collective-permute-start.16 = (bf16[128,1024]{1,0:T(8,128)(2,1)S(1)}, bf16[128,1024]{1,0:T(8,128)(2,1)S(1)}, u32[]{:S(2)}, u32[]{:S(2)}) collective-permute-start(bf16[128,1024]{1,0:T(8,128)(2,1)S(1)} %fusion), channel_id=1, source_target_pairs={{0,4},{4,0},{8,12},{12,8},{1,5},{5,1},{9,13},{13,9},{2,6},{6,2},{1... | collective-permute-start | bytes 786440 | tf_op jit(solution)/shard_map/ppermute | solution.py:412
  66.4 6.4 %collective-permute-start.18 = (bf16[128,1024]{1,0:T(8,128)(2,1)S(1)}, bf16[128,1024]{1,0:T(8,128)(2,1)S(1)}, u32[]{:S(2)}, u32[]{:S(2)}) collective-permute-start(bf16[128,1024]{1,0:T(8,128)(2,1)S(1)} %copy-done.26), channel_id=1, source_target_pairs={{0,4},{4,0},{8,12},{12,8},{1,5},{5,1},{9,13},{13,9},{2,6},{6,2},{1... | collective-permute-start | bytes 786440 | tf_op jit(solution)/shard_map/ppermute | solution.py:385
  71.3 1.4 %collective-permute-start.17 = (f32[128,128]{1,0:T(8,128)S(1)}, f32[128,128]{1,0:T(8,128)S(1)}, u32[]{:S(2)}, u32[]{:S(2)}) collective-permute-start(f32[128,128]{1,0:T(8,128)S(1)} %get-tuple-element.91), channel_id=1, source_target_pairs={{0,1},{1,0},{2,3},{3,2},{4,5},{5,4},{6,7},{7,6},{8,9},{9,8},{10,11... | collective-permute-start | bytes 196616 | tf_op jit(solution)/shard_map/ppermute | solution.py:21
  71.3 7.4 %collective-permute-start.19 = (bf16[128,1024]{1,0:T(8,128)(2,1)S(1)}, bf16[128,1024]{1,0:T(8,128)(2,1)}, u32[]{:S(2)}, u32[]{:S(2)}) collective-permute-start(bf16[128,1024]{1,0:T(8,128)(2,1)S(1)} %copy-done.23), channel_id=1, source_target_pairs={{0,0},{4,8},{8,4},{12,12},{1,1},{5,9},{9,5},{13,13},{2,2},{6,10},{... | collective-permute-start | bytes 786440 | tf_op jit(solution)/shard_map/ppermute | solution.py:385
  74.3 20.5 %all-to-all-start = ((bf16[8,160,128]{2,1,0:T(8,128)(2,1)}), bf16[8,160,128]{2,1,0:T(8,128)(2,1)S(1)}, u32[]{:S(2)}, u32[]{:S(2)}) async-start(bf16[8,160,128]{2,1,0:T(8,128)(2,1)} %shard_map.111), calls=%async_computation | async-start | bytes 655360 | tf_op jit(solution)/shard_map/all_to_all | solution.py:567
  78.7 13.8 %collective-permute-start.20 = (bf16[128,1024]{1,0:T(8,128)(2,1)}, bf16[128,1024]{1,0:T(8,128)(2,1)S(1)}, u32[]{:S(2)}, u32[]{:S(2)}) collective-permute-start(bf16[128,1024]{1,0:T(8,128)(2,1)} %collective-permute-done.19.refs_10_), channel_id=1, source_target_pairs={{0,4},{4,0},{8,12},{12,8},{1,5},{5,1},{9,13},{13,9},{2,6},{6,2},{1... | collective-permute-start | bytes 786440 | tf_op jit(solution)/shard_map/ppermute | solution.py:385
  84.2 9.0 %collective-permute-start.21 = (bf16[160,128]{1,0:T(8,128)(2,1)S(1)}, bf16[160,128]{1,0:T(8,128)(2,1)S(1)}, u32[]{:S(2)}, u32[]{:S(2)}) collective-permute-start(bf16[160,128]{1,0:T(8,128)(2,1)S(1)} %slice_bitcast_fusion.mine_ref), channel_id=1, source_target_pairs={{0,1},{1,0},{2,3},{3,2},{4,5},{5,4},{6,7},{7,6},{8,9},{9,8},{10,11... | collective-permute-start | bytes 122888 | tf_op jit(solution)/shard_map/ppermute | solution.py:21
  94.8 1.6 %collective-permute-start.22 = (bf16[8,160,128]{2,1,0:T(8,128)(2,1)S(1)}, bf16[8,160,128]{2,1,0:T(8,128)(2,1)S(1)}, u32[]{:S(2)}, u32[]{:S(2)}) collective-permute-start(bf16[8,160,128]{2,1,0:T(8,128)(2,1)S(1)} %all-to-all-done.refs_12_), channel_id=1, source_target_pairs={{0,1},{1,0},{2,3},{3,2},{4,5},{5,4},{6,7},{7,6},{8,9},{9,8},{10,11... | collective-permute-start | bytes 983048 | tf_op jit(solution)/shard_map/ppermute | solution.py:21
  (41 other events, 322.1 us)

commit v11 on v8

--- a/solution.py
+++ b/solution.py
@@ -46,7 +46,7 @@
 
 
 VMEM = pl.BlockSpec(memory_space=pltpu.VMEM)
-ANY = pl.BlockSpec(memory_space=pl.ANY)
+HBM = pl.BlockSpec(memory_space=pltpu.HBM)
 
 
 def call(kernel, out_shape, span_us, *args, scratch=(), specs=None, limit=LIMIT):
@@ -522,23 +522,21 @@
     def beside(*others):
         for r in range(1, n_dp):
             weights.extend(cyclic(after(a, *others), "dp", r) for a in (w_bc, w_dt))
-        if not ride or n_dp == 1:
-            return weights[2:], spare
-        riders.extend(relay(found[1], groups[1], [(1, 1)], *others))
-        return weights[2:], riders[1:] + spare
+        return weights[2:], []
 
     def late(*others):
         if n_dp > 1:
             relay(found[1], groups[1], second, *others)
 
-    riders = [found[0][1, 1]] if ride else []
+    if ride and n_dp > 1:
+        spare += relay(found[1], groups[1], [(1, 1)])
+    first[0] = after(first[0], *spare)
+    riders = [f[1, 1] for f in found] if ride else []
     calls = [functools.partial(inner, q) for q in range(PARTS)]
     store, inners = chains(first, own, decay, calls, beside, riders, late)
     for f, a in zip(found, riders):
         f[0, 2] = a
-    done = []
-    for f, a in zip(found, groups):
-        done += relay(f, a, [step for step in slots if step not in f], store)
+    done = [relay(f, a, [t for t in slots if t not in f], store) for f, a in zip(found, groups)]
     grad_x, keep, give = call(
         functools.partial(outer_kernel, size, PARTS),
         (
@@ -562,7 +560,7 @@
             pltpu.VMEM((1, width), F32),
         ),
     )
-    taken = after(cyclic(give, "head", 1), *done)
+    taken = after(cyclic(give, "head", 1), *[a for d in done for a in d])
     count = n_dp * n_seq
     copies = call(low_kernel, struct((count, rows + heads, rows), BF), 1.2, keep, taken)
     mine = copies[0]
@@ -590,8 +588,8 @@
         *toks,
         lows,
         swapped,
-        specs=[ANY] * (len(toks) + 2),
-        limit=2 * LIMIT,
+        specs=[HBM] * (len(toks) + 2),
+        limit=56 * 1024 * 1024,
         scratch=(
             pltpu.VMEM((n_dp, n_seq * rows, part), BF),
             pltpu.VMEM((n_dp, cols, n_seq * rows), BF),

time: 98.6 us -> 102 us (1.034)
  starting transfers between devices: 38.4 us -> 45.2 us
  local copies, waits for them, and re-layouts: 9.99 us -> 3.71 us
  waiting for transfers between devices: 33.6 us -> 35.2 us
  Pallas kernels: 14.4 us -> 15.8 us
    ppermute x6, starting transfers between devices: 16.9 us -> 24.8 us  [chains(): got[k] = lax.ppermute(value, 'seq', sorted(to.items()))]
    unnamed x56 -> x40, local copies, waits for them, and re-layouts: 8.83 us -> 2.55 us
    all_to_all x1, waiting for transfers between devices: 3.25 us -> 5.14 us  [body(): lows = lax.all_to_all(copies, ('seq', 'dp'), 0, 0, tiled=True)]
    pallas_call x12, Pallas kernels: 14.4 us -> 15.8 us  [call(): pl.pallas_call(kernel, out_shape=out_shape, grid=(1,), in_specs=specs or...]
    ppermute x6, waiting for transfers between devices: 14.5 us -> 15.6 us  [chains(): got[k] = lax.ppermute(value, 'seq', sorted(to.items()))]
  transfers between devices with their start and end apart: 24 -> 24, of which waited for: 13 -> 11; matrix products, arithmetic and copies ran while one was open for 2% -> 2% of each run, Pallas kernels for 11% -> 11%
where the time goes in v11:
time: 102 us; the launch traced here: 101 us
  starting transfers between devices  45.2 us (44%)
  waiting for transfers between devices  35.2 us (35%)
  Pallas kernels  15.8 us (15%)
  local copies, waits for them, and re-layouts  3.71 us (4%)
  between operations  1.07 us (1%)
    ppermute x6, starting transfers between devices, chains(): got[k] = lax.ppermute(value, 'seq', sorted(to.items()))  24.8 us
    pallas_call x12, Pallas kernels, call(): pl.pallas_call(kernel, out_shape=out_shape, grid=(1,), in_specs=specs or...  15.8 us
    ppermute x6, waiting for transfers between devices, chains(): got[k] = lax.ppermute(value, 'seq', sorted(to.items()))  15.6 us
    ppermute x9, waiting for transfers between devices, cyclic(): return lax.ppermute(a, axis, [(i, (i + by) % count) for i in range(count)])  11.6 us
    ppermute x8, starting transfers between devices, relay(): found[kind, hop] = lax.ppermute(source, 'seq', pairs[kind])  9.09 us
    ppermute x9, starting transfers between devices, cyclic(): return lax.ppermute(a, axis, [(i, (i + by) % count) for i in range(count)])  6.6 us
    all_to_all x1, waiting for transfers between devices, body(): lows = lax.all_to_all(copies, ('seq', 'dp'), 0, 0, tiled=True)  5.14 us
    all_to_all x1, starting transfers between devices, body(): lows = lax.all_to_all(copies, ('seq', 'dp'), 0, 0, tiled=True)  4.66 us
  transfers between devices with their start and end apart: 24, of which 11 were waited for; matrix products, arithmetic and copies ran while one was open for 2% of the time, Pallas kernels for 11%

profile of v11, /device:TPU:0, one launch (start us, length us, event | category | flops | bytes accessed | tf_op | source)
XLA Modules:
  0.0 101.5 jit_solution(16445320448415373251)
XLA Ops:
  1.7 3.0 %collective-permute-start = (bf16[128,1024]{1,0:T(8,128)(2,1)S(1)}, bf16[128,1024]{1,0:T(8,128)(2,1)S(1)}, u32[]{:S(2)}, u32[]{:S(2)}) collective-permute-start(bf16[128,1024]{1,0:T(8,128)(2,1)S(1)} %get-tuple-element.52), channel_id=1, source_target_pairs={{0,2},{2,0},{1,3},{3,1},{4,6},{6,4},{5,7},{7,5},{8,10},{10,8},{9,1... | collective-permute-start | bytes 786440 | tf_op jit(solution)/shard_map/ppermute | solution.py:21
  4.7 1.6 %collective-permute-start.2 = (bf16[128,1024]{1,0:T(8,128)(2,1)S(1)}, bf16[128,1024]{1,0:T(8,128)(2,1)S(1)}, u32[]{:S(2)}, u32[]{:S(2)}) collective-permute-start(bf16[128,1024]{1,0:T(8,128)(2,1)S(1)} %get-tuple-element.51.a_ref.refs_0_), channel_id=1, source_target_pairs={{0,4},{4,0},{8,12},{12,8},{1,5},{5,1},{9,13},{13,9},{2,6},{6,2},{1... | collective-permute-start | bytes 786440 | tf_op jit(solution)/shard_map/ppermute | solution.py:385
  7.4 3.7 %collective-permute-done.a_ref.refs_6_ = bf16[128,1024]{1,0:T(8,128)(2,1)S(1)} collective-permute-done((bf16[128,1024]{1,0:T(8,128)(2,1)S(1)}, bf16[128,1024]{1,0:T(8,128)(2,1)S(1)}, u32[]{:S(2)}, u32[]{:S(2)}) %collective-permute-start) | collective-permute-done | bytes 262176 | tf_op jit(solution)/shard_map/ppermute | solution.py:21
  11.0 1.8 %collective-permute-start.4 = (bf16[128,1024]{1,0:T(8,128)(2,1)S(1)}, bf16[128,1024]{1,0:T(8,128)(2,1)S(1)}, u32[]{:S(2)}, u32[]{:S(2)}) collective-permute-start(bf16[128,1024]{1,0:T(8,128)(2,1)S(1)} %collective-permute-done.a_ref.refs_6_), channel_id=1, source_target_pairs={{0,4},{4,0},{8,12},{12,8},{1,5},{5,1},{9,13},{13,9},{2,6},{6,2},{1... | collective-permute-start | bytes 786440 | tf_op jit(solution)/shard_map/ppermute | solution.py:385
  13.2 1.6 %collective-permute-start.1 = (f32[320,128]{1,0:T(8,128)S(1)}, f32[320,128]{1,0:T(8,128)S(1)}, u32[]{:S(2)}, u32[]{:S(2)}) collective-permute-start(f32[320,128]{1,0:T(8,128)S(1)} %shard_map.104), channel_id=1, source_target_pairs={{0,2},{2,0},{1,3},{3,1},{4,6},{6,4},{5,7},{7,5},{8,10},{10,8},{9,1... | collective-permute-start | bytes 491528 | tf_op jit(solution)/shard_map/ppermute | solution.py:21
  14.8 3.8 %collective-permute-done.1.refs_1_ = f32[320,128]{1,0:T(8,128)S(1)} collective-permute-done((f32[320,128]{1,0:T(8,128)S(1)}, f32[320,128]{1,0:T(8,128)S(1)}, u32[]{:S(2)}, u32[]{:S(2)}) %collective-permute-start.1) | collective-permute-done | bytes 163872 | tf_op jit(solution)/shard_map/ppermute | solution.py:21
  21.4 2.1 %shard_map.105 = (f32[2,2,128,1024]{3,2,1,0:T(8,128)S(1)}, f32[256,128]{1,0:T(8,128)S(1)}, f32[160,128]{1,0:T(8,128)S(1)}, bf16[128,1024]{1,0:T(8,128)(2,1)S(1)}...) custom-call(f32[320,128]{1,0:T(8,128)S(1)} %shard_map.103.refs_0_, ...), custom_call_target="tpu_custom_call" | custom-call | flops 1150000000 | bytes 1966336 | tf_op jit(solution)/shard_map/pallas_call | solution.py:54
  23.6 12.7 %collective-permute-start.9 = (bf16[128,1024]{1,0:T(8,128)(2,1)S(1)}, bf16[128,1024]{1,0:T(8,128)(2,1)S(1)}, u32[]{:S(2)}, u32[]{:S(2)}) collective-permute-start(bf16[128,1024]{1,0:T(8,128)(2,1)S(1)} %get-tuple-element.56), channel_id=1, source_target_pairs={{0,4},{4,0},{8,12},{12,8},{1,5},{5,1},{9,13},{13,9},{2,6},{6,2},{1... | collective-permute-start | bytes 786440 | tf_op jit(solution)/shard_map/ppermute | solution.py:412
  36.3 1.5 %collective-permute-start.15 = (bf16[64,1024]{1,0:T(8,128)(2,1)S(1)}, bf16[64,1024]{1,0:T(8,128)(2,1)S(1)}, u32[]{:S(2)}, u32[]{:S(2)}) collective-permute-start(bf16[64,1024]{1,0:T(8,128)(2,1)S(1)} %bitcast.60), channel_id=1, source_target_pairs={{0,2},{2,0},{1,3},{3,1},{4,6},{6,4},{5,7},{7,5},{8,10},{10,8},{9,1... | collective-permute-start | bytes 393224 | tf_op jit(solution)/shard_map/ppermute | solution.py:21
  39.3 2.3 %collective-permute-done.9.refs_3_ = bf16[128,1024]{1,0:T(8,128)(2,1)S(1)} collective-permute-done((bf16[128,1024]{1,0:T(8,128)(2,1)S(1)}, bf16[128,1024]{1,0:T(8,128)(2,1)S(1)}, u32[]{:S(2)}, u32[]{:S(2)}) %collective-permute-start.9) | collective-permute-done | bytes 262176 | tf_op jit(solution)/shard_map/ppermute | solution.py:412
  42.5 4.7 %collective-permute-start.10 = (bf16[128,1024]{1,0:T(8,128)(2,1)S(1)}, bf16[128,1024]{1,0:T(8,128)(2,1)S(1)}, u32[]{:S(2)}, u32[]{:S(2)}) collective-permute-start(bf16[128,1024]{1,0:T(8,128)(2,1)S(1)} %broadcast_select_fusion), channel_id=1, source_target_pairs={{0,4},{4,0},{8,12},{12,8},{1,5},{5,1},{9,13},{13,9},{2,6},{6,2},{1... | collective-permute-start | bytes 786440 | tf_op jit(solution)/shard_map/ppermute | solution.py:412
  48.4 3.2 %collective-permute-done.10.refs_9_ = bf16[128,1024]{1,0:T(8,128)(2,1)S(1)} collective-permute-done((bf16[128,1024]{1,0:T(8,128)(2,1)S(1)}, bf16[128,1024]{1,0:T(8,128)(2,1)S(1)}, u32[]{:S(2)}, u32[]{:S(2)}) %collective-permute-start.10) | collective-permute-done | bytes 262176 | tf_op jit(solution)/shard_map/ppermute | solution.py:412
  52.6 3.7 %collective-permute-start.13 = (bf16[128,1024]{1,0:T(8,128)(2,1)S(1)}, bf16[128,1024]{1,0:T(8,128)(2,1)S(1)}, u32[]{:S(2)}, u32[]{:S(2)}) collective-permute-start(bf16[128,1024]{1,0:T(8,128)(2,1)S(1)} %get-tuple-element.98), channel_id=1, source_target_pairs={{0,4},{4,0},{8,12},{12,8},{1,5},{5,1},{9,13},{13,9},{2,6},{6,2},{1... | collective-permute-start | bytes 786440 | tf_op jit(solution)/shard_map/ppermute | solution.py:412
  57.2 4.8 %collective-permute-done.13 = bf16[128,1024]{1,0:T(8,128)(2,1)S(1)} collective-permute-done((bf16[128,1024]{1,0:T(8,128)(2,1)S(1)}, bf16[128,1024]{1,0:T(8,128)(2,1)S(1)}, u32[]{:S(2)}, u32[]{:S(2)}) %collective-permute-start.13) | collective-permute-done | bytes 262176 | tf_op jit(solution)/shard_map/ppermute | solution.py:412
  62.2 2.4 %collective-permute-start.16 = (bf16[128,1024]{1,0:T(8,128)(2,1)S(1)}, bf16[128,1024]{1,0:T(8,128)(2,1)S(1)}, u32[]{:S(2)}, u32[]{:S(2)}) collective-permute-start(bf16[128,1024]{1,0:T(8,128)(2,1)S(1)} %fusion), channel_id=1, source_target_pairs={{0,4},{4,0},{8,12},{12,8},{1,5},{5,1},{9,13},{13,9},{2,6},{6,2},{1... | collective-permute-start | bytes 786440 | tf_op jit(solution)/shard_map/ppermute | solution.py:412
  66.2 5.2 %collective-permute-done.16 = bf16[128,1024]{1,0:T(8,128)(2,1)S(1)} collective-permute-done((bf16[128,1024]{1,0:T(8,128)(2,1)S(1)}, bf16[128,1024]{1,0:T(8,128)(2,1)S(1)}, u32[]{:S(2)}, u32[]{:S(2)}) %collective-permute-start.16) | collective-permute-done | bytes 262176 | tf_op jit(solution)/shard_map/ppermute | solution.py:412
  71.5 2.3 %collective-permute-start.20 = (bf16[128,1024]{1,0:T(8,128)(2,1)S(1)}, bf16[128,1024]{1,0:T(8,128)(2,1)S(1)}, u32[]{:S(2)}, u32[]{:S(2)}) collective-permute-start(bf16[128,1024]{1,0:T(8,128)(2,1)S(1)} %collective-permute-done.19.refs_10_), channel_id=1, source_target_pairs={{0,4},{4,0},{8,12},{12,8},{1,5},{5,1},{9,13},{13,9},{2,6},{6,2},{1... | collective-permute-start | bytes 786440 | tf_op jit(solution)/shard_map/ppermute | solution.py:385
  73.9 3.1 %shard_map.110 = (bf16[128,2048]{1,0:T(8,128)(2,1)}, f32[160,128]{1,0:T(8,128)S(1)}, f32[128,128]{1,0:T(8,128)S(1)}) custom-call(bf16[2,3,128,1024]{3,2,1,0:T(8,128)(2,1)S(1)} %bitcast_dynamic-update-slice_fusion.refs_0_, bf16[128,2048]{1,0:T(8,128)(2,1)S(1)} %bitcast.51, bf16[128,2048]{1,0:T(8,128)(2,1)S(1)} %bitcast.57, ...), custom_call_target="tpu_custom_call" | custom-call | flops 6209999872 | bytes 4178048 | tf_op jit(solution)/shard_map/pallas_call | solution.py:54
  78.2 2.8 %collective-permute-done.18.refs_5_ = bf16[128,1024]{1,0:T(8,128)(2,1)} collective-permute-done((bf16[128,1024]{1,0:T(8,128)(2,1)}, bf16[128,1024]{1,0:T(8,128)(2,1)}, u32[]{:S(2)}, u32[]{:S(2)}) %collective-permute-start.18) | collective-permute-done | bytes 262176 | tf_op jit(solution)/shard_map/ppermute | solution.py:385
  81.8 4.7 %all-to-all-start = ((bf16[8,160,128]{2,1,0:T(8,128)(2,1)}), bf16[8,160,128]{2,1,0:T(8,128)(2,1)S(1)}, u32[]{:S(2)}, u32[]{:S(2)}) async-start(bf16[8,160,128]{2,1,0:T(8,128)(2,1)} %shard_map.111), calls=%async_computation | async-start | bytes 655360 | tf_op jit(solution)/shard_map/all_to_all | solution.py:567
  88.5 1.5 %shard_map.112 = bf16[128,2048]{1,0:T(8,128)(2,1)} custom-call(bf16[160,128]{1,0:T(8,128)(2,1)S(1)} %slice_bitcast_fusion.mine_ref, bf16[160,128]{1,0:T(8,128)(2,1)S(1)} %collective-permute-done.21.other_ref, bf16[1024,256]{1,0:T(8,128)(2,1)S(1)} %copy-done.3, bf16[64,1024]{1,0:T(8,128)(2,1)S(1)} %bitcast.61, ...), custom_call_target="tpu_custom_call" | custom-call | flops 3335000064 | bytes 1392640 | tf_op jit(solution)/shard_map/pallas_call | solution.py:54
  90.0 5.1 %all-to-all-done.refs_12_ = bf16[8,160,128]{2,1,0:T(8,128)(2,1)S(1)} async-done(((bf16[8,160,128]{2,1,0:T(8,128)(2,1)}), bf16[8,160,128]{2,1,0:T(8,128)(2,1)S(1)}, u32[]{:S(2)}, u32[]{:S(2)}) %all-to-all-start) | async-done | bytes 327712 | tf_op jit(solution)/shard_map/all_to_all | solution.py:567
  95.1 1.6 %collective-permute-done.22.refs_13_ = bf16[8,160,128]{2,1,0:T(8,128)(2,1)S(1)} collective-permute-done((bf16[8,160,128]{2,1,0:T(8,128)(2,1)S(1)}, bf16[8,160,128]{2,1,0:T(8,128)(2,1)S(1)}, u32[]{:S(2)}, u32[]{:S(2)}) %collective-permute-start.22) | collective-permute-done | bytes 327712 | tf_op jit(solution)/shard_map/ppermute | solution.py:21
  97.5 4.0 %shard_map.113 = (f32[1024,256]{1,0:T(8,128)}, f32[64,1024]{1,0:T(8,128)}) custom-call(bf16[128,1024]{1,0:T(8,128)(2,1)} %copy-done.4, bf16[128,1024]{1,0:T(8,128)(2,1)} %copy-done.15, bf16[128,1024]{1,0:T(8,128)(2,1)} %copy-done.6, bf16[128,1024]{1,0:T(8,128)(2,1)} %copy-done.11, bf16[128,1024]{1,0:T(8,128)(2,1)} %collective-permute-done.7.refs_4_, ...), custom_call_target="tpu_custom_call" | custom-call | flops 4600000000 | bytes 3801088 | tf_op jit(solution)/shard_map/pallas_call | solution.py:54
  (88 shorter events, 17.2 us)
Async XLA Ops:
  1.7 9.3 %collective-permute-start = (bf16[128,1024]{1,0:T(8,128)(2,1)S(1)}, bf16[128,1024]{1,0:T(8,128)(2,1)S(1)}, u32[]{:S(2)}, u32[]{:S(2)}) collective-permute-start(bf16[128,1024]{1,0:T(8,128)(2,1)S(1)} %get-tuple-element.52), channel_id=1, source_target_pairs={{0,2},{2,0},{1,3},{3,1},{4,6},{6,4},{5,7},{7,5},{8,10},{10,8},{9,1... | collective-permute-start | bytes 786440 | tf_op jit(solution)/shard_map/ppermute | solution.py:21
  4.7 10.0 %collective-permute-start.2 = (bf16[128,1024]{1,0:T(8,128)(2,1)S(1)}, bf16[128,1024]{1,0:T(8,128)(2,1)S(1)}, u32[]{:S(2)}, u32[]{:S(2)}) collective-permute-start(bf16[128,1024]{1,0:T(8,128)(2,1)S(1)} %get-tuple-element.51.a_ref.refs_0_), channel_id=1, source_target_pairs={{0,4},{4,0},{8,12},{12,8},{1,5},{5,1},{9,13},{13,9},{2,6},{6,2},{1... | collective-permute-start | bytes 786440 | tf_op jit(solution)/shard_map/ppermute | solution.py:385
  6.3 8.4 %collective-permute-start.3 = (bf16[128,1024]{1,0:T(8,128)(2,1)S(1)}, bf16[128,1024]{1,0:T(8,128)(2,1)S(1)}, u32[]{:S(2)}, u32[]{:S(2)}) collective-permute-start(bf16[128,1024]{1,0:T(8,128)(2,1)S(1)} %get-tuple-element.51.a_ref.refs_0_), channel_id=1, source_target_pairs={{0,0},{4,8},{8,4},{12,12},{1,1},{5,9},{9,5},{13,13},{2,2},{6,10},{... | collective-permute-start | bytes 786440 | tf_op jit(solution)/shard_map/ppermute | solution.py:385
  11.0 7.5 %collective-permute-start.4 = (bf16[128,1024]{1,0:T(8,128)(2,1)S(1)}, bf16[128,1024]{1,0:T(8,128)(2,1)S(1)}, u32[]{:S(2)}, u32[]{:S(2)}) collective-permute-start(bf16[128,1024]{1,0:T(8,128)(2,1)S(1)} %collective-permute-done.a_ref.refs_6_), channel_id=1, source_target_pairs={{0,4},{4,0},{8,12},{12,8},{1,5},{5,1},{9,13},{13,9},{2,6},{6,2},{1... | collective-permute-start | bytes 786440 | tf_op jit(solution)/shard_map/ppermute | solution.py:385
  13.2 5.4 %collective-permute-start.1 = (f32[320,128]{1,0:T(8,128)S(1)}, f32[320,128]{1,0:T(8,128)S(1)}, u32[]{:S(2)}, u32[]{:S(2)}) collective-permute-start(f32[320,128]{1,0:T(8,128)S(1)} %shard_map.104), channel_id=1, source_target_pairs={{0,2},{2,0},{1,3},{3,1},{4,6},{6,4},{5,7},{7,5},{8,10},{10,8},{9,1... | collective-permute-start | bytes 491528 | tf_op jit(solution)/shard_map/ppermute | solution.py:21
  14.7 6.6 %collective-permute-start.5 = (f32[320,128]{1,0:T(8,128)S(1)}, f32[320,128]{1,0:T(8,128)S(1)}, u32[]{:S(2)}, u32[]{:S(2)}) collective-permute-start(f32[320,128]{1,0:T(8,128)S(1)} %shard_map.103.refs_0_), channel_id=1, source_target_pairs={{0,1},{1,0},{2,3},{3,2},{4,5},{5,4},{6,7},{7,6},{8,9},{9,8},{10,11... | collective-permute-start | bytes 491528 | tf_op jit(solution)/shard_map/ppermute | solution.py:21
  18.6 2.8 %collective-permute-start.6 = (f32[320,128]{1,0:T(8,128)S(1)}, f32[320,128]{1,0:T(8,128)S(1)}, u32[]{:S(2)}, u32[]{:S(2)}) collective-permute-start(f32[320,128]{1,0:T(8,128)S(1)} %collective-permute-done.1.refs_1_), channel_id=1, source_target_pairs={{0,1},{1,0},{2,3},{3,2},{4,5},{5,4},{6,7},{7,6},{8,9},{9,8},{10,11... | collective-permute-start | bytes 491528 | tf_op jit(solution)/shard_map/ppermute | solution.py:21
  19.3 4.3 %collective-permute-start.7 = (bf16[128,1024]{1,0:T(8,128)(2,1)S(1)}, bf16[128,1024]{1,0:T(8,128)(2,1)}, u32[]{:S(2)}, u32[]{:S(2)}) collective-permute-start(bf16[128,1024]{1,0:T(8,128)(2,1)S(1)} %collective-permute-done.2.refs_1_), channel_id=1, source_target_pairs={{0,0},{4,8},{8,4},{12,12},{1,1},{5,9},{9,5},{13,13},{2,2},{6,10},{... | collective-permute-start | bytes 786440 | tf_op jit(solution)/shard_map/ppermute | solution.py:385
  20.6 3.0 %collective-permute-start.8 = (bf16[128,1024]{1,0:T(8,128)(2,1)S(1)}, bf16[128,1024]{1,0:T(8,128)(2,1)S(1)}, u32[]{:S(2)}, u32[]{:S(2)}) collective-permute-start(bf16[128,1024]{1,0:T(8,128)(2,1)S(1)} %collective-permute-done.a_ref.refs_6_), channel_id=1, source_target_pairs={{0,0},{4,8},{8,4},{12,12},{1,1},{5,9},{9,5},{13,13},{2,2},{6,10},{... | collective-permute-start | bytes 786440 | tf_op jit(solution)/shard_map/ppermute | solution.py:385
  23.6 18.1 %collective-permute-start.9 = (bf16[128,1024]{1,0:T(8,128)(2,1)S(1)}, bf16[128,1024]{1,0:T(8,128)(2,1)S(1)}, u32[]{:S(2)}, u32[]{:S(2)}) collective-permute-start(bf16[128,1024]{1,0:T(8,128)(2,1)S(1)} %get-tuple-element.56), channel_id=1, source_target_pairs={{0,4},{4,0},{8,12},{12,8},{1,5},{5,1},{9,13},{13,9},{2,6},{6,2},{1... | collective-permute-start | bytes 786440 | tf_op jit(solution)/shard_map/ppermute | solution.py:412
  36.3 21.0 %collective-permute-start.15 = (bf16[64,1024]{1,0:T(8,128)(2,1)S(1)}, bf16[64,1024]{1,0:T(8,128)(2,1)S(1)}, u32[]{:S(2)}, u32[]{:S(2)}) collective-permute-start(bf16[64,1024]{1,0:T(8,128)(2,1)S(1)} %bitcast.60), channel_id=1, source_target_pairs={{0,2},{2,0},{1,3},{3,1},{4,6},{6,4},{5,7},{7,5},{8,10},{10,8},{9,1... | collective-permute-start | bytes 393224 | tf_op jit(solution)/shard_map/ppermute | solution.py:21
  37.8 19.5 %collective-permute-start.14 = (bf16[1024,256]{1,0:T(8,128)(2,1)S(1)}, bf16[1024,256]{1,0:T(8,128)(2,1)S(1)}, u32[]{:S(2)}, u32[]{:S(2)}) collective-permute-start(bf16[1024,256]{1,0:T(8,128)(2,1)S(1)} %copy-done.3), channel_id=1, source_target_pairs={{0,2},{2,0},{1,3},{3,1},{4,6},{6,4},{5,7},{7,5},{8,10},{10,8},{9,1... | collective-permute-start | bytes 1572872 | tf_op jit(solution)/shard_map/ppermute | solution.py:21
  41.8 6.6 %collective-permute-start.11 = (bf16[128,1024]{1,0:T(8,128)(2,1)S(1)}, bf16[128,1024]{1,0:T(8,128)(2,1)S(1)}, u32[]{:S(2)}, u32[]{:S(2)}) collective-permute-start(bf16[128,1024]{1,0:T(8,128)(2,1)S(1)} %fusion.3), channel_id=1, source_target_pairs={{0,0},{4,8},{8,4},{12,12},{1,1},{5,9},{9,5},{13,13},{2,2},{6,10},{... | collective-permute-start | bytes 786440 | tf_op jit(solution)/shard_map/ppermute | solution.py:412
  42.5 9.1 %collective-permute-start.10 = (bf16[128,1024]{1,0:T(8,128)(2,1)S(1)}, bf16[128,1024]{1,0:T(8,128)(2,1)S(1)}, u32[]{:S(2)}, u32[]{:S(2)}) collective-permute-start(bf16[128,1024]{1,0:T(8,128)(2,1)S(1)} %broadcast_select_fusion), channel_id=1, source_target_pairs={{0,4},{4,0},{8,12},{12,8},{1,5},{5,1},{9,13},{13,9},{2,6},{6,2},{1... | collective-permute-start | bytes 786440 | tf_op jit(solution)/shard_map/ppermute | solution.py:412
  51.9 5.4 %collective-permute-start.12 = (bf16[128,1024]{1,0:T(8,128)(2,1)S(1)}, bf16[128,1024]{1,0:T(8,128)(2,1)S(1)}, u32[]{:S(2)}, u32[]{:S(2)}) collective-permute-start(bf16[128,1024]{1,0:T(8,128)(2,1)S(1)} %get-tuple-element.99), channel_id=1, source_target_pairs={{0,0},{4,8},{8,4},{12,12},{1,1},{5,9},{9,5},{13,13},{2,2},{6,10},{... | collective-permute-start | bytes 786440 | tf_op jit(solution)/shard_map/ppermute | solution.py:412
  52.6 9.5 %collective-permute-start.13 = (bf16[128,1024]{1,0:T(8,128)(2,1)S(1)}, bf16[128,1024]{1,0:T(8,128)(2,1)S(1)}, u32[]{:S(2)}, u32[]{:S(2)}) collective-permute-start(bf16[128,1024]{1,0:T(8,128)(2,1)S(1)} %get-tuple-element.98), channel_id=1, source_target_pairs={{0,4},{4,0},{8,12},{12,8},{1,5},{5,1},{9,13},{13,9},{2,6},{6,2},{1... | collective-permute-start | bytes 786440 | tf_op jit(solution)/shard_map/ppermute | solution.py:412
  62.2 9.3 %collective-permute-start.16 = (bf16[128,1024]{1,0:T(8,128)(2,1)S(1)}, bf16[128,1024]{1,0:T(8,128)(2,1)S(1)}, u32[]{:S(2)}, u32[]{:S(2)}) collective-permute-start(bf16[128,1024]{1,0:T(8,128)(2,1)S(1)} %fusion), channel_id=1, source_target_pairs={{0,4},{4,0},{8,12},{12,8},{1,5},{5,1},{9,13},{13,9},{2,6},{6,2},{1... | collective-permute-start | bytes 786440 | tf_op jit(solution)/shard_map/ppermute | solution.py:412
  64.6 6.9 %collective-permute-start.19 = (bf16[128,1024]{1,0:T(8,128)(2,1)S(1)}, bf16[128,1024]{1,0:T(8,128)(2,1)S(1)}, u32[]{:S(2)}, u32[]{:S(2)}) collective-permute-start(bf16[128,1024]{1,0:T(8,128)(2,1)S(1)} %copy-done.17), channel_id=1, source_target_pairs={{0,0},{4,8},{8,4},{12,12},{1,1},{5,9},{9,5},{13,13},{2,2},{6,10},{... | collective-permute-start | bytes 786440 | tf_op jit(solution)/shard_map/ppermute | solution.py:385
  71.5 6.7 %collective-permute-start.20 = (bf16[128,1024]{1,0:T(8,128)(2,1)S(1)}, bf16[128,1024]{1,0:T(8,128)(2,1)S(1)}, u32[]{:S(2)}, u32[]{:S(2)}) collective-permute-start(bf16[128,1024]{1,0:T(8,128)(2,1)S(1)} %collective-permute-done.19.refs_10_), channel_id=1, source_target_pairs={{0,4},{4,0},{8,12},{12,8},{1,5},{5,1},{9,13},{13,9},{2,6},{6,2},{1... | collective-permute-start | bytes 786440 | tf_op jit(solution)/shard_map/ppermute | solution.py:385
  73.8 7.3 %collective-permute-start.18 = (bf16[128,1024]{1,0:T(8,128)(2,1)}, bf16[128,1024]{1,0:T(8,128)(2,1)}, u32[]{:S(2)}, u32[]{:S(2)}) collective-permute-start(bf16[128,1024]{1,0:T(8,128)(2,1)} %collective-permute-done.7.refs_4_), channel_id=1, source_target_pairs={{0,4},{4,0},{8,12},{12,8},{1,5},{5,1},{9,13},{13,9},{2,6},{6,2},{1... | collective-permute-start | bytes 786440 | tf_op jit(solution)/shard_map/ppermute | solution.py:385
  76.9 1.3 %collective-permute-start.17 = (f32[128,128]{1,0:T(8,128)S(1)}, f32[128,128]{1,0:T(8,128)S(1)}, u32[]{:S(2)}, u32[]{:S(2)}) collective-permute-start(f32[128,128]{1,0:T(8,128)S(1)} %get-tuple-element.90), channel_id=1, source_target_pairs={{0,1},{1,0},{2,3},{3,2},{4,5},{5,4},{6,7},{7,6},{8,9},{9,8},{10,11... | collective-permute-start | bytes 196616 | tf_op jit(solution)/shard_map/ppermute | solution.py:21
  81.8 13.3 %all-to-all-start = ((bf16[8,160,128]{2,1,0:T(8,128)(2,1)}), bf16[8,160,128]{2,1,0:T(8,128)(2,1)S(1)}, u32[]{:S(2)}, u32[]{:S(2)}) async-start(bf16[8,160,128]{2,1,0:T(8,128)(2,1)} %shard_map.111), calls=%async_computation | async-start | bytes 655360 | tf_op jit(solution)/shard_map/all_to_all | solution.py:567
  87.3 1.2 %collective-permute-start.21 = (bf16[160,128]{1,0:T(8,128)(2,1)S(1)}, bf16[160,128]{1,0:T(8,128)(2,1)S(1)}, u32[]{:S(2)}, u32[]{:S(2)}) collective-permute-start(bf16[160,128]{1,0:T(8,128)(2,1)S(1)} %slice_bitcast_fusion.mine_ref), channel_id=1, source_target_pairs={{0,1},{1,0},{2,3},{3,2},{4,5},{5,4},{6,7},{7,6},{8,9},{9,8},{10,11... | collective-permute-start | bytes 122888 | tf_op jit(solution)/shard_map/ppermute | solution.py:21
  95.1 1.6 %collective-permute-start.22 = (bf16[8,160,128]{2,1,0:T(8,128)(2,1)S(1)}, bf16[8,160,128]{2,1,0:T(8,128)(2,1)S(1)}, u32[]{:S(2)}, u32[]{:S(2)}) collective-permute-start(bf16[8,160,128]{2,1,0:T(8,128)(2,1)S(1)} %all-to-all-done.refs_12_), channel_id=1, source_target_pairs={{0,1},{1,0},{2,3},{3,2},{4,5},{5,4},{6,7},{7,6},{8,9},{9,8},{10,11... | collective-permute-start | bytes 983048 | tf_op jit(solution)/shard_map/ppermute | solution.py:21
  (20 other events, 150.3 us)

commit v12 on v11

--- a/solution.py
+++ b/solution.py
@@ -49,14 +49,15 @@
 HBM = pl.BlockSpec(memory_space=pltpu.HBM)
 
 
-def call(kernel, out_shape, span_us, *args, scratch=(), specs=None, limit=LIMIT):
+def call(kernel, out_shape, span_us, *args, scratch=(), specs=None, out_specs=None, aliases={}, limit=LIMIT):
     size = sum(a.size * a.dtype.itemsize for a in args)
     return pl.pallas_call(
         kernel,
         out_shape=out_shape,
         grid=(1,),
         in_specs=specs or [VMEM] * len(args),
-        out_specs=jax.tree.map(lambda _: VMEM, out_shape),
+        out_specs=out_specs or jax.tree.map(lambda _: VMEM, out_shape),
+        input_output_aliases=aliases,
         scratch_shapes=list(scratch),
         compiler_params=pltpu.CompilerParams(vmem_limit_bytes=limit),
         cost_estimate=pl.CostEstimate(
@@ -218,17 +219,21 @@
     sums_ref[1] = mm(pick, xg_ref[...], 1, 1)
 
 
-def outer_kernel(size, parts, *refs):
+def outer_kernel(k, chunks, size, parts, *refs):
     store_ref, x_ref, g_ref, bc_ref, hp_ref, rate_ref = refs[:6]
-    gxs, dss, sums = (refs[6 + k * parts : 6 + (k + 1) * parts] for k in range(3))
-    grad_ref, keep_ref, give_ref, wv_ref, eu_ref, io_ref = refs[6 + 3 * parts :]
-    rate = rate_ref[...].T
-    rows, width = x_ref.shape
-    heads = rate_ref.shape[1]
-    chunks, step = store_ref.shape[1] - 1, store_ref.shape[3]
-    piece = width // parts
+    gxs, dss, sums = (refs[6 + q * parts : 6 + (q + 1) * parts] for q in range(3))
+    rest = refs[6 + 3 * parts :]
+    wv_ref, eu_ref = rest[-2:]
+    rows, step = x_ref.shape
+    all_heads = rate_ref.shape[1]
+    heads = all_heads // chunks
+    mine = slice(k * heads, (k + 1) * heads)
+    piece = step // parts
     b, c = bc_ref[0:rows, :], bc_ref[rows : 2 * rows, :]
-    pre, dt, cum, grow, w = (hp_ref[k * heads : (k + 1) * heads, :] for k in range(5))
+    pre, dt, cum, grow, w = (
+        hp_ref[q * all_heads + k * heads : q * all_heads + (k + 1) * heads, :] for q in range(5)
+    )
+    rate = rate_ref[...].T[mine]
     ds = dss[0][...]
     for ref in dss[1:]:
         ds = ds + ref[...]
@@ -236,38 +241,27 @@
     dc = mm(b, ds, 0, 1, TOP)
     b_wide = jnp.concatenate(halves(b), axis=1)
     c_wide = jnp.concatenate(halves(c), axis=1)
-    for k in range(chunks):
-        place = slice(k * step, (k + 1) * step)
-        late = slice(width + k * step, width + (k + 1) * step)
-        pick = head_lanes(heads, step, size, k * step).astype(BF)
-        incoming, outgoing = store_ref[0, k], store_ref[1, k]
-        u = mm(c_wide, jnp.concatenate([incoming, incoming], axis=0), 1, 0)
-        v = mm(b_wide, jnp.concatenate([outgoing, outgoing], axis=0), 1, 0)
-        scale = spread(w, pick)
-        wx = scale * x_ref[:, place].astype(F32)
-        eg = spread(grow, pick) * g_ref[:, place].astype(F32)
-        for q in range(step // piece) if step >= piece else (0,):
-            if step >= piece:
-                at = k * step + q * piece
-                inner = slice(q * piece, (q + 1) * piece)
-                term = gxs[at // piece][...]
-            else:
-                at, inner = k * step, slice(0, step)
-                term = gxs[at // piece][:, at % piece : at % piece + step]
-            total = term + scale[:, inner] * v[:, inner]
-            grad_ref[:, at : at + total.shape[1]] = total.astype(BF)
-        wv_ref[:, place], wv_ref[:, late] = halves(wx * v)
-        eu_ref[:, place], eu_ref[:, late] = halves(eg * u)
-        db = db + mm(
-            jnp.concatenate([outgoing, outgoing], axis=1), jnp.concatenate(halves(wx), axis=1), 1, 1
-        )
-        dc = dc + mm(
-            jnp.concatenate([incoming, incoming], axis=1), jnp.concatenate(halves(eg), axis=1), 1, 1
-        )
-        io_ref[:, place] = jnp.sum(incoming.astype(F32) * outgoing.astype(F32), axis=0, keepdims=True)
-    pick = head_lanes(heads, width, size)
-    ddecay = jnp.sum(pick * io_ref[...], axis=1, keepdims=True)
-    pick = pick.astype(BF)
+    pick = head_lanes(heads, step, size).astype(BF)
+    incoming, outgoing = store_ref[0], store_ref[1]
+    u = mm(c_wide, jnp.concatenate([incoming, incoming], axis=0), 1, 0)
+    v = mm(b_wide, jnp.concatenate([outgoing, outgoing], axis=0), 1, 0)
+    scale = spread(w, pick)
+    wx = scale * x_ref[...].astype(F32)
+    eg = spread(grow, pick) * g_ref[...].astype(F32)
+    grad_ref = rest[-5] if k == chunks - 1 else rest[-4]
+    for q in range(parts):
+        place = slice(q * piece, (q + 1) * piece)
+        grad_ref[:, place] = (gxs[q][...] + scale[:, place] * v[:, place]).astype(BF)
+    wv_ref[:, :step], wv_ref[:, step:] = halves(wx * v)
+    eu_ref[:, :step], eu_ref[:, step:] = halves(eg * u)
+    db = db + mm(
+        jnp.concatenate([outgoing, outgoing], axis=1), jnp.concatenate(halves(wx), axis=1), 1, 1
+    )
+    dc = dc + mm(
+        jnp.concatenate([incoming, incoming], axis=1), jnp.concatenate(halves(eg), axis=1), 1, 1
+    )
+    both = jnp.sum(incoming.astype(F32) * outgoing.astype(F32), axis=0, keepdims=True)
+    ddecay = jnp.sum(pick.astype(F32) * both, axis=1, keepdims=True)
     pick = jnp.concatenate([pick, pick], axis=1)
     wdw = mm(pick, wv_ref[...], 1, 1)
     egu = mm(pick, eu_ref[...], 1, 1)
@@ -282,10 +276,23 @@
     gate = 1.0 / (1.0 + jnp.exp(-pre))
     small = 1e-30
     ratio = jnp.where(dt > small, gate / jnp.maximum(dt, small), 1.0)
-    core = lax.axis_index("head")
-    keep_ref[0:rows, :] = jnp.where(core == 0, db, dc)
-    keep_ref[rows:, :] = (colsum + wdw) * ratio - rate * rev * gate
-    give_ref[...] = jnp.where(core == 0, dc, db)
+    graw = (colsum + wdw) * ratio - rate * rev * gate
+    if k > 0:
+        before_ref = rest[1]
+        db = db + before_ref[0:rows, :]
+        dc = dc + before_ref[rows : 2 * rows, :]
+        graw = jnp.concatenate([before_ref[2 * rows :, :], graw], axis=0)
+    if k == chunks - 1:
+        keep_ref, give_ref = rest[-4], rest[-3]
+        core = lax.axis_index("head")
+        keep_ref[0:rows, :] = jnp.where(core == 0, db, dc)
+        keep_ref[rows:, :] = graw
+        give_ref[...] = jnp.where(core == 0, dc, db)
+    else:
+        back_ref = rest[-3]
+        back_ref[0:rows, :] = db
+        back_ref[rows : 2 * rows, :] = dc
+        back_ref[2 * rows :, :] = graw
 
 
 def low_kernel(keep_ref, taken_ref, out_ref):
@@ -390,7 +397,7 @@
     count = lax.axis_size("seq")
     place = lax.axis_index("seq")
     chunks = len(first)
-    store = jnp.zeros((2, chunks + 1) + own.shape[2:], BF)
+    stores = [jnp.zeros((3,) + own.shape[2:], BF) for _ in range(chunks)]
     got = list(first)
     done, todo, extra = [], list(inner), []
     last = count + chunks - 2
@@ -433,13 +440,11 @@
             if new:
                 got[slot] = kept[-1]
         for hop, k in steps:
-            kind = jnp.where(place == hop, 0, 1)
-            fits = (place == hop) | (place == count - hop - 1)
-            at = jnp.where(fits, k, chunks)
-            zero = jnp.zeros_like(at)
-            store = lax.dynamic_update_slice(store, got[k][None, None], (kind, at, zero, zero))
+            kind = jnp.where(place == hop, 0, jnp.where(place == count - hop - 1, 1, 2))
+            zero = jnp.zeros_like(kind)
+            stores[k] = lax.dynamic_update_slice(stores[k], got[k][None], (kind, zero, zero))
     done += [make() for make in todo]
-    return store, done
+    return stores, done
 
 
 def body(tokens, ssd_input, grad_out, w_bc, w_dt, decay_rate, dt_bias):
@@ -482,7 +487,7 @@
         )
         + (struct((state_n, step), BF),) * CHUNKS
         + (struct((1, step), F32),) * CHUNKS,
-        1.0,
+        0.1,
         *proj,
         x,
         g,
@@ -522,44 +527,48 @@
     def beside(*others):
         for r in range(1, n_dp):
             weights.extend(cyclic(after(a, *others), "dp", r) for a in (w_bc, w_dt))
-        return weights[2:], []
+        if not ride or n_dp == 1:
+            return weights[2:], []
+        riders.extend(relay(found[1], groups[1], [(1, 1)], *others))
+        return weights[2:], riders[1:]
 
     def late(*others):
         if n_dp > 1:
             relay(found[1], groups[1], second, *others)
 
-    if ride and n_dp > 1:
-        spare += relay(found[1], groups[1], [(1, 1)])
     first[0] = after(first[0], *spare)
-    riders = [f[1, 1] for f in found] if ride else []
+    riders = [found[0][1, 1]] if ride else []
     calls = [functools.partial(inner, q) for q in range(PARTS)]
-    store, inners = chains(first, own, decay, calls, beside, riders, late)
+    stores, inners = chains(first, own, decay, calls, beside, riders, late)
     for f, a in zip(found, riders):
         f[0, 2] = a
-    done = [relay(f, a, [t for t in slots if t not in f], store) for f, a in zip(found, groups)]
-    grad_x, keep, give = call(
-        functools.partial(outer_kernel, size, PARTS),
-        (
-            struct((rows, width), BF),
-            struct((rows + heads, rows), F32),
-            struct((rows, rows), F32),
-        ),
-        5.4,
-        store,
-        x,
-        g,
-        bc,
-        hp,
-        rate,
-        *[a[0] for a in inners],
-        *[a[1] for a in inners],
-        *[a[2] for a in inners],
-        scratch=(
-            pltpu.VMEM((rows, 2 * width), BF),
-            pltpu.VMEM((rows, 2 * width), BF),
-            pltpu.VMEM((1, width), F32),
-        ),
-    )
+    done = [relay(f, a, [t for t in slots if t not in f], stores[-1]) for f, a in zip(found, groups)]
+    each = PARTS // CHUNKS
+    grad_x, back = None, []
+    for k in range(CHUNKS):
+        last = k == CHUNKS - 1
+        block = pl.BlockSpec((rows, step), lambda _, k=k: (0, k))
+        made = (k + 1) * (heads // CHUNKS)
+        sums = (struct((rows + heads, rows), F32), struct((rows, rows), F32))
+        inputs = [stores[k], x, g, bc, hp, rate]
+        for q in range(3):
+            inputs += [a[q] for a in inners[k * each : (k + 1) * each]]
+        specs = [VMEM, block, block] + [VMEM] * (len(inputs) - 3)
+        if k > 0:
+            inputs += [grad_x] + back
+            specs += [HBM, VMEM]
+        grad_x, *back = call(
+            functools.partial(outer_kernel, k, CHUNKS, size, each),
+            (struct((rows, width), BF),)
+            + (sums if last else (struct((2 * rows + made, rows), F32),)),
+            5.4 / CHUNKS,
+            *inputs,
+            scratch=(pltpu.VMEM((rows, 2 * step), BF), pltpu.VMEM((rows, 2 * step), BF)),
+            specs=specs,
+            out_specs=(block,) + (VMEM,) * (2 if last else 1),
+            aliases={len(inputs) - 2: 0} if k > 0 else {},
+        )
+    keep, give = back
     taken = after(cyclic(give, "head", 1), *[a for d in done for a in d])
     count = n_dp * n_seq
     copies = call(low_kernel, struct((count, rows + heads, rows), BF), 1.2, keep, taken)

time: 102 us -> 97.3 us (0.954)
  waiting for transfers between devices: 35.2 us -> 31.4 us
  starting transfers between devices: 45.2 us -> 43.1 us
    ppermute x6, starting transfers between devices: 24.8 us -> 15.2 us  [chains(): got[k] = lax.ppermute(value, 'seq', sorted(to.items()))]
    ppermute x8, starting transfers between devices: 9.09 us -> 16.4 us  [relay(): found[kind, hop] = lax.ppermute(source, 'seq', pairs[kind])]
    ppermute x8, waiting for transfers between devices: 2.86 us -> 9.75 us  [relay(): found[kind, hop] = lax.ppermute(source, 'seq', pairs[kind])]
    ppermute x6, waiting for transfers between devices: 15.6 us -> 10.1 us  [chains(): got[k] = lax.ppermute(value, 'seq', sorted(to.items()))]
    ppermute x9, waiting for transfers between devices: 11.6 us -> 6.42 us  [cyclic(): return lax.ppermute(a, axis, [(i, (i + by) % count) for i in range(count)])]
    unnamed x40 -> x42, local copies, waits for them, and re-layouts: 2.55 us -> 3.32 us
    pallas_call x12 -> x13, Pallas kernels: 15.8 us -> 16.4 us  [call(): pl.pallas_call(kernel, out_shape=out_shape, grid=(1,), in_specs=specs or...]
  transfers between devices with their start and end apart: 24 -> 24, of which waited for: 11 -> 15; matrix products, arithmetic and copies ran while one was open for 2% -> 2% of each run, Pallas kernels for 11% -> 12%
where the time goes in v12:
time: 97.3 us; the launch traced here: 96.7 us
  starting transfers between devices  43.1 us (44%)
  waiting for transfers between devices  31.4 us (32%)
  Pallas kernels  16.4 us (17%)
  local copies, waits for them, and re-layouts  4.42 us (5%)
    ppermute x8, starting transfers between devices, relay(): found[kind, hop] = lax.ppermute(source, 'seq', pairs[kind])  16.4 us
    pallas_call x13, Pallas kernels, call(): pl.pallas_call(kernel, out_shape=out_shape, grid=(1,), in_specs=specs or...  16.4 us
    ppermute x6, starting transfers between devices, chains(): got[k] = lax.ppermute(value, 'seq', sorted(to.items()))  15.2 us
    ppermute x6, waiting for transfers between devices, chains(): got[k] = lax.ppermute(value, 'seq', sorted(to.items()))  10.1 us
    ppermute x8, waiting for transfers between devices, relay(): found[kind, hop] = lax.ppermute(source, 'seq', pairs[kind])  9.75 us
    ppermute x9, starting transfers between devices, cyclic(): return lax.ppermute(a, axis, [(i, (i + by) % count) for i in range(count)])  6.66 us
    ppermute x9, waiting for transfers between devices, cyclic(): return lax.ppermute(a, axis, [(i, (i + by) % count) for i in range(count)])  6.42 us
    all_to_all x1, waiting for transfers between devices, body(): lows = lax.all_to_all(copies, ('seq', 'dp'), 0, 0, tiled=True)  5.13 us
  transfers between devices with their start and end apart: 24, of which 15 were waited for; matrix products, arithmetic and copies ran while one was open for 2% of the time, Pallas kernels for 12%

profile of v12, /device:TPU:0, one launch (start us, length us, event | category | flops | bytes accessed | tf_op | source)
XLA Modules:
  0.0 96.7 jit_solution(4747049115385396411)
XLA Ops:
  1.7 3.0 %collective-permute-start = (bf16[128,1024]{1,0:T(8,128)(2,1)S(1)}, bf16[128,1024]{1,0:T(8,128)(2,1)S(1)}, u32[]{:S(2)}, u32[]{:S(2)}) collective-permute-start(bf16[128,1024]{1,0:T(8,128)(2,1)S(1)} %get-tuple-element.55), channel_id=1, source_target_pairs={{0,2},{2,0},{1,3},{3,1},{4,6},{6,4},{5,7},{7,5},{8,10},{10,8},{9,1... | collective-permute-start | bytes 786440 | tf_op jit(solution)/shard_map/ppermute | solution.py:21
  5.4 4.4 %collective-permute-start.2 = (bf16[128,1024]{1,0:T(8,128)(2,1)S(1)}, bf16[128,1024]{1,0:T(8,128)(2,1)S(1)}, u32[]{:S(2)}, u32[]{:S(2)}) collective-permute-start(bf16[128,1024]{1,0:T(8,128)(2,1)S(1)} %get-tuple-element.54.a_ref.refs_0_), channel_id=1, source_target_pairs={{0,4},{4,0},{8,12},{12,8},{1,5},{5,1},{9,13},{13,9},{2,6},{6,2},{1... | collective-permute-start | bytes 786440 | tf_op jit(solution)/shard_map/ppermute | solution.py:392
  11.0 1.8 %collective-permute-start.4 = (bf16[128,1024]{1,0:T(8,128)(2,1)S(1)}, bf16[128,1024]{1,0:T(8,128)(2,1)S(1)}, u32[]{:S(2)}, u32[]{:S(2)}) collective-permute-start(bf16[128,1024]{1,0:T(8,128)(2,1)S(1)} %collective-permute-done.a_ref.refs_6_), channel_id=1, source_target_pairs={{0,4},{4,0},{8,12},{12,8},{1,5},{5,1},{9,13},{13,9},{2,6},{6,2},{1... | collective-permute-start | bytes 786440 | tf_op jit(solution)/shard_map/ppermute | solution.py:392
  13.2 1.6 %collective-permute-start.1 = (f32[320,128]{1,0:T(8,128)S(1)}, f32[320,128]{1,0:T(8,128)S(1)}, u32[]{:S(2)}, u32[]{:S(2)}) collective-permute-start(f32[320,128]{1,0:T(8,128)S(1)} %shard_map.104), channel_id=1, source_target_pairs={{0,2},{2,0},{1,3},{3,1},{4,6},{6,4},{5,7},{7,5},{8,10},{10,8},{9,1... | collective-permute-start | bytes 491528 | tf_op jit(solution)/shard_map/ppermute | solution.py:21
  14.7 2.3 %collective-permute-done.2.refs_1_ = bf16[128,1024]{1,0:T(8,128)(2,1)S(1)} collective-permute-done((bf16[128,1024]{1,0:T(8,128)(2,1)S(1)}, bf16[128,1024]{1,0:T(8,128)(2,1)S(1)}, u32[]{:S(2)}, u32[]{:S(2)}) %collective-permute-start.2) | collective-permute-done | bytes 262176 | tf_op jit(solution)/shard_map/ppermute | solution.py:392
  18.6 2.7 %collective-permute-done.4.refs_7_ = bf16[128,1024]{1,0:T(8,128)(2,1)S(1)} collective-permute-done((bf16[128,1024]{1,0:T(8,128)(2,1)S(1)}, bf16[128,1024]{1,0:T(8,128)(2,1)S(1)}, u32[]{:S(2)}, u32[]{:S(2)}) %collective-permute-start.4) | collective-permute-done | bytes 262176 | tf_op jit(solution)/shard_map/ppermute | solution.py:392
  23.3 2.1 %shard_map.105 = (f32[2,2,128,1024]{3,2,1,0:T(8,128)S(1)}, f32[256,128]{1,0:T(8,128)S(1)}, f32[160,128]{1,0:T(8,128)S(1)}, bf16[128,1024]{1,0:T(8,128)(2,1)S(1)}...) custom-call(f32[320,128]{1,0:T(8,128)S(1)} %shard_map.103.refs_0_, ...), custom_call_target="tpu_custom_call" | custom-call | flops 115000000 | bytes 1966336 | tf_op jit(solution)/shard_map/pallas_call | solution.py:54
  25.5 2.0 %collective-permute-start.8 = (bf16[128,1024]{1,0:T(8,128)(2,1)S(1)}, bf16[128,1024]{1,0:T(8,128)(2,1)S(1)}, u32[]{:S(2)}, u32[]{:S(2)}) collective-permute-start(bf16[128,1024]{1,0:T(8,128)(2,1)S(1)} %get-tuple-element.59), channel_id=1, source_target_pairs={{0,4},{4,0},{8,12},{12,8},{1,5},{5,1},{9,13},{13,9},{2,6},{6,2},{1... | collective-permute-start | bytes 786440 | tf_op jit(solution)/shard_map/ppermute | solution.py:419
  28.7 1.6 %collective-permute-start.14 = (bf16[1024,256]{1,0:T(8,128)(2,1)S(1)}, bf16[1024,256]{1,0:T(8,128)(2,1)S(1)}, u32[]{:S(2)}, u32[]{:S(2)}) collective-permute-start(bf16[1024,256]{1,0:T(8,128)(2,1)S(1)} %copy-done.6), channel_id=1, source_target_pairs={{0,2},{2,0},{1,3},{3,1},{4,6},{6,4},{5,7},{7,5},{8,10},{10,8},{9,1... | collective-permute-start | bytes 1572872 | tf_op jit(solution)/shard_map/ppermute | solution.py:21
  31.3 2.6 %collective-permute-done.8.refs_3_ = bf16[128,1024]{1,0:T(8,128)(2,1)S(1)} collective-permute-done((bf16[128,1024]{1,0:T(8,128)(2,1)S(1)}, bf16[128,1024]{1,0:T(8,128)(2,1)S(1)}, u32[]{:S(2)}, u32[]{:S(2)}) %collective-permute-start.8) | collective-permute-done | bytes 262176 | tf_op jit(solution)/shard_map/ppermute | solution.py:419
  34.8 6.1 %collective-permute-start.10 = (bf16[128,1024]{1,0:T(8,128)(2,1)S(1)}, bf16[128,1024]{1,0:T(8,128)(2,1)S(1)}, u32[]{:S(2)}, u32[]{:S(2)}) collective-permute-start(bf16[128,1024]{1,0:T(8,128)(2,1)S(1)} %broadcast_select_fusion), channel_id=1, source_target_pairs={{0,4},{4,0},{8,12},{12,8},{1,5},{5,1},{9,13},{13,9},{2,6},{6,2},{1... | collective-permute-start | bytes 786440 | tf_op jit(solution)/shard_map/ppermute | solution.py:419
  41.9 3.8 %collective-permute-done.10.refs_9_ = bf16[128,1024]{1,0:T(8,128)(2,1)S(1)} collective-permute-done((bf16[128,1024]{1,0:T(8,128)(2,1)S(1)}, bf16[128,1024]{1,0:T(8,128)(2,1)S(1)}, u32[]{:S(2)}, u32[]{:S(2)}) %collective-permute-start.10) | collective-permute-done | bytes 262176 | tf_op jit(solution)/shard_map/ppermute | solution.py:419
  46.0 1.8 %collective-permute-start.13 = (bf16[128,1024]{1,0:T(8,128)(2,1)S(1)}, bf16[128,1024]{1,0:T(8,128)(2,1)S(1)}, u32[]{:S(2)}, u32[]{:S(2)}) collective-permute-start(bf16[128,1024]{1,0:T(8,128)(2,1)S(1)} %get-tuple-element.104), channel_id=1, source_target_pairs={{0,4},{4,0},{8,12},{12,8},{1,5},{5,1},{9,13},{13,9},{2,6},{6,2},{1... | collective-permute-start | bytes 786440 | tf_op jit(solution)/shard_map/ppermute | solution.py:419
  49.6 2.9 %collective-permute-done.13 = bf16[128,1024]{1,0:T(8,128)(2,1)S(1)} collective-permute-done((bf16[128,1024]{1,0:T(8,128)(2,1)S(1)}, bf16[128,1024]{1,0:T(8,128)(2,1)S(1)}, u32[]{:S(2)}, u32[]{:S(2)}) %collective-permute-start.13) | collective-permute-done | bytes 262176 | tf_op jit(solution)/shard_map/ppermute | solution.py:419
  52.6 4.0 %collective-permute-start.16 = (bf16[128,1024]{1,0:T(8,128)(2,1)S(1)}, bf16[128,1024]{1,0:T(8,128)(2,1)S(1)}, u32[]{:S(2)}, u32[]{:S(2)}) collective-permute-start(bf16[128,1024]{1,0:T(8,128)(2,1)S(1)} %fusion), channel_id=1, source_target_pairs={{0,4},{4,0},{8,12},{12,8},{1,5},{5,1},{9,13},{13,9},{2,6},{6,2},{1... | collective-permute-start | bytes 786440 | tf_op jit(solution)/shard_map/ppermute | solution.py:419
  56.6 1.9 %shard_map.110 = (bf16[128,2048]{1,0:T(8,128)(2,1)}, f32[272,128]{1,0:T(8,128)S(1)}) custom-call(bf16[3,128,1024]{2,1,0:T(8,128)(2,1)S(1)} %bitcast_dynamic-update-slice_fusion.refs_0_, bf16[128,2048]{1,0:T(8,128)(2,1)S(1)} %bitcast.45, bf16[128,2048]{1,0:T(8,128)(2,1)S(1)} %bitcast.52, f32[256,128]{1,0:T(8,128)S(1)} %get-tuple-element.81.bc_ref.refs_3_, ...), custom_call_target="tpu_custom_call" | custom-call | flops 3104999936 | bytes 2719872 | tf_op jit(solution)/shard_map/pallas_call | solution.py:54
  60.9 6.8 %collective-permute-start.18 = (bf16[128,1024]{1,0:T(8,128)(2,1)}, bf16[128,1024]{1,0:T(8,128)(2,1)S(1)}, u32[]{:S(2)}, u32[]{:S(2)}) collective-permute-start(bf16[128,1024]{1,0:T(8,128)(2,1)} %collective-permute-done.7.refs_4_), channel_id=1, source_target_pairs={{0,4},{4,0},{8,12},{12,8},{1,5},{5,1},{9,13},{13,9},{2,6},{6,2},{1... | collective-permute-start | bytes 786440 | tf_op jit(solution)/shard_map/ppermute | solution.py:392
  67.7 1.7 %shard_map.111 = (bf16[128,2048]{1,0:T(8,128)(2,1)}, f32[160,128]{1,0:T(8,128)S(1)}, f32[128,128]{1,0:T(8,128)S(1)}) custom-call(bf16[3,128,1024]{2,1,0:T(8,128)(2,1)S(1)} %bitcast_dynamic-update-slice_fusion.3.refs_0_, bf16[128,2048]{1,0:T(8,128)(2,1)S(1)} %bitcast.47, bf16[128,2048]{1,0:T(8,128)(2,1)S(1)} %bitcast.54, ...), custom_call_target="tpu_custom_call", output_to_operand_aliasing={{0}: (12, {})} | custom-call | flops 3104999936 | bytes 3383424 | tf_op jit(solution)/shard_map/pallas_call | solution.py:54
  70.7 1.9 %collective-permute-done.18.refs_5_ = bf16[128,1024]{1,0:T(8,128)(2,1)S(1)} collective-permute-done((bf16[128,1024]{1,0:T(8,128)(2,1)}, bf16[128,1024]{1,0:T(8,128)(2,1)S(1)}, u32[]{:S(2)}, u32[]{:S(2)}) %collective-permute-start.18) | collective-permute-done | bytes 262176 | tf_op jit(solution)/shard_map/ppermute | solution.py:392
  72.6 2.8 %collective-permute-done.20.refs_11_ = bf16[128,1024]{1,0:T(8,128)(2,1)S(1)} collective-permute-done((bf16[128,1024]{1,0:T(8,128)(2,1)S(1)}, bf16[128,1024]{1,0:T(8,128)(2,1)S(1)}, u32[]{:S(2)}, u32[]{:S(2)}) %collective-permute-start.20) | collective-permute-done | bytes 262176 | tf_op jit(solution)/shard_map/ppermute | solution.py:392
  76.9 4.8 %all-to-all-start = ((bf16[8,160,128]{2,1,0:T(8,128)(2,1)}), bf16[8,160,128]{2,1,0:T(8,128)(2,1)S(1)}, u32[]{:S(2)}, u32[]{:S(2)}) async-start(bf16[8,160,128]{2,1,0:T(8,128)(2,1)} %shard_map.112), calls=%async_computation | async-start | bytes 655360 | tf_op jit(solution)/shard_map/all_to_all | solution.py:576
  85.3 5.1 %all-to-all-done.refs_12_ = bf16[8,160,128]{2,1,0:T(8,128)(2,1)S(1)} async-done(((bf16[8,160,128]{2,1,0:T(8,128)(2,1)}), bf16[8,160,128]{2,1,0:T(8,128)(2,1)S(1)}, u32[]{:S(2)}, u32[]{:S(2)}) %all-to-all-start) | async-done | bytes 327712 | tf_op jit(solution)/shard_map/all_to_all | solution.py:576
  90.4 1.6 %collective-permute-done.22.refs_13_ = bf16[8,160,128]{2,1,0:T(8,128)(2,1)S(1)} collective-permute-done((bf16[8,160,128]{2,1,0:T(8,128)(2,1)S(1)}, bf16[8,160,128]{2,1,0:T(8,128)(2,1)S(1)}, u32[]{:S(2)}, u32[]{:S(2)}) %collective-permute-start.22) | collective-permute-done | bytes 327712 | tf_op jit(solution)/shard_map/ppermute | solution.py:21
  92.8 4.0 %shard_map.114 = (f32[1024,256]{1,0:T(8,128)}, f32[64,1024]{1,0:T(8,128)}) custom-call(bf16[128,1024]{1,0:T(8,128)(2,1)} %copy-done.7, bf16[128,1024]{1,0:T(8,128)(2,1)} %copy-done.15, bf16[128,1024]{1,0:T(8,128)(2,1)} %copy-done.2, bf16[128,1024]{1,0:T(8,128)(2,1)} %copy-done.11, bf16[128,1024]{1,0:T(8,128)(2,1)} %collective-permute-done.7.refs_4_, ...), custom_call_target="tpu_custom_call" | custom-call | flops 4600000000 | bytes 3801088 | tf_op jit(solution)/shard_map/pallas_call | solution.py:54
  (91 shorter events, 22.5 us)
Async XLA Ops:
  1.7 9.3 %collective-permute-start = (bf16[128,1024]{1,0:T(8,128)(2,1)S(1)}, bf16[128,1024]{1,0:T(8,128)(2,1)S(1)}, u32[]{:S(2)}, u32[]{:S(2)}) collective-permute-start(bf16[128,1024]{1,0:T(8,128)(2,1)S(1)} %get-tuple-element.55), channel_id=1, source_target_pairs={{0,2},{2,0},{1,3},{3,1},{4,6},{6,4},{5,7},{7,5},{8,10},{10,8},{9,1... | collective-permute-start | bytes 786440 | tf_op jit(solution)/shard_map/ppermute | solution.py:21
  4.7 13.7 %collective-permute-start.3 = (bf16[128,1024]{1,0:T(8,128)(2,1)S(1)}, bf16[128,1024]{1,0:T(8,128)(2,1)S(1)}, u32[]{:S(2)}, u32[]{:S(2)}) collective-permute-start(bf16[128,1024]{1,0:T(8,128)(2,1)S(1)} %get-tuple-element.54.a_ref.refs_0_), channel_id=1, source_target_pairs={{0,0},{4,8},{8,4},{12,12},{1,1},{5,9},{9,5},{13,13},{2,2},{6,10},{... | collective-permute-start | bytes 786440 | tf_op jit(solution)/shard_map/ppermute | solution.py:392
  5.4 11.7 %collective-permute-start.2 = (bf16[128,1024]{1,0:T(8,128)(2,1)S(1)}, bf16[128,1024]{1,0:T(8,128)(2,1)S(1)}, u32[]{:S(2)}, u32[]{:S(2)}) collective-permute-start(bf16[128,1024]{1,0:T(8,128)(2,1)S(1)} %get-tuple-element.54.a_ref.refs_0_), channel_id=1, source_target_pairs={{0,4},{4,0},{8,12},{12,8},{1,5},{5,1},{9,13},{13,9},{2,6},{6,2},{1... | collective-permute-start | bytes 786440 | tf_op jit(solution)/shard_map/ppermute | solution.py:392
  11.0 10.2 %collective-permute-start.4 = (bf16[128,1024]{1,0:T(8,128)(2,1)S(1)}, bf16[128,1024]{1,0:T(8,128)(2,1)S(1)}, u32[]{:S(2)}, u32[]{:S(2)}) collective-permute-start(bf16[128,1024]{1,0:T(8,128)(2,1)S(1)} %collective-permute-done.a_ref.refs_6_), channel_id=1, source_target_pairs={{0,4},{4,0},{8,12},{12,8},{1,5},{5,1},{9,13},{13,9},{2,6},{6,2},{1... | collective-permute-start | bytes 786440 | tf_op jit(solution)/shard_map/ppermute | solution.py:392
  13.2 5.4 %collective-permute-start.1 = (f32[320,128]{1,0:T(8,128)S(1)}, f32[320,128]{1,0:T(8,128)S(1)}, u32[]{:S(2)}, u32[]{:S(2)}) collective-permute-start(f32[320,128]{1,0:T(8,128)S(1)} %shard_map.104), channel_id=1, source_target_pairs={{0,2},{2,0},{1,3},{3,1},{4,6},{6,4},{5,7},{7,5},{8,10},{10,8},{9,1... | collective-permute-start | bytes 491528 | tf_op jit(solution)/shard_map/ppermute | solution.py:21
  17.1 8.4 %collective-permute-start.7 = (bf16[128,1024]{1,0:T(8,128)(2,1)S(1)}, bf16[128,1024]{1,0:T(8,128)(2,1)}, u32[]{:S(2)}, u32[]{:S(2)}) collective-permute-start(bf16[128,1024]{1,0:T(8,128)(2,1)S(1)} %collective-permute-done.2.refs_1_), channel_id=1, source_target_pairs={{0,0},{4,8},{8,4},{12,12},{1,1},{5,9},{9,5},{13,13},{2,2},{6,10},{... | collective-permute-start | bytes 786440 | tf_op jit(solution)/shard_map/ppermute | solution.py:392
  18.4 3.5 %collective-permute-start.5 = (f32[320,128]{1,0:T(8,128)S(1)}, f32[320,128]{1,0:T(8,128)S(1)}, u32[]{:S(2)}, u32[]{:S(2)}) collective-permute-start(f32[320,128]{1,0:T(8,128)S(1)} %shard_map.103.refs_0_), channel_id=1, source_target_pairs={{0,1},{1,0},{2,3},{3,2},{4,5},{5,4},{6,7},{7,6},{8,9},{9,8},{10,11... | collective-permute-start | bytes 491528 | tf_op jit(solution)/shard_map/ppermute | solution.py:21
  21.9 1.4 %collective-permute-start.6 = (f32[320,128]{1,0:T(8,128)S(1)}, f32[320,128]{1,0:T(8,128)S(1)}, u32[]{:S(2)}, u32[]{:S(2)}) collective-permute-start(f32[320,128]{1,0:T(8,128)S(1)} %collective-permute-done.1.refs_1_), channel_id=1, source_target_pairs={{0,1},{1,0},{2,3},{3,2},{4,5},{5,4},{6,7},{7,6},{8,9},{9,8},{10,11... | collective-permute-start | bytes 491528 | tf_op jit(solution)/shard_map/ppermute | solution.py:21
  25.5 8.4 %collective-permute-start.8 = (bf16[128,1024]{1,0:T(8,128)(2,1)S(1)}, bf16[128,1024]{1,0:T(8,128)(2,1)S(1)}, u32[]{:S(2)}, u32[]{:S(2)}) collective-permute-start(bf16[128,1024]{1,0:T(8,128)(2,1)S(1)} %get-tuple-element.59), channel_id=1, source_target_pairs={{0,4},{4,0},{8,12},{12,8},{1,5},{5,1},{9,13},{13,9},{2,6},{6,2},{1... | collective-permute-start | bytes 786440 | tf_op jit(solution)/shard_map/ppermute | solution.py:419
  27.5 22.1 %collective-permute-start.15 = (bf16[64,1024]{1,0:T(8,128)(2,1)S(1)}, bf16[64,1024]{1,0:T(8,128)(2,1)S(1)}, u32[]{:S(2)}, u32[]{:S(2)}) collective-permute-start(bf16[64,1024]{1,0:T(8,128)(2,1)S(1)} %bitcast.66), channel_id=1, source_target_pairs={{0,2},{2,0},{1,3},{3,1},{4,6},{6,4},{5,7},{7,5},{8,10},{10,8},{9,1... | collective-permute-start | bytes 393224 | tf_op jit(solution)/shard_map/ppermute | solution.py:21
  28.0 3.3 %collective-permute-start.9 = (bf16[128,1024]{1,0:T(8,128)(2,1)S(1)}, bf16[128,1024]{1,0:T(8,128)(2,1)S(1)}, u32[]{:S(2)}, u32[]{:S(2)}) collective-permute-start(bf16[128,1024]{1,0:T(8,128)(2,1)S(1)} %collective-permute-done.a_ref.refs_6_), channel_id=1, source_target_pairs={{0,0},{4,8},{8,4},{12,12},{1,1},{5,9},{9,5},{13,13},{2,2},{6,10},{... | collective-permute-start | bytes 786440 | tf_op jit(solution)/shard_map/ppermute | solution.py:392
  28.7 20.9 %collective-permute-start.14 = (bf16[1024,256]{1,0:T(8,128)(2,1)S(1)}, bf16[1024,256]{1,0:T(8,128)(2,1)S(1)}, u32[]{:S(2)}, u32[]{:S(2)}) collective-permute-start(bf16[1024,256]{1,0:T(8,128)(2,1)S(1)} %copy-done.6), channel_id=1, source_target_pairs={{0,2},{2,0},{1,3},{3,1},{4,6},{6,4},{5,7},{7,5},{8,10},{10,8},{9,1... | collective-permute-start | bytes 1572872 | tf_op jit(solution)/shard_map/ppermute | solution.py:21
  34.1 7.9 %collective-permute-start.11 = (bf16[128,1024]{1,0:T(8,128)(2,1)S(1)}, bf16[128,1024]{1,0:T(8,128)(2,1)S(1)}, u32[]{:S(2)}, u32[]{:S(2)}) collective-permute-start(bf16[128,1024]{1,0:T(8,128)(2,1)S(1)} %fusion.3), channel_id=1, source_target_pairs={{0,0},{4,8},{8,4},{12,12},{1,1},{5,9},{9,5},{13,13},{2,2},{6,10},{... | collective-permute-start | bytes 786440 | tf_op jit(solution)/shard_map/ppermute | solution.py:419
  34.8 10.9 %collective-permute-start.10 = (bf16[128,1024]{1,0:T(8,128)(2,1)S(1)}, bf16[128,1024]{1,0:T(8,128)(2,1)S(1)}, u32[]{:S(2)}, u32[]{:S(2)}) collective-permute-start(bf16[128,1024]{1,0:T(8,128)(2,1)S(1)} %broadcast_select_fusion), channel_id=1, source_target_pairs={{0,4},{4,0},{8,12},{12,8},{1,5},{5,1},{9,13},{13,9},{2,6},{6,2},{1... | collective-permute-start | bytes 786440 | tf_op jit(solution)/shard_map/ppermute | solution.py:419
  46.0 6.4 %collective-permute-start.13 = (bf16[128,1024]{1,0:T(8,128)(2,1)S(1)}, bf16[128,1024]{1,0:T(8,128)(2,1)S(1)}, u32[]{:S(2)}, u32[]{:S(2)}) collective-permute-start(bf16[128,1024]{1,0:T(8,128)(2,1)S(1)} %get-tuple-element.104), channel_id=1, source_target_pairs={{0,4},{4,0},{8,12},{12,8},{1,5},{5,1},{9,13},{13,9},{2,6},{6,2},{1... | collective-permute-start | bytes 786440 | tf_op jit(solution)/shard_map/ppermute | solution.py:419
  47.8 4.6 %collective-permute-start.12 = (bf16[128,1024]{1,0:T(8,128)(2,1)S(1)}, bf16[128,1024]{1,0:T(8,128)(2,1)S(1)}, u32[]{:S(2)}, u32[]{:S(2)}) collective-permute-start(bf16[128,1024]{1,0:T(8,128)(2,1)S(1)} %get-tuple-element.105), channel_id=1, source_target_pairs={{0,0},{4,8},{8,4},{12,12},{1,1},{5,9},{9,5},{13,13},{2,2},{6,10},{... | collective-permute-start | bytes 786440 | tf_op jit(solution)/shard_map/ppermute | solution.py:419
  52.6 8.3 %collective-permute-start.16 = (bf16[128,1024]{1,0:T(8,128)(2,1)S(1)}, bf16[128,1024]{1,0:T(8,128)(2,1)S(1)}, u32[]{:S(2)}, u32[]{:S(2)}) collective-permute-start(bf16[128,1024]{1,0:T(8,128)(2,1)S(1)} %fusion), channel_id=1, source_target_pairs={{0,4},{4,0},{8,12},{12,8},{1,5},{5,1},{9,13},{13,9},{2,6},{6,2},{1... | collective-permute-start | bytes 786440 | tf_op jit(solution)/shard_map/ppermute | solution.py:419
  59.4 1.5 %collective-permute-start.19 = (bf16[128,1024]{1,0:T(8,128)(2,1)S(1)}, bf16[128,1024]{1,0:T(8,128)(2,1)S(1)}, u32[]{:S(2)}, u32[]{:S(2)}) collective-permute-start(bf16[128,1024]{1,0:T(8,128)(2,1)S(1)} %copy-done.17), channel_id=1, source_target_pairs={{0,0},{4,8},{8,4},{12,12},{1,1},{5,9},{9,5},{13,13},{2,2},{6,10},{... | collective-permute-start | bytes 786440 | tf_op jit(solution)/shard_map/ppermute | solution.py:392
  60.9 11.7 %collective-permute-start.18 = (bf16[128,1024]{1,0:T(8,128)(2,1)}, bf16[128,1024]{1,0:T(8,128)(2,1)S(1)}, u32[]{:S(2)}, u32[]{:S(2)}) collective-permute-start(bf16[128,1024]{1,0:T(8,128)(2,1)} %collective-permute-done.7.refs_4_), channel_id=1, source_target_pairs={{0,4},{4,0},{8,12},{12,8},{1,5},{5,1},{9,13},{13,9},{2,6},{6,2},{1... | collective-permute-start | bytes 786440 | tf_op jit(solution)/shard_map/ppermute | solution.py:392
  67.7 7.8 %collective-permute-start.20 = (bf16[128,1024]{1,0:T(8,128)(2,1)S(1)}, bf16[128,1024]{1,0:T(8,128)(2,1)S(1)}, u32[]{:S(2)}, u32[]{:S(2)}) collective-permute-start(bf16[128,1024]{1,0:T(8,128)(2,1)S(1)} %collective-permute-done.19.refs_10_), channel_id=1, source_target_pairs={{0,4},{4,0},{8,12},{12,8},{1,5},{5,1},{9,13},{13,9},{2,6},{6,2},{1... | collective-permute-start | bytes 786440 | tf_op jit(solution)/shard_map/ppermute | solution.py:392
  69.5 1.3 %collective-permute-start.17 = (f32[128,128]{1,0:T(8,128)S(1)}, f32[128,128]{1,0:T(8,128)S(1)}, u32[]{:S(2)}, u32[]{:S(2)}) collective-permute-start(f32[128,128]{1,0:T(8,128)S(1)} %get-tuple-element.96), channel_id=1, source_target_pairs={{0,1},{1,0},{2,3},{3,2},{4,5},{5,4},{6,7},{7,6},{8,9},{9,8},{10,11... | collective-permute-start | bytes 196616 | tf_op jit(solution)/shard_map/ppermute | solution.py:21
  76.9 13.5 %all-to-all-start = ((bf16[8,160,128]{2,1,0:T(8,128)(2,1)}), bf16[8,160,128]{2,1,0:T(8,128)(2,1)S(1)}, u32[]{:S(2)}, u32[]{:S(2)}) async-start(bf16[8,160,128]{2,1,0:T(8,128)(2,1)} %shard_map.112), calls=%async_computation | async-start | bytes 655360 | tf_op jit(solution)/shard_map/all_to_all | solution.py:576
  82.5 1.2 %collective-permute-start.21 = (bf16[160,128]{1,0:T(8,128)(2,1)S(1)}, bf16[160,128]{1,0:T(8,128)(2,1)S(1)}, u32[]{:S(2)}, u32[]{:S(2)}) collective-permute-start(bf16[160,128]{1,0:T(8,128)(2,1)S(1)} %slice_bitcast_fusion.mine_ref), channel_id=1, source_target_pairs={{0,1},{1,0},{2,3},{3,2},{4,5},{5,4},{6,7},{7,6},{8,9},{9,8},{10,11... | collective-permute-start | bytes 122888 | tf_op jit(solution)/shard_map/ppermute | solution.py:21
  90.4 1.6 %collective-permute-start.22 = (bf16[8,160,128]{2,1,0:T(8,128)(2,1)S(1)}, bf16[8,160,128]{2,1,0:T(8,128)(2,1)S(1)}, u32[]{:S(2)}, u32[]{:S(2)}) collective-permute-start(bf16[8,160,128]{2,1,0:T(8,128)(2,1)S(1)} %all-to-all-done.refs_12_), channel_id=1, source_target_pairs={{0,1},{1,0},{2,3},{3,2},{4,5},{5,4},{6,7},{7,6},{8,9},{9,8},{10,11... | collective-permute-start | bytes 983048 | tf_op jit(solution)/shard_map/ppermute | solution.py:21
  (21 other events, 156.5 us)

commit v13 on v12

--- a/solution.py
+++ b/solution.py
@@ -321,13 +321,11 @@
         out_ref[:, pl.ds(at, part)] = total.astype(BF)
 
 
-def weight_kernel(scale, n_dp, n_seq, slots, *refs):
-    count = 2 * len(slots) if n_dp > 1 else len(slots)
-    toks, lows = refs[:count], refs[count:-6]
-    bc_ref, dt_ref, tok_ref, low_ref, tok_sem, low_sem = refs[-6:]
+def order_kernel(n_dp, n_seq, slots, *refs):
+    out_ref, sem = refs[-2:]
+    toks = refs[:-2]
     rows = toks[0].shape[0]
-    share = lows[0].shape[1]
-    core, place, me = lax.axis_index("head"), lax.axis_index("seq"), lax.axis_index("dp")
+    place = lax.axis_index("seq")
     even = lax.rem(place, 2) == 0
     copies = []
     for r in range(n_dp):
@@ -339,29 +337,37 @@
                 fits = fits & jnp.where(above, place < n_seq - 1, place > 0)
             at = pl.multiple_of(jnp.clip(block, 0, n_seq - 1) * rows, 128)
             source = toks[k] if r == 0 else toks[len(slots) + k].at[pl.ds((r - 1) * rows, rows)]
-            copy = pltpu.make_async_copy(source, tok_ref.at[r, pl.ds(at, rows)], tok_sem.at[r, k])
+            copy = pltpu.make_async_copy(source, out_ref.at[r, pl.ds(at, rows)], sem.at[r, k])
             copies.append((fits, copy))
+    for fits, copy in copies:
+        pl.when(fits)(copy.start)
+    for fits, copy in copies:
+        pl.when(fits)(copy.wait)
+
+
+def weight_kernel(scale, n_dp, n_seq, tok_ref, *refs):
+    lows = refs[:2]
+    bc_ref, dt_ref, low_ref, low_sem = refs[2:]
+    rows = tok_ref.shape[1] // n_seq
+    share = lows[0].shape[1]
+    core, me = lax.axis_index("head"), lax.axis_index("dp")
+    copies = []
     for r in range(n_dp):
         for s in range(n_seq):
             index = s * n_dp + lax.rem(me - r + n_dp, n_dp)
             for k in range(2):
                 row = pl.multiple_of(lax.rem(core + k, 2) * share, 16)
-                copy = pltpu.make_async_copy(
-                    lows[k].at[index],
-                    low_ref.at[r, pl.ds(row, share), pl.ds(s * rows, rows)],
-                    low_sem.at[r * n_seq + s, k],
+                copies.append(
+                    pltpu.make_async_copy(
+                        lows[k].at[index],
+                        low_ref.at[r, pl.ds(row, share), pl.ds(s * rows, rows)],
+                        low_sem.at[r * n_seq + s, k],
+                    )
                 )
-                copies.append((None, copy))
-    for fits, copy in copies:
-        if fits is None:
-            copy.start()
-        else:
-            pl.when(fits)(copy.start)
-    for fits, copy in copies:
-        if fits is None:
-            copy.wait()
-        else:
-            pl.when(fits)(copy.wait)
+    for copy in copies:
+        copy.start()
+    for copy in copies:
+        copy.wait()
     total = mm(low_ref[0], tok_ref[0], 1, 0)
     for r in range(1, n_dp):
         total = total + mm(low_ref[r], tok_ref[r], 1, 0)
@@ -422,15 +428,14 @@
         for _ in range(-(-len(todo) // (last + 1 - slot))):
             done.append(todo.pop(0)(*sent))
         if slot == 1:
-            extra, soon = beside(*sent)
+            extra = beside(*sent)
         if slot == last:
-            late(*sent)
+            k = steps[-1][1]
+            got[k] = after(got[k], *late(*sent))
         if slot < last:
             held = [got[k] for _, k in steps] + [d[0] for d in done[-1:]]
             if slot == last - 1:
                 held += extra
-            if slot == 1:
-                held += soon
             new = slot < chunks
             if new:
                 held.append(got[slot])
@@ -477,7 +482,7 @@
         near += relay(found[1], groups[1], slots[: 1 if ride else 2])
     partials[1:] = [after(a, *near) for a in partials[1:]]
     proj = partials + [cyclic(a, "head", 1) for a in partials]
-    spare = relay(found[0], groups[0], second)
+    spare = relay(found[1], groups[1], [(1, 1)]) if ride and n_dp > 1 else []
     own, bc, hp, *outs = call(
         functools.partial(state_kernel, 2 * n_dp, size, int(ride)),
         (
@@ -527,17 +532,13 @@
     def beside(*others):
         for r in range(1, n_dp):
             weights.extend(cyclic(after(a, *others), "dp", r) for a in (w_bc, w_dt))
-        if not ride or n_dp == 1:
-            return weights[2:], []
-        riders.extend(relay(found[1], groups[1], [(1, 1)], *others))
-        return weights[2:], riders[1:]
+        return weights[2:] + relay(found[0], groups[0], second, *others)
 
     def late(*others):
-        if n_dp > 1:
-            relay(found[1], groups[1], second, *others)
+        return relay(found[1], groups[1], second, *others) if n_dp > 1 else []
 
     first[0] = after(first[0], *spare)
-    riders = [found[0][1, 1]] if ride else []
+    riders = [f[1, 1] for f in found] if ride else []
     calls = [functools.partial(inner, q) for q in range(PARTS)]
     stores, inners = chains(first, own, decay, calls, beside, riders, late)
     for f, a in zip(found, riders):
@@ -583,26 +584,30 @@
         other,
         *weights,
     )
-    lows = after(lows, grads)
-    swapped = cyclic(lows, "head", 1)
     toks = []
     for f, a in zip(found, groups):
         toks += [a] + [f[step] for step in slots]
     slots = [(0, 0)] + slots
+    ordered = call(
+        functools.partial(order_kernel, n_dp, n_seq, slots),
+        struct((n_dp, n_seq * rows, part), BF),
+        1.0,
+        *after(tuple(toks), copies),
+        scratch=[pltpu.SemaphoreType.DMA((n_dp, len(slots)))],
+    )
+    lows = after(lows, grads, ordered)
+    swapped = cyclic(lows, "head", 1)
     cols = 2 * (rows + heads)
     grad_bc, grad_dt = call(
-        functools.partial(weight_kernel, 1.0 / (rows * n_seq * n_dp), n_dp, n_seq, slots),
+        functools.partial(weight_kernel, 1.0 / (rows * n_seq * n_dp), n_dp, n_seq),
         (struct((part, 2 * state_n), F32), struct((2 * heads, part), F32)),
         4.0,
-        *toks,
+        ordered,
         lows,
         swapped,
-        specs=[HBM] * (len(toks) + 2),
-        limit=56 * 1024 * 1024,
+        limit=LIMIT + 2 * n_dp * n_seq * rows * cols,
         scratch=(
-            pltpu.VMEM((n_dp, n_seq * rows, part), BF),
             pltpu.VMEM((n_dp, cols, n_seq * rows), BF),
-            pltpu.SemaphoreType.DMA((n_dp, len(slots))),
             pltpu.SemaphoreType.DMA((count, 2)),
         ),
     )

time: 97.3 us -> 92 us (0.946)
  local copies, waits for them, and re-layouts: 4.42 us -> 12.8 us
  starting transfers between devices: 43.1 us -> 36.2 us
  waiting for transfers between devices: 31.4 us -> 25.7 us
  Pallas kernels: 16.4 us -> 15 us
    unnamed x42 -> x62, local copies, waits for them, and re-layouts: 3.32 us -> 11.7 us
    ppermute x8, starting transfers between devices: 16.4 us -> 10.2 us  [relay(): found[kind, hop] = lax.ppermute(source, 'seq', pairs[kind])]
    ppermute x8, waiting for transfers between devices: 9.75 us -> 4.16 us  [relay(): found[kind, hop] = lax.ppermute(source, 'seq', pairs[kind])]
    all_to_all x1, waiting for transfers between devices: 5.13 us -> 0.01 us  [body(): lows = lax.all_to_all(copies, ('seq', 'dp'), 0, 0, tiled=True)]
    ppermute x9, waiting for transfers between devices: 6.42 us -> 10.6 us  [cyclic(): return lax.ppermute(a, axis, [(i, (i + by) % count) for i in range(count)])]
    pallas_call x13 -> x14, Pallas kernels: 16.4 us -> 15 us  [call(): pl.pallas_call(kernel, out_shape=out_shape, grid=(1,), in_specs=specs or...]
    ppermute x6, starting transfers between devices: 15.2 us -> 13.9 us  [chains(): got[k] = lax.ppermute(value, 'seq', sorted(to.items()))]
  transfers between devices with their start and end apart: 24 -> 24, of which waited for: 15 -> 11; matrix products, arithmetic and copies ran while one was open for 2% -> 2% of each run, Pallas kernels for 12% -> 13%
where the time goes in v13:
time: 92 us; the launch traced here: 91.3 us
  starting transfers between devices  36.2 us (39%)
  waiting for transfers between devices  25.7 us (28%)
  Pallas kernels  15 us (16%)
  local copies, waits for them, and re-layouts  12.8 us (14%)
  between operations  1.03 us (1%)
    pallas_call x14, Pallas kernels, call(): pl.pallas_call(kernel, out_shape=out_shape, grid=(1,), in_specs=specs or...  15 us
    ppermute x6, starting transfers between devices, chains(): got[k] = lax.ppermute(value, 'seq', sorted(to.items()))  13.9 us
    unnamed x62, local copies, waits for them, and re-layouts  11.7 us
    ppermute x6, waiting for transfers between devices, chains(): got[k] = lax.ppermute(value, 'seq', sorted(to.items()))  10.9 us
    ppermute x9, waiting for transfers between devices, cyclic(): return lax.ppermute(a, axis, [(i, (i + by) % count) for i in range(count)])  10.6 us
    ppermute x8, starting transfers between devices, relay(): found[kind, hop] = lax.ppermute(source, 'seq', pairs[kind])  10.2 us
    ppermute x9, starting transfers between devices, cyclic(): return lax.ppermute(a, axis, [(i, (i + by) % count) for i in range(count)])  7.23 us
    all_to_all x1, starting transfers between devices, body(): lows = lax.all_to_all(copies, ('seq', 'dp'), 0, 0, tiled=True)  4.9 us
  transfers between devices with their start and end apart: 24, of which 11 were waited for; matrix products, arithmetic and copies ran while one was open for 2% of the time, Pallas kernels for 13%

profile of v13, /device:TPU:0, one launch (start us, length us, event | category | flops | bytes accessed | tf_op | source)
XLA Modules:
  0.0 91.3 jit_solution(3386413866365848807)
XLA Ops:
  1.7 3.0 %collective-permute-start = (bf16[128,1024]{1,0:T(8,128)(2,1)S(1)}, bf16[128,1024]{1,0:T(8,128)(2,1)S(1)}, u32[]{:S(2)}, u32[]{:S(2)}) collective-permute-start(bf16[128,1024]{1,0:T(8,128)(2,1)S(1)} %get-tuple-element.68), channel_id=1, source_target_pairs={{0,2},{2,0},{1,3},{3,1},{4,6},{6,4},{5,7},{7,5},{8,10},{10,8},{9,1... | collective-permute-start | bytes 786440 | tf_op jit(solution)/shard_map/ppermute | solution.py:21
  4.7 1.6 %collective-permute-start.2 = (bf16[128,1024]{1,0:T(8,128)(2,1)S(1)}, bf16[128,1024]{1,0:T(8,128)(2,1)S(1)}, u32[]{:S(2)}, u32[]{:S(2)}) collective-permute-start(bf16[128,1024]{1,0:T(8,128)(2,1)S(1)} %get-tuple-element.115.a_ref.refs_0_), channel_id=1, source_target_pairs={{0,4},{4,0},{8,12},{12,8},{1,5},{5,1},{9,13},{13,9},{2,6},{6,2},{1... | collective-permute-start | bytes 786440 | tf_op jit(solution)/shard_map/ppermute | solution.py:398
  7.4 3.7 %collective-permute-done.a_ref.refs_6_ = bf16[128,1024]{1,0:T(8,128)(2,1)S(1)} collective-permute-done((bf16[128,1024]{1,0:T(8,128)(2,1)S(1)}, bf16[128,1024]{1,0:T(8,128)(2,1)S(1)}, u32[]{:S(2)}, u32[]{:S(2)}) %collective-permute-start) | collective-permute-done | bytes 262176 | tf_op jit(solution)/shard_map/ppermute | solution.py:21
  11.0 1.8 %collective-permute-start.4 = (bf16[128,1024]{1,0:T(8,128)(2,1)S(1)}, bf16[128,1024]{1,0:T(8,128)(2,1)S(1)}, u32[]{:S(2)}, u32[]{:S(2)}) collective-permute-start(bf16[128,1024]{1,0:T(8,128)(2,1)S(1)} %collective-permute-done.a_ref.refs_6_), channel_id=1, source_target_pairs={{0,4},{4,0},{8,12},{12,8},{1,5},{5,1},{9,13},{13,9},{2,6},{6,2},{1... | collective-permute-start | bytes 786440 | tf_op jit(solution)/shard_map/ppermute | solution.py:398
  13.2 1.6 %collective-permute-start.1 = (f32[320,128]{1,0:T(8,128)S(1)}, f32[320,128]{1,0:T(8,128)S(1)}, u32[]{:S(2)}, u32[]{:S(2)}) collective-permute-start(f32[320,128]{1,0:T(8,128)S(1)} %shard_map.104), channel_id=1, source_target_pairs={{0,2},{2,0},{1,3},{3,1},{4,6},{6,4},{5,7},{7,5},{8,10},{10,8},{9,1... | collective-permute-start | bytes 491528 | tf_op jit(solution)/shard_map/ppermute | solution.py:21
  15.5 3.0 %collective-permute-done.1.refs_1_ = f32[320,128]{1,0:T(8,128)S(1)} collective-permute-done((f32[320,128]{1,0:T(8,128)S(1)}, f32[320,128]{1,0:T(8,128)S(1)}, u32[]{:S(2)}, u32[]{:S(2)}) %collective-permute-start.1) | collective-permute-done | bytes 163872 | tf_op jit(solution)/shard_map/ppermute | solution.py:21
  19.3 1.4 %collective-permute-done.6.refs_3_ = f32[320,128]{1,0:T(8,128)S(1)} collective-permute-done((f32[320,128]{1,0:T(8,128)S(1)}, f32[320,128]{1,0:T(8,128)S(1)}, u32[]{:S(2)}, u32[]{:S(2)}) %collective-permute-start.6) | collective-permute-done | bytes 163872 | tf_op jit(solution)/shard_map/ppermute | solution.py:21
  20.7 2.1 %shard_map.105 = (f32[2,2,128,1024]{3,2,1,0:T(8,128)S(1)}, f32[256,128]{1,0:T(8,128)S(1)}, f32[160,128]{1,0:T(8,128)S(1)}, bf16[128,1024]{1,0:T(8,128)(2,1)S(1)}...) custom-call(f32[320,128]{1,0:T(8,128)S(1)} %shard_map.103.refs_0_, ...), custom_call_target="tpu_custom_call" | custom-call | flops 115000000 | bytes 1966336 | tf_op jit(solution)/shard_map/pallas_call | solution.py:54
  22.8 1.8 %collective-permute-start.8 = (bf16[128,1024]{1,0:T(8,128)(2,1)S(1)}, bf16[128,1024]{1,0:T(8,128)(2,1)S(1)}, u32[]{:S(2)}, u32[]{:S(2)}) collective-permute-start(bf16[128,1024]{1,0:T(8,128)(2,1)S(1)} %get-tuple-element.72), channel_id=1, source_target_pairs={{0,4},{4,0},{8,12},{12,8},{1,5},{5,1},{9,13},{13,9},{2,6},{6,2},{1... | collective-permute-start | bytes 786440 | tf_op jit(solution)/shard_map/ppermute | solution.py:425
  25.3 1.3 %collective-permute-start.14 = (bf16[64,1024]{1,0:T(8,128)(2,1)S(1)}, bf16[64,1024]{1,0:T(8,128)(2,1)S(1)}, u32[]{:S(2)}, u32[]{:S(2)}) collective-permute-start(bf16[64,1024]{1,0:T(8,128)(2,1)S(1)} %bitcast.66), channel_id=1, source_target_pairs={{0,2},{2,0},{1,3},{3,1},{4,6},{6,4},{5,7},{7,5},{8,10},{10,8},{9,1... | collective-permute-start | bytes 393224 | tf_op jit(solution)/shard_map/ppermute | solution.py:21
  28.5 2.8 %collective-permute-done.8.refs_3_ = bf16[128,1024]{1,0:T(8,128)(2,1)S(1)} collective-permute-done((bf16[128,1024]{1,0:T(8,128)(2,1)S(1)}, bf16[128,1024]{1,0:T(8,128)(2,1)S(1)}, u32[]{:S(2)}, u32[]{:S(2)}) %collective-permute-start.8) | collective-permute-done | bytes 262176 | tf_op jit(solution)/shard_map/ppermute | solution.py:425
  32.1 4.5 %collective-permute-start.9 = (bf16[128,1024]{1,0:T(8,128)(2,1)S(1)}, bf16[128,1024]{1,0:T(8,128)(2,1)S(1)}, u32[]{:S(2)}, u32[]{:S(2)}) collective-permute-start(bf16[128,1024]{1,0:T(8,128)(2,1)S(1)} %broadcast_select_fusion), channel_id=1, source_target_pairs={{0,4},{4,0},{8,12},{12,8},{1,5},{5,1},{9,13},{13,9},{2,6},{6,2},{1... | collective-permute-start | bytes 786440 | tf_op jit(solution)/shard_map/ppermute | solution.py:425
  37.6 4.1 %collective-permute-done.9.refs_9_ = bf16[128,1024]{1,0:T(8,128)(2,1)S(1)} collective-permute-done((bf16[128,1024]{1,0:T(8,128)(2,1)S(1)}, bf16[128,1024]{1,0:T(8,128)(2,1)S(1)}, u32[]{:S(2)}, u32[]{:S(2)}) %collective-permute-start.9) | collective-permute-done | bytes 262176 | tf_op jit(solution)/shard_map/ppermute | solution.py:425
  42.7 3.9 %collective-permute-start.12 = (bf16[128,1024]{1,0:T(8,128)(2,1)S(1)}, bf16[128,1024]{1,0:T(8,128)(2,1)S(1)}, u32[]{:S(2)}, u32[]{:S(2)}) collective-permute-start(bf16[128,1024]{1,0:T(8,128)(2,1)S(1)} %get-tuple-element.130), channel_id=1, source_target_pairs={{0,4},{4,0},{8,12},{12,8},{1,5},{5,1},{9,13},{13,9},{2,6},{6,2},{1... | collective-permute-start | bytes 786440 | tf_op jit(solution)/shard_map/ppermute | solution.py:425
  47.8 3.2 %collective-permute-done.12 = bf16[128,1024]{1,0:T(8,128)(2,1)S(1)} collective-permute-done((bf16[128,1024]{1,0:T(8,128)(2,1)S(1)}, bf16[128,1024]{1,0:T(8,128)(2,1)S(1)}, u32[]{:S(2)}, u32[]{:S(2)}) %collective-permute-start.12) | collective-permute-done | bytes 262176 | tf_op jit(solution)/shard_map/ppermute | solution.py:425
  51.1 2.3 %collective-permute-start.16 = (bf16[128,1024]{1,0:T(8,128)(2,1)S(1)}, bf16[128,1024]{1,0:T(8,128)(2,1)S(1)}, u32[]{:S(2)}, u32[]{:S(2)}) collective-permute-start(bf16[128,1024]{1,0:T(8,128)(2,1)S(1)} %fusion), channel_id=1, source_target_pairs={{0,4},{4,0},{8,12},{12,8},{1,5},{5,1},{9,13},{13,9},{2,6},{6,2},{1... | collective-permute-start | bytes 786440 | tf_op jit(solution)/shard_map/ppermute | solution.py:425
  54.2 1.9 %shard_map.110 = (bf16[128,2048]{1,0:T(8,128)(2,1)}, f32[272,128]{1,0:T(8,128)S(1)}) custom-call(bf16[3,128,1024]{2,1,0:T(8,128)(2,1)S(1)} %bitcast_dynamic-update-slice_fusion.refs_0_, bf16[128,2048]{1,0:T(8,128)(2,1)S(1)} %bitcast.45, bf16[128,2048]{1,0:T(8,128)(2,1)S(1)} %bitcast.52, f32[256,128]{1,0:T(8,128)S(1)} %get-tuple-element.96.bc_ref.refs_3_, ...), custom_call_target="tpu_custom_call" | custom-call | flops 3104999936 | bytes 2719872 | tf_op jit(solution)/shard_map/pallas_call | solution.py:54
  57.8 4.0 %collective-permute-start.20 = (bf16[128,1024]{1,0:T(8,128)(2,1)S(1)}, bf16[128,1024]{1,0:T(8,128)(2,1)S(1)}, u32[]{:S(2)}, u32[]{:S(2)}) collective-permute-start(bf16[128,1024]{1,0:T(8,128)(2,1)S(1)} %collective-permute-done.17.refs_10_), channel_id=1, source_target_pairs={{0,4},{4,0},{8,12},{12,8},{1,5},{5,1},{9,13},{13,9},{2,6},{6,2},{1... | collective-permute-start | bytes 786440 | tf_op jit(solution)/shard_map/ppermute | solution.py:398
  61.9 1.7 %shard_map.111 = (bf16[128,2048]{1,0:T(8,128)(2,1)}, f32[160,128]{1,0:T(8,128)S(1)}, f32[128,128]{1,0:T(8,128)S(1)}) custom-call(bf16[3,128,1024]{2,1,0:T(8,128)(2,1)S(1)} %bitcast_dynamic-update-slice_fusion.3.refs_0_, bf16[128,2048]{1,0:T(8,128)(2,1)S(1)} %bitcast.47, bf16[128,2048]{1,0:T(8,128)(2,1)S(1)} %bitcast.54, ...), custom_call_target="tpu_custom_call", output_to_operand_aliasing={{0}: (12, {})} | custom-call | flops 3104999936 | bytes 3383424 | tf_op jit(solution)/shard_map/pallas_call | solution.py:54
  64.9 2.0 %collective-permute-done.20.refs_11_ = bf16[128,1024]{1,0:T(8,128)(2,1)S(1)} collective-permute-done((bf16[128,1024]{1,0:T(8,128)(2,1)S(1)}, bf16[128,1024]{1,0:T(8,128)(2,1)S(1)}, u32[]{:S(2)}, u32[]{:S(2)}) %collective-permute-start.20) | collective-permute-done | bytes 262176 | tf_op jit(solution)/shard_map/ppermute | solution.py:398
  67.6 2.1 %collective-permute-done.19.refs_5_ = bf16[128,1024]{1,0:T(8,128)(2,1)S(1)} collective-permute-done((bf16[128,1024]{1,0:T(8,128)(2,1)S(1)}, bf16[128,1024]{1,0:T(8,128)(2,1)S(1)}, u32[]{:S(2)}, u32[]{:S(2)}) %collective-permute-start.19) | collective-permute-done | bytes 262176 | tf_op jit(solution)/shard_map/ppermute | solution.py:398
  71.2 4.9 %all-to-all-start = ((bf16[8,160,128]{2,1,0:T(8,128)(2,1)}), bf16[8,160,128]{2,1,0:T(8,128)(2,1)S(1)}, u32[]{:S(2)}, u32[]{:S(2)}) async-start(bf16[8,160,128]{2,1,0:T(8,128)(2,1)} %shard_map.112), calls=%async_computation | async-start | bytes 655360 | tf_op jit(solution)/shard_map/all_to_all | solution.py:577
  85.8 1.5 %shard_map.113 = bf16[128,2048]{1,0:T(8,128)(2,1)} custom-call(bf16[160,128]{1,0:T(8,128)(2,1)S(1)} %slice_bitcast_fusion.mine_ref, bf16[160,128]{1,0:T(8,128)(2,1)S(1)} %collective-permute-done.21.other_ref, bf16[1024,256]{1,0:T(8,128)(2,1)S(1)} %copy-done.24, bf16[64,1024]{1,0:T(8,128)(2,1)S(1)} %bitcast.67, bf16[1024,256]{1,0:T(8,128)(2,1)S(1)} %copy-done.26, ...), custom_call_target="tpu_custom_call" | custom-call | flops 3335000064 | bytes 1392640 | tf_op jit(solution)/shard_map/pallas_call | solution.py:54
  89.1 2.2 %shard_map.115 = (f32[1024,256]{1,0:T(8,128)}, f32[64,1024]{1,0:T(8,128)}) custom-call(bf16[2,512,1024]{2,1,0:T(8,128)(2,1)S(1)} %shard_map.114.tok_ref, bf16[8,160,128]{2,1,0:T(8,128)(2,1)S(1)} %all-to-all-done.refs_0_, bf16[8,160,128]{2,1,0:T(8,128)(2,1)S(1)} %collective-permute-done.22.refs_1_), custom_call_target="tpu_custom_call" | custom-call | flops 4600000000 | bytes 2752512 | tf_op jit(solution)/shard_map/pallas_call | solution.py:54
  (113 shorter events, 27.6 us)
Async XLA Ops:
  1.7 9.3 %collective-permute-start = (bf16[128,1024]{1,0:T(8,128)(2,1)S(1)}, bf16[128,1024]{1,0:T(8,128)(2,1)S(1)}, u32[]{:S(2)}, u32[]{:S(2)}) collective-permute-start(bf16[128,1024]{1,0:T(8,128)(2,1)S(1)} %get-tuple-element.68), channel_id=1, source_target_pairs={{0,2},{2,0},{1,3},{3,1},{4,6},{6,4},{5,7},{7,5},{8,10},{10,8},{9,1... | collective-permute-start | bytes 786440 | tf_op jit(solution)/shard_map/ppermute | solution.py:21
  4.7 10.7 %collective-permute-start.2 = (bf16[128,1024]{1,0:T(8,128)(2,1)S(1)}, bf16[128,1024]{1,0:T(8,128)(2,1)S(1)}, u32[]{:S(2)}, u32[]{:S(2)}) collective-permute-start(bf16[128,1024]{1,0:T(8,128)(2,1)S(1)} %get-tuple-element.115.a_ref.refs_0_), channel_id=1, source_target_pairs={{0,4},{4,0},{8,12},{12,8},{1,5},{5,1},{9,13},{13,9},{2,6},{6,2},{1... | collective-permute-start | bytes 786440 | tf_op jit(solution)/shard_map/ppermute | solution.py:398
  6.3 9.2 %collective-permute-start.3 = (bf16[128,1024]{1,0:T(8,128)(2,1)S(1)}, bf16[128,1024]{1,0:T(8,128)(2,1)S(1)}, u32[]{:S(2)}, u32[]{:S(2)}) collective-permute-start(bf16[128,1024]{1,0:T(8,128)(2,1)S(1)} %get-tuple-element.115.a_ref.refs_0_), channel_id=1, source_target_pairs={{0,0},{4,8},{8,4},{12,12},{1,1},{5,9},{9,5},{13,13},{2,2},{6,10},{... | collective-permute-start | bytes 786440 | tf_op jit(solution)/shard_map/ppermute | solution.py:398
  11.0 7.5 %collective-permute-start.4 = (bf16[128,1024]{1,0:T(8,128)(2,1)S(1)}, bf16[128,1024]{1,0:T(8,128)(2,1)S(1)}, u32[]{:S(2)}, u32[]{:S(2)}) collective-permute-start(bf16[128,1024]{1,0:T(8,128)(2,1)S(1)} %collective-permute-done.a_ref.refs_6_), channel_id=1, source_target_pairs={{0,4},{4,0},{8,12},{12,8},{1,5},{5,1},{9,13},{13,9},{2,6},{6,2},{1... | collective-permute-start | bytes 786440 | tf_op jit(solution)/shard_map/ppermute | solution.py:398
  13.2 5.4 %collective-permute-start.1 = (f32[320,128]{1,0:T(8,128)S(1)}, f32[320,128]{1,0:T(8,128)S(1)}, u32[]{:S(2)}, u32[]{:S(2)}) collective-permute-start(f32[320,128]{1,0:T(8,128)S(1)} %shard_map.104), channel_id=1, source_target_pairs={{0,2},{2,0},{1,3},{3,1},{4,6},{6,4},{5,7},{7,5},{8,10},{10,8},{9,1... | collective-permute-start | bytes 491528 | tf_op jit(solution)/shard_map/ppermute | solution.py:21
  14.7 8.1 %collective-permute-start.7 = (bf16[128,1024]{1,0:T(8,128)(2,1)S(1)}, bf16[128,1024]{1,0:T(8,128)(2,1)S(1)}, u32[]{:S(2)}, u32[]{:S(2)}) collective-permute-start(bf16[128,1024]{1,0:T(8,128)(2,1)S(1)} %collective-permute-done.a_ref.refs_6_), channel_id=1, source_target_pairs={{0,0},{4,8},{8,4},{12,12},{1,1},{5,9},{9,5},{13,13},{2,2},{6,10},{... | collective-permute-start | bytes 786440 | tf_op jit(solution)/shard_map/ppermute | solution.py:398
  15.4 3.8 %collective-permute-start.5 = (f32[320,128]{1,0:T(8,128)S(1)}, f32[320,128]{1,0:T(8,128)S(1)}, u32[]{:S(2)}, u32[]{:S(2)}) collective-permute-start(f32[320,128]{1,0:T(8,128)S(1)} %shard_map.103.refs_0_), channel_id=1, source_target_pairs={{0,1},{1,0},{2,3},{3,2},{4,5},{5,4},{6,7},{7,6},{8,9},{9,8},{10,11... | collective-permute-start | bytes 491528 | tf_op jit(solution)/shard_map/ppermute | solution.py:21
  19.3 1.4 %collective-permute-start.6 = (f32[320,128]{1,0:T(8,128)S(1)}, f32[320,128]{1,0:T(8,128)S(1)}, u32[]{:S(2)}, u32[]{:S(2)}) collective-permute-start(f32[320,128]{1,0:T(8,128)S(1)} %collective-permute-done.1.refs_1_), channel_id=1, source_target_pairs={{0,1},{1,0},{2,3},{3,2},{4,5},{5,4},{6,7},{7,6},{8,9},{9,8},{10,11... | collective-permute-start | bytes 491528 | tf_op jit(solution)/shard_map/ppermute | solution.py:21
  22.8 8.4 %collective-permute-start.8 = (bf16[128,1024]{1,0:T(8,128)(2,1)S(1)}, bf16[128,1024]{1,0:T(8,128)(2,1)S(1)}, u32[]{:S(2)}, u32[]{:S(2)}) collective-permute-start(bf16[128,1024]{1,0:T(8,128)(2,1)S(1)} %get-tuple-element.72), channel_id=1, source_target_pairs={{0,4},{4,0},{8,12},{12,8},{1,5},{5,1},{9,13},{13,9},{2,6},{6,2},{1... | collective-permute-start | bytes 786440 | tf_op jit(solution)/shard_map/ppermute | solution.py:425
  24.6 23.1 %collective-permute-start.15 = (bf16[128,1024]{1,0:T(8,128)(2,1)S(1)}, bf16[128,1024]{1,0:T(8,128)(2,1)S(1)}, u32[]{:S(2)}, u32[]{:S(2)}) collective-permute-start(bf16[128,1024]{1,0:T(8,128)(2,1)S(1)} %collective-permute-done.2.refs_1_), channel_id=1, source_target_pairs={{0,0},{4,8},{8,4},{12,12},{1,1},{5,9},{9,5},{13,13},{2,2},{6,10},{... | collective-permute-start | bytes 786440 | tf_op jit(solution)/shard_map/ppermute | solution.py:398
  25.3 22.4 %collective-permute-start.14 = (bf16[64,1024]{1,0:T(8,128)(2,1)S(1)}, bf16[64,1024]{1,0:T(8,128)(2,1)S(1)}, u32[]{:S(2)}, u32[]{:S(2)}) collective-permute-start(bf16[64,1024]{1,0:T(8,128)(2,1)S(1)} %bitcast.66), channel_id=1, source_target_pairs={{0,2},{2,0},{1,3},{3,1},{4,6},{6,4},{5,7},{7,5},{8,10},{10,8},{9,1... | collective-permute-start | bytes 393224 | tf_op jit(solution)/shard_map/ppermute | solution.py:21
  26.6 21.1 %collective-permute-start.13 = (bf16[1024,256]{1,0:T(8,128)(2,1)}, bf16[1024,256]{1,0:T(8,128)(2,1)S(1)}, u32[]{:S(2)}, u32[]{:S(2)}) collective-permute-start(bf16[1024,256]{1,0:T(8,128)(2,1)} %refs_0_.1), channel_id=1, source_target_pairs={{0,2},{2,0},{1,3},{3,1},{4,6},{6,4},{5,7},{7,5},{8,10},{10,8},{9,1... | collective-permute-start | bytes 1572872 | tf_op jit(solution)/shard_map/ppermute | solution.py:21
  31.4 6.2 %collective-permute-start.10 = (bf16[128,1024]{1,0:T(8,128)(2,1)S(1)}, bf16[128,1024]{1,0:T(8,128)(2,1)S(1)}, u32[]{:S(2)}, u32[]{:S(2)}) collective-permute-start(bf16[128,1024]{1,0:T(8,128)(2,1)S(1)} %fusion.3), channel_id=1, source_target_pairs={{0,0},{4,8},{8,4},{12,12},{1,1},{5,9},{9,5},{13,13},{2,2},{6,10},{... | collective-permute-start | bytes 786440 | tf_op jit(solution)/shard_map/ppermute | solution.py:425
  32.1 9.6 %collective-permute-start.9 = (bf16[128,1024]{1,0:T(8,128)(2,1)S(1)}, bf16[128,1024]{1,0:T(8,128)(2,1)S(1)}, u32[]{:S(2)}, u32[]{:S(2)}) collective-permute-start(bf16[128,1024]{1,0:T(8,128)(2,1)S(1)} %broadcast_select_fusion), channel_id=1, source_target_pairs={{0,4},{4,0},{8,12},{12,8},{1,5},{5,1},{9,13},{13,9},{2,6},{6,2},{1... | collective-permute-start | bytes 786440 | tf_op jit(solution)/shard_map/ppermute | solution.py:425
  42.0 5.8 %collective-permute-start.11 = (bf16[128,1024]{1,0:T(8,128)(2,1)S(1)}, bf16[128,1024]{1,0:T(8,128)(2,1)S(1)}, u32[]{:S(2)}, u32[]{:S(2)}) collective-permute-start(bf16[128,1024]{1,0:T(8,128)(2,1)S(1)} %get-tuple-element.131), channel_id=1, source_target_pairs={{0,0},{4,8},{8,4},{12,12},{1,1},{5,9},{9,5},{13,13},{2,2},{6,10},{... | collective-permute-start | bytes 786440 | tf_op jit(solution)/shard_map/ppermute | solution.py:425
  42.7 8.3 %collective-permute-start.12 = (bf16[128,1024]{1,0:T(8,128)(2,1)S(1)}, bf16[128,1024]{1,0:T(8,128)(2,1)S(1)}, u32[]{:S(2)}, u32[]{:S(2)}) collective-permute-start(bf16[128,1024]{1,0:T(8,128)(2,1)S(1)} %get-tuple-element.130), channel_id=1, source_target_pairs={{0,4},{4,0},{8,12},{12,8},{1,5},{5,1},{9,13},{13,9},{2,6},{6,2},{1... | collective-permute-start | bytes 786440 | tf_op jit(solution)/shard_map/ppermute | solution.py:425
  51.1 6.7 %collective-permute-start.16 = (bf16[128,1024]{1,0:T(8,128)(2,1)S(1)}, bf16[128,1024]{1,0:T(8,128)(2,1)S(1)}, u32[]{:S(2)}, u32[]{:S(2)}) collective-permute-start(bf16[128,1024]{1,0:T(8,128)(2,1)S(1)} %fusion), channel_id=1, source_target_pairs={{0,4},{4,0},{8,12},{12,8},{1,5},{5,1},{9,13},{13,9},{2,6},{6,2},{1... | collective-permute-start | bytes 786440 | tf_op jit(solution)/shard_map/ppermute | solution.py:425
  53.4 3.6 %collective-permute-start.17 = (bf16[128,1024]{1,0:T(8,128)(2,1)S(1)}, bf16[128,1024]{1,0:T(8,128)(2,1)S(1)}, u32[]{:S(2)}, u32[]{:S(2)}) collective-permute-start(bf16[128,1024]{1,0:T(8,128)(2,1)S(1)} %copy-done.10), channel_id=1, source_target_pairs={{0,0},{4,8},{8,4},{12,12},{1,1},{5,9},{9,5},{13,13},{2,2},{6,10},{... | collective-permute-start | bytes 786440 | tf_op jit(solution)/shard_map/ppermute | solution.py:398
  57.8 9.1 %collective-permute-start.20 = (bf16[128,1024]{1,0:T(8,128)(2,1)S(1)}, bf16[128,1024]{1,0:T(8,128)(2,1)S(1)}, u32[]{:S(2)}, u32[]{:S(2)}) collective-permute-start(bf16[128,1024]{1,0:T(8,128)(2,1)S(1)} %collective-permute-done.17.refs_10_), channel_id=1, source_target_pairs={{0,4},{4,0},{8,12},{12,8},{1,5},{5,1},{9,13},{13,9},{2,6},{6,2},{1... | collective-permute-start | bytes 786440 | tf_op jit(solution)/shard_map/ppermute | solution.py:398
  61.8 7.9 %collective-permute-start.19 = (bf16[128,1024]{1,0:T(8,128)(2,1)S(1)}, bf16[128,1024]{1,0:T(8,128)(2,1)S(1)}, u32[]{:S(2)}, u32[]{:S(2)}) collective-permute-start(bf16[128,1024]{1,0:T(8,128)(2,1)S(1)} %collective-permute-done.15.refs_4_), channel_id=1, source_target_pairs={{0,4},{4,0},{8,12},{12,8},{1,5},{5,1},{9,13},{13,9},{2,6},{6,2},{1... | collective-permute-start | bytes 786440 | tf_op jit(solution)/shard_map/ppermute | solution.py:398
  63.6 1.3 %collective-permute-start.18 = (f32[128,128]{1,0:T(8,128)S(1)}, f32[128,128]{1,0:T(8,128)S(1)}, u32[]{:S(2)}, u32[]{:S(2)}) collective-permute-start(f32[128,128]{1,0:T(8,128)S(1)} %get-tuple-element.111), channel_id=1, source_target_pairs={{0,1},{1,0},{2,3},{3,2},{4,5},{5,4},{6,7},{7,6},{8,9},{9,8},{10,11... | collective-permute-start | bytes 196616 | tf_op jit(solution)/shard_map/ppermute | solution.py:21
  71.2 16.1 %all-to-all-start = ((bf16[8,160,128]{2,1,0:T(8,128)(2,1)}), bf16[8,160,128]{2,1,0:T(8,128)(2,1)S(1)}, u32[]{:S(2)}, u32[]{:S(2)}) async-start(bf16[8,160,128]{2,1,0:T(8,128)(2,1)} %shard_map.112), calls=%async_computation | async-start | bytes 655360 | tf_op jit(solution)/shard_map/all_to_all | solution.py:577
  76.9 8.0 %collective-permute-start.21 = (bf16[160,128]{1,0:T(8,128)(2,1)S(1)}, bf16[160,128]{1,0:T(8,128)(2,1)S(1)}, u32[]{:S(2)}, u32[]{:S(2)}) collective-permute-start(bf16[160,128]{1,0:T(8,128)(2,1)S(1)} %slice_bitcast_fusion.mine_ref), channel_id=1, source_target_pairs={{0,1},{1,0},{2,3},{3,2},{4,5},{5,4},{6,7},{7,6},{8,9},{9,8},{10,11... | collective-permute-start | bytes 122888 | tf_op jit(solution)/shard_map/ppermute | solution.py:21
  87.3 1.8 %collective-permute-start.22 = (bf16[8,160,128]{2,1,0:T(8,128)(2,1)S(1)}, bf16[8,160,128]{2,1,0:T(8,128)(2,1)S(1)}, u32[]{:S(2)}, u32[]{:S(2)}) collective-permute-start(bf16[8,160,128]{2,1,0:T(8,128)(2,1)S(1)} %all-to-all-done.refs_0_), channel_id=1, source_target_pairs={{0,1},{1,0},{2,3},{3,2},{4,5},{5,4},{6,7},{7,6},{8,9},{9,8},{10,11... | collective-permute-start | bytes 983048 | tf_op jit(solution)/shard_map/ppermute | solution.py:21
  (31 other events, 151.6 us)

commit v14 on v13

--- a/solution.py
+++ b/solution.py
@@ -98,18 +98,25 @@
     a = a_ref[...]
     state_n = bc_ref.shape[1] // 2
     rows = a.shape[0]
-    bc = mm(a, bc_ref[...], 1, 0)
+    heads = dt_ref.shape[0]
+    bc = mm(a, bc_ref[...], 1, 0).astype(out_ref.dtype)
+    raw = mm(dt_ref[...], a, 1, 1)
     out_ref[0:rows, :] = bc[:, :state_n]
     out_ref[rows : 2 * rows, :] = bc[:, state_n:]
-    out_ref[2 * rows :, :] = mm(dt_ref[...], a, 1, 1)
-
-
-def project(a, w_bc, w_dt):
+    if out_ref.dtype == BF:
+        high, low = halves(raw)
+        out_ref[2 * rows : 2 * rows + heads, :] = high
+        out_ref[2 * rows + heads :, :] = low
+    else:
+        out_ref[2 * rows :, :] = raw
+
+
+def project(a, w_bc, w_dt, dtype):
     rows = a.shape[0]
-    total = 2 * rows + w_dt.shape[0]
+    total = 2 * rows + w_dt.shape[0] * (2 if dtype == BF else 1)
     return call(
         project_kernel,
-        struct((total, w_bc.shape[1] // 2), F32),
+        struct((total, w_bc.shape[1] // 2), dtype),
         2.1,
         a,
         w_bc,
@@ -128,12 +135,15 @@
     rows = x_ref.shape[0]
     rate, bias = rate_ref[...].T, bias_ref[...].T
     chunks, step = own_ref.shape[1], own_ref.shape[3]
-    first = pl.multiple_of(2 * rows + lax.axis_index("head") * heads, 8)
+    first = pl.multiple_of(2 * rows + lax.axis_index("head") * heads, 16)
     bc = proj[0][0 : 2 * rows, :]
     pre = proj[0][pl.ds(first, heads), :] + bias
     for ref in proj[1:]:
-        bc = bc + ref[0 : 2 * rows, :]
-        pre = pre + ref[pl.ds(first, heads), :]
+        bc = bc + ref[0 : 2 * rows, :].astype(F32)
+        pre = pre + ref[pl.ds(first, heads), :].astype(F32)
+        if ref.dtype == BF:
+            low = pl.multiple_of(first + (ref.shape[0] - 2 * rows) // 2, 16)
+            pre = pre + ref[pl.ds(low, heads), :].astype(F32)
     bc_ref[...] = bc
     dt = jnp.maximum(pre, 0.0) + jnp.log1p(jnp.exp(-jnp.abs(pre)))
     row = lax.broadcasted_iota(jnp.int32, (rows, rows), 0)
@@ -474,10 +484,10 @@
     ride = n_seq == 4 and all(a.shape == (state_n, step) for a in groups)
     second = [(kind, hop) for kind, hop in slots if hop == 2 and not (ride and kind == 0)]
     near = relay(found[0], groups[0], slots[:2])
-    partials = [project(items[0], w_bc, w_dt)]
+    partials = [project(items[0], w_bc, w_dt, F32)]
     for r in range(1, n_dp):
         item = after(items[r], partials[0])
-        partials.append(cyclic(project(item, w_bc, w_dt), "dp", -r))
+        partials.append(cyclic(project(item, w_bc, w_dt, BF), "dp", -r))
     if n_dp > 1:
         near += relay(found[1], groups[1], slots[: 1 if ride else 2])
     partials[1:] = [after(a, *near) for a in partials[1:]]
@@ -543,7 +553,6 @@
     stores, inners = chains(first, own, decay, calls, beside, riders, late)
     for f, a in zip(found, riders):
         f[0, 2] = a
-    done = [relay(f, a, [t for t in slots if t not in f], stores[-1]) for f, a in zip(found, groups)]
     each = PARTS // CHUNKS
     grad_x, back = None, []
     for k in range(CHUNKS):
@@ -570,10 +579,12 @@
             aliases={len(inputs) - 2: 0} if k > 0 else {},
         )
     keep, give = back
-    taken = after(cyclic(give, "head", 1), *[a for d in done for a in d])
+    taken = cyclic(give, "head", 1)
     count = n_dp * n_seq
     copies = call(low_kernel, struct((count, rows + heads, rows), BF), 1.2, keep, taken)
     mine = copies[0]
+    for f, a in zip(found, groups):
+        relay(f, a, [t for t in slots if t not in f], copies)
     lows = lax.all_to_all(copies, ("seq", "dp"), 0, 0, tiled=True)
     other = cyclic(mine, "head", 1)
     grads = call(

time: 92 us -> 95.2 us (1.035)
  local copies, waits for them, and re-layouts: 12.8 us -> 2.96 us
  waiting for transfers between devices: 25.7 us -> 33 us
  Pallas kernels: 15 us -> 18.1 us
  starting transfers between devices: 36.2 us -> 38.8 us
    unnamed x62 -> x54, local copies, waits for them, and re-layouts: 11.7 us -> 1.86 us
    ppermute x8, waiting for transfers between devices: 4.16 us -> 13.7 us  [relay(): found[kind, hop] = lax.ppermute(source, 'seq', pairs[kind])]
    ppermute x8, starting transfers between devices: 10.2 us -> 13.8 us  [relay(): found[kind, hop] = lax.ppermute(source, 'seq', pairs[kind])]
    ppermute x6, starting transfers between devices: 13.9 us -> 10.4 us  [chains(): got[k] = lax.ppermute(value, 'seq', sorted(to.items()))]
    ppermute x9, waiting for transfers between devices: 10.6 us -> 7.28 us  [cyclic(): return lax.ppermute(a, axis, [(i, (i + by) % count) for i in range(count)])]
    pallas_call x14, Pallas kernels: 15 us -> 18.1 us  [call(): pl.pallas_call(kernel, out_shape=out_shape, grid=(1,), in_specs=specs or...]
    all_to_all x1, starting transfers between devices: 4.9 us -> 7.82 us  [body(): lows = lax.all_to_all(copies, ('seq', 'dp'), 0, 0, tiled=True)]
    ppermute x6, waiting for transfers between devices: 10.9 us -> 12 us  [chains(): got[k] = lax.ppermute(value, 'seq', sorted(to.items()))]
  transfers between devices with their start and end apart: 24 -> 24, of which waited for: 11 -> 10; matrix products, arithmetic and copies ran while one was open for 2% -> 2% of each run, Pallas kernels for 13% -> 14%
where the time goes in v14:
time: 95.2 us; the launch traced here: 94.6 us
  starting transfers between devices  38.8 us (41%)
  waiting for transfers between devices  33 us (35%)
  Pallas kernels  18.1 us (19%)
  local copies, waits for them, and re-layouts  2.96 us (3%)
  between operations  1.12 us (1%)
    pallas_call x14, Pallas kernels, call(): pl.pallas_call(kernel, out_shape=out_shape, grid=(1,), in_specs=specs or...  18.1 us
    ppermute x8, starting transfers between devices, relay(): found[kind, hop] = lax.ppermute(source, 'seq', pairs[kind])  13.8 us
    ppermute x8, waiting for transfers between devices, relay(): found[kind, hop] = lax.ppermute(source, 'seq', pairs[kind])  13.7 us
    ppermute x6, waiting for transfers between devices, chains(): got[k] = lax.ppermute(value, 'seq', sorted(to.items()))  12 us
    ppermute x6, starting transfers between devices, chains(): got[k] = lax.ppermute(value, 'seq', sorted(to.items()))  10.4 us
    all_to_all x1, starting transfers between devices, body(): lows = lax.all_to_all(copies, ('seq', 'dp'), 0, 0, tiled=True)  7.82 us
    ppermute x9, waiting for transfers between devices, cyclic(): return lax.ppermute(a, axis, [(i, (i + by) % count) for i in range(count)])  7.28 us
    ppermute x9, starting transfers between devices, cyclic(): return lax.ppermute(a, axis, [(i, (i + by) % count) for i in range(count)])  6.8 us
  transfers between devices with their start and end apart: 24, of which 10 were waited for; matrix products, arithmetic and copies ran while one was open for 2% of the time, Pallas kernels for 14%

profile of v14, /device:TPU:0, one launch (start us, length us, event | category | flops | bytes accessed | tf_op | source)
XLA Modules:
  0.0 94.6 jit_solution(17301222232250458610)
XLA Ops:
  1.7 3.0 %collective-permute-start = (bf16[128,1024]{1,0:T(8,128)(2,1)S(1)}, bf16[128,1024]{1,0:T(8,128)(2,1)S(1)}, u32[]{:S(2)}, u32[]{:S(2)}) collective-permute-start(bf16[128,1024]{1,0:T(8,128)(2,1)S(1)} %get-tuple-element.67), channel_id=1, source_target_pairs={{0,2},{2,0},{1,3},{3,1},{4,6},{6,4},{5,7},{7,5},{8,10},{10,8},{9,1... | collective-permute-start | bytes 786440 | tf_op jit(solution)/shard_map/ppermute | solution.py:21
  5.4 4.4 %collective-permute-start.2 = (bf16[128,1024]{1,0:T(8,128)(2,1)S(1)}, bf16[128,1024]{1,0:T(8,128)(2,1)S(1)}, u32[]{:S(2)}, u32[]{:S(2)}) collective-permute-start(bf16[128,1024]{1,0:T(8,128)(2,1)S(1)} %get-tuple-element.113.a_ref.refs_0_), channel_id=1, source_target_pairs={{0,4},{4,0},{8,12},{12,8},{1,5},{5,1},{9,13},{13,9},{2,6},{6,2},{1... | collective-permute-start | bytes 786440 | tf_op jit(solution)/shard_map/ppermute | solution.py:408
  9.9 1.3 %shard_map.103.refs_0_ = f32[320,128]{1,0:T(8,128)S(1)} custom-call(bf16[128,1024]{1,0:T(8,128)(2,1)S(1)} %get-tuple-element.113.a_ref.refs_0_, bf16[1024,256]{1,0:T(8,128)(2,1)} %refs_0_.1, bf16[64,1024]{1,0:T(8,128)(2,1)S(1)} %bitcast.64), custom_call_target="tpu_custom_call" | custom-call | flops 2415000064 | bytes 917504 | tf_op jit(solution)/shard_map/pallas_call | solution.py:54
  12.1 4.3 %collective-permute-start.4 = (bf16[128,1024]{1,0:T(8,128)(2,1)S(1)}, bf16[128,1024]{1,0:T(8,128)(2,1)S(1)}, u32[]{:S(2)}, u32[]{:S(2)}) collective-permute-start(bf16[128,1024]{1,0:T(8,128)(2,1)S(1)} %collective-permute-done.a_ref.refs_6_), channel_id=1, source_target_pairs={{0,4},{4,0},{8,12},{12,8},{1,5},{5,1},{9,13},{13,9},{2,6},{6,2},{1... | collective-permute-start | bytes 786440 | tf_op jit(solution)/shard_map/ppermute | solution.py:408
  16.4 1.3 %shard_map.104 = bf16[384,128]{1,0:T(8,128)(2,1)S(1)} custom-call(bf16[128,1024]{1,0:T(8,128)(2,1)S(1)} %collective-permute-done.a_ref.refs_6_, bf16[1024,256]{1,0:T(8,128)(2,1)} %refs_0_.1, bf16[64,1024]{1,0:T(8,128)(2,1)S(1)} %bitcast.65), custom_call_target="tpu_custom_call" | custom-call | flops 2415000064 | bytes 917504 | tf_op jit(solution)/shard_map/pallas_call | solution.py:54
  17.8 1.6 %collective-permute-start.1 = (bf16[384,128]{1,0:T(8,128)(2,1)S(1)}, bf16[384,128]{1,0:T(8,128)(2,1)S(1)}, u32[]{:S(2)}, u32[]{:S(2)}) collective-permute-start(bf16[384,128]{1,0:T(8,128)(2,1)S(1)} %shard_map.104), channel_id=1, source_target_pairs={{0,2},{2,0},{1,3},{3,1},{4,6},{6,4},{5,7},{7,5},{8,10},{10,8},{9,1... | collective-permute-start | bytes 294920 | tf_op jit(solution)/shard_map/ppermute | solution.py:21
  19.3 3.1 %collective-permute-done.1.refs_1_ = bf16[384,128]{1,0:T(8,128)(2,1)S(1)} collective-permute-done((bf16[384,128]{1,0:T(8,128)(2,1)S(1)}, bf16[384,128]{1,0:T(8,128)(2,1)S(1)}, u32[]{:S(2)}, u32[]{:S(2)}) %collective-permute-start.1) | collective-permute-done | bytes 98336 | tf_op jit(solution)/shard_map/ppermute | solution.py:21
  24.5 2.1 %shard_map.105 = (f32[2,2,128,1024]{3,2,1,0:T(8,128)S(1)}, f32[256,128]{1,0:T(8,128)S(1)}, f32[160,128]{1,0:T(8,128)S(1)}, bf16[128,1024]{1,0:T(8,128)(2,1)S(1)}...) custom-call(f32[320,128]{1,0:T(8,128)S(1)} %shard_map.103.refs_0_, ...), custom_call_target="tpu_custom_call" | custom-call | flops 115000000 | bytes 1835264 | tf_op jit(solution)/shard_map/pallas_call | solution.py:54
  27.6 1.5 %collective-permute-start.14 = (bf16[64,1024]{1,0:T(8,128)(2,1)S(1)}, bf16[64,1024]{1,0:T(8,128)(2,1)S(1)}, u32[]{:S(2)}, u32[]{:S(2)}) collective-permute-start(bf16[64,1024]{1,0:T(8,128)(2,1)S(1)} %bitcast.66), channel_id=1, source_target_pairs={{0,2},{2,0},{1,3},{3,1},{4,6},{6,4},{5,7},{7,5},{8,10},{10,8},{9,1... | collective-permute-start | bytes 393224 | tf_op jit(solution)/shard_map/ppermute | solution.py:21
  31.4 3.7 %collective-permute-done.8.refs_3_ = bf16[128,1024]{1,0:T(8,128)(2,1)S(1)} collective-permute-done((bf16[128,1024]{1,0:T(8,128)(2,1)S(1)}, bf16[128,1024]{1,0:T(8,128)(2,1)S(1)}, u32[]{:S(2)}, u32[]{:S(2)}) %collective-permute-start.8) | collective-permute-done | bytes 262176 | tf_op jit(solution)/shard_map/ppermute | solution.py:435
  35.9 2.6 %collective-permute-start.9 = (bf16[128,1024]{1,0:T(8,128)(2,1)S(1)}, bf16[128,1024]{1,0:T(8,128)(2,1)S(1)}, u32[]{:S(2)}, u32[]{:S(2)}) collective-permute-start(bf16[128,1024]{1,0:T(8,128)(2,1)S(1)} %broadcast_select_fusion), channel_id=1, source_target_pairs={{0,4},{4,0},{8,12},{12,8},{1,5},{5,1},{9,13},{13,9},{2,6},{6,2},{1... | collective-permute-start | bytes 786440 | tf_op jit(solution)/shard_map/ppermute | solution.py:435
  39.6 4.5 %collective-permute-done.9.refs_9_ = bf16[128,1024]{1,0:T(8,128)(2,1)S(1)} collective-permute-done((bf16[128,1024]{1,0:T(8,128)(2,1)S(1)}, bf16[128,1024]{1,0:T(8,128)(2,1)S(1)}, u32[]{:S(2)}, u32[]{:S(2)}) %collective-permute-start.9) | collective-permute-done | bytes 262176 | tf_op jit(solution)/shard_map/ppermute | solution.py:435
  44.3 1.8 %collective-permute-start.12 = (bf16[128,1024]{1,0:T(8,128)(2,1)S(1)}, bf16[128,1024]{1,0:T(8,128)(2,1)S(1)}, u32[]{:S(2)}, u32[]{:S(2)}) collective-permute-start(bf16[128,1024]{1,0:T(8,128)(2,1)S(1)} %get-tuple-element.128), channel_id=1, source_target_pairs={{0,4},{4,0},{8,12},{12,8},{1,5},{5,1},{9,13},{13,9},{2,6},{6,2},{1... | collective-permute-start | bytes 786440 | tf_op jit(solution)/shard_map/ppermute | solution.py:435
  48.0 3.1 %collective-permute-done.12 = bf16[128,1024]{1,0:T(8,128)(2,1)S(1)} collective-permute-done((bf16[128,1024]{1,0:T(8,128)(2,1)S(1)}, bf16[128,1024]{1,0:T(8,128)(2,1)S(1)}, u32[]{:S(2)}, u32[]{:S(2)}) %collective-permute-start.12) | collective-permute-done | bytes 262176 | tf_op jit(solution)/shard_map/ppermute | solution.py:435
  51.1 3.7 %collective-permute-start.16 = (bf16[128,1024]{1,0:T(8,128)(2,1)S(1)}, bf16[128,1024]{1,0:T(8,128)(2,1)S(1)}, u32[]{:S(2)}, u32[]{:S(2)}) collective-permute-start(bf16[128,1024]{1,0:T(8,128)(2,1)S(1)} %fusion), channel_id=1, source_target_pairs={{0,4},{4,0},{8,12},{12,8},{1,5},{5,1},{9,13},{13,9},{2,6},{6,2},{1... | collective-permute-start | bytes 786440 | tf_op jit(solution)/shard_map/ppermute | solution.py:435
  55.6 1.9 %shard_map.110 = (bf16[128,2048]{1,0:T(8,128)(2,1)}, f32[272,128]{1,0:T(8,128)S(1)}) custom-call(bf16[3,128,1024]{2,1,0:T(8,128)(2,1)S(1)} %get-tuple-element.130.refs_0_, bf16[128,2048]{1,0:T(8,128)(2,1)S(1)} %bitcast.45, bf16[128,2048]{1,0:T(8,128)(2,1)S(1)} %bitcast.52, f32[256,128]{1,0:T(8,128)S(1)} %get-tuple-element.95.bc_ref.refs_3_, ...), custom_call_target="tpu_custom_call" | custom-call | flops 3104999936 | bytes 2719872 | tf_op jit(solution)/shard_map/pallas_call | solution.py:54
  59.3 1.7 %shard_map.111 = (bf16[128,2048]{1,0:T(8,128)(2,1)}, f32[160,128]{1,0:T(8,128)S(1)}, f32[128,128]{1,0:T(8,128)S(1)}) custom-call(bf16[3,128,1024]{2,1,0:T(8,128)(2,1)S(1)} %bitcast_dynamic-update-slice_fusion.3.refs_0_, bf16[128,2048]{1,0:T(8,128)(2,1)S(1)} %bitcast.47, bf16[128,2048]{1,0:T(8,128)(2,1)S(1)} %bitcast.54, ...), custom_call_target="tpu_custom_call", output_to_operand_aliasing={{0}: (12, {})} | custom-call | flops 3104999936 | bytes 3383424 | tf_op jit(solution)/shard_map/pallas_call | solution.py:54
  63.0 7.8 %all-to-all-start = ((bf16[8,160,128]{2,1,0:T(8,128)(2,1)}), bf16[8,160,128]{2,1,0:T(8,128)(2,1)S(1)}, u32[]{:S(2)}, u32[]{:S(2)}) async-start(bf16[8,160,128]{2,1,0:T(8,128)(2,1)} %shard_map.112), calls=%async_computation | async-start | bytes 655360 | tf_op jit(solution)/shard_map/all_to_all | solution.py:588
  71.8 2.1 %collective-permute-start.20 = (bf16[128,1024]{1,0:T(8,128)(2,1)S(1)}, bf16[128,1024]{1,0:T(8,128)(2,1)S(1)}, u32[]{:S(2)}, u32[]{:S(2)}) collective-permute-start(bf16[128,1024]{1,0:T(8,128)(2,1)S(1)} %copy-done.13), channel_id=1, source_target_pairs={{0,4},{4,0},{8,12},{12,8},{1,5},{5,1},{9,13},{13,9},{2,6},{6,2},{1... | collective-permute-start | bytes 786440 | tf_op jit(solution)/shard_map/ppermute | solution.py:408
  74.0 2.6 %shard_map.113 = bf16[128,2048]{1,0:T(8,128)(2,1)} custom-call(bf16[160,128]{1,0:T(8,128)(2,1)S(1)} %slice_bitcast_fusion.mine_ref, bf16[160,128]{1,0:T(8,128)(2,1)S(1)} %collective-permute-done.19.other_ref, bf16[1024,256]{1,0:T(8,128)(2,1)} %refs_0_.1, bf16[64,1024]{1,0:T(8,128)(2,1)S(1)} %bitcast.67, bf16[1024,256]{1,0:T(8,128)(2,1)S(1)} %copy-done.22, ...), custom_call_target="tpu_custom_call" | custom-call | flops 3335000064 | bytes 1392640 | tf_op jit(solution)/shard_map/pallas_call | solution.py:54
  76.6 8.5 %collective-permute-done.20.refs_5_ = bf16[128,1024]{1,0:T(8,128)(2,1)S(1)} collective-permute-done((bf16[128,1024]{1,0:T(8,128)(2,1)S(1)}, bf16[128,1024]{1,0:T(8,128)(2,1)S(1)}, u32[]{:S(2)}, u32[]{:S(2)}) %collective-permute-start.20) | collective-permute-done | bytes 262176 | tf_op jit(solution)/shard_map/ppermute | solution.py:408
  85.0 5.2 %collective-permute-done.21.refs_11_ = bf16[128,1024]{1,0:T(8,128)(2,1)S(1)} collective-permute-done((bf16[128,1024]{1,0:T(8,128)(2,1)S(1)}, bf16[128,1024]{1,0:T(8,128)(2,1)S(1)}, u32[]{:S(2)}, u32[]{:S(2)}) %collective-permute-start.21) | collective-permute-done | bytes 262176 | tf_op jit(solution)/shard_map/ppermute | solution.py:408
  90.7 1.6 %collective-permute-done.22.refs_1_ = bf16[8,160,128]{2,1,0:T(8,128)(2,1)S(1)} collective-permute-done((bf16[8,160,128]{2,1,0:T(8,128)(2,1)S(1)}, bf16[8,160,128]{2,1,0:T(8,128)(2,1)S(1)}, u32[]{:S(2)}, u32[]{:S(2)}) %collective-permute-start.22) | collective-permute-done | bytes 327712 | tf_op jit(solution)/shard_map/ppermute | solution.py:21
  92.3 2.2 %shard_map.115 = (f32[1024,256]{1,0:T(8,128)}, f32[64,1024]{1,0:T(8,128)}) custom-call(bf16[2,512,1024]{2,1,0:T(8,128)(2,1)S(1)} %shard_map.114.tok_ref, bf16[8,160,128]{2,1,0:T(8,128)(2,1)S(1)} %all-to-all-done.refs_0_, bf16[8,160,128]{2,1,0:T(8,128)(2,1)S(1)} %collective-permute-done.22.refs_1_), custom_call_target="tpu_custom_call" | custom-call | flops 4600000000 | bytes 2752512 | tf_op jit(solution)/shard_map/pallas_call | solution.py:54
  (104 shorter events, 17.6 us)
Async XLA Ops:
  1.7 9.5 %collective-permute-start = (bf16[128,1024]{1,0:T(8,128)(2,1)S(1)}, bf16[128,1024]{1,0:T(8,128)(2,1)S(1)}, u32[]{:S(2)}, u32[]{:S(2)}) collective-permute-start(bf16[128,1024]{1,0:T(8,128)(2,1)S(1)} %get-tuple-element.67), channel_id=1, source_target_pairs={{0,2},{2,0},{1,3},{3,1},{4,6},{6,4},{5,7},{7,5},{8,10},{10,8},{9,1... | collective-permute-start | bytes 786440 | tf_op jit(solution)/shard_map/ppermute | solution.py:21
  4.7 14.6 %collective-permute-start.3 = (bf16[128,1024]{1,0:T(8,128)(2,1)S(1)}, bf16[128,1024]{1,0:T(8,128)(2,1)S(1)}, u32[]{:S(2)}, u32[]{:S(2)}) collective-permute-start(bf16[128,1024]{1,0:T(8,128)(2,1)S(1)} %get-tuple-element.113.a_ref.refs_0_), channel_id=1, source_target_pairs={{0,0},{4,8},{8,4},{12,12},{1,1},{5,9},{9,5},{13,13},{2,2},{6,10},{... | collective-permute-start | bytes 786440 | tf_op jit(solution)/shard_map/ppermute | solution.py:408
  5.4 13.9 %collective-permute-start.2 = (bf16[128,1024]{1,0:T(8,128)(2,1)S(1)}, bf16[128,1024]{1,0:T(8,128)(2,1)S(1)}, u32[]{:S(2)}, u32[]{:S(2)}) collective-permute-start(bf16[128,1024]{1,0:T(8,128)(2,1)S(1)} %get-tuple-element.113.a_ref.refs_0_), channel_id=1, source_target_pairs={{0,4},{4,0},{8,12},{12,8},{1,5},{5,1},{9,13},{13,9},{2,6},{6,2},{1... | collective-permute-start | bytes 786440 | tf_op jit(solution)/shard_map/ppermute | solution.py:408
  11.3 15.4 %collective-permute-start.7 = (bf16[128,1024]{1,0:T(8,128)(2,1)S(1)}, bf16[128,1024]{1,0:T(8,128)(2,1)S(1)}, u32[]{:S(2)}, u32[]{:S(2)}) collective-permute-start(bf16[128,1024]{1,0:T(8,128)(2,1)S(1)} %collective-permute-done.a_ref.refs_6_), channel_id=1, source_target_pairs={{0,0},{4,8},{8,4},{12,12},{1,1},{5,9},{9,5},{13,13},{2,2},{6,10},{... | collective-permute-start | bytes 786440 | tf_op jit(solution)/shard_map/ppermute | solution.py:408
  12.1 10.4 %collective-permute-start.4 = (bf16[128,1024]{1,0:T(8,128)(2,1)S(1)}, bf16[128,1024]{1,0:T(8,128)(2,1)S(1)}, u32[]{:S(2)}, u32[]{:S(2)}) collective-permute-start(bf16[128,1024]{1,0:T(8,128)(2,1)S(1)} %collective-permute-done.a_ref.refs_6_), channel_id=1, source_target_pairs={{0,4},{4,0},{8,12},{12,8},{1,5},{5,1},{9,13},{13,9},{2,6},{6,2},{1... | collective-permute-start | bytes 786440 | tf_op jit(solution)/shard_map/ppermute | solution.py:408
  17.8 4.7 %collective-permute-start.1 = (bf16[384,128]{1,0:T(8,128)(2,1)S(1)}, bf16[384,128]{1,0:T(8,128)(2,1)S(1)}, u32[]{:S(2)}, u32[]{:S(2)}) collective-permute-start(bf16[384,128]{1,0:T(8,128)(2,1)S(1)} %shard_map.104), channel_id=1, source_target_pairs={{0,2},{2,0},{1,3},{3,1},{4,6},{6,4},{5,7},{7,5},{8,10},{10,8},{9,1... | collective-permute-start | bytes 294920 | tf_op jit(solution)/shard_map/ppermute | solution.py:21
  19.3 3.8 %collective-permute-start.5 = (f32[320,128]{1,0:T(8,128)S(1)}, f32[320,128]{1,0:T(8,128)S(1)}, u32[]{:S(2)}, u32[]{:S(2)}) collective-permute-start(f32[320,128]{1,0:T(8,128)S(1)} %shard_map.103.refs_0_), channel_id=1, source_target_pairs={{0,1},{1,0},{2,3},{3,2},{4,5},{5,4},{6,7},{7,6},{8,9},{9,8},{10,11... | collective-permute-start | bytes 491528 | tf_op jit(solution)/shard_map/ppermute | solution.py:21
  23.2 1.3 %collective-permute-start.6 = (bf16[384,128]{1,0:T(8,128)(2,1)S(1)}, bf16[384,128]{1,0:T(8,128)(2,1)S(1)}, u32[]{:S(2)}, u32[]{:S(2)}) collective-permute-start(bf16[384,128]{1,0:T(8,128)(2,1)S(1)} %collective-permute-done.1.refs_1_), channel_id=1, source_target_pairs={{0,1},{1,0},{2,3},{3,2},{4,5},{5,4},{6,7},{7,6},{8,9},{9,8},{10,11... | collective-permute-start | bytes 294920 | tf_op jit(solution)/shard_map/ppermute | solution.py:21
  26.7 8.4 %collective-permute-start.8 = (bf16[128,1024]{1,0:T(8,128)(2,1)S(1)}, bf16[128,1024]{1,0:T(8,128)(2,1)S(1)}, u32[]{:S(2)}, u32[]{:S(2)}) collective-permute-start(bf16[128,1024]{1,0:T(8,128)(2,1)S(1)} %get-tuple-element.71), channel_id=1, source_target_pairs={{0,4},{4,0},{8,12},{12,8},{1,5},{5,1},{9,13},{13,9},{2,6},{6,2},{1... | collective-permute-start | bytes 786440 | tf_op jit(solution)/shard_map/ppermute | solution.py:435
  27.6 20.3 %collective-permute-start.14 = (bf16[64,1024]{1,0:T(8,128)(2,1)S(1)}, bf16[64,1024]{1,0:T(8,128)(2,1)S(1)}, u32[]{:S(2)}, u32[]{:S(2)}) collective-permute-start(bf16[64,1024]{1,0:T(8,128)(2,1)S(1)} %bitcast.66), channel_id=1, source_target_pairs={{0,2},{2,0},{1,3},{3,1},{4,6},{6,4},{5,7},{7,5},{8,10},{10,8},{9,1... | collective-permute-start | bytes 393224 | tf_op jit(solution)/shard_map/ppermute | solution.py:21
  29.1 18.8 %collective-permute-start.15 = (bf16[128,1024]{1,0:T(8,128)(2,1)S(1)}, bf16[128,1024]{1,0:T(8,128)(2,1)S(1)}, u32[]{:S(2)}, u32[]{:S(2)}) collective-permute-start(bf16[128,1024]{1,0:T(8,128)(2,1)S(1)} %collective-permute-done.2.refs_1_), channel_id=1, source_target_pairs={{0,0},{4,8},{8,4},{12,12},{1,1},{5,9},{9,5},{13,13},{2,2},{6,10},{... | collective-permute-start | bytes 786440 | tf_op jit(solution)/shard_map/ppermute | solution.py:408
  29.7 18.2 %collective-permute-start.13 = (bf16[1024,256]{1,0:T(8,128)(2,1)}, bf16[1024,256]{1,0:T(8,128)(2,1)S(1)}, u32[]{:S(2)}, u32[]{:S(2)}) collective-permute-start(bf16[1024,256]{1,0:T(8,128)(2,1)} %refs_0_.1), channel_id=1, source_target_pairs={{0,2},{2,0},{1,3},{3,1},{4,6},{6,4},{5,7},{7,5},{8,10},{10,8},{9,1... | collective-permute-start | bytes 1572872 | tf_op jit(solution)/shard_map/ppermute | solution.py:21
  35.2 4.4 %collective-permute-start.10 = (bf16[128,1024]{1,0:T(8,128)(2,1)S(1)}, bf16[128,1024]{1,0:T(8,128)(2,1)S(1)}, u32[]{:S(2)}, u32[]{:S(2)}) collective-permute-start(bf16[128,1024]{1,0:T(8,128)(2,1)S(1)} %fusion.3), channel_id=1, source_target_pairs={{0,0},{4,8},{8,4},{12,12},{1,1},{5,9},{9,5},{13,13},{2,2},{6,10},{... | collective-permute-start | bytes 786440 | tf_op jit(solution)/shard_map/ppermute | solution.py:435
  35.9 8.1 %collective-permute-start.9 = (bf16[128,1024]{1,0:T(8,128)(2,1)S(1)}, bf16[128,1024]{1,0:T(8,128)(2,1)S(1)}, u32[]{:S(2)}, u32[]{:S(2)}) collective-permute-start(bf16[128,1024]{1,0:T(8,128)(2,1)S(1)} %broadcast_select_fusion), channel_id=1, source_target_pairs={{0,4},{4,0},{8,12},{12,8},{1,5},{5,1},{9,13},{13,9},{2,6},{6,2},{1... | collective-permute-start | bytes 786440 | tf_op jit(solution)/shard_map/ppermute | solution.py:435
  44.3 6.7 %collective-permute-start.12 = (bf16[128,1024]{1,0:T(8,128)(2,1)S(1)}, bf16[128,1024]{1,0:T(8,128)(2,1)S(1)}, u32[]{:S(2)}, u32[]{:S(2)}) collective-permute-start(bf16[128,1024]{1,0:T(8,128)(2,1)S(1)} %get-tuple-element.128), channel_id=1, source_target_pairs={{0,4},{4,0},{8,12},{12,8},{1,5},{5,1},{9,13},{13,9},{2,6},{6,2},{1... | collective-permute-start | bytes 786440 | tf_op jit(solution)/shard_map/ppermute | solution.py:435
  46.2 4.9 %collective-permute-start.11 = (bf16[128,1024]{1,0:T(8,128)(2,1)S(1)}, bf16[128,1024]{1,0:T(8,128)(2,1)S(1)}, u32[]{:S(2)}, u32[]{:S(2)}) collective-permute-start(bf16[128,1024]{1,0:T(8,128)(2,1)S(1)} %get-tuple-element.129), channel_id=1, source_target_pairs={{0,0},{4,8},{8,4},{12,12},{1,1},{5,9},{9,5},{13,13},{2,2},{6,10},{... | collective-permute-start | bytes 786440 | tf_op jit(solution)/shard_map/ppermute | solution.py:435
  51.1 8.1 %collective-permute-start.16 = (bf16[128,1024]{1,0:T(8,128)(2,1)S(1)}, bf16[128,1024]{1,0:T(8,128)(2,1)S(1)}, u32[]{:S(2)}, u32[]{:S(2)}) collective-permute-start(bf16[128,1024]{1,0:T(8,128)(2,1)S(1)} %fusion), channel_id=1, source_target_pairs={{0,4},{4,0},{8,12},{12,8},{1,5},{5,1},{9,13},{13,9},{2,6},{6,2},{1... | collective-permute-start | bytes 786440 | tf_op jit(solution)/shard_map/ppermute | solution.py:435
  54.9 3.6 %collective-permute-start.17 = (bf16[128,1024]{1,0:T(8,128)(2,1)S(1)}, bf16[128,1024]{1,0:T(8,128)(2,1)S(1)}, u32[]{:S(2)}, u32[]{:S(2)}) collective-permute-start(bf16[128,1024]{1,0:T(8,128)(2,1)S(1)} %copy-done.10), channel_id=1, source_target_pairs={{0,0},{4,8},{8,4},{12,12},{1,1},{5,9},{9,5},{13,13},{2,2},{6,10},{... | collective-permute-start | bytes 786440 | tf_op jit(solution)/shard_map/ppermute | solution.py:408
  61.0 1.3 %collective-permute-start.18 = (f32[128,128]{1,0:T(8,128)S(1)}, f32[128,128]{1,0:T(8,128)S(1)}, u32[]{:S(2)}, u32[]{:S(2)}) collective-permute-start(f32[128,128]{1,0:T(8,128)S(1)} %get-tuple-element.110), channel_id=1, source_target_pairs={{0,1},{1,0},{2,3},{3,2},{4,5},{5,4},{6,7},{7,6},{8,9},{9,8},{10,11... | collective-permute-start | bytes 196616 | tf_op jit(solution)/shard_map/ppermute | solution.py:21
  63.0 27.6 %all-to-all-start = ((bf16[8,160,128]{2,1,0:T(8,128)(2,1)}), bf16[8,160,128]{2,1,0:T(8,128)(2,1)S(1)}, u32[]{:S(2)}, u32[]{:S(2)}) async-start(bf16[8,160,128]{2,1,0:T(8,128)(2,1)} %shard_map.112), calls=%async_computation | async-start | bytes 655360 | tf_op jit(solution)/shard_map/all_to_all | solution.py:588
  71.7 2.3 %collective-permute-start.19 = (bf16[160,128]{1,0:T(8,128)(2,1)S(1)}, bf16[160,128]{1,0:T(8,128)(2,1)S(1)}, u32[]{:S(2)}, u32[]{:S(2)}) collective-permute-start(bf16[160,128]{1,0:T(8,128)(2,1)S(1)} %slice_bitcast_fusion.mine_ref), channel_id=1, source_target_pairs={{0,1},{1,0},{2,3},{3,2},{4,5},{5,4},{6,7},{7,6},{8,9},{9,8},{10,11... | collective-permute-start | bytes 122888 | tf_op jit(solution)/shard_map/ppermute | solution.py:21
  71.8 13.3 %collective-permute-start.20 = (bf16[128,1024]{1,0:T(8,128)(2,1)S(1)}, bf16[128,1024]{1,0:T(8,128)(2,1)S(1)}, u32[]{:S(2)}, u32[]{:S(2)}) collective-permute-start(bf16[128,1024]{1,0:T(8,128)(2,1)S(1)} %copy-done.13), channel_id=1, source_target_pairs={{0,4},{4,0},{8,12},{12,8},{1,5},{5,1},{9,13},{13,9},{2,6},{6,2},{1... | collective-permute-start | bytes 786440 | tf_op jit(solution)/shard_map/ppermute | solution.py:408
  73.9 16.4 %collective-permute-start.21 = (bf16[128,1024]{1,0:T(8,128)(2,1)S(1)}, bf16[128,1024]{1,0:T(8,128)(2,1)S(1)}, u32[]{:S(2)}, u32[]{:S(2)}) collective-permute-start(bf16[128,1024]{1,0:T(8,128)(2,1)S(1)} %copy-done.16), channel_id=1, source_target_pairs={{0,4},{4,0},{8,12},{12,8},{1,5},{5,1},{9,13},{13,9},{2,6},{6,2},{1... | collective-permute-start | bytes 786440 | tf_op jit(solution)/shard_map/ppermute | solution.py:408
  90.6 1.7 %collective-permute-start.22 = (bf16[8,160,128]{2,1,0:T(8,128)(2,1)S(1)}, bf16[8,160,128]{2,1,0:T(8,128)(2,1)S(1)}, u32[]{:S(2)}, u32[]{:S(2)}) collective-permute-start(bf16[8,160,128]{2,1,0:T(8,128)(2,1)S(1)} %all-to-all-done.refs_0_), channel_id=1, source_target_pairs={{0,1},{1,0},{2,3},{3,2},{4,5},{5,4},{6,7},{7,6},{8,9},{9,8},{10,11... | collective-permute-start | bytes 983048 | tf_op jit(solution)/shard_map/ppermute | solution.py:21
  (27 other events, 301.6 us)

commit v15 on v13

--- a/solution.py
+++ b/solution.py
@@ -592,7 +592,7 @@
         functools.partial(order_kernel, n_dp, n_seq, slots),
         struct((n_dp, n_seq * rows, part), BF),
         1.0,
-        *after(tuple(toks), copies),
+        *after(tuple(toks), grads),
         scratch=[pltpu.SemaphoreType.DMA((n_dp, len(slots)))],
     )
     lows = after(lows, grads, ordered)

time: 92 us -> 89.1 us (0.968)
  local copies, waits for them, and re-layouts: 12.8 us -> 4.41 us
  waiting for transfers between devices: 25.7 us -> 31.8 us
    unnamed x62, local copies, waits for them, and re-layouts: 11.7 us -> 3.3 us
    all_to_all x1, waiting for transfers between devices: 0.01 us -> 4.58 us  [body(): lows = lax.all_to_all(copies, ('seq', 'dp'), 0, 0, tiled=True)]
    ppermute x9, waiting for transfers between devices: 10.6 us -> 12.2 us  [cyclic(): return lax.ppermute(a, axis, [(i, (i + by) % count) for i in range(count)])]
  transfers between devices with their start and end apart: 24 -> 24, of which waited for: 11 -> 13; matrix products, arithmetic and copies ran while one was open for 2% -> 2% of each run, Pallas kernels for 13% -> 14%
where the time goes in v15:
time: 89.1 us; the launch traced here: 88.7 us
  starting transfers between devices  35.7 us (40%)
  waiting for transfers between devices  31.8 us (36%)
  Pallas kernels  15 us (17%)
  local copies, waits for them, and re-layouts  4.41 us (5%)
  between operations  1.11 us (1%)
    pallas_call x14, Pallas kernels, call(): pl.pallas_call(kernel, out_shape=out_shape, grid=(1,), in_specs=specs or...  15 us
    ppermute x6, starting transfers between devices, chains(): got[k] = lax.ppermute(value, 'seq', sorted(to.items()))  13.9 us
    ppermute x9, waiting for transfers between devices, cyclic(): return lax.ppermute(a, axis, [(i, (i + by) % count) for i in range(count)])  12.2 us
    ppermute x6, waiting for transfers between devices, chains(): got[k] = lax.ppermute(value, 'seq', sorted(to.items()))  10.9 us
    ppermute x8, starting transfers between devices, relay(): found[kind, hop] = lax.ppermute(source, 'seq', pairs[kind])  10.2 us
    ppermute x9, starting transfers between devices, cyclic(): return lax.ppermute(a, axis, [(i, (i + by) % count) for i in range(count)])  6.8 us
    all_to_all x1, starting transfers between devices, body(): lows = lax.all_to_all(copies, ('seq', 'dp'), 0, 0, tiled=True)  4.9 us
    all_to_all x1, waiting for transfers between devices, body(): lows = lax.all_to_all(copies, ('seq', 'dp'), 0, 0, tiled=True)  4.58 us
  transfers between devices with their start and end apart: 24, of which 13 were waited for; matrix products, arithmetic and copies ran while one was open for 2% of the time, Pallas kernels for 14%

profile of v15, /device:TPU:0, one launch (start us, length us, event | category | flops | bytes accessed | tf_op | source)
XLA Modules:
  0.0 88.7 jit_solution(834181005243224235)
XLA Ops:
  1.7 3.0 %collective-permute-start = (bf16[128,1024]{1,0:T(8,128)(2,1)S(1)}, bf16[128,1024]{1,0:T(8,128)(2,1)S(1)}, u32[]{:S(2)}, u32[]{:S(2)}) collective-permute-start(bf16[128,1024]{1,0:T(8,128)(2,1)S(1)} %get-tuple-element.68), channel_id=1, source_target_pairs={{0,2},{2,0},{1,3},{3,1},{4,6},{6,4},{5,7},{7,5},{8,10},{10,8},{9,1... | collective-permute-start | bytes 786440 | tf_op jit(solution)/shard_map/ppermute | solution.py:21
  4.7 1.6 %collective-permute-start.2 = (bf16[128,1024]{1,0:T(8,128)(2,1)S(1)}, bf16[128,1024]{1,0:T(8,128)(2,1)S(1)}, u32[]{:S(2)}, u32[]{:S(2)}) collective-permute-start(bf16[128,1024]{1,0:T(8,128)(2,1)S(1)} %get-tuple-element.115.a_ref.refs_0_), channel_id=1, source_target_pairs={{0,4},{4,0},{8,12},{12,8},{1,5},{5,1},{9,13},{13,9},{2,6},{6,2},{1... | collective-permute-start | bytes 786440 | tf_op jit(solution)/shard_map/ppermute | solution.py:398
  7.4 3.7 %collective-permute-done.a_ref.refs_6_ = bf16[128,1024]{1,0:T(8,128)(2,1)S(1)} collective-permute-done((bf16[128,1024]{1,0:T(8,128)(2,1)S(1)}, bf16[128,1024]{1,0:T(8,128)(2,1)S(1)}, u32[]{:S(2)}, u32[]{:S(2)}) %collective-permute-start) | collective-permute-done | bytes 262176 | tf_op jit(solution)/shard_map/ppermute | solution.py:21
  11.0 1.8 %collective-permute-start.4 = (bf16[128,1024]{1,0:T(8,128)(2,1)S(1)}, bf16[128,1024]{1,0:T(8,128)(2,1)S(1)}, u32[]{:S(2)}, u32[]{:S(2)}) collective-permute-start(bf16[128,1024]{1,0:T(8,128)(2,1)S(1)} %collective-permute-done.a_ref.refs_6_), channel_id=1, source_target_pairs={{0,4},{4,0},{8,12},{12,8},{1,5},{5,1},{9,13},{13,9},{2,6},{6,2},{1... | collective-permute-start | bytes 786440 | tf_op jit(solution)/shard_map/ppermute | solution.py:398
  13.2 1.6 %collective-permute-start.1 = (f32[320,128]{1,0:T(8,128)S(1)}, f32[320,128]{1,0:T(8,128)S(1)}, u32[]{:S(2)}, u32[]{:S(2)}) collective-permute-start(f32[320,128]{1,0:T(8,128)S(1)} %shard_map.104), channel_id=1, source_target_pairs={{0,2},{2,0},{1,3},{3,1},{4,6},{6,4},{5,7},{7,5},{8,10},{10,8},{9,1... | collective-permute-start | bytes 491528 | tf_op jit(solution)/shard_map/ppermute | solution.py:21
  15.5 3.0 %collective-permute-done.1.refs_1_ = f32[320,128]{1,0:T(8,128)S(1)} collective-permute-done((f32[320,128]{1,0:T(8,128)S(1)}, f32[320,128]{1,0:T(8,128)S(1)}, u32[]{:S(2)}, u32[]{:S(2)}) %collective-permute-start.1) | collective-permute-done | bytes 163872 | tf_op jit(solution)/shard_map/ppermute | solution.py:21
  20.7 2.1 %shard_map.105 = (f32[2,2,128,1024]{3,2,1,0:T(8,128)S(1)}, f32[256,128]{1,0:T(8,128)S(1)}, f32[160,128]{1,0:T(8,128)S(1)}, bf16[128,1024]{1,0:T(8,128)(2,1)S(1)}...) custom-call(f32[320,128]{1,0:T(8,128)S(1)} %shard_map.103.refs_0_, ...), custom_call_target="tpu_custom_call" | custom-call | flops 115000000 | bytes 1966336 | tf_op jit(solution)/shard_map/pallas_call | solution.py:54
  22.8 1.8 %collective-permute-start.8 = (bf16[128,1024]{1,0:T(8,128)(2,1)S(1)}, bf16[128,1024]{1,0:T(8,128)(2,1)S(1)}, u32[]{:S(2)}, u32[]{:S(2)}) collective-permute-start(bf16[128,1024]{1,0:T(8,128)(2,1)S(1)} %get-tuple-element.72), channel_id=1, source_target_pairs={{0,4},{4,0},{8,12},{12,8},{1,5},{5,1},{9,13},{13,9},{2,6},{6,2},{1... | collective-permute-start | bytes 786440 | tf_op jit(solution)/shard_map/ppermute | solution.py:425
  28.5 2.8 %collective-permute-done.8.refs_3_ = bf16[128,1024]{1,0:T(8,128)(2,1)S(1)} collective-permute-done((bf16[128,1024]{1,0:T(8,128)(2,1)S(1)}, bf16[128,1024]{1,0:T(8,128)(2,1)S(1)}, u32[]{:S(2)}, u32[]{:S(2)}) %collective-permute-start.8) | collective-permute-done | bytes 262176 | tf_op jit(solution)/shard_map/ppermute | solution.py:425
  32.1 4.5 %collective-permute-start.9 = (bf16[128,1024]{1,0:T(8,128)(2,1)S(1)}, bf16[128,1024]{1,0:T(8,128)(2,1)S(1)}, u32[]{:S(2)}, u32[]{:S(2)}) collective-permute-start(bf16[128,1024]{1,0:T(8,128)(2,1)S(1)} %broadcast_select_fusion), channel_id=1, source_target_pairs={{0,4},{4,0},{8,12},{12,8},{1,5},{5,1},{9,13},{13,9},{2,6},{6,2},{1... | collective-permute-start | bytes 786440 | tf_op jit(solution)/shard_map/ppermute | solution.py:425
  37.6 4.1 %collective-permute-done.9.refs_9_ = bf16[128,1024]{1,0:T(8,128)(2,1)S(1)} collective-permute-done((bf16[128,1024]{1,0:T(8,128)(2,1)S(1)}, bf16[128,1024]{1,0:T(8,128)(2,1)S(1)}, u32[]{:S(2)}, u32[]{:S(2)}) %collective-permute-start.9) | collective-permute-done | bytes 262176 | tf_op jit(solution)/shard_map/ppermute | solution.py:425
  42.7 3.9 %collective-permute-start.12 = (bf16[128,1024]{1,0:T(8,128)(2,1)S(1)}, bf16[128,1024]{1,0:T(8,128)(2,1)S(1)}, u32[]{:S(2)}, u32[]{:S(2)}) collective-permute-start(bf16[128,1024]{1,0:T(8,128)(2,1)S(1)} %get-tuple-element.130), channel_id=1, source_target_pairs={{0,4},{4,0},{8,12},{12,8},{1,5},{5,1},{9,13},{13,9},{2,6},{6,2},{1... | collective-permute-start | bytes 786440 | tf_op jit(solution)/shard_map/ppermute | solution.py:425
  47.8 3.2 %collective-permute-done.12 = bf16[128,1024]{1,0:T(8,128)(2,1)S(1)} collective-permute-done((bf16[128,1024]{1,0:T(8,128)(2,1)S(1)}, bf16[128,1024]{1,0:T(8,128)(2,1)S(1)}, u32[]{:S(2)}, u32[]{:S(2)}) %collective-permute-start.12) | collective-permute-done | bytes 262176 | tf_op jit(solution)/shard_map/ppermute | solution.py:425
  51.1 2.3 %collective-permute-start.16 = (bf16[128,1024]{1,0:T(8,128)(2,1)S(1)}, bf16[128,1024]{1,0:T(8,128)(2,1)S(1)}, u32[]{:S(2)}, u32[]{:S(2)}) collective-permute-start(bf16[128,1024]{1,0:T(8,128)(2,1)S(1)} %fusion), channel_id=1, source_target_pairs={{0,4},{4,0},{8,12},{12,8},{1,5},{5,1},{9,13},{13,9},{2,6},{6,2},{1... | collective-permute-start | bytes 786440 | tf_op jit(solution)/shard_map/ppermute | solution.py:425
  54.2 1.9 %shard_map.110 = (bf16[128,2048]{1,0:T(8,128)(2,1)}, f32[272,128]{1,0:T(8,128)S(1)}) custom-call(bf16[3,128,1024]{2,1,0:T(8,128)(2,1)S(1)} %bitcast_dynamic-update-slice_fusion.refs_0_, bf16[128,2048]{1,0:T(8,128)(2,1)S(1)} %bitcast.45, bf16[128,2048]{1,0:T(8,128)(2,1)S(1)} %bitcast.52, f32[256,128]{1,0:T(8,128)S(1)} %get-tuple-element.96.bc_ref.refs_3_, ...), custom_call_target="tpu_custom_call" | custom-call | flops 3104999936 | bytes 2719872 | tf_op jit(solution)/shard_map/pallas_call | solution.py:54
  57.8 4.0 %collective-permute-start.20 = (bf16[128,1024]{1,0:T(8,128)(2,1)S(1)}, bf16[128,1024]{1,0:T(8,128)(2,1)S(1)}, u32[]{:S(2)}, u32[]{:S(2)}) collective-permute-start(bf16[128,1024]{1,0:T(8,128)(2,1)S(1)} %collective-permute-done.17.refs_10_), channel_id=1, source_target_pairs={{0,4},{4,0},{8,12},{12,8},{1,5},{5,1},{9,13},{13,9},{2,6},{6,2},{1... | collective-permute-start | bytes 786440 | tf_op jit(solution)/shard_map/ppermute | solution.py:398
  61.9 1.7 %shard_map.111 = (bf16[128,2048]{1,0:T(8,128)(2,1)}, f32[160,128]{1,0:T(8,128)S(1)}, f32[128,128]{1,0:T(8,128)S(1)}) custom-call(bf16[3,128,1024]{2,1,0:T(8,128)(2,1)S(1)} %bitcast_dynamic-update-slice_fusion.3.refs_0_, bf16[128,2048]{1,0:T(8,128)(2,1)S(1)} %bitcast.47, bf16[128,2048]{1,0:T(8,128)(2,1)S(1)} %bitcast.54, ...), custom_call_target="tpu_custom_call", output_to_operand_aliasing={{0}: (12, {})} | custom-call | flops 3104999936 | bytes 3383424 | tf_op jit(solution)/shard_map/pallas_call | solution.py:54
  64.9 2.0 %collective-permute-done.20.refs_11_ = bf16[128,1024]{1,0:T(8,128)(2,1)S(1)} collective-permute-done((bf16[128,1024]{1,0:T(8,128)(2,1)S(1)}, bf16[128,1024]{1,0:T(8,128)(2,1)S(1)}, u32[]{:S(2)}, u32[]{:S(2)}) %collective-permute-start.20) | collective-permute-done | bytes 262176 | tf_op jit(solution)/shard_map/ppermute | solution.py:398
  67.6 2.1 %collective-permute-done.19.refs_5_ = bf16[128,1024]{1,0:T(8,128)(2,1)S(1)} collective-permute-done((bf16[128,1024]{1,0:T(8,128)(2,1)S(1)}, bf16[128,1024]{1,0:T(8,128)(2,1)S(1)}, u32[]{:S(2)}, u32[]{:S(2)}) %collective-permute-start.19) | collective-permute-done | bytes 262176 | tf_op jit(solution)/shard_map/ppermute | solution.py:398
  71.2 4.9 %all-to-all-start = ((bf16[8,160,128]{2,1,0:T(8,128)(2,1)}), bf16[8,160,128]{2,1,0:T(8,128)(2,1)S(1)}, u32[]{:S(2)}, u32[]{:S(2)}) async-start(bf16[8,160,128]{2,1,0:T(8,128)(2,1)} %shard_map.112), calls=%async_computation | async-start | bytes 655360 | tf_op jit(solution)/shard_map/all_to_all | solution.py:577
  78.3 1.5 %shard_map.113 = bf16[128,2048]{1,0:T(8,128)(2,1)} custom-call(bf16[160,128]{1,0:T(8,128)(2,1)S(1)} %slice_bitcast_fusion.mine_ref, bf16[160,128]{1,0:T(8,128)(2,1)S(1)} %collective-permute-done.21.other_ref, bf16[1024,256]{1,0:T(8,128)(2,1)S(1)} %copy-done.24, bf16[64,1024]{1,0:T(8,128)(2,1)S(1)} %bitcast.67, bf16[1024,256]{1,0:T(8,128)(2,1)S(1)} %copy-done.26, ...), custom_call_target="tpu_custom_call" | custom-call | flops 3335000064 | bytes 1392640 | tf_op jit(solution)/shard_map/pallas_call | solution.py:54
  80.2 4.6 %all-to-all-done.refs_0_ = bf16[8,160,128]{2,1,0:T(8,128)(2,1)S(1)} async-done(((bf16[8,160,128]{2,1,0:T(8,128)(2,1)}), bf16[8,160,128]{2,1,0:T(8,128)(2,1)S(1)}, u32[]{:S(2)}, u32[]{:S(2)}) %all-to-all-start) | async-done | bytes 327712 | tf_op jit(solution)/shard_map/all_to_all | solution.py:577
  84.8 1.6 %collective-permute-done.22.refs_1_ = bf16[8,160,128]{2,1,0:T(8,128)(2,1)S(1)} collective-permute-done((bf16[8,160,128]{2,1,0:T(8,128)(2,1)S(1)}, bf16[8,160,128]{2,1,0:T(8,128)(2,1)S(1)}, u32[]{:S(2)}, u32[]{:S(2)}) %collective-permute-start.22) | collective-permute-done | bytes 327712 | tf_op jit(solution)/shard_map/ppermute | solution.py:21
  86.4 2.2 %shard_map.115 = (f32[1024,256]{1,0:T(8,128)}, f32[64,1024]{1,0:T(8,128)}) custom-call(bf16[2,512,1024]{2,1,0:T(8,128)(2,1)S(1)} %shard_map.114.tok_ref, bf16[8,160,128]{2,1,0:T(8,128)(2,1)S(1)} %all-to-all-done.refs_0_, bf16[8,160,128]{2,1,0:T(8,128)(2,1)S(1)} %collective-permute-done.22.refs_1_), custom_call_target="tpu_custom_call" | custom-call | flops 4600000000 | bytes 2752512 | tf_op jit(solution)/shard_map/pallas_call | solution.py:54
  (113 shorter events, 21.4 us)
Async XLA Ops:
  1.7 9.3 %collective-permute-start = (bf16[128,1024]{1,0:T(8,128)(2,1)S(1)}, bf16[128,1024]{1,0:T(8,128)(2,1)S(1)}, u32[]{:S(2)}, u32[]{:S(2)}) collective-permute-start(bf16[128,1024]{1,0:T(8,128)(2,1)S(1)} %get-tuple-element.68), channel_id=1, source_target_pairs={{0,2},{2,0},{1,3},{3,1},{4,6},{6,4},{5,7},{7,5},{8,10},{10,8},{9,1... | collective-permute-start | bytes 786440 | tf_op jit(solution)/shard_map/ppermute | solution.py:21
  4.7 10.7 %collective-permute-start.2 = (bf16[128,1024]{1,0:T(8,128)(2,1)S(1)}, bf16[128,1024]{1,0:T(8,128)(2,1)S(1)}, u32[]{:S(2)}, u32[]{:S(2)}) collective-permute-start(bf16[128,1024]{1,0:T(8,128)(2,1)S(1)} %get-tuple-element.115.a_ref.refs_0_), channel_id=1, source_target_pairs={{0,4},{4,0},{8,12},{12,8},{1,5},{5,1},{9,13},{13,9},{2,6},{6,2},{1... | collective-permute-start | bytes 786440 | tf_op jit(solution)/shard_map/ppermute | solution.py:398
  6.3 9.2 %collective-permute-start.3 = (bf16[128,1024]{1,0:T(8,128)(2,1)S(1)}, bf16[128,1024]{1,0:T(8,128)(2,1)S(1)}, u32[]{:S(2)}, u32[]{:S(2)}) collective-permute-start(bf16[128,1024]{1,0:T(8,128)(2,1)S(1)} %get-tuple-element.115.a_ref.refs_0_), channel_id=1, source_target_pairs={{0,0},{4,8},{8,4},{12,12},{1,1},{5,9},{9,5},{13,13},{2,2},{6,10},{... | collective-permute-start | bytes 786440 | tf_op jit(solution)/shard_map/ppermute | solution.py:398
  11.0 7.5 %collective-permute-start.4 = (bf16[128,1024]{1,0:T(8,128)(2,1)S(1)}, bf16[128,1024]{1,0:T(8,128)(2,1)S(1)}, u32[]{:S(2)}, u32[]{:S(2)}) collective-permute-start(bf16[128,1024]{1,0:T(8,128)(2,1)S(1)} %collective-permute-done.a_ref.refs_6_), channel_id=1, source_target_pairs={{0,4},{4,0},{8,12},{12,8},{1,5},{5,1},{9,13},{13,9},{2,6},{6,2},{1... | collective-permute-start | bytes 786440 | tf_op jit(solution)/shard_map/ppermute | solution.py:398
  13.2 5.4 %collective-permute-start.1 = (f32[320,128]{1,0:T(8,128)S(1)}, f32[320,128]{1,0:T(8,128)S(1)}, u32[]{:S(2)}, u32[]{:S(2)}) collective-permute-start(f32[320,128]{1,0:T(8,128)S(1)} %shard_map.104), channel_id=1, source_target_pairs={{0,2},{2,0},{1,3},{3,1},{4,6},{6,4},{5,7},{7,5},{8,10},{10,8},{9,1... | collective-permute-start | bytes 491528 | tf_op jit(solution)/shard_map/ppermute | solution.py:21
  14.7 8.1 %collective-permute-start.7 = (bf16[128,1024]{1,0:T(8,128)(2,1)S(1)}, bf16[128,1024]{1,0:T(8,128)(2,1)S(1)}, u32[]{:S(2)}, u32[]{:S(2)}) collective-permute-start(bf16[128,1024]{1,0:T(8,128)(2,1)S(1)} %collective-permute-done.a_ref.refs_6_), channel_id=1, source_target_pairs={{0,0},{4,8},{8,4},{12,12},{1,1},{5,9},{9,5},{13,13},{2,2},{6,10},{... | collective-permute-start | bytes 786440 | tf_op jit(solution)/shard_map/ppermute | solution.py:398
  15.4 3.8 %collective-permute-start.5 = (f32[320,128]{1,0:T(8,128)S(1)}, f32[320,128]{1,0:T(8,128)S(1)}, u32[]{:S(2)}, u32[]{:S(2)}) collective-permute-start(f32[320,128]{1,0:T(8,128)S(1)} %shard_map.103.refs_0_), channel_id=1, source_target_pairs={{0,1},{1,0},{2,3},{3,2},{4,5},{5,4},{6,7},{7,6},{8,9},{9,8},{10,11... | collective-permute-start | bytes 491528 | tf_op jit(solution)/shard_map/ppermute | solution.py:21
  19.3 1.4 %collective-permute-start.6 = (f32[320,128]{1,0:T(8,128)S(1)}, f32[320,128]{1,0:T(8,128)S(1)}, u32[]{:S(2)}, u32[]{:S(2)}) collective-permute-start(f32[320,128]{1,0:T(8,128)S(1)} %collective-permute-done.1.refs_1_), channel_id=1, source_target_pairs={{0,1},{1,0},{2,3},{3,2},{4,5},{5,4},{6,7},{7,6},{8,9},{9,8},{10,11... | collective-permute-start | bytes 491528 | tf_op jit(solution)/shard_map/ppermute | solution.py:21
  22.8 8.4 %collective-permute-start.8 = (bf16[128,1024]{1,0:T(8,128)(2,1)S(1)}, bf16[128,1024]{1,0:T(8,128)(2,1)S(1)}, u32[]{:S(2)}, u32[]{:S(2)}) collective-permute-start(bf16[128,1024]{1,0:T(8,128)(2,1)S(1)} %get-tuple-element.72), channel_id=1, source_target_pairs={{0,4},{4,0},{8,12},{12,8},{1,5},{5,1},{9,13},{13,9},{2,6},{6,2},{1... | collective-permute-start | bytes 786440 | tf_op jit(solution)/shard_map/ppermute | solution.py:425
  24.6 23.1 %collective-permute-start.15 = (bf16[128,1024]{1,0:T(8,128)(2,1)S(1)}, bf16[128,1024]{1,0:T(8,128)(2,1)S(1)}, u32[]{:S(2)}, u32[]{:S(2)}) collective-permute-start(bf16[128,1024]{1,0:T(8,128)(2,1)S(1)} %collective-permute-done.2.refs_1_), channel_id=1, source_target_pairs={{0,0},{4,8},{8,4},{12,12},{1,1},{5,9},{9,5},{13,13},{2,2},{6,10},{... | collective-permute-start | bytes 786440 | tf_op jit(solution)/shard_map/ppermute | solution.py:398
  25.3 22.4 %collective-permute-start.14 = (bf16[64,1024]{1,0:T(8,128)(2,1)S(1)}, bf16[64,1024]{1,0:T(8,128)(2,1)S(1)}, u32[]{:S(2)}, u32[]{:S(2)}) collective-permute-start(bf16[64,1024]{1,0:T(8,128)(2,1)S(1)} %bitcast.66), channel_id=1, source_target_pairs={{0,2},{2,0},{1,3},{3,1},{4,6},{6,4},{5,7},{7,5},{8,10},{10,8},{9,1... | collective-permute-start | bytes 393224 | tf_op jit(solution)/shard_map/ppermute | solution.py:21
  26.6 21.1 %collective-permute-start.13 = (bf16[1024,256]{1,0:T(8,128)(2,1)}, bf16[1024,256]{1,0:T(8,128)(2,1)S(1)}, u32[]{:S(2)}, u32[]{:S(2)}) collective-permute-start(bf16[1024,256]{1,0:T(8,128)(2,1)} %refs_0_.1), channel_id=1, source_target_pairs={{0,2},{2,0},{1,3},{3,1},{4,6},{6,4},{5,7},{7,5},{8,10},{10,8},{9,1... | collective-permute-start | bytes 1572872 | tf_op jit(solution)/shard_map/ppermute | solution.py:21
  31.4 6.2 %collective-permute-start.10 = (bf16[128,1024]{1,0:T(8,128)(2,1)S(1)}, bf16[128,1024]{1,0:T(8,128)(2,1)S(1)}, u32[]{:S(2)}, u32[]{:S(2)}) collective-permute-start(bf16[128,1024]{1,0:T(8,128)(2,1)S(1)} %fusion.3), channel_id=1, source_target_pairs={{0,0},{4,8},{8,4},{12,12},{1,1},{5,9},{9,5},{13,13},{2,2},{6,10},{... | collective-permute-start | bytes 786440 | tf_op jit(solution)/shard_map/ppermute | solution.py:425
  32.1 9.6 %collective-permute-start.9 = (bf16[128,1024]{1,0:T(8,128)(2,1)S(1)}, bf16[128,1024]{1,0:T(8,128)(2,1)S(1)}, u32[]{:S(2)}, u32[]{:S(2)}) collective-permute-start(bf16[128,1024]{1,0:T(8,128)(2,1)S(1)} %broadcast_select_fusion), channel_id=1, source_target_pairs={{0,4},{4,0},{8,12},{12,8},{1,5},{5,1},{9,13},{13,9},{2,6},{6,2},{1... | collective-permute-start | bytes 786440 | tf_op jit(solution)/shard_map/ppermute | solution.py:425
  42.0 5.8 %collective-permute-start.11 = (bf16[128,1024]{1,0:T(8,128)(2,1)S(1)}, bf16[128,1024]{1,0:T(8,128)(2,1)S(1)}, u32[]{:S(2)}, u32[]{:S(2)}) collective-permute-start(bf16[128,1024]{1,0:T(8,128)(2,1)S(1)} %get-tuple-element.131), channel_id=1, source_target_pairs={{0,0},{4,8},{8,4},{12,12},{1,1},{5,9},{9,5},{13,13},{2,2},{6,10},{... | collective-permute-start | bytes 786440 | tf_op jit(solution)/shard_map/ppermute | solution.py:425
  42.7 8.3 %collective-permute-start.12 = (bf16[128,1024]{1,0:T(8,128)(2,1)S(1)}, bf16[128,1024]{1,0:T(8,128)(2,1)S(1)}, u32[]{:S(2)}, u32[]{:S(2)}) collective-permute-start(bf16[128,1024]{1,0:T(8,128)(2,1)S(1)} %get-tuple-element.130), channel_id=1, source_target_pairs={{0,4},{4,0},{8,12},{12,8},{1,5},{5,1},{9,13},{13,9},{2,6},{6,2},{1... | collective-permute-start | bytes 786440 | tf_op jit(solution)/shard_map/ppermute | solution.py:425
  51.1 6.7 %collective-permute-start.16 = (bf16[128,1024]{1,0:T(8,128)(2,1)S(1)}, bf16[128,1024]{1,0:T(8,128)(2,1)S(1)}, u32[]{:S(2)}, u32[]{:S(2)}) collective-permute-start(bf16[128,1024]{1,0:T(8,128)(2,1)S(1)} %fusion), channel_id=1, source_target_pairs={{0,4},{4,0},{8,12},{12,8},{1,5},{5,1},{9,13},{13,9},{2,6},{6,2},{1... | collective-permute-start | bytes 786440 | tf_op jit(solution)/shard_map/ppermute | solution.py:425
  53.4 3.6 %collective-permute-start.17 = (bf16[128,1024]{1,0:T(8,128)(2,1)S(1)}, bf16[128,1024]{1,0:T(8,128)(2,1)S(1)}, u32[]{:S(2)}, u32[]{:S(2)}) collective-permute-start(bf16[128,1024]{1,0:T(8,128)(2,1)S(1)} %copy-done.10), channel_id=1, source_target_pairs={{0,0},{4,8},{8,4},{12,12},{1,1},{5,9},{9,5},{13,13},{2,2},{6,10},{... | collective-permute-start | bytes 786440 | tf_op jit(solution)/shard_map/ppermute | solution.py:398
  57.8 9.1 %collective-permute-start.20 = (bf16[128,1024]{1,0:T(8,128)(2,1)S(1)}, bf16[128,1024]{1,0:T(8,128)(2,1)S(1)}, u32[]{:S(2)}, u32[]{:S(2)}) collective-permute-start(bf16[128,1024]{1,0:T(8,128)(2,1)S(1)} %collective-permute-done.17.refs_10_), channel_id=1, source_target_pairs={{0,4},{4,0},{8,12},{12,8},{1,5},{5,1},{9,13},{13,9},{2,6},{6,2},{1... | collective-permute-start | bytes 786440 | tf_op jit(solution)/shard_map/ppermute | solution.py:398
  61.8 7.9 %collective-permute-start.19 = (bf16[128,1024]{1,0:T(8,128)(2,1)S(1)}, bf16[128,1024]{1,0:T(8,128)(2,1)S(1)}, u32[]{:S(2)}, u32[]{:S(2)}) collective-permute-start(bf16[128,1024]{1,0:T(8,128)(2,1)S(1)} %collective-permute-done.15.refs_4_), channel_id=1, source_target_pairs={{0,4},{4,0},{8,12},{12,8},{1,5},{5,1},{9,13},{13,9},{2,6},{6,2},{1... | collective-permute-start | bytes 786440 | tf_op jit(solution)/shard_map/ppermute | solution.py:398
  63.6 1.3 %collective-permute-start.18 = (f32[128,128]{1,0:T(8,128)S(1)}, f32[128,128]{1,0:T(8,128)S(1)}, u32[]{:S(2)}, u32[]{:S(2)}) collective-permute-start(f32[128,128]{1,0:T(8,128)S(1)} %get-tuple-element.111), channel_id=1, source_target_pairs={{0,1},{1,0},{2,3},{3,2},{4,5},{5,4},{6,7},{7,6},{8,9},{9,8},{10,11... | collective-permute-start | bytes 196616 | tf_op jit(solution)/shard_map/ppermute | solution.py:21
  71.2 13.6 %all-to-all-start = ((bf16[8,160,128]{2,1,0:T(8,128)(2,1)}), bf16[8,160,128]{2,1,0:T(8,128)(2,1)S(1)}, u32[]{:S(2)}, u32[]{:S(2)}) async-start(bf16[8,160,128]{2,1,0:T(8,128)(2,1)} %shard_map.112), calls=%async_computation | async-start | bytes 655360 | tf_op jit(solution)/shard_map/all_to_all | solution.py:577
  77.0 1.3 %collective-permute-start.21 = (bf16[160,128]{1,0:T(8,128)(2,1)S(1)}, bf16[160,128]{1,0:T(8,128)(2,1)S(1)}, u32[]{:S(2)}, u32[]{:S(2)}) collective-permute-start(bf16[160,128]{1,0:T(8,128)(2,1)S(1)} %slice_bitcast_fusion.mine_ref), channel_id=1, source_target_pairs={{0,1},{1,0},{2,3},{3,2},{4,5},{5,4},{6,7},{7,6},{8,9},{9,8},{10,11... | collective-permute-start | bytes 122888 | tf_op jit(solution)/shard_map/ppermute | solution.py:21
  84.8 1.6 %collective-permute-start.22 = (bf16[8,160,128]{2,1,0:T(8,128)(2,1)S(1)}, bf16[8,160,128]{2,1,0:T(8,128)(2,1)S(1)}, u32[]{:S(2)}, u32[]{:S(2)}) collective-permute-start(bf16[8,160,128]{2,1,0:T(8,128)(2,1)S(1)} %all-to-all-done.refs_0_), channel_id=1, source_target_pairs={{0,1},{1,0},{2,3},{3,2},{4,5},{5,4},{6,7},{7,6},{8,9},{9,8},{10,11... | collective-permute-start | bytes 983048 | tf_op jit(solution)/shard_map/ppermute | solution.py:21
  (31 other events, 193.7 us)

commit v16 on v15

--- a/solution.py
+++ b/solution.py
@@ -399,7 +399,7 @@
     return [found[step] for step in steps]
 
 
-def chains(first, own, decay, inner, beside, riders, late):
+def chains(first, own, decay, inner, beside, riders, cross, late):
     count = lax.axis_size("seq")
     place = lax.axis_index("seq")
     chunks = len(first)
@@ -429,9 +429,11 @@
             done.append(todo.pop(0)(*sent))
         if slot == 1:
             extra = beside(*sent)
+        if slot == max(last - 1, 1):
+            crossed = cross(*sent)
         if slot == last:
             k = steps[-1][1]
-            got[k] = after(got[k], *late(*sent))
+            got[k] = after(got[k], *late(*sent), *crossed)
         if slot < last:
             held = [got[k] for _, k in steps] + [d[0] for d in done[-1:]]
             if slot == last - 1:
@@ -530,9 +532,12 @@
     weights = [w_bc, w_dt]
 
     def beside(*others):
+        return relay(found[0], groups[0], second, *others)
+
+    def cross(*others):
         for r in range(1, n_dp):
             weights.extend(cyclic(after(a, *others), "dp", r) for a in (w_bc, w_dt))
-        return weights[2:] + relay(found[0], groups[0], second, *others)
+        return weights[2:]
 
     def late(*others):
         return relay(found[1], groups[1], second, *others) if n_dp > 1 else []
@@ -540,7 +545,7 @@
     first[0] = after(first[0], *spare)
     riders = [f[1, 1] for f in found] if ride else []
     calls = [functools.partial(inner, q) for q in range(PARTS)]
-    stores, inners = chains(first, own, decay, calls, beside, riders, late)
+    stores, inners = chains(first, own, decay, calls, beside, riders, cross, late)
     for f, a in zip(found, riders):
         f[0, 2] = a
     done = [relay(f, a, [t for t in slots if t not in f], stores[-1]) for f, a in zip(found, groups)]

time: 89.1 us -> 90.4 us (1.015)
  waiting for transfers between devices: 31.8 us -> 35.3 us
  starting transfers between devices: 35.7 us -> 33.5 us
    ppermute x9, waiting for transfers between devices: 12.2 us -> 15.9 us  [cyclic(): return lax.ppermute(a, axis, [(i, (i + by) % count) for i in range(count)])]
    ppermute x8, starting transfers between devices: 10.2 us -> 8.15 us  [relay(): found[kind, hop] = lax.ppermute(source, 'seq', pairs[kind])]
    unnamed x62 -> x64, local copies, waits for them, and re-layouts: 3.3 us -> 3.28 us
  transfers between devices with their start and end apart: 24 -> 24, of which waited for: 13 -> 13; matrix products, arithmetic and copies ran while one was open for 2% -> 2% of each run, Pallas kernels for 14% -> 13%
where the time goes in v16:
time: 90.4 us; the launch traced here: 89.9 us
  waiting for transfers between devices  35.3 us (39%)
  starting transfers between devices  33.5 us (37%)
  Pallas kernels  15.1 us (17%)
  local copies, waits for them, and re-layouts  4.39 us (5%)
  between operations  1.11 us (1%)
    ppermute x9, waiting for transfers between devices, cyclic(): return lax.ppermute(a, axis, [(i, (i + by) % count) for i in range(count)])  15.9 us
    pallas_call x14, Pallas kernels, call(): pl.pallas_call(kernel, out_shape=out_shape, grid=(1,), in_specs=specs or...  15.1 us
    ppermute x6, starting transfers between devices, chains(): got[k] = lax.ppermute(value, 'seq', sorted(to.items()))  13.9 us
    ppermute x6, waiting for transfers between devices, chains(): got[k] = lax.ppermute(value, 'seq', sorted(to.items()))  10.2 us
    ppermute x8, starting transfers between devices, relay(): found[kind, hop] = lax.ppermute(source, 'seq', pairs[kind])  8.15 us
    ppermute x9, starting transfers between devices, cyclic(): return lax.ppermute(a, axis, [(i, (i + by) % count) for i in range(count)])  6.8 us
    all_to_all x1, starting transfers between devices, body(): lows = lax.all_to_all(copies, ('seq', 'dp'), 0, 0, tiled=True)  4.65 us
    ppermute x8, waiting for transfers between devices, relay(): found[kind, hop] = lax.ppermute(source, 'seq', pairs[kind])  4.61 us
  transfers between devices with their start and end apart: 24, of which 13 were waited for; matrix products, arithmetic and copies ran while one was open for 2% of the time, Pallas kernels for 13%

profile of v16, /device:TPU:0, one launch (start us, length us, event | category | flops | bytes accessed | tf_op | source)
XLA Modules:
  0.0 89.9 jit_solution(10012009312547119609)
XLA Ops:
  1.7 3.0 %collective-permute-start = (bf16[128,1024]{1,0:T(8,128)(2,1)S(1)}, bf16[128,1024]{1,0:T(8,128)(2,1)S(1)}, u32[]{:S(2)}, u32[]{:S(2)}) collective-permute-start(bf16[128,1024]{1,0:T(8,128)(2,1)S(1)} %get-tuple-element.68), channel_id=1, source_target_pairs={{0,2},{2,0},{1,3},{3,1},{4,6},{6,4},{5,7},{7,5},{8,10},{10,8},{9,1... | collective-permute-start | bytes 786440 | tf_op jit(solution)/shard_map/ppermute | solution.py:21
  4.7 1.6 %collective-permute-start.2 = (bf16[128,1024]{1,0:T(8,128)(2,1)S(1)}, bf16[128,1024]{1,0:T(8,128)(2,1)S(1)}, u32[]{:S(2)}, u32[]{:S(2)}) collective-permute-start(bf16[128,1024]{1,0:T(8,128)(2,1)S(1)} %get-tuple-element.115.a_ref.refs_0_), channel_id=1, source_target_pairs={{0,4},{4,0},{8,12},{12,8},{1,5},{5,1},{9,13},{13,9},{2,6},{6,2},{1... | collective-permute-start | bytes 786440 | tf_op jit(solution)/shard_map/ppermute | solution.py:398
  7.4 3.7 %collective-permute-done.a_ref.refs_6_ = bf16[128,1024]{1,0:T(8,128)(2,1)S(1)} collective-permute-done((bf16[128,1024]{1,0:T(8,128)(2,1)S(1)}, bf16[128,1024]{1,0:T(8,128)(2,1)S(1)}, u32[]{:S(2)}, u32[]{:S(2)}) %collective-permute-start) | collective-permute-done | bytes 262176 | tf_op jit(solution)/shard_map/ppermute | solution.py:21
  11.0 1.8 %collective-permute-start.4 = (bf16[128,1024]{1,0:T(8,128)(2,1)S(1)}, bf16[128,1024]{1,0:T(8,128)(2,1)S(1)}, u32[]{:S(2)}, u32[]{:S(2)}) collective-permute-start(bf16[128,1024]{1,0:T(8,128)(2,1)S(1)} %collective-permute-done.a_ref.refs_6_), channel_id=1, source_target_pairs={{0,4},{4,0},{8,12},{12,8},{1,5},{5,1},{9,13},{13,9},{2,6},{6,2},{1... | collective-permute-start | bytes 786440 | tf_op jit(solution)/shard_map/ppermute | solution.py:398
  13.2 1.6 %collective-permute-start.1 = (f32[320,128]{1,0:T(8,128)S(1)}, f32[320,128]{1,0:T(8,128)S(1)}, u32[]{:S(2)}, u32[]{:S(2)}) collective-permute-start(f32[320,128]{1,0:T(8,128)S(1)} %shard_map.104), channel_id=1, source_target_pairs={{0,2},{2,0},{1,3},{3,1},{4,6},{6,4},{5,7},{7,5},{8,10},{10,8},{9,1... | collective-permute-start | bytes 491528 | tf_op jit(solution)/shard_map/ppermute | solution.py:21
  15.5 3.0 %collective-permute-done.1.refs_1_ = f32[320,128]{1,0:T(8,128)S(1)} collective-permute-done((f32[320,128]{1,0:T(8,128)S(1)}, f32[320,128]{1,0:T(8,128)S(1)}, u32[]{:S(2)}, u32[]{:S(2)}) %collective-permute-start.1) | collective-permute-done | bytes 163872 | tf_op jit(solution)/shard_map/ppermute | solution.py:21
  19.3 1.4 %collective-permute-done.6.refs_3_ = f32[320,128]{1,0:T(8,128)S(1)} collective-permute-done((f32[320,128]{1,0:T(8,128)S(1)}, f32[320,128]{1,0:T(8,128)S(1)}, u32[]{:S(2)}, u32[]{:S(2)}) %collective-permute-start.6) | collective-permute-done | bytes 163872 | tf_op jit(solution)/shard_map/ppermute | solution.py:21
  20.7 2.1 %shard_map.105 = (f32[2,2,128,1024]{3,2,1,0:T(8,128)S(1)}, f32[256,128]{1,0:T(8,128)S(1)}, f32[160,128]{1,0:T(8,128)S(1)}, bf16[128,1024]{1,0:T(8,128)(2,1)S(1)}...) custom-call(f32[320,128]{1,0:T(8,128)S(1)} %shard_map.103.refs_0_, ...), custom_call_target="tpu_custom_call" | custom-call | flops 115000000 | bytes 1966336 | tf_op jit(solution)/shard_map/pallas_call | solution.py:54
  22.8 1.8 %collective-permute-start.8 = (bf16[128,1024]{1,0:T(8,128)(2,1)S(1)}, bf16[128,1024]{1,0:T(8,128)(2,1)S(1)}, u32[]{:S(2)}, u32[]{:S(2)}) collective-permute-start(bf16[128,1024]{1,0:T(8,128)(2,1)S(1)} %get-tuple-element.72), channel_id=1, source_target_pairs={{0,4},{4,0},{8,12},{12,8},{1,5},{5,1},{9,13},{13,9},{2,6},{6,2},{1... | collective-permute-start | bytes 786440 | tf_op jit(solution)/shard_map/ppermute | solution.py:425
  26.4 4.9 %collective-permute-done.8.refs_3_ = bf16[128,1024]{1,0:T(8,128)(2,1)S(1)} collective-permute-done((bf16[128,1024]{1,0:T(8,128)(2,1)S(1)}, bf16[128,1024]{1,0:T(8,128)(2,1)S(1)}, u32[]{:S(2)}, u32[]{:S(2)}) %collective-permute-start.8) | collective-permute-done | bytes 262176 | tf_op jit(solution)/shard_map/ppermute | solution.py:425
  32.1 4.5 %collective-permute-start.9 = (bf16[128,1024]{1,0:T(8,128)(2,1)S(1)}, bf16[128,1024]{1,0:T(8,128)(2,1)S(1)}, u32[]{:S(2)}, u32[]{:S(2)}) collective-permute-start(bf16[128,1024]{1,0:T(8,128)(2,1)S(1)} %broadcast_select_fusion), channel_id=1, source_target_pairs={{0,4},{4,0},{8,12},{12,8},{1,5},{5,1},{9,13},{13,9},{2,6},{6,2},{1... | collective-permute-start | bytes 786440 | tf_op jit(solution)/shard_map/ppermute | solution.py:425
  37.6 4.1 %collective-permute-done.9.refs_9_ = bf16[128,1024]{1,0:T(8,128)(2,1)S(1)} collective-permute-done((bf16[128,1024]{1,0:T(8,128)(2,1)S(1)}, bf16[128,1024]{1,0:T(8,128)(2,1)S(1)}, u32[]{:S(2)}, u32[]{:S(2)}) %collective-permute-start.9) | collective-permute-done | bytes 262176 | tf_op jit(solution)/shard_map/ppermute | solution.py:425
  42.7 3.9 %collective-permute-start.12 = (bf16[128,1024]{1,0:T(8,128)(2,1)S(1)}, bf16[128,1024]{1,0:T(8,128)(2,1)S(1)}, u32[]{:S(2)}, u32[]{:S(2)}) collective-permute-start(bf16[128,1024]{1,0:T(8,128)(2,1)S(1)} %get-tuple-element.130), channel_id=1, source_target_pairs={{0,4},{4,0},{8,12},{12,8},{1,5},{5,1},{9,13},{13,9},{2,6},{6,2},{1... | collective-permute-start | bytes 786440 | tf_op jit(solution)/shard_map/ppermute | solution.py:425
  51.1 2.3 %collective-permute-start.14 = (bf16[128,1024]{1,0:T(8,128)(2,1)S(1)}, bf16[128,1024]{1,0:T(8,128)(2,1)S(1)}, u32[]{:S(2)}, u32[]{:S(2)}) collective-permute-start(bf16[128,1024]{1,0:T(8,128)(2,1)S(1)} %fusion), channel_id=1, source_target_pairs={{0,4},{4,0},{8,12},{12,8},{1,5},{5,1},{9,13},{13,9},{2,6},{6,2},{1... | collective-permute-start | bytes 786440 | tf_op jit(solution)/shard_map/ppermute | solution.py:425
  54.1 1.9 %shard_map.110 = (bf16[128,2048]{1,0:T(8,128)(2,1)}, f32[272,128]{1,0:T(8,128)S(1)}) custom-call(bf16[3,128,1024]{2,1,0:T(8,128)(2,1)S(1)} %bitcast_dynamic-update-slice_fusion.refs_0_, bf16[128,2048]{1,0:T(8,128)(2,1)S(1)} %bitcast.45, bf16[128,2048]{1,0:T(8,128)(2,1)S(1)} %bitcast.52, f32[256,128]{1,0:T(8,128)S(1)} %get-tuple-element.96.bc_ref.refs_3_, ...), custom_call_target="tpu_custom_call" | custom-call | flops 3104999936 | bytes 2719872 | tf_op jit(solution)/shard_map/pallas_call | solution.py:54
  57.0 3.8 %collective-permute-done.16.refs_2_ = bf16[1024,256]{1,0:T(8,128)(2,1)S(1)} collective-permute-done((bf16[1024,256]{1,0:T(8,128)(2,1)S(1)}, bf16[1024,256]{1,0:T(8,128)(2,1)S(1)}, u32[]{:S(2)}, u32[]{:S(2)}) %collective-permute-start.16) | collective-permute-done | bytes 524320 | tf_op jit(solution)/shard_map/ppermute | solution.py:21
  62.9 1.8 %shard_map.111 = (bf16[128,2048]{1,0:T(8,128)(2,1)}, f32[160,128]{1,0:T(8,128)S(1)}, f32[128,128]{1,0:T(8,128)S(1)}) custom-call(bf16[3,128,1024]{2,1,0:T(8,128)(2,1)S(1)} %bitcast_dynamic-update-slice_fusion.3.refs_0_, bf16[128,2048]{1,0:T(8,128)(2,1)S(1)} %bitcast.47, bf16[128,2048]{1,0:T(8,128)(2,1)S(1)} %bitcast.54, ...), custom_call_target="tpu_custom_call", output_to_operand_aliasing={{0}: (12, {})} | custom-call | flops 3104999936 | bytes 3383424 | tf_op jit(solution)/shard_map/pallas_call | solution.py:54
  66.0 2.5 %collective-permute-done.20.refs_11_ = bf16[128,1024]{1,0:T(8,128)(2,1)S(1)} collective-permute-done((bf16[128,1024]{1,0:T(8,128)(2,1)S(1)}, bf16[128,1024]{1,0:T(8,128)(2,1)S(1)}, u32[]{:S(2)}, u32[]{:S(2)}) %collective-permute-start.20) | collective-permute-done | bytes 262176 | tf_op jit(solution)/shard_map/ppermute | solution.py:398
  69.2 2.1 %collective-permute-done.19.refs_5_ = bf16[128,1024]{1,0:T(8,128)(2,1)S(1)} collective-permute-done((bf16[128,1024]{1,0:T(8,128)(2,1)S(1)}, bf16[128,1024]{1,0:T(8,128)(2,1)S(1)}, u32[]{:S(2)}, u32[]{:S(2)}) %collective-permute-start.19) | collective-permute-done | bytes 262176 | tf_op jit(solution)/shard_map/ppermute | solution.py:398
  72.8 4.6 %all-to-all-start = ((bf16[8,160,128]{2,1,0:T(8,128)(2,1)}), bf16[8,160,128]{2,1,0:T(8,128)(2,1)S(1)}, u32[]{:S(2)}, u32[]{:S(2)}) async-start(bf16[8,160,128]{2,1,0:T(8,128)(2,1)} %shard_map.112), calls=%async_computation | async-start | bytes 655360 | tf_op jit(solution)/shard_map/all_to_all | solution.py:582
  79.6 1.5 %shard_map.113 = bf16[128,2048]{1,0:T(8,128)(2,1)} custom-call(bf16[160,128]{1,0:T(8,128)(2,1)S(1)} %slice_bitcast_fusion.mine_ref, bf16[160,128]{1,0:T(8,128)(2,1)S(1)} %collective-permute-done.21.other_ref, bf16[1024,256]{1,0:T(8,128)(2,1)S(1)} %copy-done.25, bf16[64,1024]{1,0:T(8,128)(2,1)S(1)} %bitcast.67, bf16[1024,256]{1,0:T(8,128)(2,1)S(1)} %copy-done.27, ...), custom_call_target="tpu_custom_call" | custom-call | flops 3335000064 | bytes 1392640 | tf_op jit(solution)/shard_map/pallas_call | solution.py:54
  81.5 4.6 %all-to-all-done.refs_0_ = bf16[8,160,128]{2,1,0:T(8,128)(2,1)S(1)} async-done(((bf16[8,160,128]{2,1,0:T(8,128)(2,1)}), bf16[8,160,128]{2,1,0:T(8,128)(2,1)S(1)}, u32[]{:S(2)}, u32[]{:S(2)}) %all-to-all-start) | async-done | bytes 327712 | tf_op jit(solution)/shard_map/all_to_all | solution.py:582
  86.1 1.6 %collective-permute-done.22.refs_1_ = bf16[8,160,128]{2,1,0:T(8,128)(2,1)S(1)} collective-permute-done((bf16[8,160,128]{2,1,0:T(8,128)(2,1)S(1)}, bf16[8,160,128]{2,1,0:T(8,128)(2,1)S(1)}, u32[]{:S(2)}, u32[]{:S(2)}) %collective-permute-start.22) | collective-permute-done | bytes 327712 | tf_op jit(solution)/shard_map/ppermute | solution.py:21
  87.7 2.2 %shard_map.115 = (f32[1024,256]{1,0:T(8,128)}, f32[64,1024]{1,0:T(8,128)}) custom-call(bf16[2,512,1024]{2,1,0:T(8,128)(2,1)S(1)} %shard_map.114.tok_ref, bf16[8,160,128]{2,1,0:T(8,128)(2,1)S(1)} %all-to-all-done.refs_0_, bf16[8,160,128]{2,1,0:T(8,128)(2,1)S(1)} %collective-permute-done.22.refs_1_), custom_call_target="tpu_custom_call" | custom-call | flops 4600000000 | bytes 2752512 | tf_op jit(solution)/shard_map/pallas_call | solution.py:54
  (115 shorter events, 22.5 us)
Async XLA Ops:
  1.7 9.3 %collective-permute-start = (bf16[128,1024]{1,0:T(8,128)(2,1)S(1)}, bf16[128,1024]{1,0:T(8,128)(2,1)S(1)}, u32[]{:S(2)}, u32[]{:S(2)}) collective-permute-start(bf16[128,1024]{1,0:T(8,128)(2,1)S(1)} %get-tuple-element.68), channel_id=1, source_target_pairs={{0,2},{2,0},{1,3},{3,1},{4,6},{6,4},{5,7},{7,5},{8,10},{10,8},{9,1... | collective-permute-start | bytes 786440 | tf_op jit(solution)/shard_map/ppermute | solution.py:21
  4.7 10.7 %collective-permute-start.2 = (bf16[128,1024]{1,0:T(8,128)(2,1)S(1)}, bf16[128,1024]{1,0:T(8,128)(2,1)S(1)}, u32[]{:S(2)}, u32[]{:S(2)}) collective-permute-start(bf16[128,1024]{1,0:T(8,128)(2,1)S(1)} %get-tuple-element.115.a_ref.refs_0_), channel_id=1, source_target_pairs={{0,4},{4,0},{8,12},{12,8},{1,5},{5,1},{9,13},{13,9},{2,6},{6,2},{1... | collective-permute-start | bytes 786440 | tf_op jit(solution)/shard_map/ppermute | solution.py:398
  6.3 9.2 %collective-permute-start.3 = (bf16[128,1024]{1,0:T(8,128)(2,1)S(1)}, bf16[128,1024]{1,0:T(8,128)(2,1)S(1)}, u32[]{:S(2)}, u32[]{:S(2)}) collective-permute-start(bf16[128,1024]{1,0:T(8,128)(2,1)S(1)} %get-tuple-element.115.a_ref.refs_0_), channel_id=1, source_target_pairs={{0,0},{4,8},{8,4},{12,12},{1,1},{5,9},{9,5},{13,13},{2,2},{6,10},{... | collective-permute-start | bytes 786440 | tf_op jit(solution)/shard_map/ppermute | solution.py:398
  11.0 7.5 %collective-permute-start.4 = (bf16[128,1024]{1,0:T(8,128)(2,1)S(1)}, bf16[128,1024]{1,0:T(8,128)(2,1)S(1)}, u32[]{:S(2)}, u32[]{:S(2)}) collective-permute-start(bf16[128,1024]{1,0:T(8,128)(2,1)S(1)} %collective-permute-done.a_ref.refs_6_), channel_id=1, source_target_pairs={{0,4},{4,0},{8,12},{12,8},{1,5},{5,1},{9,13},{13,9},{2,6},{6,2},{1... | collective-permute-start | bytes 786440 | tf_op jit(solution)/shard_map/ppermute | solution.py:398
  13.2 5.4 %collective-permute-start.1 = (f32[320,128]{1,0:T(8,128)S(1)}, f32[320,128]{1,0:T(8,128)S(1)}, u32[]{:S(2)}, u32[]{:S(2)}) collective-permute-start(f32[320,128]{1,0:T(8,128)S(1)} %shard_map.104), channel_id=1, source_target_pairs={{0,2},{2,0},{1,3},{3,1},{4,6},{6,4},{5,7},{7,5},{8,10},{10,8},{9,1... | collective-permute-start | bytes 491528 | tf_op jit(solution)/shard_map/ppermute | solution.py:21
  14.7 8.1 %collective-permute-start.7 = (bf16[128,1024]{1,0:T(8,128)(2,1)S(1)}, bf16[128,1024]{1,0:T(8,128)(2,1)S(1)}, u32[]{:S(2)}, u32[]{:S(2)}) collective-permute-start(bf16[128,1024]{1,0:T(8,128)(2,1)S(1)} %collective-permute-done.a_ref.refs_6_), channel_id=1, source_target_pairs={{0,0},{4,8},{8,4},{12,12},{1,1},{5,9},{9,5},{13,13},{2,2},{6,10},{... | collective-permute-start | bytes 786440 | tf_op jit(solution)/shard_map/ppermute | solution.py:398
  15.4 3.8 %collective-permute-start.5 = (f32[320,128]{1,0:T(8,128)S(1)}, f32[320,128]{1,0:T(8,128)S(1)}, u32[]{:S(2)}, u32[]{:S(2)}) collective-permute-start(f32[320,128]{1,0:T(8,128)S(1)} %shard_map.103.refs_0_), channel_id=1, source_target_pairs={{0,1},{1,0},{2,3},{3,2},{4,5},{5,4},{6,7},{7,6},{8,9},{9,8},{10,11... | collective-permute-start | bytes 491528 | tf_op jit(solution)/shard_map/ppermute | solution.py:21
  19.2 1.4 %collective-permute-start.6 = (f32[320,128]{1,0:T(8,128)S(1)}, f32[320,128]{1,0:T(8,128)S(1)}, u32[]{:S(2)}, u32[]{:S(2)}) collective-permute-start(f32[320,128]{1,0:T(8,128)S(1)} %collective-permute-done.1.refs_1_), channel_id=1, source_target_pairs={{0,1},{1,0},{2,3},{3,2},{4,5},{5,4},{6,7},{7,6},{8,9},{9,8},{10,11... | collective-permute-start | bytes 491528 | tf_op jit(solution)/shard_map/ppermute | solution.py:21
  22.8 8.4 %collective-permute-start.8 = (bf16[128,1024]{1,0:T(8,128)(2,1)S(1)}, bf16[128,1024]{1,0:T(8,128)(2,1)S(1)}, u32[]{:S(2)}, u32[]{:S(2)}) collective-permute-start(bf16[128,1024]{1,0:T(8,128)(2,1)S(1)} %get-tuple-element.72), channel_id=1, source_target_pairs={{0,4},{4,0},{8,12},{12,8},{1,5},{5,1},{9,13},{13,9},{2,6},{6,2},{1... | collective-permute-start | bytes 786440 | tf_op jit(solution)/shard_map/ppermute | solution.py:425
  24.6 25.1 %collective-permute-start.13 = (bf16[128,1024]{1,0:T(8,128)(2,1)S(1)}, bf16[128,1024]{1,0:T(8,128)(2,1)S(1)}, u32[]{:S(2)}, u32[]{:S(2)}) collective-permute-start(bf16[128,1024]{1,0:T(8,128)(2,1)S(1)} %collective-permute-done.2.refs_1_), channel_id=1, source_target_pairs={{0,0},{4,8},{8,4},{12,12},{1,1},{5,9},{9,5},{13,13},{2,2},{6,10},{... | collective-permute-start | bytes 786440 | tf_op jit(solution)/shard_map/ppermute | solution.py:398
  31.4 6.2 %collective-permute-start.10 = (bf16[128,1024]{1,0:T(8,128)(2,1)S(1)}, bf16[128,1024]{1,0:T(8,128)(2,1)S(1)}, u32[]{:S(2)}, u32[]{:S(2)}) collective-permute-start(bf16[128,1024]{1,0:T(8,128)(2,1)S(1)} %fusion.3), channel_id=1, source_target_pairs={{0,0},{4,8},{8,4},{12,12},{1,1},{5,9},{9,5},{13,13},{2,2},{6,10},{... | collective-permute-start | bytes 786440 | tf_op jit(solution)/shard_map/ppermute | solution.py:425
  32.1 9.6 %collective-permute-start.9 = (bf16[128,1024]{1,0:T(8,128)(2,1)S(1)}, bf16[128,1024]{1,0:T(8,128)(2,1)S(1)}, u32[]{:S(2)}, u32[]{:S(2)}) collective-permute-start(bf16[128,1024]{1,0:T(8,128)(2,1)S(1)} %broadcast_select_fusion), channel_id=1, source_target_pairs={{0,4},{4,0},{8,12},{12,8},{1,5},{5,1},{9,13},{13,9},{2,6},{6,2},{1... | collective-permute-start | bytes 786440 | tf_op jit(solution)/shard_map/ppermute | solution.py:425
  42.0 7.8 %collective-permute-start.11 = (bf16[128,1024]{1,0:T(8,128)(2,1)S(1)}, bf16[128,1024]{1,0:T(8,128)(2,1)S(1)}, u32[]{:S(2)}, u32[]{:S(2)}) collective-permute-start(bf16[128,1024]{1,0:T(8,128)(2,1)S(1)} %get-tuple-element.131), channel_id=1, source_target_pairs={{0,0},{4,8},{8,4},{12,12},{1,1},{5,9},{9,5},{13,13},{2,2},{6,10},{... | collective-permute-start | bytes 786440 | tf_op jit(solution)/shard_map/ppermute | solution.py:425
  42.7 8.3 %collective-permute-start.12 = (bf16[128,1024]{1,0:T(8,128)(2,1)S(1)}, bf16[128,1024]{1,0:T(8,128)(2,1)S(1)}, u32[]{:S(2)}, u32[]{:S(2)}) collective-permute-start(bf16[128,1024]{1,0:T(8,128)(2,1)S(1)} %get-tuple-element.130), channel_id=1, source_target_pairs={{0,4},{4,0},{8,12},{12,8},{1,5},{5,1},{9,13},{13,9},{2,6},{6,2},{1... | collective-permute-start | bytes 786440 | tf_op jit(solution)/shard_map/ppermute | solution.py:425
  46.6 10.4 %collective-permute-start.17 = (bf16[64,1024]{1,0:T(8,128)(2,1)S(1)}, bf16[64,1024]{1,0:T(8,128)(2,1)S(1)}, u32[]{:S(2)}, u32[]{:S(2)}) collective-permute-start(bf16[64,1024]{1,0:T(8,128)(2,1)S(1)} %bitcast.66), channel_id=1, source_target_pairs={{0,2},{2,0},{1,3},{3,1},{4,6},{6,4},{5,7},{7,5},{8,10},{10,8},{9,1... | collective-permute-start | bytes 393224 | tf_op jit(solution)/shard_map/ppermute | solution.py:21
  47.9 12.8 %collective-permute-start.16 = (bf16[1024,256]{1,0:T(8,128)(2,1)S(1)}, bf16[1024,256]{1,0:T(8,128)(2,1)S(1)}, u32[]{:S(2)}, u32[]{:S(2)}) collective-permute-start(bf16[1024,256]{1,0:T(8,128)(2,1)S(1)} %copy-done.24), channel_id=1, source_target_pairs={{0,2},{2,0},{1,3},{3,1},{4,6},{6,4},{5,7},{7,5},{8,10},{10,8},{9,1... | collective-permute-start | bytes 1572872 | tf_op jit(solution)/shard_map/ppermute | solution.py:21
  51.1 9.7 %collective-permute-start.14 = (bf16[128,1024]{1,0:T(8,128)(2,1)S(1)}, bf16[128,1024]{1,0:T(8,128)(2,1)S(1)}, u32[]{:S(2)}, u32[]{:S(2)}) collective-permute-start(bf16[128,1024]{1,0:T(8,128)(2,1)S(1)} %fusion), channel_id=1, source_target_pairs={{0,4},{4,0},{8,12},{12,8},{1,5},{5,1},{9,13},{13,9},{2,6},{6,2},{1... | collective-permute-start | bytes 786440 | tf_op jit(solution)/shard_map/ppermute | solution.py:425
  53.4 7.4 %collective-permute-start.15 = (bf16[128,1024]{1,0:T(8,128)(2,1)S(1)}, bf16[128,1024]{1,0:T(8,128)(2,1)S(1)}, u32[]{:S(2)}, u32[]{:S(2)}) collective-permute-start(bf16[128,1024]{1,0:T(8,128)(2,1)S(1)} %copy-done.10), channel_id=1, source_target_pairs={{0,0},{4,8},{8,4},{12,12},{1,1},{5,9},{9,5},{13,13},{2,2},{6,10},{... | collective-permute-start | bytes 786440 | tf_op jit(solution)/shard_map/ppermute | solution.py:398
  60.8 7.7 %collective-permute-start.20 = (bf16[128,1024]{1,0:T(8,128)(2,1)S(1)}, bf16[128,1024]{1,0:T(8,128)(2,1)S(1)}, u32[]{:S(2)}, u32[]{:S(2)}) collective-permute-start(bf16[128,1024]{1,0:T(8,128)(2,1)S(1)} %collective-permute-done.15.refs_10_), channel_id=1, source_target_pairs={{0,4},{4,0},{8,12},{12,8},{1,5},{5,1},{9,13},{13,9},{2,6},{6,2},{1... | collective-permute-start | bytes 786440 | tf_op jit(solution)/shard_map/ppermute | solution.py:398
  61.8 9.5 %collective-permute-start.19 = (bf16[128,1024]{1,0:T(8,128)(2,1)S(1)}, bf16[128,1024]{1,0:T(8,128)(2,1)S(1)}, u32[]{:S(2)}, u32[]{:S(2)}) collective-permute-start(bf16[128,1024]{1,0:T(8,128)(2,1)S(1)} %collective-permute-done.13.refs_4_), channel_id=1, source_target_pairs={{0,4},{4,0},{8,12},{12,8},{1,5},{5,1},{9,13},{13,9},{2,6},{6,2},{1... | collective-permute-start | bytes 786440 | tf_op jit(solution)/shard_map/ppermute | solution.py:398
  64.7 1.3 %collective-permute-start.18 = (f32[128,128]{1,0:T(8,128)S(1)}, f32[128,128]{1,0:T(8,128)S(1)}, u32[]{:S(2)}, u32[]{:S(2)}) collective-permute-start(f32[128,128]{1,0:T(8,128)S(1)} %get-tuple-element.111), channel_id=1, source_target_pairs={{0,1},{1,0},{2,3},{3,2},{4,5},{5,4},{6,7},{7,6},{8,9},{9,8},{10,11... | collective-permute-start | bytes 196616 | tf_op jit(solution)/shard_map/ppermute | solution.py:21
  72.8 13.3 %all-to-all-start = ((bf16[8,160,128]{2,1,0:T(8,128)(2,1)}), bf16[8,160,128]{2,1,0:T(8,128)(2,1)S(1)}, u32[]{:S(2)}, u32[]{:S(2)}) async-start(bf16[8,160,128]{2,1,0:T(8,128)(2,1)} %shard_map.112), calls=%async_computation | async-start | bytes 655360 | tf_op jit(solution)/shard_map/all_to_all | solution.py:582
  78.3 1.3 %collective-permute-start.21 = (bf16[160,128]{1,0:T(8,128)(2,1)S(1)}, bf16[160,128]{1,0:T(8,128)(2,1)S(1)}, u32[]{:S(2)}, u32[]{:S(2)}) collective-permute-start(bf16[160,128]{1,0:T(8,128)(2,1)S(1)} %slice_bitcast_fusion.mine_ref), channel_id=1, source_target_pairs={{0,1},{1,0},{2,3},{3,2},{4,5},{5,4},{6,7},{7,6},{8,9},{9,8},{10,11... | collective-permute-start | bytes 122888 | tf_op jit(solution)/shard_map/ppermute | solution.py:21
  86.1 1.6 %collective-permute-start.22 = (bf16[8,160,128]{2,1,0:T(8,128)(2,1)S(1)}, bf16[8,160,128]{2,1,0:T(8,128)(2,1)S(1)}, u32[]{:S(2)}, u32[]{:S(2)}) collective-permute-start(bf16[8,160,128]{2,1,0:T(8,128)(2,1)S(1)} %all-to-all-done.refs_0_), channel_id=1, source_target_pairs={{0,1},{1,0},{2,3},{3,2},{4,5},{5,4},{6,7},{7,6},{8,9},{9,8},{10,11... | collective-permute-start | bytes 983048 | tf_op jit(solution)/shard_map/ppermute | solution.py:21
  (32 other events, 190.2 us)

commit v17 on v15

--- a/solution.py
+++ b/solution.py
@@ -474,15 +474,14 @@
     ride = n_seq == 4 and all(a.shape == (state_n, step) for a in groups)
     second = [(kind, hop) for kind, hop in slots if hop == 2 and not (ride and kind == 0)]
     near = relay(found[0], groups[0], slots[:2])
-    partials = [project(items[0], w_bc, w_dt)]
+    partials, local = [project(items[0], w_bc, w_dt)], []
     for r in range(1, n_dp):
         item = after(items[r], partials[0])
-        partials.append(cyclic(project(item, w_bc, w_dt), "dp", -r))
-    if n_dp > 1:
-        near += relay(found[1], groups[1], slots[: 1 if ride else 2])
+        local.append(project(item, w_bc, w_dt))
+        partials.append(cyclic(local[-1], "dp", -r))
+    spare = relay(found[1], groups[1], slots[:2], *local) if n_dp > 1 else []
     partials[1:] = [after(a, *near) for a in partials[1:]]
     proj = partials + [cyclic(a, "head", 1) for a in partials]
-    spare = relay(found[1], groups[1], [(1, 1)]) if ride and n_dp > 1 else []
     own, bc, hp, *outs = call(
         functools.partial(state_kernel, 2 * n_dp, size, int(ride)),
         (
@@ -570,7 +569,18 @@
             aliases={len(inputs) - 2: 0} if k > 0 else {},
         )
     keep, give = back
-    taken = after(cyclic(give, "head", 1), *[a for d in done for a in d])
+    toks = []
+    for f, a in zip(found, groups):
+        toks += [a] + [f[step] for step in slots]
+    slots = [(0, 0)] + slots
+    ordered = call(
+        functools.partial(order_kernel, n_dp, n_seq, slots),
+        struct((n_dp, n_seq * rows, part), BF),
+        1.0,
+        *toks,
+        scratch=[pltpu.SemaphoreType.DMA((n_dp, len(slots)))],
+    )
+    taken = after(cyclic(give, "head", 1), ordered)
     count = n_dp * n_seq
     copies = call(low_kernel, struct((count, rows + heads, rows), BF), 1.2, keep, taken)
     mine = copies[0]
@@ -584,18 +594,7 @@
         other,
         *weights,
     )
-    toks = []
-    for f, a in zip(found, groups):
-        toks += [a] + [f[step] for step in slots]
-    slots = [(0, 0)] + slots
-    ordered = call(
-        functools.partial(order_kernel, n_dp, n_seq, slots),
-        struct((n_dp, n_seq * rows, part), BF),
-        1.0,
-        *after(tuple(toks), grads),
-        scratch=[pltpu.SemaphoreType.DMA((n_dp, len(slots)))],
-    )
-    lows = after(lows, grads, ordered)
+    lows = after(lows, grads)
     swapped = cyclic(lows, "head", 1)
     cols = 2 * (rows + heads)
     grad_bc, grad_dt = call(

time: 89.1 us -> 86.6 us (0.972)
  waiting for transfers between devices: 31.8 us -> 29.2 us
    ppermute x9, waiting for transfers between devices: 12.2 us -> 9.22 us  [cyclic(): return lax.ppermute(a, axis, [(i, (i + by) % count) for i in range(count)])]
    ppermute x6, starting transfers between devices: 13.9 us -> 16.2 us  [chains(): got[k] = lax.ppermute(value, 'seq', sorted(to.items()))]
    ppermute x8, starting transfers between devices: 10.2 us -> 8.9 us  [relay(): found[kind, hop] = lax.ppermute(source, 'seq', pairs[kind])]
    all_to_all x1, waiting for transfers between devices: 4.58 us -> 3.32 us  [body(): lows = lax.all_to_all(copies, ('seq', 'dp'), 0, 0, tiled=True)]
    ppermute x8, waiting for transfers between devices: 4.16 us -> 5.4 us  [relay(): found[kind, hop] = lax.ppermute(source, 'seq', pairs[kind])]
    unnamed x62 -> x30, local copies, waits for them, and re-layouts: 3.3 us -> 2.91 us
where the time goes in v17:
time: 86.6 us; the launch traced here: 86.1 us
  starting transfers between devices  36.3 us (42%)
  waiting for transfers between devices  29.2 us (34%)
  Pallas kernels  15 us (17%)
  local copies, waits for them, and re-layouts  4.02 us (5%)
  between operations  0.99 us (1%)
    ppermute x6, starting transfers between devices, chains(): got[k] = lax.ppermute(value, 'seq', sorted(to.items()))  16.2 us
    pallas_call x14, Pallas kernels, call(): pl.pallas_call(kernel, out_shape=out_shape, grid=(1,), in_specs=specs or...  15 us
    ppermute x6, waiting for transfers between devices, chains(): got[k] = lax.ppermute(value, 'seq', sorted(to.items()))  11.3 us
    ppermute x9, waiting for transfers between devices, cyclic(): return lax.ppermute(a, axis, [(i, (i + by) % count) for i in range(count)])  9.22 us
    ppermute x8, starting transfers between devices, relay(): found[kind, hop] = lax.ppermute(source, 'seq', pairs[kind])  8.9 us
    ppermute x9, starting transfers between devices, cyclic(): return lax.ppermute(a, axis, [(i, (i + by) % count) for i in range(count)])  6.98 us
    ppermute x8, waiting for transfers between devices, relay(): found[kind, hop] = lax.ppermute(source, 'seq', pairs[kind])  5.4 us
    all_to_all x1, starting transfers between devices, body(): lows = lax.all_to_all(copies, ('seq', 'dp'), 0, 0, tiled=True)  4.17 us
  transfers between devices with their start and end apart: 24, of which 13 were waited for; matrix products, arithmetic and copies ran while one was open for 2% of the time, Pallas kernels for 14%

profile of v17, /device:TPU:0, one launch (start us, length us, event | category | flops | bytes accessed | tf_op | source)
XLA Modules:
  0.0 86.1 jit_solution(2138349444610355729)
XLA Ops:
  1.7 3.0 %collective-permute-start = (bf16[128,1024]{1,0:T(8,128)(2,1)S(1)}, bf16[128,1024]{1,0:T(8,128)(2,1)S(1)}, u32[]{:S(2)}, u32[]{:S(2)}) collective-permute-start(bf16[128,1024]{1,0:T(8,128)(2,1)S(1)} %get-tuple-element.57), channel_id=1, source_target_pairs={{0,2},{2,0},{1,3},{3,1},{4,6},{6,4},{5,7},{7,5},{8,10},{10,8},{9,1... | collective-permute-start | bytes 786440 | tf_op jit(solution)/shard_map/ppermute | solution.py:21
  4.7 1.6 %collective-permute-start.2 = (bf16[128,1024]{1,0:T(8,128)(2,1)S(1)}, bf16[128,1024]{1,0:T(8,128)(2,1)S(1)}, u32[]{:S(2)}, u32[]{:S(2)}) collective-permute-start(bf16[128,1024]{1,0:T(8,128)(2,1)S(1)} %get-tuple-element.56.a_ref.refs_0_), channel_id=1, source_target_pairs={{0,4},{4,0},{8,12},{12,8},{1,5},{5,1},{9,13},{13,9},{2,6},{6,2},{1... | collective-permute-start | bytes 786440 | tf_op jit(solution)/shard_map/ppermute | solution.py:398
  7.3 3.7 %collective-permute-done.a_ref.refs_6_ = bf16[128,1024]{1,0:T(8,128)(2,1)S(1)} collective-permute-done((bf16[128,1024]{1,0:T(8,128)(2,1)S(1)}, bf16[128,1024]{1,0:T(8,128)(2,1)S(1)}, u32[]{:S(2)}, u32[]{:S(2)}) %collective-permute-start) | collective-permute-done | bytes 262176 | tf_op jit(solution)/shard_map/ppermute | solution.py:21
  11.3 1.8 %collective-permute-start.1 = (f32[320,128]{1,0:T(8,128)S(1)}, f32[320,128]{1,0:T(8,128)S(1)}, u32[]{:S(2)}, u32[]{:S(2)}) collective-permute-start(f32[320,128]{1,0:T(8,128)S(1)} %shard_map.104), channel_id=1, source_target_pairs={{0,2},{2,0},{1,3},{3,1},{4,6},{6,4},{5,7},{7,5},{8,10},{10,8},{9,1... | collective-permute-start | bytes 491528 | tf_op jit(solution)/shard_map/ppermute | solution.py:21
  13.1 1.6 %collective-permute-start.6 = (bf16[128,1024]{1,0:T(8,128)(2,1)S(1)}, bf16[128,1024]{1,0:T(8,128)(2,1)S(1)}, u32[]{:S(2)}, u32[]{:S(2)}) collective-permute-start(bf16[128,1024]{1,0:T(8,128)(2,1)S(1)} %collective-permute-done.a_ref.refs_6_), channel_id=1, source_target_pairs={{0,4},{4,0},{8,12},{12,8},{1,5},{5,1},{9,13},{13,9},{2,6},{6,2},{1... | collective-permute-start | bytes 786440 | tf_op jit(solution)/shard_map/ppermute | solution.py:398
  18.2 2.1 %shard_map.105 = (f32[2,2,128,1024]{3,2,1,0:T(8,128)S(1)}, f32[256,128]{1,0:T(8,128)S(1)}, f32[160,128]{1,0:T(8,128)S(1)}, bf16[128,1024]{1,0:T(8,128)(2,1)S(1)}...) custom-call(f32[320,128]{1,0:T(8,128)S(1)} %shard_map.103.refs_0_, ...), custom_call_target="tpu_custom_call" | custom-call | flops 115000000 | bytes 1966336 | tf_op jit(solution)/shard_map/pallas_call | solution.py:54
  20.4 4.2 %collective-permute-start.8 = (bf16[128,1024]{1,0:T(8,128)(2,1)S(1)}, bf16[128,1024]{1,0:T(8,128)(2,1)S(1)}, u32[]{:S(2)}, u32[]{:S(2)}) collective-permute-start(bf16[128,1024]{1,0:T(8,128)(2,1)S(1)} %get-tuple-element.62), channel_id=1, source_target_pairs={{0,4},{4,0},{8,12},{12,8},{1,5},{5,1},{9,13},{13,9},{2,6},{6,2},{1... | collective-permute-start | bytes 786440 | tf_op jit(solution)/shard_map/ppermute | solution.py:425
  28.4 2.1 %collective-permute-done.8.refs_3_ = bf16[128,1024]{1,0:T(8,128)(2,1)S(1)} collective-permute-done((bf16[128,1024]{1,0:T(8,128)(2,1)S(1)}, bf16[128,1024]{1,0:T(8,128)(2,1)S(1)}, u32[]{:S(2)}, u32[]{:S(2)}) %collective-permute-start.8) | collective-permute-done | bytes 262176 | tf_op jit(solution)/shard_map/ppermute | solution.py:425
  31.4 3.5 %collective-permute-start.9 = (bf16[128,1024]{1,0:T(8,128)(2,1)S(1)}, bf16[128,1024]{1,0:T(8,128)(2,1)S(1)}, u32[]{:S(2)}, u32[]{:S(2)}) collective-permute-start(bf16[128,1024]{1,0:T(8,128)(2,1)S(1)} %broadcast_select_fusion), channel_id=1, source_target_pairs={{0,4},{4,0},{8,12},{12,8},{1,5},{5,1},{9,13},{13,9},{2,6},{6,2},{1... | collective-permute-start | bytes 786440 | tf_op jit(solution)/shard_map/ppermute | solution.py:425
  35.9 3.5 %collective-permute-done.9.refs_9_ = bf16[128,1024]{1,0:T(8,128)(2,1)S(1)} collective-permute-done((bf16[128,1024]{1,0:T(8,128)(2,1)S(1)}, bf16[128,1024]{1,0:T(8,128)(2,1)S(1)}, u32[]{:S(2)}, u32[]{:S(2)}) %collective-permute-start.9) | collective-permute-done | bytes 262176 | tf_op jit(solution)/shard_map/ppermute | solution.py:425
  40.4 4.8 %collective-permute-start.12 = (bf16[128,1024]{1,0:T(8,128)(2,1)S(1)}, bf16[128,1024]{1,0:T(8,128)(2,1)S(1)}, u32[]{:S(2)}, u32[]{:S(2)}) collective-permute-start(bf16[128,1024]{1,0:T(8,128)(2,1)S(1)} %get-tuple-element.108), channel_id=1, source_target_pairs={{0,4},{4,0},{8,12},{12,8},{1,5},{5,1},{9,13},{13,9},{2,6},{6,2},{1... | collective-permute-start | bytes 786440 | tf_op jit(solution)/shard_map/ppermute | solution.py:425
  46.3 3.9 %collective-permute-done.12 = bf16[128,1024]{1,0:T(8,128)(2,1)S(1)} collective-permute-done((bf16[128,1024]{1,0:T(8,128)(2,1)S(1)}, bf16[128,1024]{1,0:T(8,128)(2,1)S(1)}, u32[]{:S(2)}, u32[]{:S(2)}) %collective-permute-start.12) | collective-permute-done | bytes 262176 | tf_op jit(solution)/shard_map/ppermute | solution.py:425
  50.3 2.4 %collective-permute-start.16 = (bf16[128,1024]{1,0:T(8,128)(2,1)S(1)}, bf16[128,1024]{1,0:T(8,128)(2,1)S(1)}, u32[]{:S(2)}, u32[]{:S(2)}) collective-permute-start(bf16[128,1024]{1,0:T(8,128)(2,1)S(1)} %fusion), channel_id=1, source_target_pairs={{0,4},{4,0},{8,12},{12,8},{1,5},{5,1},{9,13},{13,9},{2,6},{6,2},{1... | collective-permute-start | bytes 786440 | tf_op jit(solution)/shard_map/ppermute | solution.py:425
  53.4 1.9 %shard_map.110 = (bf16[128,2048]{1,0:T(8,128)(2,1)}, f32[272,128]{1,0:T(8,128)S(1)}) custom-call(bf16[3,128,1024]{2,1,0:T(8,128)(2,1)S(1)} %bitcast_dynamic-update-slice_fusion.refs_0_, bf16[128,2048]{1,0:T(8,128)(2,1)S(1)} %bitcast.45, bf16[128,2048]{1,0:T(8,128)(2,1)S(1)} %bitcast.52, f32[256,128]{1,0:T(8,128)S(1)} %get-tuple-element.86.bc_ref.refs_3_, ...), custom_call_target="tpu_custom_call" | custom-call | flops 3104999936 | bytes 2719872 | tf_op jit(solution)/shard_map/pallas_call | solution.py:54
  56.3 1.8 %collective-permute-done.16 = bf16[128,1024]{1,0:T(8,128)(2,1)S(1)} collective-permute-done((bf16[128,1024]{1,0:T(8,128)(2,1)S(1)}, bf16[128,1024]{1,0:T(8,128)(2,1)S(1)}, u32[]{:S(2)}, u32[]{:S(2)}) %collective-permute-start.16) | collective-permute-done | bytes 262176 | tf_op jit(solution)/shard_map/ppermute | solution.py:425
  58.1 3.0 %collective-permute-start.20 = (bf16[128,1024]{1,0:T(8,128)(2,1)S(1)}, bf16[128,1024]{1,0:T(8,128)(2,1)S(1)}, u32[]{:S(2)}, u32[]{:S(2)}) collective-permute-start(bf16[128,1024]{1,0:T(8,128)(2,1)S(1)} %collective-permute-done.17.refs_10_), channel_id=1, source_target_pairs={{0,4},{4,0},{8,12},{12,8},{1,5},{5,1},{9,13},{13,9},{2,6},{6,2},{1... | collective-permute-start | bytes 786440 | tf_op jit(solution)/shard_map/ppermute | solution.py:398
  61.2 1.7 %shard_map.111 = (bf16[128,2048]{1,0:T(8,128)(2,1)}, f32[160,128]{1,0:T(8,128)S(1)}, f32[128,128]{1,0:T(8,128)S(1)}) custom-call(bf16[3,128,1024]{2,1,0:T(8,128)(2,1)S(1)} %bitcast_dynamic-update-slice_fusion.3.refs_0_, bf16[128,2048]{1,0:T(8,128)(2,1)S(1)} %bitcast.47, bf16[128,2048]{1,0:T(8,128)(2,1)S(1)} %bitcast.54, ...), custom_call_target="tpu_custom_call", output_to_operand_aliasing={{0}: (12, {})} | custom-call | flops 3104999936 | bytes 3383424 | tf_op jit(solution)/shard_map/pallas_call | solution.py:54
  62.9 2.6 %collective-permute-done.20.refs_11_ = bf16[128,1024]{1,0:T(8,128)(2,1)S(1)} collective-permute-done((bf16[128,1024]{1,0:T(8,128)(2,1)S(1)}, bf16[128,1024]{1,0:T(8,128)(2,1)S(1)}, u32[]{:S(2)}, u32[]{:S(2)}) %collective-permute-start.20) | collective-permute-done | bytes 262176 | tf_op jit(solution)/shard_map/ppermute | solution.py:398
  65.5 2.8 %collective-permute-done.19.refs_5_ = bf16[128,1024]{1,0:T(8,128)(2,1)S(1)} collective-permute-done((bf16[128,1024]{1,0:T(8,128)(2,1)S(1)}, bf16[128,1024]{1,0:T(8,128)(2,1)S(1)}, u32[]{:S(2)}, u32[]{:S(2)}) %collective-permute-start.19) | collective-permute-done | bytes 262176 | tf_op jit(solution)/shard_map/ppermute | solution.py:398
  69.4 4.2 %all-to-all-start = ((bf16[8,160,128]{2,1,0:T(8,128)(2,1)}), bf16[8,160,128]{2,1,0:T(8,128)(2,1)S(1)}, u32[]{:S(2)}, u32[]{:S(2)}) async-start(bf16[8,160,128]{2,1,0:T(8,128)(2,1)} %shard_map.113), calls=%async_computation | async-start | bytes 655360 | tf_op jit(solution)/shard_map/all_to_all | solution.py:587
  77.4 1.5 %shard_map.114 = bf16[128,2048]{1,0:T(8,128)(2,1)} custom-call(bf16[160,128]{1,0:T(8,128)(2,1)S(1)} %slice_bitcast_fusion.mine_ref, bf16[160,128]{1,0:T(8,128)(2,1)S(1)} %collective-permute-done.21.other_ref, bf16[1024,256]{1,0:T(8,128)(2,1)S(1)} %copy-done.8, bf16[64,1024]{1,0:T(8,128)(2,1)S(1)} %bitcast.67, bf16[1024,256]{1,0:T(8,128)(2,1)S(1)} %copy-done.10, ...), custom_call_target="tpu_custom_call" | custom-call | flops 3335000064 | bytes 1392640 | tf_op jit(solution)/shard_map/pallas_call | solution.py:54
  78.9 3.3 %all-to-all-done.refs_0_ = bf16[8,160,128]{2,1,0:T(8,128)(2,1)S(1)} async-done(((bf16[8,160,128]{2,1,0:T(8,128)(2,1)}), bf16[8,160,128]{2,1,0:T(8,128)(2,1)S(1)}, u32[]{:S(2)}, u32[]{:S(2)}) %all-to-all-start) | async-done | bytes 327712 | tf_op jit(solution)/shard_map/all_to_all | solution.py:587
  82.2 1.6 %collective-permute-done.22.refs_1_ = bf16[8,160,128]{2,1,0:T(8,128)(2,1)S(1)} collective-permute-done((bf16[8,160,128]{2,1,0:T(8,128)(2,1)S(1)}, bf16[8,160,128]{2,1,0:T(8,128)(2,1)S(1)}, u32[]{:S(2)}, u32[]{:S(2)}) %collective-permute-start.22) | collective-permute-done | bytes 327712 | tf_op jit(solution)/shard_map/ppermute | solution.py:21
  83.9 2.2 %shard_map.115 = (f32[1024,256]{1,0:T(8,128)}, f32[64,1024]{1,0:T(8,128)}) custom-call(bf16[2,512,1024]{2,1,0:T(8,128)(2,1)S(1)} %shard_map.112.tok_ref, bf16[8,160,128]{2,1,0:T(8,128)(2,1)S(1)} %all-to-all-done.refs_0_, bf16[8,160,128]{2,1,0:T(8,128)(2,1)S(1)} %collective-permute-done.22.refs_1_), custom_call_target="tpu_custom_call" | custom-call | flops 4600000000 | bytes 2752512 | tf_op jit(solution)/shard_map/pallas_call | solution.py:54
  (81 shorter events, 20.2 us)
Async XLA Ops:
  1.7 9.3 %collective-permute-start = (bf16[128,1024]{1,0:T(8,128)(2,1)S(1)}, bf16[128,1024]{1,0:T(8,128)(2,1)S(1)}, u32[]{:S(2)}, u32[]{:S(2)}) collective-permute-start(bf16[128,1024]{1,0:T(8,128)(2,1)S(1)} %get-tuple-element.57), channel_id=1, source_target_pairs={{0,2},{2,0},{1,3},{3,1},{4,6},{6,4},{5,7},{7,5},{8,10},{10,8},{9,1... | collective-permute-start | bytes 786440 | tf_op jit(solution)/shard_map/ppermute | solution.py:21
  4.7 10.7 %collective-permute-start.2 = (bf16[128,1024]{1,0:T(8,128)(2,1)S(1)}, bf16[128,1024]{1,0:T(8,128)(2,1)S(1)}, u32[]{:S(2)}, u32[]{:S(2)}) collective-permute-start(bf16[128,1024]{1,0:T(8,128)(2,1)S(1)} %get-tuple-element.56.a_ref.refs_0_), channel_id=1, source_target_pairs={{0,4},{4,0},{8,12},{12,8},{1,5},{5,1},{9,13},{13,9},{2,6},{6,2},{1... | collective-permute-start | bytes 786440 | tf_op jit(solution)/shard_map/ppermute | solution.py:398
  6.3 9.2 %collective-permute-start.3 = (bf16[128,1024]{1,0:T(8,128)(2,1)S(1)}, bf16[128,1024]{1,0:T(8,128)(2,1)S(1)}, u32[]{:S(2)}, u32[]{:S(2)}) collective-permute-start(bf16[128,1024]{1,0:T(8,128)(2,1)S(1)} %get-tuple-element.56.a_ref.refs_0_), channel_id=1, source_target_pairs={{0,0},{4,8},{8,4},{12,12},{1,1},{5,9},{9,5},{13,13},{2,2},{6,10},{... | collective-permute-start | bytes 786440 | tf_op jit(solution)/shard_map/ppermute | solution.py:398
  11.3 5.5 %collective-permute-start.1 = (f32[320,128]{1,0:T(8,128)S(1)}, f32[320,128]{1,0:T(8,128)S(1)}, u32[]{:S(2)}, u32[]{:S(2)}) collective-permute-start(f32[320,128]{1,0:T(8,128)S(1)} %shard_map.104), channel_id=1, source_target_pairs={{0,2},{2,0},{1,3},{3,1},{4,6},{6,4},{5,7},{7,5},{8,10},{10,8},{9,1... | collective-permute-start | bytes 491528 | tf_op jit(solution)/shard_map/ppermute | solution.py:21
  13.1 7.2 %collective-permute-start.6 = (bf16[128,1024]{1,0:T(8,128)(2,1)S(1)}, bf16[128,1024]{1,0:T(8,128)(2,1)S(1)}, u32[]{:S(2)}, u32[]{:S(2)}) collective-permute-start(bf16[128,1024]{1,0:T(8,128)(2,1)S(1)} %collective-permute-done.a_ref.refs_6_), channel_id=1, source_target_pairs={{0,4},{4,0},{8,12},{12,8},{1,5},{5,1},{9,13},{13,9},{2,6},{6,2},{1... | collective-permute-start | bytes 786440 | tf_op jit(solution)/shard_map/ppermute | solution.py:398
  14.7 5.7 %collective-permute-start.7 = (bf16[128,1024]{1,0:T(8,128)(2,1)S(1)}, bf16[128,1024]{1,0:T(8,128)(2,1)S(1)}, u32[]{:S(2)}, u32[]{:S(2)}) collective-permute-start(bf16[128,1024]{1,0:T(8,128)(2,1)S(1)} %collective-permute-done.a_ref.refs_6_), channel_id=1, source_target_pairs={{0,0},{4,8},{8,4},{12,12},{1,1},{5,9},{9,5},{13,13},{2,2},{6,10},{... | collective-permute-start | bytes 786440 | tf_op jit(solution)/shard_map/ppermute | solution.py:398
  15.4 1.5 %collective-permute-start.4 = (f32[320,128]{1,0:T(8,128)S(1)}, f32[320,128]{1,0:T(8,128)S(1)}, u32[]{:S(2)}, u32[]{:S(2)}) collective-permute-start(f32[320,128]{1,0:T(8,128)S(1)} %shard_map.103.refs_0_), channel_id=1, source_target_pairs={{0,1},{1,0},{2,3},{3,2},{4,5},{5,4},{6,7},{7,6},{8,9},{9,8},{10,11... | collective-permute-start | bytes 491528 | tf_op jit(solution)/shard_map/ppermute | solution.py:21
  16.8 1.4 %collective-permute-start.5 = (f32[320,128]{1,0:T(8,128)S(1)}, f32[320,128]{1,0:T(8,128)S(1)}, u32[]{:S(2)}, u32[]{:S(2)}) collective-permute-start(f32[320,128]{1,0:T(8,128)S(1)} %collective-permute-done.1.refs_1_), channel_id=1, source_target_pairs={{0,1},{1,0},{2,3},{3,2},{4,5},{5,4},{6,7},{7,6},{8,9},{9,8},{10,11... | collective-permute-start | bytes 491528 | tf_op jit(solution)/shard_map/ppermute | solution.py:21
  20.4 10.1 %collective-permute-start.8 = (bf16[128,1024]{1,0:T(8,128)(2,1)S(1)}, bf16[128,1024]{1,0:T(8,128)(2,1)S(1)}, u32[]{:S(2)}, u32[]{:S(2)}) collective-permute-start(bf16[128,1024]{1,0:T(8,128)(2,1)S(1)} %get-tuple-element.62), channel_id=1, source_target_pairs={{0,4},{4,0},{8,12},{12,8},{1,5},{5,1},{9,13},{13,9},{2,6},{6,2},{1... | collective-permute-start | bytes 786440 | tf_op jit(solution)/shard_map/ppermute | solution.py:425
  24.6 21.6 %collective-permute-start.15 = (bf16[128,1024]{1,0:T(8,128)(2,1)S(1)}, bf16[128,1024]{1,0:T(8,128)(2,1)S(1)}, u32[]{:S(2)}, u32[]{:S(2)}) collective-permute-start(bf16[128,1024]{1,0:T(8,128)(2,1)S(1)} %collective-permute-done.2.refs_1_), channel_id=1, source_target_pairs={{0,0},{4,8},{8,4},{12,12},{1,1},{5,9},{9,5},{13,13},{2,2},{6,10},{... | collective-permute-start | bytes 786440 | tf_op jit(solution)/shard_map/ppermute | solution.py:398
  25.3 20.9 %collective-permute-start.14 = (bf16[64,1024]{1,0:T(8,128)(2,1)S(1)}, bf16[64,1024]{1,0:T(8,128)(2,1)S(1)}, u32[]{:S(2)}, u32[]{:S(2)}) collective-permute-start(bf16[64,1024]{1,0:T(8,128)(2,1)S(1)} %bitcast.66), channel_id=1, source_target_pairs={{0,2},{2,0},{1,3},{3,1},{4,6},{6,4},{5,7},{7,5},{8,10},{10,8},{9,1... | collective-permute-start | bytes 393224 | tf_op jit(solution)/shard_map/ppermute | solution.py:21
  25.9 20.4 %collective-permute-start.13 = (bf16[1024,256]{1,0:T(8,128)(2,1)}, bf16[1024,256]{1,0:T(8,128)(2,1)S(1)}, u32[]{:S(2)}, u32[]{:S(2)}) collective-permute-start(bf16[1024,256]{1,0:T(8,128)(2,1)} %refs_0_.1), channel_id=1, source_target_pairs={{0,2},{2,0},{1,3},{3,1},{4,6},{6,4},{5,7},{7,5},{8,10},{10,8},{9,1... | collective-permute-start | bytes 1572872 | tf_op jit(solution)/shard_map/ppermute | solution.py:21
  30.6 5.3 %collective-permute-start.10 = (bf16[128,1024]{1,0:T(8,128)(2,1)S(1)}, bf16[128,1024]{1,0:T(8,128)(2,1)S(1)}, u32[]{:S(2)}, u32[]{:S(2)}) collective-permute-start(bf16[128,1024]{1,0:T(8,128)(2,1)S(1)} %fusion.3), channel_id=1, source_target_pairs={{0,0},{4,8},{8,4},{12,12},{1,1},{5,9},{9,5},{13,13},{2,2},{6,10},{... | collective-permute-start | bytes 786440 | tf_op jit(solution)/shard_map/ppermute | solution.py:425
  31.4 8.0 %collective-permute-start.9 = (bf16[128,1024]{1,0:T(8,128)(2,1)S(1)}, bf16[128,1024]{1,0:T(8,128)(2,1)S(1)}, u32[]{:S(2)}, u32[]{:S(2)}) collective-permute-start(bf16[128,1024]{1,0:T(8,128)(2,1)S(1)} %broadcast_select_fusion), channel_id=1, source_target_pairs={{0,4},{4,0},{8,12},{12,8},{1,5},{5,1},{9,13},{13,9},{2,6},{6,2},{1... | collective-permute-start | bytes 786440 | tf_op jit(solution)/shard_map/ppermute | solution.py:425
  39.7 6.6 %collective-permute-start.11 = (bf16[128,1024]{1,0:T(8,128)(2,1)S(1)}, bf16[128,1024]{1,0:T(8,128)(2,1)S(1)}, u32[]{:S(2)}, u32[]{:S(2)}) collective-permute-start(bf16[128,1024]{1,0:T(8,128)(2,1)S(1)} %get-tuple-element.109), channel_id=1, source_target_pairs={{0,0},{4,8},{8,4},{12,12},{1,1},{5,9},{9,5},{13,13},{2,2},{6,10},{... | collective-permute-start | bytes 786440 | tf_op jit(solution)/shard_map/ppermute | solution.py:425
  40.4 9.8 %collective-permute-start.12 = (bf16[128,1024]{1,0:T(8,128)(2,1)S(1)}, bf16[128,1024]{1,0:T(8,128)(2,1)S(1)}, u32[]{:S(2)}, u32[]{:S(2)}) collective-permute-start(bf16[128,1024]{1,0:T(8,128)(2,1)S(1)} %get-tuple-element.108), channel_id=1, source_target_pairs={{0,4},{4,0},{8,12},{12,8},{1,5},{5,1},{9,13},{13,9},{2,6},{6,2},{1... | collective-permute-start | bytes 786440 | tf_op jit(solution)/shard_map/ppermute | solution.py:425
  50.3 7.7 %collective-permute-start.16 = (bf16[128,1024]{1,0:T(8,128)(2,1)S(1)}, bf16[128,1024]{1,0:T(8,128)(2,1)S(1)}, u32[]{:S(2)}, u32[]{:S(2)}) collective-permute-start(bf16[128,1024]{1,0:T(8,128)(2,1)S(1)} %fusion), channel_id=1, source_target_pairs={{0,4},{4,0},{8,12},{12,8},{1,5},{5,1},{9,13},{13,9},{2,6},{6,2},{1... | collective-permute-start | bytes 786440 | tf_op jit(solution)/shard_map/ppermute | solution.py:425
  52.7 3.6 %collective-permute-start.17 = (bf16[128,1024]{1,0:T(8,128)(2,1)S(1)}, bf16[128,1024]{1,0:T(8,128)(2,1)S(1)}, u32[]{:S(2)}, u32[]{:S(2)}) collective-permute-start(bf16[128,1024]{1,0:T(8,128)(2,1)S(1)} %collective-permute-done.6.refs_7_), channel_id=1, source_target_pairs={{0,0},{4,8},{8,4},{12,12},{1,1},{5,9},{9,5},{13,13},{2,2},{6,10},{... | collective-permute-start | bytes 786440 | tf_op jit(solution)/shard_map/ppermute | solution.py:398
  58.1 7.4 %collective-permute-start.20 = (bf16[128,1024]{1,0:T(8,128)(2,1)S(1)}, bf16[128,1024]{1,0:T(8,128)(2,1)S(1)}, u32[]{:S(2)}, u32[]{:S(2)}) collective-permute-start(bf16[128,1024]{1,0:T(8,128)(2,1)S(1)} %collective-permute-done.17.refs_10_), channel_id=1, source_target_pairs={{0,4},{4,0},{8,12},{12,8},{1,5},{5,1},{9,13},{13,9},{2,6},{6,2},{1... | collective-permute-start | bytes 786440 | tf_op jit(solution)/shard_map/ppermute | solution.py:398
  61.1 7.2 %collective-permute-start.19 = (bf16[128,1024]{1,0:T(8,128)(2,1)S(1)}, bf16[128,1024]{1,0:T(8,128)(2,1)S(1)}, u32[]{:S(2)}, u32[]{:S(2)}) collective-permute-start(bf16[128,1024]{1,0:T(8,128)(2,1)S(1)} %collective-permute-done.15.refs_4_), channel_id=1, source_target_pairs={{0,4},{4,0},{8,12},{12,8},{1,5},{5,1},{9,13},{13,9},{2,6},{6,2},{1... | collective-permute-start | bytes 786440 | tf_op jit(solution)/shard_map/ppermute | solution.py:398
  62.9 5.7 %collective-permute-start.18 = (f32[128,128]{1,0:T(8,128)S(1)}, f32[128,128]{1,0:T(8,128)S(1)}, u32[]{:S(2)}, u32[]{:S(2)}) collective-permute-start(f32[128,128]{1,0:T(8,128)S(1)} %get-tuple-element.101), channel_id=1, source_target_pairs={{0,1},{1,0},{2,3},{3,2},{4,5},{5,4},{6,7},{7,6},{8,9},{9,8},{10,11... | collective-permute-start | bytes 196616 | tf_op jit(solution)/shard_map/ppermute | solution.py:21
  69.4 12.8 %all-to-all-start = ((bf16[8,160,128]{2,1,0:T(8,128)(2,1)}), bf16[8,160,128]{2,1,0:T(8,128)(2,1)S(1)}, u32[]{:S(2)}, u32[]{:S(2)}) async-start(bf16[8,160,128]{2,1,0:T(8,128)(2,1)} %shard_map.113), calls=%async_computation | async-start | bytes 655360 | tf_op jit(solution)/shard_map/all_to_all | solution.py:587
  74.4 1.2 %collective-permute-start.21 = (bf16[160,128]{1,0:T(8,128)(2,1)S(1)}, bf16[160,128]{1,0:T(8,128)(2,1)S(1)}, u32[]{:S(2)}, u32[]{:S(2)}) collective-permute-start(bf16[160,128]{1,0:T(8,128)(2,1)S(1)} %slice_bitcast_fusion.mine_ref), channel_id=1, source_target_pairs={{0,1},{1,0},{2,3},{3,2},{4,5},{5,4},{6,7},{7,6},{8,9},{9,8},{10,11... | collective-permute-start | bytes 122888 | tf_op jit(solution)/shard_map/ppermute | solution.py:21
  82.2 1.6 %collective-permute-start.22 = (bf16[8,160,128]{2,1,0:T(8,128)(2,1)S(1)}, bf16[8,160,128]{2,1,0:T(8,128)(2,1)S(1)}, u32[]{:S(2)}, u32[]{:S(2)}) collective-permute-start(bf16[8,160,128]{2,1,0:T(8,128)(2,1)S(1)} %all-to-all-done.refs_0_), channel_id=1, source_target_pairs={{0,1},{1,0},{2,3},{3,2},{4,5},{5,4},{6,7},{7,6},{8,9},{9,8},{10,11... | collective-permute-start | bytes 983048 | tf_op jit(solution)/shard_map/ppermute | solution.py:21
  (15 other events, 128.5 us)

commit v18 on v17

--- a/solution.py
+++ b/solution.py
@@ -85,13 +85,19 @@
     return groups, pairs
 
 
-def split_kernel(a_ref, *outs):
+def split_kernel(a_ref, *refs):
+    outs, sem = refs[:-1], refs[-1]
     count = len(outs)
     me = lax.axis_index("dp")
     part = outs[0].shape[1]
+    copies = []
     for r in range(count):
         at = pl.multiple_of(lax.rem(me + r, count) * part, 128)
-        outs[r][...] = a_ref[:, pl.ds(at, part)]
+        copies.append(pltpu.make_async_copy(a_ref.at[:, pl.ds(at, part)], outs[r], sem.at[r]))
+    for copy in copies:
+        copy.start()
+    for copy in copies:
+        copy.wait()
 
 
 def project_kernel(a_ref, bc_ref, dt_ref, out_ref):
@@ -399,7 +405,7 @@
     return [found[step] for step in steps]
 
 
-def chains(first, own, decay, inner, beside, riders, late):
+def chains(first, own, decay, inner, beside, riders):
     count = lax.axis_size("seq")
     place = lax.axis_index("seq")
     chunks = len(first)
@@ -429,9 +435,6 @@
             done.append(todo.pop(0)(*sent))
         if slot == 1:
             extra = beside(*sent)
-        if slot == last:
-            k = steps[-1][1]
-            got[k] = after(got[k], *late(*sent))
         if slot < last:
             held = [got[k] for _, k in steps] + [d[0] for d in done[-1:]]
             if slot == last - 1:
@@ -463,7 +466,14 @@
     w_dt = w_dt.T
     rate, bias = decay_rate[None], dt_bias[None]
 
-    pieces = call(split_kernel, [struct((rows, part), BF)] * n_dp, 1.9, feats)
+    pieces = call(
+        split_kernel,
+        [struct((rows, part), BF)] * n_dp,
+        1.9,
+        feats,
+        scratch=[pltpu.SemaphoreType.DMA((n_dp,))],
+        specs=[HBM],
+    )
     items = [pieces[0]] + [cyclic(pieces[r], "dp", r) for r in range(1, n_dp)]
     groups = items[:1]
     if n_dp > 1:
@@ -531,15 +541,12 @@
     def beside(*others):
         for r in range(1, n_dp):
             weights.extend(cyclic(after(a, *others), "dp", r) for a in (w_bc, w_dt))
-        return weights[2:] + relay(found[0], groups[0], second, *others)
-
-    def late(*others):
-        return relay(found[1], groups[1], second, *others) if n_dp > 1 else []
+        return weights[2:] + [a for f, b in zip(found, groups) for a in relay(f, b, second, *others)]
 
     first[0] = after(first[0], *spare)
     riders = [f[1, 1] for f in found] if ride else []
     calls = [functools.partial(inner, q) for q in range(PARTS)]
-    stores, inners = chains(first, own, decay, calls, beside, riders, late)
+    stores, inners = chains(first, own, decay, calls, beside, riders)
     for f, a in zip(found, riders):
         f[0, 2] = a
     done = [relay(f, a, [t for t in slots if t not in f], stores[-1]) for f, a in zip(found, groups)]

time: 86.6 us -> 92.9 us (1.073)
  starting transfers between devices: 36.3 us -> 45.4 us
  waiting for transfers between devices: 29.2 us -> 26.3 us
    ppermute x8, starting transfers between devices: 8.9 us -> 14 us  [relay(): found[kind, hop] = lax.ppermute(source, 'seq', pairs[kind])]
    ppermute x9, waiting for transfers between devices: 9.22 us -> 4.79 us  [cyclic(): return lax.ppermute(a, axis, [(i, (i + by) % count) for i in range(count)])]
    ppermute x6, starting transfers between devices: 16.2 us -> 19.7 us  [chains(): got[k] = lax.ppermute(value, 'seq', sorted(to.items()))]
    ppermute x8, waiting for transfers between devices: 5.4 us -> 7.11 us  [relay(): found[kind, hop] = lax.ppermute(source, 'seq', pairs[kind])]
    unnamed x30 -> x32, local copies, waits for them, and re-layouts: 2.91 us -> 3.04 us
  transfers between devices with their start and end apart: 24 -> 24, of which waited for: 13 -> 13; matrix products, arithmetic and copies ran while one was open for 2% -> 2% of each run, Pallas kernels for 14% -> 13%
where the time goes in v18:
time: 92.9 us; the launch traced here: 92.4 us
  starting transfers between devices  45.4 us (49%)
  waiting for transfers between devices  26.3 us (28%)
  Pallas kernels  15 us (16%)
  local copies, waits for them, and re-layouts  4.15 us (4%)
  between operations  0.94 us (1%)
    ppermute x6, starting transfers between devices, chains(): got[k] = lax.ppermute(value, 'seq', sorted(to.items()))  19.7 us
    pallas_call x14, Pallas kernels, call(): pl.pallas_call(kernel, out_shape=out_shape, grid=(1,), in_specs=specs or...  15 us
    ppermute x8, starting transfers between devices, relay(): found[kind, hop] = lax.ppermute(source, 'seq', pairs[kind])  14 us
    ppermute x6, waiting for transfers between devices, chains(): got[k] = lax.ppermute(value, 'seq', sorted(to.items()))  11.1 us
    ppermute x8, waiting for transfers between devices, relay(): found[kind, hop] = lax.ppermute(source, 'seq', pairs[kind])  7.11 us
    ppermute x9, starting transfers between devices, cyclic(): return lax.ppermute(a, axis, [(i, (i + by) % count) for i in range(count)])  6.64 us
    all_to_all x1, starting transfers between devices, body(): lows = lax.all_to_all(copies, ('seq', 'dp'), 0, 0, tiled=True)  5.06 us
    ppermute x9, waiting for transfers between devices, cyclic(): return lax.ppermute(a, axis, [(i, (i + by) % count) for i in range(count)])  4.79 us
  transfers between devices with their start and end apart: 24, of which 13 were waited for; matrix products, arithmetic and copies ran while one was open for 2% of the time, Pallas kernels for 13%

profile of v18, /device:TPU:0, one launch (start us, length us, event | category | flops | bytes accessed | tf_op | source)
XLA Modules:
  0.0 92.4 jit_solution(4401484057910035046)
XLA Ops:
  1.7 3.0 %collective-permute-start = (bf16[128,1024]{1,0:T(8,128)(2,1)S(1)}, bf16[128,1024]{1,0:T(8,128)(2,1)S(1)}, u32[]{:S(2)}, u32[]{:S(2)}) collective-permute-start(bf16[128,1024]{1,0:T(8,128)(2,1)S(1)} %get-tuple-element.56), channel_id=1, source_target_pairs={{0,2},{2,0},{1,3},{3,1},{4,6},{6,4},{5,7},{7,5},{8,10},{10,8},{9,1... | collective-permute-start | bytes 786440 | tf_op jit(solution)/shard_map/ppermute | solution.py:21
  5.4 4.4 %collective-permute-start.2 = (bf16[128,1024]{1,0:T(8,128)(2,1)S(1)}, bf16[128,1024]{1,0:T(8,128)(2,1)S(1)}, u32[]{:S(2)}, u32[]{:S(2)}) collective-permute-start(bf16[128,1024]{1,0:T(8,128)(2,1)S(1)} %get-tuple-element.55.a_ref.refs_0_), channel_id=1, source_target_pairs={{0,4},{4,0},{8,12},{12,8},{1,5},{5,1},{9,13},{13,9},{2,6},{6,2},{1... | collective-permute-start | bytes 786440 | tf_op jit(solution)/shard_map/ppermute | solution.py:404
  11.4 1.8 %collective-permute-start.1 = (f32[320,128]{1,0:T(8,128)S(1)}, f32[320,128]{1,0:T(8,128)S(1)}, u32[]{:S(2)}, u32[]{:S(2)}) collective-permute-start(f32[320,128]{1,0:T(8,128)S(1)} %shard_map.104), channel_id=1, source_target_pairs={{0,2},{2,0},{1,3},{3,1},{4,6},{6,4},{5,7},{7,5},{8,10},{10,8},{9,1... | collective-permute-start | bytes 491528 | tf_op jit(solution)/shard_map/ppermute | solution.py:21
  13.8 4.5 %collective-permute-start.6 = (bf16[128,1024]{1,0:T(8,128)(2,1)S(1)}, bf16[128,1024]{1,0:T(8,128)(2,1)S(1)}, u32[]{:S(2)}, u32[]{:S(2)}) collective-permute-start(bf16[128,1024]{1,0:T(8,128)(2,1)S(1)} %collective-permute-done.a_ref.refs_6_), channel_id=1, source_target_pairs={{0,4},{4,0},{8,12},{12,8},{1,5},{5,1},{9,13},{13,9},{2,6},{6,2},{1... | collective-permute-start | bytes 786440 | tf_op jit(solution)/shard_map/ppermute | solution.py:404
  19.9 2.1 %shard_map.105 = (f32[2,2,128,1024]{3,2,1,0:T(8,128)S(1)}, f32[256,128]{1,0:T(8,128)S(1)}, f32[160,128]{1,0:T(8,128)S(1)}, bf16[128,1024]{1,0:T(8,128)(2,1)S(1)}...) custom-call(f32[320,128]{1,0:T(8,128)S(1)} %shard_map.103.refs_0_, ...), custom_call_target="tpu_custom_call" | custom-call | flops 115000000 | bytes 1966336 | tf_op jit(solution)/shard_map/pallas_call | solution.py:54
  23.2 1.7 %collective-permute-start.8 = (bf16[128,1024]{1,0:T(8,128)(2,1)S(1)}, bf16[128,1024]{1,0:T(8,128)(2,1)S(1)}, u32[]{:S(2)}, u32[]{:S(2)}) collective-permute-start(bf16[128,1024]{1,0:T(8,128)(2,1)S(1)} %get-tuple-element.61), channel_id=1, source_target_pairs={{0,4},{4,0},{8,12},{12,8},{1,5},{5,1},{9,13},{13,9},{2,6},{6,2},{1... | collective-permute-start | bytes 786440 | tf_op jit(solution)/shard_map/ppermute | solution.py:431
  27.8 2.8 %collective-permute-done.8.refs_3_ = bf16[128,1024]{1,0:T(8,128)(2,1)S(1)} collective-permute-done((bf16[128,1024]{1,0:T(8,128)(2,1)S(1)}, bf16[128,1024]{1,0:T(8,128)(2,1)S(1)}, u32[]{:S(2)}, u32[]{:S(2)}) %collective-permute-start.8) | collective-permute-done | bytes 262176 | tf_op jit(solution)/shard_map/ppermute | solution.py:431
  31.5 4.4 %collective-permute-start.9 = (bf16[128,1024]{1,0:T(8,128)(2,1)S(1)}, bf16[128,1024]{1,0:T(8,128)(2,1)S(1)}, u32[]{:S(2)}, u32[]{:S(2)}) collective-permute-start(bf16[128,1024]{1,0:T(8,128)(2,1)S(1)} %broadcast_select_fusion), channel_id=1, source_target_pairs={{0,4},{4,0},{8,12},{12,8},{1,5},{5,1},{9,13},{13,9},{2,6},{6,2},{1... | collective-permute-start | bytes 786440 | tf_op jit(solution)/shard_map/ppermute | solution.py:431
  37.9 3.3 %collective-permute-done.9.refs_9_ = bf16[128,1024]{1,0:T(8,128)(2,1)S(1)} collective-permute-done((bf16[128,1024]{1,0:T(8,128)(2,1)S(1)}, bf16[128,1024]{1,0:T(8,128)(2,1)S(1)}, u32[]{:S(2)}, u32[]{:S(2)}) %collective-permute-start.9) | collective-permute-done | bytes 262176 | tf_op jit(solution)/shard_map/ppermute | solution.py:431
  41.5 6.2 %collective-permute-start.12 = (bf16[128,1024]{1,0:T(8,128)(2,1)S(1)}, bf16[128,1024]{1,0:T(8,128)(2,1)S(1)}, u32[]{:S(2)}, u32[]{:S(2)}) collective-permute-start(bf16[128,1024]{1,0:T(8,128)(2,1)S(1)} %get-tuple-element.106), channel_id=1, source_target_pairs={{0,4},{4,0},{8,12},{12,8},{1,5},{5,1},{9,13},{13,9},{2,6},{6,2},{1... | collective-permute-start | bytes 786440 | tf_op jit(solution)/shard_map/ppermute | solution.py:431
  49.5 2.6 %collective-permute-done.12 = bf16[128,1024]{1,0:T(8,128)(2,1)S(1)} collective-permute-done((bf16[128,1024]{1,0:T(8,128)(2,1)S(1)}, bf16[128,1024]{1,0:T(8,128)(2,1)S(1)}, u32[]{:S(2)}, u32[]{:S(2)}) %collective-permute-start.12) | collective-permute-done | bytes 262176 | tf_op jit(solution)/shard_map/ppermute | solution.py:431
  52.2 6.0 %collective-permute-start.17 = (bf16[128,1024]{1,0:T(8,128)(2,1)S(1)}, bf16[128,1024]{1,0:T(8,128)(2,1)S(1)}, u32[]{:S(2)}, u32[]{:S(2)}) collective-permute-start(bf16[128,1024]{1,0:T(8,128)(2,1)S(1)} %fusion), channel_id=1, source_target_pairs={{0,4},{4,0},{8,12},{12,8},{1,5},{5,1},{9,13},{13,9},{2,6},{6,2},{1... | collective-permute-start | bytes 786440 | tf_op jit(solution)/shard_map/ppermute | solution.py:431
  58.2 1.9 %shard_map.110 = (bf16[128,2048]{1,0:T(8,128)(2,1)}, f32[272,128]{1,0:T(8,128)S(1)}) custom-call(bf16[3,128,1024]{2,1,0:T(8,128)(2,1)S(1)} %bitcast_dynamic-update-slice_fusion.refs_0_, bf16[128,2048]{1,0:T(8,128)(2,1)S(1)} %bitcast.45, bf16[128,2048]{1,0:T(8,128)(2,1)S(1)} %bitcast.52, f32[256,128]{1,0:T(8,128)S(1)} %get-tuple-element.84.bc_ref.refs_3_, ...), custom_call_target="tpu_custom_call" | custom-call | flops 3104999936 | bytes 2719872 | tf_op jit(solution)/shard_map/pallas_call | solution.py:54
  61.0 2.5 %collective-permute-done.17 = bf16[128,1024]{1,0:T(8,128)(2,1)S(1)} collective-permute-done((bf16[128,1024]{1,0:T(8,128)(2,1)S(1)}, bf16[128,1024]{1,0:T(8,128)(2,1)S(1)}, u32[]{:S(2)}, u32[]{:S(2)}) %collective-permute-start.17) | collective-permute-done | bytes 262176 | tf_op jit(solution)/shard_map/ppermute | solution.py:431
  63.5 2.4 %collective-permute-start.19 = (bf16[128,1024]{1,0:T(8,128)(2,1)S(1)}, bf16[128,1024]{1,0:T(8,128)(2,1)S(1)}, u32[]{:S(2)}, u32[]{:S(2)}) collective-permute-start(bf16[128,1024]{1,0:T(8,128)(2,1)S(1)} %collective-permute-done.15.refs_4_), channel_id=1, source_target_pairs={{0,4},{4,0},{8,12},{12,8},{1,5},{5,1},{9,13},{13,9},{2,6},{6,2},{1... | collective-permute-start | bytes 786440 | tf_op jit(solution)/shard_map/ppermute | solution.py:404
  65.9 1.8 %shard_map.111 = (bf16[128,2048]{1,0:T(8,128)(2,1)}, f32[160,128]{1,0:T(8,128)S(1)}, f32[128,128]{1,0:T(8,128)S(1)}) custom-call(bf16[3,128,1024]{2,1,0:T(8,128)(2,1)S(1)} %bitcast_dynamic-update-slice_fusion.3.refs_0_, bf16[128,2048]{1,0:T(8,128)(2,1)S(1)} %bitcast.47, bf16[128,2048]{1,0:T(8,128)(2,1)S(1)} %bitcast.54, ...), custom_call_target="tpu_custom_call", output_to_operand_aliasing={{0}: (12, {})} | custom-call | flops 3104999936 | bytes 3383424 | tf_op jit(solution)/shard_map/pallas_call | solution.py:54
  67.7 3.2 %collective-permute-done.19.refs_5_ = bf16[128,1024]{1,0:T(8,128)(2,1)S(1)} collective-permute-done((bf16[128,1024]{1,0:T(8,128)(2,1)S(1)}, bf16[128,1024]{1,0:T(8,128)(2,1)S(1)}, u32[]{:S(2)}, u32[]{:S(2)}) %collective-permute-start.19) | collective-permute-done | bytes 262176 | tf_op jit(solution)/shard_map/ppermute | solution.py:404
  70.9 2.8 %collective-permute-done.20.refs_11_ = bf16[128,1024]{1,0:T(8,128)(2,1)S(1)} collective-permute-done((bf16[128,1024]{1,0:T(8,128)(2,1)S(1)}, bf16[128,1024]{1,0:T(8,128)(2,1)S(1)}, u32[]{:S(2)}, u32[]{:S(2)}) %collective-permute-start.20) | collective-permute-done | bytes 262176 | tf_op jit(solution)/shard_map/ppermute | solution.py:404
  74.8 5.1 %all-to-all-start = ((bf16[8,160,128]{2,1,0:T(8,128)(2,1)}), bf16[8,160,128]{2,1,0:T(8,128)(2,1)S(1)}, u32[]{:S(2)}, u32[]{:S(2)}) async-start(bf16[8,160,128]{2,1,0:T(8,128)(2,1)} %shard_map.113), calls=%async_computation | async-start | bytes 655360 | tf_op jit(solution)/shard_map/all_to_all | solution.py:594
  80.7 1.2 %collective-permute-done.21.other_ref = bf16[160,128]{1,0:T(8,128)(2,1)S(1)} collective-permute-done((bf16[160,128]{1,0:T(8,128)(2,1)S(1)}, bf16[160,128]{1,0:T(8,128)(2,1)S(1)}, u32[]{:S(2)}, u32[]{:S(2)}) %collective-permute-start.21) | collective-permute-done | bytes 40992 | tf_op jit(solution)/shard_map/ppermute | solution.py:21
  83.7 1.5 %shard_map.114 = bf16[128,2048]{1,0:T(8,128)(2,1)} custom-call(bf16[160,128]{1,0:T(8,128)(2,1)S(1)} %slice_bitcast_fusion.mine_ref, bf16[160,128]{1,0:T(8,128)(2,1)S(1)} %collective-permute-done.21.other_ref, bf16[1024,256]{1,0:T(8,128)(2,1)S(1)} %copy-done.9, bf16[64,1024]{1,0:T(8,128)(2,1)S(1)} %bitcast.67, bf16[1024,256]{1,0:T(8,128)(2,1)S(1)} %copy-done.11, ...), custom_call_target="tpu_custom_call" | custom-call | flops 3335000064 | bytes 1392640 | tf_op jit(solution)/shard_map/pallas_call | solution.py:54
  85.2 3.3 %all-to-all-done.refs_0_ = bf16[8,160,128]{2,1,0:T(8,128)(2,1)S(1)} async-done(((bf16[8,160,128]{2,1,0:T(8,128)(2,1)}), bf16[8,160,128]{2,1,0:T(8,128)(2,1)S(1)}, u32[]{:S(2)}, u32[]{:S(2)}) %all-to-all-start) | async-done | bytes 327712 | tf_op jit(solution)/shard_map/all_to_all | solution.py:594
  88.6 1.6 %collective-permute-done.22.refs_1_ = bf16[8,160,128]{2,1,0:T(8,128)(2,1)S(1)} collective-permute-done((bf16[8,160,128]{2,1,0:T(8,128)(2,1)S(1)}, bf16[8,160,128]{2,1,0:T(8,128)(2,1)S(1)}, u32[]{:S(2)}, u32[]{:S(2)}) %collective-permute-start.22) | collective-permute-done | bytes 327712 | tf_op jit(solution)/shard_map/ppermute | solution.py:21
  90.2 2.2 %shard_map.115 = (f32[1024,256]{1,0:T(8,128)}, f32[64,1024]{1,0:T(8,128)}) custom-call(bf16[2,512,1024]{2,1,0:T(8,128)(2,1)S(1)} %shard_map.112.tok_ref, bf16[8,160,128]{2,1,0:T(8,128)(2,1)S(1)} %all-to-all-done.refs_0_, bf16[8,160,128]{2,1,0:T(8,128)(2,1)S(1)} %collective-permute-done.22.refs_1_), custom_call_target="tpu_custom_call" | custom-call | flops 4600000000 | bytes 2752512 | tf_op jit(solution)/shard_map/pallas_call | solution.py:54
  (82 shorter events, 19.1 us)
Async XLA Ops:
  1.7 9.3 %collective-permute-start = (bf16[128,1024]{1,0:T(8,128)(2,1)S(1)}, bf16[128,1024]{1,0:T(8,128)(2,1)S(1)}, u32[]{:S(2)}, u32[]{:S(2)}) collective-permute-start(bf16[128,1024]{1,0:T(8,128)(2,1)S(1)} %get-tuple-element.56), channel_id=1, source_target_pairs={{0,2},{2,0},{1,3},{3,1},{4,6},{6,4},{5,7},{7,5},{8,10},{10,8},{9,1... | collective-permute-start | bytes 786440 | tf_op jit(solution)/shard_map/ppermute | solution.py:21
  4.7 13.5 %collective-permute-start.3 = (bf16[128,1024]{1,0:T(8,128)(2,1)S(1)}, bf16[128,1024]{1,0:T(8,128)(2,1)S(1)}, u32[]{:S(2)}, u32[]{:S(2)}) collective-permute-start(bf16[128,1024]{1,0:T(8,128)(2,1)S(1)} %get-tuple-element.55.a_ref.refs_0_), channel_id=1, source_target_pairs={{0,0},{4,8},{8,4},{12,12},{1,1},{5,9},{9,5},{13,13},{2,2},{6,10},{... | collective-permute-start | bytes 786440 | tf_op jit(solution)/shard_map/ppermute | solution.py:404
  5.4 12.9 %collective-permute-start.2 = (bf16[128,1024]{1,0:T(8,128)(2,1)S(1)}, bf16[128,1024]{1,0:T(8,128)(2,1)S(1)}, u32[]{:S(2)}, u32[]{:S(2)}) collective-permute-start(bf16[128,1024]{1,0:T(8,128)(2,1)S(1)} %get-tuple-element.55.a_ref.refs_0_), channel_id=1, source_target_pairs={{0,4},{4,0},{8,12},{12,8},{1,5},{5,1},{9,13},{13,9},{2,6},{6,2},{1... | collective-permute-start | bytes 786440 | tf_op jit(solution)/shard_map/ppermute | solution.py:404
  11.4 6.9 %collective-permute-start.1 = (f32[320,128]{1,0:T(8,128)S(1)}, f32[320,128]{1,0:T(8,128)S(1)}, u32[]{:S(2)}, u32[]{:S(2)}) collective-permute-start(f32[320,128]{1,0:T(8,128)S(1)} %shard_map.104), channel_id=1, source_target_pairs={{0,2},{2,0},{1,3},{3,1},{4,6},{6,4},{5,7},{7,5},{8,10},{10,8},{9,1... | collective-permute-start | bytes 491528 | tf_op jit(solution)/shard_map/ppermute | solution.py:21
  13.2 8.9 %collective-permute-start.7 = (bf16[128,1024]{1,0:T(8,128)(2,1)S(1)}, bf16[128,1024]{1,0:T(8,128)(2,1)S(1)}, u32[]{:S(2)}, u32[]{:S(2)}) collective-permute-start(bf16[128,1024]{1,0:T(8,128)(2,1)S(1)} %collective-permute-done.a_ref.refs_6_), channel_id=1, source_target_pairs={{0,0},{4,8},{8,4},{12,12},{1,1},{5,9},{9,5},{13,13},{2,2},{6,10},{... | collective-permute-start | bytes 786440 | tf_op jit(solution)/shard_map/ppermute | solution.py:404
  13.8 9.3 %collective-permute-start.6 = (bf16[128,1024]{1,0:T(8,128)(2,1)S(1)}, bf16[128,1024]{1,0:T(8,128)(2,1)S(1)}, u32[]{:S(2)}, u32[]{:S(2)}) collective-permute-start(bf16[128,1024]{1,0:T(8,128)(2,1)S(1)} %collective-permute-done.a_ref.refs_6_), channel_id=1, source_target_pairs={{0,4},{4,0},{8,12},{12,8},{1,5},{5,1},{9,13},{13,9},{2,6},{6,2},{1... | collective-permute-start | bytes 786440 | tf_op jit(solution)/shard_map/ppermute | solution.py:404
  18.3 1.4 %collective-permute-start.4 = (f32[320,128]{1,0:T(8,128)S(1)}, f32[320,128]{1,0:T(8,128)S(1)}, u32[]{:S(2)}, u32[]{:S(2)}) collective-permute-start(f32[320,128]{1,0:T(8,128)S(1)} %shard_map.103.refs_0_), channel_id=1, source_target_pairs={{0,1},{1,0},{2,3},{3,2},{4,5},{5,4},{6,7},{7,6},{8,9},{9,8},{10,11... | collective-permute-start | bytes 491528 | tf_op jit(solution)/shard_map/ppermute | solution.py:21
  18.3 1.6 %collective-permute-start.5 = (f32[320,128]{1,0:T(8,128)S(1)}, f32[320,128]{1,0:T(8,128)S(1)}, u32[]{:S(2)}, u32[]{:S(2)}) collective-permute-start(f32[320,128]{1,0:T(8,128)S(1)} %collective-permute-done.1.refs_1_), channel_id=1, source_target_pairs={{0,1},{1,0},{2,3},{3,2},{4,5},{5,4},{6,7},{7,6},{8,9},{9,8},{10,11... | collective-permute-start | bytes 491528 | tf_op jit(solution)/shard_map/ppermute | solution.py:21
  23.2 7.5 %collective-permute-start.8 = (bf16[128,1024]{1,0:T(8,128)(2,1)S(1)}, bf16[128,1024]{1,0:T(8,128)(2,1)S(1)}, u32[]{:S(2)}, u32[]{:S(2)}) collective-permute-start(bf16[128,1024]{1,0:T(8,128)(2,1)S(1)} %get-tuple-element.61), channel_id=1, source_target_pairs={{0,4},{4,0},{8,12},{12,8},{1,5},{5,1},{9,13},{13,9},{2,6},{6,2},{1... | collective-permute-start | bytes 786440 | tf_op jit(solution)/shard_map/ppermute | solution.py:431
  24.9 22.8 %collective-permute-start.14 = (bf16[64,1024]{1,0:T(8,128)(2,1)S(1)}, bf16[64,1024]{1,0:T(8,128)(2,1)S(1)}, u32[]{:S(2)}, u32[]{:S(2)}) collective-permute-start(bf16[64,1024]{1,0:T(8,128)(2,1)S(1)} %bitcast.66), channel_id=1, source_target_pairs={{0,2},{2,0},{1,3},{3,1},{4,6},{6,4},{5,7},{7,5},{8,10},{10,8},{9,1... | collective-permute-start | bytes 393224 | tf_op jit(solution)/shard_map/ppermute | solution.py:21
  25.4 24.0 %collective-permute-start.15 = (bf16[128,1024]{1,0:T(8,128)(2,1)S(1)}, bf16[128,1024]{1,0:T(8,128)(2,1)S(1)}, u32[]{:S(2)}, u32[]{:S(2)}) collective-permute-start(bf16[128,1024]{1,0:T(8,128)(2,1)S(1)} %collective-permute-done.2.refs_1_), channel_id=1, source_target_pairs={{0,0},{4,8},{8,4},{12,12},{1,1},{5,9},{9,5},{13,13},{2,2},{6,10},{... | collective-permute-start | bytes 786440 | tf_op jit(solution)/shard_map/ppermute | solution.py:404
  26.1 23.3 %collective-permute-start.16 = (bf16[128,1024]{1,0:T(8,128)(2,1)S(1)}, bf16[128,1024]{1,0:T(8,128)(2,1)S(1)}, u32[]{:S(2)}, u32[]{:S(2)}) collective-permute-start(bf16[128,1024]{1,0:T(8,128)(2,1)S(1)} %collective-permute-done.6.refs_7_), channel_id=1, source_target_pairs={{0,0},{4,8},{8,4},{12,12},{1,1},{5,9},{9,5},{13,13},{2,2},{6,10},{... | collective-permute-start | bytes 786440 | tf_op jit(solution)/shard_map/ppermute | solution.py:404
  30.8 6.2 %collective-permute-start.10 = (bf16[128,1024]{1,0:T(8,128)(2,1)S(1)}, bf16[128,1024]{1,0:T(8,128)(2,1)S(1)}, u32[]{:S(2)}, u32[]{:S(2)}) collective-permute-start(bf16[128,1024]{1,0:T(8,128)(2,1)S(1)} %fusion.3), channel_id=1, source_target_pairs={{0,0},{4,8},{8,4},{12,12},{1,1},{5,9},{9,5},{13,13},{2,2},{6,10},{... | collective-permute-start | bytes 786440 | tf_op jit(solution)/shard_map/ppermute | solution.py:431
  31.5 9.6 %collective-permute-start.9 = (bf16[128,1024]{1,0:T(8,128)(2,1)S(1)}, bf16[128,1024]{1,0:T(8,128)(2,1)S(1)}, u32[]{:S(2)}, u32[]{:S(2)}) collective-permute-start(bf16[128,1024]{1,0:T(8,128)(2,1)S(1)} %broadcast_select_fusion), channel_id=1, source_target_pairs={{0,4},{4,0},{8,12},{12,8},{1,5},{5,1},{9,13},{13,9},{2,6},{6,2},{1... | collective-permute-start | bytes 786440 | tf_op jit(solution)/shard_map/ppermute | solution.py:431
  37.1 12.3 %collective-permute-start.13 = (bf16[1024,256]{1,0:T(8,128)(2,1)S(1)}, bf16[1024,256]{1,0:T(8,128)(2,1)S(1)}, u32[]{:S(2)}, u32[]{:S(2)}) collective-permute-start(bf16[1024,256]{1,0:T(8,128)(2,1)S(1)} %copy-done.8), channel_id=1, source_target_pairs={{0,2},{2,0},{1,3},{3,1},{4,6},{6,4},{5,7},{7,5},{8,10},{10,8},{9,1... | collective-permute-start | bytes 1572872 | tf_op jit(solution)/shard_map/ppermute | solution.py:21
  41.5 10.6 %collective-permute-start.12 = (bf16[128,1024]{1,0:T(8,128)(2,1)S(1)}, bf16[128,1024]{1,0:T(8,128)(2,1)S(1)}, u32[]{:S(2)}, u32[]{:S(2)}) collective-permute-start(bf16[128,1024]{1,0:T(8,128)(2,1)S(1)} %get-tuple-element.106), channel_id=1, source_target_pairs={{0,4},{4,0},{8,12},{12,8},{1,5},{5,1},{9,13},{13,9},{2,6},{6,2},{1... | collective-permute-start | bytes 786440 | tf_op jit(solution)/shard_map/ppermute | solution.py:431
  47.7 4.3 %collective-permute-start.11 = (bf16[128,1024]{1,0:T(8,128)(2,1)S(1)}, bf16[128,1024]{1,0:T(8,128)(2,1)S(1)}, u32[]{:S(2)}, u32[]{:S(2)}) collective-permute-start(bf16[128,1024]{1,0:T(8,128)(2,1)S(1)} %get-tuple-element.107), channel_id=1, source_target_pairs={{0,0},{4,8},{8,4},{12,12},{1,1},{5,9},{9,5},{13,13},{2,2},{6,10},{... | collective-permute-start | bytes 786440 | tf_op jit(solution)/shard_map/ppermute | solution.py:431
  52.2 11.3 %collective-permute-start.17 = (bf16[128,1024]{1,0:T(8,128)(2,1)S(1)}, bf16[128,1024]{1,0:T(8,128)(2,1)S(1)}, u32[]{:S(2)}, u32[]{:S(2)}) collective-permute-start(bf16[128,1024]{1,0:T(8,128)(2,1)S(1)} %fusion), channel_id=1, source_target_pairs={{0,4},{4,0},{8,12},{12,8},{1,5},{5,1},{9,13},{13,9},{2,6},{6,2},{1... | collective-permute-start | bytes 786440 | tf_op jit(solution)/shard_map/ppermute | solution.py:431
  63.5 7.4 %collective-permute-start.19 = (bf16[128,1024]{1,0:T(8,128)(2,1)S(1)}, bf16[128,1024]{1,0:T(8,128)(2,1)S(1)}, u32[]{:S(2)}, u32[]{:S(2)}) collective-permute-start(bf16[128,1024]{1,0:T(8,128)(2,1)S(1)} %collective-permute-done.15.refs_4_), channel_id=1, source_target_pairs={{0,4},{4,0},{8,12},{12,8},{1,5},{5,1},{9,13},{13,9},{2,6},{6,2},{1... | collective-permute-start | bytes 786440 | tf_op jit(solution)/shard_map/ppermute | solution.py:404
  65.9 7.9 %collective-permute-start.20 = (bf16[128,1024]{1,0:T(8,128)(2,1)S(1)}, bf16[128,1024]{1,0:T(8,128)(2,1)S(1)}, u32[]{:S(2)}, u32[]{:S(2)}) collective-permute-start(bf16[128,1024]{1,0:T(8,128)(2,1)S(1)} %collective-permute-done.16.refs_10_), channel_id=1, source_target_pairs={{0,4},{4,0},{8,12},{12,8},{1,5},{5,1},{9,13},{13,9},{2,6},{6,2},{1... | collective-permute-start | bytes 786440 | tf_op jit(solution)/shard_map/ppermute | solution.py:404
  67.7 6.4 %collective-permute-start.18 = (f32[128,128]{1,0:T(8,128)S(1)}, f32[128,128]{1,0:T(8,128)S(1)}, u32[]{:S(2)}, u32[]{:S(2)}) collective-permute-start(f32[128,128]{1,0:T(8,128)S(1)} %get-tuple-element.99), channel_id=1, source_target_pairs={{0,1},{1,0},{2,3},{3,2},{4,5},{5,4},{6,7},{7,6},{8,9},{9,8},{10,11... | collective-permute-start | bytes 196616 | tf_op jit(solution)/shard_map/ppermute | solution.py:21
  74.8 13.7 %all-to-all-start = ((bf16[8,160,128]{2,1,0:T(8,128)(2,1)}), bf16[8,160,128]{2,1,0:T(8,128)(2,1)S(1)}, u32[]{:S(2)}, u32[]{:S(2)}) async-start(bf16[8,160,128]{2,1,0:T(8,128)(2,1)} %shard_map.113), calls=%async_computation | async-start | bytes 655360 | tf_op jit(solution)/shard_map/all_to_all | solution.py:594
  80.7 1.2 %collective-permute-start.21 = (bf16[160,128]{1,0:T(8,128)(2,1)S(1)}, bf16[160,128]{1,0:T(8,128)(2,1)S(1)}, u32[]{:S(2)}, u32[]{:S(2)}) collective-permute-start(bf16[160,128]{1,0:T(8,128)(2,1)S(1)} %slice_bitcast_fusion.mine_ref), channel_id=1, source_target_pairs={{0,1},{1,0},{2,3},{3,2},{4,5},{5,4},{6,7},{7,6},{8,9},{9,8},{10,11... | collective-permute-start | bytes 122888 | tf_op jit(solution)/shard_map/ppermute | solution.py:21
  88.6 1.6 %collective-permute-start.22 = (bf16[8,160,128]{2,1,0:T(8,128)(2,1)S(1)}, bf16[8,160,128]{2,1,0:T(8,128)(2,1)S(1)}, u32[]{:S(2)}, u32[]{:S(2)}) collective-permute-start(bf16[8,160,128]{2,1,0:T(8,128)(2,1)S(1)} %all-to-all-done.refs_0_), channel_id=1, source_target_pairs={{0,1},{1,0},{2,3},{3,2},{4,5},{5,4},{6,7},{7,6},{8,9},{9,8},{10,11... | collective-permute-start | bytes 983048 | tf_op jit(solution)/shard_map/ppermute | solution.py:21
  (16 other events, 99.6 us)

commit v19 on v17

--- a/solution.py
+++ b/solution.py
@@ -580,12 +580,12 @@
         *toks,
         scratch=[pltpu.SemaphoreType.DMA((n_dp, len(slots)))],
     )
-    taken = after(cyclic(give, "head", 1), ordered)
+    taken = cyclic(give, "head", 1)
     count = n_dp * n_seq
     copies = call(low_kernel, struct((count, rows + heads, rows), BF), 1.2, keep, taken)
     mine = copies[0]
     lows = lax.all_to_all(copies, ("seq", "dp"), 0, 0, tiled=True)
-    other = cyclic(mine, "head", 1)
+    other = cyclic(after(mine, ordered), "head", 1)
     grads = call(
         functools.partial(token_kernel, n_dp),
         struct((rows, width), BF),

time: 86.6 us -> 93.9 us (1.084)
  local copies, waits for them, and re-layouts: 4.02 us -> 10 us
  Pallas kernels: 15 us -> 16.1 us
    unnamed x30 -> x54, local copies, waits for them, and re-layouts: 2.91 us -> 8.91 us
    ppermute x8, waiting for transfers between devices: 5.4 us -> 9.44 us  [relay(): found[kind, hop] = lax.ppermute(source, 'seq', pairs[kind])]
    all_to_all x1, waiting for transfers between devices: 3.32 us -> 0.01 us  [body(): lows = lax.all_to_all(copies, ('seq', 'dp'), 0, 0, tiled=True)]
    ppermute x8, starting transfers between devices: 8.9 us -> 11.3 us  [relay(): found[kind, hop] = lax.ppermute(source, 'seq', pairs[kind])]
    ppermute x6, starting transfers between devices: 16.2 us -> 15 us  [chains(): got[k] = lax.ppermute(value, 'seq', sorted(to.items()))]
    pallas_call x14, Pallas kernels: 15 us -> 16.1 us  [call(): pl.pallas_call(kernel, out_shape=out_shape, grid=(1,), in_specs=specs or...]
    ppermute x6, waiting for transfers between devices: 11.3 us -> 10.2 us  [chains(): got[k] = lax.ppermute(value, 'seq', sorted(to.items()))]
  transfers between devices with their start and end apart: 24 -> 24, of which waited for: 13 -> 12; matrix products, arithmetic and copies ran while one was open for 2% -> 2% of each run, Pallas kernels for 14% -> 13%
where the time goes in v19:
time: 93.9 us; the launch traced here: 93.2 us
  starting transfers between devices  36.9 us (39%)
  waiting for transfers between devices  28.7 us (31%)
  Pallas kernels  16.1 us (17%)
  local copies, waits for them, and re-layouts  10 us (11%)
  between operations  1.02 us (1%)
    pallas_call x14, Pallas kernels, call(): pl.pallas_call(kernel, out_shape=out_shape, grid=(1,), in_specs=specs or...  16.1 us
    ppermute x6, starting transfers between devices, chains(): got[k] = lax.ppermute(value, 'seq', sorted(to.items()))  15 us
    ppermute x8, starting transfers between devices, relay(): found[kind, hop] = lax.ppermute(source, 'seq', pairs[kind])  11.3 us
    ppermute x6, waiting for transfers between devices, chains(): got[k] = lax.ppermute(value, 'seq', sorted(to.items()))  10.2 us
    ppermute x8, waiting for transfers between devices, relay(): found[kind, hop] = lax.ppermute(source, 'seq', pairs[kind])  9.44 us
    ppermute x9, waiting for transfers between devices, cyclic(): return lax.ppermute(a, axis, [(i, (i + by) % count) for i in range(count)])  9.02 us
    unnamed x54, local copies, waits for them, and re-layouts  8.91 us
    ppermute x9, starting transfers between devices, cyclic(): return lax.ppermute(a, axis, [(i, (i + by) % count) for i in range(count)])  7.15 us
  transfers between devices with their start and end apart: 24, of which 12 were waited for; matrix products, arithmetic and copies ran while one was open for 2% of the time, Pallas kernels for 13%

profile of v19, /device:TPU:0, one launch (start us, length us, event | category | flops | bytes accessed | tf_op | source)
XLA Modules:
  0.0 93.2 jit_solution(14294798042347204825)
XLA Ops:
  1.7 3.0 %collective-permute-start = (bf16[128,1024]{1,0:T(8,128)(2,1)S(1)}, bf16[128,1024]{1,0:T(8,128)(2,1)S(1)}, u32[]{:S(2)}, u32[]{:S(2)}) collective-permute-start(bf16[128,1024]{1,0:T(8,128)(2,1)S(1)} %get-tuple-element.57), channel_id=1, source_target_pairs={{0,2},{2,0},{1,3},{3,1},{4,6},{6,4},{5,7},{7,5},{8,10},{10,8},{9,1... | collective-permute-start | bytes 786440 | tf_op jit(solution)/shard_map/ppermute | solution.py:21
  4.7 1.6 %collective-permute-start.2 = (bf16[128,1024]{1,0:T(8,128)(2,1)S(1)}, bf16[128,1024]{1,0:T(8,128)(2,1)S(1)}, u32[]{:S(2)}, u32[]{:S(2)}) collective-permute-start(bf16[128,1024]{1,0:T(8,128)(2,1)S(1)} %get-tuple-element.56.a_ref.refs_0_), channel_id=1, source_target_pairs={{0,4},{4,0},{8,12},{12,8},{1,5},{5,1},{9,13},{13,9},{2,6},{6,2},{1... | collective-permute-start | bytes 786440 | tf_op jit(solution)/shard_map/ppermute | solution.py:398
  7.4 3.7 %collective-permute-done.a_ref.refs_6_ = bf16[128,1024]{1,0:T(8,128)(2,1)S(1)} collective-permute-done((bf16[128,1024]{1,0:T(8,128)(2,1)S(1)}, bf16[128,1024]{1,0:T(8,128)(2,1)S(1)}, u32[]{:S(2)}, u32[]{:S(2)}) %collective-permute-start) | collective-permute-done | bytes 262176 | tf_op jit(solution)/shard_map/ppermute | solution.py:21
  11.3 1.8 %collective-permute-start.1 = (f32[320,128]{1,0:T(8,128)S(1)}, f32[320,128]{1,0:T(8,128)S(1)}, u32[]{:S(2)}, u32[]{:S(2)}) collective-permute-start(f32[320,128]{1,0:T(8,128)S(1)} %shard_map.104), channel_id=1, source_target_pairs={{0,2},{2,0},{1,3},{3,1},{4,6},{6,4},{5,7},{7,5},{8,10},{10,8},{9,1... | collective-permute-start | bytes 491528 | tf_op jit(solution)/shard_map/ppermute | solution.py:21
  13.1 1.6 %collective-permute-start.6 = (bf16[128,1024]{1,0:T(8,128)(2,1)S(1)}, bf16[128,1024]{1,0:T(8,128)(2,1)S(1)}, u32[]{:S(2)}, u32[]{:S(2)}) collective-permute-start(bf16[128,1024]{1,0:T(8,128)(2,1)S(1)} %collective-permute-done.a_ref.refs_6_), channel_id=1, source_target_pairs={{0,4},{4,0},{8,12},{12,8},{1,5},{5,1},{9,13},{13,9},{2,6},{6,2},{1... | collective-permute-start | bytes 786440 | tf_op jit(solution)/shard_map/ppermute | solution.py:398
  18.2 2.1 %shard_map.105 = (f32[2,2,128,1024]{3,2,1,0:T(8,128)S(1)}, f32[256,128]{1,0:T(8,128)S(1)}, f32[160,128]{1,0:T(8,128)S(1)}, bf16[128,1024]{1,0:T(8,128)(2,1)S(1)}...) custom-call(f32[320,128]{1,0:T(8,128)S(1)} %shard_map.103.refs_0_, ...), custom_call_target="tpu_custom_call" | custom-call | flops 115000000 | bytes 1966336 | tf_op jit(solution)/shard_map/pallas_call | solution.py:54
  21.1 3.6 %collective-permute-start.8 = (bf16[128,1024]{1,0:T(8,128)(2,1)S(1)}, bf16[128,1024]{1,0:T(8,128)(2,1)S(1)}, u32[]{:S(2)}, u32[]{:S(2)}) collective-permute-start(bf16[128,1024]{1,0:T(8,128)(2,1)S(1)} %get-tuple-element.62), channel_id=1, source_target_pairs={{0,4},{4,0},{8,12},{12,8},{1,5},{5,1},{9,13},{13,9},{2,6},{6,2},{1... | collective-permute-start | bytes 786440 | tf_op jit(solution)/shard_map/ppermute | solution.py:425
  26.5 1.5 %collective-permute-start.13 = (bf16[1024,256]{1,0:T(8,128)(2,1)}, bf16[1024,256]{1,0:T(8,128)(2,1)S(1)}, u32[]{:S(2)}, u32[]{:S(2)}) collective-permute-start(bf16[1024,256]{1,0:T(8,128)(2,1)} %refs_0_.1), channel_id=1, source_target_pairs={{0,2},{2,0},{1,3},{3,1},{4,6},{6,4},{5,7},{7,5},{8,10},{10,8},{9,1... | collective-permute-start | bytes 1572872 | tf_op jit(solution)/shard_map/ppermute | solution.py:21
  29.1 2.1 %collective-permute-done.8.refs_3_ = bf16[128,1024]{1,0:T(8,128)(2,1)S(1)} collective-permute-done((bf16[128,1024]{1,0:T(8,128)(2,1)S(1)}, bf16[128,1024]{1,0:T(8,128)(2,1)S(1)}, u32[]{:S(2)}, u32[]{:S(2)}) %collective-permute-start.8) | collective-permute-done | bytes 262176 | tf_op jit(solution)/shard_map/ppermute | solution.py:425
  32.0 3.1 %collective-permute-start.9 = (bf16[128,1024]{1,0:T(8,128)(2,1)S(1)}, bf16[128,1024]{1,0:T(8,128)(2,1)S(1)}, u32[]{:S(2)}, u32[]{:S(2)}) collective-permute-start(bf16[128,1024]{1,0:T(8,128)(2,1)S(1)} %broadcast_select_fusion), channel_id=1, source_target_pairs={{0,4},{4,0},{8,12},{12,8},{1,5},{5,1},{9,13},{13,9},{2,6},{6,2},{1... | collective-permute-start | bytes 786440 | tf_op jit(solution)/shard_map/ppermute | solution.py:425
  36.1 4.8 %collective-permute-done.9.refs_9_ = bf16[128,1024]{1,0:T(8,128)(2,1)S(1)} collective-permute-done((bf16[128,1024]{1,0:T(8,128)(2,1)S(1)}, bf16[128,1024]{1,0:T(8,128)(2,1)S(1)}, u32[]{:S(2)}, u32[]{:S(2)}) %collective-permute-start.9) | collective-permute-done | bytes 262176 | tf_op jit(solution)/shard_map/ppermute | solution.py:425
  41.9 4.8 %collective-permute-start.12 = (bf16[128,1024]{1,0:T(8,128)(2,1)S(1)}, bf16[128,1024]{1,0:T(8,128)(2,1)S(1)}, u32[]{:S(2)}, u32[]{:S(2)}) collective-permute-start(bf16[128,1024]{1,0:T(8,128)(2,1)S(1)} %get-tuple-element.108), channel_id=1, source_target_pairs={{0,4},{4,0},{8,12},{12,8},{1,5},{5,1},{9,13},{13,9},{2,6},{6,2},{1... | collective-permute-start | bytes 786440 | tf_op jit(solution)/shard_map/ppermute | solution.py:425
  47.8 3.2 %collective-permute-done.12 = bf16[128,1024]{1,0:T(8,128)(2,1)S(1)} collective-permute-done((bf16[128,1024]{1,0:T(8,128)(2,1)S(1)}, bf16[128,1024]{1,0:T(8,128)(2,1)S(1)}, u32[]{:S(2)}, u32[]{:S(2)}) %collective-permute-start.12) | collective-permute-done | bytes 262176 | tf_op jit(solution)/shard_map/ppermute | solution.py:425
  51.1 2.3 %collective-permute-start.16 = (bf16[128,1024]{1,0:T(8,128)(2,1)S(1)}, bf16[128,1024]{1,0:T(8,128)(2,1)S(1)}, u32[]{:S(2)}, u32[]{:S(2)}) collective-permute-start(bf16[128,1024]{1,0:T(8,128)(2,1)S(1)} %fusion), channel_id=1, source_target_pairs={{0,4},{4,0},{8,12},{12,8},{1,5},{5,1},{9,13},{13,9},{2,6},{6,2},{1... | collective-permute-start | bytes 786440 | tf_op jit(solution)/shard_map/ppermute | solution.py:425
  54.8 1.9 %shard_map.110 = (bf16[128,2048]{1,0:T(8,128)(2,1)}, f32[272,128]{1,0:T(8,128)S(1)}) custom-call(bf16[3,128,1024]{2,1,0:T(8,128)(2,1)S(1)} %bitcast_dynamic-update-slice_fusion.refs_0_, bf16[128,2048]{1,0:T(8,128)(2,1)S(1)} %bitcast.45, bf16[128,2048]{1,0:T(8,128)(2,1)S(1)} %bitcast.52, f32[256,128]{1,0:T(8,128)S(1)} %get-tuple-element.86.bc_ref.refs_3_, ...), custom_call_target="tpu_custom_call" | custom-call | flops 3104999936 | bytes 2719872 | tf_op jit(solution)/shard_map/pallas_call | solution.py:54
  57.8 1.7 %shard_map.111 = (bf16[128,2048]{1,0:T(8,128)(2,1)}, f32[160,128]{1,0:T(8,128)S(1)}, f32[128,128]{1,0:T(8,128)S(1)}) custom-call(bf16[3,128,1024]{2,1,0:T(8,128)(2,1)S(1)} %bitcast_dynamic-update-slice_fusion.3.refs_0_, bf16[128,2048]{1,0:T(8,128)(2,1)S(1)} %bitcast.47, bf16[128,2048]{1,0:T(8,128)(2,1)S(1)} %bitcast.54, ...), custom_call_target="tpu_custom_call", output_to_operand_aliasing={{0}: (12, {})} | custom-call | flops 3104999936 | bytes 3383424 | tf_op jit(solution)/shard_map/pallas_call | solution.py:54
  59.5 4.0 %collective-permute-start.20 = (bf16[128,1024]{1,0:T(8,128)(2,1)}, bf16[128,1024]{1,0:T(8,128)(2,1)S(1)}, u32[]{:S(2)}, u32[]{:S(2)}) collective-permute-start(bf16[128,1024]{1,0:T(8,128)(2,1)} %collective-permute-done.17.refs_10_), channel_id=1, source_target_pairs={{0,4},{4,0},{8,12},{12,8},{1,5},{5,1},{9,13},{13,9},{2,6},{6,2},{1... | collective-permute-start | bytes 786440 | tf_op jit(solution)/shard_map/ppermute | solution.py:398
  64.3 3.4 %all-to-all-start = ((bf16[8,160,128]{2,1,0:T(8,128)(2,1)}), bf16[8,160,128]{2,1,0:T(8,128)(2,1)S(1)}, u32[]{:S(2)}, u32[]{:S(2)}) async-start(bf16[8,160,128]{2,1,0:T(8,128)(2,1)} %shard_map.112), calls=%async_computation | async-start | bytes 655360 | tf_op jit(solution)/shard_map/all_to_all | solution.py:587
  68.6 2.4 %collective-permute-done.20.refs_11_ = bf16[128,1024]{1,0:T(8,128)(2,1)S(1)} collective-permute-done((bf16[128,1024]{1,0:T(8,128)(2,1)}, bf16[128,1024]{1,0:T(8,128)(2,1)S(1)}, u32[]{:S(2)}, u32[]{:S(2)}) %collective-permute-start.20) | collective-permute-done | bytes 262176 | tf_op jit(solution)/shard_map/ppermute | solution.py:398
  71.6 7.1 %collective-permute-done.19.refs_5_ = bf16[128,1024]{1,0:T(8,128)(2,1)S(1)} collective-permute-done((bf16[128,1024]{1,0:T(8,128)(2,1)}, bf16[128,1024]{1,0:T(8,128)(2,1)S(1)}, u32[]{:S(2)}, u32[]{:S(2)}) %collective-permute-start.19) | collective-permute-done | bytes 262176 | tf_op jit(solution)/shard_map/ppermute | solution.py:398
  85.1 1.4 %shard_map.113.tok_ref = bf16[2,512,1024]{2,1,0:T(8,128)(2,1)S(1)} custom-call(bf16[128,1024]{1,0:T(8,128)(2,1)S(1)} %copy-done.4, bf16[128,1024]{1,0:T(8,128)(2,1)S(1)} %copy-done.8, bf16[128,1024]{1,0:T(8,128)(2,1)S(1)} %collective-permute-done.3.refs_8_.refs_2_, bf16[128,1024]{1,0:T(8,128)(2,1)S(1)} %collective-permute-done.8.refs_3_, ...), custom_call_target="tpu_custom_call" | custom-call | flops 1150000000 | bytes 3145728 | tf_op jit(solution)/shard_map/pallas_call | solution.py:54
  87.8 1.5 %shard_map.114 = bf16[128,2048]{1,0:T(8,128)(2,1)} custom-call(bf16[160,128]{1,0:T(8,128)(2,1)S(1)} %slice_bitcast_fusion.mine_ref, bf16[160,128]{1,0:T(8,128)(2,1)S(1)} %collective-permute-done.21.other_ref, bf16[1024,256]{1,0:T(8,128)(2,1)S(1)} %copy-done.20, bf16[64,1024]{1,0:T(8,128)(2,1)S(1)} %bitcast.67, bf16[1024,256]{1,0:T(8,128)(2,1)S(1)} %copy-done.22, ...), custom_call_target="tpu_custom_call" | custom-call | flops 3335000064 | bytes 1392640 | tf_op jit(solution)/shard_map/pallas_call | solution.py:54
  89.5 1.5 %collective-permute-done.22.refs_1_ = bf16[8,160,128]{2,1,0:T(8,128)(2,1)S(1)} collective-permute-done((bf16[8,160,128]{2,1,0:T(8,128)(2,1)S(1)}, bf16[8,160,128]{2,1,0:T(8,128)(2,1)S(1)}, u32[]{:S(2)}, u32[]{:S(2)}) %collective-permute-start.22) | collective-permute-done | bytes 327712 | tf_op jit(solution)/shard_map/ppermute | solution.py:21
  91.0 2.2 %shard_map.115 = (f32[1024,256]{1,0:T(8,128)}, f32[64,1024]{1,0:T(8,128)}) custom-call(bf16[2,512,1024]{2,1,0:T(8,128)(2,1)S(1)} %shard_map.113.tok_ref, bf16[8,160,128]{2,1,0:T(8,128)(2,1)S(1)} %all-to-all-done.refs_0_, bf16[8,160,128]{2,1,0:T(8,128)(2,1)S(1)} %collective-permute-done.22.refs_1_), custom_call_target="tpu_custom_call" | custom-call | flops 4600000000 | bytes 2752512 | tf_op jit(solution)/shard_map/pallas_call | solution.py:54
  (105 shorter events, 26.0 us)
Async XLA Ops:
  1.7 9.3 %collective-permute-start = (bf16[128,1024]{1,0:T(8,128)(2,1)S(1)}, bf16[128,1024]{1,0:T(8,128)(2,1)S(1)}, u32[]{:S(2)}, u32[]{:S(2)}) collective-permute-start(bf16[128,1024]{1,0:T(8,128)(2,1)S(1)} %get-tuple-element.57), channel_id=1, source_target_pairs={{0,2},{2,0},{1,3},{3,1},{4,6},{6,4},{5,7},{7,5},{8,10},{10,8},{9,1... | collective-permute-start | bytes 786440 | tf_op jit(solution)/shard_map/ppermute | solution.py:21
  4.7 10.7 %collective-permute-start.2 = (bf16[128,1024]{1,0:T(8,128)(2,1)S(1)}, bf16[128,1024]{1,0:T(8,128)(2,1)S(1)}, u32[]{:S(2)}, u32[]{:S(2)}) collective-permute-start(bf16[128,1024]{1,0:T(8,128)(2,1)S(1)} %get-tuple-element.56.a_ref.refs_0_), channel_id=1, source_target_pairs={{0,4},{4,0},{8,12},{12,8},{1,5},{5,1},{9,13},{13,9},{2,6},{6,2},{1... | collective-permute-start | bytes 786440 | tf_op jit(solution)/shard_map/ppermute | solution.py:398
  6.3 9.2 %collective-permute-start.3 = (bf16[128,1024]{1,0:T(8,128)(2,1)S(1)}, bf16[128,1024]{1,0:T(8,128)(2,1)S(1)}, u32[]{:S(2)}, u32[]{:S(2)}) collective-permute-start(bf16[128,1024]{1,0:T(8,128)(2,1)S(1)} %get-tuple-element.56.a_ref.refs_0_), channel_id=1, source_target_pairs={{0,0},{4,8},{8,4},{12,12},{1,1},{5,9},{9,5},{13,13},{2,2},{6,10},{... | collective-permute-start | bytes 786440 | tf_op jit(solution)/shard_map/ppermute | solution.py:398
  11.3 5.5 %collective-permute-start.1 = (f32[320,128]{1,0:T(8,128)S(1)}, f32[320,128]{1,0:T(8,128)S(1)}, u32[]{:S(2)}, u32[]{:S(2)}) collective-permute-start(f32[320,128]{1,0:T(8,128)S(1)} %shard_map.104), channel_id=1, source_target_pairs={{0,2},{2,0},{1,3},{3,1},{4,6},{6,4},{5,7},{7,5},{8,10},{10,8},{9,1... | collective-permute-start | bytes 491528 | tf_op jit(solution)/shard_map/ppermute | solution.py:21
  13.1 7.2 %collective-permute-start.6 = (bf16[128,1024]{1,0:T(8,128)(2,1)S(1)}, bf16[128,1024]{1,0:T(8,128)(2,1)S(1)}, u32[]{:S(2)}, u32[]{:S(2)}) collective-permute-start(bf16[128,1024]{1,0:T(8,128)(2,1)S(1)} %collective-permute-done.a_ref.refs_6_), channel_id=1, source_target_pairs={{0,4},{4,0},{8,12},{12,8},{1,5},{5,1},{9,13},{13,9},{2,6},{6,2},{1... | collective-permute-start | bytes 786440 | tf_op jit(solution)/shard_map/ppermute | solution.py:398
  14.7 5.7 %collective-permute-start.7 = (bf16[128,1024]{1,0:T(8,128)(2,1)S(1)}, bf16[128,1024]{1,0:T(8,128)(2,1)S(1)}, u32[]{:S(2)}, u32[]{:S(2)}) collective-permute-start(bf16[128,1024]{1,0:T(8,128)(2,1)S(1)} %collective-permute-done.a_ref.refs_6_), channel_id=1, source_target_pairs={{0,0},{4,8},{8,4},{12,12},{1,1},{5,9},{9,5},{13,13},{2,2},{6,10},{... | collective-permute-start | bytes 786440 | tf_op jit(solution)/shard_map/ppermute | solution.py:398
  15.4 1.5 %collective-permute-start.4 = (f32[320,128]{1,0:T(8,128)S(1)}, f32[320,128]{1,0:T(8,128)S(1)}, u32[]{:S(2)}, u32[]{:S(2)}) collective-permute-start(f32[320,128]{1,0:T(8,128)S(1)} %shard_map.103.refs_0_), channel_id=1, source_target_pairs={{0,1},{1,0},{2,3},{3,2},{4,5},{5,4},{6,7},{7,6},{8,9},{9,8},{10,11... | collective-permute-start | bytes 491528 | tf_op jit(solution)/shard_map/ppermute | solution.py:21
  16.8 1.4 %collective-permute-start.5 = (f32[320,128]{1,0:T(8,128)S(1)}, f32[320,128]{1,0:T(8,128)S(1)}, u32[]{:S(2)}, u32[]{:S(2)}) collective-permute-start(f32[320,128]{1,0:T(8,128)S(1)} %collective-permute-done.1.refs_1_), channel_id=1, source_target_pairs={{0,1},{1,0},{2,3},{3,2},{4,5},{5,4},{6,7},{7,6},{8,9},{9,8},{10,11... | collective-permute-start | bytes 491528 | tf_op jit(solution)/shard_map/ppermute | solution.py:21
  21.1 10.1 %collective-permute-start.8 = (bf16[128,1024]{1,0:T(8,128)(2,1)S(1)}, bf16[128,1024]{1,0:T(8,128)(2,1)S(1)}, u32[]{:S(2)}, u32[]{:S(2)}) collective-permute-start(bf16[128,1024]{1,0:T(8,128)(2,1)S(1)} %get-tuple-element.62), channel_id=1, source_target_pairs={{0,4},{4,0},{8,12},{12,8},{1,5},{5,1},{9,13},{13,9},{2,6},{6,2},{1... | collective-permute-start | bytes 786440 | tf_op jit(solution)/shard_map/ppermute | solution.py:425
  24.6 23.1 %collective-permute-start.15 = (bf16[128,1024]{1,0:T(8,128)(2,1)S(1)}, bf16[128,1024]{1,0:T(8,128)(2,1)}, u32[]{:S(2)}, u32[]{:S(2)}) collective-permute-start(bf16[128,1024]{1,0:T(8,128)(2,1)S(1)} %collective-permute-done.2.refs_1_), channel_id=1, source_target_pairs={{0,0},{4,8},{8,4},{12,12},{1,1},{5,9},{9,5},{13,13},{2,2},{6,10},{... | collective-permute-start | bytes 786440 | tf_op jit(solution)/shard_map/ppermute | solution.py:398
  26.0 21.7 %collective-permute-start.14 = (bf16[64,1024]{1,0:T(8,128)(2,1)S(1)}, bf16[64,1024]{1,0:T(8,128)(2,1)S(1)}, u32[]{:S(2)}, u32[]{:S(2)}) collective-permute-start(bf16[64,1024]{1,0:T(8,128)(2,1)S(1)} %bitcast.66), channel_id=1, source_target_pairs={{0,2},{2,0},{1,3},{3,1},{4,6},{6,4},{5,7},{7,5},{8,10},{10,8},{9,1... | collective-permute-start | bytes 393224 | tf_op jit(solution)/shard_map/ppermute | solution.py:21
  26.5 21.2 %collective-permute-start.13 = (bf16[1024,256]{1,0:T(8,128)(2,1)}, bf16[1024,256]{1,0:T(8,128)(2,1)S(1)}, u32[]{:S(2)}, u32[]{:S(2)}) collective-permute-start(bf16[1024,256]{1,0:T(8,128)(2,1)} %refs_0_.1), channel_id=1, source_target_pairs={{0,2},{2,0},{1,3},{3,1},{4,6},{6,4},{5,7},{7,5},{8,10},{10,8},{9,1... | collective-permute-start | bytes 1572872 | tf_op jit(solution)/shard_map/ppermute | solution.py:21
  31.3 4.8 %collective-permute-start.10 = (bf16[128,1024]{1,0:T(8,128)(2,1)S(1)}, bf16[128,1024]{1,0:T(8,128)(2,1)S(1)}, u32[]{:S(2)}, u32[]{:S(2)}) collective-permute-start(bf16[128,1024]{1,0:T(8,128)(2,1)S(1)} %fusion.3), channel_id=1, source_target_pairs={{0,0},{4,8},{8,4},{12,12},{1,1},{5,9},{9,5},{13,13},{2,2},{6,10},{... | collective-permute-start | bytes 786440 | tf_op jit(solution)/shard_map/ppermute | solution.py:425
  32.0 8.9 %collective-permute-start.9 = (bf16[128,1024]{1,0:T(8,128)(2,1)S(1)}, bf16[128,1024]{1,0:T(8,128)(2,1)S(1)}, u32[]{:S(2)}, u32[]{:S(2)}) collective-permute-start(bf16[128,1024]{1,0:T(8,128)(2,1)S(1)} %broadcast_select_fusion), channel_id=1, source_target_pairs={{0,4},{4,0},{8,12},{12,8},{1,5},{5,1},{9,13},{13,9},{2,6},{6,2},{1... | collective-permute-start | bytes 786440 | tf_op jit(solution)/shard_map/ppermute | solution.py:425
  41.2 6.6 %collective-permute-start.11 = (bf16[128,1024]{1,0:T(8,128)(2,1)S(1)}, bf16[128,1024]{1,0:T(8,128)(2,1)S(1)}, u32[]{:S(2)}, u32[]{:S(2)}) collective-permute-start(bf16[128,1024]{1,0:T(8,128)(2,1)S(1)} %get-tuple-element.109), channel_id=1, source_target_pairs={{0,0},{4,8},{8,4},{12,12},{1,1},{5,9},{9,5},{13,13},{2,2},{6,10},{... | collective-permute-start | bytes 786440 | tf_op jit(solution)/shard_map/ppermute | solution.py:425
  41.9 9.1 %collective-permute-start.12 = (bf16[128,1024]{1,0:T(8,128)(2,1)S(1)}, bf16[128,1024]{1,0:T(8,128)(2,1)S(1)}, u32[]{:S(2)}, u32[]{:S(2)}) collective-permute-start(bf16[128,1024]{1,0:T(8,128)(2,1)S(1)} %get-tuple-element.108), channel_id=1, source_target_pairs={{0,4},{4,0},{8,12},{12,8},{1,5},{5,1},{9,13},{13,9},{2,6},{6,2},{1... | collective-permute-start | bytes 786440 | tf_op jit(solution)/shard_map/ppermute | solution.py:425
  51.1 6.6 %collective-permute-start.16 = (bf16[128,1024]{1,0:T(8,128)(2,1)S(1)}, bf16[128,1024]{1,0:T(8,128)(2,1)S(1)}, u32[]{:S(2)}, u32[]{:S(2)}) collective-permute-start(bf16[128,1024]{1,0:T(8,128)(2,1)S(1)} %fusion), channel_id=1, source_target_pairs={{0,4},{4,0},{8,12},{12,8},{1,5},{5,1},{9,13},{13,9},{2,6},{6,2},{1... | collective-permute-start | bytes 786440 | tf_op jit(solution)/shard_map/ppermute | solution.py:425
  53.4 4.3 %collective-permute-start.17 = (bf16[128,1024]{1,0:T(8,128)(2,1)S(1)}, bf16[128,1024]{1,0:T(8,128)(2,1)}, u32[]{:S(2)}, u32[]{:S(2)}) collective-permute-start(bf16[128,1024]{1,0:T(8,128)(2,1)S(1)} %copy-done.10), channel_id=1, source_target_pairs={{0,0},{4,8},{8,4},{12,12},{1,1},{5,9},{9,5},{13,13},{2,2},{6,10},{... | collective-permute-start | bytes 786440 | tf_op jit(solution)/shard_map/ppermute | solution.py:398
  59.5 4.1 %collective-permute-start.18 = (f32[128,128]{1,0:T(8,128)S(1)}, f32[128,128]{1,0:T(8,128)S(1)}, u32[]{:S(2)}, u32[]{:S(2)}) collective-permute-start(f32[128,128]{1,0:T(8,128)S(1)} %get-tuple-element.101), channel_id=1, source_target_pairs={{0,1},{1,0},{2,3},{3,2},{4,5},{5,4},{6,7},{7,6},{8,9},{9,8},{10,11... | collective-permute-start | bytes 196616 | tf_op jit(solution)/shard_map/ppermute | solution.py:21
  59.5 11.4 %collective-permute-start.20 = (bf16[128,1024]{1,0:T(8,128)(2,1)}, bf16[128,1024]{1,0:T(8,128)(2,1)S(1)}, u32[]{:S(2)}, u32[]{:S(2)}) collective-permute-start(bf16[128,1024]{1,0:T(8,128)(2,1)} %collective-permute-done.17.refs_10_), channel_id=1, source_target_pairs={{0,4},{4,0},{8,12},{12,8},{1,5},{5,1},{9,13},{13,9},{2,6},{6,2},{1... | collective-permute-start | bytes 786440 | tf_op jit(solution)/shard_map/ppermute | solution.py:398
  63.5 15.1 %collective-permute-start.19 = (bf16[128,1024]{1,0:T(8,128)(2,1)}, bf16[128,1024]{1,0:T(8,128)(2,1)S(1)}, u32[]{:S(2)}, u32[]{:S(2)}) collective-permute-start(bf16[128,1024]{1,0:T(8,128)(2,1)} %collective-permute-done.15.refs_4_), channel_id=1, source_target_pairs={{0,4},{4,0},{8,12},{12,8},{1,5},{5,1},{9,13},{13,9},{2,6},{6,2},{1... | collective-permute-start | bytes 786440 | tf_op jit(solution)/shard_map/ppermute | solution.py:398
  64.3 25.0 %all-to-all-start = ((bf16[8,160,128]{2,1,0:T(8,128)(2,1)}), bf16[8,160,128]{2,1,0:T(8,128)(2,1)S(1)}, u32[]{:S(2)}, u32[]{:S(2)}) async-start(bf16[8,160,128]{2,1,0:T(8,128)(2,1)} %shard_map.112), calls=%async_computation | async-start | bytes 655360 | tf_op jit(solution)/shard_map/all_to_all | solution.py:587
  86.5 1.3 %collective-permute-start.21 = (bf16[160,128]{1,0:T(8,128)(2,1)S(1)}, bf16[160,128]{1,0:T(8,128)(2,1)S(1)}, u32[]{:S(2)}, u32[]{:S(2)}) collective-permute-start(bf16[160,128]{1,0:T(8,128)(2,1)S(1)} %slice_bitcast_fusion.mine_ref), channel_id=1, source_target_pairs={{0,1},{1,0},{2,3},{3,2},{4,5},{5,4},{6,7},{7,6},{8,9},{9,8},{10,11... | collective-permute-start | bytes 122888 | tf_op jit(solution)/shard_map/ppermute | solution.py:21
  89.4 1.6 %collective-permute-start.22 = (bf16[8,160,128]{2,1,0:T(8,128)(2,1)S(1)}, bf16[8,160,128]{2,1,0:T(8,128)(2,1)S(1)}, u32[]{:S(2)}, u32[]{:S(2)}) collective-permute-start(bf16[8,160,128]{2,1,0:T(8,128)(2,1)S(1)} %all-to-all-done.refs_0_), channel_id=1, source_target_pairs={{0,1},{1,0},{2,3},{3,2},{4,5},{5,4},{6,7},{7,6},{8,9},{9,8},{10,11... | collective-permute-start | bytes 983048 | tf_op jit(solution)/shard_map/ppermute | solution.py:21
  (27 other events, 127.9 us)

commit v20 on v17

--- a/solution.py
+++ b/solution.py
@@ -345,25 +345,21 @@
         pl.when(fits)(copy.wait)
 
 
-def weight_kernel(scale, n_dp, n_seq, tok_ref, *refs):
-    lows = refs[:2]
-    bc_ref, dt_ref, low_ref, low_sem = refs[2:]
+def weight_kernel(scale, n_dp, n_seq, tok_ref, source_ref, *refs):
+    low_ref, low_sem = refs[-2:]
     rows = tok_ref.shape[1] // n_seq
-    share = lows[0].shape[1]
     core, me = lax.axis_index("head"), lax.axis_index("dp")
     copies = []
     for r in range(n_dp):
         for s in range(n_seq):
             index = s * n_dp + lax.rem(me - r + n_dp, n_dp)
-            for k in range(2):
-                row = pl.multiple_of(lax.rem(core + k, 2) * share, 16)
-                copies.append(
-                    pltpu.make_async_copy(
-                        lows[k].at[index],
-                        low_ref.at[r, pl.ds(row, share), pl.ds(s * rows, rows)],
-                        low_sem.at[r * n_seq + s, k],
-                    )
+            copies.append(
+                pltpu.make_async_copy(
+                    source_ref.at[index],
+                    low_ref.at[r, :, pl.ds(s * rows, rows)],
+                    low_sem.at[r * n_seq + s],
                 )
+            )
     for copy in copies:
         copy.start()
     for copy in copies:
@@ -372,11 +368,18 @@
     for r in range(1, n_dp):
         total = total + mm(low_ref[r], tok_ref[r], 1, 0)
     total = total * scale
-    half = bc_ref.shape[1] // 2
-    heads = dt_ref.shape[0] // 2
-    for k in range(2):
-        bc_ref[:, k * half : (k + 1) * half] = total[k * share : k * share + half].T
-        dt_ref[k * heads : (k + 1) * heads, :] = total[k * share + half : (k + 1) * share]
+    if len(refs) == 4:
+        bc_ref, dt_ref = refs[:2]
+        half = bc_ref.shape[1]
+        bc_ref[...] = total[:half].T
+        dt_ref[...] = total[half:]
+        return
+    own_bc, own_dt, bc_ref, dt_ref = refs[:4]
+    half, heads = own_bc.shape[1], own_dt.shape[0]
+    for k, (first, second) in enumerate(((own_bc[...], own_dt[...]), (total[:half].T, total[half:]))):
+        side = lax.rem(core + k, 2)
+        bc_ref[:, pl.ds(pl.multiple_of(side * half, 128), half)] = first
+        dt_ref[pl.ds(pl.multiple_of(side * heads, 8), heads), :] = second
 
 
 def relays(count):
@@ -597,19 +600,22 @@
     lows = after(lows, grads)
     swapped = cyclic(lows, "head", 1)
     cols = 2 * (rows + heads)
-    grad_bc, grad_dt = call(
-        functools.partial(weight_kernel, 1.0 / (rows * n_seq * n_dp), n_dp, n_seq),
-        (struct((part, 2 * state_n), F32), struct((2 * heads, part), F32)),
-        4.0,
-        ordered,
-        lows,
-        swapped,
-        limit=LIMIT + 2 * n_dp * n_seq * rows * cols,
-        scratch=(
-            pltpu.VMEM((n_dp, cols, n_seq * rows), BF),
-            pltpu.SemaphoreType.DMA((count, 2)),
-        ),
-    )
+    halves_made = []
+    for k, source in enumerate((lows, swapped)):
+        halves_made = call(
+            functools.partial(weight_kernel, 1.0 / (rows * n_seq * n_dp), n_dp, n_seq),
+            (struct((part, (k + 1) * state_n), F32), struct(((k + 1) * heads, part), F32)),
+            2.0,
+            ordered,
+            source,
+            *halves_made,
+            limit=LIMIT + 2 * n_dp * n_seq * rows * cols,
+            scratch=(
+                pltpu.VMEM((n_dp, rows + heads, n_seq * rows), BF),
+                pltpu.SemaphoreType.DMA((count,)),
+            ),
+        )
+    grad_bc, grad_dt = halves_made
     return grad_x[None], grads[None], grad_bc, grad_dt.T
 
 

time: 86.6 us -> 86.1 us (level)
    pallas_call x14 -> x15, Pallas kernels: 15 us -> 15.2 us  [call(): pl.pallas_call(kernel, out_shape=out_shape, grid=(1,), in_specs=specs or...]
  transfers between devices with their start and end apart: 24 -> 24, of which waited for: 13 -> 13; matrix products, arithmetic and copies ran while one was open for 2% -> 2% of each run, Pallas kernels for 14% -> 15%
where the time goes in v20:
time: 86.1 us; the launch traced here: 85.6 us
  starting transfers between devices  36.3 us (42%)
  waiting for transfers between devices  28.5 us (33%)
  Pallas kernels  15.2 us (18%)
  local copies, waits for them, and re-layouts  4.02 us (5%)
  between operations  1 us (1%)
    ppermute x6, starting transfers between devices, chains(): got[k] = lax.ppermute(value, 'seq', sorted(to.items()))  16.2 us
    pallas_call x15, Pallas kernels, call(): pl.pallas_call(kernel, out_shape=out_shape, grid=(1,), in_specs=specs or...  15.2 us
    ppermute x6, waiting for transfers between devices, chains(): got[k] = lax.ppermute(value, 'seq', sorted(to.items()))  11.3 us
    ppermute x8, starting transfers between devices, relay(): found[kind, hop] = lax.ppermute(source, 'seq', pairs[kind])  8.9 us
    ppermute x9, waiting for transfers between devices, cyclic(): return lax.ppermute(a, axis, [(i, (i + by) % count) for i in range(count)])  8.46 us
    ppermute x9, starting transfers between devices, cyclic(): return lax.ppermute(a, axis, [(i, (i + by) % count) for i in range(count)])  6.98 us
    ppermute x8, waiting for transfers between devices, relay(): found[kind, hop] = lax.ppermute(source, 'seq', pairs[kind])  5.4 us
    all_to_all x1, starting transfers between devices, body(): lows = lax.all_to_all(copies, ('seq', 'dp'), 0, 0, tiled=True)  4.17 us
  transfers between devices with their start and end apart: 24, of which 13 were waited for; matrix products, arithmetic and copies ran while one was open for 2% of the time, Pallas kernels for 15%

profile of v20, /device:TPU:0, one launch (start us, length us, event | category | flops | bytes accessed | tf_op | source)
XLA Modules:
  0.0 85.6 jit_solution(5561129508959480049)
XLA Ops:
  1.7 3.0 %collective-permute-start = (bf16[128,1024]{1,0:T(8,128)(2,1)S(1)}, bf16[128,1024]{1,0:T(8,128)(2,1)S(1)}, u32[]{:S(2)}, u32[]{:S(2)}) collective-permute-start(bf16[128,1024]{1,0:T(8,128)(2,1)S(1)} %get-tuple-element.59), channel_id=1, source_target_pairs={{0,2},{2,0},{1,3},{3,1},{4,6},{6,4},{5,7},{7,5},{8,10},{10,8},{9,1... | collective-permute-start | bytes 786440 | tf_op jit(solution)/shard_map/ppermute | solution.py:21
  4.7 1.6 %collective-permute-start.2 = (bf16[128,1024]{1,0:T(8,128)(2,1)S(1)}, bf16[128,1024]{1,0:T(8,128)(2,1)S(1)}, u32[]{:S(2)}, u32[]{:S(2)}) collective-permute-start(bf16[128,1024]{1,0:T(8,128)(2,1)S(1)} %get-tuple-element.58.a_ref.refs_0_), channel_id=1, source_target_pairs={{0,4},{4,0},{8,12},{12,8},{1,5},{5,1},{9,13},{13,9},{2,6},{6,2},{1... | collective-permute-start | bytes 786440 | tf_op jit(solution)/shard_map/ppermute | solution.py:401
  7.3 3.7 %collective-permute-done.a_ref.refs_6_ = bf16[128,1024]{1,0:T(8,128)(2,1)S(1)} collective-permute-done((bf16[128,1024]{1,0:T(8,128)(2,1)S(1)}, bf16[128,1024]{1,0:T(8,128)(2,1)S(1)}, u32[]{:S(2)}, u32[]{:S(2)}) %collective-permute-start) | collective-permute-done | bytes 262176 | tf_op jit(solution)/shard_map/ppermute | solution.py:21
  11.3 1.8 %collective-permute-start.1 = (f32[320,128]{1,0:T(8,128)S(1)}, f32[320,128]{1,0:T(8,128)S(1)}, u32[]{:S(2)}, u32[]{:S(2)}) collective-permute-start(f32[320,128]{1,0:T(8,128)S(1)} %shard_map.104), channel_id=1, source_target_pairs={{0,2},{2,0},{1,3},{3,1},{4,6},{6,4},{5,7},{7,5},{8,10},{10,8},{9,1... | collective-permute-start | bytes 491528 | tf_op jit(solution)/shard_map/ppermute | solution.py:21
  13.1 1.6 %collective-permute-start.6 = (bf16[128,1024]{1,0:T(8,128)(2,1)S(1)}, bf16[128,1024]{1,0:T(8,128)(2,1)S(1)}, u32[]{:S(2)}, u32[]{:S(2)}) collective-permute-start(bf16[128,1024]{1,0:T(8,128)(2,1)S(1)} %collective-permute-done.a_ref.refs_6_), channel_id=1, source_target_pairs={{0,4},{4,0},{8,12},{12,8},{1,5},{5,1},{9,13},{13,9},{2,6},{6,2},{1... | collective-permute-start | bytes 786440 | tf_op jit(solution)/shard_map/ppermute | solution.py:401
  18.2 2.1 %shard_map.105 = (f32[2,2,128,1024]{3,2,1,0:T(8,128)S(1)}, f32[256,128]{1,0:T(8,128)S(1)}, f32[160,128]{1,0:T(8,128)S(1)}, bf16[128,1024]{1,0:T(8,128)(2,1)S(1)}...) custom-call(f32[320,128]{1,0:T(8,128)S(1)} %shard_map.103.refs_0_, ...), custom_call_target="tpu_custom_call" | custom-call | flops 115000000 | bytes 1966336 | tf_op jit(solution)/shard_map/pallas_call | solution.py:54
  20.4 4.2 %collective-permute-start.8 = (bf16[128,1024]{1,0:T(8,128)(2,1)S(1)}, bf16[128,1024]{1,0:T(8,128)(2,1)S(1)}, u32[]{:S(2)}, u32[]{:S(2)}) collective-permute-start(bf16[128,1024]{1,0:T(8,128)(2,1)S(1)} %get-tuple-element.64), channel_id=1, source_target_pairs={{0,4},{4,0},{8,12},{12,8},{1,5},{5,1},{9,13},{13,9},{2,6},{6,2},{1... | collective-permute-start | bytes 786440 | tf_op jit(solution)/shard_map/ppermute | solution.py:428
  25.9 1.5 %collective-permute-start.13 = (bf16[1024,256]{1,0:T(8,128)(2,1)}, bf16[1024,256]{1,0:T(8,128)(2,1)S(1)}, u32[]{:S(2)}, u32[]{:S(2)}) collective-permute-start(bf16[1024,256]{1,0:T(8,128)(2,1)} %refs_0_.1), channel_id=1, source_target_pairs={{0,2},{2,0},{1,3},{3,1},{4,6},{6,4},{5,7},{7,5},{8,10},{10,8},{9,1... | collective-permute-start | bytes 1572872 | tf_op jit(solution)/shard_map/ppermute | solution.py:21
  28.4 2.1 %collective-permute-done.8.refs_3_ = bf16[128,1024]{1,0:T(8,128)(2,1)S(1)} collective-permute-done((bf16[128,1024]{1,0:T(8,128)(2,1)S(1)}, bf16[128,1024]{1,0:T(8,128)(2,1)S(1)}, u32[]{:S(2)}, u32[]{:S(2)}) %collective-permute-start.8) | collective-permute-done | bytes 262176 | tf_op jit(solution)/shard_map/ppermute | solution.py:428
  31.4 3.5 %collective-permute-start.9 = (bf16[128,1024]{1,0:T(8,128)(2,1)S(1)}, bf16[128,1024]{1,0:T(8,128)(2,1)S(1)}, u32[]{:S(2)}, u32[]{:S(2)}) collective-permute-start(bf16[128,1024]{1,0:T(8,128)(2,1)S(1)} %broadcast_select_fusion), channel_id=1, source_target_pairs={{0,4},{4,0},{8,12},{12,8},{1,5},{5,1},{9,13},{13,9},{2,6},{6,2},{1... | collective-permute-start | bytes 786440 | tf_op jit(solution)/shard_map/ppermute | solution.py:428
  35.9 3.5 %collective-permute-done.9.refs_9_ = bf16[128,1024]{1,0:T(8,128)(2,1)S(1)} collective-permute-done((bf16[128,1024]{1,0:T(8,128)(2,1)S(1)}, bf16[128,1024]{1,0:T(8,128)(2,1)S(1)}, u32[]{:S(2)}, u32[]{:S(2)}) %collective-permute-start.9) | collective-permute-done | bytes 262176 | tf_op jit(solution)/shard_map/ppermute | solution.py:428
  40.4 4.8 %collective-permute-start.12 = (bf16[128,1024]{1,0:T(8,128)(2,1)S(1)}, bf16[128,1024]{1,0:T(8,128)(2,1)S(1)}, u32[]{:S(2)}, u32[]{:S(2)}) collective-permute-start(bf16[128,1024]{1,0:T(8,128)(2,1)S(1)} %get-tuple-element.112), channel_id=1, source_target_pairs={{0,4},{4,0},{8,12},{12,8},{1,5},{5,1},{9,13},{13,9},{2,6},{6,2},{1... | collective-permute-start | bytes 786440 | tf_op jit(solution)/shard_map/ppermute | solution.py:428
  46.3 3.9 %collective-permute-done.12 = bf16[128,1024]{1,0:T(8,128)(2,1)S(1)} collective-permute-done((bf16[128,1024]{1,0:T(8,128)(2,1)S(1)}, bf16[128,1024]{1,0:T(8,128)(2,1)S(1)}, u32[]{:S(2)}, u32[]{:S(2)}) %collective-permute-start.12) | collective-permute-done | bytes 262176 | tf_op jit(solution)/shard_map/ppermute | solution.py:428
  50.3 2.4 %collective-permute-start.16 = (bf16[128,1024]{1,0:T(8,128)(2,1)S(1)}, bf16[128,1024]{1,0:T(8,128)(2,1)S(1)}, u32[]{:S(2)}, u32[]{:S(2)}) collective-permute-start(bf16[128,1024]{1,0:T(8,128)(2,1)S(1)} %fusion), channel_id=1, source_target_pairs={{0,4},{4,0},{8,12},{12,8},{1,5},{5,1},{9,13},{13,9},{2,6},{6,2},{1... | collective-permute-start | bytes 786440 | tf_op jit(solution)/shard_map/ppermute | solution.py:428
  53.4 1.9 %shard_map.110 = (bf16[128,2048]{1,0:T(8,128)(2,1)}, f32[272,128]{1,0:T(8,128)S(1)}) custom-call(bf16[3,128,1024]{2,1,0:T(8,128)(2,1)S(1)} %bitcast_dynamic-update-slice_fusion.refs_0_, bf16[128,2048]{1,0:T(8,128)(2,1)S(1)} %bitcast.45, bf16[128,2048]{1,0:T(8,128)(2,1)S(1)} %bitcast.52, f32[256,128]{1,0:T(8,128)S(1)} %get-tuple-element.88.bc_ref.refs_3_, ...), custom_call_target="tpu_custom_call" | custom-call | flops 3104999936 | bytes 2719872 | tf_op jit(solution)/shard_map/pallas_call | solution.py:54
  56.3 1.8 %collective-permute-done.16 = bf16[128,1024]{1,0:T(8,128)(2,1)S(1)} collective-permute-done((bf16[128,1024]{1,0:T(8,128)(2,1)S(1)}, bf16[128,1024]{1,0:T(8,128)(2,1)S(1)}, u32[]{:S(2)}, u32[]{:S(2)}) %collective-permute-start.16) | collective-permute-done | bytes 262176 | tf_op jit(solution)/shard_map/ppermute | solution.py:428
  58.1 3.0 %collective-permute-start.20 = (bf16[128,1024]{1,0:T(8,128)(2,1)S(1)}, bf16[128,1024]{1,0:T(8,128)(2,1)S(1)}, u32[]{:S(2)}, u32[]{:S(2)}) collective-permute-start(bf16[128,1024]{1,0:T(8,128)(2,1)S(1)} %collective-permute-done.17.refs_10_), channel_id=1, source_target_pairs={{0,4},{4,0},{8,12},{12,8},{1,5},{5,1},{9,13},{13,9},{2,6},{6,2},{1... | collective-permute-start | bytes 786440 | tf_op jit(solution)/shard_map/ppermute | solution.py:401
  61.2 1.7 %shard_map.111 = (bf16[128,2048]{1,0:T(8,128)(2,1)}, f32[160,128]{1,0:T(8,128)S(1)}, f32[128,128]{1,0:T(8,128)S(1)}) custom-call(bf16[3,128,1024]{2,1,0:T(8,128)(2,1)S(1)} %bitcast_dynamic-update-slice_fusion.3.refs_0_, bf16[128,2048]{1,0:T(8,128)(2,1)S(1)} %bitcast.47, bf16[128,2048]{1,0:T(8,128)(2,1)S(1)} %bitcast.54, ...), custom_call_target="tpu_custom_call", output_to_operand_aliasing={{0}: (12, {})} | custom-call | flops 3104999936 | bytes 3383424 | tf_op jit(solution)/shard_map/pallas_call | solution.py:54
  62.9 2.6 %collective-permute-done.20.refs_11_ = bf16[128,1024]{1,0:T(8,128)(2,1)S(1)} collective-permute-done((bf16[128,1024]{1,0:T(8,128)(2,1)S(1)}, bf16[128,1024]{1,0:T(8,128)(2,1)S(1)}, u32[]{:S(2)}, u32[]{:S(2)}) %collective-permute-start.20) | collective-permute-done | bytes 262176 | tf_op jit(solution)/shard_map/ppermute | solution.py:401
  65.5 2.8 %collective-permute-done.19.refs_5_ = bf16[128,1024]{1,0:T(8,128)(2,1)S(1)} collective-permute-done((bf16[128,1024]{1,0:T(8,128)(2,1)S(1)}, bf16[128,1024]{1,0:T(8,128)(2,1)S(1)}, u32[]{:S(2)}, u32[]{:S(2)}) %collective-permute-start.19) | collective-permute-done | bytes 262176 | tf_op jit(solution)/shard_map/ppermute | solution.py:401
  69.4 4.2 %all-to-all-start = ((bf16[8,160,128]{2,1,0:T(8,128)(2,1)}), bf16[8,160,128]{2,1,0:T(8,128)(2,1)S(1)}, u32[]{:S(2)}, u32[]{:S(2)}) async-start(bf16[8,160,128]{2,1,0:T(8,128)(2,1)} %shard_map.113), calls=%async_computation | async-start | bytes 655360 | tf_op jit(solution)/shard_map/all_to_all | solution.py:590
  77.4 1.5 %shard_map.114 = bf16[128,2048]{1,0:T(8,128)(2,1)} custom-call(bf16[160,128]{1,0:T(8,128)(2,1)S(1)} %slice_bitcast_fusion.mine_ref, bf16[160,128]{1,0:T(8,128)(2,1)S(1)} %collective-permute-done.21.other_ref, bf16[1024,256]{1,0:T(8,128)(2,1)S(1)} %copy-done.8, bf16[64,1024]{1,0:T(8,128)(2,1)S(1)} %bitcast.67, bf16[1024,256]{1,0:T(8,128)(2,1)S(1)} %copy-done.10, ...), custom_call_target="tpu_custom_call" | custom-call | flops 3335000064 | bytes 1392640 | tf_op jit(solution)/shard_map/pallas_call | solution.py:54
  78.9 3.3 %all-to-all-done.source_ref = bf16[8,160,128]{2,1,0:T(8,128)(2,1)S(1)} async-done(((bf16[8,160,128]{2,1,0:T(8,128)(2,1)}), bf16[8,160,128]{2,1,0:T(8,128)(2,1)S(1)}, u32[]{:S(2)}, u32[]{:S(2)}) %all-to-all-start) | async-done | bytes 327712 | tf_op jit(solution)/shard_map/all_to_all | solution.py:590
  83.9 1.7 %shard_map.116 = (f32[1024,256]{1,0:T(8,128)}, f32[64,1024]{1,0:T(8,128)}) custom-call(bf16[2,512,1024]{2,1,0:T(8,128)(2,1)S(1)} %shard_map.112.tok_ref, bf16[8,160,128]{2,1,0:T(8,128)(2,1)S(1)} %collective-permute-done.22.source_ref, f32[1024,128]{1,0:T(8,128)S(1)} %get-tuple-element.108.refs_0_, f32[32,1024]{1,0:T(8,128)S(1)} %get-tuple-element.109.refs_1_), custom_call_target="tpu_custom_call" | custom-call | flops 2300000000 | bytes 3080192 | tf_op jit(solution)/shard_map/pallas_call | solution.py:54
  (82 shorter events, 20.4 us)
Async XLA Ops:
  1.7 9.3 %collective-permute-start = (bf16[128,1024]{1,0:T(8,128)(2,1)S(1)}, bf16[128,1024]{1,0:T(8,128)(2,1)S(1)}, u32[]{:S(2)}, u32[]{:S(2)}) collective-permute-start(bf16[128,1024]{1,0:T(8,128)(2,1)S(1)} %get-tuple-element.59), channel_id=1, source_target_pairs={{0,2},{2,0},{1,3},{3,1},{4,6},{6,4},{5,7},{7,5},{8,10},{10,8},{9,1... | collective-permute-start | bytes 786440 | tf_op jit(solution)/shard_map/ppermute | solution.py:21
  4.7 10.7 %collective-permute-start.2 = (bf16[128,1024]{1,0:T(8,128)(2,1)S(1)}, bf16[128,1024]{1,0:T(8,128)(2,1)S(1)}, u32[]{:S(2)}, u32[]{:S(2)}) collective-permute-start(bf16[128,1024]{1,0:T(8,128)(2,1)S(1)} %get-tuple-element.58.a_ref.refs_0_), channel_id=1, source_target_pairs={{0,4},{4,0},{8,12},{12,8},{1,5},{5,1},{9,13},{13,9},{2,6},{6,2},{1... | collective-permute-start | bytes 786440 | tf_op jit(solution)/shard_map/ppermute | solution.py:401
  6.3 9.2 %collective-permute-start.3 = (bf16[128,1024]{1,0:T(8,128)(2,1)S(1)}, bf16[128,1024]{1,0:T(8,128)(2,1)S(1)}, u32[]{:S(2)}, u32[]{:S(2)}) collective-permute-start(bf16[128,1024]{1,0:T(8,128)(2,1)S(1)} %get-tuple-element.58.a_ref.refs_0_), channel_id=1, source_target_pairs={{0,0},{4,8},{8,4},{12,12},{1,1},{5,9},{9,5},{13,13},{2,2},{6,10},{... | collective-permute-start | bytes 786440 | tf_op jit(solution)/shard_map/ppermute | solution.py:401
  11.3 5.5 %collective-permute-start.1 = (f32[320,128]{1,0:T(8,128)S(1)}, f32[320,128]{1,0:T(8,128)S(1)}, u32[]{:S(2)}, u32[]{:S(2)}) collective-permute-start(f32[320,128]{1,0:T(8,128)S(1)} %shard_map.104), channel_id=1, source_target_pairs={{0,2},{2,0},{1,3},{3,1},{4,6},{6,4},{5,7},{7,5},{8,10},{10,8},{9,1... | collective-permute-start | bytes 491528 | tf_op jit(solution)/shard_map/ppermute | solution.py:21
  13.1 7.2 %collective-permute-start.6 = (bf16[128,1024]{1,0:T(8,128)(2,1)S(1)}, bf16[128,1024]{1,0:T(8,128)(2,1)S(1)}, u32[]{:S(2)}, u32[]{:S(2)}) collective-permute-start(bf16[128,1024]{1,0:T(8,128)(2,1)S(1)} %collective-permute-done.a_ref.refs_6_), channel_id=1, source_target_pairs={{0,4},{4,0},{8,12},{12,8},{1,5},{5,1},{9,13},{13,9},{2,6},{6,2},{1... | collective-permute-start | bytes 786440 | tf_op jit(solution)/shard_map/ppermute | solution.py:401
  14.7 5.7 %collective-permute-start.7 = (bf16[128,1024]{1,0:T(8,128)(2,1)S(1)}, bf16[128,1024]{1,0:T(8,128)(2,1)S(1)}, u32[]{:S(2)}, u32[]{:S(2)}) collective-permute-start(bf16[128,1024]{1,0:T(8,128)(2,1)S(1)} %collective-permute-done.a_ref.refs_6_), channel_id=1, source_target_pairs={{0,0},{4,8},{8,4},{12,12},{1,1},{5,9},{9,5},{13,13},{2,2},{6,10},{... | collective-permute-start | bytes 786440 | tf_op jit(solution)/shard_map/ppermute | solution.py:401
  15.4 1.5 %collective-permute-start.4 = (f32[320,128]{1,0:T(8,128)S(1)}, f32[320,128]{1,0:T(8,128)S(1)}, u32[]{:S(2)}, u32[]{:S(2)}) collective-permute-start(f32[320,128]{1,0:T(8,128)S(1)} %shard_map.103.refs_0_), channel_id=1, source_target_pairs={{0,1},{1,0},{2,3},{3,2},{4,5},{5,4},{6,7},{7,6},{8,9},{9,8},{10,11... | collective-permute-start | bytes 491528 | tf_op jit(solution)/shard_map/ppermute | solution.py:21
  16.8 1.4 %collective-permute-start.5 = (f32[320,128]{1,0:T(8,128)S(1)}, f32[320,128]{1,0:T(8,128)S(1)}, u32[]{:S(2)}, u32[]{:S(2)}) collective-permute-start(f32[320,128]{1,0:T(8,128)S(1)} %collective-permute-done.1.refs_1_), channel_id=1, source_target_pairs={{0,1},{1,0},{2,3},{3,2},{4,5},{5,4},{6,7},{7,6},{8,9},{9,8},{10,11... | collective-permute-start | bytes 491528 | tf_op jit(solution)/shard_map/ppermute | solution.py:21
  20.4 10.1 %collective-permute-start.8 = (bf16[128,1024]{1,0:T(8,128)(2,1)S(1)}, bf16[128,1024]{1,0:T(8,128)(2,1)S(1)}, u32[]{:S(2)}, u32[]{:S(2)}) collective-permute-start(bf16[128,1024]{1,0:T(8,128)(2,1)S(1)} %get-tuple-element.64), channel_id=1, source_target_pairs={{0,4},{4,0},{8,12},{12,8},{1,5},{5,1},{9,13},{13,9},{2,6},{6,2},{1... | collective-permute-start | bytes 786440 | tf_op jit(solution)/shard_map/ppermute | solution.py:428
  24.6 21.6 %collective-permute-start.15 = (bf16[128,1024]{1,0:T(8,128)(2,1)S(1)}, bf16[128,1024]{1,0:T(8,128)(2,1)S(1)}, u32[]{:S(2)}, u32[]{:S(2)}) collective-permute-start(bf16[128,1024]{1,0:T(8,128)(2,1)S(1)} %collective-permute-done.2.refs_1_), channel_id=1, source_target_pairs={{0,0},{4,8},{8,4},{12,12},{1,1},{5,9},{9,5},{13,13},{2,2},{6,10},{... | collective-permute-start | bytes 786440 | tf_op jit(solution)/shard_map/ppermute | solution.py:401
  25.3 20.9 %collective-permute-start.14 = (bf16[64,1024]{1,0:T(8,128)(2,1)S(1)}, bf16[64,1024]{1,0:T(8,128)(2,1)S(1)}, u32[]{:S(2)}, u32[]{:S(2)}) collective-permute-start(bf16[64,1024]{1,0:T(8,128)(2,1)S(1)} %bitcast.66), channel_id=1, source_target_pairs={{0,2},{2,0},{1,3},{3,1},{4,6},{6,4},{5,7},{7,5},{8,10},{10,8},{9,1... | collective-permute-start | bytes 393224 | tf_op jit(solution)/shard_map/ppermute | solution.py:21
  25.9 20.4 %collective-permute-start.13 = (bf16[1024,256]{1,0:T(8,128)(2,1)}, bf16[1024,256]{1,0:T(8,128)(2,1)S(1)}, u32[]{:S(2)}, u32[]{:S(2)}) collective-permute-start(bf16[1024,256]{1,0:T(8,128)(2,1)} %refs_0_.1), channel_id=1, source_target_pairs={{0,2},{2,0},{1,3},{3,1},{4,6},{6,4},{5,7},{7,5},{8,10},{10,8},{9,1... | collective-permute-start | bytes 1572872 | tf_op jit(solution)/shard_map/ppermute | solution.py:21
  30.6 5.3 %collective-permute-start.10 = (bf16[128,1024]{1,0:T(8,128)(2,1)S(1)}, bf16[128,1024]{1,0:T(8,128)(2,1)S(1)}, u32[]{:S(2)}, u32[]{:S(2)}) collective-permute-start(bf16[128,1024]{1,0:T(8,128)(2,1)S(1)} %fusion.3), channel_id=1, source_target_pairs={{0,0},{4,8},{8,4},{12,12},{1,1},{5,9},{9,5},{13,13},{2,2},{6,10},{... | collective-permute-start | bytes 786440 | tf_op jit(solution)/shard_map/ppermute | solution.py:428
  31.4 8.0 %collective-permute-start.9 = (bf16[128,1024]{1,0:T(8,128)(2,1)S(1)}, bf16[128,1024]{1,0:T(8,128)(2,1)S(1)}, u32[]{:S(2)}, u32[]{:S(2)}) collective-permute-start(bf16[128,1024]{1,0:T(8,128)(2,1)S(1)} %broadcast_select_fusion), channel_id=1, source_target_pairs={{0,4},{4,0},{8,12},{12,8},{1,5},{5,1},{9,13},{13,9},{2,6},{6,2},{1... | collective-permute-start | bytes 786440 | tf_op jit(solution)/shard_map/ppermute | solution.py:428
  39.7 6.6 %collective-permute-start.11 = (bf16[128,1024]{1,0:T(8,128)(2,1)S(1)}, bf16[128,1024]{1,0:T(8,128)(2,1)S(1)}, u32[]{:S(2)}, u32[]{:S(2)}) collective-permute-start(bf16[128,1024]{1,0:T(8,128)(2,1)S(1)} %get-tuple-element.113), channel_id=1, source_target_pairs={{0,0},{4,8},{8,4},{12,12},{1,1},{5,9},{9,5},{13,13},{2,2},{6,10},{... | collective-permute-start | bytes 786440 | tf_op jit(solution)/shard_map/ppermute | solution.py:428
  40.4 9.8 %collective-permute-start.12 = (bf16[128,1024]{1,0:T(8,128)(2,1)S(1)}, bf16[128,1024]{1,0:T(8,128)(2,1)S(1)}, u32[]{:S(2)}, u32[]{:S(2)}) collective-permute-start(bf16[128,1024]{1,0:T(8,128)(2,1)S(1)} %get-tuple-element.112), channel_id=1, source_target_pairs={{0,4},{4,0},{8,12},{12,8},{1,5},{5,1},{9,13},{13,9},{2,6},{6,2},{1... | collective-permute-start | bytes 786440 | tf_op jit(solution)/shard_map/ppermute | solution.py:428
  50.3 7.7 %collective-permute-start.16 = (bf16[128,1024]{1,0:T(8,128)(2,1)S(1)}, bf16[128,1024]{1,0:T(8,128)(2,1)S(1)}, u32[]{:S(2)}, u32[]{:S(2)}) collective-permute-start(bf16[128,1024]{1,0:T(8,128)(2,1)S(1)} %fusion), channel_id=1, source_target_pairs={{0,4},{4,0},{8,12},{12,8},{1,5},{5,1},{9,13},{13,9},{2,6},{6,2},{1... | collective-permute-start | bytes 786440 | tf_op jit(solution)/shard_map/ppermute | solution.py:428
  52.7 3.6 %collective-permute-start.17 = (bf16[128,1024]{1,0:T(8,128)(2,1)S(1)}, bf16[128,1024]{1,0:T(8,128)(2,1)S(1)}, u32[]{:S(2)}, u32[]{:S(2)}) collective-permute-start(bf16[128,1024]{1,0:T(8,128)(2,1)S(1)} %collective-permute-done.6.refs_7_), channel_id=1, source_target_pairs={{0,0},{4,8},{8,4},{12,12},{1,1},{5,9},{9,5},{13,13},{2,2},{6,10},{... | collective-permute-start | bytes 786440 | tf_op jit(solution)/shard_map/ppermute | solution.py:401
  58.1 7.4 %collective-permute-start.20 = (bf16[128,1024]{1,0:T(8,128)(2,1)S(1)}, bf16[128,1024]{1,0:T(8,128)(2,1)S(1)}, u32[]{:S(2)}, u32[]{:S(2)}) collective-permute-start(bf16[128,1024]{1,0:T(8,128)(2,1)S(1)} %collective-permute-done.17.refs_10_), channel_id=1, source_target_pairs={{0,4},{4,0},{8,12},{12,8},{1,5},{5,1},{9,13},{13,9},{2,6},{6,2},{1... | collective-permute-start | bytes 786440 | tf_op jit(solution)/shard_map/ppermute | solution.py:401
  61.1 7.2 %collective-permute-start.19 = (bf16[128,1024]{1,0:T(8,128)(2,1)S(1)}, bf16[128,1024]{1,0:T(8,128)(2,1)S(1)}, u32[]{:S(2)}, u32[]{:S(2)}) collective-permute-start(bf16[128,1024]{1,0:T(8,128)(2,1)S(1)} %collective-permute-done.15.refs_4_), channel_id=1, source_target_pairs={{0,4},{4,0},{8,12},{12,8},{1,5},{5,1},{9,13},{13,9},{2,6},{6,2},{1... | collective-permute-start | bytes 786440 | tf_op jit(solution)/shard_map/ppermute | solution.py:401
  62.9 5.7 %collective-permute-start.18 = (f32[128,128]{1,0:T(8,128)S(1)}, f32[128,128]{1,0:T(8,128)S(1)}, u32[]{:S(2)}, u32[]{:S(2)}) collective-permute-start(f32[128,128]{1,0:T(8,128)S(1)} %get-tuple-element.103), channel_id=1, source_target_pairs={{0,1},{1,0},{2,3},{3,2},{4,5},{5,4},{6,7},{7,6},{8,9},{9,8},{10,11... | collective-permute-start | bytes 196616 | tf_op jit(solution)/shard_map/ppermute | solution.py:21
  69.4 12.8 %all-to-all-start = ((bf16[8,160,128]{2,1,0:T(8,128)(2,1)}), bf16[8,160,128]{2,1,0:T(8,128)(2,1)S(1)}, u32[]{:S(2)}, u32[]{:S(2)}) async-start(bf16[8,160,128]{2,1,0:T(8,128)(2,1)} %shard_map.113), calls=%async_computation | async-start | bytes 655360 | tf_op jit(solution)/shard_map/all_to_all | solution.py:590
  74.4 1.2 %collective-permute-start.21 = (bf16[160,128]{1,0:T(8,128)(2,1)S(1)}, bf16[160,128]{1,0:T(8,128)(2,1)S(1)}, u32[]{:S(2)}, u32[]{:S(2)}) collective-permute-start(bf16[160,128]{1,0:T(8,128)(2,1)S(1)} %slice_bitcast_fusion.mine_ref), channel_id=1, source_target_pairs={{0,1},{1,0},{2,3},{3,2},{4,5},{5,4},{6,7},{7,6},{8,9},{9,8},{10,11... | collective-permute-start | bytes 122888 | tf_op jit(solution)/shard_map/ppermute | solution.py:21
  82.2 1.6 %collective-permute-start.22 = (bf16[8,160,128]{2,1,0:T(8,128)(2,1)S(1)}, bf16[8,160,128]{2,1,0:T(8,128)(2,1)S(1)}, u32[]{:S(2)}, u32[]{:S(2)}) collective-permute-start(bf16[8,160,128]{2,1,0:T(8,128)(2,1)S(1)} %all-to-all-done.source_ref), channel_id=1, source_target_pairs={{0,1},{1,0},{2,3},{3,2},{4,5},{5,4},{6,7},{7,6},{8,9},{9,8},{10,11... | collective-permute-start | bytes 983048 | tf_op jit(solution)/shard_map/ppermute | solution.py:21
  (15 other events, 128.5 us)

commit v21 on v20

--- a/solution.py
+++ b/solution.py
@@ -508,7 +508,7 @@
     shared = []
 
     def inner(q, *others):
-        held = after(bc, *others) if others else bc
+        held = after(bc, *others, *(spare if q == 0 else [])) if others else bc
         square = struct((rows, rows), F32)
         block = pl.BlockSpec((rows, span), lambda _: (0, q))
         out = call(
@@ -539,7 +539,7 @@
     def late(*others):
         return relay(found[1], groups[1], second, *others) if n_dp > 1 else []
 
-    first[0] = after(first[0], *spare)
+    first[0] = after(first[0], *spare[: 1 if ride else 2])
     riders = [f[1, 1] for f in found] if ride else []
     calls = [functools.partial(inner, q) for q in range(PARTS)]
     stores, inners = chains(first, own, decay, calls, beside, riders, late)

time: 86.1 us -> 86.5 us (level)
  waiting for transfers between devices: 28.5 us -> 30.3 us
  starting transfers between devices: 36.3 us -> 34.8 us
    ppermute x6, starting transfers between devices: 16.2 us -> 14.5 us  [chains(): got[k] = lax.ppermute(value, 'seq', sorted(to.items()))]
    ppermute x8, waiting for transfers between devices: 5.4 us -> 6.51 us  [relay(): found[kind, hop] = lax.ppermute(source, 'seq', pairs[kind])]
    ppermute x8, starting transfers between devices: 8.9 us -> 9.87 us  [relay(): found[kind, hop] = lax.ppermute(source, 'seq', pairs[kind])]
where the time goes in v21:
time: 86.5 us; the launch traced here: 86 us
  starting transfers between devices  34.8 us (40%)
  waiting for transfers between devices  30.3 us (35%)
  Pallas kernels  15.2 us (18%)
  local copies, waits for them, and re-layouts  4.02 us (5%)
  between operations  1 us (1%)
    pallas_call x15, Pallas kernels, call(): pl.pallas_call(kernel, out_shape=out_shape, grid=(1,), in_specs=specs or...  15.2 us
    ppermute x6, starting transfers between devices, chains(): got[k] = lax.ppermute(value, 'seq', sorted(to.items()))  14.5 us
    ppermute x6, waiting for transfers between devices, chains(): got[k] = lax.ppermute(value, 'seq', sorted(to.items()))  12.1 us
    ppermute x8, starting transfers between devices, relay(): found[kind, hop] = lax.ppermute(source, 'seq', pairs[kind])  9.87 us
    ppermute x9, waiting for transfers between devices, cyclic(): return lax.ppermute(a, axis, [(i, (i + by) % count) for i in range(count)])  8.46 us
    ppermute x9, starting transfers between devices, cyclic(): return lax.ppermute(a, axis, [(i, (i + by) % count) for i in range(count)])  6.98 us
    ppermute x8, waiting for transfers between devices, relay(): found[kind, hop] = lax.ppermute(source, 'seq', pairs[kind])  6.51 us
    all_to_all x1, starting transfers between devices, body(): lows = lax.all_to_all(copies, ('seq', 'dp'), 0, 0, tiled=True)  3.43 us
  transfers between devices with their start and end apart: 24, of which 13 were waited for; matrix products, arithmetic and copies ran while one was open for 2% of the time, Pallas kernels for 15%

profile of v21, /device:TPU:0, one launch (start us, length us, event | category | flops | bytes accessed | tf_op | source)
XLA Modules:
  0.0 86.0 jit_solution(12980438536957288562)
XLA Ops:
  1.7 3.0 %collective-permute-start = (bf16[128,1024]{1,0:T(8,128)(2,1)S(1)}, bf16[128,1024]{1,0:T(8,128)(2,1)S(1)}, u32[]{:S(2)}, u32[]{:S(2)}) collective-permute-start(bf16[128,1024]{1,0:T(8,128)(2,1)S(1)} %get-tuple-element.59), channel_id=1, source_target_pairs={{0,2},{2,0},{1,3},{3,1},{4,6},{6,4},{5,7},{7,5},{8,10},{10,8},{9,1... | collective-permute-start | bytes 786440 | tf_op jit(solution)/shard_map/ppermute | solution.py:21
  4.7 1.6 %collective-permute-start.2 = (bf16[128,1024]{1,0:T(8,128)(2,1)S(1)}, bf16[128,1024]{1,0:T(8,128)(2,1)S(1)}, u32[]{:S(2)}, u32[]{:S(2)}) collective-permute-start(bf16[128,1024]{1,0:T(8,128)(2,1)S(1)} %get-tuple-element.58.a_ref.refs_0_), channel_id=1, source_target_pairs={{0,4},{4,0},{8,12},{12,8},{1,5},{5,1},{9,13},{13,9},{2,6},{6,2},{1... | collective-permute-start | bytes 786440 | tf_op jit(solution)/shard_map/ppermute | solution.py:401
  7.3 3.7 %collective-permute-done.a_ref.refs_6_ = bf16[128,1024]{1,0:T(8,128)(2,1)S(1)} collective-permute-done((bf16[128,1024]{1,0:T(8,128)(2,1)S(1)}, bf16[128,1024]{1,0:T(8,128)(2,1)S(1)}, u32[]{:S(2)}, u32[]{:S(2)}) %collective-permute-start) | collective-permute-done | bytes 262176 | tf_op jit(solution)/shard_map/ppermute | solution.py:21
  11.3 1.8 %collective-permute-start.1 = (f32[320,128]{1,0:T(8,128)S(1)}, f32[320,128]{1,0:T(8,128)S(1)}, u32[]{:S(2)}, u32[]{:S(2)}) collective-permute-start(f32[320,128]{1,0:T(8,128)S(1)} %shard_map.104), channel_id=1, source_target_pairs={{0,2},{2,0},{1,3},{3,1},{4,6},{6,4},{5,7},{7,5},{8,10},{10,8},{9,1... | collective-permute-start | bytes 491528 | tf_op jit(solution)/shard_map/ppermute | solution.py:21
  13.1 1.6 %collective-permute-start.6 = (bf16[128,1024]{1,0:T(8,128)(2,1)S(1)}, bf16[128,1024]{1,0:T(8,128)(2,1)S(1)}, u32[]{:S(2)}, u32[]{:S(2)}) collective-permute-start(bf16[128,1024]{1,0:T(8,128)(2,1)S(1)} %collective-permute-done.a_ref.refs_6_), channel_id=1, source_target_pairs={{0,4},{4,0},{8,12},{12,8},{1,5},{5,1},{9,13},{13,9},{2,6},{6,2},{1... | collective-permute-start | bytes 786440 | tf_op jit(solution)/shard_map/ppermute | solution.py:401
  16.9 1.3 %collective-permute-done.5.refs_3_ = f32[320,128]{1,0:T(8,128)S(1)} collective-permute-done((f32[320,128]{1,0:T(8,128)S(1)}, f32[320,128]{1,0:T(8,128)S(1)}, u32[]{:S(2)}, u32[]{:S(2)}) %collective-permute-start.5) | collective-permute-done | bytes 163872 | tf_op jit(solution)/shard_map/ppermute | solution.py:21
  18.2 2.1 %shard_map.105 = (f32[2,2,128,1024]{3,2,1,0:T(8,128)S(1)}, f32[256,128]{1,0:T(8,128)S(1)}, f32[160,128]{1,0:T(8,128)S(1)}, bf16[128,1024]{1,0:T(8,128)(2,1)S(1)}...) custom-call(f32[320,128]{1,0:T(8,128)S(1)} %shard_map.103.refs_0_, ...), custom_call_target="tpu_custom_call" | custom-call | flops 115000000 | bytes 1966336 | tf_op jit(solution)/shard_map/pallas_call | solution.py:54
  20.4 3.4 %collective-permute-start.7 = (bf16[128,1024]{1,0:T(8,128)(2,1)S(1)}, bf16[128,1024]{1,0:T(8,128)(2,1)S(1)}, u32[]{:S(2)}, u32[]{:S(2)}) collective-permute-start(bf16[128,1024]{1,0:T(8,128)(2,1)S(1)} %get-tuple-element.64), channel_id=1, source_target_pairs={{0,4},{4,0},{8,12},{12,8},{1,5},{5,1},{9,13},{13,9},{2,6},{6,2},{1... | collective-permute-start | bytes 786440 | tf_op jit(solution)/shard_map/ppermute | solution.py:428
  25.0 1.5 %collective-permute-start.13 = (bf16[1024,256]{1,0:T(8,128)(2,1)}, bf16[1024,256]{1,0:T(8,128)(2,1)S(1)}, u32[]{:S(2)}, u32[]{:S(2)}) collective-permute-start(bf16[1024,256]{1,0:T(8,128)(2,1)} %refs_0_.1), channel_id=1, source_target_pairs={{0,2},{2,0},{1,3},{3,1},{4,6},{6,4},{5,7},{7,5},{8,10},{10,8},{9,1... | collective-permute-start | bytes 1572872 | tf_op jit(solution)/shard_map/ppermute | solution.py:21
  27.6 2.9 %collective-permute-done.7.refs_3_ = bf16[128,1024]{1,0:T(8,128)(2,1)S(1)} collective-permute-done((bf16[128,1024]{1,0:T(8,128)(2,1)S(1)}, bf16[128,1024]{1,0:T(8,128)(2,1)S(1)}, u32[]{:S(2)}, u32[]{:S(2)}) %collective-permute-start.7) | collective-permute-done | bytes 262176 | tf_op jit(solution)/shard_map/ppermute | solution.py:428
  31.4 3.0 %collective-permute-start.9 = (bf16[128,1024]{1,0:T(8,128)(2,1)S(1)}, bf16[128,1024]{1,0:T(8,128)(2,1)S(1)}, u32[]{:S(2)}, u32[]{:S(2)}) collective-permute-start(bf16[128,1024]{1,0:T(8,128)(2,1)S(1)} %broadcast_select_fusion), channel_id=1, source_target_pairs={{0,4},{4,0},{8,12},{12,8},{1,5},{5,1},{9,13},{13,9},{2,6},{6,2},{1... | collective-permute-start | bytes 786440 | tf_op jit(solution)/shard_map/ppermute | solution.py:428
  35.4 4.9 %collective-permute-done.9.refs_9_ = bf16[128,1024]{1,0:T(8,128)(2,1)S(1)} collective-permute-done((bf16[128,1024]{1,0:T(8,128)(2,1)S(1)}, bf16[128,1024]{1,0:T(8,128)(2,1)S(1)}, u32[]{:S(2)}, u32[]{:S(2)}) %collective-permute-start.9) | collective-permute-done | bytes 262176 | tf_op jit(solution)/shard_map/ppermute | solution.py:428
  41.4 4.8 %collective-permute-start.12 = (bf16[128,1024]{1,0:T(8,128)(2,1)S(1)}, bf16[128,1024]{1,0:T(8,128)(2,1)S(1)}, u32[]{:S(2)}, u32[]{:S(2)}) collective-permute-start(bf16[128,1024]{1,0:T(8,128)(2,1)S(1)} %get-tuple-element.112), channel_id=1, source_target_pairs={{0,4},{4,0},{8,12},{12,8},{1,5},{5,1},{9,13},{13,9},{2,6},{6,2},{1... | collective-permute-start | bytes 786440 | tf_op jit(solution)/shard_map/ppermute | solution.py:428
  47.3 3.3 %collective-permute-done.12 = bf16[128,1024]{1,0:T(8,128)(2,1)S(1)} collective-permute-done((bf16[128,1024]{1,0:T(8,128)(2,1)S(1)}, bf16[128,1024]{1,0:T(8,128)(2,1)S(1)}, u32[]{:S(2)}, u32[]{:S(2)}) %collective-permute-start.12) | collective-permute-done | bytes 262176 | tf_op jit(solution)/shard_map/ppermute | solution.py:428
  50.7 2.0 %collective-permute-start.16 = (bf16[128,1024]{1,0:T(8,128)(2,1)S(1)}, bf16[128,1024]{1,0:T(8,128)(2,1)S(1)}, u32[]{:S(2)}, u32[]{:S(2)}) collective-permute-start(bf16[128,1024]{1,0:T(8,128)(2,1)S(1)} %fusion), channel_id=1, source_target_pairs={{0,4},{4,0},{8,12},{12,8},{1,5},{5,1},{9,13},{13,9},{2,6},{6,2},{1... | collective-permute-start | bytes 786440 | tf_op jit(solution)/shard_map/ppermute | solution.py:428
  53.4 1.9 %shard_map.110 = (bf16[128,2048]{1,0:T(8,128)(2,1)}, f32[272,128]{1,0:T(8,128)S(1)}) custom-call(bf16[3,128,1024]{2,1,0:T(8,128)(2,1)S(1)} %bitcast_dynamic-update-slice_fusion.refs_0_, bf16[128,2048]{1,0:T(8,128)(2,1)S(1)} %bitcast.45, bf16[128,2048]{1,0:T(8,128)(2,1)S(1)} %bitcast.52, f32[256,128]{1,0:T(8,128)S(1)} %get-tuple-element.88.bc_ref.refs_3_, ...), custom_call_target="tpu_custom_call" | custom-call | flops 3104999936 | bytes 2719872 | tf_op jit(solution)/shard_map/pallas_call | solution.py:54
  57.2 4.0 %collective-permute-start.20 = (bf16[128,1024]{1,0:T(8,128)(2,1)S(1)}, bf16[128,1024]{1,0:T(8,128)(2,1)S(1)}, u32[]{:S(2)}, u32[]{:S(2)}) collective-permute-start(bf16[128,1024]{1,0:T(8,128)(2,1)S(1)} %collective-permute-done.17.refs_10_), channel_id=1, source_target_pairs={{0,4},{4,0},{8,12},{12,8},{1,5},{5,1},{9,13},{13,9},{2,6},{6,2},{1... | collective-permute-start | bytes 786440 | tf_op jit(solution)/shard_map/ppermute | solution.py:401
  61.2 1.7 %shard_map.111 = (bf16[128,2048]{1,0:T(8,128)(2,1)}, f32[160,128]{1,0:T(8,128)S(1)}, f32[128,128]{1,0:T(8,128)S(1)}) custom-call(bf16[3,128,1024]{2,1,0:T(8,128)(2,1)S(1)} %bitcast_dynamic-update-slice_fusion.3.refs_0_, bf16[128,2048]{1,0:T(8,128)(2,1)S(1)} %bitcast.47, bf16[128,2048]{1,0:T(8,128)(2,1)S(1)} %bitcast.54, ...), custom_call_target="tpu_custom_call", output_to_operand_aliasing={{0}: (12, {})} | custom-call | flops 3104999936 | bytes 3383424 | tf_op jit(solution)/shard_map/pallas_call | solution.py:54
  63.0 3.7 %collective-permute-done.20.refs_11_ = bf16[128,1024]{1,0:T(8,128)(2,1)S(1)} collective-permute-done((bf16[128,1024]{1,0:T(8,128)(2,1)S(1)}, bf16[128,1024]{1,0:T(8,128)(2,1)S(1)}, u32[]{:S(2)}, u32[]{:S(2)}) %collective-permute-start.20) | collective-permute-done | bytes 262176 | tf_op jit(solution)/shard_map/ppermute | solution.py:401
  66.7 2.8 %collective-permute-done.19.refs_5_ = bf16[128,1024]{1,0:T(8,128)(2,1)S(1)} collective-permute-done((bf16[128,1024]{1,0:T(8,128)(2,1)S(1)}, bf16[128,1024]{1,0:T(8,128)(2,1)S(1)}, u32[]{:S(2)}, u32[]{:S(2)}) %collective-permute-start.19) | collective-permute-done | bytes 262176 | tf_op jit(solution)/shard_map/ppermute | solution.py:401
  70.6 3.4 %all-to-all-start = ((bf16[8,160,128]{2,1,0:T(8,128)(2,1)}), bf16[8,160,128]{2,1,0:T(8,128)(2,1)S(1)}, u32[]{:S(2)}, u32[]{:S(2)}) async-start(bf16[8,160,128]{2,1,0:T(8,128)(2,1)} %shard_map.113), calls=%async_computation | async-start | bytes 655360 | tf_op jit(solution)/shard_map/all_to_all | solution.py:590
  77.8 1.5 %shard_map.114 = bf16[128,2048]{1,0:T(8,128)(2,1)} custom-call(bf16[160,128]{1,0:T(8,128)(2,1)S(1)} %slice_bitcast_fusion.mine_ref, bf16[160,128]{1,0:T(8,128)(2,1)S(1)} %collective-permute-done.21.other_ref, bf16[1024,256]{1,0:T(8,128)(2,1)S(1)} %copy-done.8, bf16[64,1024]{1,0:T(8,128)(2,1)S(1)} %bitcast.67, bf16[1024,256]{1,0:T(8,128)(2,1)S(1)} %copy-done.10, ...), custom_call_target="tpu_custom_call" | custom-call | flops 3335000064 | bytes 1392640 | tf_op jit(solution)/shard_map/pallas_call | solution.py:54
  79.4 3.3 %all-to-all-done.source_ref = bf16[8,160,128]{2,1,0:T(8,128)(2,1)S(1)} async-done(((bf16[8,160,128]{2,1,0:T(8,128)(2,1)}), bf16[8,160,128]{2,1,0:T(8,128)(2,1)S(1)}, u32[]{:S(2)}, u32[]{:S(2)}) %all-to-all-start) | async-done | bytes 327712 | tf_op jit(solution)/shard_map/all_to_all | solution.py:590
  84.2 1.7 %shard_map.116 = (f32[1024,256]{1,0:T(8,128)}, f32[64,1024]{1,0:T(8,128)}) custom-call(bf16[2,512,1024]{2,1,0:T(8,128)(2,1)S(1)} %shard_map.112.tok_ref, bf16[8,160,128]{2,1,0:T(8,128)(2,1)S(1)} %collective-permute-done.22.source_ref, f32[1024,128]{1,0:T(8,128)S(1)} %get-tuple-element.108.refs_0_, f32[32,1024]{1,0:T(8,128)S(1)} %get-tuple-element.109.refs_1_), custom_call_target="tpu_custom_call" | custom-call | flops 2300000000 | bytes 3080192 | tf_op jit(solution)/shard_map/pallas_call | solution.py:54
  (82 shorter events, 19.9 us)
Async XLA Ops:
  1.7 9.3 %collective-permute-start = (bf16[128,1024]{1,0:T(8,128)(2,1)S(1)}, bf16[128,1024]{1,0:T(8,128)(2,1)S(1)}, u32[]{:S(2)}, u32[]{:S(2)}) collective-permute-start(bf16[128,1024]{1,0:T(8,128)(2,1)S(1)} %get-tuple-element.59), channel_id=1, source_target_pairs={{0,2},{2,0},{1,3},{3,1},{4,6},{6,4},{5,7},{7,5},{8,10},{10,8},{9,1... | collective-permute-start | bytes 786440 | tf_op jit(solution)/shard_map/ppermute | solution.py:21
  4.7 10.7 %collective-permute-start.2 = (bf16[128,1024]{1,0:T(8,128)(2,1)S(1)}, bf16[128,1024]{1,0:T(8,128)(2,1)S(1)}, u32[]{:S(2)}, u32[]{:S(2)}) collective-permute-start(bf16[128,1024]{1,0:T(8,128)(2,1)S(1)} %get-tuple-element.58.a_ref.refs_0_), channel_id=1, source_target_pairs={{0,4},{4,0},{8,12},{12,8},{1,5},{5,1},{9,13},{13,9},{2,6},{6,2},{1... | collective-permute-start | bytes 786440 | tf_op jit(solution)/shard_map/ppermute | solution.py:401
  6.3 9.2 %collective-permute-start.3 = (bf16[128,1024]{1,0:T(8,128)(2,1)S(1)}, bf16[128,1024]{1,0:T(8,128)(2,1)S(1)}, u32[]{:S(2)}, u32[]{:S(2)}) collective-permute-start(bf16[128,1024]{1,0:T(8,128)(2,1)S(1)} %get-tuple-element.58.a_ref.refs_0_), channel_id=1, source_target_pairs={{0,0},{4,8},{8,4},{12,12},{1,1},{5,9},{9,5},{13,13},{2,2},{6,10},{... | collective-permute-start | bytes 786440 | tf_op jit(solution)/shard_map/ppermute | solution.py:401
  11.3 5.5 %collective-permute-start.1 = (f32[320,128]{1,0:T(8,128)S(1)}, f32[320,128]{1,0:T(8,128)S(1)}, u32[]{:S(2)}, u32[]{:S(2)}) collective-permute-start(f32[320,128]{1,0:T(8,128)S(1)} %shard_map.104), channel_id=1, source_target_pairs={{0,2},{2,0},{1,3},{3,1},{4,6},{6,4},{5,7},{7,5},{8,10},{10,8},{9,1... | collective-permute-start | bytes 491528 | tf_op jit(solution)/shard_map/ppermute | solution.py:21
  13.1 7.2 %collective-permute-start.6 = (bf16[128,1024]{1,0:T(8,128)(2,1)S(1)}, bf16[128,1024]{1,0:T(8,128)(2,1)S(1)}, u32[]{:S(2)}, u32[]{:S(2)}) collective-permute-start(bf16[128,1024]{1,0:T(8,128)(2,1)S(1)} %collective-permute-done.a_ref.refs_6_), channel_id=1, source_target_pairs={{0,4},{4,0},{8,12},{12,8},{1,5},{5,1},{9,13},{13,9},{2,6},{6,2},{1... | collective-permute-start | bytes 786440 | tf_op jit(solution)/shard_map/ppermute | solution.py:401
  14.7 9.0 %collective-permute-start.8 = (bf16[128,1024]{1,0:T(8,128)(2,1)S(1)}, bf16[128,1024]{1,0:T(8,128)(2,1)S(1)}, u32[]{:S(2)}, u32[]{:S(2)}) collective-permute-start(bf16[128,1024]{1,0:T(8,128)(2,1)S(1)} %collective-permute-done.a_ref.refs_6_), channel_id=1, source_target_pairs={{0,0},{4,8},{8,4},{12,12},{1,1},{5,9},{9,5},{13,13},{2,2},{6,10},{... | collective-permute-start | bytes 786440 | tf_op jit(solution)/shard_map/ppermute | solution.py:401
  15.4 1.5 %collective-permute-start.4 = (f32[320,128]{1,0:T(8,128)S(1)}, f32[320,128]{1,0:T(8,128)S(1)}, u32[]{:S(2)}, u32[]{:S(2)}) collective-permute-start(f32[320,128]{1,0:T(8,128)S(1)} %shard_map.103.refs_0_), channel_id=1, source_target_pairs={{0,1},{1,0},{2,3},{3,2},{4,5},{5,4},{6,7},{7,6},{8,9},{9,8},{10,11... | collective-permute-start | bytes 491528 | tf_op jit(solution)/shard_map/ppermute | solution.py:21
  16.8 1.4 %collective-permute-start.5 = (f32[320,128]{1,0:T(8,128)S(1)}, f32[320,128]{1,0:T(8,128)S(1)}, u32[]{:S(2)}, u32[]{:S(2)}) collective-permute-start(f32[320,128]{1,0:T(8,128)S(1)} %collective-permute-done.1.refs_1_), channel_id=1, source_target_pairs={{0,1},{1,0},{2,3},{3,2},{4,5},{5,4},{6,7},{7,6},{8,9},{9,8},{10,11... | collective-permute-start | bytes 491528 | tf_op jit(solution)/shard_map/ppermute | solution.py:21
  20.4 10.1 %collective-permute-start.7 = (bf16[128,1024]{1,0:T(8,128)(2,1)S(1)}, bf16[128,1024]{1,0:T(8,128)(2,1)S(1)}, u32[]{:S(2)}, u32[]{:S(2)}) collective-permute-start(bf16[128,1024]{1,0:T(8,128)(2,1)S(1)} %get-tuple-element.64), channel_id=1, source_target_pairs={{0,4},{4,0},{8,12},{12,8},{1,5},{5,1},{9,13},{13,9},{2,6},{6,2},{1... | collective-permute-start | bytes 786440 | tf_op jit(solution)/shard_map/ppermute | solution.py:428
  23.8 23.5 %collective-permute-start.15 = (bf16[128,1024]{1,0:T(8,128)(2,1)S(1)}, bf16[128,1024]{1,0:T(8,128)(2,1)S(1)}, u32[]{:S(2)}, u32[]{:S(2)}) collective-permute-start(bf16[128,1024]{1,0:T(8,128)(2,1)S(1)} %collective-permute-done.2.refs_1_), channel_id=1, source_target_pairs={{0,0},{4,8},{8,4},{12,12},{1,1},{5,9},{9,5},{13,13},{2,2},{6,10},{... | collective-permute-start | bytes 786440 | tf_op jit(solution)/shard_map/ppermute | solution.py:401
  24.4 22.8 %collective-permute-start.14 = (bf16[64,1024]{1,0:T(8,128)(2,1)S(1)}, bf16[64,1024]{1,0:T(8,128)(2,1)S(1)}, u32[]{:S(2)}, u32[]{:S(2)}) collective-permute-start(bf16[64,1024]{1,0:T(8,128)(2,1)S(1)} %bitcast.66), channel_id=1, source_target_pairs={{0,2},{2,0},{1,3},{3,1},{4,6},{6,4},{5,7},{7,5},{8,10},{10,8},{9,1... | collective-permute-start | bytes 393224 | tf_op jit(solution)/shard_map/ppermute | solution.py:21
  25.0 22.2 %collective-permute-start.13 = (bf16[1024,256]{1,0:T(8,128)(2,1)}, bf16[1024,256]{1,0:T(8,128)(2,1)S(1)}, u32[]{:S(2)}, u32[]{:S(2)}) collective-permute-start(bf16[1024,256]{1,0:T(8,128)(2,1)} %refs_0_.1), channel_id=1, source_target_pairs={{0,2},{2,0},{1,3},{3,1},{4,6},{6,4},{5,7},{7,5},{8,10},{10,8},{9,1... | collective-permute-start | bytes 1572872 | tf_op jit(solution)/shard_map/ppermute | solution.py:21
  30.6 4.8 %collective-permute-start.10 = (bf16[128,1024]{1,0:T(8,128)(2,1)S(1)}, bf16[128,1024]{1,0:T(8,128)(2,1)S(1)}, u32[]{:S(2)}, u32[]{:S(2)}) collective-permute-start(bf16[128,1024]{1,0:T(8,128)(2,1)S(1)} %fusion.3), channel_id=1, source_target_pairs={{0,0},{4,8},{8,4},{12,12},{1,1},{5,9},{9,5},{13,13},{2,2},{6,10},{... | collective-permute-start | bytes 786440 | tf_op jit(solution)/shard_map/ppermute | solution.py:428
  31.4 9.0 %collective-permute-start.9 = (bf16[128,1024]{1,0:T(8,128)(2,1)S(1)}, bf16[128,1024]{1,0:T(8,128)(2,1)S(1)}, u32[]{:S(2)}, u32[]{:S(2)}) collective-permute-start(bf16[128,1024]{1,0:T(8,128)(2,1)S(1)} %broadcast_select_fusion), channel_id=1, source_target_pairs={{0,4},{4,0},{8,12},{12,8},{1,5},{5,1},{9,13},{13,9},{2,6},{6,2},{1... | collective-permute-start | bytes 786440 | tf_op jit(solution)/shard_map/ppermute | solution.py:428
  40.7 6.6 %collective-permute-start.11 = (bf16[128,1024]{1,0:T(8,128)(2,1)S(1)}, bf16[128,1024]{1,0:T(8,128)(2,1)S(1)}, u32[]{:S(2)}, u32[]{:S(2)}) collective-permute-start(bf16[128,1024]{1,0:T(8,128)(2,1)S(1)} %get-tuple-element.113), channel_id=1, source_target_pairs={{0,0},{4,8},{8,4},{12,12},{1,1},{5,9},{9,5},{13,13},{2,2},{6,10},{... | collective-permute-start | bytes 786440 | tf_op jit(solution)/shard_map/ppermute | solution.py:428
  41.4 9.2 %collective-permute-start.12 = (bf16[128,1024]{1,0:T(8,128)(2,1)S(1)}, bf16[128,1024]{1,0:T(8,128)(2,1)S(1)}, u32[]{:S(2)}, u32[]{:S(2)}) collective-permute-start(bf16[128,1024]{1,0:T(8,128)(2,1)S(1)} %get-tuple-element.112), channel_id=1, source_target_pairs={{0,4},{4,0},{8,12},{12,8},{1,5},{5,1},{9,13},{13,9},{2,6},{6,2},{1... | collective-permute-start | bytes 786440 | tf_op jit(solution)/shard_map/ppermute | solution.py:428
  50.7 6.4 %collective-permute-start.16 = (bf16[128,1024]{1,0:T(8,128)(2,1)S(1)}, bf16[128,1024]{1,0:T(8,128)(2,1)S(1)}, u32[]{:S(2)}, u32[]{:S(2)}) collective-permute-start(bf16[128,1024]{1,0:T(8,128)(2,1)S(1)} %fusion), channel_id=1, source_target_pairs={{0,4},{4,0},{8,12},{12,8},{1,5},{5,1},{9,13},{13,9},{2,6},{6,2},{1... | collective-permute-start | bytes 786440 | tf_op jit(solution)/shard_map/ppermute | solution.py:428
  52.7 3.6 %collective-permute-start.17 = (bf16[128,1024]{1,0:T(8,128)(2,1)S(1)}, bf16[128,1024]{1,0:T(8,128)(2,1)S(1)}, u32[]{:S(2)}, u32[]{:S(2)}) collective-permute-start(bf16[128,1024]{1,0:T(8,128)(2,1)S(1)} %collective-permute-done.6.refs_7_), channel_id=1, source_target_pairs={{0,0},{4,8},{8,4},{12,12},{1,1},{5,9},{9,5},{13,13},{2,2},{6,10},{... | collective-permute-start | bytes 786440 | tf_op jit(solution)/shard_map/ppermute | solution.py:401
  57.2 9.5 %collective-permute-start.20 = (bf16[128,1024]{1,0:T(8,128)(2,1)S(1)}, bf16[128,1024]{1,0:T(8,128)(2,1)S(1)}, u32[]{:S(2)}, u32[]{:S(2)}) collective-permute-start(bf16[128,1024]{1,0:T(8,128)(2,1)S(1)} %collective-permute-done.17.refs_10_), channel_id=1, source_target_pairs={{0,4},{4,0},{8,12},{12,8},{1,5},{5,1},{9,13},{13,9},{2,6},{6,2},{1... | collective-permute-start | bytes 786440 | tf_op jit(solution)/shard_map/ppermute | solution.py:401
  61.2 8.3 %collective-permute-start.19 = (bf16[128,1024]{1,0:T(8,128)(2,1)S(1)}, bf16[128,1024]{1,0:T(8,128)(2,1)S(1)}, u32[]{:S(2)}, u32[]{:S(2)}) collective-permute-start(bf16[128,1024]{1,0:T(8,128)(2,1)S(1)} %collective-permute-done.15.refs_4_), channel_id=1, source_target_pairs={{0,4},{4,0},{8,12},{12,8},{1,5},{5,1},{9,13},{13,9},{2,6},{6,2},{1... | collective-permute-start | bytes 786440 | tf_op jit(solution)/shard_map/ppermute | solution.py:401
  63.0 6.8 %collective-permute-start.18 = (f32[128,128]{1,0:T(8,128)S(1)}, f32[128,128]{1,0:T(8,128)S(1)}, u32[]{:S(2)}, u32[]{:S(2)}) collective-permute-start(f32[128,128]{1,0:T(8,128)S(1)} %get-tuple-element.103), channel_id=1, source_target_pairs={{0,1},{1,0},{2,3},{3,2},{4,5},{5,4},{6,7},{7,6},{8,9},{9,8},{10,11... | collective-permute-start | bytes 196616 | tf_op jit(solution)/shard_map/ppermute | solution.py:21
  70.6 12.0 %all-to-all-start = ((bf16[8,160,128]{2,1,0:T(8,128)(2,1)}), bf16[8,160,128]{2,1,0:T(8,128)(2,1)S(1)}, u32[]{:S(2)}, u32[]{:S(2)}) async-start(bf16[8,160,128]{2,1,0:T(8,128)(2,1)} %shard_map.113), calls=%async_computation | async-start | bytes 655360 | tf_op jit(solution)/shard_map/all_to_all | solution.py:590
  74.8 1.2 %collective-permute-start.21 = (bf16[160,128]{1,0:T(8,128)(2,1)S(1)}, bf16[160,128]{1,0:T(8,128)(2,1)S(1)}, u32[]{:S(2)}, u32[]{:S(2)}) collective-permute-start(bf16[160,128]{1,0:T(8,128)(2,1)S(1)} %slice_bitcast_fusion.mine_ref), channel_id=1, source_target_pairs={{0,1},{1,0},{2,3},{3,2},{4,5},{5,4},{6,7},{7,6},{8,9},{9,8},{10,11... | collective-permute-start | bytes 122888 | tf_op jit(solution)/shard_map/ppermute | solution.py:21
  82.6 1.6 %collective-permute-start.22 = (bf16[8,160,128]{2,1,0:T(8,128)(2,1)S(1)}, bf16[8,160,128]{2,1,0:T(8,128)(2,1)S(1)}, u32[]{:S(2)}, u32[]{:S(2)}) collective-permute-start(bf16[8,160,128]{2,1,0:T(8,128)(2,1)S(1)} %all-to-all-done.source_ref), channel_id=1, source_target_pairs={{0,1},{1,0},{2,3},{3,2},{4,5},{5,4},{6,7},{7,6},{8,9},{9,8},{10,11... | collective-permute-start | bytes 983048 | tf_op jit(solution)/shard_map/ppermute | solution.py:21
  (15 other events, 126.3 us)

commit v22 on v20

--- a/solution.py
+++ b/solution.py
@@ -466,7 +466,7 @@
     w_dt = w_dt.T
     rate, bias = decay_rate[None], dt_bias[None]
 
-    pieces = call(split_kernel, [struct((rows, part), BF)] * n_dp, 1.9, feats)
+    pieces = call(split_kernel, [struct((rows, part), BF)] * n_dp, 1.9, feats, limit=48 * 1024 * 1024)
     items = [pieces[0]] + [cyclic(pieces[r], "dp", r) for r in range(1, n_dp)]
     groups = items[:1]
     if n_dp > 1:

time: 86.1 us -> 86.1 us (level)
  no operation moved by 1% of the time
where the time goes in v22:
time: 86.1 us; the launch traced here: 85.6 us
  starting transfers between devices  36.3 us (42%)
  waiting for transfers between devices  28.5 us (33%)
  Pallas kernels  15.2 us (18%)
  local copies, waits for them, and re-layouts  4.02 us (5%)
  between operations  1 us (1%)
    ppermute x6, starting transfers between devices, chains(): got[k] = lax.ppermute(value, 'seq', sorted(to.items()))  16.2 us
    pallas_call x15, Pallas kernels, call(): pl.pallas_call(kernel, out_shape=out_shape, grid=(1,), in_specs=specs or...  15.2 us
    ppermute x6, waiting for transfers between devices, chains(): got[k] = lax.ppermute(value, 'seq', sorted(to.items()))  11.3 us
    ppermute x8, starting transfers between devices, relay(): found[kind, hop] = lax.ppermute(source, 'seq', pairs[kind])  8.9 us
    ppermute x9, waiting for transfers between devices, cyclic(): return lax.ppermute(a, axis, [(i, (i + by) % count) for i in range(count)])  8.46 us
    ppermute x9, starting transfers between devices, cyclic(): return lax.ppermute(a, axis, [(i, (i + by) % count) for i in range(count)])  6.98 us
    ppermute x8, waiting for transfers between devices, relay(): found[kind, hop] = lax.ppermute(source, 'seq', pairs[kind])  5.4 us
    all_to_all x1, starting transfers between devices, body(): lows = lax.all_to_all(copies, ('seq', 'dp'), 0, 0, tiled=True)  4.17 us
  transfers between devices with their start and end apart: 24, of which 13 were waited for; matrix products, arithmetic and copies ran while one was open for 2% of the time, Pallas kernels for 15%

profile of v22, /device:TPU:0, one launch (start us, length us, event | category | flops | bytes accessed | tf_op | source)
XLA Modules:
  0.0 85.6 jit_solution(11908883254821471875)
XLA Ops:
  1.7 3.0 %collective-permute-start = (bf16[128,1024]{1,0:T(8,128)(2,1)S(1)}, bf16[128,1024]{1,0:T(8,128)(2,1)S(1)}, u32[]{:S(2)}, u32[]{:S(2)}) collective-permute-start(bf16[128,1024]{1,0:T(8,128)(2,1)S(1)} %get-tuple-element.59), channel_id=1, source_target_pairs={{0,2},{2,0},{1,3},{3,1},{4,6},{6,4},{5,7},{7,5},{8,10},{10,8},{9,1... | collective-permute-start | bytes 786440 | tf_op jit(solution)/shard_map/ppermute | solution.py:21
  4.7 1.6 %collective-permute-start.2 = (bf16[128,1024]{1,0:T(8,128)(2,1)S(1)}, bf16[128,1024]{1,0:T(8,128)(2,1)S(1)}, u32[]{:S(2)}, u32[]{:S(2)}) collective-permute-start(bf16[128,1024]{1,0:T(8,128)(2,1)S(1)} %get-tuple-element.58.a_ref.refs_0_), channel_id=1, source_target_pairs={{0,4},{4,0},{8,12},{12,8},{1,5},{5,1},{9,13},{13,9},{2,6},{6,2},{1... | collective-permute-start | bytes 786440 | tf_op jit(solution)/shard_map/ppermute | solution.py:401
  7.3 3.7 %collective-permute-done.a_ref.refs_6_ = bf16[128,1024]{1,0:T(8,128)(2,1)S(1)} collective-permute-done((bf16[128,1024]{1,0:T(8,128)(2,1)S(1)}, bf16[128,1024]{1,0:T(8,128)(2,1)S(1)}, u32[]{:S(2)}, u32[]{:S(2)}) %collective-permute-start) | collective-permute-done | bytes 262176 | tf_op jit(solution)/shard_map/ppermute | solution.py:21
  11.3 1.8 %collective-permute-start.1 = (f32[320,128]{1,0:T(8,128)S(1)}, f32[320,128]{1,0:T(8,128)S(1)}, u32[]{:S(2)}, u32[]{:S(2)}) collective-permute-start(f32[320,128]{1,0:T(8,128)S(1)} %shard_map.104), channel_id=1, source_target_pairs={{0,2},{2,0},{1,3},{3,1},{4,6},{6,4},{5,7},{7,5},{8,10},{10,8},{9,1... | collective-permute-start | bytes 491528 | tf_op jit(solution)/shard_map/ppermute | solution.py:21
  13.1 1.6 %collective-permute-start.6 = (bf16[128,1024]{1,0:T(8,128)(2,1)S(1)}, bf16[128,1024]{1,0:T(8,128)(2,1)S(1)}, u32[]{:S(2)}, u32[]{:S(2)}) collective-permute-start(bf16[128,1024]{1,0:T(8,128)(2,1)S(1)} %collective-permute-done.a_ref.refs_6_), channel_id=1, source_target_pairs={{0,4},{4,0},{8,12},{12,8},{1,5},{5,1},{9,13},{13,9},{2,6},{6,2},{1... | collective-permute-start | bytes 786440 | tf_op jit(solution)/shard_map/ppermute | solution.py:401
  18.2 2.1 %shard_map.105 = (f32[2,2,128,1024]{3,2,1,0:T(8,128)S(1)}, f32[256,128]{1,0:T(8,128)S(1)}, f32[160,128]{1,0:T(8,128)S(1)}, bf16[128,1024]{1,0:T(8,128)(2,1)S(1)}...) custom-call(f32[320,128]{1,0:T(8,128)S(1)} %shard_map.103.refs_0_, ...), custom_call_target="tpu_custom_call" | custom-call | flops 115000000 | bytes 1966336 | tf_op jit(solution)/shard_map/pallas_call | solution.py:54
  20.4 4.2 %collective-permute-start.8 = (bf16[128,1024]{1,0:T(8,128)(2,1)S(1)}, bf16[128,1024]{1,0:T(8,128)(2,1)S(1)}, u32[]{:S(2)}, u32[]{:S(2)}) collective-permute-start(bf16[128,1024]{1,0:T(8,128)(2,1)S(1)} %get-tuple-element.64), channel_id=1, source_target_pairs={{0,4},{4,0},{8,12},{12,8},{1,5},{5,1},{9,13},{13,9},{2,6},{6,2},{1... | collective-permute-start | bytes 786440 | tf_op jit(solution)/shard_map/ppermute | solution.py:428
  25.9 1.5 %collective-permute-start.13 = (bf16[1024,256]{1,0:T(8,128)(2,1)}, bf16[1024,256]{1,0:T(8,128)(2,1)S(1)}, u32[]{:S(2)}, u32[]{:S(2)}) collective-permute-start(bf16[1024,256]{1,0:T(8,128)(2,1)} %refs_0_.1), channel_id=1, source_target_pairs={{0,2},{2,0},{1,3},{3,1},{4,6},{6,4},{5,7},{7,5},{8,10},{10,8},{9,1... | collective-permute-start | bytes 1572872 | tf_op jit(solution)/shard_map/ppermute | solution.py:21
  28.4 2.1 %collective-permute-done.8.refs_3_ = bf16[128,1024]{1,0:T(8,128)(2,1)S(1)} collective-permute-done((bf16[128,1024]{1,0:T(8,128)(2,1)S(1)}, bf16[128,1024]{1,0:T(8,128)(2,1)S(1)}, u32[]{:S(2)}, u32[]{:S(2)}) %collective-permute-start.8) | collective-permute-done | bytes 262176 | tf_op jit(solution)/shard_map/ppermute | solution.py:428
  31.4 3.5 %collective-permute-start.9 = (bf16[128,1024]{1,0:T(8,128)(2,1)S(1)}, bf16[128,1024]{1,0:T(8,128)(2,1)S(1)}, u32[]{:S(2)}, u32[]{:S(2)}) collective-permute-start(bf16[128,1024]{1,0:T(8,128)(2,1)S(1)} %broadcast_select_fusion), channel_id=1, source_target_pairs={{0,4},{4,0},{8,12},{12,8},{1,5},{5,1},{9,13},{13,9},{2,6},{6,2},{1... | collective-permute-start | bytes 786440 | tf_op jit(solution)/shard_map/ppermute | solution.py:428
  35.9 3.5 %collective-permute-done.9.refs_9_ = bf16[128,1024]{1,0:T(8,128)(2,1)S(1)} collective-permute-done((bf16[128,1024]{1,0:T(8,128)(2,1)S(1)}, bf16[128,1024]{1,0:T(8,128)(2,1)S(1)}, u32[]{:S(2)}, u32[]{:S(2)}) %collective-permute-start.9) | collective-permute-done | bytes 262176 | tf_op jit(solution)/shard_map/ppermute | solution.py:428
  40.4 4.8 %collective-permute-start.12 = (bf16[128,1024]{1,0:T(8,128)(2,1)S(1)}, bf16[128,1024]{1,0:T(8,128)(2,1)S(1)}, u32[]{:S(2)}, u32[]{:S(2)}) collective-permute-start(bf16[128,1024]{1,0:T(8,128)(2,1)S(1)} %get-tuple-element.112), channel_id=1, source_target_pairs={{0,4},{4,0},{8,12},{12,8},{1,5},{5,1},{9,13},{13,9},{2,6},{6,2},{1... | collective-permute-start | bytes 786440 | tf_op jit(solution)/shard_map/ppermute | solution.py:428
  46.3 3.9 %collective-permute-done.12 = bf16[128,1024]{1,0:T(8,128)(2,1)S(1)} collective-permute-done((bf16[128,1024]{1,0:T(8,128)(2,1)S(1)}, bf16[128,1024]{1,0:T(8,128)(2,1)S(1)}, u32[]{:S(2)}, u32[]{:S(2)}) %collective-permute-start.12) | collective-permute-done | bytes 262176 | tf_op jit(solution)/shard_map/ppermute | solution.py:428
  50.3 2.4 %collective-permute-start.16 = (bf16[128,1024]{1,0:T(8,128)(2,1)S(1)}, bf16[128,1024]{1,0:T(8,128)(2,1)S(1)}, u32[]{:S(2)}, u32[]{:S(2)}) collective-permute-start(bf16[128,1024]{1,0:T(8,128)(2,1)S(1)} %fusion), channel_id=1, source_target_pairs={{0,4},{4,0},{8,12},{12,8},{1,5},{5,1},{9,13},{13,9},{2,6},{6,2},{1... | collective-permute-start | bytes 786440 | tf_op jit(solution)/shard_map/ppermute | solution.py:428
  53.4 1.9 %shard_map.110 = (bf16[128,2048]{1,0:T(8,128)(2,1)}, f32[272,128]{1,0:T(8,128)S(1)}) custom-call(bf16[3,128,1024]{2,1,0:T(8,128)(2,1)S(1)} %bitcast_dynamic-update-slice_fusion.refs_0_, bf16[128,2048]{1,0:T(8,128)(2,1)S(1)} %bitcast.45, bf16[128,2048]{1,0:T(8,128)(2,1)S(1)} %bitcast.52, f32[256,128]{1,0:T(8,128)S(1)} %get-tuple-element.88.bc_ref.refs_3_, ...), custom_call_target="tpu_custom_call" | custom-call | flops 3104999936 | bytes 2719872 | tf_op jit(solution)/shard_map/pallas_call | solution.py:54
  56.3 1.8 %collective-permute-done.16 = bf16[128,1024]{1,0:T(8,128)(2,1)S(1)} collective-permute-done((bf16[128,1024]{1,0:T(8,128)(2,1)S(1)}, bf16[128,1024]{1,0:T(8,128)(2,1)S(1)}, u32[]{:S(2)}, u32[]{:S(2)}) %collective-permute-start.16) | collective-permute-done | bytes 262176 | tf_op jit(solution)/shard_map/ppermute | solution.py:428
  58.1 3.0 %collective-permute-start.20 = (bf16[128,1024]{1,0:T(8,128)(2,1)S(1)}, bf16[128,1024]{1,0:T(8,128)(2,1)S(1)}, u32[]{:S(2)}, u32[]{:S(2)}) collective-permute-start(bf16[128,1024]{1,0:T(8,128)(2,1)S(1)} %collective-permute-done.17.refs_10_), channel_id=1, source_target_pairs={{0,4},{4,0},{8,12},{12,8},{1,5},{5,1},{9,13},{13,9},{2,6},{6,2},{1... | collective-permute-start | bytes 786440 | tf_op jit(solution)/shard_map/ppermute | solution.py:401
  61.2 1.7 %shard_map.111 = (bf16[128,2048]{1,0:T(8,128)(2,1)}, f32[160,128]{1,0:T(8,128)S(1)}, f32[128,128]{1,0:T(8,128)S(1)}) custom-call(bf16[3,128,1024]{2,1,0:T(8,128)(2,1)S(1)} %bitcast_dynamic-update-slice_fusion.3.refs_0_, bf16[128,2048]{1,0:T(8,128)(2,1)S(1)} %bitcast.47, bf16[128,2048]{1,0:T(8,128)(2,1)S(1)} %bitcast.54, ...), custom_call_target="tpu_custom_call", output_to_operand_aliasing={{0}: (12, {})} | custom-call | flops 3104999936 | bytes 3383424 | tf_op jit(solution)/shard_map/pallas_call | solution.py:54
  62.9 2.6 %collective-permute-done.20.refs_11_ = bf16[128,1024]{1,0:T(8,128)(2,1)S(1)} collective-permute-done((bf16[128,1024]{1,0:T(8,128)(2,1)S(1)}, bf16[128,1024]{1,0:T(8,128)(2,1)S(1)}, u32[]{:S(2)}, u32[]{:S(2)}) %collective-permute-start.20) | collective-permute-done | bytes 262176 | tf_op jit(solution)/shard_map/ppermute | solution.py:401
  65.5 2.8 %collective-permute-done.19.refs_5_ = bf16[128,1024]{1,0:T(8,128)(2,1)S(1)} collective-permute-done((bf16[128,1024]{1,0:T(8,128)(2,1)S(1)}, bf16[128,1024]{1,0:T(8,128)(2,1)S(1)}, u32[]{:S(2)}, u32[]{:S(2)}) %collective-permute-start.19) | collective-permute-done | bytes 262176 | tf_op jit(solution)/shard_map/ppermute | solution.py:401
  69.4 4.2 %all-to-all-start = ((bf16[8,160,128]{2,1,0:T(8,128)(2,1)}), bf16[8,160,128]{2,1,0:T(8,128)(2,1)S(1)}, u32[]{:S(2)}, u32[]{:S(2)}) async-start(bf16[8,160,128]{2,1,0:T(8,128)(2,1)} %shard_map.113), calls=%async_computation | async-start | bytes 655360 | tf_op jit(solution)/shard_map/all_to_all | solution.py:590
  77.4 1.5 %shard_map.114 = bf16[128,2048]{1,0:T(8,128)(2,1)} custom-call(bf16[160,128]{1,0:T(8,128)(2,1)S(1)} %slice_bitcast_fusion.mine_ref, bf16[160,128]{1,0:T(8,128)(2,1)S(1)} %collective-permute-done.21.other_ref, bf16[1024,256]{1,0:T(8,128)(2,1)S(1)} %copy-done.8, bf16[64,1024]{1,0:T(8,128)(2,1)S(1)} %bitcast.67, bf16[1024,256]{1,0:T(8,128)(2,1)S(1)} %copy-done.10, ...), custom_call_target="tpu_custom_call" | custom-call | flops 3335000064 | bytes 1392640 | tf_op jit(solution)/shard_map/pallas_call | solution.py:54
  78.9 3.3 %all-to-all-done.source_ref = bf16[8,160,128]{2,1,0:T(8,128)(2,1)S(1)} async-done(((bf16[8,160,128]{2,1,0:T(8,128)(2,1)}), bf16[8,160,128]{2,1,0:T(8,128)(2,1)S(1)}, u32[]{:S(2)}, u32[]{:S(2)}) %all-to-all-start) | async-done | bytes 327712 | tf_op jit(solution)/shard_map/all_to_all | solution.py:590
  83.9 1.7 %shard_map.116 = (f32[1024,256]{1,0:T(8,128)}, f32[64,1024]{1,0:T(8,128)}) custom-call(bf16[2,512,1024]{2,1,0:T(8,128)(2,1)S(1)} %shard_map.112.tok_ref, bf16[8,160,128]{2,1,0:T(8,128)(2,1)S(1)} %collective-permute-done.22.source_ref, f32[1024,128]{1,0:T(8,128)S(1)} %get-tuple-element.108.refs_0_, f32[32,1024]{1,0:T(8,128)S(1)} %get-tuple-element.109.refs_1_), custom_call_target="tpu_custom_call" | custom-call | flops 2300000000 | bytes 3080192 | tf_op jit(solution)/shard_map/pallas_call | solution.py:54
  (82 shorter events, 20.4 us)
Async XLA Ops:
  1.7 9.3 %collective-permute-start = (bf16[128,1024]{1,0:T(8,128)(2,1)S(1)}, bf16[128,1024]{1,0:T(8,128)(2,1)S(1)}, u32[]{:S(2)}, u32[]{:S(2)}) collective-permute-start(bf16[128,1024]{1,0:T(8,128)(2,1)S(1)} %get-tuple-element.59), channel_id=1, source_target_pairs={{0,2},{2,0},{1,3},{3,1},{4,6},{6,4},{5,7},{7,5},{8,10},{10,8},{9,1... | collective-permute-start | bytes 786440 | tf_op jit(solution)/shard_map/ppermute | solution.py:21
  4.7 10.7 %collective-permute-start.2 = (bf16[128,1024]{1,0:T(8,128)(2,1)S(1)}, bf16[128,1024]{1,0:T(8,128)(2,1)S(1)}, u32[]{:S(2)}, u32[]{:S(2)}) collective-permute-start(bf16[128,1024]{1,0:T(8,128)(2,1)S(1)} %get-tuple-element.58.a_ref.refs_0_), channel_id=1, source_target_pairs={{0,4},{4,0},{8,12},{12,8},{1,5},{5,1},{9,13},{13,9},{2,6},{6,2},{1... | collective-permute-start | bytes 786440 | tf_op jit(solution)/shard_map/ppermute | solution.py:401
  6.3 9.2 %collective-permute-start.3 = (bf16[128,1024]{1,0:T(8,128)(2,1)S(1)}, bf16[128,1024]{1,0:T(8,128)(2,1)S(1)}, u32[]{:S(2)}, u32[]{:S(2)}) collective-permute-start(bf16[128,1024]{1,0:T(8,128)(2,1)S(1)} %get-tuple-element.58.a_ref.refs_0_), channel_id=1, source_target_pairs={{0,0},{4,8},{8,4},{12,12},{1,1},{5,9},{9,5},{13,13},{2,2},{6,10},{... | collective-permute-start | bytes 786440 | tf_op jit(solution)/shard_map/ppermute | solution.py:401
  11.3 5.5 %collective-permute-start.1 = (f32[320,128]{1,0:T(8,128)S(1)}, f32[320,128]{1,0:T(8,128)S(1)}, u32[]{:S(2)}, u32[]{:S(2)}) collective-permute-start(f32[320,128]{1,0:T(8,128)S(1)} %shard_map.104), channel_id=1, source_target_pairs={{0,2},{2,0},{1,3},{3,1},{4,6},{6,4},{5,7},{7,5},{8,10},{10,8},{9,1... | collective-permute-start | bytes 491528 | tf_op jit(solution)/shard_map/ppermute | solution.py:21
  13.1 7.2 %collective-permute-start.6 = (bf16[128,1024]{1,0:T(8,128)(2,1)S(1)}, bf16[128,1024]{1,0:T(8,128)(2,1)S(1)}, u32[]{:S(2)}, u32[]{:S(2)}) collective-permute-start(bf16[128,1024]{1,0:T(8,128)(2,1)S(1)} %collective-permute-done.a_ref.refs_6_), channel_id=1, source_target_pairs={{0,4},{4,0},{8,12},{12,8},{1,5},{5,1},{9,13},{13,9},{2,6},{6,2},{1... | collective-permute-start | bytes 786440 | tf_op jit(solution)/shard_map/ppermute | solution.py:401
  14.7 5.7 %collective-permute-start.7 = (bf16[128,1024]{1,0:T(8,128)(2,1)S(1)}, bf16[128,1024]{1,0:T(8,128)(2,1)S(1)}, u32[]{:S(2)}, u32[]{:S(2)}) collective-permute-start(bf16[128,1024]{1,0:T(8,128)(2,1)S(1)} %collective-permute-done.a_ref.refs_6_), channel_id=1, source_target_pairs={{0,0},{4,8},{8,4},{12,12},{1,1},{5,9},{9,5},{13,13},{2,2},{6,10},{... | collective-permute-start | bytes 786440 | tf_op jit(solution)/shard_map/ppermute | solution.py:401
  15.4 1.5 %collective-permute-start.4 = (f32[320,128]{1,0:T(8,128)S(1)}, f32[320,128]{1,0:T(8,128)S(1)}, u32[]{:S(2)}, u32[]{:S(2)}) collective-permute-start(f32[320,128]{1,0:T(8,128)S(1)} %shard_map.103.refs_0_), channel_id=1, source_target_pairs={{0,1},{1,0},{2,3},{3,2},{4,5},{5,4},{6,7},{7,6},{8,9},{9,8},{10,11... | collective-permute-start | bytes 491528 | tf_op jit(solution)/shard_map/ppermute | solution.py:21
  16.8 1.4 %collective-permute-start.5 = (f32[320,128]{1,0:T(8,128)S(1)}, f32[320,128]{1,0:T(8,128)S(1)}, u32[]{:S(2)}, u32[]{:S(2)}) collective-permute-start(f32[320,128]{1,0:T(8,128)S(1)} %collective-permute-done.1.refs_1_), channel_id=1, source_target_pairs={{0,1},{1,0},{2,3},{3,2},{4,5},{5,4},{6,7},{7,6},{8,9},{9,8},{10,11... | collective-permute-start | bytes 491528 | tf_op jit(solution)/shard_map/ppermute | solution.py:21
  20.4 10.1 %collective-permute-start.8 = (bf16[128,1024]{1,0:T(8,128)(2,1)S(1)}, bf16[128,1024]{1,0:T(8,128)(2,1)S(1)}, u32[]{:S(2)}, u32[]{:S(2)}) collective-permute-start(bf16[128,1024]{1,0:T(8,128)(2,1)S(1)} %get-tuple-element.64), channel_id=1, source_target_pairs={{0,4},{4,0},{8,12},{12,8},{1,5},{5,1},{9,13},{13,9},{2,6},{6,2},{1... | collective-permute-start | bytes 786440 | tf_op jit(solution)/shard_map/ppermute | solution.py:428
  24.6 21.6 %collective-permute-start.15 = (bf16[128,1024]{1,0:T(8,128)(2,1)S(1)}, bf16[128,1024]{1,0:T(8,128)(2,1)S(1)}, u32[]{:S(2)}, u32[]{:S(2)}) collective-permute-start(bf16[128,1024]{1,0:T(8,128)(2,1)S(1)} %collective-permute-done.2.refs_1_), channel_id=1, source_target_pairs={{0,0},{4,8},{8,4},{12,12},{1,1},{5,9},{9,5},{13,13},{2,2},{6,10},{... | collective-permute-start | bytes 786440 | tf_op jit(solution)/shard_map/ppermute | solution.py:401
  25.3 20.9 %collective-permute-start.14 = (bf16[64,1024]{1,0:T(8,128)(2,1)S(1)}, bf16[64,1024]{1,0:T(8,128)(2,1)S(1)}, u32[]{:S(2)}, u32[]{:S(2)}) collective-permute-start(bf16[64,1024]{1,0:T(8,128)(2,1)S(1)} %bitcast.66), channel_id=1, source_target_pairs={{0,2},{2,0},{1,3},{3,1},{4,6},{6,4},{5,7},{7,5},{8,10},{10,8},{9,1... | collective-permute-start | bytes 393224 | tf_op jit(solution)/shard_map/ppermute | solution.py:21
  25.9 20.4 %collective-permute-start.13 = (bf16[1024,256]{1,0:T(8,128)(2,1)}, bf16[1024,256]{1,0:T(8,128)(2,1)S(1)}, u32[]{:S(2)}, u32[]{:S(2)}) collective-permute-start(bf16[1024,256]{1,0:T(8,128)(2,1)} %refs_0_.1), channel_id=1, source_target_pairs={{0,2},{2,0},{1,3},{3,1},{4,6},{6,4},{5,7},{7,5},{8,10},{10,8},{9,1... | collective-permute-start | bytes 1572872 | tf_op jit(solution)/shard_map/ppermute | solution.py:21
  30.6 5.3 %collective-permute-start.10 = (bf16[128,1024]{1,0:T(8,128)(2,1)S(1)}, bf16[128,1024]{1,0:T(8,128)(2,1)S(1)}, u32[]{:S(2)}, u32[]{:S(2)}) collective-permute-start(bf16[128,1024]{1,0:T(8,128)(2,1)S(1)} %fusion.3), channel_id=1, source_target_pairs={{0,0},{4,8},{8,4},{12,12},{1,1},{5,9},{9,5},{13,13},{2,2},{6,10},{... | collective-permute-start | bytes 786440 | tf_op jit(solution)/shard_map/ppermute | solution.py:428
  31.4 8.0 %collective-permute-start.9 = (bf16[128,1024]{1,0:T(8,128)(2,1)S(1)}, bf16[128,1024]{1,0:T(8,128)(2,1)S(1)}, u32[]{:S(2)}, u32[]{:S(2)}) collective-permute-start(bf16[128,1024]{1,0:T(8,128)(2,1)S(1)} %broadcast_select_fusion), channel_id=1, source_target_pairs={{0,4},{4,0},{8,12},{12,8},{1,5},{5,1},{9,13},{13,9},{2,6},{6,2},{1... | collective-permute-start | bytes 786440 | tf_op jit(solution)/shard_map/ppermute | solution.py:428
  39.7 6.6 %collective-permute-start.11 = (bf16[128,1024]{1,0:T(8,128)(2,1)S(1)}, bf16[128,1024]{1,0:T(8,128)(2,1)S(1)}, u32[]{:S(2)}, u32[]{:S(2)}) collective-permute-start(bf16[128,1024]{1,0:T(8,128)(2,1)S(1)} %get-tuple-element.113), channel_id=1, source_target_pairs={{0,0},{4,8},{8,4},{12,12},{1,1},{5,9},{9,5},{13,13},{2,2},{6,10},{... | collective-permute-start | bytes 786440 | tf_op jit(solution)/shard_map/ppermute | solution.py:428
  40.4 9.8 %collective-permute-start.12 = (bf16[128,1024]{1,0:T(8,128)(2,1)S(1)}, bf16[128,1024]{1,0:T(8,128)(2,1)S(1)}, u32[]{:S(2)}, u32[]{:S(2)}) collective-permute-start(bf16[128,1024]{1,0:T(8,128)(2,1)S(1)} %get-tuple-element.112), channel_id=1, source_target_pairs={{0,4},{4,0},{8,12},{12,8},{1,5},{5,1},{9,13},{13,9},{2,6},{6,2},{1... | collective-permute-start | bytes 786440 | tf_op jit(solution)/shard_map/ppermute | solution.py:428
  50.3 7.7 %collective-permute-start.16 = (bf16[128,1024]{1,0:T(8,128)(2,1)S(1)}, bf16[128,1024]{1,0:T(8,128)(2,1)S(1)}, u32[]{:S(2)}, u32[]{:S(2)}) collective-permute-start(bf16[128,1024]{1,0:T(8,128)(2,1)S(1)} %fusion), channel_id=1, source_target_pairs={{0,4},{4,0},{8,12},{12,8},{1,5},{5,1},{9,13},{13,9},{2,6},{6,2},{1... | collective-permute-start | bytes 786440 | tf_op jit(solution)/shard_map/ppermute | solution.py:428
  52.7 3.6 %collective-permute-start.17 = (bf16[128,1024]{1,0:T(8,128)(2,1)S(1)}, bf16[128,1024]{1,0:T(8,128)(2,1)S(1)}, u32[]{:S(2)}, u32[]{:S(2)}) collective-permute-start(bf16[128,1024]{1,0:T(8,128)(2,1)S(1)} %collective-permute-done.6.refs_7_), channel_id=1, source_target_pairs={{0,0},{4,8},{8,4},{12,12},{1,1},{5,9},{9,5},{13,13},{2,2},{6,10},{... | collective-permute-start | bytes 786440 | tf_op jit(solution)/shard_map/ppermute | solution.py:401
  58.1 7.4 %collective-permute-start.20 = (bf16[128,1024]{1,0:T(8,128)(2,1)S(1)}, bf16[128,1024]{1,0:T(8,128)(2,1)S(1)}, u32[]{:S(2)}, u32[]{:S(2)}) collective-permute-start(bf16[128,1024]{1,0:T(8,128)(2,1)S(1)} %collective-permute-done.17.refs_10_), channel_id=1, source_target_pairs={{0,4},{4,0},{8,12},{12,8},{1,5},{5,1},{9,13},{13,9},{2,6},{6,2},{1... | collective-permute-start | bytes 786440 | tf_op jit(solution)/shard_map/ppermute | solution.py:401
  61.1 7.2 %collective-permute-start.19 = (bf16[128,1024]{1,0:T(8,128)(2,1)S(1)}, bf16[128,1024]{1,0:T(8,128)(2,1)S(1)}, u32[]{:S(2)}, u32[]{:S(2)}) collective-permute-start(bf16[128,1024]{1,0:T(8,128)(2,1)S(1)} %collective-permute-done.15.refs_4_), channel_id=1, source_target_pairs={{0,4},{4,0},{8,12},{12,8},{1,5},{5,1},{9,13},{13,9},{2,6},{6,2},{1... | collective-permute-start | bytes 786440 | tf_op jit(solution)/shard_map/ppermute | solution.py:401
  62.9 5.7 %collective-permute-start.18 = (f32[128,128]{1,0:T(8,128)S(1)}, f32[128,128]{1,0:T(8,128)S(1)}, u32[]{:S(2)}, u32[]{:S(2)}) collective-permute-start(f32[128,128]{1,0:T(8,128)S(1)} %get-tuple-element.103), channel_id=1, source_target_pairs={{0,1},{1,0},{2,3},{3,2},{4,5},{5,4},{6,7},{7,6},{8,9},{9,8},{10,11... | collective-permute-start | bytes 196616 | tf_op jit(solution)/shard_map/ppermute | solution.py:21
  69.4 12.8 %all-to-all-start = ((bf16[8,160,128]{2,1,0:T(8,128)(2,1)}), bf16[8,160,128]{2,1,0:T(8,128)(2,1)S(1)}, u32[]{:S(2)}, u32[]{:S(2)}) async-start(bf16[8,160,128]{2,1,0:T(8,128)(2,1)} %shard_map.113), calls=%async_computation | async-start | bytes 655360 | tf_op jit(solution)/shard_map/all_to_all | solution.py:590
  74.4 1.2 %collective-permute-start.21 = (bf16[160,128]{1,0:T(8,128)(2,1)S(1)}, bf16[160,128]{1,0:T(8,128)(2,1)S(1)}, u32[]{:S(2)}, u32[]{:S(2)}) collective-permute-start(bf16[160,128]{1,0:T(8,128)(2,1)S(1)} %slice_bitcast_fusion.mine_ref), channel_id=1, source_target_pairs={{0,1},{1,0},{2,3},{3,2},{4,5},{5,4},{6,7},{7,6},{8,9},{9,8},{10,11... | collective-permute-start | bytes 122888 | tf_op jit(solution)/shard_map/ppermute | solution.py:21
  82.2 1.6 %collective-permute-start.22 = (bf16[8,160,128]{2,1,0:T(8,128)(2,1)S(1)}, bf16[8,160,128]{2,1,0:T(8,128)(2,1)S(1)}, u32[]{:S(2)}, u32[]{:S(2)}) collective-permute-start(bf16[8,160,128]{2,1,0:T(8,128)(2,1)S(1)} %all-to-all-done.source_ref), channel_id=1, source_target_pairs={{0,1},{1,0},{2,3},{3,2},{4,5},{5,4},{6,7},{7,6},{8,9},{9,8},{10,11... | collective-permute-start | bytes 983048 | tf_op jit(solution)/shard_map/ppermute | solution.py:21
  (15 other events, 128.5 us)
